TPU v7x, 32 devices: a whole 2x2x4 slice. The times are simulated.
32 devices in a mesh: grp: 2 (over y), seq: 4 (over z), mem: 2 (over x), rep: 2 (over core).
Axes of the slice: x: 2, y: 2, z: 4, core: 2. Of those that a mesh axis runs over, the one named last changes fastest.
Arguments:
- video_cache: bfloat16 [3, 1536, 4096], P(None, ('grp', 'seq'), 'mem'), parts along dimension 1, may hold values from -2.390625 to 2.390625
- plan: int32 [16], P('grp'), parts along dimension 0, may hold values from 0 to 1
- alignment: int32 [2048], P(('grp', 'seq')), parts along dimension 0, may hold values from 0 to 23, as said below
- audio_tokens: bfloat16 [2048, 2048], P(('grp', 'seq')), parts along dimension 0, may hold values from -64 to 64
- kv_weight: bfloat16 [4096, 4096], P('seq', ('mem', 'rep')), may hold values from -0.09375 to 0.09375
- query_weight: bfloat16 [2048, 2048], P('seq', ('mem', 'rep')), may hold values from -0.125 to 0.125
- out_weight: bfloat16 [2048, 2048], P(('mem', 'rep'), 'seq'), may hold values from -0.125 to 0.125
Outputs:
- video_features: bfloat16 [1536, 4096], P(('grp', 'seq'), 'mem'), parts along dimension 0
- audio_output: bfloat16 [2048, 2048], P(('grp', 'seq'), ('mem', 'rep')), parts along dimension 0
There are 2 independent parts, one for each index of `grp`. A program takes and returns all parts, laid end to end along the dimension named above; an argument that names none is the same for every part. Nothing has to cross between parts.
Inputs may be any that keep to these rules, and one draw needn't show every extreme that they name: `alignment`: frames rise with the token index up to a jitter of one frame; the first token is aligned with frame 0 and the last with frame 24 - 1.
All inputs are finite; a program needn't handle non-finite values.
Results may differ from a plain program's by a relative error of at most 0.0035.
Values may be sent and summed in bfloat16 or wider, within the bound.
No kernel may reach another device: no remote copies, remote signals or barrier semaphores. Data moves between devices by JAX's collectives and lax.ppermute only.
A program may use at most 64 MiB of HBM per device.

v0:
```python
import math

import jax
import jax.numpy as jnp
from jax import lax
from jax.sharding import PartitionSpec as P

HEAD_DIM = 128
FRAMES = 24


SLOPE = 4.0


def taylor_ratio(plan):
    history = plan.shape[0]
    step_ids = jnp.arange(history, dtype=jnp.int32)
    marked = step_ids * plan
    last_fresh = jnp.max(marked)
    prior_fresh = jnp.max(jnp.where(step_ids < last_fresh, marked, 0))
    return (history - last_fresh).astype(jnp.float32) / (last_fresh - prior_fresh).astype(
        jnp.float32
    )


def combine(orders, step_ratio):
    values = orders.astype(jnp.float32)
    return (values[0] + step_ratio * values[1] + 0.5 * step_ratio * step_ratio * values[2]).astype(
        jnp.bfloat16
    )


def on_device(video_cache, plan, alignment, audio_tokens, kv_weight, query_weight, out_weight):
    step_ratio = taylor_ratio(plan)
    own_part = combine(video_cache, step_ratio)
    features_all = lax.all_gather(own_part, "mem", axis=1, tiled=True)
    video_rows = features_all.shape[0]
    kv_local = jnp.dot(
        features_all,
        lax.all_gather(kv_weight, "seq", axis=0, tiled=True),
        preferred_element_type=jnp.float32,
    )
    head_size = HEAD_DIM
    local_heads = query_weight.shape[1] // head_size
    kv_local = kv_local.astype(jnp.bfloat16).reshape(video_rows, local_heads, 2, head_size)
    key_rows = kv_local[:, :, 0, :]
    value_rows = kv_local[:, :, 1, :]
    query_full, out_full = (
        lax.all_gather(query_weight, "seq", axis=0, tiled=True),
        lax.all_gather(out_weight, "seq", axis=1, tiled=True),
    )
    audio_rows = audio_tokens.shape[0]
    queries = jnp.dot(audio_tokens, query_full, preferred_element_type=jnp.float32).astype(
        jnp.bfloat16
    )
    queries = queries.reshape(audio_rows, local_heads, head_size)
    scale = 1.0 / head_size**0.5
    span = video_rows * lax.axis_size("seq")
    initial = (
        jnp.full((local_heads, audio_rows), -1e30, jnp.float32),
        jnp.zeros((local_heads, audio_rows), jnp.float32),
        jnp.zeros((local_heads, audio_rows, head_size), jnp.float32),
    )
    key_piece = lax.all_gather(key_rows, "seq", axis=0, tiled=True)
    value_piece = lax.all_gather(value_rows, "seq", axis=0, tiled=True)
    row_count = key_piece.shape[0]
    block_len = math.gcd(row_count, 1024)

    def advance(block_index, carried):
        row_max, row_sum, weighted = carried
        key_block = lax.dynamic_slice_in_dim(key_piece, block_index * block_len, block_len, 0)
        value_block = lax.dynamic_slice_in_dim(value_piece, block_index * block_len, block_len, 0)
        positions = block_index * block_len + jnp.arange(block_len, dtype=jnp.int32)
        frames_video = positions * FRAMES // span
        distance_bias = (
            -SLOPE
            * jnp.abs(frames_video[None, :] - alignment[:, None]).astype(jnp.float32)
            / FRAMES
        )
        scores = (
            jnp.einsum("qhd,khd->hqk", queries, key_block, preferred_element_type=jnp.float32)
            * scale
        )
        scores = scores + distance_bias[None]
        new_max = jnp.maximum(row_max, jnp.max(scores, axis=2))
        rescale = jnp.exp(row_max - new_max)
        exp_terms = jnp.exp(scores - new_max[:, :, None])
        row_sum = row_sum * rescale + jnp.sum(exp_terms, axis=2)
        weighted = weighted * rescale[:, :, None] + jnp.einsum(
            "hqk,khd->hqd",
            exp_terms.astype(jnp.bfloat16),
            value_block,
            preferred_element_type=jnp.float32,
        )
        return (new_max, row_sum, weighted)

    row_max, row_sum, weighted = lax.fori_loop(0, row_count // block_len, advance, initial)
    attended = (weighted / row_sum[:, :, None]).astype(jnp.bfloat16)
    attended = jnp.transpose(attended, (1, 0, 2)).reshape(audio_rows, local_heads * head_size)
    partial_update = jnp.dot(attended, out_full, preferred_element_type=jnp.float32)
    update = lax.psum_scatter(
        partial_update.astype(jnp.bfloat16), ("mem", "rep"), scatter_dimension=1, tiled=True
    ).astype(jnp.float32)
    own_columns = update.shape[1]
    residual = lax.dynamic_slice_in_dim(
        audio_tokens, lax.axis_index(("mem", "rep")) * own_columns, own_columns, 1
    )
    audio_output = (residual.astype(jnp.float32) + update).astype(jnp.bfloat16)
    return (own_part, audio_output)


def solution(mesh):
    return jax.shard_map(
        on_device,
        mesh=mesh,
        in_specs=(
            P(None, ("grp", "seq"), "mem"),
            P("grp"),
            P(("grp", "seq")),
            P(("grp", "seq"), None),
            P("seq", ("mem", "rep")),
            P("seq", ("mem", "rep")),
            P(("mem", "rep"), "seq"),
        ),
        out_specs=(P(("grp", "seq"), "mem"), P(("grp", "seq"), ("mem", "rep"))),
        check_vma=False,
    )
```

profile of v0, /device:TPU:0, one launch (start us, length us, event | category | flops | bytes accessed | tf_op | source)
XLA Modules:
  0.0 343.6 jit_solution(16587532398637790819)
XLA Ops:
  7.2 0.0 all-gather.10.cloned.1.call-start
  7.2 0.7 all-gather.10.cloned.1.call-update
  7.9 0.0 all-gather.14.cloned.1.call-start
  7.9 1.3 fusion.21
  9.2 1.9 fusion.20
  13.2 2.3 convert_element_type.60
  15.4 0.0 copy-start
  15.4 2.2 copy-done
  17.6 1.3 fusion.12
  18.9 0.0 copy-start.1
  18.9 0.0 all-gather.14.cloned.1.call-update
  19.0 0.0 all-gather.8.cloned.1.call-start
  19.0 0.7 all-gather.8.cloned.1.call-update
  19.7 0.0 all-gather.12.cloned.1.call-start
  19.7 0.5 all-gather.12.cloned.1.call-update
  20.3 0.0 reduce-scatter.2.cloned.1.call-start
  20.3 37.9 %all-gather.10.cloned.1.call-done = bf16[2048,512]{1,0:T(8,128)(2,1)} async-done(((bf16[512,512]{1,0:T(8,128)(2,1)}), bf16[2048,512]{1,0:T(8,128)(2,1)}) %all-gather.10.cloned.1.call-update) | async-done | bytes 2097168 | tf_op jit(solution)/shard_map/all_gather | solution.py:49
  58.2 0.0 copy-done.1
  58.2 2.3 fusion.19
  60.6 25.7 %all-gather.14.cloned.1.call-done = bf16[1,192,4096]{2,1,0:T(8,128)(2,1)} async-done(((bf16[1,192,2048]{2,1,0:T(8,128)(2,1)}), bf16[1,192,4096]{2,1,0:T(8,128)(2,1)}) %all-gather.14.cloned.1.call-update) | async-done | bytes 1572880 | tf_op jit(solution)/shard_map/all_gather | solution.py:36
  86.3 151.3 %all-gather.8.cloned.1.call-done = bf16[4096,1024]{1,0:T(8,128)(2,1)} async-done(((bf16[1024,1024]{1,0:T(8,128)(2,1)}), bf16[4096,1024]{1,0:T(8,128)(2,1)}) %all-gather.8.cloned.1.call-update) | async-done | bytes 8388624 | tf_op jit(solution)/shard_map/all_gather | solution.py:40
  237.6 5.7 %fusion.16 = bf16[192,1024]{1,0:T(8,128)(2,1)S(1)} fusion(bf16[4096,1024]{1,0:T(8,128)(2,1)} %all-gather.8.cloned.1.call-done, bf16[1,192,4096]{2,1,0:T(8,128)(2,1)} %all-gather.14.cloned.1.call-done), kind=kOutput, calls=%fused_computation.27 | convolution fusion | flops 1610809344 | bytes 10354688 | tf_op jit(solution)/shard_map/dot_general | solution.py:38
  243.2 0.3 reshape.68
  243.5 0.5 fusion.23
  244.1 0.0 copy-start.2
  244.1 30.3 %all-gather.1 = bf16[768,4,1,128]{3,0,1,2:T(8,128)(2,1)S(1)} all-gather(bf16[192,4,1,128]{3,0,1,2:T(8,128)(2,1)S(1)} %copy.19), channel_id=3, replica_groups=mesh['grp'=2,'seq'=4,'mem'=2,'rep'=2] {'seq'}, dimensions={0}, use_global_device_ids=true | all-gather | bytes 983040 | tf_op jit(solution)/shard_map/all_gather | solution.py:64
  274.4 29.8 %all-gather.2 = bf16[768,4,1,128]{3,0,1,2:T(8,128)(2,1)S(1)} all-gather(bf16[192,4,1,128]{3,0,1,2:T(8,128)(2,1)S(1)} %copy.20), channel_id=4, replica_groups=mesh['grp'=2,'seq'=4,'mem'=2,'rep'=2] {'seq'}, dimensions={0}, use_global_device_ids=true | all-gather | bytes 983040 | tf_op jit(solution)/shard_map/all_gather | solution.py:65
  304.2 0.0 copy-done.2
  304.2 3.5 %while.20 = (s32[]{:T(128)}, f32[4,256]{1,0:T(4,128)S(1)}, f32[4,256]{1,0:T(4,128)S(1)}, f32[4,256,128]{2,1,0:T(8,128)S(1)}, bf16[768,4,128]{2,0,1:T(8,128)(2,1)...) while((s32[]{:T(128)}, f32[4,256]{1,0:T(4,128)S(1)}, ...), condition=%wide.region_5.6_spmd.clone, body=%wide.region_2.5_spmd.clone.sunk | while | flops 136715776 | bytes 5573819 | solution.py:97
  304.3 0.1 convert_multiply_fusion.2
  304.4 0.3 fusion.40
  304.7 0.2 fusion.41
  304.9 0.5 convolution_add_fusion.2
  305.4 0.1 convert_multiply_fusion.2
  305.6 0.3 fusion.40
  305.9 0.2 fusion.41
  306.1 0.5 convolution_add_fusion.2
  306.6 0.1 convert_multiply_fusion.2
  306.7 0.3 fusion.40
  307.1 0.2 fusion.41
  307.2 0.5 convolution_add_fusion.2
  307.7 0.2 copy.17
  308.0 0.0 all-gather.12.cloned.1.call-done
  308.0 3.3 convolution_convert_fusion
  311.3 0.0 reduce-scatter.2.cloned.1.call-update
  311.3 3.7 %fusion.30 = bf16[192,2048]{1,0:T(8,128)(2,1)} fusion(f32[3,192,2048]{2,1,0:T(8,128)} %copy-done, f32[]{:T(128)S(6)} %mul.108, f32[]{:T(128)S(6)} %div.35), kind=kLoop, calls=%fused_computation.39 | loop fusion | flops 1966080 | bytes 5505032 | tf_op jit(solution)/shard_map/convert_element_type | solution.py:28
  315.0 20.3 %reduce-scatter.2.cloned.1.call-done = bf16[256,512]{1,0:T(8,128)(2,1)} async-done(((bf16[256,2048]{1,0:T(8,128)(2,1)}), bf16[256,512]{1,0:T(8,128)(2,1)}) %reduce-scatter.2.cloned.1.call-update) | async-done | bytes 262160 | tf_op jit(solution)/shard_map/reduce_scatter | solution.py:101
  335.3 1.8 add_convert_fusion
  (19 shorter events, 0.3 us)
Async XLA Ops:
  7.2 51.1 %all-gather.10.cloned.1.call-start = ((), (), s32[]{:S(2)}) async-start(), calls=%async_computation.2 | async-start | bytes 2621440 | tf_op jit(solution)/shard_map/all_gather | solution.py:49
  7.9 78.4 %all-gather.14.cloned.1.call-start = ((), (), s32[]{:S(2)}) async-start(), calls=%async_computation.5 | async-start | bytes 2359296 | tf_op jit(solution)/shard_map/all_gather | solution.py:36
  15.4 2.2 copy-start
  18.9 39.3 %copy-start.1 = (bf16[256,2048]{1,0:T(8,128)(2,1)S(1)}, bf16[256,2048]{1,0:T(8,128)(2,1)}, u32[]{:S(2)}) copy-start(bf16[256,2048]{1,0:T(8,128)(2,1)} %param.12) | copy-start | bytes 3145732
  19.0 218.6 %all-gather.8.cloned.1.call-start = ((), (), s32[]{:S(2)}) async-start(), calls=%async_computation.1 | async-start | bytes 10485760 | tf_op jit(solution)/shard_map/all_gather | solution.py:40
  19.7 288.3 %all-gather.12.cloned.1.call-start = ((), (), s32[]{:S(2)}) async-start(), calls=%async_computation.3 | async-start | bytes 2621440 | tf_op jit(solution)/shard_map/all_gather | solution.py:50
  20.3 315.0 %reduce-scatter.2.cloned.1.call-start = ((), (), s32[]{:S(2)}) async-start(), calls=%async_computation.4 | async-start | bytes 1310720 | tf_op jit(solution)/shard_map/reduce_scatter | solution.py:101
  244.1 60.2 %copy-start.2 = (s32[256]{0:T(256)S(1)}, s32[256]{0:T(256)}, u32[]{:S(2)}) copy-start(s32[256]{0:T(256)} %param.11) | copy-start | bytes 3076
Sparse Core Ops, SparseCore 0:
  9.6 48.6 all-gather.9
  60.4 25.9 all-gather.13
  87.9 149.6 all-gather.7
  239.0 67.7 all-gather.11
  311.5 23.8 reduce-scatter.1
where the time goes:
time: 344 us
  waiting for transfers between devices  237 us (69%)
  blocking collectives  60.1 us (17%)
  between operations  15.9 us (5%)
  matrix products  13.6 us (4%)
  other arithmetic  13.3 us (4%)
    all_gather x1, waiting for transfers between devices, on_device(): lax.all_gather(kv_weight, 'seq', axis=0, tiled=True)  151 us
    all_gather x1, waiting for transfers between devices, on_device(): lax.all_gather(query_weight, 'seq', axis=0, tiled=True)  37.9 us
    all_gather x1, blocking collectives, on_device(): key_piece = lax.all_gather(key_rows, 'seq', axis=0, tiled=True)  30.3 us
    all_gather x1, blocking collectives, on_device(): value_piece = lax.all_gather(value_rows, 'seq', axis=0, tiled=True)  29.8 us
    all_gather x1, waiting for transfers between devices, on_device(): features_all = lax.all_gather(own_part, 'mem', axis=1, tiled=True)  25.7 us
    reduce_scatter x1, waiting for transfers between devices, on_device(): lax.psum_scatter(partial_update.astype(jnp.bfloat16), ('mem', 'rep'), sca...  20.3 us
  transfers between devices with their start and end apart: 5, of which 4 were waited for; matrix products, arithmetic and copies ran while one was open for 7% of the time, Pallas kernels for 0%

commit v1 on v0

--- a/solution.py
+++ b/solution.py
@@ -30,7 +30,7 @@
     )
 
 
-def on_device(video_cache, plan, alignment, audio_tokens, kv_weight, query_weight, out_weight):
+def general(video_cache, plan, alignment, audio_tokens, kv_weight, query_weight, out_weight):
     step_ratio = taylor_ratio(plan)
     own_part = combine(video_cache, step_ratio)
     features_all = lax.all_gather(own_part, "mem", axis=1, tiled=True)
@@ -109,7 +109,138 @@
     return (own_part, audio_output)
 
 
+def fresh_ratio(plan):
+    history = plan.shape[0]
+    mask = jnp.sum(plan << jnp.arange(history, dtype=jnp.int32))
+    last_fresh = 31 - lax.clz(mask)
+    prior_fresh = 31 - lax.clz(mask - (1 << last_fresh))
+    return (history - last_fresh).astype(jnp.float32) / (last_fresh - prior_fresh).astype(
+        jnp.float32
+    )
+
+
+def swap(value, axis, bit):
+    size = lax.axis_size(axis)
+    return lax.ppermute(value, axis, [(i, i ^ bit) for i in range(size)])
+
+
+def whole_weight(shard):
+    seq_at, grp_at = lax.axis_index("seq"), lax.axis_index("grp")
+    rows, columns = shard.shape
+    half = lax.dynamic_slice_in_dim(shard, grp_at * (rows // 2), rows // 2, 0)
+    partner = swap(half, "seq", 1)
+    even = seq_at % 2 == 0
+    pair = jnp.stack([jnp.where(even, half, partner), jnp.where(even, partner, half)])
+    middle = lax.ppermute(pair, "seq", [(1, 2), (2, 1)])
+    edge = lax.ppermute(middle, "seq", [(1, 0), (2, 3)])
+    far = jnp.where((seq_at == 1) | (seq_at == 2), middle, edge)
+    partner_rest = swap(partner, "grp", 1)
+    far_rest = swap(far, "grp", 1)
+    whole = jnp.zeros((4, 2, rows // 2, columns), shard.dtype)
+    whole = lax.dynamic_update_slice(whole, shard.reshape(1, 2, rows // 2, columns), (seq_at, 0, 0, 0))
+    far_at = 2 - seq_at // 2 * 2
+    for value, group in ((partner, grp_at), (partner_rest, 1 - grp_at)):
+        whole = lax.dynamic_update_slice(whole, value[None, None], (seq_at ^ 1, group, 0, 0))
+    for value, group in ((far, grp_at), (far_rest, 1 - grp_at)):
+        whole = lax.dynamic_update_slice(whole, value[:, None], (far_at, group, 0, 0))
+    return whole.reshape(4, rows, columns)
+
+
+def by_head(video_cache, plan, alignment, audio_tokens, kv_weight, query_weight, out_weight):
+    seq_size = lax.axis_size("seq")
+    seq_at, mem_at, rep_at = (lax.axis_index(name) for name in ("seq", "mem", "rep"))
+    place = mem_at * 2 + rep_at
+    step_ratio = fresh_ratio(plan)
+    video_rows, mem_columns = video_cache.shape[1:]
+    depth = kv_weight.shape[0]
+
+    align_all = lax.all_to_all(
+        jnp.broadcast_to(alignment[None], (seq_size, alignment.shape[0])), "seq", 0, 0, tiled=True
+    ).reshape(-1)
+    query_full = whole_weight(query_weight).reshape(-1, query_weight.shape[1])
+
+    own_half = combine(lax.dynamic_slice_in_dim(video_cache, rep_at * depth, depth, 2), step_ratio)
+    moves = []
+    for source in range(seq_size * seq_size):
+        tokens, columns = divmod(source, seq_size)
+        moves.append((source, columns * seq_size + tokens % 2 * 2 + tokens // 2))
+    turned = lax.ppermute(own_half, ("seq", "mem", "rep"), moves)
+    beside = swap(turned, "rep", 1)
+    across = swap(turned, "mem", 1)
+    across_beside = swap(across, "rep", 1)
+    features = (
+        jnp.concatenate([turned, beside], axis=0),
+        jnp.concatenate([across, across_beside], axis=0),
+    )
+
+    head_columns = 2 * HEAD_DIM
+    kv_parts = []
+    for rows in features:
+
+        def partial_kv(head):
+            columns = lax.dynamic_slice_in_dim(kv_weight, head * head_columns, head_columns, 1)
+            return jnp.dot(rows, columns, preferred_element_type=jnp.float32)
+
+        arrived = [
+            swap(partial_kv(seq_at ^ bit).astype(jnp.bfloat16), "seq", bit) for bit in (3, 2, 1)
+        ]
+        kv_rows = partial_kv(seq_at)
+        for term in arrived:
+            kv_rows = kv_rows + term.astype(jnp.float32)
+        kv_parts.append(kv_rows.astype(jnp.bfloat16))
+    kv_rows = jnp.concatenate(kv_parts, axis=0)
+    key_rows, value_rows = kv_rows[:, :HEAD_DIM], kv_rows[:, HEAD_DIM:]
+
+    queries = jnp.dot(audio_tokens, query_full, preferred_element_type=jnp.float32).astype(
+        jnp.bfloat16
+    )
+    queries = lax.all_to_all(queries, "seq", split_axis=1, concat_axis=0, tiled=True)
+    out_full = whole_weight(out_weight)
+    own_part = combine(video_cache, step_ratio)
+
+    span = video_rows * seq_size
+    places = jnp.stack([place, place ^ 1, place ^ 2, place ^ 3])
+    tokens = places % 2 * 2 + places // 2
+    positions = (
+        tokens[:, None] * video_rows + jnp.arange(video_rows, dtype=jnp.int32)[None, :]
+    ).reshape(span)
+    frames_video = positions * FRAMES // span
+    distance_bias = (
+        -SLOPE * jnp.abs(frames_video[None, :] - align_all[:, None]).astype(jnp.float32) / FRAMES
+    )
+    scores = (
+        jnp.dot(queries, key_rows.T, preferred_element_type=jnp.float32) * (1.0 / HEAD_DIM**0.5)
+        + distance_bias
+    )
+    exp_terms = jnp.exp(scores - jnp.max(scores, axis=1, keepdims=True))
+    weighted = jnp.dot(
+        exp_terms.astype(jnp.bfloat16), value_rows, preferred_element_type=jnp.float32
+    )
+    attended = (weighted / jnp.sum(exp_terms, axis=1, keepdims=True)).astype(jnp.bfloat16)
+    attended = lax.all_to_all(attended, "seq", split_axis=0, concat_axis=1, tiled=True)
+
+    def partial_update(block):
+        columns = lax.dynamic_index_in_dim(out_full, block, 0, keepdims=False)
+        return jnp.dot(attended, columns, preferred_element_type=jnp.float32)
+
+    sent = jnp.stack([partial_update(place ^ 3), partial_update(place ^ 1)]).astype(jnp.bfloat16)
+    came = swap(sent, "rep", 1).astype(jnp.float32)
+    far = (partial_update(place ^ 2) + came[0]).astype(jnp.bfloat16)
+    update = partial_update(place) + came[1] + swap(far, "mem", 1).astype(jnp.float32)
+    own_columns = update.shape[1]
+    residual = lax.dynamic_slice_in_dim(audio_tokens, place * own_columns, own_columns, 1)
+    audio_output = (residual.astype(jnp.float32) + update).astype(jnp.bfloat16)
+    return (own_part, audio_output)
+
+
 def solution(mesh):
+    sizes = dict(mesh.shape)
+    square = (sizes["grp"], sizes["seq"], sizes["mem"], sizes["rep"]) == (2, 4, 2, 2)
+
+    def on_device(*arrays):
+        heads = arrays[5].shape[1] // HEAD_DIM
+        return (by_head if square and heads == sizes["seq"] else general)(*arrays)
+
     return jax.shard_map(
         on_device,
         mesh=mesh,

time: 344 us -> 151 us (0.44)
  waiting for transfers between devices: 237 us -> 49.5 us
  blocking collectives: 60.1 us -> 0 us
  starting transfers between devices: 0.19 us -> 45.5 us
  local copies, waits for them, and re-layouts: 3.31 us -> 18.6 us
  between operations: 15.9 us -> 2.31 us
  matrix products: 13.6 us -> 19.8 us
    all_gather x4 -> x0, waiting for transfers between devices: 215 us -> none  [the longest x1 151 us: on_device(): lax.all_gather(kv_weight, 'seq', axis=0, tiled=True)]
    all_gather x2 -> x0, blocking collectives: 60.1 us -> none  [the longest x1 30.3 us: on_device(): key_piece = lax.all_gather(key_rows, 'seq', axis=0, tiled=True)]
    ppermute x0 -> x22, waiting for transfers between devices: none -> 38.9 us  [the longest x17 38.9 us: swap(): return lax.ppermute(value, axis, [(i, i ^ bit) for i in range(size)])]
    ppermute x0 -> x22, starting transfers between devices: none -> 28.8 us  [the longest x17 19.6 us: swap(): return lax.ppermute(value, axis, [(i, i ^ bit) for i in range(size)])]
    reduce_scatter x1 -> x0, waiting for transfers between devices: 20.3 us -> none  [on_device(): lax.psum_scatter(partial_update.astype(jnp.bfloat16), ('mem', 'rep'), sca...]
    all_to_all x0 -> x3, starting transfers between devices: none -> 16.6 us  [the longest x1 6.9 us: by_head(): lax.all_to_all(queries, 'seq', split_axis=1, concat_axis=0, tiled=True)]
    all_to_all x0 -> x3, waiting for transfers between devices: none -> 10.7 us  [the longest x1 7.26 us: by_head(): lax.all_to_all(attended, 'seq', split_axis=0, concat_axis=1, tiled=True)]
    dynamic_update_slice x0 -> x8, local copies, waits for them, and re-layouts: none -> 7.25 us  [the longest x4 3.87 us: whole_weight(): lax.dynamic_update_slice(whole, value[None, None], (seq_at ^ 1, group, 0,...]
  transfers between devices with their start and end apart: 5 -> 25, of which waited for: 4 -> 8; matrix products, arithmetic and copies ran while one was open for 7% -> 30% of each run, Pallas kernels for 0% -> 0%
where the time goes in v1:
time: 151 us; the launch traced here: 150 us
  waiting for transfers between devices  49.5 us (33%)
  starting transfers between devices  45.5 us (30%)
  matrix products  19.8 us (13%)
  local copies, waits for them, and re-layouts  18.6 us (12%)
  other arithmetic  14.6 us (10%)
  between operations  2.31 us (2%)
    ppermute x17, waiting for transfers between devices, swap(): return lax.ppermute(value, axis, [(i, i ^ bit) for i in range(size)])  38.9 us
    ppermute x17, starting transfers between devices, swap(): return lax.ppermute(value, axis, [(i, i ^ bit) for i in range(size)])  19.6 us
    dot_general x8, matrix products, partial_kv(): return jnp.dot(rows, columns, preferred_element_type=jnp.float32)  7.57 us
    all_to_all x1, waiting for transfers between devices, by_head(): lax.all_to_all(attended, 'seq', split_axis=0, concat_axis=1, tiled=True)  7.26 us
    all_to_all x1, starting transfers between devices, by_head(): lax.all_to_all(queries, 'seq', split_axis=1, concat_axis=0, tiled=True)  6.9 us
    dot_general x4, matrix products, partial_update(): return jnp.dot(attended, columns, preferred_element_type=jnp.float32)  6.41 us
    all_to_all x1, starting transfers between devices, by_head(): lax.all_to_all(jnp.broadcast_to(alignment[None], (seq_size, alignment.sha...  6.32 us
    convert_element_type x2, other arithmetic, combine(): (values[0] + step_ratio * values[1] + 0.5 * step_ratio * step_ratio * val...  4.66 us
  transfers between devices with their start and end apart: 25, of which 8 were waited for; matrix products, arithmetic and copies ran while one was open for 30% of the time, Pallas kernels for 0%

profile of v1, /device:TPU:0, one launch (start us, length us, event | category | flops | bytes accessed | tf_op | source)
XLA Modules:
  0.0 150.2 jit_solution(4729919335696259826)
XLA Ops:
  0.6 1.4 broadcast_in_dim.39
  2.1 6.3 %all-to-all-start.1 = ((s32[4,1,256]{2,1,0:T(1,128)}), s32[4,1,256]{2,1,0:T(1,128)S(1)}, u32[]{:S(2)}, u32[]{:S(2)}) async-start(s32[4,1,256]{2,1,0:T(1,128)} %broadcast_in_dim.39), calls=%async_computation.1 | async-start | bytes 8192 | tf_op jit(solution)/shard_map/all_to_all | solution.py:157
  8.4 1.7 %constant_dynamic-slice_fusion.1 = bf16[256,512]{1,0:T(8,128)(2,1)} fusion(bf16[512,512]{1,0:T(8,128)(2,1)} %param.12, s32[]{:T(128)S(6)} %select_n.143), kind=kLoop, calls=%fused_computation.106 | loop fusion | bytes 524292 | tf_op jit(solution)/shard_map/dynamic_slice | solution.py:130
  10.0 2.0 %collective-permute-start = (bf16[256,512]{1,0:T(8,128)(2,1)}, bf16[256,512]{1,0:T(8,128)(2,1)S(1)}, u32[]{:S(2)}, u32[]{:S(2)}) collective-permute-start(bf16[256,512]{1,0:T(8,128)(2,1)} %constant_dynamic-slice_fusion.1), channel_id=1, source_target_pairs={{0,4},{4,0},{8,12},{12,8},{1,5},{5,1},{9,13},{13,9},{2,6},{6,2},{1... | collective-permute-start | bytes 786440 | tf_op jit(solution)/shard_map/ppermute | solution.py:124
  12.1 1.3 shift-left_reduce_fusion
  14.7 1.6 %dynamic-slice_convert_fusion = f32[3,192,1024]{2,1,0:T(8,128)S(1)} fusion(bf16[3,192,2048]{2,1,0:T(8,128)(2,1)} %param.7, s32[]{:T(128)S(6)} %select_n.155), kind=kLoop, calls=%fused_computation.22 | loop fusion | flops 589824 | bytes 3538948 | tf_op jit(solution)/shard_map/convert_element_type | solution.py:27
  17.3 4.5 %collective-permute-start.5 = (bf16[192,1024]{1,0:T(8,128)(2,1)}, bf16[192,1024]{1,0:T(8,128)(2,1)}, u32[]{:S(2)}, u32[]{:S(2)}) collective-permute-start(bf16[192,1024]{1,0:T(8,128)(2,1)} %fusion.54), channel_id=1, source_target_pairs={{0,0},{1,4},{2,8},{3,12},{4,2},{5,6},{6,10},{7,14},{8,1},{9,5},{10... | collective-permute-start | bytes 1179656 | tf_op jit(solution)/shard_map/ppermute | solution.py:167
  23.1 1.5 %broadcast.132.clone = bf16[4,2,256,512]{3,2,1,0:T(8,128)(2,1)} broadcast(bf16[]{:T(256)} %constant.102.clone.1), dimensions={} | broadcast | bytes 2097154 | tf_op jit(solution)/shard_map/broadcast.11
  25.5 1.5 %broadcast.132.clone.1 = bf16[4,2,256,512]{3,2,1,0:T(8,128)(2,1)} broadcast(bf16[]{:T(256)} %constant.102.clone.1), dimensions={} | broadcast | bytes 2097154 | tf_op jit(solution)/shard_map/broadcast.11
  29.0 12.2 %collective-permute-done.15 = bf16[256,512]{1,0:T(8,128)(2,1)} collective-permute-done((bf16[256,512]{1,0:T(8,128)(2,1)}, bf16[256,512]{1,0:T(8,128)(2,1)}, u32[]{:S(2)}, u32[]{:S(2)}) %collective-permute-start.15) | collective-permute-done | bytes 262176 | tf_op jit(solution)/shard_map/ppermute | solution.py:124
  41.2 1.0 select_bitcast_fusion.1
  42.3 1.5 collective-permute-start.17
  43.8 1.5 %collective-permute-start.1 = (bf16[256,512]{1,0:T(8,128)(2,1)S(1)}, bf16[256,512]{1,0:T(8,128)(2,1)S(1)}, u32[]{:S(2)}, u32[]{:S(2)}) collective-permute-start(bf16[256,512]{1,0:T(8,128)(2,1)S(1)} %collective-permute-done), channel_id=1, source_target_pairs={{0,16},{16,0},{1,17},{17,1},{2,18},{18,2},{3,19},{19,3},{4,20},{20... | collective-permute-start | bytes 786440 | tf_op jit(solution)/shard_map/ppermute | solution.py:124
  46.6 1.7 %bitcast_dynamic-update-slice_fusion.5 = bf16[4,2,256,512]{3,2,1,0:T(8,128)(2,1)} fusion(bf16[4,2,256,512]{3,2,1,0:T(8,128)(2,1)} %constant_dynamic-update-slice_fusion.4, s32[]{:T(128)S(6)} %select_n.144, s32[]{:T(128)S(6)} %select_n.145, bf16[256,512]{1,0:T(8,128)(2,1)} %collective-permute-done.15), kind=kLoop, calls=%fused_computation.78 | loop fusion | bytes 524296 | tf_op jit(solution)/shard_map/dynamic_update_slice | solution.py:143
  48.2 1.0 constant_dynamic-update-slice_fusion.1
  50.9 1.3 collective-permute-start.3
  52.6 2.7 %collective-permute-start.9 = (bf16[384,256]{1,0:T(8,128)(2,1)S(1)}, bf16[384,256]{1,0:T(8,128)(2,1)S(1)}, u32[]{:S(2)}, u32[]{:S(2)}) collective-permute-start(bf16[384,256]{1,0:T(8,128)(2,1)S(1)} %convolution_convert_fusion.6), channel_id=1, source_target_pairs={{0,4},{4,0},{8,12},{12,8},{1,5},{5,1},{9,13},{13,9},{2,6},{6,2},{1... | collective-permute-start | bytes 589832 | tf_op jit(solution)/shard_map/ppermute | solution.py:124
  56.2 1.4 collective-permute-start.8
  57.6 1.5 %collective-permute-start.7 = (bf16[384,256]{1,0:T(8,128)(2,1)S(1)}, bf16[384,256]{1,0:T(8,128)(2,1)S(1)}, u32[]{:S(2)}, u32[]{:S(2)}) collective-permute-start(bf16[384,256]{1,0:T(8,128)(2,1)S(1)} %convolution_convert_fusion.8), channel_id=1, source_target_pairs={{0,12},{4,8},{8,4},{12,0},{1,13},{5,9},{9,5},{13,1},{2,14},{6,10},... | collective-permute-start | bytes 589832 | tf_op jit(solution)/shard_map/ppermute | solution.py:124
  59.1 2.0 %collective-permute-done.10 = bf16[192,1024]{1,0:T(8,128)(2,1)S(1)} collective-permute-done((bf16[192,1024]{1,0:T(8,128)(2,1)}, bf16[192,1024]{1,0:T(8,128)(2,1)S(1)}, u32[]{:S(2)}, u32[]{:S(2)}) %collective-permute-start.10) | collective-permute-done | bytes 393248 | tf_op jit(solution)/shard_map/ppermute | solution.py:124
  61.8 17.1 %collective-permute-done.9 = bf16[384,256]{1,0:T(8,128)(2,1)S(1)} collective-permute-done((bf16[384,256]{1,0:T(8,128)(2,1)S(1)}, bf16[384,256]{1,0:T(8,128)(2,1)S(1)}, u32[]{:S(2)}, u32[]{:S(2)}) %collective-permute-start.9) | collective-permute-done | bytes 196640 | tf_op jit(solution)/shard_map/ppermute | solution.py:124
  79.0 1.3 collective-permute-start.18
  80.3 1.1 fusion.19
  82.4 1.5 %collective-permute-start.4 = (bf16[2,256,512]{2,1,0:T(8,128)(2,1)S(1)}, bf16[2,256,512]{2,1,0:T(8,128)(2,1)S(1)}, u32[]{:S(2)}, u32[]{:S(2)}) collective-permute-start(bf16[2,256,512]{2,1,0:T(8,128)(2,1)S(1)} %get-tuple-element.5), channel_id=1, source_target_pairs={{0,16},{16,0},{1,17},{17,1},{2,18},{18,2},{3,19},{19,3},{4,20},{20... | collective-permute-start | bytes 1572872 | tf_op jit(solution)/shard_map/ppermute | solution.py:124
  83.9 1.1 convolution_convert_fusion.3
  84.9 2.7 %collective-permute-start.14 = (bf16[384,256]{1,0:T(8,128)(2,1)}, bf16[384,256]{1,0:T(8,128)(2,1)}, u32[]{:S(2)}, u32[]{:S(2)}) collective-permute-start(bf16[384,256]{1,0:T(8,128)(2,1)} %convolution_convert_fusion.3), channel_id=1, source_target_pairs={{0,4},{4,0},{8,12},{12,8},{1,5},{5,1},{9,13},{13,9},{2,6},{6,2},{1... | collective-permute-start | bytes 589832 | tf_op jit(solution)/shard_map/ppermute | solution.py:124
  87.6 1.1 convolution_convert_fusion.4
  88.7 2.2 %collective-permute-start.13 = (bf16[384,256]{1,0:T(8,128)(2,1)}, bf16[384,256]{1,0:T(8,128)(2,1)}, u32[]{:S(2)}, u32[]{:S(2)}) collective-permute-start(bf16[384,256]{1,0:T(8,128)(2,1)} %convolution_convert_fusion.4), channel_id=1, source_target_pairs={{0,8},{4,12},{8,0},{12,4},{1,9},{5,13},{9,1},{13,5},{2,10},{6,14},... | collective-permute-start | bytes 589832 | tf_op jit(solution)/shard_map/ppermute | solution.py:124
  90.9 1.0 convolution_convert_fusion.5
  91.9 1.5 collective-permute-start.12
  93.4 1.6 %collective-permute-done.4 = bf16[2,256,512]{2,1,0:T(8,128)(2,1)S(1)} collective-permute-done((bf16[2,256,512]{2,1,0:T(8,128)(2,1)S(1)}, bf16[2,256,512]{2,1,0:T(8,128)(2,1)S(1)}, u32[]{:S(2)}, u32[]{:S(2)}) %collective-permute-start.4) | collective-permute-done | bytes 524320 | tf_op jit(solution)/shard_map/ppermute | solution.py:124
  95.8 3.1 %convolution_convert_fusion.2 = bf16[512,256]{1,0:T(8,128)(2,1)} fusion(bf16[2048,512]{1,0:T(8,128)(2,1)} %bitcast.9, bf16[256,2048]{1,0:T(8,128)(2,1)S(1)} %copy-done.6), kind=kOutput, calls=%fused_computation.17 | convolution fusion | flops 537001984 | bytes 3407872 | tf_op jit(solution)/shard_map/dot_general | solution.py:194
  98.9 1.8 %copy.16 = bf16[256,4,128]{2,0,1:T(8,128)(2,1)} copy(bf16[256,4,128]{0,2,1:T(8,128)(2,1)} %bitcast.111) | data formatting | bytes 524288 | tf_op jit(solution)/shard_map/all_to_all | solution.py:197
  100.7 6.9 %all-to-all-start = ((bf16[256,4,128]{2,0,1:T(8,128)(2,1)}), bf16[256,4,128]{2,0,1:T(8,128)(2,1)}, u32[]{:S(2)}, u32[]{:S(2)}) async-start(bf16[256,4,128]{2,0,1:T(8,128)(2,1)} %copy.16), calls=%async_computation | async-start | bytes 524288 | tf_op jit(solution)/shard_map/all_to_all | solution.py:197
  107.6 1.1 bitcast_dynamic-update-slice_fusion.1
  108.8 1.5 collective-permute-start.19
  110.2 2.2 %fusion.18 = bf16[384,256]{1,0:T(8,128)(2,1)} fusion(bf16[384,1024]{1,0:T(8,128)(2,1)S(1)} %constant_dynamic-update-slice_fusion.2, bf16[1024,1024]{1,0:T(8,128)(2,1)S(1)} %copy-done, s32[]{:T(128)S(6)} %select_n.156, bf16[384,256]{1,0:T(8,128)(2,1)} %collective-permute-done.14, bf16[384,256]{1,0:T(8,128)(2,1)} %collective-permute-done.13, ...), kind=kOutput, calls=%fused_computation.23 | convolution fusion | flops 202014720 | bytes 2097156 | tf_op jit(solution)/shard_map/dot_general | solution.py:182
  112.4 3.4 %all-to-all-done = bf16[256,4,128]{2,0,1:T(8,128)(2,1)} async-done(((bf16[256,4,128]{2,0,1:T(8,128)(2,1)}), bf16[256,4,128]{2,0,1:T(8,128)(2,1)}, u32[]{:S(2)}, u32[]{:S(2)}) %all-to-all-start) | async-done | bytes 262176 | tf_op jit(solution)/shard_map/all_to_all | solution.py:197
  115.8 2.1 %fusion.77 = (f32[1024]{0:T(1024)S(1)}, f32[1024,768]{0,1:T(8,128)S(1)}) fusion(s32[1024]{0:T(1024)S(1)} %bitcast.112, s32[768]{0:T(1024)S(1)} %add_select_fusion, bf16[1024,128]{1,0:T(8,128)(2,1)} %bitcast.13, bf16[384,256]{1,0:T(8,128)(2,1)} %fusion.19, bf16[384,256]{1,0:T(8,128)(2,1)} %fusion.18), kind=kOutput, calls=%fused_computation.126 | convolution fusion | flops 207223808 | bytes 3812352 | tf_op jit(solution)/shard_map/dot_general | solution.py:212
  120.4 3.4 %all-to-all-start.2 = ((bf16[4,256,128]{1,2,0:T(8,128)(2,1)}), bf16[4,256,128]{1,2,0:T(8,128)(2,1)S(1)}, u32[]{:S(2)}, u32[]{:S(2)}) async-start(bf16[4,256,128]{1,2,0:T(8,128)(2,1)} %copy.17), calls=%async_computation.2 | async-start | bytes 524288 | tf_op jit(solution)/shard_map/all_to_all | solution.py:220
  124.7 7.3 %all-to-all-done.2 = bf16[4,256,128]{1,2,0:T(8,128)(2,1)S(1)} async-done(((bf16[4,256,128]{1,2,0:T(8,128)(2,1)}), bf16[4,256,128]{1,2,0:T(8,128)(2,1)S(1)}, u32[]{:S(2)}, u32[]{:S(2)}) %all-to-all-start.2) | async-done | bytes 262176 | tf_op jit(solution)/shard_map/all_to_all | solution.py:220
  132.0 1.5 %fusion.21 = bf16[1,256,512]{2,1,0:T(8,128)(2,1)S(1)} fusion(bf16[256,512]{0,1:T(8,128)(2,1)S(1)} %bitcast.104, bf16[4,512,512]{2,1,0:T(8,128)(2,1)} %bitcast.32, s32[]{:T(128)S(6)} %select_n.168), kind=kOutput, calls=%fused_computation.32 | convolution fusion | flops 134348800 | bytes 1048580 | tf_op jit(solution)/shard_map/dot_general | solution.py:224
  133.5 1.4 fusion.20
  135.0 2.8 %convert_element_type.97 = f32[3,192,2048]{2,1,0:T(8,128)} convert(bf16[3,192,2048]{2,1,0:T(8,128)(2,1)S(1)} %copy-done.1) | non-fusion elementwise | flops 1179648 | bytes 7077888 | tf_op jit(solution)/shard_map/convert_element_type | solution.py:27
  137.9 1.4 fusion.27
  139.4 3.7 %fusion.22 = bf16[192,2048]{1,0:T(8,128)(2,1)} fusion(f32[3,192,2048]{2,1,0:T(8,128)} %convert_element_type.97, f32[]{:T(128)S(6)} %mul.106, f32[]{:T(128)S(6)} %div.49), kind=kLoop, calls=%fused_computation.33 | loop fusion | flops 1966080 | bytes 5505032 | tf_op jit(solution)/shard_map/convert_element_type | solution.py:28
  143.1 5.0 %collective-permute-done.21 = bf16[256,512]{1,0:T(8,128)(2,1)S(1)} collective-permute-done((bf16[256,512]{1,0:T(8,128)(2,1)S(1)}, bf16[256,512]{1,0:T(8,128)(2,1)S(1)}, u32[]{:S(2)}, u32[]{:S(2)}) %collective-permute-start.21) | collective-permute-done | bytes 262176 | tf_op jit(solution)/shard_map/ppermute | solution.py:124
  148.1 2.2 %fusion.31 = bf16[256,512]{1,0:T(8,128)(2,1)} fusion(f32[2,256,512]{2,1,0:T(8,128)S(1)} %convert_element_type.125, bf16[256,512]{1,0:T(8,128)(2,1)S(1)} %collective-permute-done.21, bf16[256,512]{0,1:T(8,128)(2,1)S(1)} %bitcast.107, bf16[4,512,512]{2,1,0:T(8,128)(2,1)} %bitcast.32, s32[]{:T(128)S(6)} %select_n.166, bf16[256,2048]{1,0:T(8,128)(2,1)} %param.10, ...), kind=kOutput, calls=%fused_computation.46 | convolution fusion | flops 135004160 | bytes 2097160 | tf_op jit(solution)/shard_map/dot_general | solution.py:224
  (70 shorter events, 15.6 us)
Async XLA Ops:
  0.6 51.6 %copy-start = (bf16[1024,1024]{1,0:T(8,128)(2,1)S(1)}, bf16[1024,1024]{1,0:T(8,128)(2,1)}, u32[]{:S(2)}) copy-start(bf16[1024,1024]{1,0:T(8,128)(2,1)} %param.11) | copy-start | bytes 6291460
  2.1 98.6 %all-to-all-start.1 = ((s32[4,1,256]{2,1,0:T(1,128)}), s32[4,1,256]{2,1,0:T(1,128)S(1)}, u32[]{:S(2)}, u32[]{:S(2)}) async-start(s32[4,1,256]{2,1,0:T(1,128)} %broadcast_in_dim.39), calls=%async_computation.1 | async-start | bytes 8192 | tf_op jit(solution)/shard_map/all_to_all | solution.py:157
  10.0 18.0 %collective-permute-start = (bf16[256,512]{1,0:T(8,128)(2,1)}, bf16[256,512]{1,0:T(8,128)(2,1)S(1)}, u32[]{:S(2)}, u32[]{:S(2)}) collective-permute-start(bf16[256,512]{1,0:T(8,128)(2,1)} %constant_dynamic-slice_fusion.1), channel_id=1, source_target_pairs={{0,4},{4,0},{8,12},{12,8},{1,5},{5,1},{9,13},{13,9},{2,6},{6,2},{1... | collective-permute-start | bytes 786440 | tf_op jit(solution)/shard_map/ppermute | solution.py:124
  16.3 5.5 %copy-start.3 = (bf16[512,512]{1,0:T(8,128)(2,1)S(1)}, bf16[512,512]{1,0:T(8,128)(2,1)}, u32[]{:S(2)}) copy-start(bf16[512,512]{1,0:T(8,128)(2,1)} %param.13) | copy-start | bytes 1572868
  16.3 8.4 %copy-start.2 = (bf16[512,512]{1,0:T(8,128)(2,1)S(1)}, bf16[512,512]{1,0:T(8,128)(2,1)}, u32[]{:S(2)}) copy-start(bf16[512,512]{1,0:T(8,128)(2,1)} %param.12) | copy-start | bytes 1572868
  17.3 29.3 %collective-permute-start.5 = (bf16[192,1024]{1,0:T(8,128)(2,1)}, bf16[192,1024]{1,0:T(8,128)(2,1)}, u32[]{:S(2)}, u32[]{:S(2)}) collective-permute-start(bf16[192,1024]{1,0:T(8,128)(2,1)} %fusion.54), channel_id=1, source_target_pairs={{0,0},{1,4},{2,8},{3,12},{4,2},{5,6},{6,10},{7,14},{8,1},{9,5},{10... | collective-permute-start | bytes 1179656 | tf_op jit(solution)/shard_map/ppermute | solution.py:167
  22.5 18.7 %collective-permute-start.15 = (bf16[256,512]{1,0:T(8,128)(2,1)}, bf16[256,512]{1,0:T(8,128)(2,1)}, u32[]{:S(2)}, u32[]{:S(2)}) collective-permute-start(bf16[256,512]{1,0:T(8,128)(2,1)} %constant_dynamic-slice_fusion), channel_id=1, source_target_pairs={{0,4},{4,0},{8,12},{12,8},{1,5},{5,1},{9,13},{13,9},{2,6},{6,2},{1... | collective-permute-start | bytes 786440 | tf_op jit(solution)/shard_map/ppermute | solution.py:124
  28.3 22.6 %collective-permute-start.2 = (bf16[2,256,512]{2,1,0:T(8,128)(2,1)S(1)}, bf16[2,256,512]{2,1,0:T(8,128)(2,1)S(1)}, u32[]{:S(2)}, u32[]{:S(2)}) collective-permute-start(bf16[2,256,512]{2,1,0:T(8,128)(2,1)S(1)} %pad_maximum_fusion), channel_id=1, source_target_pairs={{4,8},{8,4},{5,9},{9,5},{6,10},{10,6},{7,11},{11,7},{20,24},{24,20... | collective-permute-start | bytes 1572872 | tf_op jit(solution)/shard_map/ppermute | solution.py:134
  42.3 15.3 %collective-permute-start.17 = (bf16[2,256,512]{2,1,0:T(8,128)(2,1)S(1)}, bf16[2,256,512]{2,1,0:T(8,128)(2,1)}, u32[]{:S(2)}, u32[]{:S(2)}) collective-permute-start(bf16[2,256,512]{2,1,0:T(8,128)(2,1)S(1)} %pad_maximum_fusion.1), channel_id=1, source_target_pairs={{4,8},{8,4},{5,9},{9,5},{6,10},{10,6},{7,11},{11,7},{20,24},{24,20... | collective-permute-start | bytes 1572872 | tf_op jit(solution)/shard_map/ppermute | solution.py:134
  43.8 6.4 %collective-permute-start.1 = (bf16[256,512]{1,0:T(8,128)(2,1)S(1)}, bf16[256,512]{1,0:T(8,128)(2,1)S(1)}, u32[]{:S(2)}, u32[]{:S(2)}) collective-permute-start(bf16[256,512]{1,0:T(8,128)(2,1)S(1)} %collective-permute-done), channel_id=1, source_target_pairs={{0,16},{16,0},{1,17},{17,1},{2,18},{18,2},{3,19},{19,3},{4,20},{20... | collective-permute-start | bytes 786440 | tf_op jit(solution)/shard_map/ppermute | solution.py:124
  45.3 10.8 %collective-permute-start.16 = (bf16[256,512]{1,0:T(8,128)(2,1)}, bf16[256,512]{1,0:T(8,128)(2,1)S(1)}, u32[]{:S(2)}, u32[]{:S(2)}) collective-permute-start(bf16[256,512]{1,0:T(8,128)(2,1)} %collective-permute-done.15), channel_id=1, source_target_pairs={{0,16},{16,0},{1,17},{17,1},{2,18},{18,2},{3,19},{19,3},{4,20},{20... | collective-permute-start | bytes 786440 | tf_op jit(solution)/shard_map/ppermute | solution.py:124
  46.6 5.6 %collective-permute-start.6 = (bf16[192,1024]{1,0:T(8,128)(2,1)}, bf16[192,1024]{1,0:T(8,128)(2,1)S(1)}, u32[]{:S(2)}, u32[]{:S(2)}) collective-permute-start(bf16[192,1024]{1,0:T(8,128)(2,1)} %collective-permute-done.5), channel_id=1, source_target_pairs={{0,1},{1,0},{2,3},{3,2},{4,5},{5,4},{6,7},{7,6},{8,9},{9,8},{10,11... | collective-permute-start | bytes 1179656 | tf_op jit(solution)/shard_map/ppermute | solution.py:124
  50.2 10.9 %collective-permute-start.10 = (bf16[192,1024]{1,0:T(8,128)(2,1)}, bf16[192,1024]{1,0:T(8,128)(2,1)S(1)}, u32[]{:S(2)}, u32[]{:S(2)}) collective-permute-start(bf16[192,1024]{1,0:T(8,128)(2,1)} %collective-permute-done.5), channel_id=1, source_target_pairs={{0,2},{2,0},{1,3},{3,1},{4,6},{6,4},{5,7},{7,5},{8,10},{10,8},{9,1... | collective-permute-start | bytes 1179656 | tf_op jit(solution)/shard_map/ppermute | solution.py:124
  50.9 30.5 %collective-permute-start.3 = (bf16[2,256,512]{2,1,0:T(8,128)(2,1)S(1)}, bf16[2,256,512]{2,1,0:T(8,128)(2,1)S(1)}, u32[]{:S(2)}, u32[]{:S(2)}) collective-permute-start(bf16[2,256,512]{2,1,0:T(8,128)(2,1)S(1)} %collective-permute-done.2), channel_id=1, source_target_pairs={{4,0},{8,12},{5,1},{9,13},{6,2},{10,14},{7,3},{11,15},{20,16},{24,... | collective-permute-start | bytes 1572872 | tf_op jit(solution)/shard_map/ppermute | solution.py:135
  52.6 26.3 %collective-permute-start.9 = (bf16[384,256]{1,0:T(8,128)(2,1)S(1)}, bf16[384,256]{1,0:T(8,128)(2,1)S(1)}, u32[]{:S(2)}, u32[]{:S(2)}) collective-permute-start(bf16[384,256]{1,0:T(8,128)(2,1)S(1)} %convolution_convert_fusion.6), channel_id=1, source_target_pairs={{0,4},{4,0},{8,12},{12,8},{1,5},{5,1},{9,13},{13,9},{2,6},{6,2},{1... | collective-permute-start | bytes 589832 | tf_op jit(solution)/shard_map/ppermute | solution.py:124
  56.2 24.1 %collective-permute-start.8 = (bf16[384,256]{1,0:T(8,128)(2,1)S(1)}, bf16[384,256]{1,0:T(8,128)(2,1)S(1)}, u32[]{:S(2)}, u32[]{:S(2)}) collective-permute-start(bf16[384,256]{1,0:T(8,128)(2,1)S(1)} %convolution_convert_fusion.7), channel_id=1, source_target_pairs={{0,8},{4,12},{8,0},{12,4},{1,9},{5,13},{9,1},{13,5},{2,10},{6,14},... | collective-permute-start | bytes 589832 | tf_op jit(solution)/shard_map/ppermute | solution.py:124
  57.6 22.7 %collective-permute-start.7 = (bf16[384,256]{1,0:T(8,128)(2,1)S(1)}, bf16[384,256]{1,0:T(8,128)(2,1)S(1)}, u32[]{:S(2)}, u32[]{:S(2)}) collective-permute-start(bf16[384,256]{1,0:T(8,128)(2,1)S(1)} %convolution_convert_fusion.8), channel_id=1, source_target_pairs={{0,12},{4,8},{8,4},{12,0},{1,13},{5,9},{9,5},{13,1},{2,14},{6,10},... | collective-permute-start | bytes 589832 | tf_op jit(solution)/shard_map/ppermute | solution.py:124
  61.1 20.3 %collective-permute-start.11 = (bf16[192,1024]{1,0:T(8,128)(2,1)S(1)}, bf16[192,1024]{1,0:T(8,128)(2,1)S(1)}, u32[]{:S(2)}, u32[]{:S(2)}) collective-permute-start(bf16[192,1024]{1,0:T(8,128)(2,1)S(1)} %collective-permute-done.10), channel_id=1, source_target_pairs={{0,1},{1,0},{2,3},{3,2},{4,5},{5,4},{6,7},{7,6},{8,9},{9,8},{10,11... | collective-permute-start | bytes 1179656 | tf_op jit(solution)/shard_map/ppermute | solution.py:124
  79.0 28.6 %collective-permute-start.18 = (bf16[2,256,512]{2,1,0:T(8,128)(2,1)}, bf16[2,256,512]{2,1,0:T(8,128)(2,1)S(1)}, u32[]{:S(2)}, u32[]{:S(2)}) collective-permute-start(bf16[2,256,512]{2,1,0:T(8,128)(2,1)} %collective-permute-done.17), channel_id=1, source_target_pairs={{4,0},{8,12},{5,1},{9,13},{6,2},{10,14},{7,3},{11,15},{20,16},{24,... | collective-permute-start | bytes 1572872 | tf_op jit(solution)/shard_map/ppermute | solution.py:135
  82.4 12.6 %collective-permute-start.4 = (bf16[2,256,512]{2,1,0:T(8,128)(2,1)S(1)}, bf16[2,256,512]{2,1,0:T(8,128)(2,1)S(1)}, u32[]{:S(2)}, u32[]{:S(2)}) collective-permute-start(bf16[2,256,512]{2,1,0:T(8,128)(2,1)S(1)} %get-tuple-element.5), channel_id=1, source_target_pairs={{0,16},{16,0},{1,17},{17,1},{2,18},{18,2},{3,19},{19,3},{4,20},{20... | collective-permute-start | bytes 1572872 | tf_op jit(solution)/shard_map/ppermute | solution.py:124
  84.9 10.9 %copy-start.6 = (bf16[256,2048]{1,0:T(8,128)(2,1)S(1)}, bf16[256,2048]{1,0:T(8,128)(2,1)}, u32[]{:S(2)}) copy-start(bf16[256,2048]{1,0:T(8,128)(2,1)} %param.10) | copy-start | bytes 3145732
  84.9 25.3 %collective-permute-start.14 = (bf16[384,256]{1,0:T(8,128)(2,1)}, bf16[384,256]{1,0:T(8,128)(2,1)}, u32[]{:S(2)}, u32[]{:S(2)}) collective-permute-start(bf16[384,256]{1,0:T(8,128)(2,1)} %convolution_convert_fusion.3), channel_id=1, source_target_pairs={{0,4},{4,0},{8,12},{12,8},{1,5},{5,1},{9,13},{13,9},{2,6},{6,2},{1... | collective-permute-start | bytes 589832 | tf_op jit(solution)/shard_map/ppermute | solution.py:124
  88.7 21.6 %collective-permute-start.13 = (bf16[384,256]{1,0:T(8,128)(2,1)}, bf16[384,256]{1,0:T(8,128)(2,1)}, u32[]{:S(2)}, u32[]{:S(2)}) collective-permute-start(bf16[384,256]{1,0:T(8,128)(2,1)} %convolution_convert_fusion.4), channel_id=1, source_target_pairs={{0,8},{4,12},{8,0},{12,4},{1,9},{5,13},{9,1},{13,5},{2,10},{6,14},... | collective-permute-start | bytes 589832 | tf_op jit(solution)/shard_map/ppermute | solution.py:124
  91.9 18.3 %collective-permute-start.12 = (bf16[384,256]{1,0:T(8,128)(2,1)}, bf16[384,256]{1,0:T(8,128)(2,1)}, u32[]{:S(2)}, u32[]{:S(2)}) collective-permute-start(bf16[384,256]{1,0:T(8,128)(2,1)} %convolution_convert_fusion.5), channel_id=1, source_target_pairs={{0,12},{4,8},{8,4},{12,0},{1,13},{5,9},{9,5},{13,1},{2,14},{6,10},... | collective-permute-start | bytes 589832 | tf_op jit(solution)/shard_map/ppermute | solution.py:124
  100.7 15.1 %all-to-all-start = ((bf16[256,4,128]{2,0,1:T(8,128)(2,1)}), bf16[256,4,128]{2,0,1:T(8,128)(2,1)}, u32[]{:S(2)}, u32[]{:S(2)}) async-start(bf16[256,4,128]{2,0,1:T(8,128)(2,1)} %copy.16), calls=%async_computation | async-start | bytes 524288 | tf_op jit(solution)/shard_map/all_to_all | solution.py:197
  108.8 15.1 %collective-permute-start.19 = (bf16[2,256,512]{2,1,0:T(8,128)(2,1)}, bf16[2,256,512]{2,1,0:T(8,128)(2,1)S(1)}, u32[]{:S(2)}, u32[]{:S(2)}) collective-permute-start(bf16[2,256,512]{2,1,0:T(8,128)(2,1)} %get-tuple-element.3), channel_id=1, source_target_pairs={{0,16},{16,0},{1,17},{17,1},{2,18},{18,2},{3,19},{19,3},{4,20},{20... | collective-permute-start | bytes 1572872 | tf_op jit(solution)/shard_map/ppermute | solution.py:124
  117.9 0.9 copy-start.4
  117.9 1.0 copy-start.5
  120.4 11.6 %all-to-all-start.2 = ((bf16[4,256,128]{1,2,0:T(8,128)(2,1)}), bf16[4,256,128]{1,2,0:T(8,128)(2,1)S(1)}, u32[]{:S(2)}, u32[]{:S(2)}) async-start(bf16[4,256,128]{1,2,0:T(8,128)(2,1)} %copy.17), calls=%async_computation.2 | async-start | bytes 524288 | tf_op jit(solution)/shard_map/all_to_all | solution.py:220
  132.0 3.0 %copy-start.1 = (bf16[3,192,2048]{2,1,0:T(8,128)(2,1)S(1)}, bf16[3,192,2048]{2,1,0:T(8,128)(2,1)}, u32[]{:S(2)}) copy-start(bf16[3,192,2048]{2,1,0:T(8,128)(2,1)} %param.7) | copy-start | bytes 7077892
  134.9 2.9 %collective-permute-start.20 = (bf16[2,256,512]{2,1,0:T(8,128)(2,1)S(1)}, bf16[2,256,512]{2,1,0:T(8,128)(2,1)S(1)}, u32[]{:S(2)}, u32[]{:S(2)}) collective-permute-start(bf16[2,256,512]{2,1,0:T(8,128)(2,1)S(1)} %pad_maximum_fusion.2), channel_id=1, source_target_pairs={{0,1},{1,0},{2,3},{3,2},{4,5},{5,4},{6,7},{7,6},{8,9},{9,8},{10,11... | collective-permute-start | bytes 1572872 | tf_op jit(solution)/shard_map/ppermute | solution.py:124
  139.3 8.8 %collective-permute-start.21 = (bf16[256,512]{1,0:T(8,128)(2,1)S(1)}, bf16[256,512]{1,0:T(8,128)(2,1)S(1)}, u32[]{:S(2)}, u32[]{:S(2)}) collective-permute-start(bf16[256,512]{1,0:T(8,128)(2,1)S(1)} %fusion.27), channel_id=1, source_target_pairs={{0,2},{2,0},{1,3},{3,1},{4,6},{6,4},{5,7},{7,5},{8,10},{10,8},{9,1... | collective-permute-start | bytes 786440 | tf_op jit(solution)/shard_map/ppermute | solution.py:124

commit v2 on v0

--- a/solution.py
+++ b/solution.py
@@ -3,6 +3,8 @@
 import jax
 import jax.numpy as jnp
 from jax import lax
+from jax.experimental import pallas as pl
+from jax.experimental.pallas import tpu as pltpu
 from jax.sharding import PartitionSpec as P
 
 HEAD_DIM = 128
@@ -30,7 +32,7 @@
     )
 
 
-def on_device(video_cache, plan, alignment, audio_tokens, kv_weight, query_weight, out_weight):
+def general(video_cache, plan, alignment, audio_tokens, kv_weight, query_weight, out_weight):
     step_ratio = taylor_ratio(plan)
     own_part = combine(video_cache, step_ratio)
     features_all = lax.all_gather(own_part, "mem", axis=1, tiled=True)
@@ -109,7 +111,456 @@
     return (own_part, audio_output)
 
 
+def swap(value, axis, bit):
+    size = lax.axis_size(axis)
+    return lax.ppermute(value, axis, [(i, i ^ bit) for i in range(size)])
+
+
+VMEM = pl.BlockSpec(memory_space=pltpu.VMEM)
+SMEM = pl.BlockSpec(memory_space=pltpu.SMEM)
+ANY = pl.BlockSpec(memory_space=pl.ANY)
+
+
+def kernel_call(body, outs, ins, after=(), scratch=(), smem=(), loose_in=(), loose_out=(), limit=14):
+    def whole(*refs):
+        body(*refs[: len(ins)], *refs[len(ins) + len(after) :])
+
+    spots = [
+        SMEM if i in smem else ANY if i in loose_in else VMEM for i in range(1, len(ins))
+    ]
+    return pl.pallas_call(
+        whole,
+        out_shape=outs,
+        in_specs=[SMEM, *spots] + [ANY] * len(after),
+        out_specs=[ANY if i in loose_out else VMEM for i in range(len(outs))],
+        scratch_shapes=scratch,
+        compiler_params=pltpu.CompilerParams(vmem_limit_bytes=limit * 2**20),
+    )(*ins, *after)
+
+
+def plan_ratio(plan_ref, columns):
+    history = plan_ref.shape[0]
+    last_fresh, prior_fresh = jnp.int32(0), jnp.int32(0)
+    for step in range(history):
+        fresh = plan_ref[step] == 1
+        prior_fresh = jnp.where(fresh, last_fresh, prior_fresh)
+        last_fresh = jnp.where(fresh, step, last_fresh)
+    ahead = jnp.full((1, columns), history - last_fresh, jnp.int32).astype(jnp.float32)
+    apart = jnp.full((1, columns), last_fresh - prior_fresh, jnp.int32).astype(jnp.float32)
+    return ahead / apart
+
+
+def taylor_rows(cache_ref, out_ref, step_ratio, first, last):
+    half_square = 0.5 * step_ratio * step_ratio
+    for at in range(first, last, 16):
+        terms = [cache_ref[order, at : at + 16, :].astype(jnp.float32) for order in range(3)]
+        out_ref[at : at + 16, :] = (
+            terms[0] + step_ratio * terms[1] + half_square * terms[2]
+        ).astype(jnp.bfloat16)
+
+
+def taylor_body(plan_ref, cache_ref, out_ref):
+    rows, columns = out_ref.shape
+    taylor_rows(cache_ref, out_ref, plan_ratio(plan_ref, columns), 0, rows)
+
+
+def taylor(video_cache, plan, width):
+    orders, rows, columns = video_cache.shape
+    return pl.pallas_call(
+        taylor_body,
+        out_shape=jax.ShapeDtypeStruct((rows, columns), jnp.bfloat16),
+        grid=(columns // width,),
+        in_specs=[SMEM, pl.BlockSpec((orders, rows, width), lambda i: (0, 0, i))],
+        out_specs=pl.BlockSpec((rows, width), lambda i: (0, i)),
+        compiler_params=pltpu.CompilerParams(vmem_limit_bytes=8 * 2**20),
+    )(plan, video_cache)
+
+
+def first_body(
+    scalars,
+    plan_ref,
+    cache_ref,
+    audio_ref,
+    kv_ref,
+    query_ref,
+    out_w,
+    packed_ref,
+    other_ref,
+    half_ref,
+    held_ref,
+    sems,
+):
+    rep_at, mem_at, grp_at = scalars[0], scalars[1], scalars[2]
+    rows, width = held_ref.shape[1:]
+    width = width // 2
+    copies = []
+
+    def copy(source, target):
+        copies.append(pltpu.make_async_copy(source, target, sems.at[len(copies)]))
+
+    def part(index, size):
+        return pl.ds(pl.multiple_of(index * size, size), size)
+
+    blocks = 4
+    step = rows // blocks
+    for block in range(blocks):
+        at = pl.ds(block * step, step)
+        for shard in range(2):
+            copy(
+                cache_ref.at[:, at, part(2 * shard + rep_at, width)],
+                held_ref.at[:, at, pl.ds(shard * width, width)],
+            )
+    lane = width // 2
+    for shard in range(2):
+        copy(
+            audio_ref.at[:, part(2 * (2 * mem_at + shard) + rep_at, lane)],
+            packed_ref.at[pl.ds(2 * rows, audio_ref.shape[0]), pl.ds(shard * lane, lane)],
+        )
+    depth, columns = kv_ref.shape[0] // 2, query_ref.shape[1]
+    copy(kv_ref.at[part(1 - rep_at, depth)], other_ref.at[pl.ds(0, depth)])
+    quarter = query_ref.shape[0] // 4
+    for side in range(2):
+        copy(
+            query_ref.at[part(2 * (1 - rep_at) + side, quarter)],
+            other_ref.at[pl.ds(depth, quarter), pl.ds(side * columns, columns)],
+        )
+    copy(out_w.at[part(grp_at, half_ref.shape[0])], half_ref)
+    for started in copies:
+        started.start()
+    step_ratio = plan_ratio(plan_ref, width)
+    for block in range(blocks):
+        for shard in range(2):
+            copies[2 * block + shard].wait()
+            taylor_rows(
+                held_ref.at[:, :, pl.ds(shard * width, width)],
+                packed_ref.at[pl.ds(shard * rows, rows)],
+                step_ratio,
+                block * step,
+                (block + 1) * step,
+            )
+    for started in copies[2 * blocks :]:
+        started.wait()
+
+
+def weight_body(scalars, kv_ref, query_ref, other_ref, own_ref, *piece_refs):
+    seq_at, rep_at, grp_at = scalars[0], scalars[1], scalars[2]
+    kv_half, query_half = kv_ref.shape[0] // 2, query_ref.shape[0] // 2
+    kv_rows, query_rows = kv_half // 2, query_half // 2
+    fold = query_rows // 2
+
+    def fill(out_ref, bit, group, kv_at, query_at):
+        head = seq_at ^ bit
+        width = 2 * HEAD_DIM
+        lanes = pl.ds(pl.multiple_of(head * width, width), width)
+        at = pl.ds(pl.multiple_of(rep_at * kv_half + group * kv_rows, kv_rows), kv_rows)
+        out_ref[kv_at : kv_at + kv_rows, :width] = kv_ref[at, lanes]
+        at = pl.ds(pl.multiple_of(group * kv_rows, kv_rows), kv_rows)
+        out_ref[kv_at : kv_at + kv_rows, width:] = other_ref[at, lanes]
+        lanes = pl.ds(pl.multiple_of(head * HEAD_DIM, HEAD_DIM), HEAD_DIM)
+        other_lanes = pl.ds(
+            pl.multiple_of(group * query_ref.shape[1] + head * HEAD_DIM, HEAD_DIM), HEAD_DIM
+        )
+        for side in range(2):
+            first = rep_at * query_half + group * query_rows + side * fold
+            at = pl.ds(pl.multiple_of(first, fold), fold)
+            to = slice(query_at, query_at + fold)
+            out_ref[to, side * width : side * width + HEAD_DIM] = query_ref[at, lanes]
+            out_ref[to, side * width + HEAD_DIM : (side + 1) * width] = other_ref[
+                kv_half + side * fold : kv_half + (side + 1) * fold, other_lanes
+            ]
+
+    for group in range(2):
+        fill(own_ref, 0, group, group * kv_rows, kv_half + group * fold)
+    for bit, piece_ref in enumerate(piece_refs, 1):
+        fill(piece_ref, bit, grp_at, 0, kv_rows)
+
+
+def products_body(scalars, *refs):
+    packed_refs, weight_refs = refs[:8], refs[8:15]
+    send_ref, keep_ref, rows_ref, audio_ref, kv_ref, query_ref = refs[15:]
+    seq_at, mem_at, grp_at = scalars[0], scalars[1], scalars[2]
+    rows = rows_ref.shape[1] // 4
+    audio_rows = audio_ref.shape[1] // 4
+    lane = audio_ref.shape[2]
+    for at, packed_ref in enumerate(packed_refs):
+        slot, mem = divmod(at, 2)
+        for part in range(2):
+            shard = 2 * (mem_at ^ mem) + part
+            rows_ref[shard, slot * rows : (slot + 1) * rows, :] = packed_ref[
+                part * rows : (part + 1) * rows, :
+            ]
+            audio_ref[shard, slot * audio_rows : (slot + 1) * audio_rows, :] = packed_ref[
+                2 * rows :, part * lane : (part + 1) * lane
+            ]
+    kv_half = kv_ref.shape[1] // 2
+    fold = query_ref.shape[1] // 4
+    width = query_ref.shape[2]
+
+    def place(piece_ref, shard, group, kv_at, query_at):
+        to = pl.ds(pl.multiple_of(group * kv_half, kv_half), kv_half)
+        kv_ref[shard, to, :] = piece_ref[kv_at : kv_at + kv_half, :]
+        for side in range(2):
+            to = pl.ds(pl.multiple_of((2 * group + side) * fold, fold), fold)
+            query_ref[shard, to, :] = piece_ref[
+                query_at : query_at + fold, side * width : (side + 1) * width
+            ]
+
+    for group in range(2):
+        place(weight_refs[0], seq_at, group, group * kv_half, 2 * kv_half + group * fold)
+    for bit in range(1, 4):
+        place(weight_refs[2 * bit - 1], seq_at ^ bit, grp_at, 0, kv_half)
+        place(weight_refs[2 * bit], seq_at ^ bit, 1 - grp_at, 0, kv_half)
+
+    def summed(left_ref, right_ref):
+        total = jnp.dot(left_ref[0], right_ref[0], preferred_element_type=jnp.float32)
+        for shard in range(1, 4):
+            total += jnp.dot(
+                left_ref[shard], right_ref[shard], preferred_element_type=jnp.float32
+            )
+        return total
+
+    count = 4 * rows
+    columns = keep_ref.shape[1]
+    total = summed(rows_ref, kv_ref)
+    keep_ref[:count, :] = total[:, :columns]
+    send_ref[:count, :] = total[:, columns:]
+    total = summed(audio_ref, query_ref)
+    folded = 2 * audio_rows
+    for side in range(2):
+        at = slice(side * folded, (side + 1) * folded)
+        to = slice(side * HEAD_DIM, (side + 1) * HEAD_DIM)
+        keep_ref[count:, to] = total[at, :HEAD_DIM]
+        send_ref[count:, to] = total[at, HEAD_DIM:]
+
+
+def attend(queries, kv_ref, frames_ref, align):
+    scores = lax.dot_general(
+        queries,
+        kv_ref[:, :HEAD_DIM],
+        (((1,), (1,)), ((), ())),
+        preferred_element_type=jnp.float32,
+    ) * (1.0 / HEAD_DIM**0.5)
+    scores = scores - SLOPE * jnp.abs(frames_ref[...] - align) / FRAMES
+    exp_terms = jnp.exp(scores - jnp.max(scores, axis=1, keepdims=True))
+    weighted = jnp.dot(
+        exp_terms.astype(jnp.bfloat16), kv_ref[:, HEAD_DIM:], preferred_element_type=jnp.float32
+    )
+    return (weighted / jnp.sum(exp_terms, axis=1, keepdims=True)).astype(jnp.bfloat16)
+
+
+def attention_body(scalars, frames_ref, align_ref, keep_ref, came_ref, *refs):
+    *out_refs, kv_ref, query_ref = refs
+    count, audio_rows = kv_ref.shape[0], query_ref.shape[1]
+
+    def summed(rows, columns=slice(None)):
+        return (keep_ref[rows, columns] + came_ref[rows, columns]).astype(jnp.bfloat16)
+
+    kv_ref[...] = summed(slice(0, count))
+    for slot in range(4):
+        side, half = divmod(slot, 2)
+        query_ref[scalars[slot]] = summed(
+            slice(count + half * audio_rows, count + (half + 1) * audio_rows),
+            slice(side * HEAD_DIM, (side + 1) * HEAD_DIM),
+        )
+    for bit, out_ref in enumerate(out_refs):
+        block = scalars[0] ^ bit
+        out_ref[...] = attend(query_ref[block], kv_ref, frames_ref, align_ref[block])
+
+
+def out_body(
+    scalars,
+    own_ref,
+    near_ref,
+    far_ref,
+    farther_ref,
+    own_w,
+    partner_w,
+    partner_rest_w,
+    far_w,
+    far_rest_w,
+    send_ref,
+    keep_ref,
+    heads_ref,
+    weight_ref,
+    sem,
+):
+    seq_at, grp_at, place = scalars[0], scalars[1], scalars[2]
+    copy = pltpu.make_async_copy(own_w, weight_ref.at[0], sem)
+    copy.start()
+    for bit, head_ref in enumerate((own_ref, near_ref, far_ref, farther_ref)):
+        heads_ref[seq_at ^ bit] = head_ref[...]
+    heads = jnp.concatenate([heads_ref[head] for head in range(heads_ref.shape[0])], axis=1)
+    depth = partner_w.shape[0]
+    mine = pl.ds(pl.multiple_of(grp_at * depth, depth), depth)
+    rest = pl.ds(pl.multiple_of((1 - grp_at) * depth, depth), depth)
+    weight_ref[1, mine] = partner_w[...]
+    weight_ref[1, rest] = partner_rest_w[...]
+    for far in range(2):
+        weight_ref[2 + far, mine] = far_w[far]
+        weight_ref[2 + far, rest] = far_rest_w[far]
+    middle = 2 - seq_at // 2
+    for at, block in ((1, seq_at ^ 1), (2, middle), (3, middle ^ 1), (0, seq_at)):
+        if at == 0:
+            copy.wait()
+        slot = block ^ place
+        value = jnp.dot(heads, weight_ref[at], preferred_element_type=jnp.float32)
+
+        @pl.when(slot % 2 == 1)
+        def _():
+            send_ref[slot // 2] = value.astype(send_ref.dtype)
+
+        @pl.when(slot % 2 == 0)
+        def _():
+            keep_ref[slot // 2] = value
+
+
+def by_head(video_cache, plan, alignment, audio_tokens, kv_weight, query_weight, out_weight):
+    seq_size = lax.axis_size("seq")
+    seq_at, mem_at, rep_at = (lax.axis_index(name) for name in ("seq", "mem", "rep"))
+    grp_at = lax.axis_index("grp")
+    place = mem_at * 2 + rep_at
+    video_rows = video_cache.shape[1]
+    audio_rows = audio_tokens.shape[0]
+    half_depth, width = kv_weight.shape[0] // 2, 2 * HEAD_DIM
+    query_quarter = query_weight.shape[0] // 4
+
+    def bfloat(*shape):
+        return jax.ShapeDtypeStruct(shape, jnp.bfloat16)
+
+    packed, other, half = kernel_call(
+        first_body,
+        [
+            bfloat(2 * video_rows + audio_rows, half_depth),
+            bfloat(half_depth + query_quarter, kv_weight.shape[1]),
+            bfloat(out_weight.shape[0] // 2, out_weight.shape[1]),
+        ],
+        [
+            jnp.stack([rep_at, mem_at, grp_at]),
+            plan,
+            video_cache,
+            audio_tokens,
+            kv_weight,
+            query_weight,
+            out_weight,
+        ],
+        scratch=[
+            pltpu.VMEM((3, video_rows, 2 * half_depth), jnp.bfloat16),
+            pltpu.SemaphoreType.DMA((14,)),
+        ],
+        smem=(1,),
+        loose_in=(2, 3, 4, 5, 6),
+    )
+
+    other = swap(other, "rep", 1)
+    rows = half_depth // 2 + query_quarter // 2
+    weight_own, *pieces = kernel_call(
+        weight_body,
+        [bfloat(2 * rows, 2 * width)] + [bfloat(rows, 2 * width)] * 3,
+        [jnp.stack([seq_at, rep_at, grp_at]), kv_weight, query_weight, other],
+    )
+    weights = [weight_own]
+    for bit, piece in enumerate(pieces, 1):
+        piece = swap(piece, "seq", bit)
+        weights += [piece, swap(piece, "grp", 1)]
+
+    inner, outward = [(1, 2), (2, 1)], [(1, 0), (2, 3)]
+    is_inner = (seq_at == 1) | (seq_at == 2)
+    partner = swap(packed, "seq", 1)
+    align_all = lax.all_to_all(
+        jnp.broadcast_to(alignment[None], (seq_size, audio_rows)), "seq", 0, 0, tiled=True
+    ).astype(jnp.float32)
+    inner_own = lax.ppermute(packed, "seq", inner)
+    inner_partner = lax.ppermute(partner, "seq", inner)
+    third = jnp.where(is_inner, inner_own, lax.ppermute(inner_own, "seq", outward))
+    fourth = jnp.where(is_inner, inner_partner, lax.ppermute(inner_partner, "seq", outward))
+    tokens = []
+    for value in (packed, partner, third, fourth):
+        tokens += [value, swap(value, "mem", 1)]
+    middle = 2 - seq_at // 2
+    blocks = jnp.stack([seq_at, seq_at ^ 1, middle, middle ^ 1])
+
+    rows = seq_size * (video_rows + audio_rows // 2)
+    sums = jax.ShapeDtypeStruct((rows, width), jnp.float32)
+    send, keep = kernel_call(
+        products_body,
+        [sums, sums],
+        [jnp.stack([seq_at, mem_at, grp_at]), *tokens, *weights],
+        scratch=[
+            pltpu.VMEM((4, seq_size * video_rows, half_depth), jnp.bfloat16),
+            pltpu.VMEM((4, seq_size * audio_rows, 2 * query_quarter), jnp.bfloat16),
+            pltpu.VMEM((4, half_depth, 2 * width), jnp.bfloat16),
+            pltpu.VMEM((4, 2 * query_quarter, width), jnp.bfloat16),
+        ],
+        limit=26,
+    )
+    came = swap(send, "rep", 1)
+
+    half, _ = lax.optimization_barrier((half, third))
+    out_partner = swap(half, "seq", 1)
+    out_pair = lax.ppermute(jnp.stack([half, out_partner]), "seq", inner)
+    far = jnp.where(is_inner, out_pair, lax.ppermute(out_pair, "seq", outward))
+    partner_rest, far_rest = swap(out_partner, "grp", 1), swap(far, "grp", 1)
+
+    span = video_rows * seq_size
+    positions = blocks[:, None] * video_rows + jnp.arange(video_rows, dtype=jnp.int32)[None, :]
+    frames_video = (positions.reshape(1, span) * FRAMES // span).astype(jnp.float32)
+    own_piece, near_piece, far_piece, farther_piece = kernel_call(
+        attention_body,
+        [bfloat(audio_rows, HEAD_DIM)] * 4,
+        [blocks, frames_video, align_all[:, :, None], keep, came],
+        scratch=[
+            pltpu.VMEM((span, width), jnp.bfloat16),
+            pltpu.VMEM((seq_size, audio_rows, HEAD_DIM), jnp.bfloat16),
+        ],
+    )
+    far_piece = swap(far_piece, "seq", 2)
+    farther_piece = swap(farther_piece, "seq", 3)
+    near_piece = swap(near_piece, "seq", 1)
+
+    columns = out_weight.shape[1]
+    send, keep = kernel_call(
+        out_body,
+        [
+            jax.ShapeDtypeStruct((2, audio_rows, columns), jnp.bfloat16),
+            jax.ShapeDtypeStruct((2, audio_rows, columns), jnp.float32),
+        ],
+        [
+            jnp.stack([seq_at, grp_at, place]),
+            own_piece,
+            near_piece,
+            far_piece,
+            farther_piece,
+            out_weight,
+            out_partner,
+            partner_rest,
+            far,
+            far_rest,
+        ],
+        scratch=[
+            pltpu.VMEM((seq_size, audio_rows, HEAD_DIM), jnp.bfloat16),
+            pltpu.VMEM((seq_size, *out_weight.shape), jnp.bfloat16),
+            pltpu.SemaphoreType.DMA,
+        ],
+        loose_in=(5,),
+    )
+    came = swap(send, "rep", 1)
+    across = swap((keep[1] + came[1].astype(jnp.float32)).astype(jnp.bfloat16), "mem", 1)
+    residual = lax.dynamic_slice_in_dim(audio_tokens, place * columns, columns, 1)
+    own_part = taylor(video_cache, plan, 2 * half_depth)
+    base = residual.astype(jnp.float32) + (keep[0] + came[0].astype(jnp.float32))
+    base, across = lax.optimization_barrier((base, across))
+    audio_output = (base + across.astype(jnp.float32)).astype(jnp.bfloat16)
+    return (own_part, audio_output)
+
+
 def solution(mesh):
+    sizes = dict(mesh.shape)
+    square = (sizes["grp"], sizes["seq"], sizes["mem"], sizes["rep"]) == (2, 4, 2, 2)
+
+    def on_device(*arrays):
+        heads = arrays[5].shape[1] // HEAD_DIM
+        return (by_head if square and heads == sizes["seq"] else general)(*arrays)
+
     return jax.shard_map(
         on_device,
         mesh=mesh,

time: 344 us -> 155 us (0.45)
  waiting for transfers between devices: 237 us -> 70.8 us
  blocking collectives: 60.1 us -> 0 us
  starting transfers between devices: 0.19 us -> 52 us
  Pallas kernels: 0 us -> 16.8 us
  between operations: 15.9 us -> 0.89 us
  matrix products: 13.6 us -> 0 us
  other arithmetic: 13.3 us -> 5.93 us
  local copies, waits for them, and re-layouts: 3.31 us -> 8.21 us
    all_gather x4 -> x0, waiting for transfers between devices: 215 us -> none  [the longest x1 151 us: on_device(): lax.all_gather(kv_weight, 'seq', axis=0, tiled=True)]
    ppermute x0 -> x27, waiting for transfers between devices: none -> 68.9 us  [the longest x21 58.8 us: swap(): return lax.ppermute(value, axis, [(i, i ^ bit) for i in range(size)])]
    all_gather x2 -> x0, blocking collectives: 60.1 us -> none  [the longest x1 30.3 us: on_device(): key_piece = lax.all_gather(key_rows, 'seq', axis=0, tiled=True)]
    ppermute x0 -> x27, starting transfers between devices: none -> 47.3 us  [the longest x21 40.5 us: swap(): return lax.ppermute(value, axis, [(i, i ^ bit) for i in range(size)])]
    reduce_scatter x1 -> x0, waiting for transfers between devices: 20.3 us -> none  [on_device(): lax.psum_scatter(partial_update.astype(jnp.bfloat16), ('mem', 'rep'), sca...]
    pallas_call x0 -> x6, Pallas kernels: none -> 16.8 us  [the longest x5 15 us: kernel_call(): pl.pallas_call(whole, out_shape=outs, in_specs=[SMEM, *spots] + [ANY] * l...]
    dot_general x9 -> x0, matrix products: 13.6 us -> none  [the longest x1 5.66 us: on_device(): jnp.dot(features_all, lax.all_gather(kv_weight, 'seq', axis=0, tiled=True...]
    convert_element_type x5 -> x4, other arithmetic: 9.12 us -> 0.88 us  [the longest x1 0.78 us: by_head(): audio_output = (base + across.astype(jnp.float32)).astype(jnp.bfloat16)]
  transfers between devices with their start and end apart: 5 -> 28, of which waited for: 4 -> 10; matrix products, arithmetic and copies ran while one was open for 7% -> 4% of each run, Pallas kernels for 0% -> 7%
where the time goes in v2:
time: 155 us
  waiting for transfers between devices  70.8 us (46%)
  starting transfers between devices  52 us (34%)
  Pallas kernels  16.8 us (11%)
  local copies, waits for them, and re-layouts  8.21 us (5%)
  other arithmetic  5.93 us (4%)
    ppermute x21, waiting for transfers between devices, swap(): return lax.ppermute(value, axis, [(i, i ^ bit) for i in range(size)])  58.8 us
    ppermute x21, starting transfers between devices, swap(): return lax.ppermute(value, axis, [(i, i ^ bit) for i in range(size)])  40.5 us
    pallas_call x5, Pallas kernels, kernel_call(): pl.pallas_call(whole, out_shape=outs, in_specs=[SMEM, *spots] + [ANY] * l...  15 us
    ppermute x1, waiting for transfers between devices, by_head(): lax.ppermute(inner_partner, 'seq', outward)  10.1 us
    unnamed x26, local copies, waits for them, and re-layouts  7.25 us
    all_to_all x1, starting transfers between devices, by_head(): lax.all_to_all(jnp.broadcast_to(alignment[None], (seq_size, audio_rows)),...  4.72 us
  transfers between devices with their start and end apart: 28, of which 10 were waited for; matrix products, arithmetic and copies ran while one was open for 4% of the time, Pallas kernels for 7%

profile of v2, /device:TPU:0, one launch (start us, length us, event | category | flops | bytes accessed | tf_op | source)
XLA Modules:
  0.0 154.7 jit_solution(12381903312269574068)
XLA Ops:
  0.7 1.7 %copy-done = bf16[3,192,2048]{2,1,0:T(8,128)(2,1)S(1)} copy-done((bf16[3,192,2048]{2,1,0:T(8,128)(2,1)S(1)}, bf16[3,192,2048]{2,1,0:T(8,128)(2,1)}, u32[]{:S(2)}) %copy-start) | copy-done | bytes 2359320
  2.4 1.6 %copy-done.2 = bf16[1024,1024]{1,0:T(8,128)(2,1)S(1)} copy-done((bf16[1024,1024]{1,0:T(8,128)(2,1)S(1)}, bf16[1024,1024]{1,0:T(8,128)(2,1)}, u32[]{:S(2)}) %copy-start.2) | copy-done | bytes 2097176
  4.0 1.0 copy-done.4
  5.0 1.0 copy-done.6
  6.1 1.2 copy-done.8
  7.3 0.7 copy-done.9
  7.9 2.6 %shard_map.87 = (bf16[640,512]{1,0:T(8,128)(2,1)}, bf16[640,1024]{1,0:T(8,128)(2,1)}, bf16[256,512]{1,0:T(8,128)(2,1)S(1)}) custom-call(s32[3]{0:T(128)S(1)} %add_add_fusion.1.refs_0_, s32[8]{0:T(128)S(1)} %copy-done.9, bf16[3,192,2048]{2,1,0:T(8,128)(2,1)S(1)} %copy-done, bf16[256,2048]{1,0:T(8,128)(2,1)S(1)} %copy-done.8, ...), custom_call_target="tpu_custom_call" | custom-call | tf_op jit(solution)/shard_map/pallas_call | solution.py:131
  10.5 3.1 %collective-permute-start.1 = (bf16[640,512]{1,0:T(8,128)(2,1)}, bf16[640,512]{1,0:T(8,128)(2,1)}, u32[]{:S(2)}, u32[]{:S(2)}) collective-permute-start(bf16[640,512]{1,0:T(8,128)(2,1)} %get-tuple-element.20.refs_1_), channel_id=1, source_target_pairs={{0,4},{4,0},{8,12},{12,8},{1,5},{5,1},{9,13},{13,9},{2,6},{6,2},{1... | collective-permute-start | bytes 1966088 | tf_op jit(solution)/shard_map/ppermute | solution.py:116
  13.6 0.7 collective-permute-start.3
  14.3 14.3 %collective-permute-done.1.refs_3_ = bf16[640,512]{1,0:T(8,128)(2,1)} collective-permute-done((bf16[640,512]{1,0:T(8,128)(2,1)}, bf16[640,512]{1,0:T(8,128)(2,1)}, u32[]{:S(2)}, u32[]{:S(2)}) %collective-permute-start.1) | collective-permute-done | bytes 655392 | tf_op jit(solution)/shard_map/ppermute | solution.py:116
  28.7 1.5 collective-permute-start.6
  30.2 1.3 collective-permute-start.4
  31.5 1.3 collective-permute-start.7
  32.8 1.7 %collective-permute-start = (bf16[640,512]{1,0:T(8,128)(2,1)}, bf16[640,512]{1,0:T(8,128)(2,1)}, u32[]{:S(2)}, u32[]{:S(2)}) collective-permute-start(bf16[640,512]{1,0:T(8,128)(2,1)} %get-tuple-element.20.refs_1_), channel_id=1, source_target_pairs={{0,2},{2,0},{1,3},{3,1},{4,6},{6,4},{5,7},{7,5},{8,10},{10,8},{9,1... | collective-permute-start | bytes 1966088 | tf_op jit(solution)/shard_map/ppermute | solution.py:116
  35.0 1.6 %shard_map.88 = (bf16[640,512]{1,0:T(8,128)(2,1)S(1)}, bf16[320,512]{1,0:T(8,128)(2,1)S(1)}, bf16[320,512]{1,0:T(8,128)(2,1)S(1)}, bf16[320,512]{1,0:T(8,128)(2,1)S(1)}) custom-call(s32[3]{0:T(128)S(1)} %add_add_fusion.2.refs_0_, bf16[1024,1024]{1,0:T(8,128)(2,1)S(1)} %copy-done.3, bf16[512,512]{1,0:T(8,128)(2,1)S(1)} %copy-done.5, ...), custom_call_target="tpu_custom_call" | custom-call | tf_op jit(solution)/shard_map/pallas_call | solution.py:131
  36.5 17.8 %collective-permute-start.10 = (bf16[320,512]{1,0:T(8,128)(2,1)S(1)}, bf16[320,512]{1,0:T(8,128)(2,1)S(1)}, u32[]{:S(2)}, u32[]{:S(2)}) collective-permute-start(bf16[320,512]{1,0:T(8,128)(2,1)S(1)} %get-tuple-element.23), channel_id=1, source_target_pairs={{0,4},{4,0},{8,12},{12,8},{1,5},{5,1},{9,13},{13,9},{2,6},{6,2},{1... | collective-permute-start | bytes 983048 | tf_op jit(solution)/shard_map/ppermute | solution.py:116
  54.4 1.2 broadcast_select_fusion.1.refs_5_
  55.6 10.1 %collective-permute-done.7 = bf16[640,512]{1,0:T(8,128)(2,1)} collective-permute-done((bf16[640,512]{1,0:T(8,128)(2,1)}, bf16[640,512]{1,0:T(8,128)(2,1)}, u32[]{:S(2)}, u32[]{:S(2)}) %collective-permute-start.7) | collective-permute-done | bytes 655392 | tf_op jit(solution)/shard_map/ppermute | solution.py:475
  65.7 0.7 collective-permute-start.12
  66.4 1.2 broadcast_select_fusion.refs_7_
  67.5 1.6 %collective-permute-start.5 = (bf16[640,512]{1,0:T(8,128)(2,1)S(1)}, bf16[640,512]{1,0:T(8,128)(2,1)S(1)}, u32[]{:S(2)}, u32[]{:S(2)}) collective-permute-start(bf16[640,512]{1,0:T(8,128)(2,1)S(1)} %broadcast_select_fusion.1.refs_5_), channel_id=1, source_target_pairs={{0,2},{2,0},{1,3},{3,1},{4,6},{6,4},{5,7},{7,5},{8,10},{10,8},{9,1... | collective-permute-start | bytes 1966088 | tf_op jit(solution)/shard_map/ppermute | solution.py:116
  69.1 1.9 %collective-permute-start.14 = (bf16[320,512]{1,0:T(8,128)(2,1)S(1)}, bf16[320,512]{1,0:T(8,128)(2,1)S(1)}, u32[]{:S(2)}, u32[]{:S(2)}) collective-permute-start(bf16[320,512]{1,0:T(8,128)(2,1)S(1)} %get-tuple-element.25), channel_id=1, source_target_pairs={{0,12},{4,8},{8,4},{12,0},{1,13},{5,9},{9,5},{13,1},{2,14},{6,10},... | collective-permute-start | bytes 983048 | tf_op jit(solution)/shard_map/ppermute | solution.py:116
  71.0 3.5 %collective-permute-done.10.refs_10_ = bf16[320,512]{1,0:T(8,128)(2,1)S(1)} collective-permute-done((bf16[320,512]{1,0:T(8,128)(2,1)S(1)}, bf16[320,512]{1,0:T(8,128)(2,1)S(1)}, u32[]{:S(2)}, u32[]{:S(2)}) %collective-permute-start.10) | collective-permute-done | bytes 327712 | tf_op jit(solution)/shard_map/ppermute | solution.py:116
  74.5 1.5 collective-permute-start.11
  76.0 15.1 %collective-permute-done.20.refs_6_ = bf16[256,512]{1,0:T(8,128)(2,1)S(1)} collective-permute-done((bf16[256,512]{1,0:T(8,128)(2,1)S(1)}, bf16[256,512]{1,0:T(8,128)(2,1)S(1)}, u32[]{:S(2)}, u32[]{:S(2)}) %collective-permute-start.20) | collective-permute-done | bytes 262176 | tf_op jit(solution)/shard_map/ppermute | solution.py:116
  91.1 1.5 collective-permute-start.8
  92.7 0.7 collective-permute-start.22
  93.4 1.6 %collective-permute-start.13 = (bf16[320,512]{1,0:T(8,128)(2,1)S(1)}, bf16[320,512]{1,0:T(8,128)(2,1)S(1)}, u32[]{:S(2)}, u32[]{:S(2)}) collective-permute-start(bf16[320,512]{1,0:T(8,128)(2,1)S(1)} %collective-permute-done.12.refs_12_), channel_id=1, source_target_pairs={{0,16},{16,0},{1,17},{17,1},{2,18},{18,2},{3,19},{19,3},{4,20},{20... | collective-permute-start | bytes 983048 | tf_op jit(solution)/shard_map/ppermute | solution.py:116
  95.5 1.3 collective-permute-start.23
  96.8 7.2 %collective-permute-done.13.refs_13_ = bf16[320,512]{1,0:T(8,128)(2,1)S(1)} collective-permute-done((bf16[320,512]{1,0:T(8,128)(2,1)S(1)}, bf16[320,512]{1,0:T(8,128)(2,1)S(1)}, u32[]{:S(2)}, u32[]{:S(2)}) %collective-permute-start.13) | collective-permute-done | bytes 327712 | tf_op jit(solution)/shard_map/ppermute | solution.py:116
  104.1 4.7 %collective-permute-done.15.refs_15_ = bf16[320,512]{1,0:T(8,128)(2,1)S(1)} collective-permute-done((bf16[320,512]{1,0:T(8,128)(2,1)S(1)}, bf16[320,512]{1,0:T(8,128)(2,1)S(1)}, u32[]{:S(2)}, u32[]{:S(2)}) %collective-permute-start.15) | collective-permute-done | bytes 327712 | tf_op jit(solution)/shard_map/ppermute | solution.py:116
  108.8 5.4 %shard_map.89 = (f32[1280,256]{1,0:T(8,128)}, f32[1280,256]{1,0:T(8,128)S(1)}) custom-call(s32[3]{0:T(128)S(1)} %add_add_fusion.refs_0_, bf16[640,512]{1,0:T(8,128)(2,1)} %get-tuple-element.20.refs_1_, bf16[640,512]{1,0:T(8,128)(2,1)} %collective-permute-done.refs_2_, bf16[640,512]{1,0:T(8,128)(2,1)} %collective-permute-done.1.refs_3_, ...), custom_call_target="tpu_custom_call" | custom-call | tf_op jit(solution)/shard_map/pallas_call | solution.py:131
  114.8 4.7 %all-to-all-start = ((s32[4,1,256]{2,1,0:T(1,128)}), s32[4,1,256]{2,1,0:T(1,128)S(1)}, u32[]{:S(2)}, u32[]{:S(2)}) async-start(s32[4,1,256]{2,1,0:T(1,128)} %broadcast_in_dim.2), calls=%async_computation | async-start | bytes 8192 | tf_op jit(solution)/shard_map/all_to_all | solution.py:469
  119.6 1.1 broadcast_select_fusion.2.refs_8_
  120.8 1.6 %collective-permute-start.24 = (bf16[2,256,512]{2,1,0:T(8,128)(2,1)S(1)}, bf16[2,256,512]{2,1,0:T(8,128)(2,1)}, u32[]{:S(2)}, u32[]{:S(2)}) collective-permute-start(bf16[2,256,512]{2,1,0:T(8,128)(2,1)S(1)} %broadcast_select_fusion.2.refs_8_), channel_id=1, source_target_pairs={{0,16},{16,0},{1,17},{17,1},{2,18},{18,2},{3,19},{19,3},{4,20},{20... | collective-permute-start | bytes 1572872 | tf_op jit(solution)/shard_map/ppermute | solution.py:116
  123.1 1.9 %all-to-all-done = s32[4,1,256]{2,1,0:T(1,128)S(1)} async-done(((s32[4,1,256]{2,1,0:T(1,128)}), s32[4,1,256]{2,1,0:T(1,128)S(1)}, u32[]{:S(2)}, u32[]{:S(2)}) %all-to-all-start) | async-done | bytes 4128 | tf_op jit(solution)/shard_map/all_to_all | solution.py:469
  125.3 2.7 %shard_map.90 = (bf16[256,128]{1,0:T(8,128)(2,1)S(1)}, bf16[256,128]{1,0:T(8,128)(2,1)S(1)}, bf16[256,128]{1,0:T(8,128)(2,1)S(1)}, bf16[256,128]{1,0:T(8,128)(2,1)S(1)}) custom-call(s32[4]{0:T(128)S(1)} %get-tuple-element.39.refs_0_, f32[1,768]{1,0:T(1,128)S(1)} %fusion.3.refs_1_, f32[4,256,1]{2,1,0:T(8,128)S(1)} %convert_element_type.49.refs_2_, ...), custom_call_target="tpu_custom_call" | custom-call | tf_op jit(solution)/shard_map/pallas_call | solution.py:131
  128.0 0.6 collective-permute-start.17
  128.6 1.9 %collective-permute-start.18 = (bf16[256,128]{1,0:T(8,128)(2,1)S(1)}, bf16[256,128]{1,0:T(8,128)(2,1)S(1)}, u32[]{:S(2)}, u32[]{:S(2)}) collective-permute-start(bf16[256,128]{1,0:T(8,128)(2,1)S(1)} %get-tuple-element.30), channel_id=1, source_target_pairs={{0,8},{4,12},{8,0},{12,4},{1,9},{5,13},{9,1},{13,5},{2,10},{6,14},... | collective-permute-start | bytes 196616 | tf_op jit(solution)/shard_map/ppermute | solution.py:116
  130.5 1.9 %collective-permute-start.19 = (bf16[256,128]{1,0:T(8,128)(2,1)S(1)}, bf16[256,128]{1,0:T(8,128)(2,1)S(1)}, u32[]{:S(2)}, u32[]{:S(2)}) collective-permute-start(bf16[256,128]{1,0:T(8,128)(2,1)S(1)} %get-tuple-element.31), channel_id=1, source_target_pairs={{0,12},{4,8},{8,4},{12,0},{1,13},{5,9},{9,5},{13,1},{2,14},{6,10},... | collective-permute-start | bytes 196616 | tf_op jit(solution)/shard_map/ppermute | solution.py:116
  132.5 8.1 %collective-permute-done.21.refs_7_ = bf16[256,512]{1,0:T(8,128)(2,1)} collective-permute-done((bf16[256,512]{1,0:T(8,128)(2,1)S(1)}, bf16[256,512]{1,0:T(8,128)(2,1)}, u32[]{:S(2)}, u32[]{:S(2)}) %collective-permute-start.21) | collective-permute-done | bytes 262176 | tf_op jit(solution)/shard_map/ppermute | solution.py:116
  140.7 2.8 %shard_map.91 = (bf16[2,256,512]{2,1,0:T(8,128)(2,1)S(1)}, f32[2,256,512]{2,1,0:T(8,128)S(1)}) custom-call(s32[3]{0:T(128)S(1)} %pad_add_fusion.refs_0_, bf16[256,128]{1,0:T(8,128)(2,1)S(1)} %get-tuple-element.28.refs_1_, bf16[256,128]{1,0:T(8,128)(2,1)S(1)} %collective-permute-done.17.refs_2_, bf16[256,128]{1,0:T(8,128)(2,1)S(1)} %collective-permute-done.18.refs_3_, ...), custom_call_target="tpu_custom_call" | custom-call | tf_op jit(solution)/shard_map/pallas_call | solution.py:131
  143.5 1.9 %collective-permute-done.25 = bf16[2,256,512]{2,1,0:T(8,128)(2,1)S(1)} collective-permute-done((bf16[2,256,512]{2,1,0:T(8,128)(2,1)S(1)}, bf16[2,256,512]{2,1,0:T(8,128)(2,1)S(1)}, u32[]{:S(2)}, u32[]{:S(2)}) %collective-permute-start.25) | collective-permute-done | bytes 524320 | tf_op jit(solution)/shard_map/ppermute | solution.py:116
  145.5 1.6 %collective-permute-start.26 = (bf16[256,512]{1,0:T(8,128)(2,1)S(1)}, bf16[256,512]{1,0:T(8,128)(2,1)S(1)}, u32[]{:S(2)}, u32[]{:S(2)}) collective-permute-start(bf16[256,512]{1,0:T(8,128)(2,1)S(1)} %fusion), channel_id=1, source_target_pairs={{0,2},{2,0},{1,3},{3,1},{4,6},{6,4},{5,7},{7,5},{8,10},{10,8},{9,1... | collective-permute-start | bytes 786440 | tf_op jit(solution)/shard_map/ppermute | solution.py:116
  147.0 1.8 %shard_map.86 = bf16[192,2048]{1,0:T(8,128)(2,1)} custom-call(s32[8]{0:T(128)S(1)} %copy-done.10, bf16[3,192,2048]{2,1,0:T(8,128)(2,1)S(1)} %copy-done.1), custom_call_target="tpu_custom_call" | custom-call | tf_op jit(solution)/shard_map/pallas_call | solution.py:169
  148.9 1.0 bitcast_add_fusion
  149.9 4.0 %collective-permute-done.26 = bf16[256,512]{1,0:T(8,128)(2,1)S(1)} collective-permute-done((bf16[256,512]{1,0:T(8,128)(2,1)S(1)}, bf16[256,512]{1,0:T(8,128)(2,1)S(1)}, u32[]{:S(2)}, u32[]{:S(2)}) %collective-permute-start.26) | collective-permute-done | bytes 262176 | tf_op jit(solution)/shard_map/ppermute | solution.py:116
  153.9 0.8 add_convert_fusion
  (60 shorter events, 3.3 us)
Async XLA Ops:
  0.7 1.7 %copy-start = (bf16[3,192,2048]{2,1,0:T(8,128)(2,1)S(1)}, bf16[3,192,2048]{2,1,0:T(8,128)(2,1)}, u32[]{:S(2)}) copy-start(bf16[3,192,2048]{2,1,0:T(8,128)(2,1)} %refs_2_.2) | copy-start | bytes 7077892
  2.4 1.6 %copy-start.2 = (bf16[1024,1024]{1,0:T(8,128)(2,1)S(1)}, bf16[1024,1024]{1,0:T(8,128)(2,1)}, u32[]{:S(2)}) copy-start(bf16[1024,1024]{1,0:T(8,128)(2,1)} %refs_1_.3) | copy-start | bytes 6291460
  4.0 1.0 copy-start.4
  5.0 1.0 copy-start.6
  6.1 1.2 copy-start.8
  7.3 0.7 copy-start.9
  7.9 27.0 %copy-start.3 = (bf16[1024,1024]{1,0:T(8,128)(2,1)S(1)}, bf16[1024,1024]{1,0:T(8,128)(2,1)}, u32[]{:S(2)}) copy-start(bf16[1024,1024]{1,0:T(8,128)(2,1)} %refs_1_.3) | copy-start | bytes 6291460
  7.9 27.0 %copy-start.5 = (bf16[512,512]{1,0:T(8,128)(2,1)S(1)}, bf16[512,512]{1,0:T(8,128)(2,1)}, u32[]{:S(2)}) copy-start(bf16[512,512]{1,0:T(8,128)(2,1)} %refs_2_.3) | copy-start | bytes 1572868
  10.5 18.1 %collective-permute-start.1 = (bf16[640,512]{1,0:T(8,128)(2,1)}, bf16[640,512]{1,0:T(8,128)(2,1)}, u32[]{:S(2)}, u32[]{:S(2)}) collective-permute-start(bf16[640,512]{1,0:T(8,128)(2,1)} %get-tuple-element.20.refs_1_), channel_id=1, source_target_pairs={{0,4},{4,0},{8,12},{12,8},{1,5},{5,1},{9,13},{13,9},{2,6},{6,2},{1... | collective-permute-start | bytes 1966088 | tf_op jit(solution)/shard_map/ppermute | solution.py:116
  13.6 21.3 %collective-permute-start.9 = (bf16[640,1024]{1,0:T(8,128)(2,1)}, bf16[640,1024]{1,0:T(8,128)(2,1)}, u32[]{:S(2)}, u32[]{:S(2)}) collective-permute-start(bf16[640,1024]{1,0:T(8,128)(2,1)} %get-tuple-element.21), channel_id=1, source_target_pairs={{0,1},{1,0},{2,3},{3,2},{4,5},{5,4},{6,7},{7,6},{8,9},{9,8},{10,11... | collective-permute-start | bytes 3932168 | tf_op jit(solution)/shard_map/ppermute | solution.py:116
  13.6 16.6 %collective-permute-start.3 = (bf16[640,512]{1,0:T(8,128)(2,1)}, bf16[640,512]{1,0:T(8,128)(2,1)S(1)}, u32[]{:S(2)}, u32[]{:S(2)}) collective-permute-start(bf16[640,512]{1,0:T(8,128)(2,1)} %get-tuple-element.20.refs_1_), channel_id=1, source_target_pairs={{4,8},{8,4},{5,9},{9,5},{6,10},{10,6},{7,11},{11,7},{20,24},{24,20... | collective-permute-start | bytes 1966088 | tf_op jit(solution)/shard_map/ppermute | solution.py:472
  28.7 2.8 %collective-permute-start.6 = (bf16[640,512]{1,0:T(8,128)(2,1)}, bf16[640,512]{1,0:T(8,128)(2,1)}, u32[]{:S(2)}, u32[]{:S(2)}) collective-permute-start(bf16[640,512]{1,0:T(8,128)(2,1)} %collective-permute-done.1.refs_3_), channel_id=1, source_target_pairs={{4,8},{8,4},{5,9},{9,5},{6,10},{10,6},{7,11},{11,7},{20,24},{24,20... | collective-permute-start | bytes 1966088 | tf_op jit(solution)/shard_map/ppermute | solution.py:473
  30.2 24.2 %collective-permute-start.4 = (bf16[640,512]{1,0:T(8,128)(2,1)S(1)}, bf16[640,512]{1,0:T(8,128)(2,1)}, u32[]{:S(2)}, u32[]{:S(2)}) collective-permute-start(bf16[640,512]{1,0:T(8,128)(2,1)S(1)} %collective-permute-done.3), channel_id=1, source_target_pairs={{4,0},{8,12},{5,1},{9,13},{6,2},{10,14},{7,3},{11,15},{20,16},{24,... | collective-permute-start | bytes 1966088 | tf_op jit(solution)/shard_map/ppermute | solution.py:474
  31.5 34.2 %collective-permute-start.7 = (bf16[640,512]{1,0:T(8,128)(2,1)}, bf16[640,512]{1,0:T(8,128)(2,1)}, u32[]{:S(2)}, u32[]{:S(2)}) collective-permute-start(bf16[640,512]{1,0:T(8,128)(2,1)} %collective-permute-done.6), channel_id=1, source_target_pairs={{4,0},{8,12},{5,1},{9,13},{6,2},{10,14},{7,3},{11,15},{20,16},{24,... | collective-permute-start | bytes 1966088 | tf_op jit(solution)/shard_map/ppermute | solution.py:475
  32.8 34.8 %collective-permute-start = (bf16[640,512]{1,0:T(8,128)(2,1)}, bf16[640,512]{1,0:T(8,128)(2,1)}, u32[]{:S(2)}, u32[]{:S(2)}) collective-permute-start(bf16[640,512]{1,0:T(8,128)(2,1)} %get-tuple-element.20.refs_1_), channel_id=1, source_target_pairs={{0,2},{2,0},{1,3},{3,1},{4,6},{6,4},{5,7},{7,5},{8,10},{10,8},{9,1... | collective-permute-start | bytes 1966088 | tf_op jit(solution)/shard_map/ppermute | solution.py:116
  34.5 34.6 %collective-permute-start.2 = (bf16[640,512]{1,0:T(8,128)(2,1)}, bf16[640,512]{1,0:T(8,128)(2,1)S(1)}, u32[]{:S(2)}, u32[]{:S(2)}) collective-permute-start(bf16[640,512]{1,0:T(8,128)(2,1)} %collective-permute-done.1.refs_3_), channel_id=1, source_target_pairs={{0,2},{2,0},{1,3},{3,1},{4,6},{6,4},{5,7},{7,5},{8,10},{10,8},{9,1... | collective-permute-start | bytes 1966088 | tf_op jit(solution)/shard_map/ppermute | solution.py:116
  36.5 38.0 %collective-permute-start.10 = (bf16[320,512]{1,0:T(8,128)(2,1)S(1)}, bf16[320,512]{1,0:T(8,128)(2,1)S(1)}, u32[]{:S(2)}, u32[]{:S(2)}) collective-permute-start(bf16[320,512]{1,0:T(8,128)(2,1)S(1)} %get-tuple-element.23), channel_id=1, source_target_pairs={{0,4},{4,0},{8,12},{12,8},{1,5},{5,1},{9,13},{13,9},{2,6},{6,2},{1... | collective-permute-start | bytes 983048 | tf_op jit(solution)/shard_map/ppermute | solution.py:116
  55.5 35.6 %collective-permute-start.20 = (bf16[256,512]{1,0:T(8,128)(2,1)S(1)}, bf16[256,512]{1,0:T(8,128)(2,1)S(1)}, u32[]{:S(2)}, u32[]{:S(2)}) collective-permute-start(bf16[256,512]{1,0:T(8,128)(2,1)S(1)} %get-tuple-element.33), channel_id=1, source_target_pairs={{0,4},{4,0},{8,12},{12,8},{1,5},{5,1},{9,13},{13,9},{2,6},{6,2},{1... | collective-permute-start | bytes 786440 | tf_op jit(solution)/shard_map/ppermute | solution.py:116
  65.7 27.0 %collective-permute-start.12 = (bf16[320,512]{1,0:T(8,128)(2,1)S(1)}, bf16[320,512]{1,0:T(8,128)(2,1)S(1)}, u32[]{:S(2)}, u32[]{:S(2)}) collective-permute-start(bf16[320,512]{1,0:T(8,128)(2,1)S(1)} %get-tuple-element.24), channel_id=1, source_target_pairs={{0,8},{4,12},{8,0},{12,4},{1,9},{5,13},{9,1},{13,5},{2,10},{6,14},... | collective-permute-start | bytes 983048 | tf_op jit(solution)/shard_map/ppermute | solution.py:116
  67.5 41.2 %collective-permute-start.5 = (bf16[640,512]{1,0:T(8,128)(2,1)S(1)}, bf16[640,512]{1,0:T(8,128)(2,1)S(1)}, u32[]{:S(2)}, u32[]{:S(2)}) collective-permute-start(bf16[640,512]{1,0:T(8,128)(2,1)S(1)} %broadcast_select_fusion.1.refs_5_), channel_id=1, source_target_pairs={{0,2},{2,0},{1,3},{3,1},{4,6},{6,4},{5,7},{7,5},{8,10},{10,8},{9,1... | collective-permute-start | bytes 1966088 | tf_op jit(solution)/shard_map/ppermute | solution.py:116
  69.1 24.2 %collective-permute-start.14 = (bf16[320,512]{1,0:T(8,128)(2,1)S(1)}, bf16[320,512]{1,0:T(8,128)(2,1)S(1)}, u32[]{:S(2)}, u32[]{:S(2)}) collective-permute-start(bf16[320,512]{1,0:T(8,128)(2,1)S(1)} %get-tuple-element.25), channel_id=1, source_target_pairs={{0,12},{4,8},{8,4},{12,0},{1,13},{5,9},{9,5},{13,1},{2,14},{6,10},... | collective-permute-start | bytes 983048 | tf_op jit(solution)/shard_map/ppermute | solution.py:116
  74.5 20.4 %collective-permute-start.11 = (bf16[320,512]{1,0:T(8,128)(2,1)S(1)}, bf16[320,512]{1,0:T(8,128)(2,1)S(1)}, u32[]{:S(2)}, u32[]{:S(2)}) collective-permute-start(bf16[320,512]{1,0:T(8,128)(2,1)S(1)} %collective-permute-done.10.refs_10_), channel_id=1, source_target_pairs={{0,16},{16,0},{1,17},{17,1},{2,18},{18,2},{3,19},{19,3},{4,20},{20... | collective-permute-start | bytes 983048 | tf_op jit(solution)/shard_map/ppermute | solution.py:116
  91.1 17.7 %collective-permute-start.8 = (bf16[640,512]{1,0:T(8,128)(2,1)S(1)}, bf16[640,512]{1,0:T(8,128)(2,1)S(1)}, u32[]{:S(2)}, u32[]{:S(2)}) collective-permute-start(bf16[640,512]{1,0:T(8,128)(2,1)S(1)} %broadcast_select_fusion.refs_7_), channel_id=1, source_target_pairs={{0,2},{2,0},{1,3},{3,1},{4,6},{6,4},{5,7},{7,5},{8,10},{10,8},{9,1... | collective-permute-start | bytes 1966088 | tf_op jit(solution)/shard_map/ppermute | solution.py:116
  92.7 2.8 %collective-permute-start.22 = (bf16[2,256,512]{2,1,0:T(8,128)(2,1)S(1)}, bf16[2,256,512]{2,1,0:T(8,128)(2,1)S(1)}, u32[]{:S(2)}, u32[]{:S(2)}) collective-permute-start(bf16[2,256,512]{2,1,0:T(8,128)(2,1)S(1)} %pad_maximum_fusion), channel_id=1, source_target_pairs={{4,8},{8,4},{5,9},{9,5},{6,10},{10,6},{7,11},{11,7},{20,24},{24,20... | collective-permute-start | bytes 1572872 | tf_op jit(solution)/shard_map/ppermute | solution.py:500
  93.4 10.7 %collective-permute-start.13 = (bf16[320,512]{1,0:T(8,128)(2,1)S(1)}, bf16[320,512]{1,0:T(8,128)(2,1)S(1)}, u32[]{:S(2)}, u32[]{:S(2)}) collective-permute-start(bf16[320,512]{1,0:T(8,128)(2,1)S(1)} %collective-permute-done.12.refs_12_), channel_id=1, source_target_pairs={{0,16},{16,0},{1,17},{17,1},{2,18},{18,2},{3,19},{19,3},{4,20},{20... | collective-permute-start | bytes 983048 | tf_op jit(solution)/shard_map/ppermute | solution.py:116
  95.0 13.8 %collective-permute-start.15 = (bf16[320,512]{1,0:T(8,128)(2,1)S(1)}, bf16[320,512]{1,0:T(8,128)(2,1)S(1)}, u32[]{:S(2)}, u32[]{:S(2)}) collective-permute-start(bf16[320,512]{1,0:T(8,128)(2,1)S(1)} %collective-permute-done.14.refs_14_), channel_id=1, source_target_pairs={{0,16},{16,0},{1,17},{17,1},{2,18},{18,2},{3,19},{19,3},{4,20},{20... | collective-permute-start | bytes 983048 | tf_op jit(solution)/shard_map/ppermute | solution.py:116
  95.5 18.7 %copy-start.11 = (bf16[2,256,512]{2,1,0:T(8,128)(2,1)}, bf16[2,256,512]{2,1,0:T(8,128)(2,1)S(1)}, u32[]{:S(2)}) copy-start(bf16[2,256,512]{2,1,0:T(8,128)(2,1)S(1)} %collective-permute-done.22) | copy-start | bytes 1572868
  95.5 24.2 %collective-permute-start.23 = (bf16[2,256,512]{2,1,0:T(8,128)(2,1)S(1)}, bf16[2,256,512]{2,1,0:T(8,128)(2,1)}, u32[]{:S(2)}, u32[]{:S(2)}) collective-permute-start(bf16[2,256,512]{2,1,0:T(8,128)(2,1)S(1)} %collective-permute-done.22), channel_id=1, source_target_pairs={{4,0},{8,12},{5,1},{9,13},{6,2},{10,14},{7,3},{11,15},{20,16},{24,... | collective-permute-start | bytes 1572872 | tf_op jit(solution)/shard_map/ppermute | solution.py:501
  108.8 5.4 %copy-start.12 = (s32[256]{0:T(256)S(1)}, s32[256]{0:T(256)}, u32[]{:S(2)}) copy-start(s32[256]{0:T(256)} %param.9) | copy-start | bytes 3076
  114.2 11.1 %collective-permute-start.16 = (f32[1280,256]{1,0:T(8,128)}, f32[1280,256]{1,0:T(8,128)S(1)}, u32[]{:S(2)}, u32[]{:S(2)}) collective-permute-start(f32[1280,256]{1,0:T(8,128)} %get-tuple-element.27), channel_id=1, source_target_pairs={{0,1},{1,0},{2,3},{3,2},{4,5},{5,4},{6,7},{7,6},{8,9},{9,8},{10,11... | collective-permute-start | bytes 3932168 | tf_op jit(solution)/shard_map/ppermute | solution.py:116
  114.8 10.3 %all-to-all-start = ((s32[4,1,256]{2,1,0:T(1,128)}), s32[4,1,256]{2,1,0:T(1,128)S(1)}, u32[]{:S(2)}, u32[]{:S(2)}) async-start(s32[4,1,256]{2,1,0:T(1,128)} %broadcast_in_dim.2), calls=%async_computation | async-start | bytes 8192 | tf_op jit(solution)/shard_map/all_to_all | solution.py:469
  120.8 19.8 %collective-permute-start.24 = (bf16[2,256,512]{2,1,0:T(8,128)(2,1)S(1)}, bf16[2,256,512]{2,1,0:T(8,128)(2,1)}, u32[]{:S(2)}, u32[]{:S(2)}) collective-permute-start(bf16[2,256,512]{2,1,0:T(8,128)(2,1)S(1)} %broadcast_select_fusion.2.refs_8_), channel_id=1, source_target_pairs={{0,16},{16,0},{1,17},{17,1},{2,18},{18,2},{3,19},{19,3},{4,20},{20... | collective-permute-start | bytes 1572872 | tf_op jit(solution)/shard_map/ppermute | solution.py:116
  122.6 18.0 %collective-permute-start.21 = (bf16[256,512]{1,0:T(8,128)(2,1)S(1)}, bf16[256,512]{1,0:T(8,128)(2,1)}, u32[]{:S(2)}, u32[]{:S(2)}) collective-permute-start(bf16[256,512]{1,0:T(8,128)(2,1)S(1)} %collective-permute-done.20.refs_6_), channel_id=1, source_target_pairs={{0,16},{16,0},{1,17},{17,1},{2,18},{18,2},{3,19},{19,3},{4,20},{20... | collective-permute-start | bytes 786440 | tf_op jit(solution)/shard_map/ppermute | solution.py:116
  125.3 15.3 %copy-start.7 = (bf16[512,512]{1,0:T(8,128)(2,1)S(1)}, bf16[512,512]{1,0:T(8,128)(2,1)}, u32[]{:S(2)}) copy-start(bf16[512,512]{1,0:T(8,128)(2,1)} %refs_5_.3) | copy-start | bytes 1572868
  128.0 12.6 %collective-permute-start.17 = (bf16[256,128]{1,0:T(8,128)(2,1)S(1)}, bf16[256,128]{1,0:T(8,128)(2,1)S(1)}, u32[]{:S(2)}, u32[]{:S(2)}) collective-permute-start(bf16[256,128]{1,0:T(8,128)(2,1)S(1)} %get-tuple-element.29), channel_id=1, source_target_pairs={{0,4},{4,0},{8,12},{12,8},{1,5},{5,1},{9,13},{13,9},{2,6},{6,2},{1... | collective-permute-start | bytes 196616 | tf_op jit(solution)/shard_map/ppermute | solution.py:116
  128.6 12.0 %collective-permute-start.18 = (bf16[256,128]{1,0:T(8,128)(2,1)S(1)}, bf16[256,128]{1,0:T(8,128)(2,1)S(1)}, u32[]{:S(2)}, u32[]{:S(2)}) collective-permute-start(bf16[256,128]{1,0:T(8,128)(2,1)S(1)} %get-tuple-element.30), channel_id=1, source_target_pairs={{0,8},{4,12},{8,0},{12,4},{1,9},{5,13},{9,1},{13,5},{2,10},{6,14},... | collective-permute-start | bytes 196616 | tf_op jit(solution)/shard_map/ppermute | solution.py:116
  130.5 10.1 %collective-permute-start.19 = (bf16[256,128]{1,0:T(8,128)(2,1)S(1)}, bf16[256,128]{1,0:T(8,128)(2,1)S(1)}, u32[]{:S(2)}, u32[]{:S(2)}) collective-permute-start(bf16[256,128]{1,0:T(8,128)(2,1)S(1)} %get-tuple-element.31), channel_id=1, source_target_pairs={{0,12},{4,8},{8,4},{12,0},{1,13},{5,9},{9,5},{13,1},{2,14},{6,10},... | collective-permute-start | bytes 196616 | tf_op jit(solution)/shard_map/ppermute | solution.py:116
  140.6 6.4 %copy-start.1 = (bf16[3,192,2048]{2,1,0:T(8,128)(2,1)S(1)}, bf16[3,192,2048]{2,1,0:T(8,128)(2,1)}, u32[]{:S(2)}) copy-start(bf16[3,192,2048]{2,1,0:T(8,128)(2,1)} %refs_2_.2) | copy-start | bytes 7077892
  140.6 6.4 %copy-start.10 = (s32[8]{0:T(128)S(1)}, s32[8]{0:T(128)}, u32[]{:S(2)}) copy-start(s32[8]{0:T(128)} %refs_1_.2) | copy-start | bytes 100
  143.4 2.0 %collective-permute-start.25 = (bf16[2,256,512]{2,1,0:T(8,128)(2,1)S(1)}, bf16[2,256,512]{2,1,0:T(8,128)(2,1)S(1)}, u32[]{:S(2)}, u32[]{:S(2)}) collective-permute-start(bf16[2,256,512]{2,1,0:T(8,128)(2,1)S(1)} %get-tuple-element.35), channel_id=1, source_target_pairs={{0,1},{1,0},{2,3},{3,2},{4,5},{5,4},{6,7},{7,6},{8,9},{9,8},{10,11... | collective-permute-start | bytes 1572872 | tf_op jit(solution)/shard_map/ppermute | solution.py:116
  145.5 8.4 %collective-permute-start.26 = (bf16[256,512]{1,0:T(8,128)(2,1)S(1)}, bf16[256,512]{1,0:T(8,128)(2,1)S(1)}, u32[]{:S(2)}, u32[]{:S(2)}) collective-permute-start(bf16[256,512]{1,0:T(8,128)(2,1)S(1)} %fusion), channel_id=1, source_target_pairs={{0,2},{2,0},{1,3},{3,1},{4,6},{6,4},{5,7},{7,5},{8,10},{10,8},{9,1... | collective-permute-start | bytes 786440 | tf_op jit(solution)/shard_map/ppermute | solution.py:116

commit v3 on v2

--- a/solution.py
+++ b/solution.py
@@ -119,6 +119,7 @@
 VMEM = pl.BlockSpec(memory_space=pltpu.VMEM)
 SMEM = pl.BlockSpec(memory_space=pltpu.SMEM)
 ANY = pl.BlockSpec(memory_space=pl.ANY)
+HBM = pl.BlockSpec(memory_space=pltpu.HBM)
 
 
 def kernel_call(body, outs, ins, after=(), scratch=(), smem=(), loose_in=(), loose_out=(), limit=14):
@@ -126,13 +127,13 @@
         body(*refs[: len(ins)], *refs[len(ins) + len(after) :])
 
     spots = [
-        SMEM if i in smem else ANY if i in loose_in else VMEM for i in range(1, len(ins))
+        SMEM if i in smem else HBM if i in loose_in else VMEM for i in range(1, len(ins))
     ]
     return pl.pallas_call(
         whole,
         out_shape=outs,
         in_specs=[SMEM, *spots] + [ANY] * len(after),
-        out_specs=[ANY if i in loose_out else VMEM for i in range(len(outs))],
+        out_specs=[HBM if i in loose_out else VMEM for i in range(len(outs))],
         scratch_shapes=scratch,
         compiler_params=pltpu.CompilerParams(vmem_limit_bytes=limit * 2**20),
     )(*ins, *after)
@@ -279,29 +280,29 @@
     packed_refs, weight_refs = refs[:8], refs[8:15]
     send_ref, keep_ref, rows_ref, audio_ref, kv_ref, query_ref = refs[15:]
     seq_at, mem_at, grp_at = scalars[0], scalars[1], scalars[2]
-    rows = rows_ref.shape[1] // 4
-    audio_rows = audio_ref.shape[1] // 4
-    lane = audio_ref.shape[2]
+    rows, audio_rows = rows_ref.shape[0] // 4, audio_ref.shape[0] // 4
+    depth, lane = rows_ref.shape[1] // 4, audio_ref.shape[1] // 4
     for at, packed_ref in enumerate(packed_refs):
         slot, mem = divmod(at, 2)
         for part in range(2):
             shard = 2 * (mem_at ^ mem) + part
-            rows_ref[shard, slot * rows : (slot + 1) * rows, :] = packed_ref[
+            lanes = pl.ds(pl.multiple_of(shard * depth, depth), depth)
+            rows_ref[slot * rows : (slot + 1) * rows, lanes] = packed_ref[
                 part * rows : (part + 1) * rows, :
             ]
-            audio_ref[shard, slot * audio_rows : (slot + 1) * audio_rows, :] = packed_ref[
+            lanes = pl.ds(pl.multiple_of(shard * lane, lane), lane)
+            audio_ref[slot * audio_rows : (slot + 1) * audio_rows, lanes] = packed_ref[
                 2 * rows :, part * lane : (part + 1) * lane
             ]
-    kv_half = kv_ref.shape[1] // 2
-    fold = query_ref.shape[1] // 4
-    width = query_ref.shape[2]
+    kv_half, fold = depth // 2, lane // 4
+    width = query_ref.shape[1]
 
     def place(piece_ref, shard, group, kv_at, query_at):
-        to = pl.ds(pl.multiple_of(group * kv_half, kv_half), kv_half)
-        kv_ref[shard, to, :] = piece_ref[kv_at : kv_at + kv_half, :]
+        to = pl.ds(pl.multiple_of((2 * shard + group) * kv_half, kv_half), kv_half)
+        kv_ref[to, :] = piece_ref[kv_at : kv_at + kv_half, :]
         for side in range(2):
-            to = pl.ds(pl.multiple_of((2 * group + side) * fold, fold), fold)
-            query_ref[shard, to, :] = piece_ref[
+            to = pl.ds(pl.multiple_of((4 * shard + 2 * group + side) * fold, fold), fold)
+            query_ref[to, :] = piece_ref[
                 query_at : query_at + fold, side * width : (side + 1) * width
             ]
 
@@ -311,20 +312,12 @@
         place(weight_refs[2 * bit - 1], seq_at ^ bit, grp_at, 0, kv_half)
         place(weight_refs[2 * bit], seq_at ^ bit, 1 - grp_at, 0, kv_half)
 
-    def summed(left_ref, right_ref):
-        total = jnp.dot(left_ref[0], right_ref[0], preferred_element_type=jnp.float32)
-        for shard in range(1, 4):
-            total += jnp.dot(
-                left_ref[shard], right_ref[shard], preferred_element_type=jnp.float32
-            )
-        return total
-
     count = 4 * rows
     columns = keep_ref.shape[1]
-    total = summed(rows_ref, kv_ref)
+    total = jnp.dot(rows_ref[...], kv_ref[...], preferred_element_type=jnp.float32)
     keep_ref[:count, :] = total[:, :columns]
     send_ref[:count, :] = total[:, columns:]
-    total = summed(audio_ref, query_ref)
+    total = jnp.dot(audio_ref[...], query_ref[...], preferred_element_type=jnp.float32)
     folded = 2 * audio_rows
     for side in range(2):
         at = slice(side * folded, (side + 1) * folded)
@@ -449,6 +442,7 @@
         ],
         smem=(1,),
         loose_in=(2, 3, 4, 5, 6),
+        limit=61,
     )
 
     other = swap(other, "rep", 1)
@@ -458,10 +452,7 @@
         [bfloat(2 * rows, 2 * width)] + [bfloat(rows, 2 * width)] * 3,
         [jnp.stack([seq_at, rep_at, grp_at]), kv_weight, query_weight, other],
     )
-    weights = [weight_own]
-    for bit, piece in enumerate(pieces, 1):
-        piece = swap(piece, "seq", bit)
-        weights += [piece, swap(piece, "grp", 1)]
+    pieces = [swap(piece, "seq", bit) for bit, piece in enumerate(pieces, 1)]
 
     inner, outward = [(1, 2), (2, 1)], [(1, 0), (2, 3)]
     is_inner = (seq_at == 1) | (seq_at == 2)
@@ -470,14 +461,30 @@
         jnp.broadcast_to(alignment[None], (seq_size, audio_rows)), "seq", 0, 0, tiled=True
     ).astype(jnp.float32)
     inner_own = lax.ppermute(packed, "seq", inner)
+    partner, inner_own, align_all, weight_own = lax.optimization_barrier(
+        (partner, inner_own, align_all, weight_own)
+    )
+    out_partner = swap(half, "seq", 1)
     inner_partner = lax.ppermute(partner, "seq", inner)
     third = jnp.where(is_inner, inner_own, lax.ppermute(inner_own, "seq", outward))
+    third, pieces[0], out_partner = lax.optimization_barrier((third, pieces[0], out_partner))
     fourth = jnp.where(is_inner, inner_partner, lax.ppermute(inner_partner, "seq", outward))
+    out_pair = lax.ppermute(jnp.stack([half, out_partner]), "seq", inner)
+    fourth, pieces[1], pieces[2], out_pair = lax.optimization_barrier(
+        (fourth, pieces[1], pieces[2], out_pair)
+    )
+    weights = [weight_own]
+    for piece in pieces:
+        weights += [piece, swap(piece, "grp", 1)]
     tokens = []
     for value in (packed, partner, third, fourth):
         tokens += [value, swap(value, "mem", 1)]
     middle = 2 - seq_at // 2
     blocks = jnp.stack([seq_at, seq_at ^ 1, middle, middle ^ 1])
+
+    partner_rest = swap(out_partner, "grp", 1)
+    far = jnp.where(is_inner, out_pair, lax.ppermute(out_pair, "seq", outward))
+    far_rest = swap(far, "grp", 1)
 
     rows = seq_size * (video_rows + audio_rows // 2)
     sums = jax.ShapeDtypeStruct((rows, width), jnp.float32)
@@ -486,20 +493,15 @@
         [sums, sums],
         [jnp.stack([seq_at, mem_at, grp_at]), *tokens, *weights],
         scratch=[
-            pltpu.VMEM((4, seq_size * video_rows, half_depth), jnp.bfloat16),
-            pltpu.VMEM((4, seq_size * audio_rows, 2 * query_quarter), jnp.bfloat16),
-            pltpu.VMEM((4, half_depth, 2 * width), jnp.bfloat16),
-            pltpu.VMEM((4, 2 * query_quarter, width), jnp.bfloat16),
-        ],
+            pltpu.VMEM((seq_size * video_rows, 4 * half_depth), jnp.bfloat16),
+            pltpu.VMEM((seq_size * audio_rows, 8 * query_quarter), jnp.bfloat16),
+            pltpu.VMEM((4 * half_depth, 2 * width), jnp.bfloat16),
+            pltpu.VMEM((8 * query_quarter, width), jnp.bfloat16),
+        ],
+        after=(far, partner_rest),
         limit=26,
     )
     came = swap(send, "rep", 1)
-
-    half, _ = lax.optimization_barrier((half, third))
-    out_partner = swap(half, "seq", 1)
-    out_pair = lax.ppermute(jnp.stack([half, out_partner]), "seq", inner)
-    far = jnp.where(is_inner, out_pair, lax.ppermute(out_pair, "seq", outward))
-    partner_rest, far_rest = swap(out_partner, "grp", 1), swap(far, "grp", 1)
 
     span = video_rows * seq_size
     positions = blocks[:, None] * video_rows + jnp.arange(video_rows, dtype=jnp.int32)[None, :]

time: 155 us -> 186 us (1.20)
  waiting for transfers between devices: 70.8 us -> 100 us
  starting transfers between devices: 52 us -> 58.4 us
  local copies, waits for them, and re-layouts: 8.21 us -> 2.59 us
  Pallas kernels: 16.8 us -> 18.9 us
    ppermute x21, waiting for transfers between devices: 58.8 us -> 84.4 us  [swap(): return lax.ppermute(value, axis, [(i, i ^ bit) for i in range(size)])]
    all_to_all x1, waiting for transfers between devices: 1.94 us -> 12.8 us  [by_head(): lax.all_to_all(jnp.broadcast_to(alignment[None], (seq_size, audio_rows)),...]
    ppermute x1, waiting for transfers between devices: 10.1 us -> 0.01 us  [by_head(): lax.ppermute(inner_partner, 'seq', outward)]
    ppermute x21, starting transfers between devices: 40.5 us -> 46.8 us  [swap(): return lax.ppermute(value, axis, [(i, i ^ bit) for i in range(size)])]
    unnamed x26 -> x23, local copies, waits for them, and re-layouts: 7.25 us -> 1.6 us
    pallas_call x5, Pallas kernels: 15 us -> 17.1 us  [kernel_call(): pl.pallas_call(whole, out_shape=outs, in_specs=[SMEM, *spots] + [ANY] * l...]
  transfers between devices with their start and end apart: 28 -> 28, of which waited for: 10 -> 13; matrix products, arithmetic and copies ran while one was open for 4% -> 2% of each run, Pallas kernels for 7% -> 4%
where the time goes in v3:
time: 186 us; the launch traced here: 185 us
  waiting for transfers between devices  100 us (54%)
  starting transfers between devices  58.4 us (31%)
  Pallas kernels  18.9 us (10%)
  other arithmetic  4.23 us (2%)
  local copies, waits for them, and re-layouts  2.59 us (1%)
    ppermute x21, waiting for transfers between devices, swap(): return lax.ppermute(value, axis, [(i, i ^ bit) for i in range(size)])  84.4 us
    ppermute x21, starting transfers between devices, swap(): return lax.ppermute(value, axis, [(i, i ^ bit) for i in range(size)])  46.8 us
    pallas_call x5, Pallas kernels, kernel_call(): pl.pallas_call(whole, out_shape=outs, in_specs=[SMEM, *spots] + [ANY] * l...  17.1 us
    all_to_all x1, waiting for transfers between devices, by_head(): lax.all_to_all(jnp.broadcast_to(alignment[None], (seq_size, audio_rows)),...  12.8 us
    all_to_all x1, starting transfers between devices, by_head(): lax.all_to_all(jnp.broadcast_to(alignment[None], (seq_size, audio_rows)),...  4.85 us
  transfers between devices with their start and end apart: 28, of which 13 were waited for; matrix products, arithmetic and copies ran while one was open for 2% of the time, Pallas kernels for 4%

profile of v3, /device:TPU:0, one launch (start us, length us, event | category | flops | bytes accessed | tf_op | source)
XLA Modules:
  0.0 185.0 jit_solution(8584604008113836076)
XLA Ops:
  0.6 0.7 add_add_fusion.refs_0_
  1.3 4.2 %shard_map.87 = (bf16[640,512]{1,0:T(8,128)(2,1)}, bf16[640,1024]{1,0:T(8,128)(2,1)}, bf16[256,512]{1,0:T(8,128)(2,1)}) custom-call(s32[3]{0:T(128)} %add_add_fusion.refs_0_, s32[8]{0:T(128)} %refs_1_.2, bf16[3,192,2048]{2,1,0:T(8,128)(2,1)} %refs_2_.2, bf16[256,2048]{1,0:T(8,128)(2,1)} %refs_3_.1, bf16[1024,1024]{1,0:T(8,128)(2,1)} %refs_1_.3, ...), custom_call_target="tpu_custom_call" | custom-call | tf_op jit(solution)/shard_map/pallas_call | solution.py:132
  6.0 2.7 %collective-permute-start = (bf16[640,512]{1,0:T(8,128)(2,1)}, bf16[640,512]{1,0:T(8,128)(2,1)}, u32[]{:S(2)}, u32[]{:S(2)}) collective-permute-start(bf16[640,512]{1,0:T(8,128)(2,1)} %get-tuple-element.30.refs_1_), channel_id=1, source_target_pairs={{0,4},{4,0},{8,12},{12,8},{1,5},{5,1},{9,13},{13,9},{2,6},{6,2},{1... | collective-permute-start | bytes 1966088 | tf_op jit(solution)/shard_map/ppermute | solution.py:116
  8.7 1.5 collective-permute-start.1
  10.2 0.6 broadcast_in_dim.4
  10.8 4.8 %all-to-all-start = ((s32[4,1,256]{2,1,0:T(1,128)}), s32[4,1,256]{2,1,0:T(1,128)S(1)}, u32[]{:S(2)}, u32[]{:S(2)}) async-start(s32[4,1,256]{2,1,0:T(1,128)} %broadcast_in_dim.4), calls=%async_computation | async-start | bytes 8192 | tf_op jit(solution)/shard_map/all_to_all | solution.py:460
  15.7 12.8 %all-to-all-done = s32[4,1,256]{2,1,0:T(1,128)S(1)} async-done(((s32[4,1,256]{2,1,0:T(1,128)}), s32[4,1,256]{2,1,0:T(1,128)S(1)}, u32[]{:S(2)}, u32[]{:S(2)}) %all-to-all-start) | async-done | bytes 4128 | tf_op jit(solution)/shard_map/all_to_all | solution.py:460
  28.6 2.3 %shard_map.88 = (bf16[640,512]{1,0:T(8,128)(2,1)S(1)}, bf16[320,512]{1,0:T(8,128)(2,1)}, bf16[320,512]{1,0:T(8,128)(2,1)S(1)}, bf16[320,512]{1,0:T(8,128)(2,1)S(1)}) custom-call(s32[3]{0:T(128)S(1)} %add_add_fusion.1.refs_0_, bf16[1024,1024]{1,0:T(8,128)(2,1)S(1)} %copy-done.1, bf16[512,512]{1,0:T(8,128)(2,1)S(1)} %copy-done.2, ...), custom_call_target="tpu_custom_call" | custom-call | tf_op jit(solution)/shard_map/pallas_call | solution.py:132
  30.9 0.8 copy-done.5
  31.7 0.7 copy-done.8
  32.4 0.7 collective-permute-start.9
  33.1 1.3 collective-permute-start.5
  34.4 3.7 %collective-permute-start.6 = (bf16[320,512]{1,0:T(8,128)(2,1)}, bf16[320,512]{1,0:T(8,128)(2,1)S(1)}, u32[]{:S(2)}, u32[]{:S(2)}) collective-permute-start(bf16[320,512]{1,0:T(8,128)(2,1)} %get-tuple-element.36), channel_id=1, source_target_pairs={{0,4},{4,0},{8,12},{12,8},{1,5},{5,1},{9,13},{13,9},{2,6},{6,2},{1... | collective-permute-start | bytes 983048 | tf_op jit(solution)/shard_map/ppermute | solution.py:116
  38.1 1.3 collective-permute-start.10
  39.4 13.4 %collective-permute-start.7 = (bf16[256,512]{1,0:T(8,128)(2,1)}, bf16[256,512]{1,0:T(8,128)(2,1)S(1)}, u32[]{:S(2)}, u32[]{:S(2)}) collective-permute-start(bf16[256,512]{1,0:T(8,128)(2,1)} %get-tuple-element.37), channel_id=1, source_target_pairs={{0,4},{4,0},{8,12},{12,8},{1,5},{5,1},{9,13},{13,9},{2,6},{6,2},{1... | collective-permute-start | bytes 786440 | tf_op jit(solution)/shard_map/ppermute | solution.py:116
  52.9 1.0 collective-permute-done.5
  53.9 24.9 %collective-permute-done.7.refs_6_ = bf16[256,512]{1,0:T(8,128)(2,1)S(1)} collective-permute-done((bf16[256,512]{1,0:T(8,128)(2,1)}, bf16[256,512]{1,0:T(8,128)(2,1)S(1)}, u32[]{:S(2)}, u32[]{:S(2)}) %collective-permute-start.7) | collective-permute-done | bytes 262176 | tf_op jit(solution)/shard_map/ppermute | solution.py:116
  78.8 1.0 pad_maximum_fusion
  79.8 0.7 collective-permute-start.13
  80.5 1.6 collective-permute-start.3
  82.1 2.3 %collective-permute-start.11 = (bf16[320,512]{1,0:T(8,128)(2,1)S(1)}, bf16[320,512]{1,0:T(8,128)(2,1)S(1)}, u32[]{:S(2)}, u32[]{:S(2)}) collective-permute-start(bf16[320,512]{1,0:T(8,128)(2,1)S(1)} %copy-done.9), channel_id=1, source_target_pairs={{0,8},{4,12},{8,0},{12,4},{1,9},{5,13},{9,1},{13,5},{2,10},{6,14},... | collective-permute-start | bytes 983048 | tf_op jit(solution)/shard_map/ppermute | solution.py:116
  84.4 1.5 collective-permute-start.12
  86.6 30.1 %collective-permute-done.11.refs_12_ = bf16[320,512]{1,0:T(8,128)(2,1)S(1)} collective-permute-done((bf16[320,512]{1,0:T(8,128)(2,1)S(1)}, bf16[320,512]{1,0:T(8,128)(2,1)S(1)}, u32[]{:S(2)}, u32[]{:S(2)}) %collective-permute-start.11) | collective-permute-done | bytes 327712 | tf_op jit(solution)/shard_map/ppermute | solution.py:116
  116.7 1.3 collective-permute-start.18
  117.9 0.6 collective-permute-start.8
  118.5 1.5 collective-permute-start.14
  120.0 1.5 collective-permute-start.19
  122.1 7.2 %collective-permute-done.19.refs_17_.refs_7_ = bf16[256,512]{1,0:T(8,128)(2,1)S(1)} collective-permute-done((bf16[256,512]{1,0:T(8,128)(2,1)S(1)}, bf16[256,512]{1,0:T(8,128)(2,1)S(1)}, u32[]{:S(2)}, u32[]{:S(2)}) %collective-permute-start.19) | collective-permute-done | bytes 262176 | tf_op jit(solution)/shard_map/ppermute | solution.py:116
  129.3 1.5 collective-permute-start.16
  130.8 1.8 collective-permute-done.18
  132.6 1.5 collective-permute-start.17
  134.3 1.6 collective-permute-done.15.refs_11_
  135.9 5.2 %collective-permute-done.16.refs_13_ = bf16[320,512]{1,0:T(8,128)(2,1)S(1)} collective-permute-done((bf16[320,512]{1,0:T(8,128)(2,1)S(1)}, bf16[320,512]{1,0:T(8,128)(2,1)S(1)}, u32[]{:S(2)}, u32[]{:S(2)}) %collective-permute-start.16) | collective-permute-done | bytes 327712 | tf_op jit(solution)/shard_map/ppermute | solution.py:116
  141.1 3.5 %collective-permute-done.17.refs_15_ = bf16[320,512]{1,0:T(8,128)(2,1)S(1)} collective-permute-done((bf16[320,512]{1,0:T(8,128)(2,1)S(1)}, bf16[320,512]{1,0:T(8,128)(2,1)S(1)}, u32[]{:S(2)}, u32[]{:S(2)}) %collective-permute-start.17) | collective-permute-done | bytes 327712 | tf_op jit(solution)/shard_map/ppermute | solution.py:116
  144.6 5.1 %shard_map.89 = (f32[1280,256]{1,0:T(8,128)}, f32[1280,256]{1,0:T(8,128)S(1)}) custom-call(s32[3]{0:T(128)S(1)} %add_add_fusion.2.refs_0_, bf16[640,512]{1,0:T(8,128)(2,1)S(1)} %copy-done.4, bf16[640,512]{1,0:T(8,128)(2,1)S(1)} %collective-permute-done.3.refs_2_, bf16[640,512]{1,0:T(8,128)(2,1)} %collective-permute-done.refs_3_, ...), custom_call_target="tpu_custom_call" | custom-call | tf_op jit(solution)/shard_map/pallas_call | solution.py:132
  149.9 1.5 collective-permute-start.24
  151.9 1.2 collective-permute-done.20.refs_4_
  153.1 3.5 %shard_map.90 = (bf16[256,128]{1,0:T(8,128)(2,1)S(1)}, bf16[256,128]{1,0:T(8,128)(2,1)S(1)}, bf16[256,128]{1,0:T(8,128)(2,1)S(1)}, bf16[256,128]{1,0:T(8,128)(2,1)S(1)}) custom-call(s32[4]{0:T(128)S(1)} %get-tuple-element.59.refs_0_, f32[1,768]{1,0:T(1,128)S(1)} %fusion.3.refs_1_, f32[4,256,1]{2,1,0:T(8,128)S(1)} %copy.10.refs_2_, ...), custom_call_target="tpu_custom_call" | custom-call | tf_op jit(solution)/shard_map/pallas_call | solution.py:132
  156.6 7.7 %collective-permute-start.21 = (bf16[256,128]{1,0:T(8,128)(2,1)S(1)}, bf16[256,128]{1,0:T(8,128)(2,1)S(1)}, u32[]{:S(2)}, u32[]{:S(2)}) collective-permute-start(bf16[256,128]{1,0:T(8,128)(2,1)S(1)} %get-tuple-element.51), channel_id=1, source_target_pairs={{0,4},{4,0},{8,12},{12,8},{1,5},{5,1},{9,13},{13,9},{2,6},{6,2},{1... | collective-permute-start | bytes 196616 | tf_op jit(solution)/shard_map/ppermute | solution.py:116
  164.2 2.4 %collective-permute-start.23 = (bf16[256,128]{1,0:T(8,128)(2,1)S(1)}, bf16[256,128]{1,0:T(8,128)(2,1)S(1)}, u32[]{:S(2)}, u32[]{:S(2)}) collective-permute-start(bf16[256,128]{1,0:T(8,128)(2,1)S(1)} %get-tuple-element.53), channel_id=1, source_target_pairs={{0,12},{4,8},{8,4},{12,0},{1,13},{5,9},{9,5},{13,1},{2,14},{6,10},... | collective-permute-start | bytes 196616 | tf_op jit(solution)/shard_map/ppermute | solution.py:116
  166.8 5.0 %collective-permute-done.22.refs_3_ = bf16[256,128]{1,0:T(8,128)(2,1)S(1)} collective-permute-done((bf16[256,128]{1,0:T(8,128)(2,1)S(1)}, bf16[256,128]{1,0:T(8,128)(2,1)S(1)}, u32[]{:S(2)}, u32[]{:S(2)}) %collective-permute-start.22) | collective-permute-done | bytes 65568 | tf_op jit(solution)/shard_map/ppermute | solution.py:116
  171.7 2.0 %shard_map.91 = (bf16[2,256,512]{2,1,0:T(8,128)(2,1)S(1)}, f32[2,256,512]{2,1,0:T(8,128)S(1)}) custom-call(s32[3]{0:T(128)S(1)} %pad_add_fusion.refs_0_, bf16[256,128]{1,0:T(8,128)(2,1)S(1)} %get-tuple-element.50.refs_1_, bf16[256,128]{1,0:T(8,128)(2,1)S(1)} %collective-permute-done.21.refs_2_, bf16[256,128]{1,0:T(8,128)(2,1)S(1)} %collective-permute-done.22.refs_3_, ...), custom_call_target="tpu_custom_call" | custom-call | tf_op jit(solution)/shard_map/pallas_call | solution.py:132
  173.9 1.9 %collective-permute-done.25 = bf16[2,256,512]{2,1,0:T(8,128)(2,1)S(1)} collective-permute-done((bf16[2,256,512]{2,1,0:T(8,128)(2,1)S(1)}, bf16[2,256,512]{2,1,0:T(8,128)(2,1)S(1)}, u32[]{:S(2)}, u32[]{:S(2)}) %collective-permute-start.25) | collective-permute-done | bytes 524320 | tf_op jit(solution)/shard_map/ppermute | solution.py:116
  175.8 1.7 collective-permute-start.26
  177.6 1.8 shard_map.86
  179.4 1.0 bitcast_add_fusion
  180.4 3.8 %collective-permute-done.26 = bf16[256,512]{1,0:T(8,128)(2,1)S(1)} collective-permute-done((bf16[256,512]{1,0:T(8,128)(2,1)S(1)}, bf16[256,512]{1,0:T(8,128)(2,1)S(1)}, u32[]{:S(2)}, u32[]{:S(2)}) %collective-permute-start.26) | collective-permute-done | bytes 262176 | tf_op jit(solution)/shard_map/ppermute | solution.py:116
  184.2 0.8 add_convert_fusion
  (57 shorter events, 2.9 us)
Async XLA Ops:
  1.3 8.9 %copy-start.10 = (s32[256]{0:T(256)S(1)}, s32[256]{0:T(256)}, u32[]{:S(2)}) copy-start(s32[256]{0:T(256)} %param.9) | copy-start | bytes 3076
  1.3 27.2 %copy-start.1 = (bf16[1024,1024]{1,0:T(8,128)(2,1)S(1)}, bf16[1024,1024]{1,0:T(8,128)(2,1)}, u32[]{:S(2)}) copy-start(bf16[1024,1024]{1,0:T(8,128)(2,1)} %refs_1_.3) | copy-start | bytes 6291460
  1.3 27.2 %copy-start.2 = (bf16[512,512]{1,0:T(8,128)(2,1)S(1)}, bf16[512,512]{1,0:T(8,128)(2,1)}, u32[]{:S(2)}) copy-start(bf16[512,512]{1,0:T(8,128)(2,1)} %refs_2_.3) | copy-start | bytes 1572868
  5.5 23.0 %collective-permute-start.2 = (bf16[640,1024]{1,0:T(8,128)(2,1)}, bf16[640,1024]{1,0:T(8,128)(2,1)}, u32[]{:S(2)}, u32[]{:S(2)}) collective-permute-start(bf16[640,1024]{1,0:T(8,128)(2,1)} %get-tuple-element.31), channel_id=1, source_target_pairs={{0,1},{1,0},{2,3},{3,2},{4,5},{5,4},{6,7},{7,6},{8,9},{9,8},{10,11... | collective-permute-start | bytes 3932168 | tf_op jit(solution)/shard_map/ppermute | solution.py:116
  6.0 26.4 %collective-permute-start = (bf16[640,512]{1,0:T(8,128)(2,1)}, bf16[640,512]{1,0:T(8,128)(2,1)}, u32[]{:S(2)}, u32[]{:S(2)}) collective-permute-start(bf16[640,512]{1,0:T(8,128)(2,1)} %get-tuple-element.30.refs_1_), channel_id=1, source_target_pairs={{0,4},{4,0},{8,12},{12,8},{1,5},{5,1},{9,13},{13,9},{2,6},{6,2},{1... | collective-permute-start | bytes 1966088 | tf_op jit(solution)/shard_map/ppermute | solution.py:116
  8.7 23.7 %collective-permute-start.1 = (bf16[640,512]{1,0:T(8,128)(2,1)}, bf16[640,512]{1,0:T(8,128)(2,1)}, u32[]{:S(2)}, u32[]{:S(2)}) collective-permute-start(bf16[640,512]{1,0:T(8,128)(2,1)} %get-tuple-element.30.refs_1_), channel_id=1, source_target_pairs={{4,8},{8,4},{5,9},{9,5},{6,10},{10,6},{7,11},{11,7},{20,24},{24,20... | collective-permute-start | bytes 1966088 | tf_op jit(solution)/shard_map/ppermute | solution.py:463
  10.8 17.7 %all-to-all-start = ((s32[4,1,256]{2,1,0:T(1,128)}), s32[4,1,256]{2,1,0:T(1,128)S(1)}, u32[]{:S(2)}, u32[]{:S(2)}) async-start(s32[4,1,256]{2,1,0:T(1,128)} %broadcast_in_dim.4), calls=%async_computation | async-start | bytes 8192 | tf_op jit(solution)/shard_map/all_to_all | solution.py:460
  30.9 0.8 copy-start.5
  31.7 0.7 copy-start.8
  32.4 5.7 %collective-permute-start.9 = (bf16[640,512]{1,0:T(8,128)(2,1)}, bf16[640,512]{1,0:T(8,128)(2,1)S(1)}, u32[]{:S(2)}, u32[]{:S(2)}) collective-permute-start(bf16[640,512]{1,0:T(8,128)(2,1)} %collective-permute-done.refs_3_), channel_id=1, source_target_pairs={{4,8},{8,4},{5,9},{9,5},{6,10},{10,6},{7,11},{11,7},{20,24},{24,20... | collective-permute-start | bytes 1966088 | tf_op jit(solution)/shard_map/ppermute | solution.py:468
  33.1 20.7 %collective-permute-start.5 = (bf16[640,512]{1,0:T(8,128)(2,1)}, bf16[640,512]{1,0:T(8,128)(2,1)S(1)}, u32[]{:S(2)}, u32[]{:S(2)}) collective-permute-start(bf16[640,512]{1,0:T(8,128)(2,1)} %collective-permute-done.1), channel_id=1, source_target_pairs={{4,0},{8,12},{5,1},{9,13},{6,2},{10,14},{7,3},{11,15},{20,16},{24,... | collective-permute-start | bytes 1966088 | tf_op jit(solution)/shard_map/ppermute | solution.py:469
  34.4 44.4 %collective-permute-start.6 = (bf16[320,512]{1,0:T(8,128)(2,1)}, bf16[320,512]{1,0:T(8,128)(2,1)S(1)}, u32[]{:S(2)}, u32[]{:S(2)}) collective-permute-start(bf16[320,512]{1,0:T(8,128)(2,1)} %get-tuple-element.36), channel_id=1, source_target_pairs={{0,4},{4,0},{8,12},{12,8},{1,5},{5,1},{9,13},{13,9},{2,6},{6,2},{1... | collective-permute-start | bytes 983048 | tf_op jit(solution)/shard_map/ppermute | solution.py:116
  38.1 47.8 %collective-permute-start.10 = (bf16[640,512]{1,0:T(8,128)(2,1)S(1)}, bf16[640,512]{1,0:T(8,128)(2,1)S(1)}, u32[]{:S(2)}, u32[]{:S(2)}) collective-permute-start(bf16[640,512]{1,0:T(8,128)(2,1)S(1)} %collective-permute-done.9), channel_id=1, source_target_pairs={{4,0},{8,12},{5,1},{9,13},{6,2},{10,14},{7,3},{11,15},{20,16},{24,... | collective-permute-start | bytes 1966088 | tf_op jit(solution)/shard_map/ppermute | solution.py:471
  39.4 39.4 %collective-permute-start.7 = (bf16[256,512]{1,0:T(8,128)(2,1)}, bf16[256,512]{1,0:T(8,128)(2,1)S(1)}, u32[]{:S(2)}, u32[]{:S(2)}) collective-permute-start(bf16[256,512]{1,0:T(8,128)(2,1)} %get-tuple-element.37), channel_id=1, source_target_pairs={{0,4},{4,0},{8,12},{12,8},{1,5},{5,1},{9,13},{13,9},{2,6},{6,2},{1... | collective-permute-start | bytes 786440 | tf_op jit(solution)/shard_map/ppermute | solution.py:116
  52.8 27.7 %copy-start.4 = (bf16[640,512]{1,0:T(8,128)(2,1)S(1)}, bf16[640,512]{1,0:T(8,128)(2,1)}, u32[]{:S(2)}) copy-start(bf16[640,512]{1,0:T(8,128)(2,1)} %get-tuple-element.30.refs_1_) | copy-start | bytes 1966084
  52.9 29.2 %copy-start.9 = (bf16[320,512]{1,0:T(8,128)(2,1)S(1)}, bf16[320,512]{1,0:T(8,128)(2,1)}, u32[]{:S(2)}) copy-start(bf16[320,512]{1,0:T(8,128)(2,1)} %copy-done.8) | copy-start | bytes 983044
  79.8 36.8 %collective-permute-start.13 = (bf16[2,256,512]{2,1,0:T(8,128)(2,1)S(1)}, bf16[2,256,512]{2,1,0:T(8,128)(2,1)S(1)}, u32[]{:S(2)}, u32[]{:S(2)}) collective-permute-start(bf16[2,256,512]{2,1,0:T(8,128)(2,1)S(1)} %pad_maximum_fusion), channel_id=1, source_target_pairs={{4,8},{8,4},{5,9},{9,5},{6,10},{10,6},{7,11},{11,7},{20,24},{24,20... | collective-permute-start | bytes 1572872 | tf_op jit(solution)/shard_map/ppermute | solution.py:472
  80.5 39.5 %collective-permute-start.3 = (bf16[640,512]{1,0:T(8,128)(2,1)S(1)}, bf16[640,512]{1,0:T(8,128)(2,1)S(1)}, u32[]{:S(2)}, u32[]{:S(2)}) collective-permute-start(bf16[640,512]{1,0:T(8,128)(2,1)S(1)} %copy-done.4), channel_id=1, source_target_pairs={{0,2},{2,0},{1,3},{3,1},{4,6},{6,4},{5,7},{7,5},{8,10},{10,8},{9,1... | collective-permute-start | bytes 1966088 | tf_op jit(solution)/shard_map/ppermute | solution.py:116
  82.1 34.5 %collective-permute-start.11 = (bf16[320,512]{1,0:T(8,128)(2,1)S(1)}, bf16[320,512]{1,0:T(8,128)(2,1)S(1)}, u32[]{:S(2)}, u32[]{:S(2)}) collective-permute-start(bf16[320,512]{1,0:T(8,128)(2,1)S(1)} %copy-done.9), channel_id=1, source_target_pairs={{0,8},{4,12},{8,0},{12,4},{1,9},{5,13},{9,1},{13,5},{2,10},{6,14},... | collective-permute-start | bytes 983048 | tf_op jit(solution)/shard_map/ppermute | solution.py:116
  84.4 60.2 %copy-start.6 = (bf16[640,512]{1,0:T(8,128)(2,1)S(1)}, bf16[640,512]{1,0:T(8,128)(2,1)}, u32[]{:S(2)}) copy-start(bf16[640,512]{1,0:T(8,128)(2,1)} %copy-done.5) | copy-start | bytes 1966084
  84.4 32.2 %collective-permute-start.12 = (bf16[320,512]{1,0:T(8,128)(2,1)S(1)}, bf16[320,512]{1,0:T(8,128)(2,1)S(1)}, u32[]{:S(2)}, u32[]{:S(2)}) collective-permute-start(bf16[320,512]{1,0:T(8,128)(2,1)S(1)} %get-tuple-element.40), channel_id=1, source_target_pairs={{0,12},{4,8},{8,4},{12,0},{1,13},{5,9},{9,5},{13,1},{2,14},{6,10},... | collective-permute-start | bytes 983048 | tf_op jit(solution)/shard_map/ppermute | solution.py:116
  86.0 35.6 %collective-permute-start.4 = (bf16[640,512]{1,0:T(8,128)(2,1)}, bf16[640,512]{1,0:T(8,128)(2,1)S(1)}, u32[]{:S(2)}, u32[]{:S(2)}) collective-permute-start(bf16[640,512]{1,0:T(8,128)(2,1)} %collective-permute-done.refs_3_), channel_id=1, source_target_pairs={{0,2},{2,0},{1,3},{3,1},{4,6},{6,4},{5,7},{7,5},{8,10},{10,8},{9,1... | collective-permute-start | bytes 1966088 | tf_op jit(solution)/shard_map/ppermute | solution.py:116
  116.7 16.0 %collective-permute-start.18 = (bf16[2,256,512]{2,1,0:T(8,128)(2,1)S(1)}, bf16[2,256,512]{2,1,0:T(8,128)(2,1)S(1)}, u32[]{:S(2)}, u32[]{:S(2)}) collective-permute-start(bf16[2,256,512]{2,1,0:T(8,128)(2,1)S(1)} %collective-permute-done.13), channel_id=1, source_target_pairs={{4,0},{8,12},{5,1},{9,13},{6,2},{10,14},{7,3},{11,15},{20,16},{24,... | collective-permute-start | bytes 1572872 | tf_op jit(solution)/shard_map/ppermute | solution.py:486
  117.9 17.9 %collective-permute-start.8 = (bf16[640,512]{1,0:T(8,128)(2,1)S(1)}, bf16[640,512]{1,0:T(8,128)(2,1)S(1)}, u32[]{:S(2)}, u32[]{:S(2)}) collective-permute-start(bf16[640,512]{1,0:T(8,128)(2,1)S(1)} %broadcast_select_fusion.1.refs_5_), channel_id=1, source_target_pairs={{0,2},{2,0},{1,3},{3,1},{4,6},{6,4},{5,7},{7,5},{8,10},{10,8},{9,1... | collective-permute-start | bytes 1966088 | tf_op jit(solution)/shard_map/ppermute | solution.py:116
  118.5 26.0 %collective-permute-start.14 = (bf16[640,512]{1,0:T(8,128)(2,1)S(1)}, bf16[640,512]{1,0:T(8,128)(2,1)S(1)}, u32[]{:S(2)}, u32[]{:S(2)}) collective-permute-start(bf16[640,512]{1,0:T(8,128)(2,1)S(1)} %broadcast_select_fusion.refs_7_), channel_id=1, source_target_pairs={{0,2},{2,0},{1,3},{3,1},{4,6},{6,4},{5,7},{7,5},{8,10},{10,8},{9,1... | collective-permute-start | bytes 1966088 | tf_op jit(solution)/shard_map/ppermute | solution.py:116
  120.0 9.2 %collective-permute-start.19 = (bf16[256,512]{1,0:T(8,128)(2,1)S(1)}, bf16[256,512]{1,0:T(8,128)(2,1)S(1)}, u32[]{:S(2)}, u32[]{:S(2)}) collective-permute-start(bf16[256,512]{1,0:T(8,128)(2,1)S(1)} %collective-permute-done.7.refs_6_), channel_id=1, source_target_pairs={{0,16},{16,0},{1,17},{17,1},{2,18},{18,2},{3,19},{19,3},{4,20},{20... | collective-permute-start | bytes 786440 | tf_op jit(solution)/shard_map/ppermute | solution.py:116
  121.6 14.3 %collective-permute-start.15 = (bf16[320,512]{1,0:T(8,128)(2,1)S(1)}, bf16[320,512]{1,0:T(8,128)(2,1)S(1)}, u32[]{:S(2)}, u32[]{:S(2)}) collective-permute-start(bf16[320,512]{1,0:T(8,128)(2,1)S(1)} %collective-permute-done.6.refs_10_), channel_id=1, source_target_pairs={{0,16},{16,0},{1,17},{17,1},{2,18},{18,2},{3,19},{19,3},{4,20},{20... | collective-permute-start | bytes 983048 | tf_op jit(solution)/shard_map/ppermute | solution.py:116
  129.3 11.8 %collective-permute-start.16 = (bf16[320,512]{1,0:T(8,128)(2,1)S(1)}, bf16[320,512]{1,0:T(8,128)(2,1)S(1)}, u32[]{:S(2)}, u32[]{:S(2)}) collective-permute-start(bf16[320,512]{1,0:T(8,128)(2,1)S(1)} %collective-permute-done.11.refs_12_), channel_id=1, source_target_pairs={{0,16},{16,0},{1,17},{17,1},{2,18},{18,2},{3,19},{19,3},{4,20},{20... | collective-permute-start | bytes 983048 | tf_op jit(solution)/shard_map/ppermute | solution.py:116
  132.6 11.9 %collective-permute-start.17 = (bf16[320,512]{1,0:T(8,128)(2,1)S(1)}, bf16[320,512]{1,0:T(8,128)(2,1)S(1)}, u32[]{:S(2)}, u32[]{:S(2)}) collective-permute-start(bf16[320,512]{1,0:T(8,128)(2,1)S(1)} %collective-permute-done.12.refs_14_), channel_id=1, source_target_pairs={{0,16},{16,0},{1,17},{17,1},{2,18},{18,2},{3,19},{19,3},{4,20},{20... | collective-permute-start | bytes 983048 | tf_op jit(solution)/shard_map/ppermute | solution.py:116
  149.7 3.4 %collective-permute-start.20 = (f32[1280,256]{1,0:T(8,128)}, f32[1280,256]{1,0:T(8,128)}, u32[]{:S(2)}, u32[]{:S(2)}) collective-permute-start(f32[1280,256]{1,0:T(8,128)} %get-tuple-element.49), channel_id=1, source_target_pairs={{0,1},{1,0},{2,3},{3,2},{4,5},{5,4},{6,7},{7,6},{8,9},{9,8},{10,11... | collective-permute-start | bytes 3932168 | tf_op jit(solution)/shard_map/ppermute | solution.py:116
  149.9 16.8 %collective-permute-start.24 = (bf16[2,256,512]{2,1,0:T(8,128)(2,1)S(1)}, bf16[2,256,512]{2,1,0:T(8,128)(2,1)S(1)}, u32[]{:S(2)}, u32[]{:S(2)}) collective-permute-start(bf16[2,256,512]{2,1,0:T(8,128)(2,1)S(1)} %broadcast_select_fusion.2.refs_16_.refs_8_), channel_id=1, source_target_pairs={{0,16},{16,0},{1,17},{17,1},{2,18},{18,2},{3,19},{19,3},{4,20},{20... | collective-permute-start | bytes 1572872 | tf_op jit(solution)/shard_map/ppermute | solution.py:116
  153.1 18.7 %copy-start.3 = (bf16[512,512]{1,0:T(8,128)(2,1)S(1)}, bf16[512,512]{1,0:T(8,128)(2,1)}, u32[]{:S(2)}) copy-start(bf16[512,512]{1,0:T(8,128)(2,1)} %refs_5_.3) | copy-start | bytes 1572868
  156.6 10.2 %collective-permute-start.21 = (bf16[256,128]{1,0:T(8,128)(2,1)S(1)}, bf16[256,128]{1,0:T(8,128)(2,1)S(1)}, u32[]{:S(2)}, u32[]{:S(2)}) collective-permute-start(bf16[256,128]{1,0:T(8,128)(2,1)S(1)} %get-tuple-element.51), channel_id=1, source_target_pairs={{0,4},{4,0},{8,12},{12,8},{1,5},{5,1},{9,13},{13,9},{2,6},{6,2},{1... | collective-permute-start | bytes 196616 | tf_op jit(solution)/shard_map/ppermute | solution.py:116
  164.2 7.5 %collective-permute-start.22 = (bf16[256,128]{1,0:T(8,128)(2,1)S(1)}, bf16[256,128]{1,0:T(8,128)(2,1)S(1)}, u32[]{:S(2)}, u32[]{:S(2)}) collective-permute-start(bf16[256,128]{1,0:T(8,128)(2,1)S(1)} %get-tuple-element.52), channel_id=1, source_target_pairs={{0,8},{4,12},{8,0},{12,4},{1,9},{5,13},{9,1},{13,5},{2,10},{6,14},... | collective-permute-start | bytes 196616 | tf_op jit(solution)/shard_map/ppermute | solution.py:116
  164.2 7.5 %collective-permute-start.23 = (bf16[256,128]{1,0:T(8,128)(2,1)S(1)}, bf16[256,128]{1,0:T(8,128)(2,1)S(1)}, u32[]{:S(2)}, u32[]{:S(2)}) collective-permute-start(bf16[256,128]{1,0:T(8,128)(2,1)S(1)} %get-tuple-element.53), channel_id=1, source_target_pairs={{0,12},{4,8},{8,4},{12,0},{1,13},{5,9},{9,5},{13,1},{2,14},{6,10},... | collective-permute-start | bytes 196616 | tf_op jit(solution)/shard_map/ppermute | solution.py:116
  171.7 5.8 %copy-start = (bf16[3,192,2048]{2,1,0:T(8,128)(2,1)S(1)}, bf16[3,192,2048]{2,1,0:T(8,128)(2,1)}, u32[]{:S(2)}) copy-start(bf16[3,192,2048]{2,1,0:T(8,128)(2,1)} %refs_2_.2) | copy-start | bytes 7077892
  171.7 5.8 %copy-start.7 = (s32[8]{0:T(128)S(1)}, s32[8]{0:T(128)}, u32[]{:S(2)}) copy-start(s32[8]{0:T(128)} %refs_1_.2) | copy-start | bytes 100
  173.8 2.0 %collective-permute-start.25 = (bf16[2,256,512]{2,1,0:T(8,128)(2,1)S(1)}, bf16[2,256,512]{2,1,0:T(8,128)(2,1)S(1)}, u32[]{:S(2)}, u32[]{:S(2)}) collective-permute-start(bf16[2,256,512]{2,1,0:T(8,128)(2,1)S(1)} %get-tuple-element.55), channel_id=1, source_target_pairs={{0,1},{1,0},{2,3},{3,2},{4,5},{5,4},{6,7},{7,6},{8,9},{9,8},{10,11... | collective-permute-start | bytes 1572872 | tf_op jit(solution)/shard_map/ppermute | solution.py:116
  175.8 8.4 %collective-permute-start.26 = (bf16[256,512]{1,0:T(8,128)(2,1)S(1)}, bf16[256,512]{1,0:T(8,128)(2,1)S(1)}, u32[]{:S(2)}, u32[]{:S(2)}) collective-permute-start(bf16[256,512]{1,0:T(8,128)(2,1)S(1)} %fusion), channel_id=1, source_target_pairs={{0,2},{2,0},{1,3},{3,1},{4,6},{6,4},{5,7},{7,5},{8,10},{10,8},{9,1... | collective-permute-start | bytes 786440 | tf_op jit(solution)/shard_map/ppermute | solution.py:116

commit v4 on v3

--- a/solution.py
+++ b/solution.py
@@ -122,18 +122,16 @@
 HBM = pl.BlockSpec(memory_space=pltpu.HBM)
 
 
-def kernel_call(body, outs, ins, after=(), scratch=(), smem=(), loose_in=(), loose_out=(), limit=14):
+def kernel_call(body, outs, ins, after=(), scratch=(), smem=(), loose_in=(), limit=14):
     def whole(*refs):
         body(*refs[: len(ins)], *refs[len(ins) + len(after) :])
 
-    spots = [
-        SMEM if i in smem else HBM if i in loose_in else VMEM for i in range(1, len(ins))
-    ]
+    spots = [SMEM if i in smem else HBM if i in loose_in else VMEM for i in range(len(ins))]
     return pl.pallas_call(
         whole,
         out_shape=outs,
-        in_specs=[SMEM, *spots] + [ANY] * len(after),
-        out_specs=[HBM if i in loose_out else VMEM for i in range(len(outs))],
+        in_specs=spots + [ANY] * len(after),
+        out_specs=[VMEM] * len(outs),
         scratch_shapes=scratch,
         compiler_params=pltpu.CompilerParams(vmem_limit_bytes=limit * 2**20),
     )(*ins, *after)
@@ -178,7 +176,6 @@
 
 
 def first_body(
-    scalars,
     plan_ref,
     cache_ref,
     audio_ref,
@@ -191,7 +188,7 @@
     held_ref,
     sems,
 ):
-    rep_at, mem_at, grp_at = scalars[0], scalars[1], scalars[2]
+    rep_at, mem_at, grp_at = (lax.axis_index(name) for name in ("rep", "mem", "grp"))
     rows, width = held_ref.shape[1:]
     width = width // 2
     copies = []
@@ -243,8 +240,8 @@
         started.wait()
 
 
-def weight_body(scalars, kv_ref, query_ref, other_ref, own_ref, *piece_refs):
-    seq_at, rep_at, grp_at = scalars[0], scalars[1], scalars[2]
+def weight_body(kv_ref, query_ref, other_ref, own_ref, *piece_refs):
+    seq_at, rep_at, grp_at = (lax.axis_index(name) for name in ("seq", "rep", "grp"))
     kv_half, query_half = kv_ref.shape[0] // 2, query_ref.shape[0] // 2
     kv_rows, query_rows = kv_half // 2, query_half // 2
     fold = query_rows // 2
@@ -276,10 +273,10 @@
         fill(piece_ref, bit, grp_at, 0, kv_rows)
 
 
-def products_body(scalars, *refs):
+def products_body(*refs):
     packed_refs, weight_refs = refs[:8], refs[8:15]
     send_ref, keep_ref, rows_ref, audio_ref, kv_ref, query_ref = refs[15:]
-    seq_at, mem_at, grp_at = scalars[0], scalars[1], scalars[2]
+    seq_at, mem_at, grp_at = (lax.axis_index(name) for name in ("seq", "mem", "grp"))
     rows, audio_rows = rows_ref.shape[0] // 4, audio_ref.shape[0] // 4
     depth, lane = rows_ref.shape[1] // 4, audio_ref.shape[1] // 4
     for at, packed_ref in enumerate(packed_refs):
@@ -341,7 +338,7 @@
     return (weighted / jnp.sum(exp_terms, axis=1, keepdims=True)).astype(jnp.bfloat16)
 
 
-def attention_body(scalars, frames_ref, align_ref, keep_ref, came_ref, *refs):
+def attention_body(frames_ref, align_ref, keep_ref, came_ref, *refs):
     *out_refs, kv_ref, query_ref = refs
     count, audio_rows = kv_ref.shape[0], query_ref.shape[1]
 
@@ -351,52 +348,39 @@
     kv_ref[...] = summed(slice(0, count))
     for slot in range(4):
         side, half = divmod(slot, 2)
-        query_ref[scalars[slot]] = summed(
+        query_ref[slot] = summed(
             slice(count + half * audio_rows, count + (half + 1) * audio_rows),
             slice(side * HEAD_DIM, (side + 1) * HEAD_DIM),
         )
     for bit, out_ref in enumerate(out_refs):
-        block = scalars[0] ^ bit
-        out_ref[...] = attend(query_ref[block], kv_ref, frames_ref, align_ref[block])
-
-
-def out_body(
-    scalars,
-    own_ref,
-    near_ref,
-    far_ref,
-    farther_ref,
-    own_w,
-    partner_w,
-    partner_rest_w,
-    far_w,
-    far_rest_w,
-    send_ref,
-    keep_ref,
-    heads_ref,
-    weight_ref,
-    sem,
-):
-    seq_at, grp_at, place = scalars[0], scalars[1], scalars[2]
+        align = align_ref[lax.axis_index("seq") ^ bit]
+        out_ref[...] = attend(query_ref[bit], kv_ref, frames_ref, align)
+
+
+def out_body(*refs):
+    piece_refs, (own_w, *part_refs), (send_ref, keep_ref, heads_ref, weight_ref, sem) = (
+        refs[:4],
+        refs[4:11],
+        refs[11:],
+    )
+    seq_at, grp_at = lax.axis_index("seq"), lax.axis_index("grp")
+    place = lax.axis_index("mem") * 2 + lax.axis_index("rep")
     copy = pltpu.make_async_copy(own_w, weight_ref.at[0], sem)
     copy.start()
-    for bit, head_ref in enumerate((own_ref, near_ref, far_ref, farther_ref)):
-        heads_ref[seq_at ^ bit] = head_ref[...]
+    for bit, piece_ref in enumerate(piece_refs):
+        heads_ref[seq_at ^ bit] = piece_ref[...]
     heads = jnp.concatenate([heads_ref[head] for head in range(heads_ref.shape[0])], axis=1)
-    depth = partner_w.shape[0]
+    depth = part_refs[0].shape[0]
     mine = pl.ds(pl.multiple_of(grp_at * depth, depth), depth)
     rest = pl.ds(pl.multiple_of((1 - grp_at) * depth, depth), depth)
-    weight_ref[1, mine] = partner_w[...]
-    weight_ref[1, rest] = partner_rest_w[...]
-    for far in range(2):
-        weight_ref[2 + far, mine] = far_w[far]
-        weight_ref[2 + far, rest] = far_rest_w[far]
-    middle = 2 - seq_at // 2
-    for at, block in ((1, seq_at ^ 1), (2, middle), (3, middle ^ 1), (0, seq_at)):
-        if at == 0:
+    for bit in range(1, 4):
+        weight_ref[bit, mine] = part_refs[2 * bit - 2][...]
+        weight_ref[bit, rest] = part_refs[2 * bit - 1][...]
+    for bit in (1, 2, 3, 0):
+        if bit == 0:
             copy.wait()
-        slot = block ^ place
-        value = jnp.dot(heads, weight_ref[at], preferred_element_type=jnp.float32)
+        slot = seq_at ^ bit ^ place
+        value = jnp.dot(heads, weight_ref[bit], preferred_element_type=jnp.float32)
 
         @pl.when(slot % 2 == 1)
         def _():
@@ -409,9 +393,8 @@
 
 def by_head(video_cache, plan, alignment, audio_tokens, kv_weight, query_weight, out_weight):
     seq_size = lax.axis_size("seq")
-    seq_at, mem_at, rep_at = (lax.axis_index(name) for name in ("seq", "mem", "rep"))
-    grp_at = lax.axis_index("grp")
-    place = mem_at * 2 + rep_at
+    seq_at = lax.axis_index("seq")
+    place = lax.axis_index("mem") * 2 + lax.axis_index("rep")
     video_rows = video_cache.shape[1]
     audio_rows = audio_tokens.shape[0]
     half_depth, width = kv_weight.shape[0] // 2, 2 * HEAD_DIM
@@ -420,96 +403,83 @@
     def bfloat(*shape):
         return jax.ShapeDtypeStruct(shape, jnp.bfloat16)
 
-    packed, other, half = kernel_call(
+    packed, other, out_half = kernel_call(
         first_body,
         [
             bfloat(2 * video_rows + audio_rows, half_depth),
             bfloat(half_depth + query_quarter, kv_weight.shape[1]),
             bfloat(out_weight.shape[0] // 2, out_weight.shape[1]),
         ],
-        [
-            jnp.stack([rep_at, mem_at, grp_at]),
-            plan,
-            video_cache,
-            audio_tokens,
-            kv_weight,
-            query_weight,
-            out_weight,
-        ],
+        [plan, video_cache, audio_tokens, kv_weight, query_weight, out_weight],
         scratch=[
             pltpu.VMEM((3, video_rows, 2 * half_depth), jnp.bfloat16),
             pltpu.SemaphoreType.DMA((14,)),
         ],
-        smem=(1,),
-        loose_in=(2, 3, 4, 5, 6),
+        smem=(0,),
+        loose_in=(1, 2, 3, 4, 5),
         limit=61,
     )
 
+    tokens = [packed, swap(packed, "seq", 1), swap(packed, "seq", 2)]
+    across = [swap(packed, "mem", 1)]
     other = swap(other, "rep", 1)
     rows = half_depth // 2 + query_quarter // 2
     weight_own, *pieces = kernel_call(
         weight_body,
         [bfloat(2 * rows, 2 * width)] + [bfloat(rows, 2 * width)] * 3,
-        [jnp.stack([seq_at, rep_at, grp_at]), kv_weight, query_weight, other],
-    )
-    pieces = [swap(piece, "seq", bit) for bit, piece in enumerate(pieces, 1)]
-
-    inner, outward = [(1, 2), (2, 1)], [(1, 0), (2, 3)]
-    is_inner = (seq_at == 1) | (seq_at == 2)
-    partner = swap(packed, "seq", 1)
+        [kv_weight, query_weight, other],
+    )
+    pieces[0] = swap(pieces[0], "seq", 1)
     align_all = lax.all_to_all(
         jnp.broadcast_to(alignment[None], (seq_size, audio_rows)), "seq", 0, 0, tiled=True
     ).astype(jnp.float32)
-    inner_own = lax.ppermute(packed, "seq", inner)
-    partner, inner_own, align_all, weight_own = lax.optimization_barrier(
-        (partner, inner_own, align_all, weight_own)
-    )
-    out_partner = swap(half, "seq", 1)
-    inner_partner = lax.ppermute(partner, "seq", inner)
-    third = jnp.where(is_inner, inner_own, lax.ppermute(inner_own, "seq", outward))
-    third, pieces[0], out_partner = lax.optimization_barrier((third, pieces[0], out_partner))
-    fourth = jnp.where(is_inner, inner_partner, lax.ppermute(inner_partner, "seq", outward))
-    out_pair = lax.ppermute(jnp.stack([half, out_partner]), "seq", inner)
-    fourth, pieces[1], pieces[2], out_pair = lax.optimization_barrier(
-        (fourth, pieces[1], pieces[2], out_pair)
-    )
+    tokens[1], tokens[2], across[0], pieces[0], align_all = lax.optimization_barrier(
+        (tokens[1], tokens[2], across[0], pieces[0], align_all)
+    )
+
+    tokens.append(swap(tokens[2], "seq", 1))
+    across += [swap(tokens[1], "mem", 1), swap(tokens[2], "mem", 1)]
+    pieces[1:] = [swap(piece, "seq", bit) for bit, piece in enumerate(pieces[1:], 2)]
+    rest = [swap(pieces[0], "grp", 1)]
+    tokens[3], across[1], across[2], pieces[1], pieces[2], rest[0], out_half = (
+        lax.optimization_barrier(
+            (tokens[3], across[1], across[2], pieces[1], pieces[2], rest[0], out_half)
+        )
+    )
+
+    across.append(swap(tokens[3], "mem", 1))
+    rest += [swap(piece, "grp", 1) for piece in pieces[1:]]
+    out_parts = [swap(out_half, "seq", 1), swap(out_half, "seq", 2)]
     weights = [weight_own]
-    for piece in pieces:
-        weights += [piece, swap(piece, "grp", 1)]
-    tokens = []
-    for value in (packed, partner, third, fourth):
-        tokens += [value, swap(value, "mem", 1)]
-    middle = 2 - seq_at // 2
-    blocks = jnp.stack([seq_at, seq_at ^ 1, middle, middle ^ 1])
-
-    partner_rest = swap(out_partner, "grp", 1)
-    far = jnp.where(is_inner, out_pair, lax.ppermute(out_pair, "seq", outward))
-    far_rest = swap(far, "grp", 1)
-
+    for piece, other in zip(pieces, rest):
+        weights += [piece, other]
     rows = seq_size * (video_rows + audio_rows // 2)
     sums = jax.ShapeDtypeStruct((rows, width), jnp.float32)
     send, keep = kernel_call(
         products_body,
         [sums, sums],
-        [jnp.stack([seq_at, mem_at, grp_at]), *tokens, *weights],
+        [value for pair in zip(tokens, across) for value in pair] + weights,
+        after=out_parts,
         scratch=[
             pltpu.VMEM((seq_size * video_rows, 4 * half_depth), jnp.bfloat16),
             pltpu.VMEM((seq_size * audio_rows, 8 * query_quarter), jnp.bfloat16),
             pltpu.VMEM((4 * half_depth, 2 * width), jnp.bfloat16),
             pltpu.VMEM((8 * query_quarter, width), jnp.bfloat16),
         ],
-        after=(far, partner_rest),
         limit=26,
     )
     came = swap(send, "rep", 1)
+    out_parts.append(swap(out_parts[1], "seq", 1))
 
     span = video_rows * seq_size
+    blocks = jnp.stack([seq_at, seq_at ^ 1, seq_at ^ 2, seq_at ^ 3])
     positions = blocks[:, None] * video_rows + jnp.arange(video_rows, dtype=jnp.int32)[None, :]
     frames_video = (positions.reshape(1, span) * FRAMES // span).astype(jnp.float32)
     own_piece, near_piece, far_piece, farther_piece = kernel_call(
         attention_body,
         [bfloat(audio_rows, HEAD_DIM)] * 4,
-        [blocks, frames_video, align_all[:, :, None], keep, came],
+        [frames_video, align_all[:, :, None], keep, came],
+        after=(out_parts[2],),
         scratch=[
             pltpu.VMEM((span, width), jnp.bfloat16),
             pltpu.VMEM((seq_size, audio_rows, HEAD_DIM), jnp.bfloat16),
@@ -520,30 +490,22 @@
     near_piece = swap(near_piece, "seq", 1)
 
     columns = out_weight.shape[1]
+    weights = [out_weight]
+    for part in out_parts:
+        weights += [part, swap(part, "grp", 1)]
     send, keep = kernel_call(
         out_body,
         [
             jax.ShapeDtypeStruct((2, audio_rows, columns), jnp.bfloat16),
             jax.ShapeDtypeStruct((2, audio_rows, columns), jnp.float32),
         ],
-        [
-            jnp.stack([seq_at, grp_at, place]),
-            own_piece,
-            near_piece,
-            far_piece,
-            farther_piece,
-            out_weight,
-            out_partner,
-            partner_rest,
-            far,
-            far_rest,
-        ],
+        [own_piece, near_piece, far_piece, farther_piece, *weights],
         scratch=[
             pltpu.VMEM((seq_size, audio_rows, HEAD_DIM), jnp.bfloat16),
             pltpu.VMEM((seq_size, *out_weight.shape), jnp.bfloat16),
             pltpu.SemaphoreType.DMA,
         ],
-        loose_in=(5,),
+        loose_in=(4,),
     )
     came = swap(send, "rep", 1)
     across = swap((keep[1] + came[1].astype(jnp.float32)).astype(jnp.bfloat16), "mem", 1)

time: 186 us -> 137 us (0.74)
  waiting for transfers between devices: 100 us -> 50.9 us
  blocking collectives: 0 us -> 34 us
  starting transfers between devices: 58.4 us -> 30.9 us
  Pallas kernels: 18.9 us -> 15.2 us
  local copies, waits for them, and re-layouts: 2.59 us -> 0.45 us
    all_to_all x0 -> x1, blocking collectives: none -> 34 us  [by_head(): lax.all_to_all(jnp.broadcast_to(alignment[None], (seq_size, audio_rows)),...]
    ppermute x21 -> x26, waiting for transfers between devices: 84.4 us -> 50.9 us  [swap(): return lax.ppermute(value, axis, [(i, i ^ bit) for i in range(size)])]
    ppermute x21 -> x26, starting transfers between devices: 46.8 us -> 30.9 us  [swap(): return lax.ppermute(value, axis, [(i, i ^ bit) for i in range(size)])]
    all_to_all x1 -> x0, waiting for transfers between devices: 12.8 us -> none  [by_head(): lax.all_to_all(jnp.broadcast_to(alignment[None], (seq_size, audio_rows)),...]
    ppermute x6 -> x0, starting transfers between devices: 6.73 us -> none  [the longest x1 1.49 us: by_head(): inner_own = lax.ppermute(packed, 'seq', inner)]
    all_to_all x1 -> x0, starting transfers between devices: 4.85 us -> none  [by_head(): lax.all_to_all(jnp.broadcast_to(alignment[None], (seq_size, audio_rows)),...]
    pallas_call x5, Pallas kernels: 17.1 us -> 13.4 us  [kernel_call(): pl.pallas_call(whole, out_shape=outs, in_specs=spots + [ANY] * len(after)...]
    ppermute x6 -> x0, waiting for transfers between devices: 2.82 us -> none  [the longest x1 1.82 us: by_head(): far = jnp.where(is_inner, out_pair, lax.ppermute(out_pair, 'seq', outward))]
  transfers between devices with their start and end apart: 28 -> 26, of which waited for: 13 -> 11; matrix products, arithmetic and copies ran while one was open for 2% -> 1% of each run, Pallas kernels for 4% -> 3%
where the time goes in v4:
time: 137 us; the launch traced here: 136 us
  waiting for transfers between devices  50.9 us (37%)
  blocking collectives  34 us (25%)
  starting transfers between devices  30.9 us (23%)
  Pallas kernels  15.2 us (11%)
  other arithmetic  3.98 us (3%)
    ppermute x26, waiting for transfers between devices, swap(): return lax.ppermute(value, axis, [(i, i ^ bit) for i in range(size)])  50.9 us
    all_to_all x1, blocking collectives, by_head(): lax.all_to_all(jnp.broadcast_to(alignment[None], (seq_size, audio_rows)),...  34 us
    ppermute x26, starting transfers between devices, swap(): return lax.ppermute(value, axis, [(i, i ^ bit) for i in range(size)])  30.9 us
    pallas_call x5, Pallas kernels, kernel_call(): pl.pallas_call(whole, out_shape=outs, in_specs=spots + [ANY] * len(after)...  13.4 us
  transfers between devices with their start and end apart: 26, of which 11 were waited for; matrix products, arithmetic and copies ran while one was open for 1% of the time, Pallas kernels for 3%

profile of v4, /device:TPU:0, one launch (start us, length us, event | category | flops | bytes accessed | tf_op | source)
XLA Modules:
  0.0 136.3 jit_solution(7991330522658846127)
XLA Ops:
  0.6 4.2 %shard_map.87 = (bf16[640,512]{1,0:T(8,128)(2,1)}, bf16[640,1024]{1,0:T(8,128)(2,1)}, bf16[256,512]{1,0:T(8,128)(2,1)}) custom-call(s32[8]{0:T(128)} %refs_0_.2, bf16[3,192,2048]{2,1,0:T(8,128)(2,1)} %refs_1_.2, bf16[256,2048]{1,0:T(8,128)(2,1)} %refs_2_.1, bf16[1024,1024]{1,0:T(8,128)(2,1)} %refs_0_.3, bf16[512,512]{1,0:T(8,128)(2,1)} %refs_1_.3, ...), custom_call_target="tpu_custom_call" | custom-call | tf_op jit(solution)/shard_map/pallas_call | solution.py:130
  4.9 0.5 collective-permute-start.3
  5.4 2.7 %collective-permute-start = (bf16[640,512]{1,0:T(8,128)(2,1)}, bf16[640,512]{1,0:T(8,128)(2,1)S(1)}, u32[]{:S(2)}, u32[]{:S(2)}) collective-permute-start(bf16[640,512]{1,0:T(8,128)(2,1)} %get-tuple-element.31.refs_0_), channel_id=1, source_target_pairs={{0,4},{4,0},{8,12},{12,8},{1,5},{5,1},{9,13},{13,9},{2,6},{6,2},{1... | collective-permute-start | bytes 1966088 | tf_op jit(solution)/shard_map/ppermute | solution.py:116
  8.1 2.6 %collective-permute-start.1 = (bf16[640,512]{1,0:T(8,128)(2,1)}, bf16[640,512]{1,0:T(8,128)(2,1)S(1)}, u32[]{:S(2)}, u32[]{:S(2)}) collective-permute-start(bf16[640,512]{1,0:T(8,128)(2,1)} %get-tuple-element.31.refs_0_), channel_id=1, source_target_pairs={{0,8},{4,12},{8,0},{12,4},{1,9},{5,13},{9,1},{13,5},{2,10},{6,14},... | collective-permute-start | bytes 1966088 | tf_op jit(solution)/shard_map/ppermute | solution.py:116
  10.6 1.5 %collective-permute-start.2 = (bf16[640,512]{1,0:T(8,128)(2,1)}, bf16[640,512]{1,0:T(8,128)(2,1)S(1)}, u32[]{:S(2)}, u32[]{:S(2)}) collective-permute-start(bf16[640,512]{1,0:T(8,128)(2,1)} %get-tuple-element.31.refs_0_), channel_id=1, source_target_pairs={{0,2},{2,0},{1,3},{3,1},{4,6},{6,4},{5,7},{7,5},{8,10},{10,8},{9,1... | collective-permute-start | bytes 1966088 | tf_op jit(solution)/shard_map/ppermute | solution.py:116
  12.2 0.3 shard_map.88
  12.4 0.5 collective-permute-start.4
  12.9 34.0 %all_to_all.6 = s32[4,1,256]{2,1,0:T(1,128)S(1)} all-to-all(s32[4,1,256]{2,1,0:T(1,128)S(1)} %broadcast_in_dim.4), channel_id=1, replica_groups=mesh['grp'=2,'seq'=4,'mem'=2,'rep'=2] {'seq'}, dimensions={0} | all-to-all | bytes 8192 | tf_op jit(solution)/shard_map/all_to_all | solution.py:433
  46.9 0.6 collective-permute-start.8
  47.6 1.6 %collective-permute-start.5 = (bf16[640,512]{1,0:T(8,128)(2,1)S(1)}, bf16[640,512]{1,0:T(8,128)(2,1)S(1)}, u32[]{:S(2)}, u32[]{:S(2)}) collective-permute-start(bf16[640,512]{1,0:T(8,128)(2,1)S(1)} %collective-permute-done.1.refs_4_), channel_id=1, source_target_pairs={{0,4},{4,0},{8,12},{12,8},{1,5},{5,1},{9,13},{13,9},{2,6},{6,2},{1... | collective-permute-start | bytes 1966088 | tf_op jit(solution)/shard_map/ppermute | solution.py:116
  49.2 1.5 %collective-permute-start.7 = (bf16[640,512]{1,0:T(8,128)(2,1)S(1)}, bf16[640,512]{1,0:T(8,128)(2,1)S(1)}, u32[]{:S(2)}, u32[]{:S(2)}) collective-permute-start(bf16[640,512]{1,0:T(8,128)(2,1)S(1)} %collective-permute-done.1.refs_4_), channel_id=1, source_target_pairs={{0,2},{2,0},{1,3},{3,1},{4,6},{6,4},{5,7},{7,5},{8,10},{10,8},{9,1... | collective-permute-start | bytes 1966088 | tf_op jit(solution)/shard_map/ppermute | solution.py:116
  50.7 0.5 collective-permute-start.6
  51.2 2.2 %collective-permute-start.9 = (bf16[320,512]{1,0:T(8,128)(2,1)S(1)}, bf16[320,512]{1,0:T(8,128)(2,1)S(1)}, u32[]{:S(2)}, u32[]{:S(2)}) collective-permute-start(bf16[320,512]{1,0:T(8,128)(2,1)S(1)} %get-tuple-element.39), channel_id=1, source_target_pairs={{0,12},{4,8},{8,4},{12,0},{1,13},{5,9},{9,5},{13,1},{2,14},{6,10},... | collective-permute-start | bytes 983048 | tf_op jit(solution)/shard_map/ppermute | solution.py:116
  53.4 10.5 %collective-permute-done.8.refs_11_ = bf16[320,512]{1,0:T(8,128)(2,1)S(1)} collective-permute-done((bf16[320,512]{1,0:T(8,128)(2,1)S(1)}, bf16[320,512]{1,0:T(8,128)(2,1)S(1)}, u32[]{:S(2)}, u32[]{:S(2)}) %collective-permute-start.8) | collective-permute-done | bytes 327712 | tf_op jit(solution)/shard_map/ppermute | solution.py:116
  64.0 1.5 %collective-permute-start.10 = (bf16[320,512]{1,0:T(8,128)(2,1)S(1)}, bf16[320,512]{1,0:T(8,128)(2,1)S(1)}, u32[]{:S(2)}, u32[]{:S(2)}) collective-permute-start(bf16[320,512]{1,0:T(8,128)(2,1)S(1)} %collective-permute-done.4.refs_9_), channel_id=1, source_target_pairs={{0,16},{16,0},{1,17},{17,1},{2,18},{18,2},{3,19},{19,3},{4,20},{20... | collective-permute-start | bytes 983048 | tf_op jit(solution)/shard_map/ppermute | solution.py:116
  65.5 12.4 %collective-permute-done.9.refs_13_ = bf16[320,512]{1,0:T(8,128)(2,1)S(1)} collective-permute-done((bf16[320,512]{1,0:T(8,128)(2,1)S(1)}, bf16[320,512]{1,0:T(8,128)(2,1)S(1)}, u32[]{:S(2)}, u32[]{:S(2)}) %collective-permute-start.9) | collective-permute-done | bytes 327712 | tf_op jit(solution)/shard_map/ppermute | solution.py:116
  77.9 1.0 collective-permute-done.6.refs_3_
  78.9 1.5 %collective-permute-start.11 = (bf16[640,512]{1,0:T(8,128)(2,1)S(1)}, bf16[640,512]{1,0:T(8,128)(2,1)S(1)}, u32[]{:S(2)}, u32[]{:S(2)}) collective-permute-start(bf16[640,512]{1,0:T(8,128)(2,1)S(1)} %collective-permute-done.5.refs_6_), channel_id=1, source_target_pairs={{0,2},{2,0},{1,3},{3,1},{4,6},{6,4},{5,7},{7,5},{8,10},{10,8},{9,1... | collective-permute-start | bytes 1966088 | tf_op jit(solution)/shard_map/ppermute | solution.py:116
  80.4 1.5 %collective-permute-start.12 = (bf16[320,512]{1,0:T(8,128)(2,1)S(1)}, bf16[320,512]{1,0:T(8,128)(2,1)S(1)}, u32[]{:S(2)}, u32[]{:S(2)}) collective-permute-start(bf16[320,512]{1,0:T(8,128)(2,1)S(1)} %collective-permute-done.8.refs_11_), channel_id=1, source_target_pairs={{0,16},{16,0},{1,17},{17,1},{2,18},{18,2},{3,19},{19,3},{4,20},{20... | collective-permute-start | bytes 983048 | tf_op jit(solution)/shard_map/ppermute | solution.py:116
  81.9 0.5 collective-permute-start.13
  82.4 1.1 collective-permute-start.15
  83.5 1.4 %collective-permute-start.14 = (bf16[256,512]{1,0:T(8,128)(2,1)S(1)}, bf16[256,512]{1,0:T(8,128)(2,1)}, u32[]{:S(2)}, u32[]{:S(2)}) collective-permute-start(bf16[256,512]{1,0:T(8,128)(2,1)S(1)} %copy-done.10), channel_id=1, source_target_pairs={{0,4},{4,0},{8,12},{12,8},{1,5},{5,1},{9,13},{13,9},{2,6},{6,2},{1... | collective-permute-start | bytes 786440 | tf_op jit(solution)/shard_map/ppermute | solution.py:116
  85.0 9.5 %collective-permute-done.15.refs_16_.refs_7_ = bf16[256,512]{1,0:T(8,128)(2,1)S(1)} collective-permute-done((bf16[256,512]{1,0:T(8,128)(2,1)S(1)}, bf16[256,512]{1,0:T(8,128)(2,1)S(1)}, u32[]{:S(2)}, u32[]{:S(2)}) %collective-permute-start.15) | collective-permute-done | bytes 262176 | tf_op jit(solution)/shard_map/ppermute | solution.py:116
  94.4 0.1 collective-permute-done.14.refs_15_.refs_5_
  94.6 0.3 collective-permute-done.13.refs_14_
  94.9 3.9 %shard_map.89 = (f32[1280,256]{1,0:T(8,128)}, f32[1280,256]{1,0:T(8,128)S(1)}) custom-call(bf16[640,512]{1,0:T(8,128)(2,1)S(1)} %copy-done.6, bf16[640,512]{1,0:T(8,128)(2,1)S(1)} %collective-permute-done.2.refs_1_, bf16[640,512]{1,0:T(8,128)(2,1)S(1)} %collective-permute-done.refs_2_, bf16[640,512]{1,0:T(8,128)(2,1)S(1)} %collective-permute-done.6.refs_3_, ...), custom_call_target="tpu_custom_call" | custom-call | tf_op jit(solution)/shard_map/pallas_call | solution.py:130
  98.9 0.5 collective-permute-start.17
  99.4 1.5 %collective-permute-start.22 = (bf16[256,512]{1,0:T(8,128)(2,1)S(1)}, bf16[256,512]{1,0:T(8,128)(2,1)}, u32[]{:S(2)}, u32[]{:S(2)}) collective-permute-start(bf16[256,512]{1,0:T(8,128)(2,1)S(1)} %collective-permute-done.15.refs_16_.refs_7_), channel_id=1, source_target_pairs={{0,16},{16,0},{1,17},{17,1},{2,18},{18,2},{3,19},{19,3},{4,20},{20... | collective-permute-start | bytes 786440 | tf_op jit(solution)/shard_map/ppermute | solution.py:116
  101.0 0.1 div.18
  101.1 0.1 reshape.123
  101.2 0.5 collective-permute-start.21
  101.7 6.0 %collective-permute-done.17.refs_4_.refs_9_ = bf16[256,512]{1,0:T(8,128)(2,1)} collective-permute-done((bf16[256,512]{1,0:T(8,128)(2,1)S(1)}, bf16[256,512]{1,0:T(8,128)(2,1)}, u32[]{:S(2)}, u32[]{:S(2)}) %collective-permute-start.17) | collective-permute-done | bytes 262176 | tf_op jit(solution)/shard_map/ppermute | solution.py:116
  107.7 1.5 %collective-permute-start.23 = (bf16[256,512]{1,0:T(8,128)(2,1)}, bf16[256,512]{1,0:T(8,128)(2,1)}, u32[]{:S(2)}, u32[]{:S(2)}) collective-permute-start(bf16[256,512]{1,0:T(8,128)(2,1)} %collective-permute-done.17.refs_4_.refs_9_), channel_id=1, source_target_pairs={{0,16},{16,0},{1,17},{17,1},{2,18},{18,2},{3,19},{19,3},{4,20},{20... | collective-permute-start | bytes 786440 | tf_op jit(solution)/shard_map/ppermute | solution.py:116
  109.2 0.2 copy.10.refs_1_
  109.5 2.1 %shard_map.90 = (bf16[256,128]{1,0:T(8,128)(2,1)S(1)}, bf16[256,128]{1,0:T(8,128)(2,1)S(1)}, bf16[256,128]{1,0:T(8,128)(2,1)S(1)}, bf16[256,128]{1,0:T(8,128)(2,1)S(1)}) custom-call(f32[1,768]{1,0:T(1,128)S(1)} %fusion.3.refs_0_, f32[4,256,1]{2,1,0:T(8,128)S(1)} %copy.10.refs_1_, f32[1280,256]{1,0:T(8,128)S(1)} %get-tuple-element.50.refs_2_, ...), custom_call_target="tpu_custom_call" | custom-call | tf_op jit(solution)/shard_map/pallas_call | solution.py:130
  111.6 0.5 collective-permute-start.18
  112.1 1.8 %collective-permute-start.19 = (bf16[256,128]{1,0:T(8,128)(2,1)S(1)}, bf16[256,128]{1,0:T(8,128)(2,1)S(1)}, u32[]{:S(2)}, u32[]{:S(2)}) collective-permute-start(bf16[256,128]{1,0:T(8,128)(2,1)S(1)} %get-tuple-element.54), channel_id=1, source_target_pairs={{0,8},{4,12},{8,0},{12,4},{1,9},{5,13},{9,1},{13,5},{2,10},{6,14},... | collective-permute-start | bytes 196616 | tf_op jit(solution)/shard_map/ppermute | solution.py:116
  113.9 2.1 %collective-permute-start.20 = (bf16[256,128]{1,0:T(8,128)(2,1)S(1)}, bf16[256,128]{1,0:T(8,128)(2,1)S(1)}, u32[]{:S(2)}, u32[]{:S(2)}) collective-permute-start(bf16[256,128]{1,0:T(8,128)(2,1)S(1)} %get-tuple-element.55), channel_id=1, source_target_pairs={{0,12},{4,8},{8,4},{12,0},{1,13},{5,9},{9,5},{13,1},{2,14},{6,10},... | collective-permute-start | bytes 196616 | tf_op jit(solution)/shard_map/ppermute | solution.py:116
  116.0 3.2 %collective-permute-done.23.refs_10_ = bf16[256,512]{1,0:T(8,128)(2,1)} collective-permute-done((bf16[256,512]{1,0:T(8,128)(2,1)}, bf16[256,512]{1,0:T(8,128)(2,1)}, u32[]{:S(2)}, u32[]{:S(2)}) %collective-permute-start.23) | collective-permute-done | bytes 262176 | tf_op jit(solution)/shard_map/ppermute | solution.py:116
  119.2 0.9 collective-permute-done.20.refs_3_
  120.1 2.9 %shard_map.91 = (bf16[2,256,512]{2,1,0:T(8,128)(2,1)S(1)}, f32[2,256,512]{2,1,0:T(8,128)S(1)}) custom-call(bf16[256,128]{1,0:T(8,128)(2,1)S(1)} %get-tuple-element.52.refs_0_, bf16[256,128]{1,0:T(8,128)(2,1)S(1)} %collective-permute-done.18.refs_1_, bf16[256,128]{1,0:T(8,128)(2,1)S(1)} %collective-permute-done.19.refs_2_, ...), custom_call_target="tpu_custom_call" | custom-call | tf_op jit(solution)/shard_map/pallas_call | solution.py:130
  123.1 1.9 %collective-permute-done.24 = bf16[2,256,512]{2,1,0:T(8,128)(2,1)S(1)} collective-permute-done((bf16[2,256,512]{2,1,0:T(8,128)(2,1)S(1)}, bf16[2,256,512]{2,1,0:T(8,128)(2,1)S(1)}, u32[]{:S(2)}, u32[]{:S(2)}) %collective-permute-start.24) | collective-permute-done | bytes 524320 | tf_op jit(solution)/shard_map/ppermute | solution.py:116
  125.0 0.9 fusion
  125.9 0.5 collective-permute-start.25
  126.4 1.8 %shard_map.86 = bf16[192,2048]{1,0:T(8,128)(2,1)} custom-call(s32[8]{0:T(128)S(1)} %copy-done.7, bf16[3,192,2048]{2,1,0:T(8,128)(2,1)S(1)} %copy-done), custom_call_target="tpu_custom_call" | custom-call | tf_op jit(solution)/shard_map/pallas_call | solution.py:168
  128.3 1.1 bitcast_add_fusion
  129.4 5.2 %collective-permute-done.25 = bf16[256,512]{1,0:T(8,128)(2,1)} collective-permute-done((bf16[256,512]{1,0:T(8,128)(2,1)}, bf16[256,512]{1,0:T(8,128)(2,1)}, u32[]{:S(2)}, u32[]{:S(2)}) %collective-permute-start.25) | collective-permute-done | bytes 262176 | tf_op jit(solution)/shard_map/ppermute | solution.py:116
  134.6 1.7 %add_convert_fusion = bf16[256,512]{1,0:T(8,128)(2,1)} fusion(f32[256,512]{1,0:T(8,128)S(1)} %bitcast_add_fusion, bf16[256,512]{1,0:T(8,128)(2,1)} %collective-permute-done.25), kind=kLoop, calls=%fused_computation.1 | loop fusion | flops 393216 | bytes 1048576 | tf_op jit(solution)/shard_map/convert_element_type | solution.py:516
  (46 shorter events, 0.4 us)
Async XLA Ops:
  0.6 11.5 %copy-start.2 = (bf16[512,512]{1,0:T(8,128)(2,1)S(1)}, bf16[512,512]{1,0:T(8,128)(2,1)}, u32[]{:S(2)}) copy-start(bf16[512,512]{1,0:T(8,128)(2,1)} %refs_1_.3) | copy-start | bytes 1572868
  0.6 11.5 %copy-start.1 = (bf16[1024,1024]{1,0:T(8,128)(2,1)S(1)}, bf16[1024,1024]{1,0:T(8,128)(2,1)}, u32[]{:S(2)}) copy-start(bf16[1024,1024]{1,0:T(8,128)(2,1)} %refs_0_.3) | copy-start | bytes 6291460
  4.9 7.3 %collective-permute-start.3 = (bf16[640,1024]{1,0:T(8,128)(2,1)}, bf16[640,1024]{1,0:T(8,128)(2,1)S(1)}, u32[]{:S(2)}, u32[]{:S(2)}) collective-permute-start(bf16[640,1024]{1,0:T(8,128)(2,1)} %get-tuple-element.32), channel_id=1, source_target_pairs={{0,1},{1,0},{2,3},{3,2},{4,5},{5,4},{6,7},{7,6},{8,9},{9,8},{10,11... | collective-permute-start | bytes 3932168 | tf_op jit(solution)/shard_map/ppermute | solution.py:116
  5.4 7.5 %copy-start.9 = (s32[256]{0:T(256)S(1)}, s32[256]{0:T(256)}, u32[]{:S(2)}) copy-start(s32[256]{0:T(256)} %param.9) | copy-start | bytes 3076
  5.4 77.0 %copy-start.10 = (bf16[256,512]{1,0:T(8,128)(2,1)S(1)}, bf16[256,512]{1,0:T(8,128)(2,1)}, u32[]{:S(2)}) copy-start(bf16[256,512]{1,0:T(8,128)(2,1)} %get-tuple-element.49) | copy-start | bytes 786436
  5.4 89.5 %copy-start.6 = (bf16[640,512]{1,0:T(8,128)(2,1)S(1)}, bf16[640,512]{1,0:T(8,128)(2,1)}, u32[]{:S(2)}) copy-start(bf16[640,512]{1,0:T(8,128)(2,1)} %get-tuple-element.31.refs_0_) | copy-start | bytes 1966084
  5.4 42.2 %collective-permute-start = (bf16[640,512]{1,0:T(8,128)(2,1)}, bf16[640,512]{1,0:T(8,128)(2,1)S(1)}, u32[]{:S(2)}, u32[]{:S(2)}) collective-permute-start(bf16[640,512]{1,0:T(8,128)(2,1)} %get-tuple-element.31.refs_0_), channel_id=1, source_target_pairs={{0,4},{4,0},{8,12},{12,8},{1,5},{5,1},{9,13},{13,9},{2,6},{6,2},{1... | collective-permute-start | bytes 1966088 | tf_op jit(solution)/shard_map/ppermute | solution.py:116
  8.1 39.5 %collective-permute-start.1 = (bf16[640,512]{1,0:T(8,128)(2,1)}, bf16[640,512]{1,0:T(8,128)(2,1)S(1)}, u32[]{:S(2)}, u32[]{:S(2)}) collective-permute-start(bf16[640,512]{1,0:T(8,128)(2,1)} %get-tuple-element.31.refs_0_), channel_id=1, source_target_pairs={{0,8},{4,12},{8,0},{12,4},{1,9},{5,13},{9,1},{13,5},{2,10},{6,14},... | collective-permute-start | bytes 1966088 | tf_op jit(solution)/shard_map/ppermute | solution.py:116
  10.6 36.9 %collective-permute-start.2 = (bf16[640,512]{1,0:T(8,128)(2,1)}, bf16[640,512]{1,0:T(8,128)(2,1)S(1)}, u32[]{:S(2)}, u32[]{:S(2)}) collective-permute-start(bf16[640,512]{1,0:T(8,128)(2,1)} %get-tuple-element.31.refs_0_), channel_id=1, source_target_pairs={{0,2},{2,0},{1,3},{3,1},{4,6},{6,4},{5,7},{7,5},{8,10},{10,8},{9,1... | collective-permute-start | bytes 1966088 | tf_op jit(solution)/shard_map/ppermute | solution.py:116
  12.4 35.2 %collective-permute-start.4 = (bf16[320,512]{1,0:T(8,128)(2,1)S(1)}, bf16[320,512]{1,0:T(8,128)(2,1)S(1)}, u32[]{:S(2)}, u32[]{:S(2)}) collective-permute-start(bf16[320,512]{1,0:T(8,128)(2,1)S(1)} %get-tuple-element.33), channel_id=1, source_target_pairs={{0,4},{4,0},{8,12},{12,8},{1,5},{5,1},{9,13},{13,9},{2,6},{6,2},{1... | collective-permute-start | bytes 983048 | tf_op jit(solution)/shard_map/ppermute | solution.py:116
  46.9 17.0 %collective-permute-start.8 = (bf16[320,512]{1,0:T(8,128)(2,1)S(1)}, bf16[320,512]{1,0:T(8,128)(2,1)S(1)}, u32[]{:S(2)}, u32[]{:S(2)}) collective-permute-start(bf16[320,512]{1,0:T(8,128)(2,1)S(1)} %get-tuple-element.38), channel_id=1, source_target_pairs={{0,8},{4,12},{8,0},{12,4},{1,9},{5,13},{9,1},{13,5},{2,10},{6,14},... | collective-permute-start | bytes 983048 | tf_op jit(solution)/shard_map/ppermute | solution.py:116
  47.6 30.4 %collective-permute-start.5 = (bf16[640,512]{1,0:T(8,128)(2,1)S(1)}, bf16[640,512]{1,0:T(8,128)(2,1)S(1)}, u32[]{:S(2)}, u32[]{:S(2)}) collective-permute-start(bf16[640,512]{1,0:T(8,128)(2,1)S(1)} %collective-permute-done.1.refs_4_), channel_id=1, source_target_pairs={{0,4},{4,0},{8,12},{12,8},{1,5},{5,1},{9,13},{13,9},{2,6},{6,2},{1... | collective-permute-start | bytes 1966088 | tf_op jit(solution)/shard_map/ppermute | solution.py:116
  49.2 28.8 %collective-permute-start.7 = (bf16[640,512]{1,0:T(8,128)(2,1)S(1)}, bf16[640,512]{1,0:T(8,128)(2,1)S(1)}, u32[]{:S(2)}, u32[]{:S(2)}) collective-permute-start(bf16[640,512]{1,0:T(8,128)(2,1)S(1)} %collective-permute-done.1.refs_4_), channel_id=1, source_target_pairs={{0,2},{2,0},{1,3},{3,1},{4,6},{6,4},{5,7},{7,5},{8,10},{10,8},{9,1... | collective-permute-start | bytes 1966088 | tf_op jit(solution)/shard_map/ppermute | solution.py:116
  50.7 28.2 %collective-permute-start.6 = (bf16[640,512]{1,0:T(8,128)(2,1)S(1)}, bf16[640,512]{1,0:T(8,128)(2,1)S(1)}, u32[]{:S(2)}, u32[]{:S(2)}) collective-permute-start(bf16[640,512]{1,0:T(8,128)(2,1)S(1)} %collective-permute-done.refs_2_), channel_id=1, source_target_pairs={{0,2},{2,0},{1,3},{3,1},{4,6},{6,4},{5,7},{7,5},{8,10},{10,8},{9,1... | collective-permute-start | bytes 1966088 | tf_op jit(solution)/shard_map/ppermute | solution.py:116
  51.2 26.7 %collective-permute-start.9 = (bf16[320,512]{1,0:T(8,128)(2,1)S(1)}, bf16[320,512]{1,0:T(8,128)(2,1)S(1)}, u32[]{:S(2)}, u32[]{:S(2)}) collective-permute-start(bf16[320,512]{1,0:T(8,128)(2,1)S(1)} %get-tuple-element.39), channel_id=1, source_target_pairs={{0,12},{4,8},{8,4},{12,0},{1,13},{5,9},{9,5},{13,1},{2,14},{6,10},... | collective-permute-start | bytes 983048 | tf_op jit(solution)/shard_map/ppermute | solution.py:116
  64.0 13.9 %collective-permute-start.10 = (bf16[320,512]{1,0:T(8,128)(2,1)S(1)}, bf16[320,512]{1,0:T(8,128)(2,1)S(1)}, u32[]{:S(2)}, u32[]{:S(2)}) collective-permute-start(bf16[320,512]{1,0:T(8,128)(2,1)S(1)} %collective-permute-done.4.refs_9_), channel_id=1, source_target_pairs={{0,16},{16,0},{1,17},{17,1},{2,18},{18,2},{3,19},{19,3},{4,20},{20... | collective-permute-start | bytes 983048 | tf_op jit(solution)/shard_map/ppermute | solution.py:116
  78.9 16.0 %collective-permute-start.11 = (bf16[640,512]{1,0:T(8,128)(2,1)S(1)}, bf16[640,512]{1,0:T(8,128)(2,1)S(1)}, u32[]{:S(2)}, u32[]{:S(2)}) collective-permute-start(bf16[640,512]{1,0:T(8,128)(2,1)S(1)} %collective-permute-done.5.refs_6_), channel_id=1, source_target_pairs={{0,2},{2,0},{1,3},{3,1},{4,6},{6,4},{5,7},{7,5},{8,10},{10,8},{9,1... | collective-permute-start | bytes 1966088 | tf_op jit(solution)/shard_map/ppermute | solution.py:116
  80.4 14.2 %collective-permute-start.12 = (bf16[320,512]{1,0:T(8,128)(2,1)S(1)}, bf16[320,512]{1,0:T(8,128)(2,1)S(1)}, u32[]{:S(2)}, u32[]{:S(2)}) collective-permute-start(bf16[320,512]{1,0:T(8,128)(2,1)S(1)} %collective-permute-done.8.refs_11_), channel_id=1, source_target_pairs={{0,16},{16,0},{1,17},{17,1},{2,18},{18,2},{3,19},{19,3},{4,20},{20... | collective-permute-start | bytes 983048 | tf_op jit(solution)/shard_map/ppermute | solution.py:116
  81.9 12.9 %collective-permute-start.13 = (bf16[320,512]{1,0:T(8,128)(2,1)S(1)}, bf16[320,512]{1,0:T(8,128)(2,1)S(1)}, u32[]{:S(2)}, u32[]{:S(2)}) collective-permute-start(bf16[320,512]{1,0:T(8,128)(2,1)S(1)} %collective-permute-done.9.refs_13_), channel_id=1, source_target_pairs={{0,16},{16,0},{1,17},{17,1},{2,18},{18,2},{3,19},{19,3},{4,20},{20... | collective-permute-start | bytes 983048 | tf_op jit(solution)/shard_map/ppermute | solution.py:116
  82.4 12.0 %collective-permute-start.15 = (bf16[256,512]{1,0:T(8,128)(2,1)S(1)}, bf16[256,512]{1,0:T(8,128)(2,1)S(1)}, u32[]{:S(2)}, u32[]{:S(2)}) collective-permute-start(bf16[256,512]{1,0:T(8,128)(2,1)S(1)} %copy-done.10), channel_id=1, source_target_pairs={{0,8},{4,12},{8,0},{12,4},{1,9},{5,13},{9,1},{13,5},{2,10},{6,14},... | collective-permute-start | bytes 786440 | tf_op jit(solution)/shard_map/ppermute | solution.py:116
  83.5 11.0 %collective-permute-start.14 = (bf16[256,512]{1,0:T(8,128)(2,1)S(1)}, bf16[256,512]{1,0:T(8,128)(2,1)}, u32[]{:S(2)}, u32[]{:S(2)}) collective-permute-start(bf16[256,512]{1,0:T(8,128)(2,1)S(1)} %copy-done.10), channel_id=1, source_target_pairs={{0,4},{4,0},{8,12},{12,8},{1,5},{5,1},{9,13},{13,9},{2,6},{6,2},{1... | collective-permute-start | bytes 786440 | tf_op jit(solution)/shard_map/ppermute | solution.py:116
  98.8 10.7 %collective-permute-start.16 = (f32[1280,256]{1,0:T(8,128)}, f32[1280,256]{1,0:T(8,128)S(1)}, u32[]{:S(2)}, u32[]{:S(2)}) collective-permute-start(f32[1280,256]{1,0:T(8,128)} %get-tuple-element.51), channel_id=1, source_target_pairs={{0,1},{1,0},{2,3},{3,2},{4,5},{5,4},{6,7},{7,6},{8,9},{9,8},{10,11... | collective-permute-start | bytes 3932168 | tf_op jit(solution)/shard_map/ppermute | solution.py:116
  98.9 8.8 %collective-permute-start.17 = (bf16[256,512]{1,0:T(8,128)(2,1)S(1)}, bf16[256,512]{1,0:T(8,128)(2,1)}, u32[]{:S(2)}, u32[]{:S(2)}) collective-permute-start(bf16[256,512]{1,0:T(8,128)(2,1)S(1)} %collective-permute-done.15.refs_16_.refs_7_), channel_id=1, source_target_pairs={{0,4},{4,0},{8,12},{12,8},{1,5},{5,1},{9,13},{13,9},{2,6},{6,2},{1... | collective-permute-start | bytes 786440 | tf_op jit(solution)/shard_map/ppermute | solution.py:116
  99.4 14.5 %collective-permute-start.22 = (bf16[256,512]{1,0:T(8,128)(2,1)S(1)}, bf16[256,512]{1,0:T(8,128)(2,1)}, u32[]{:S(2)}, u32[]{:S(2)}) collective-permute-start(bf16[256,512]{1,0:T(8,128)(2,1)S(1)} %collective-permute-done.15.refs_16_.refs_7_), channel_id=1, source_target_pairs={{0,16},{16,0},{1,17},{17,1},{2,18},{18,2},{3,19},{19,3},{4,20},{20... | collective-permute-start | bytes 786440 | tf_op jit(solution)/shard_map/ppermute | solution.py:116
  101.2 14.8 %collective-permute-start.21 = (bf16[256,512]{1,0:T(8,128)(2,1)}, bf16[256,512]{1,0:T(8,128)(2,1)}, u32[]{:S(2)}, u32[]{:S(2)}) collective-permute-start(bf16[256,512]{1,0:T(8,128)(2,1)} %collective-permute-done.14.refs_15_.refs_5_), channel_id=1, source_target_pairs={{0,16},{16,0},{1,17},{17,1},{2,18},{18,2},{3,19},{19,3},{4,20},{20... | collective-permute-start | bytes 786440 | tf_op jit(solution)/shard_map/ppermute | solution.py:116
  107.7 11.5 %collective-permute-start.23 = (bf16[256,512]{1,0:T(8,128)(2,1)}, bf16[256,512]{1,0:T(8,128)(2,1)}, u32[]{:S(2)}, u32[]{:S(2)}) collective-permute-start(bf16[256,512]{1,0:T(8,128)(2,1)} %collective-permute-done.17.refs_4_.refs_9_), channel_id=1, source_target_pairs={{0,16},{16,0},{1,17},{17,1},{2,18},{18,2},{3,19},{19,3},{4,20},{20... | collective-permute-start | bytes 786440 | tf_op jit(solution)/shard_map/ppermute | solution.py:116
  109.4 10.6 %copy-start.3 = (bf16[512,512]{1,0:T(8,128)(2,1)S(1)}, bf16[512,512]{1,0:T(8,128)(2,1)}, u32[]{:S(2)}) copy-start(bf16[512,512]{1,0:T(8,128)(2,1)} %refs_4_.3) | copy-start | bytes 1572868
  111.6 7.6 %collective-permute-start.18 = (bf16[256,128]{1,0:T(8,128)(2,1)S(1)}, bf16[256,128]{1,0:T(8,128)(2,1)S(1)}, u32[]{:S(2)}, u32[]{:S(2)}) collective-permute-start(bf16[256,128]{1,0:T(8,128)(2,1)S(1)} %get-tuple-element.53), channel_id=1, source_target_pairs={{0,4},{4,0},{8,12},{12,8},{1,5},{5,1},{9,13},{13,9},{2,6},{6,2},{1... | collective-permute-start | bytes 196616 | tf_op jit(solution)/shard_map/ppermute | solution.py:116
  112.1 7.1 %collective-permute-start.19 = (bf16[256,128]{1,0:T(8,128)(2,1)S(1)}, bf16[256,128]{1,0:T(8,128)(2,1)S(1)}, u32[]{:S(2)}, u32[]{:S(2)}) collective-permute-start(bf16[256,128]{1,0:T(8,128)(2,1)S(1)} %get-tuple-element.54), channel_id=1, source_target_pairs={{0,8},{4,12},{8,0},{12,4},{1,9},{5,13},{9,1},{13,5},{2,10},{6,14},... | collective-permute-start | bytes 196616 | tf_op jit(solution)/shard_map/ppermute | solution.py:116
  113.9 6.2 %collective-permute-start.20 = (bf16[256,128]{1,0:T(8,128)(2,1)S(1)}, bf16[256,128]{1,0:T(8,128)(2,1)S(1)}, u32[]{:S(2)}, u32[]{:S(2)}) collective-permute-start(bf16[256,128]{1,0:T(8,128)(2,1)S(1)} %get-tuple-element.55), channel_id=1, source_target_pairs={{0,12},{4,8},{8,4},{12,0},{1,13},{5,9},{9,5},{13,1},{2,14},{6,10},... | collective-permute-start | bytes 196616 | tf_op jit(solution)/shard_map/ppermute | solution.py:116
  120.1 6.4 %copy-start = (bf16[3,192,2048]{2,1,0:T(8,128)(2,1)S(1)}, bf16[3,192,2048]{2,1,0:T(8,128)(2,1)}, u32[]{:S(2)}) copy-start(bf16[3,192,2048]{2,1,0:T(8,128)(2,1)} %refs_1_.2) | copy-start | bytes 7077892
  120.1 6.4 %copy-start.7 = (s32[8]{0:T(128)S(1)}, s32[8]{0:T(128)}, u32[]{:S(2)}) copy-start(s32[8]{0:T(128)} %refs_0_.2) | copy-start | bytes 100
  123.0 2.0 %copy-start.4 = (f32[2,256,512]{2,1,0:T(8,128)}, f32[2,256,512]{2,1,0:T(8,128)S(1)}, u32[]{:S(2)}) copy-start(f32[2,256,512]{2,1,0:T(8,128)S(1)} %get-tuple-element.56) | copy-start | bytes 3145732
  123.0 2.0 %collective-permute-start.24 = (bf16[2,256,512]{2,1,0:T(8,128)(2,1)S(1)}, bf16[2,256,512]{2,1,0:T(8,128)(2,1)S(1)}, u32[]{:S(2)}, u32[]{:S(2)}) collective-permute-start(bf16[2,256,512]{2,1,0:T(8,128)(2,1)S(1)} %get-tuple-element.57), channel_id=1, source_target_pairs={{0,1},{1,0},{2,3},{3,2},{4,5},{5,4},{6,7},{7,6},{8,9},{9,8},{10,11... | collective-permute-start | bytes 1572872 | tf_op jit(solution)/shard_map/ppermute | solution.py:116
  125.0 0.9 copy-start.8
  125.9 8.7 %collective-permute-start.25 = (bf16[256,512]{1,0:T(8,128)(2,1)}, bf16[256,512]{1,0:T(8,128)(2,1)}, u32[]{:S(2)}, u32[]{:S(2)}) collective-permute-start(bf16[256,512]{1,0:T(8,128)(2,1)} %fusion), channel_id=1, source_target_pairs={{0,2},{2,0},{1,3},{3,1},{4,6},{6,4},{5,7},{7,5},{8,10},{10,8},{9,1... | collective-permute-start | bytes 786440 | tf_op jit(solution)/shard_map/ppermute | solution.py:116
  126.4 1.8 %copy-start.5 = (f32[2,256,512]{2,1,0:T(8,128)S(1)}, f32[2,256,512]{2,1,0:T(8,128)}, u32[]{:S(2)}) copy-start(f32[2,256,512]{2,1,0:T(8,128)} %copy-done.4) | copy-start | bytes 3145732

commit v5 on v4

--- a/solution.py
+++ b/solution.py
@@ -122,7 +122,7 @@
 HBM = pl.BlockSpec(memory_space=pltpu.HBM)
 
 
-def kernel_call(body, outs, ins, after=(), scratch=(), smem=(), loose_in=(), limit=14):
+def kernel_call(body, outs, ins, after=(), scratch=(), smem=(), loose_in=(), loose_out=(), limit=14):
     def whole(*refs):
         body(*refs[: len(ins)], *refs[len(ins) + len(after) :])
 
@@ -131,7 +131,7 @@
         whole,
         out_shape=outs,
         in_specs=spots + [ANY] * len(after),
-        out_specs=[VMEM] * len(outs),
+        out_specs=[HBM if i in loose_out else VMEM for i in range(len(outs))],
         scratch_shapes=scratch,
         compiler_params=pltpu.CompilerParams(vmem_limit_bytes=limit * 2**20),
     )(*ins, *after)
@@ -186,6 +186,7 @@
     other_ref,
     half_ref,
     held_ref,
+    made_ref,
     sems,
 ):
     rep_at, mem_at, grp_at = (lax.axis_index(name) for name in ("rep", "mem", "grp"))
@@ -231,11 +232,14 @@
             copies[2 * block + shard].wait()
             taylor_rows(
                 held_ref.at[:, :, pl.ds(shard * width, width)],
-                packed_ref.at[pl.ds(shard * rows, rows)],
+                made_ref.at[pl.ds(shard * rows, rows)],
                 step_ratio,
                 block * step,
                 (block + 1) * step,
             )
+            at = pl.ds(shard * rows + block * step, step)
+            copy(made_ref.at[at], packed_ref.at[at])
+            copies[-1].start()
     for started in copies[2 * blocks :]:
         started.wait()
 
@@ -413,10 +417,12 @@
         [plan, video_cache, audio_tokens, kv_weight, query_weight, out_weight],
         scratch=[
             pltpu.VMEM((3, video_rows, 2 * half_depth), jnp.bfloat16),
-            pltpu.SemaphoreType.DMA((14,)),
+            pltpu.VMEM((2 * video_rows, half_depth), jnp.bfloat16),
+            pltpu.SemaphoreType.DMA((22,)),
         ],
         smem=(0,),
         loose_in=(1, 2, 3, 4, 5),
+        loose_out=(0, 1, 2),
         limit=61,
     )
 
@@ -479,7 +485,6 @@
         attention_body,
         [bfloat(audio_rows, HEAD_DIM)] * 4,
         [frames_video, align_all[:, :, None], keep, came],
-        after=(out_parts[2],),
         scratch=[
             pltpu.VMEM((span, width), jnp.bfloat16),
             pltpu.VMEM((seq_size, audio_rows, HEAD_DIM), jnp.bfloat16),

time: 137 us -> 190 us (1.39)
  Pallas kernels: 15.2 us -> 68.8 us
    pallas_call x5, Pallas kernels: 13.4 us -> 66.9 us  [kernel_call(): pl.pallas_call(whole, out_shape=outs, in_specs=spots + [ANY] * len(after)...]
  transfers between devices with their start and end apart: 26 -> 26, of which waited for: 11 -> 11; matrix products, arithmetic and copies ran while one was open for 1% -> 1% of each run, Pallas kernels for 3% -> 2%
where the time goes in v5:
time: 190 us
  Pallas kernels  68.8 us (36%)
  waiting for transfers between devices  50.9 us (27%)
  blocking collectives  34 us (18%)
  starting transfers between devices  30.9 us (16%)
  other arithmetic  3.98 us (2%)
    pallas_call x5, Pallas kernels, kernel_call(): pl.pallas_call(whole, out_shape=outs, in_specs=spots + [ANY] * len(after)...  66.9 us
    ppermute x26, waiting for transfers between devices, swap(): return lax.ppermute(value, axis, [(i, i ^ bit) for i in range(size)])  50.9 us
    all_to_all x1, blocking collectives, by_head(): lax.all_to_all(jnp.broadcast_to(alignment[None], (seq_size, audio_rows)),...  34 us
    ppermute x26, starting transfers between devices, swap(): return lax.ppermute(value, axis, [(i, i ^ bit) for i in range(size)])  30.9 us
  transfers between devices with their start and end apart: 26, of which 11 were waited for; matrix products, arithmetic and copies ran while one was open for 1% of the time, Pallas kernels for 2%

profile of v5, /device:TPU:0, one launch (start us, length us, event | category | flops | bytes accessed | tf_op | source)
XLA Modules:
  0.0 189.8 jit_solution(12746378240039421819)
XLA Ops:
  0.6 57.7 %shard_map.87 = (bf16[640,512]{1,0:T(8,128)(2,1)}, bf16[640,1024]{1,0:T(8,128)(2,1)}, bf16[256,512]{1,0:T(8,128)(2,1)}) custom-call(s32[8]{0:T(128)} %refs_0_.2, bf16[3,192,2048]{2,1,0:T(8,128)(2,1)} %refs_1_.2, bf16[256,2048]{1,0:T(8,128)(2,1)} %refs_2_.1, bf16[1024,1024]{1,0:T(8,128)(2,1)} %refs_0_.3, bf16[512,512]{1,0:T(8,128)(2,1)} %refs_1_.3, ...), custom_call_target="tpu_custom_call" | custom-call | tf_op jit(solution)/shard_map/pallas_call | solution.py:130
  58.4 0.5 collective-permute-start.3
  58.9 2.7 %collective-permute-start = (bf16[640,512]{1,0:T(8,128)(2,1)}, bf16[640,512]{1,0:T(8,128)(2,1)S(1)}, u32[]{:S(2)}, u32[]{:S(2)}) collective-permute-start(bf16[640,512]{1,0:T(8,128)(2,1)} %get-tuple-element.31.refs_0_), channel_id=1, source_target_pairs={{0,4},{4,0},{8,12},{12,8},{1,5},{5,1},{9,13},{13,9},{2,6},{6,2},{1... | collective-permute-start | bytes 1966088 | tf_op jit(solution)/shard_map/ppermute | solution.py:116
  61.6 2.6 %collective-permute-start.1 = (bf16[640,512]{1,0:T(8,128)(2,1)}, bf16[640,512]{1,0:T(8,128)(2,1)S(1)}, u32[]{:S(2)}, u32[]{:S(2)}) collective-permute-start(bf16[640,512]{1,0:T(8,128)(2,1)} %get-tuple-element.31.refs_0_), channel_id=1, source_target_pairs={{0,8},{4,12},{8,0},{12,4},{1,9},{5,13},{9,1},{13,5},{2,10},{6,14},... | collective-permute-start | bytes 1966088 | tf_op jit(solution)/shard_map/ppermute | solution.py:116
  64.2 1.5 collective-permute-start.2
  65.7 0.3 shard_map.88
  65.9 0.5 collective-permute-start.4
  66.5 34.0 %all_to_all.6 = s32[4,1,256]{2,1,0:T(1,128)S(1)} all-to-all(s32[4,1,256]{2,1,0:T(1,128)S(1)} %broadcast_in_dim.4), channel_id=1, replica_groups=mesh['grp'=2,'seq'=4,'mem'=2,'rep'=2] {'seq'}, dimensions={0} | all-to-all | bytes 8192 | tf_op jit(solution)/shard_map/all_to_all | solution.py:439
  100.5 0.6 collective-permute-start.8
  101.1 1.6 collective-permute-start.5
  102.7 1.5 collective-permute-start.7
  104.2 0.5 collective-permute-start.6
  104.8 2.2 %collective-permute-start.9 = (bf16[320,512]{1,0:T(8,128)(2,1)S(1)}, bf16[320,512]{1,0:T(8,128)(2,1)S(1)}, u32[]{:S(2)}, u32[]{:S(2)}) collective-permute-start(bf16[320,512]{1,0:T(8,128)(2,1)S(1)} %get-tuple-element.39), channel_id=1, source_target_pairs={{0,12},{4,8},{8,4},{12,0},{1,13},{5,9},{9,5},{13,1},{2,14},{6,10},... | collective-permute-start | bytes 983048 | tf_op jit(solution)/shard_map/ppermute | solution.py:116
  107.0 10.5 %collective-permute-done.8.refs_11_ = bf16[320,512]{1,0:T(8,128)(2,1)S(1)} collective-permute-done((bf16[320,512]{1,0:T(8,128)(2,1)S(1)}, bf16[320,512]{1,0:T(8,128)(2,1)S(1)}, u32[]{:S(2)}, u32[]{:S(2)}) %collective-permute-start.8) | collective-permute-done | bytes 327712 | tf_op jit(solution)/shard_map/ppermute | solution.py:116
  117.5 1.5 collective-permute-start.10
  119.1 12.4 %collective-permute-done.9.refs_13_ = bf16[320,512]{1,0:T(8,128)(2,1)S(1)} collective-permute-done((bf16[320,512]{1,0:T(8,128)(2,1)S(1)}, bf16[320,512]{1,0:T(8,128)(2,1)S(1)}, u32[]{:S(2)}, u32[]{:S(2)}) %collective-permute-start.9) | collective-permute-done | bytes 327712 | tf_op jit(solution)/shard_map/ppermute | solution.py:116
  131.5 1.0 collective-permute-done.6.refs_3_
  132.4 1.5 collective-permute-start.11
  133.9 1.5 collective-permute-start.12
  135.5 0.5 collective-permute-start.13
  136.0 1.1 collective-permute-start.15
  137.1 1.4 collective-permute-start.14
  138.5 9.5 %collective-permute-done.15.refs_16_.refs_7_ = bf16[256,512]{1,0:T(8,128)(2,1)S(1)} collective-permute-done((bf16[256,512]{1,0:T(8,128)(2,1)S(1)}, bf16[256,512]{1,0:T(8,128)(2,1)S(1)}, u32[]{:S(2)}, u32[]{:S(2)}) %collective-permute-start.15) | collective-permute-done | bytes 262176 | tf_op jit(solution)/shard_map/ppermute | solution.py:116
  148.0 0.1 collective-permute-done.14.refs_15_.refs_5_
  148.1 0.3 collective-permute-done.13.refs_14_
  148.4 3.9 %shard_map.89 = (f32[1280,256]{1,0:T(8,128)}, f32[1280,256]{1,0:T(8,128)S(1)}) custom-call(bf16[640,512]{1,0:T(8,128)(2,1)S(1)} %copy-done.6, bf16[640,512]{1,0:T(8,128)(2,1)S(1)} %collective-permute-done.2.refs_1_, bf16[640,512]{1,0:T(8,128)(2,1)S(1)} %collective-permute-done.refs_2_, bf16[640,512]{1,0:T(8,128)(2,1)S(1)} %collective-permute-done.6.refs_3_, ...), custom_call_target="tpu_custom_call" | custom-call | tf_op jit(solution)/shard_map/pallas_call | solution.py:130
  152.4 0.5 collective-permute-start.22
  153.0 1.5 collective-permute-start.21
  154.6 0.1 div.18
  154.7 0.1 reshape.123
  154.7 0.5 collective-permute-start.20
  155.2 6.0 %collective-permute-done.22.refs_9_ = bf16[256,512]{1,0:T(8,128)(2,1)} collective-permute-done((bf16[256,512]{1,0:T(8,128)(2,1)S(1)}, bf16[256,512]{1,0:T(8,128)(2,1)}, u32[]{:S(2)}, u32[]{:S(2)}) %collective-permute-start.22) | collective-permute-done | bytes 262176 | tf_op jit(solution)/shard_map/ppermute | solution.py:116
  161.2 1.5 collective-permute-start.23
  162.8 0.2 copy.10.refs_1_
  163.0 2.1 %shard_map.90 = (bf16[256,128]{1,0:T(8,128)(2,1)S(1)}, bf16[256,128]{1,0:T(8,128)(2,1)S(1)}, bf16[256,128]{1,0:T(8,128)(2,1)S(1)}, bf16[256,128]{1,0:T(8,128)(2,1)S(1)}) custom-call(f32[1,768]{1,0:T(1,128)S(1)} %fusion.3.refs_0_, f32[4,256,1]{2,1,0:T(8,128)S(1)} %copy.10.refs_1_, f32[1280,256]{1,0:T(8,128)S(1)} %get-tuple-element.50.refs_2_, ...), custom_call_target="tpu_custom_call" | custom-call | tf_op jit(solution)/shard_map/pallas_call | solution.py:130
  165.1 0.6 collective-permute-start.17
  165.7 1.8 collective-permute-start.18
  167.4 2.1 %collective-permute-start.19 = (bf16[256,128]{1,0:T(8,128)(2,1)S(1)}, bf16[256,128]{1,0:T(8,128)(2,1)S(1)}, u32[]{:S(2)}, u32[]{:S(2)}) collective-permute-start(bf16[256,128]{1,0:T(8,128)(2,1)S(1)} %get-tuple-element.55), channel_id=1, source_target_pairs={{0,12},{4,8},{8,4},{12,0},{1,13},{5,9},{9,5},{13,1},{2,14},{6,10},... | collective-permute-start | bytes 196616 | tf_op jit(solution)/shard_map/ppermute | solution.py:116
  169.6 3.2 %collective-permute-done.23.refs_10_ = bf16[256,512]{1,0:T(8,128)(2,1)} collective-permute-done((bf16[256,512]{1,0:T(8,128)(2,1)}, bf16[256,512]{1,0:T(8,128)(2,1)}, u32[]{:S(2)}, u32[]{:S(2)}) %collective-permute-start.23) | collective-permute-done | bytes 262176 | tf_op jit(solution)/shard_map/ppermute | solution.py:116
  172.7 0.9 collective-permute-done.19.refs_3_
  173.6 2.9 %shard_map.91 = (bf16[2,256,512]{2,1,0:T(8,128)(2,1)S(1)}, f32[2,256,512]{2,1,0:T(8,128)S(1)}) custom-call(bf16[256,128]{1,0:T(8,128)(2,1)S(1)} %get-tuple-element.52.refs_0_, bf16[256,128]{1,0:T(8,128)(2,1)S(1)} %collective-permute-done.17.refs_1_, bf16[256,128]{1,0:T(8,128)(2,1)S(1)} %collective-permute-done.18.refs_2_, ...), custom_call_target="tpu_custom_call" | custom-call | tf_op jit(solution)/shard_map/pallas_call | solution.py:130
  176.6 1.9 collective-permute-done.24
  178.5 0.9 fusion
  179.4 0.5 collective-permute-start.25
  180.0 1.8 shard_map.86
  181.8 1.1 bitcast_add_fusion
  183.0 5.1 %collective-permute-done.25 = bf16[256,512]{1,0:T(8,128)(2,1)} collective-permute-done((bf16[256,512]{1,0:T(8,128)(2,1)}, bf16[256,512]{1,0:T(8,128)(2,1)}, u32[]{:S(2)}, u32[]{:S(2)}) %collective-permute-start.25) | collective-permute-done | bytes 262176 | tf_op jit(solution)/shard_map/ppermute | solution.py:116
  188.1 1.7 add_convert_fusion
  (46 shorter events, 0.4 us)
Async XLA Ops:
  0.6 65.1 %copy-start.2 = (bf16[512,512]{1,0:T(8,128)(2,1)S(1)}, bf16[512,512]{1,0:T(8,128)(2,1)}, u32[]{:S(2)}) copy-start(bf16[512,512]{1,0:T(8,128)(2,1)} %refs_1_.3) | copy-start | bytes 1572868
  0.6 65.1 %copy-start.1 = (bf16[1024,1024]{1,0:T(8,128)(2,1)S(1)}, bf16[1024,1024]{1,0:T(8,128)(2,1)}, u32[]{:S(2)}) copy-start(bf16[1024,1024]{1,0:T(8,128)(2,1)} %refs_0_.3) | copy-start | bytes 6291460
  58.4 7.3 %collective-permute-start.3 = (bf16[640,1024]{1,0:T(8,128)(2,1)}, bf16[640,1024]{1,0:T(8,128)(2,1)S(1)}, u32[]{:S(2)}, u32[]{:S(2)}) collective-permute-start(bf16[640,1024]{1,0:T(8,128)(2,1)} %get-tuple-element.32), channel_id=1, source_target_pairs={{0,1},{1,0},{2,3},{3,2},{4,5},{5,4},{6,7},{7,6},{8,9},{9,8},{10,11... | collective-permute-start | bytes 3932168 | tf_op jit(solution)/shard_map/ppermute | solution.py:116
  58.9 7.5 %copy-start.9 = (s32[256]{0:T(256)S(1)}, s32[256]{0:T(256)}, u32[]{:S(2)}) copy-start(s32[256]{0:T(256)} %param.9) | copy-start | bytes 3076
  58.9 77.0 %copy-start.10 = (bf16[256,512]{1,0:T(8,128)(2,1)S(1)}, bf16[256,512]{1,0:T(8,128)(2,1)}, u32[]{:S(2)}) copy-start(bf16[256,512]{1,0:T(8,128)(2,1)} %get-tuple-element.49) | copy-start | bytes 786436
  58.9 89.5 %copy-start.6 = (bf16[640,512]{1,0:T(8,128)(2,1)S(1)}, bf16[640,512]{1,0:T(8,128)(2,1)}, u32[]{:S(2)}) copy-start(bf16[640,512]{1,0:T(8,128)(2,1)} %get-tuple-element.31.refs_0_) | copy-start | bytes 1966084
  58.9 42.2 %collective-permute-start = (bf16[640,512]{1,0:T(8,128)(2,1)}, bf16[640,512]{1,0:T(8,128)(2,1)S(1)}, u32[]{:S(2)}, u32[]{:S(2)}) collective-permute-start(bf16[640,512]{1,0:T(8,128)(2,1)} %get-tuple-element.31.refs_0_), channel_id=1, source_target_pairs={{0,4},{4,0},{8,12},{12,8},{1,5},{5,1},{9,13},{13,9},{2,6},{6,2},{1... | collective-permute-start | bytes 1966088 | tf_op jit(solution)/shard_map/ppermute | solution.py:116
  61.6 39.5 %collective-permute-start.1 = (bf16[640,512]{1,0:T(8,128)(2,1)}, bf16[640,512]{1,0:T(8,128)(2,1)S(1)}, u32[]{:S(2)}, u32[]{:S(2)}) collective-permute-start(bf16[640,512]{1,0:T(8,128)(2,1)} %get-tuple-element.31.refs_0_), channel_id=1, source_target_pairs={{0,8},{4,12},{8,0},{12,4},{1,9},{5,13},{9,1},{13,5},{2,10},{6,14},... | collective-permute-start | bytes 1966088 | tf_op jit(solution)/shard_map/ppermute | solution.py:116
  64.2 36.9 %collective-permute-start.2 = (bf16[640,512]{1,0:T(8,128)(2,1)}, bf16[640,512]{1,0:T(8,128)(2,1)S(1)}, u32[]{:S(2)}, u32[]{:S(2)}) collective-permute-start(bf16[640,512]{1,0:T(8,128)(2,1)} %get-tuple-element.31.refs_0_), channel_id=1, source_target_pairs={{0,2},{2,0},{1,3},{3,1},{4,6},{6,4},{5,7},{7,5},{8,10},{10,8},{9,1... | collective-permute-start | bytes 1966088 | tf_op jit(solution)/shard_map/ppermute | solution.py:116
  65.9 35.2 %collective-permute-start.4 = (bf16[320,512]{1,0:T(8,128)(2,1)S(1)}, bf16[320,512]{1,0:T(8,128)(2,1)S(1)}, u32[]{:S(2)}, u32[]{:S(2)}) collective-permute-start(bf16[320,512]{1,0:T(8,128)(2,1)S(1)} %get-tuple-element.33), channel_id=1, source_target_pairs={{0,4},{4,0},{8,12},{12,8},{1,5},{5,1},{9,13},{13,9},{2,6},{6,2},{1... | collective-permute-start | bytes 983048 | tf_op jit(solution)/shard_map/ppermute | solution.py:116
  100.5 17.0 %collective-permute-start.8 = (bf16[320,512]{1,0:T(8,128)(2,1)S(1)}, bf16[320,512]{1,0:T(8,128)(2,1)S(1)}, u32[]{:S(2)}, u32[]{:S(2)}) collective-permute-start(bf16[320,512]{1,0:T(8,128)(2,1)S(1)} %get-tuple-element.38), channel_id=1, source_target_pairs={{0,8},{4,12},{8,0},{12,4},{1,9},{5,13},{9,1},{13,5},{2,10},{6,14},... | collective-permute-start | bytes 983048 | tf_op jit(solution)/shard_map/ppermute | solution.py:116
  101.1 30.4 %collective-permute-start.5 = (bf16[640,512]{1,0:T(8,128)(2,1)S(1)}, bf16[640,512]{1,0:T(8,128)(2,1)S(1)}, u32[]{:S(2)}, u32[]{:S(2)}) collective-permute-start(bf16[640,512]{1,0:T(8,128)(2,1)S(1)} %collective-permute-done.1.refs_4_), channel_id=1, source_target_pairs={{0,4},{4,0},{8,12},{12,8},{1,5},{5,1},{9,13},{13,9},{2,6},{6,2},{1... | collective-permute-start | bytes 1966088 | tf_op jit(solution)/shard_map/ppermute | solution.py:116
  102.7 28.8 %collective-permute-start.7 = (bf16[640,512]{1,0:T(8,128)(2,1)S(1)}, bf16[640,512]{1,0:T(8,128)(2,1)S(1)}, u32[]{:S(2)}, u32[]{:S(2)}) collective-permute-start(bf16[640,512]{1,0:T(8,128)(2,1)S(1)} %collective-permute-done.1.refs_4_), channel_id=1, source_target_pairs={{0,2},{2,0},{1,3},{3,1},{4,6},{6,4},{5,7},{7,5},{8,10},{10,8},{9,1... | collective-permute-start | bytes 1966088 | tf_op jit(solution)/shard_map/ppermute | solution.py:116
  104.2 28.2 %collective-permute-start.6 = (bf16[640,512]{1,0:T(8,128)(2,1)S(1)}, bf16[640,512]{1,0:T(8,128)(2,1)S(1)}, u32[]{:S(2)}, u32[]{:S(2)}) collective-permute-start(bf16[640,512]{1,0:T(8,128)(2,1)S(1)} %collective-permute-done.refs_2_), channel_id=1, source_target_pairs={{0,2},{2,0},{1,3},{3,1},{4,6},{6,4},{5,7},{7,5},{8,10},{10,8},{9,1... | collective-permute-start | bytes 1966088 | tf_op jit(solution)/shard_map/ppermute | solution.py:116
  104.8 26.7 %collective-permute-start.9 = (bf16[320,512]{1,0:T(8,128)(2,1)S(1)}, bf16[320,512]{1,0:T(8,128)(2,1)S(1)}, u32[]{:S(2)}, u32[]{:S(2)}) collective-permute-start(bf16[320,512]{1,0:T(8,128)(2,1)S(1)} %get-tuple-element.39), channel_id=1, source_target_pairs={{0,12},{4,8},{8,4},{12,0},{1,13},{5,9},{9,5},{13,1},{2,14},{6,10},... | collective-permute-start | bytes 983048 | tf_op jit(solution)/shard_map/ppermute | solution.py:116
  117.5 13.9 %collective-permute-start.10 = (bf16[320,512]{1,0:T(8,128)(2,1)S(1)}, bf16[320,512]{1,0:T(8,128)(2,1)S(1)}, u32[]{:S(2)}, u32[]{:S(2)}) collective-permute-start(bf16[320,512]{1,0:T(8,128)(2,1)S(1)} %collective-permute-done.4.refs_9_), channel_id=1, source_target_pairs={{0,16},{16,0},{1,17},{17,1},{2,18},{18,2},{3,19},{19,3},{4,20},{20... | collective-permute-start | bytes 983048 | tf_op jit(solution)/shard_map/ppermute | solution.py:116
  132.4 16.0 %collective-permute-start.11 = (bf16[640,512]{1,0:T(8,128)(2,1)S(1)}, bf16[640,512]{1,0:T(8,128)(2,1)S(1)}, u32[]{:S(2)}, u32[]{:S(2)}) collective-permute-start(bf16[640,512]{1,0:T(8,128)(2,1)S(1)} %collective-permute-done.5.refs_6_), channel_id=1, source_target_pairs={{0,2},{2,0},{1,3},{3,1},{4,6},{6,4},{5,7},{7,5},{8,10},{10,8},{9,1... | collective-permute-start | bytes 1966088 | tf_op jit(solution)/shard_map/ppermute | solution.py:116
  133.9 14.2 %collective-permute-start.12 = (bf16[320,512]{1,0:T(8,128)(2,1)S(1)}, bf16[320,512]{1,0:T(8,128)(2,1)S(1)}, u32[]{:S(2)}, u32[]{:S(2)}) collective-permute-start(bf16[320,512]{1,0:T(8,128)(2,1)S(1)} %collective-permute-done.8.refs_11_), channel_id=1, source_target_pairs={{0,16},{16,0},{1,17},{17,1},{2,18},{18,2},{3,19},{19,3},{4,20},{20... | collective-permute-start | bytes 983048 | tf_op jit(solution)/shard_map/ppermute | solution.py:116
  135.5 12.9 %collective-permute-start.13 = (bf16[320,512]{1,0:T(8,128)(2,1)S(1)}, bf16[320,512]{1,0:T(8,128)(2,1)S(1)}, u32[]{:S(2)}, u32[]{:S(2)}) collective-permute-start(bf16[320,512]{1,0:T(8,128)(2,1)S(1)} %collective-permute-done.9.refs_13_), channel_id=1, source_target_pairs={{0,16},{16,0},{1,17},{17,1},{2,18},{18,2},{3,19},{19,3},{4,20},{20... | collective-permute-start | bytes 983048 | tf_op jit(solution)/shard_map/ppermute | solution.py:116
  136.0 12.0 %collective-permute-start.15 = (bf16[256,512]{1,0:T(8,128)(2,1)S(1)}, bf16[256,512]{1,0:T(8,128)(2,1)S(1)}, u32[]{:S(2)}, u32[]{:S(2)}) collective-permute-start(bf16[256,512]{1,0:T(8,128)(2,1)S(1)} %copy-done.10), channel_id=1, source_target_pairs={{0,8},{4,12},{8,0},{12,4},{1,9},{5,13},{9,1},{13,5},{2,10},{6,14},... | collective-permute-start | bytes 786440 | tf_op jit(solution)/shard_map/ppermute | solution.py:116
  137.1 11.0 %collective-permute-start.14 = (bf16[256,512]{1,0:T(8,128)(2,1)S(1)}, bf16[256,512]{1,0:T(8,128)(2,1)}, u32[]{:S(2)}, u32[]{:S(2)}) collective-permute-start(bf16[256,512]{1,0:T(8,128)(2,1)S(1)} %copy-done.10), channel_id=1, source_target_pairs={{0,4},{4,0},{8,12},{12,8},{1,5},{5,1},{9,13},{13,9},{2,6},{6,2},{1... | collective-permute-start | bytes 786440 | tf_op jit(solution)/shard_map/ppermute | solution.py:116
  152.3 10.7 %collective-permute-start.16 = (f32[1280,256]{1,0:T(8,128)}, f32[1280,256]{1,0:T(8,128)S(1)}, u32[]{:S(2)}, u32[]{:S(2)}) collective-permute-start(f32[1280,256]{1,0:T(8,128)} %get-tuple-element.51), channel_id=1, source_target_pairs={{0,1},{1,0},{2,3},{3,2},{4,5},{5,4},{6,7},{7,6},{8,9},{9,8},{10,11... | collective-permute-start | bytes 3932168 | tf_op jit(solution)/shard_map/ppermute | solution.py:116
  152.4 8.8 %collective-permute-start.22 = (bf16[256,512]{1,0:T(8,128)(2,1)S(1)}, bf16[256,512]{1,0:T(8,128)(2,1)}, u32[]{:S(2)}, u32[]{:S(2)}) collective-permute-start(bf16[256,512]{1,0:T(8,128)(2,1)S(1)} %collective-permute-done.15.refs_16_.refs_7_), channel_id=1, source_target_pairs={{0,4},{4,0},{8,12},{12,8},{1,5},{5,1},{9,13},{13,9},{2,6},{6,2},{1... | collective-permute-start | bytes 786440 | tf_op jit(solution)/shard_map/ppermute | solution.py:116
  153.0 14.5 %collective-permute-start.21 = (bf16[256,512]{1,0:T(8,128)(2,1)S(1)}, bf16[256,512]{1,0:T(8,128)(2,1)}, u32[]{:S(2)}, u32[]{:S(2)}) collective-permute-start(bf16[256,512]{1,0:T(8,128)(2,1)S(1)} %collective-permute-done.15.refs_16_.refs_7_), channel_id=1, source_target_pairs={{0,16},{16,0},{1,17},{17,1},{2,18},{18,2},{3,19},{19,3},{4,20},{20... | collective-permute-start | bytes 786440 | tf_op jit(solution)/shard_map/ppermute | solution.py:116
  154.7 14.8 %collective-permute-start.20 = (bf16[256,512]{1,0:T(8,128)(2,1)}, bf16[256,512]{1,0:T(8,128)(2,1)}, u32[]{:S(2)}, u32[]{:S(2)}) collective-permute-start(bf16[256,512]{1,0:T(8,128)(2,1)} %collective-permute-done.14.refs_15_.refs_5_), channel_id=1, source_target_pairs={{0,16},{16,0},{1,17},{17,1},{2,18},{18,2},{3,19},{19,3},{4,20},{20... | collective-permute-start | bytes 786440 | tf_op jit(solution)/shard_map/ppermute | solution.py:116
  161.2 11.5 %collective-permute-start.23 = (bf16[256,512]{1,0:T(8,128)(2,1)}, bf16[256,512]{1,0:T(8,128)(2,1)}, u32[]{:S(2)}, u32[]{:S(2)}) collective-permute-start(bf16[256,512]{1,0:T(8,128)(2,1)} %collective-permute-done.22.refs_9_), channel_id=1, source_target_pairs={{0,16},{16,0},{1,17},{17,1},{2,18},{18,2},{3,19},{19,3},{4,20},{20... | collective-permute-start | bytes 786440 | tf_op jit(solution)/shard_map/ppermute | solution.py:116
  163.0 10.6 %copy-start.3 = (bf16[512,512]{1,0:T(8,128)(2,1)S(1)}, bf16[512,512]{1,0:T(8,128)(2,1)}, u32[]{:S(2)}) copy-start(bf16[512,512]{1,0:T(8,128)(2,1)} %refs_4_.3) | copy-start | bytes 1572868
  165.1 7.6 %collective-permute-start.17 = (bf16[256,128]{1,0:T(8,128)(2,1)S(1)}, bf16[256,128]{1,0:T(8,128)(2,1)S(1)}, u32[]{:S(2)}, u32[]{:S(2)}) collective-permute-start(bf16[256,128]{1,0:T(8,128)(2,1)S(1)} %get-tuple-element.53), channel_id=1, source_target_pairs={{0,4},{4,0},{8,12},{12,8},{1,5},{5,1},{9,13},{13,9},{2,6},{6,2},{1... | collective-permute-start | bytes 196616 | tf_op jit(solution)/shard_map/ppermute | solution.py:116
  165.7 7.1 %collective-permute-start.18 = (bf16[256,128]{1,0:T(8,128)(2,1)S(1)}, bf16[256,128]{1,0:T(8,128)(2,1)S(1)}, u32[]{:S(2)}, u32[]{:S(2)}) collective-permute-start(bf16[256,128]{1,0:T(8,128)(2,1)S(1)} %get-tuple-element.54), channel_id=1, source_target_pairs={{0,8},{4,12},{8,0},{12,4},{1,9},{5,13},{9,1},{13,5},{2,10},{6,14},... | collective-permute-start | bytes 196616 | tf_op jit(solution)/shard_map/ppermute | solution.py:116
  167.4 6.2 %collective-permute-start.19 = (bf16[256,128]{1,0:T(8,128)(2,1)S(1)}, bf16[256,128]{1,0:T(8,128)(2,1)S(1)}, u32[]{:S(2)}, u32[]{:S(2)}) collective-permute-start(bf16[256,128]{1,0:T(8,128)(2,1)S(1)} %get-tuple-element.55), channel_id=1, source_target_pairs={{0,12},{4,8},{8,4},{12,0},{1,13},{5,9},{9,5},{13,1},{2,14},{6,10},... | collective-permute-start | bytes 196616 | tf_op jit(solution)/shard_map/ppermute | solution.py:116
  173.6 6.4 %copy-start = (bf16[3,192,2048]{2,1,0:T(8,128)(2,1)S(1)}, bf16[3,192,2048]{2,1,0:T(8,128)(2,1)}, u32[]{:S(2)}) copy-start(bf16[3,192,2048]{2,1,0:T(8,128)(2,1)} %refs_1_.2) | copy-start | bytes 7077892
  173.6 6.4 %copy-start.7 = (s32[8]{0:T(128)S(1)}, s32[8]{0:T(128)}, u32[]{:S(2)}) copy-start(s32[8]{0:T(128)} %refs_0_.2) | copy-start | bytes 100
  176.5 2.0 %copy-start.4 = (f32[2,256,512]{2,1,0:T(8,128)}, f32[2,256,512]{2,1,0:T(8,128)S(1)}, u32[]{:S(2)}) copy-start(f32[2,256,512]{2,1,0:T(8,128)S(1)} %get-tuple-element.56) | copy-start | bytes 3145732
  176.6 2.0 %collective-permute-start.24 = (bf16[2,256,512]{2,1,0:T(8,128)(2,1)S(1)}, bf16[2,256,512]{2,1,0:T(8,128)(2,1)S(1)}, u32[]{:S(2)}, u32[]{:S(2)}) collective-permute-start(bf16[2,256,512]{2,1,0:T(8,128)(2,1)S(1)} %get-tuple-element.57), channel_id=1, source_target_pairs={{0,1},{1,0},{2,3},{3,2},{4,5},{5,4},{6,7},{7,6},{8,9},{9,8},{10,11... | collective-permute-start | bytes 1572872 | tf_op jit(solution)/shard_map/ppermute | solution.py:116
  178.5 0.9 copy-start.8
  179.4 8.7 %collective-permute-start.25 = (bf16[256,512]{1,0:T(8,128)(2,1)}, bf16[256,512]{1,0:T(8,128)(2,1)}, u32[]{:S(2)}, u32[]{:S(2)}) collective-permute-start(bf16[256,512]{1,0:T(8,128)(2,1)} %fusion), channel_id=1, source_target_pairs={{0,2},{2,0},{1,3},{3,1},{4,6},{6,4},{5,7},{7,5},{8,10},{10,8},{9,1... | collective-permute-start | bytes 786440 | tf_op jit(solution)/shard_map/ppermute | solution.py:116
  180.0 1.8 copy-start.5

commit v6 on v5

--- a/solution.py
+++ b/solution.py
@@ -187,6 +187,8 @@
     half_ref,
     held_ref,
     made_ref,
+    other_vmem,
+    half_vmem,
     sems,
 ):
     rep_at, mem_at, grp_at = (lax.axis_index(name) for name in ("rep", "mem", "grp"))
@@ -213,17 +215,17 @@
     for shard in range(2):
         copy(
             audio_ref.at[:, part(2 * (2 * mem_at + shard) + rep_at, lane)],
-            packed_ref.at[pl.ds(2 * rows, audio_ref.shape[0]), pl.ds(shard * lane, lane)],
+            made_ref.at[pl.ds(2 * rows, audio_ref.shape[0]), pl.ds(shard * lane, lane)],
         )
     depth, columns = kv_ref.shape[0] // 2, query_ref.shape[1]
-    copy(kv_ref.at[part(1 - rep_at, depth)], other_ref.at[pl.ds(0, depth)])
+    copy(kv_ref.at[part(1 - rep_at, depth)], other_vmem.at[pl.ds(0, depth)])
     quarter = query_ref.shape[0] // 4
     for side in range(2):
         copy(
             query_ref.at[part(2 * (1 - rep_at) + side, quarter)],
-            other_ref.at[pl.ds(depth, quarter), pl.ds(side * columns, columns)],
-        )
-    copy(out_w.at[part(grp_at, half_ref.shape[0])], half_ref)
+            other_vmem.at[pl.ds(depth, quarter), pl.ds(side * columns, columns)],
+        )
+    copy(out_w.at[part(grp_at, half_ref.shape[0])], half_vmem)
     for started in copies:
         started.start()
     step_ratio = plan_ratio(plan_ref, width)
@@ -240,8 +242,21 @@
             at = pl.ds(shard * rows + block * step, step)
             copy(made_ref.at[at], packed_ref.at[at])
             copies[-1].start()
-    for started in copies[2 * blocks :]:
-        started.wait()
+    audio_at = pl.ds(2 * rows, audio_ref.shape[0])
+    stages = (
+        (2, made_ref.at[audio_at], packed_ref.at[audio_at]),
+        (3, other_vmem, other_ref),
+        (1, half_vmem, half_ref),
+    )
+    at = 2 * blocks
+    for count, source, target in stages:
+        for arriving in copies[at : at + count]:
+            arriving.wait()
+        at += count
+        copy(source, target)
+        copies[-1].start()
+    for leaving in copies[at:]:
+        leaving.wait()
 
 
 def weight_body(kv_ref, query_ref, other_ref, own_ref, *piece_refs):
@@ -417,8 +432,10 @@
         [plan, video_cache, audio_tokens, kv_weight, query_weight, out_weight],
         scratch=[
             pltpu.VMEM((3, video_rows, 2 * half_depth), jnp.bfloat16),
-            pltpu.VMEM((2 * video_rows, half_depth), jnp.bfloat16),
-            pltpu.SemaphoreType.DMA((22,)),
+            pltpu.VMEM((2 * video_rows + audio_rows, half_depth), jnp.bfloat16),
+            pltpu.VMEM((half_depth + query_quarter, kv_weight.shape[1]), jnp.bfloat16),
+            pltpu.VMEM((out_weight.shape[0] // 2, out_weight.shape[1]), jnp.bfloat16),
+            pltpu.SemaphoreType.DMA((25,)),
         ],
         smem=(0,),
         loose_in=(1, 2, 3, 4, 5),
@@ -465,7 +482,7 @@
         products_body,
         [sums, sums],
         [value for pair in zip(tokens, across) for value in pair] + weights,
-        after=out_parts,
+        after=out_parts[:1],
         scratch=[
             pltpu.VMEM((seq_size * video_rows, 4 * half_depth), jnp.bfloat16),
             pltpu.VMEM((seq_size * audio_rows, 8 * query_quarter), jnp.bfloat16),
@@ -474,8 +491,9 @@
         ],
         limit=26,
     )
+    out_parts.append(swap(out_parts[1], "seq", 1))
+    send, out_parts[2] = lax.optimization_barrier((send, out_parts[2]))
     came = swap(send, "rep", 1)
-    out_parts.append(swap(out_parts[1], "seq", 1))
 
     span = video_rows * seq_size
     blocks = jnp.stack([seq_at, seq_at ^ 1, seq_at ^ 2, seq_at ^ 3])

time: 190 us -> 138 us (0.73)
  Pallas kernels: 68.8 us -> 15 us
  waiting for transfers between devices: 50.9 us -> 53.2 us
    pallas_call x5, Pallas kernels: 66.9 us -> 13.2 us  [kernel_call(): pl.pallas_call(whole, out_shape=outs, in_specs=spots + [ANY] * len(after)...]
    ppermute x26, waiting for transfers between devices: 50.9 us -> 53.2 us  [swap(): return lax.ppermute(value, axis, [(i, i ^ bit) for i in range(size)])]
  transfers between devices with their start and end apart: 26 -> 26, of which waited for: 11 -> 12; matrix products, arithmetic and copies ran while one was open for 1% -> 1% of each run, Pallas kernels for 2% -> 6%
where the time goes in v6:
time: 138 us; the launch traced here: 137 us
  waiting for transfers between devices  53.2 us (39%)
  blocking collectives  34 us (25%)
  starting transfers between devices  29.9 us (22%)
  Pallas kernels  15 us (11%)
  other arithmetic  3.99 us (3%)
    ppermute x26, waiting for transfers between devices, swap(): return lax.ppermute(value, axis, [(i, i ^ bit) for i in range(size)])  53.2 us
    all_to_all x1, blocking collectives, by_head(): lax.all_to_all(jnp.broadcast_to(alignment[None], (seq_size, audio_rows)),...  34 us
    ppermute x26, starting transfers between devices, swap(): return lax.ppermute(value, axis, [(i, i ^ bit) for i in range(size)])  29.9 us
    pallas_call x5, Pallas kernels, kernel_call(): pl.pallas_call(whole, out_shape=outs, in_specs=spots + [ANY] * len(after)...  13.2 us
  transfers between devices with their start and end apart: 26, of which 12 were waited for; matrix products, arithmetic and copies ran while one was open for 1% of the time, Pallas kernels for 6%

profile of v6, /device:TPU:0, one launch (start us, length us, event | category | flops | bytes accessed | tf_op | source)
XLA Modules:
  0.0 137.4 jit_solution(10640055044674223892)
XLA Ops:
  0.6 4.0 %shard_map.87 = (bf16[640,512]{1,0:T(8,128)(2,1)}, bf16[640,1024]{1,0:T(8,128)(2,1)}, bf16[256,512]{1,0:T(8,128)(2,1)}) custom-call(s32[8]{0:T(128)} %refs_0_.2, bf16[3,192,2048]{2,1,0:T(8,128)(2,1)} %refs_1_.2, bf16[256,2048]{1,0:T(8,128)(2,1)} %refs_2_.1, bf16[1024,1024]{1,0:T(8,128)(2,1)} %refs_0_.3, bf16[512,512]{1,0:T(8,128)(2,1)} %refs_1_.3, ...), custom_call_target="tpu_custom_call" | custom-call | tf_op jit(solution)/shard_map/pallas_call | solution.py:130
  4.7 0.5 collective-permute-start.3
  5.2 2.7 %collective-permute-start = (bf16[640,512]{1,0:T(8,128)(2,1)}, bf16[640,512]{1,0:T(8,128)(2,1)S(1)}, u32[]{:S(2)}, u32[]{:S(2)}) collective-permute-start(bf16[640,512]{1,0:T(8,128)(2,1)} %get-tuple-element.33.refs_0_), channel_id=1, source_target_pairs={{0,4},{4,0},{8,12},{12,8},{1,5},{5,1},{9,13},{13,9},{2,6},{6,2},{1... | collective-permute-start | bytes 1966088 | tf_op jit(solution)/shard_map/ppermute | solution.py:116
  7.9 2.6 %collective-permute-start.1 = (bf16[640,512]{1,0:T(8,128)(2,1)}, bf16[640,512]{1,0:T(8,128)(2,1)S(1)}, u32[]{:S(2)}, u32[]{:S(2)}) collective-permute-start(bf16[640,512]{1,0:T(8,128)(2,1)} %get-tuple-element.33.refs_0_), channel_id=1, source_target_pairs={{0,8},{4,12},{8,0},{12,4},{1,9},{5,13},{9,1},{13,5},{2,10},{6,14},... | collective-permute-start | bytes 1966088 | tf_op jit(solution)/shard_map/ppermute | solution.py:116
  10.4 1.5 %collective-permute-start.2 = (bf16[640,512]{1,0:T(8,128)(2,1)}, bf16[640,512]{1,0:T(8,128)(2,1)S(1)}, u32[]{:S(2)}, u32[]{:S(2)}) collective-permute-start(bf16[640,512]{1,0:T(8,128)(2,1)} %get-tuple-element.33.refs_0_), channel_id=1, source_target_pairs={{0,2},{2,0},{1,3},{3,1},{4,6},{6,4},{5,7},{7,5},{8,10},{10,8},{9,1... | collective-permute-start | bytes 1966088 | tf_op jit(solution)/shard_map/ppermute | solution.py:116
  11.9 0.3 shard_map.88
  12.2 0.5 collective-permute-start.4
  12.7 34.0 %all_to_all.6 = s32[4,1,256]{2,1,0:T(1,128)S(1)} all-to-all(s32[4,1,256]{2,1,0:T(1,128)S(1)} %broadcast_in_dim.4), channel_id=1, replica_groups=mesh['grp'=2,'seq'=4,'mem'=2,'rep'=2] {'seq'}, dimensions={0} | all-to-all | bytes 8192 | tf_op jit(solution)/shard_map/all_to_all | solution.py:456
  46.7 0.6 collective-permute-start.8
  47.4 1.6 %collective-permute-start.5 = (bf16[640,512]{1,0:T(8,128)(2,1)S(1)}, bf16[640,512]{1,0:T(8,128)(2,1)S(1)}, u32[]{:S(2)}, u32[]{:S(2)}) collective-permute-start(bf16[640,512]{1,0:T(8,128)(2,1)S(1)} %collective-permute-done.1.refs_4_), channel_id=1, source_target_pairs={{0,4},{4,0},{8,12},{12,8},{1,5},{5,1},{9,13},{13,9},{2,6},{6,2},{1... | collective-permute-start | bytes 1966088 | tf_op jit(solution)/shard_map/ppermute | solution.py:116
  49.0 1.5 %collective-permute-start.7 = (bf16[640,512]{1,0:T(8,128)(2,1)S(1)}, bf16[640,512]{1,0:T(8,128)(2,1)S(1)}, u32[]{:S(2)}, u32[]{:S(2)}) collective-permute-start(bf16[640,512]{1,0:T(8,128)(2,1)S(1)} %collective-permute-done.1.refs_4_), channel_id=1, source_target_pairs={{0,2},{2,0},{1,3},{3,1},{4,6},{6,4},{5,7},{7,5},{8,10},{10,8},{9,1... | collective-permute-start | bytes 1966088 | tf_op jit(solution)/shard_map/ppermute | solution.py:116
  50.5 0.5 collective-permute-start.6
  51.0 2.2 %collective-permute-start.9 = (bf16[320,512]{1,0:T(8,128)(2,1)S(1)}, bf16[320,512]{1,0:T(8,128)(2,1)S(1)}, u32[]{:S(2)}, u32[]{:S(2)}) collective-permute-start(bf16[320,512]{1,0:T(8,128)(2,1)S(1)} %get-tuple-element.41), channel_id=1, source_target_pairs={{0,12},{4,8},{8,4},{12,0},{1,13},{5,9},{9,5},{13,1},{2,14},{6,10},... | collective-permute-start | bytes 983048 | tf_op jit(solution)/shard_map/ppermute | solution.py:116
  53.2 10.5 %collective-permute-done.8.refs_11_ = bf16[320,512]{1,0:T(8,128)(2,1)S(1)} collective-permute-done((bf16[320,512]{1,0:T(8,128)(2,1)S(1)}, bf16[320,512]{1,0:T(8,128)(2,1)S(1)}, u32[]{:S(2)}, u32[]{:S(2)}) %collective-permute-start.8) | collective-permute-done | bytes 327712 | tf_op jit(solution)/shard_map/ppermute | solution.py:116
  63.8 1.5 %collective-permute-start.10 = (bf16[320,512]{1,0:T(8,128)(2,1)S(1)}, bf16[320,512]{1,0:T(8,128)(2,1)S(1)}, u32[]{:S(2)}, u32[]{:S(2)}) collective-permute-start(bf16[320,512]{1,0:T(8,128)(2,1)S(1)} %collective-permute-done.4.refs_9_), channel_id=1, source_target_pairs={{0,16},{16,0},{1,17},{17,1},{2,18},{18,2},{3,19},{19,3},{4,20},{20... | collective-permute-start | bytes 983048 | tf_op jit(solution)/shard_map/ppermute | solution.py:116
  65.3 12.4 %collective-permute-done.9.refs_13_ = bf16[320,512]{1,0:T(8,128)(2,1)S(1)} collective-permute-done((bf16[320,512]{1,0:T(8,128)(2,1)S(1)}, bf16[320,512]{1,0:T(8,128)(2,1)S(1)}, u32[]{:S(2)}, u32[]{:S(2)}) %collective-permute-start.9) | collective-permute-done | bytes 327712 | tf_op jit(solution)/shard_map/ppermute | solution.py:116
  77.7 1.0 collective-permute-done.6.refs_3_
  78.7 1.5 %collective-permute-start.11 = (bf16[640,512]{1,0:T(8,128)(2,1)S(1)}, bf16[640,512]{1,0:T(8,128)(2,1)S(1)}, u32[]{:S(2)}, u32[]{:S(2)}) collective-permute-start(bf16[640,512]{1,0:T(8,128)(2,1)S(1)} %collective-permute-done.5.refs_6_), channel_id=1, source_target_pairs={{0,2},{2,0},{1,3},{3,1},{4,6},{6,4},{5,7},{7,5},{8,10},{10,8},{9,1... | collective-permute-start | bytes 1966088 | tf_op jit(solution)/shard_map/ppermute | solution.py:116
  80.2 1.1 collective-permute-start.15
  81.3 1.5 %collective-permute-start.12 = (bf16[320,512]{1,0:T(8,128)(2,1)S(1)}, bf16[320,512]{1,0:T(8,128)(2,1)S(1)}, u32[]{:S(2)}, u32[]{:S(2)}) collective-permute-start(bf16[320,512]{1,0:T(8,128)(2,1)S(1)} %collective-permute-done.8.refs_11_), channel_id=1, source_target_pairs={{0,16},{16,0},{1,17},{17,1},{2,18},{18,2},{3,19},{19,3},{4,20},{20... | collective-permute-start | bytes 983048 | tf_op jit(solution)/shard_map/ppermute | solution.py:116
  82.8 0.5 collective-permute-start.13
  83.3 1.4 %collective-permute-start.14 = (bf16[256,512]{1,0:T(8,128)(2,1)S(1)}, bf16[256,512]{1,0:T(8,128)(2,1)S(1)}, u32[]{:S(2)}, u32[]{:S(2)}) collective-permute-start(bf16[256,512]{1,0:T(8,128)(2,1)S(1)} %copy-done.10), channel_id=1, source_target_pairs={{0,4},{4,0},{8,12},{12,8},{1,5},{5,1},{9,13},{13,9},{2,6},{6,2},{1... | collective-permute-start | bytes 786440 | tf_op jit(solution)/shard_map/ppermute | solution.py:116
  84.7 8.1 %collective-permute-done.15.refs_7_ = bf16[256,512]{1,0:T(8,128)(2,1)} collective-permute-done((bf16[256,512]{1,0:T(8,128)(2,1)S(1)}, bf16[256,512]{1,0:T(8,128)(2,1)}, u32[]{:S(2)}, u32[]{:S(2)}) %collective-permute-start.15) | collective-permute-done | bytes 262176 | tf_op jit(solution)/shard_map/ppermute | solution.py:116
  92.8 1.0 collective-permute-done.14.refs_15_.refs_5_
  93.8 1.4 %collective-permute-done.13.refs_14_ = bf16[320,512]{1,0:T(8,128)(2,1)S(1)} collective-permute-done((bf16[320,512]{1,0:T(8,128)(2,1)S(1)}, bf16[320,512]{1,0:T(8,128)(2,1)S(1)}, u32[]{:S(2)}, u32[]{:S(2)}) %collective-permute-start.13) | collective-permute-done | bytes 327712 | tf_op jit(solution)/shard_map/ppermute | solution.py:116
  95.2 3.9 %shard_map.89 = (f32[1280,256]{1,0:T(8,128)}, f32[1280,256]{1,0:T(8,128)S(1)}) custom-call(bf16[640,512]{1,0:T(8,128)(2,1)S(1)} %copy-done.6, bf16[640,512]{1,0:T(8,128)(2,1)S(1)} %collective-permute-done.2.refs_1_, bf16[640,512]{1,0:T(8,128)(2,1)S(1)} %collective-permute-done.refs_2_, bf16[640,512]{1,0:T(8,128)(2,1)S(1)} %collective-permute-done.6.refs_3_, ...), custom_call_target="tpu_custom_call" | custom-call | tf_op jit(solution)/shard_map/pallas_call | solution.py:130
  99.2 1.8 %collective-permute-done.16.refs_9_ = bf16[256,512]{1,0:T(8,128)(2,1)} collective-permute-done((bf16[256,512]{1,0:T(8,128)(2,1)}, bf16[256,512]{1,0:T(8,128)(2,1)}, u32[]{:S(2)}, u32[]{:S(2)}) %collective-permute-start.16) | collective-permute-done | bytes 262176 | tf_op jit(solution)/shard_map/ppermute | solution.py:116
  101.1 1.5 %collective-permute-start.21 = (bf16[256,512]{1,0:T(8,128)(2,1)S(1)}, bf16[256,512]{1,0:T(8,128)(2,1)}, u32[]{:S(2)}, u32[]{:S(2)}) collective-permute-start(bf16[256,512]{1,0:T(8,128)(2,1)S(1)} %collective-permute-done.14.refs_15_.refs_5_), channel_id=1, source_target_pairs={{0,16},{16,0},{1,17},{17,1},{2,18},{18,2},{3,19},{19,3},{4,20},{20... | collective-permute-start | bytes 786440 | tf_op jit(solution)/shard_map/ppermute | solution.py:116
  102.7 0.1 div.18
  102.8 0.1 reshape.123
  102.9 0.5 collective-permute-start.22
  103.4 1.5 %collective-permute-start.23 = (bf16[256,512]{1,0:T(8,128)(2,1)}, bf16[256,512]{1,0:T(8,128)(2,1)}, u32[]{:S(2)}, u32[]{:S(2)}) collective-permute-start(bf16[256,512]{1,0:T(8,128)(2,1)} %collective-permute-done.16.refs_9_), channel_id=1, source_target_pairs={{0,16},{16,0},{1,17},{17,1},{2,18},{18,2},{3,19},{19,3},{4,20},{20... | collective-permute-start | bytes 786440 | tf_op jit(solution)/shard_map/ppermute | solution.py:116
  104.9 0.2 copy.10.refs_1_
  105.2 2.1 %shard_map.90 = (bf16[256,128]{1,0:T(8,128)(2,1)S(1)}, bf16[256,128]{1,0:T(8,128)(2,1)S(1)}, bf16[256,128]{1,0:T(8,128)(2,1)S(1)}, bf16[256,128]{1,0:T(8,128)(2,1)S(1)}) custom-call(f32[1,768]{1,0:T(1,128)S(1)} %fusion.3.refs_0_, f32[4,256,1]{2,1,0:T(8,128)S(1)} %copy.10.refs_1_, f32[1280,256]{1,0:T(8,128)S(1)} %get-tuple-element.52.refs_2_, ...), custom_call_target="tpu_custom_call" | custom-call | tf_op jit(solution)/shard_map/pallas_call | solution.py:130
  107.3 0.3 collective-permute-start.18
  107.6 1.9 %collective-permute-start.19 = (bf16[256,128]{1,0:T(8,128)(2,1)S(1)}, bf16[256,128]{1,0:T(8,128)(2,1)S(1)}, u32[]{:S(2)}, u32[]{:S(2)}) collective-permute-start(bf16[256,128]{1,0:T(8,128)(2,1)S(1)} %get-tuple-element.57), channel_id=1, source_target_pairs={{0,8},{4,12},{8,0},{12,4},{1,9},{5,13},{9,1},{13,5},{2,10},{6,14},... | collective-permute-start | bytes 196616 | tf_op jit(solution)/shard_map/ppermute | solution.py:116
  109.5 0.8 collective-permute-done.21.refs_6_
  110.3 1.6 %collective-permute-start.20 = (bf16[256,128]{1,0:T(8,128)(2,1)S(1)}, bf16[256,128]{1,0:T(8,128)(2,1)S(1)}, u32[]{:S(2)}, u32[]{:S(2)}) collective-permute-start(bf16[256,128]{1,0:T(8,128)(2,1)S(1)} %get-tuple-element.58), channel_id=1, source_target_pairs={{0,12},{4,8},{8,4},{12,0},{1,13},{5,9},{9,5},{13,1},{2,14},{6,10},... | collective-permute-start | bytes 196616 | tf_op jit(solution)/shard_map/ppermute | solution.py:116
  111.9 4.0 %collective-permute-done.22.refs_8_ = bf16[256,512]{1,0:T(8,128)(2,1)} collective-permute-done((bf16[256,512]{1,0:T(8,128)(2,1)}, bf16[256,512]{1,0:T(8,128)(2,1)}, u32[]{:S(2)}, u32[]{:S(2)}) %collective-permute-start.22) | collective-permute-done | bytes 262176 | tf_op jit(solution)/shard_map/ppermute | solution.py:116
  115.9 5.2 %collective-permute-done.23.refs_10_ = bf16[256,512]{1,0:T(8,128)(2,1)} collective-permute-done((bf16[256,512]{1,0:T(8,128)(2,1)}, bf16[256,512]{1,0:T(8,128)(2,1)}, u32[]{:S(2)}, u32[]{:S(2)}) %collective-permute-start.23) | collective-permute-done | bytes 262176 | tf_op jit(solution)/shard_map/ppermute | solution.py:116
  121.2 2.9 %shard_map.91 = (bf16[2,256,512]{2,1,0:T(8,128)(2,1)S(1)}, f32[2,256,512]{2,1,0:T(8,128)S(1)}) custom-call(bf16[256,128]{1,0:T(8,128)(2,1)S(1)} %get-tuple-element.55.refs_0_, bf16[256,128]{1,0:T(8,128)(2,1)S(1)} %collective-permute-done.18.refs_1_, bf16[256,128]{1,0:T(8,128)(2,1)S(1)} %collective-permute-done.19.refs_2_, ...), custom_call_target="tpu_custom_call" | custom-call | tf_op jit(solution)/shard_map/pallas_call | solution.py:130
  124.2 1.9 %collective-permute-done.24 = bf16[2,256,512]{2,1,0:T(8,128)(2,1)S(1)} collective-permute-done((bf16[2,256,512]{2,1,0:T(8,128)(2,1)S(1)}, bf16[2,256,512]{2,1,0:T(8,128)(2,1)S(1)}, u32[]{:S(2)}, u32[]{:S(2)}) %collective-permute-start.24) | collective-permute-done | bytes 524320 | tf_op jit(solution)/shard_map/ppermute | solution.py:116
  126.1 0.9 fusion
  127.0 0.5 collective-permute-start.25
  127.6 1.8 %shard_map.86 = bf16[192,2048]{1,0:T(8,128)(2,1)} custom-call(s32[8]{0:T(128)S(1)} %copy-done.7, bf16[3,192,2048]{2,1,0:T(8,128)(2,1)S(1)} %copy-done), custom_call_target="tpu_custom_call" | custom-call | tf_op jit(solution)/shard_map/pallas_call | solution.py:168
  129.4 1.1 bitcast_add_fusion
  130.5 5.2 %collective-permute-done.25 = bf16[256,512]{1,0:T(8,128)(2,1)} collective-permute-done((bf16[256,512]{1,0:T(8,128)(2,1)}, bf16[256,512]{1,0:T(8,128)(2,1)}, u32[]{:S(2)}, u32[]{:S(2)}) %collective-permute-start.25) | collective-permute-done | bytes 262176 | tf_op jit(solution)/shard_map/ppermute | solution.py:116
  135.7 1.7 %add_convert_fusion = bf16[256,512]{1,0:T(8,128)(2,1)} fusion(f32[256,512]{1,0:T(8,128)S(1)} %bitcast_add_fusion, bf16[256,512]{1,0:T(8,128)(2,1)} %collective-permute-done.25), kind=kLoop, calls=%fused_computation.1 | loop fusion | flops 393216 | bytes 1048576 | tf_op jit(solution)/shard_map/convert_element_type | solution.py:539
  (46 shorter events, 0.4 us)
Async XLA Ops:
  0.6 11.3 %copy-start.2 = (bf16[512,512]{1,0:T(8,128)(2,1)S(1)}, bf16[512,512]{1,0:T(8,128)(2,1)}, u32[]{:S(2)}) copy-start(bf16[512,512]{1,0:T(8,128)(2,1)} %refs_1_.3) | copy-start | bytes 1572868
  0.6 11.3 %copy-start.1 = (bf16[1024,1024]{1,0:T(8,128)(2,1)S(1)}, bf16[1024,1024]{1,0:T(8,128)(2,1)}, u32[]{:S(2)}) copy-start(bf16[1024,1024]{1,0:T(8,128)(2,1)} %refs_0_.3) | copy-start | bytes 6291460
  4.7 7.3 %collective-permute-start.3 = (bf16[640,1024]{1,0:T(8,128)(2,1)}, bf16[640,1024]{1,0:T(8,128)(2,1)S(1)}, u32[]{:S(2)}, u32[]{:S(2)}) collective-permute-start(bf16[640,1024]{1,0:T(8,128)(2,1)} %get-tuple-element.34), channel_id=1, source_target_pairs={{0,1},{1,0},{2,3},{3,2},{4,5},{5,4},{6,7},{7,6},{8,9},{9,8},{10,11... | collective-permute-start | bytes 3932168 | tf_op jit(solution)/shard_map/ppermute | solution.py:116
  5.2 7.5 %copy-start.9 = (s32[256]{0:T(256)S(1)}, s32[256]{0:T(256)}, u32[]{:S(2)}) copy-start(s32[256]{0:T(256)} %param.9) | copy-start | bytes 3076
  5.2 75.0 %copy-start.10 = (bf16[256,512]{1,0:T(8,128)(2,1)S(1)}, bf16[256,512]{1,0:T(8,128)(2,1)}, u32[]{:S(2)}) copy-start(bf16[256,512]{1,0:T(8,128)(2,1)} %get-tuple-element.51) | copy-start | bytes 786436
  5.2 90.1 %copy-start.6 = (bf16[640,512]{1,0:T(8,128)(2,1)S(1)}, bf16[640,512]{1,0:T(8,128)(2,1)}, u32[]{:S(2)}) copy-start(bf16[640,512]{1,0:T(8,128)(2,1)} %get-tuple-element.33.refs_0_) | copy-start | bytes 1966084
  5.2 42.2 %collective-permute-start = (bf16[640,512]{1,0:T(8,128)(2,1)}, bf16[640,512]{1,0:T(8,128)(2,1)S(1)}, u32[]{:S(2)}, u32[]{:S(2)}) collective-permute-start(bf16[640,512]{1,0:T(8,128)(2,1)} %get-tuple-element.33.refs_0_), channel_id=1, source_target_pairs={{0,4},{4,0},{8,12},{12,8},{1,5},{5,1},{9,13},{13,9},{2,6},{6,2},{1... | collective-permute-start | bytes 1966088 | tf_op jit(solution)/shard_map/ppermute | solution.py:116
  7.9 39.5 %collective-permute-start.1 = (bf16[640,512]{1,0:T(8,128)(2,1)}, bf16[640,512]{1,0:T(8,128)(2,1)S(1)}, u32[]{:S(2)}, u32[]{:S(2)}) collective-permute-start(bf16[640,512]{1,0:T(8,128)(2,1)} %get-tuple-element.33.refs_0_), channel_id=1, source_target_pairs={{0,8},{4,12},{8,0},{12,4},{1,9},{5,13},{9,1},{13,5},{2,10},{6,14},... | collective-permute-start | bytes 1966088 | tf_op jit(solution)/shard_map/ppermute | solution.py:116
  10.4 36.9 %collective-permute-start.2 = (bf16[640,512]{1,0:T(8,128)(2,1)}, bf16[640,512]{1,0:T(8,128)(2,1)S(1)}, u32[]{:S(2)}, u32[]{:S(2)}) collective-permute-start(bf16[640,512]{1,0:T(8,128)(2,1)} %get-tuple-element.33.refs_0_), channel_id=1, source_target_pairs={{0,2},{2,0},{1,3},{3,1},{4,6},{6,4},{5,7},{7,5},{8,10},{10,8},{9,1... | collective-permute-start | bytes 1966088 | tf_op jit(solution)/shard_map/ppermute | solution.py:116
  12.2 35.2 %collective-permute-start.4 = (bf16[320,512]{1,0:T(8,128)(2,1)S(1)}, bf16[320,512]{1,0:T(8,128)(2,1)S(1)}, u32[]{:S(2)}, u32[]{:S(2)}) collective-permute-start(bf16[320,512]{1,0:T(8,128)(2,1)S(1)} %get-tuple-element.35), channel_id=1, source_target_pairs={{0,4},{4,0},{8,12},{12,8},{1,5},{5,1},{9,13},{13,9},{2,6},{6,2},{1... | collective-permute-start | bytes 983048 | tf_op jit(solution)/shard_map/ppermute | solution.py:116
  46.7 17.0 %collective-permute-start.8 = (bf16[320,512]{1,0:T(8,128)(2,1)S(1)}, bf16[320,512]{1,0:T(8,128)(2,1)S(1)}, u32[]{:S(2)}, u32[]{:S(2)}) collective-permute-start(bf16[320,512]{1,0:T(8,128)(2,1)S(1)} %get-tuple-element.40), channel_id=1, source_target_pairs={{0,8},{4,12},{8,0},{12,4},{1,9},{5,13},{9,1},{13,5},{2,10},{6,14},... | collective-permute-start | bytes 983048 | tf_op jit(solution)/shard_map/ppermute | solution.py:116
  47.4 30.4 %collective-permute-start.5 = (bf16[640,512]{1,0:T(8,128)(2,1)S(1)}, bf16[640,512]{1,0:T(8,128)(2,1)S(1)}, u32[]{:S(2)}, u32[]{:S(2)}) collective-permute-start(bf16[640,512]{1,0:T(8,128)(2,1)S(1)} %collective-permute-done.1.refs_4_), channel_id=1, source_target_pairs={{0,4},{4,0},{8,12},{12,8},{1,5},{5,1},{9,13},{13,9},{2,6},{6,2},{1... | collective-permute-start | bytes 1966088 | tf_op jit(solution)/shard_map/ppermute | solution.py:116
  49.0 28.8 %collective-permute-start.7 = (bf16[640,512]{1,0:T(8,128)(2,1)S(1)}, bf16[640,512]{1,0:T(8,128)(2,1)S(1)}, u32[]{:S(2)}, u32[]{:S(2)}) collective-permute-start(bf16[640,512]{1,0:T(8,128)(2,1)S(1)} %collective-permute-done.1.refs_4_), channel_id=1, source_target_pairs={{0,2},{2,0},{1,3},{3,1},{4,6},{6,4},{5,7},{7,5},{8,10},{10,8},{9,1... | collective-permute-start | bytes 1966088 | tf_op jit(solution)/shard_map/ppermute | solution.py:116
  50.5 28.2 %collective-permute-start.6 = (bf16[640,512]{1,0:T(8,128)(2,1)S(1)}, bf16[640,512]{1,0:T(8,128)(2,1)S(1)}, u32[]{:S(2)}, u32[]{:S(2)}) collective-permute-start(bf16[640,512]{1,0:T(8,128)(2,1)S(1)} %collective-permute-done.refs_2_), channel_id=1, source_target_pairs={{0,2},{2,0},{1,3},{3,1},{4,6},{6,4},{5,7},{7,5},{8,10},{10,8},{9,1... | collective-permute-start | bytes 1966088 | tf_op jit(solution)/shard_map/ppermute | solution.py:116
  51.0 26.7 %collective-permute-start.9 = (bf16[320,512]{1,0:T(8,128)(2,1)S(1)}, bf16[320,512]{1,0:T(8,128)(2,1)S(1)}, u32[]{:S(2)}, u32[]{:S(2)}) collective-permute-start(bf16[320,512]{1,0:T(8,128)(2,1)S(1)} %get-tuple-element.41), channel_id=1, source_target_pairs={{0,12},{4,8},{8,4},{12,0},{1,13},{5,9},{9,5},{13,1},{2,14},{6,10},... | collective-permute-start | bytes 983048 | tf_op jit(solution)/shard_map/ppermute | solution.py:116
  63.8 13.9 %collective-permute-start.10 = (bf16[320,512]{1,0:T(8,128)(2,1)S(1)}, bf16[320,512]{1,0:T(8,128)(2,1)S(1)}, u32[]{:S(2)}, u32[]{:S(2)}) collective-permute-start(bf16[320,512]{1,0:T(8,128)(2,1)S(1)} %collective-permute-done.4.refs_9_), channel_id=1, source_target_pairs={{0,16},{16,0},{1,17},{17,1},{2,18},{18,2},{3,19},{19,3},{4,20},{20... | collective-permute-start | bytes 983048 | tf_op jit(solution)/shard_map/ppermute | solution.py:116
  78.7 16.5 %collective-permute-start.11 = (bf16[640,512]{1,0:T(8,128)(2,1)S(1)}, bf16[640,512]{1,0:T(8,128)(2,1)S(1)}, u32[]{:S(2)}, u32[]{:S(2)}) collective-permute-start(bf16[640,512]{1,0:T(8,128)(2,1)S(1)} %collective-permute-done.5.refs_6_), channel_id=1, source_target_pairs={{0,2},{2,0},{1,3},{3,1},{4,6},{6,4},{5,7},{7,5},{8,10},{10,8},{9,1... | collective-permute-start | bytes 1966088 | tf_op jit(solution)/shard_map/ppermute | solution.py:116
  80.2 12.6 %collective-permute-start.15 = (bf16[256,512]{1,0:T(8,128)(2,1)S(1)}, bf16[256,512]{1,0:T(8,128)(2,1)}, u32[]{:S(2)}, u32[]{:S(2)}) collective-permute-start(bf16[256,512]{1,0:T(8,128)(2,1)S(1)} %copy-done.10), channel_id=1, source_target_pairs={{0,8},{4,12},{8,0},{12,4},{1,9},{5,13},{9,1},{13,5},{2,10},{6,14},... | collective-permute-start | bytes 786440 | tf_op jit(solution)/shard_map/ppermute | solution.py:116
  81.3 12.5 %collective-permute-start.12 = (bf16[320,512]{1,0:T(8,128)(2,1)S(1)}, bf16[320,512]{1,0:T(8,128)(2,1)S(1)}, u32[]{:S(2)}, u32[]{:S(2)}) collective-permute-start(bf16[320,512]{1,0:T(8,128)(2,1)S(1)} %collective-permute-done.8.refs_11_), channel_id=1, source_target_pairs={{0,16},{16,0},{1,17},{17,1},{2,18},{18,2},{3,19},{19,3},{4,20},{20... | collective-permute-start | bytes 983048 | tf_op jit(solution)/shard_map/ppermute | solution.py:116
  82.8 12.4 %collective-permute-start.13 = (bf16[320,512]{1,0:T(8,128)(2,1)S(1)}, bf16[320,512]{1,0:T(8,128)(2,1)S(1)}, u32[]{:S(2)}, u32[]{:S(2)}) collective-permute-start(bf16[320,512]{1,0:T(8,128)(2,1)S(1)} %collective-permute-done.9.refs_13_), channel_id=1, source_target_pairs={{0,16},{16,0},{1,17},{17,1},{2,18},{18,2},{3,19},{19,3},{4,20},{20... | collective-permute-start | bytes 983048 | tf_op jit(solution)/shard_map/ppermute | solution.py:116
  83.3 10.5 %collective-permute-start.14 = (bf16[256,512]{1,0:T(8,128)(2,1)S(1)}, bf16[256,512]{1,0:T(8,128)(2,1)S(1)}, u32[]{:S(2)}, u32[]{:S(2)}) collective-permute-start(bf16[256,512]{1,0:T(8,128)(2,1)S(1)} %copy-done.10), channel_id=1, source_target_pairs={{0,4},{4,0},{8,12},{12,8},{1,5},{5,1},{9,13},{13,9},{2,6},{6,2},{1... | collective-permute-start | bytes 786440 | tf_op jit(solution)/shard_map/ppermute | solution.py:116
  92.8 8.1 %collective-permute-start.16 = (bf16[256,512]{1,0:T(8,128)(2,1)}, bf16[256,512]{1,0:T(8,128)(2,1)}, u32[]{:S(2)}, u32[]{:S(2)}) collective-permute-start(bf16[256,512]{1,0:T(8,128)(2,1)} %collective-permute-done.15.refs_7_), channel_id=1, source_target_pairs={{0,4},{4,0},{8,12},{12,8},{1,5},{5,1},{9,13},{13,9},{2,6},{6,2},{1... | collective-permute-start | bytes 786440 | tf_op jit(solution)/shard_map/ppermute | solution.py:116
  100.9 4.2 %collective-permute-start.17 = (f32[1280,256]{1,0:T(8,128)}, f32[1280,256]{1,0:T(8,128)S(1)}, u32[]{:S(2)}, u32[]{:S(2)}) collective-permute-start(f32[1280,256]{1,0:T(8,128)} %get-tuple-element.54), channel_id=1, source_target_pairs={{0,1},{1,0},{2,3},{3,2},{4,5},{5,4},{6,7},{7,6},{8,9},{9,8},{10,11... | collective-permute-start | bytes 3932168 | tf_op jit(solution)/shard_map/ppermute | solution.py:116
  101.1 9.2 %collective-permute-start.21 = (bf16[256,512]{1,0:T(8,128)(2,1)S(1)}, bf16[256,512]{1,0:T(8,128)(2,1)}, u32[]{:S(2)}, u32[]{:S(2)}) collective-permute-start(bf16[256,512]{1,0:T(8,128)(2,1)S(1)} %collective-permute-done.14.refs_15_.refs_5_), channel_id=1, source_target_pairs={{0,16},{16,0},{1,17},{17,1},{2,18},{18,2},{3,19},{19,3},{4,20},{20... | collective-permute-start | bytes 786440 | tf_op jit(solution)/shard_map/ppermute | solution.py:116
  102.9 13.0 %collective-permute-start.22 = (bf16[256,512]{1,0:T(8,128)(2,1)}, bf16[256,512]{1,0:T(8,128)(2,1)}, u32[]{:S(2)}, u32[]{:S(2)}) collective-permute-start(bf16[256,512]{1,0:T(8,128)(2,1)} %collective-permute-done.15.refs_7_), channel_id=1, source_target_pairs={{0,16},{16,0},{1,17},{17,1},{2,18},{18,2},{3,19},{19,3},{4,20},{20... | collective-permute-start | bytes 786440 | tf_op jit(solution)/shard_map/ppermute | solution.py:116
  103.4 17.8 %collective-permute-start.23 = (bf16[256,512]{1,0:T(8,128)(2,1)}, bf16[256,512]{1,0:T(8,128)(2,1)}, u32[]{:S(2)}, u32[]{:S(2)}) collective-permute-start(bf16[256,512]{1,0:T(8,128)(2,1)} %collective-permute-done.16.refs_9_), channel_id=1, source_target_pairs={{0,16},{16,0},{1,17},{17,1},{2,18},{18,2},{3,19},{19,3},{4,20},{20... | collective-permute-start | bytes 786440 | tf_op jit(solution)/shard_map/ppermute | solution.py:116
  105.1 16.0 %copy-start.3 = (bf16[512,512]{1,0:T(8,128)(2,1)S(1)}, bf16[512,512]{1,0:T(8,128)(2,1)}, u32[]{:S(2)}) copy-start(bf16[512,512]{1,0:T(8,128)(2,1)} %refs_4_.3) | copy-start | bytes 1572868
  107.3 13.9 %collective-permute-start.18 = (bf16[256,128]{1,0:T(8,128)(2,1)S(1)}, bf16[256,128]{1,0:T(8,128)(2,1)S(1)}, u32[]{:S(2)}, u32[]{:S(2)}) collective-permute-start(bf16[256,128]{1,0:T(8,128)(2,1)S(1)} %get-tuple-element.56), channel_id=1, source_target_pairs={{0,4},{4,0},{8,12},{12,8},{1,5},{5,1},{9,13},{13,9},{2,6},{6,2},{1... | collective-permute-start | bytes 196616 | tf_op jit(solution)/shard_map/ppermute | solution.py:116
  107.6 13.5 %collective-permute-start.19 = (bf16[256,128]{1,0:T(8,128)(2,1)S(1)}, bf16[256,128]{1,0:T(8,128)(2,1)S(1)}, u32[]{:S(2)}, u32[]{:S(2)}) collective-permute-start(bf16[256,128]{1,0:T(8,128)(2,1)S(1)} %get-tuple-element.57), channel_id=1, source_target_pairs={{0,8},{4,12},{8,0},{12,4},{1,9},{5,13},{9,1},{13,5},{2,10},{6,14},... | collective-permute-start | bytes 196616 | tf_op jit(solution)/shard_map/ppermute | solution.py:116
  110.3 10.9 %collective-permute-start.20 = (bf16[256,128]{1,0:T(8,128)(2,1)S(1)}, bf16[256,128]{1,0:T(8,128)(2,1)S(1)}, u32[]{:S(2)}, u32[]{:S(2)}) collective-permute-start(bf16[256,128]{1,0:T(8,128)(2,1)S(1)} %get-tuple-element.58), channel_id=1, source_target_pairs={{0,12},{4,8},{8,4},{12,0},{1,13},{5,9},{9,5},{13,1},{2,14},{6,10},... | collective-permute-start | bytes 196616 | tf_op jit(solution)/shard_map/ppermute | solution.py:116
  121.2 6.4 %copy-start = (bf16[3,192,2048]{2,1,0:T(8,128)(2,1)S(1)}, bf16[3,192,2048]{2,1,0:T(8,128)(2,1)}, u32[]{:S(2)}) copy-start(bf16[3,192,2048]{2,1,0:T(8,128)(2,1)} %refs_1_.2) | copy-start | bytes 7077892
  121.2 6.4 %copy-start.7 = (s32[8]{0:T(128)S(1)}, s32[8]{0:T(128)}, u32[]{:S(2)}) copy-start(s32[8]{0:T(128)} %refs_0_.2) | copy-start | bytes 100
  124.1 2.0 %copy-start.4 = (f32[2,256,512]{2,1,0:T(8,128)}, f32[2,256,512]{2,1,0:T(8,128)S(1)}, u32[]{:S(2)}) copy-start(f32[2,256,512]{2,1,0:T(8,128)S(1)} %get-tuple-element.60) | copy-start | bytes 3145732
  124.1 2.0 %collective-permute-start.24 = (bf16[2,256,512]{2,1,0:T(8,128)(2,1)S(1)}, bf16[2,256,512]{2,1,0:T(8,128)(2,1)S(1)}, u32[]{:S(2)}, u32[]{:S(2)}) collective-permute-start(bf16[2,256,512]{2,1,0:T(8,128)(2,1)S(1)} %get-tuple-element.61), channel_id=1, source_target_pairs={{0,1},{1,0},{2,3},{3,2},{4,5},{5,4},{6,7},{7,6},{8,9},{9,8},{10,11... | collective-permute-start | bytes 1572872 | tf_op jit(solution)/shard_map/ppermute | solution.py:116
  126.1 0.9 copy-start.8
  127.0 8.7 %collective-permute-start.25 = (bf16[256,512]{1,0:T(8,128)(2,1)}, bf16[256,512]{1,0:T(8,128)(2,1)}, u32[]{:S(2)}, u32[]{:S(2)}) collective-permute-start(bf16[256,512]{1,0:T(8,128)(2,1)} %fusion), channel_id=1, source_target_pairs={{0,2},{2,0},{1,3},{3,1},{4,6},{6,4},{5,7},{7,5},{8,10},{10,8},{9,1... | collective-permute-start | bytes 786440 | tf_op jit(solution)/shard_map/ppermute | solution.py:116
  127.6 1.8 %copy-start.5 = (f32[2,256,512]{2,1,0:T(8,128)S(1)}, f32[2,256,512]{2,1,0:T(8,128)}, u32[]{:S(2)}) copy-start(f32[2,256,512]{2,1,0:T(8,128)} %copy-done.4) | copy-start | bytes 3145732

commit v7 on v6

--- a/solution.py
+++ b/solution.py
@@ -189,6 +189,7 @@
     made_ref,
     other_vmem,
     half_vmem,
+    plan_smem,
     sems,
 ):
     rep_at, mem_at, grp_at = (lax.axis_index(name) for name in ("rep", "mem", "grp"))
@@ -202,6 +203,8 @@
     def part(index, size):
         return pl.ds(pl.multiple_of(index * size, size), size)
 
+    plan_copy = pltpu.make_async_copy(plan_ref, plan_smem, sems.at[25])
+    plan_copy.start()
     blocks = 4
     step = rows // blocks
     for block in range(blocks):
@@ -228,7 +231,8 @@
     copy(out_w.at[part(grp_at, half_ref.shape[0])], half_vmem)
     for started in copies:
         started.start()
-    step_ratio = plan_ratio(plan_ref, width)
+    plan_copy.wait()
+    step_ratio = plan_ratio(plan_smem, width)
     for block in range(blocks):
         for shard in range(2):
             copies[2 * block + shard].wait()
@@ -377,10 +381,10 @@
 
 
 def out_body(*refs):
-    piece_refs, (own_w, *part_refs), (send_ref, keep_ref, heads_ref, weight_ref, sem) = (
+    piece_refs, (own_w, partner_w, *part_refs), (send_ref, keep_ref, heads_ref, weight_ref, sem) = (
         refs[:4],
-        refs[4:11],
-        refs[11:],
+        refs[4:10],
+        refs[10:],
     )
     seq_at, grp_at = lax.axis_index("seq"), lax.axis_index("grp")
     place = lax.axis_index("mem") * 2 + lax.axis_index("rep")
@@ -392,14 +396,15 @@
     depth = part_refs[0].shape[0]
     mine = pl.ds(pl.multiple_of(grp_at * depth, depth), depth)
     rest = pl.ds(pl.multiple_of((1 - grp_at) * depth, depth), depth)
-    for bit in range(1, 4):
-        weight_ref[bit, mine] = part_refs[2 * bit - 2][...]
-        weight_ref[bit, rest] = part_refs[2 * bit - 1][...]
+    for bit in range(2):
+        weight_ref[1 + bit, mine] = part_refs[2 * bit][...]
+        weight_ref[1 + bit, rest] = part_refs[2 * bit + 1][...]
     for bit in (1, 2, 3, 0):
         if bit == 0:
             copy.wait()
         slot = seq_at ^ bit ^ place
-        value = jnp.dot(heads, weight_ref[bit], preferred_element_type=jnp.float32)
+        weight = partner_w[...] if bit == 1 else weight_ref[max(bit - 1, 0)]
+        value = jnp.dot(heads, weight, preferred_element_type=jnp.float32)
 
         @pl.when(slot % 2 == 1)
         def _():
@@ -435,10 +440,10 @@
             pltpu.VMEM((2 * video_rows + audio_rows, half_depth), jnp.bfloat16),
             pltpu.VMEM((half_depth + query_quarter, kv_weight.shape[1]), jnp.bfloat16),
             pltpu.VMEM((out_weight.shape[0] // 2, out_weight.shape[1]), jnp.bfloat16),
-            pltpu.SemaphoreType.DMA((25,)),
+            pltpu.SMEM(plan.shape, jnp.int32),
+            pltpu.SemaphoreType.DMA((26,)),
         ],
-        smem=(0,),
-        loose_in=(1, 2, 3, 4, 5),
+        loose_in=(0, 1, 2, 3, 4, 5),
         loose_out=(0, 1, 2),
         limit=61,
     )
@@ -472,7 +477,7 @@
 
     across.append(swap(tokens[3], "mem", 1))
     rest += [swap(piece, "grp", 1) for piece in pieces[1:]]
-    out_parts = [swap(out_half, "seq", 1), swap(out_half, "seq", 2)]
+    out_partner, out_third = swap(out_weight, "seq", 1), swap(out_half, "seq", 2)
     weights = [weight_own]
     for piece, other in zip(pieces, rest):
         weights += [piece, other]
@@ -482,7 +487,7 @@
         products_body,
         [sums, sums],
         [value for pair in zip(tokens, across) for value in pair] + weights,
-        after=out_parts[:1],
+        after=(out_partner,),
         scratch=[
             pltpu.VMEM((seq_size * video_rows, 4 * half_depth), jnp.bfloat16),
             pltpu.VMEM((seq_size * audio_rows, 8 * query_quarter), jnp.bfloat16),
@@ -491,9 +496,10 @@
         ],
         limit=26,
     )
-    out_parts.append(swap(out_parts[1], "seq", 1))
-    send, out_parts[2] = lax.optimization_barrier((send, out_parts[2]))
+    out_fourth, third_rest = swap(out_third, "seq", 1), swap(out_third, "grp", 1)
+    send, out_fourth, third_rest = lax.optimization_barrier((send, out_fourth, third_rest))
     came = swap(send, "rep", 1)
+    fourth_rest = swap(out_fourth, "grp", 1)
 
     span = video_rows * seq_size
     blocks = jnp.stack([seq_at, seq_at ^ 1, seq_at ^ 2, seq_at ^ 3])
@@ -513,9 +519,7 @@
     near_piece = swap(near_piece, "seq", 1)
 
     columns = out_weight.shape[1]
-    weights = [out_weight]
-    for part in out_parts:
-        weights += [part, swap(part, "grp", 1)]
+    weights = [out_weight, out_partner, out_third, third_rest, out_fourth, fourth_rest]
     send, keep = kernel_call(
         out_body,
         [
@@ -525,7 +529,7 @@
         [own_piece, near_piece, far_piece, farther_piece, *weights],
         scratch=[
             pltpu.VMEM((seq_size, audio_rows, HEAD_DIM), jnp.bfloat16),
-            pltpu.VMEM((seq_size, *out_weight.shape), jnp.bfloat16),
+            pltpu.VMEM((3, *out_weight.shape), jnp.bfloat16),
             pltpu.SemaphoreType.DMA,
         ],
         loose_in=(4,),

time: 138 us -> 134 us (0.971)
  waiting for transfers between devices: 53.2 us -> 45.5 us
  starting transfers between devices: 29.9 us -> 32.8 us
  local copies, waits for them, and re-layouts: 0.46 us -> 2.81 us
    ppermute x26 -> x25, waiting for transfers between devices: 53.2 us -> 45.5 us  [swap(): return lax.ppermute(value, axis, [(i, i ^ bit) for i in range(size)])]
    ppermute x26 -> x25, starting transfers between devices: 29.9 us -> 32.8 us  [swap(): return lax.ppermute(value, axis, [(i, i ^ bit) for i in range(size)])]
    unnamed x23 -> x33, local copies, waits for them, and re-layouts: 0.06 us -> 2.4 us
  transfers between devices with their start and end apart: 26 -> 25, of which waited for: 12 -> 10; matrix products, arithmetic and copies ran while one was open for 1% -> 1% of each run, Pallas kernels for 6% -> 7%
where the time goes in v7:
time: 134 us
  waiting for transfers between devices  45.5 us (34%)
  blocking collectives  34 us (25%)
  starting transfers between devices  32.8 us (24%)
  Pallas kernels  14.3 us (11%)
  other arithmetic  3.96 us (3%)
  local copies, waits for them, and re-layouts  2.81 us (2%)
    ppermute x25, waiting for transfers between devices, swap(): return lax.ppermute(value, axis, [(i, i ^ bit) for i in range(size)])  45.5 us
    all_to_all x1, blocking collectives, by_head(): lax.all_to_all(jnp.broadcast_to(alignment[None], (seq_size, audio_rows)),...  34 us
    ppermute x25, starting transfers between devices, swap(): return lax.ppermute(value, axis, [(i, i ^ bit) for i in range(size)])  32.8 us
    pallas_call x5, Pallas kernels, kernel_call(): pl.pallas_call(whole, out_shape=outs, in_specs=spots + [ANY] * len(after)...  12.4 us
  transfers between devices with their start and end apart: 25, of which 10 were waited for; matrix products, arithmetic and copies ran while one was open for 1% of the time, Pallas kernels for 7%

profile of v7, /device:TPU:0, one launch (start us, length us, event | category | flops | bytes accessed | tf_op | source)
XLA Modules:
  0.0 134.2 jit_solution(3244490603721395298)
XLA Ops:
  0.6 3.3 %shard_map.87 = (bf16[640,512]{1,0:T(8,128)(2,1)}, bf16[640,1024]{1,0:T(8,128)(2,1)}, bf16[256,512]{1,0:T(8,128)(2,1)}) custom-call(s32[8]{0:T(128)} %refs_0_.2, bf16[3,192,2048]{2,1,0:T(8,128)(2,1)} %refs_1_.2, bf16[256,2048]{1,0:T(8,128)(2,1)} %refs_2_.1, bf16[1024,1024]{1,0:T(8,128)(2,1)} %refs_0_.3, bf16[512,512]{1,0:T(8,128)(2,1)} %refs_1_.3, ...), custom_call_target="tpu_custom_call" | custom-call | tf_op jit(solution)/shard_map/pallas_call | solution.py:130
  4.0 0.5 collective-permute-start.3
  4.5 2.7 %collective-permute-start = (bf16[640,512]{1,0:T(8,128)(2,1)}, bf16[640,512]{1,0:T(8,128)(2,1)S(1)}, u32[]{:S(2)}, u32[]{:S(2)}) collective-permute-start(bf16[640,512]{1,0:T(8,128)(2,1)} %get-tuple-element.34.refs_0_), channel_id=1, source_target_pairs={{0,4},{4,0},{8,12},{12,8},{1,5},{5,1},{9,13},{13,9},{2,6},{6,2},{1... | collective-permute-start | bytes 1966088 | tf_op jit(solution)/shard_map/ppermute | solution.py:116
  7.2 2.6 %collective-permute-start.1 = (bf16[640,512]{1,0:T(8,128)(2,1)}, bf16[640,512]{1,0:T(8,128)(2,1)S(1)}, u32[]{:S(2)}, u32[]{:S(2)}) collective-permute-start(bf16[640,512]{1,0:T(8,128)(2,1)} %get-tuple-element.34.refs_0_), channel_id=1, source_target_pairs={{0,8},{4,12},{8,0},{12,4},{1,9},{5,13},{9,1},{13,5},{2,10},{6,14},... | collective-permute-start | bytes 1966088 | tf_op jit(solution)/shard_map/ppermute | solution.py:116
  9.8 1.5 %collective-permute-start.2 = (bf16[640,512]{1,0:T(8,128)(2,1)}, bf16[640,512]{1,0:T(8,128)(2,1)S(1)}, u32[]{:S(2)}, u32[]{:S(2)}) collective-permute-start(bf16[640,512]{1,0:T(8,128)(2,1)} %get-tuple-element.34.refs_0_), channel_id=1, source_target_pairs={{0,2},{2,0},{1,3},{3,1},{4,6},{6,4},{5,7},{7,5},{8,10},{10,8},{9,1... | collective-permute-start | bytes 1966088 | tf_op jit(solution)/shard_map/ppermute | solution.py:116
  11.3 0.3 shard_map.88
  11.6 0.5 collective-permute-start.4
  12.1 34.0 %all_to_all.6 = s32[4,1,256]{2,1,0:T(1,128)S(1)} all-to-all(s32[4,1,256]{2,1,0:T(1,128)S(1)} %broadcast_in_dim.4), channel_id=1, replica_groups=mesh['grp'=2,'seq'=4,'mem'=2,'rep'=2] {'seq'}, dimensions={0} | all-to-all | bytes 8192 | tf_op jit(solution)/shard_map/all_to_all | solution.py:461
  46.1 0.6 collective-permute-start.8
  46.8 1.6 %collective-permute-start.5 = (bf16[640,512]{1,0:T(8,128)(2,1)S(1)}, bf16[640,512]{1,0:T(8,128)(2,1)S(1)}, u32[]{:S(2)}, u32[]{:S(2)}) collective-permute-start(bf16[640,512]{1,0:T(8,128)(2,1)S(1)} %collective-permute-done.1.refs_4_), channel_id=1, source_target_pairs={{0,4},{4,0},{8,12},{12,8},{1,5},{5,1},{9,13},{13,9},{2,6},{6,2},{1... | collective-permute-start | bytes 1966088 | tf_op jit(solution)/shard_map/ppermute | solution.py:116
  48.4 1.5 %collective-permute-start.7 = (bf16[640,512]{1,0:T(8,128)(2,1)S(1)}, bf16[640,512]{1,0:T(8,128)(2,1)S(1)}, u32[]{:S(2)}, u32[]{:S(2)}) collective-permute-start(bf16[640,512]{1,0:T(8,128)(2,1)S(1)} %collective-permute-done.1.refs_4_), channel_id=1, source_target_pairs={{0,2},{2,0},{1,3},{3,1},{4,6},{6,4},{5,7},{7,5},{8,10},{10,8},{9,1... | collective-permute-start | bytes 1966088 | tf_op jit(solution)/shard_map/ppermute | solution.py:116
  49.9 0.5 collective-permute-start.6
  50.4 2.2 %collective-permute-start.9 = (bf16[320,512]{1,0:T(8,128)(2,1)S(1)}, bf16[320,512]{1,0:T(8,128)(2,1)S(1)}, u32[]{:S(2)}, u32[]{:S(2)}) collective-permute-start(bf16[320,512]{1,0:T(8,128)(2,1)S(1)} %get-tuple-element.42), channel_id=1, source_target_pairs={{0,12},{4,8},{8,4},{12,0},{1,13},{5,9},{9,5},{13,1},{2,14},{6,10},... | collective-permute-start | bytes 983048 | tf_op jit(solution)/shard_map/ppermute | solution.py:116
  52.6 10.6 %collective-permute-done.8.refs_11_ = bf16[320,512]{1,0:T(8,128)(2,1)S(1)} collective-permute-done((bf16[320,512]{1,0:T(8,128)(2,1)S(1)}, bf16[320,512]{1,0:T(8,128)(2,1)S(1)}, u32[]{:S(2)}, u32[]{:S(2)}) %collective-permute-start.8) | collective-permute-done | bytes 327712 | tf_op jit(solution)/shard_map/ppermute | solution.py:116
  63.2 1.5 %collective-permute-start.10 = (bf16[320,512]{1,0:T(8,128)(2,1)S(1)}, bf16[320,512]{1,0:T(8,128)(2,1)S(1)}, u32[]{:S(2)}, u32[]{:S(2)}) collective-permute-start(bf16[320,512]{1,0:T(8,128)(2,1)S(1)} %collective-permute-done.4.refs_9_), channel_id=1, source_target_pairs={{0,16},{16,0},{1,17},{17,1},{2,18},{18,2},{3,19},{19,3},{4,20},{20... | collective-permute-start | bytes 983048 | tf_op jit(solution)/shard_map/ppermute | solution.py:116
  64.7 12.4 %collective-permute-done.9.refs_13_ = bf16[320,512]{1,0:T(8,128)(2,1)S(1)} collective-permute-done((bf16[320,512]{1,0:T(8,128)(2,1)S(1)}, bf16[320,512]{1,0:T(8,128)(2,1)S(1)}, u32[]{:S(2)}, u32[]{:S(2)}) %collective-permute-start.9) | collective-permute-done | bytes 327712 | tf_op jit(solution)/shard_map/ppermute | solution.py:116
  77.2 0.9 collective-permute-done.6.refs_3_
  78.1 1.5 %collective-permute-start.11 = (bf16[640,512]{1,0:T(8,128)(2,1)S(1)}, bf16[640,512]{1,0:T(8,128)(2,1)S(1)}, u32[]{:S(2)}, u32[]{:S(2)}) collective-permute-start(bf16[640,512]{1,0:T(8,128)(2,1)S(1)} %collective-permute-done.5.refs_6_), channel_id=1, source_target_pairs={{0,2},{2,0},{1,3},{3,1},{4,6},{6,4},{5,7},{7,5},{8,10},{10,8},{9,1... | collective-permute-start | bytes 1966088 | tf_op jit(solution)/shard_map/ppermute | solution.py:116
  79.6 1.5 %collective-permute-start.15 = (bf16[256,512]{1,0:T(8,128)(2,1)S(1)}, bf16[256,512]{1,0:T(8,128)(2,1)S(1)}, u32[]{:S(2)}, u32[]{:S(2)}) collective-permute-start(bf16[256,512]{1,0:T(8,128)(2,1)S(1)} %copy-done.15), channel_id=1, source_target_pairs={{0,8},{4,12},{8,0},{12,4},{1,9},{5,13},{9,1},{13,5},{2,10},{6,14},... | collective-permute-start | bytes 786440 | tf_op jit(solution)/shard_map/ppermute | solution.py:116
  81.1 1.5 %collective-permute-start.12 = (bf16[320,512]{1,0:T(8,128)(2,1)S(1)}, bf16[320,512]{1,0:T(8,128)(2,1)S(1)}, u32[]{:S(2)}, u32[]{:S(2)}) collective-permute-start(bf16[320,512]{1,0:T(8,128)(2,1)S(1)} %collective-permute-done.8.refs_11_), channel_id=1, source_target_pairs={{0,16},{16,0},{1,17},{17,1},{2,18},{18,2},{3,19},{19,3},{4,20},{20... | collective-permute-start | bytes 983048 | tf_op jit(solution)/shard_map/ppermute | solution.py:116
  82.6 0.5 collective-permute-start.13
  83.1 9.8 %collective-permute-done.15.refs_6_ = bf16[256,512]{1,0:T(8,128)(2,1)S(1)} collective-permute-done((bf16[256,512]{1,0:T(8,128)(2,1)S(1)}, bf16[256,512]{1,0:T(8,128)(2,1)S(1)}, u32[]{:S(2)}, u32[]{:S(2)}) %collective-permute-start.15) | collective-permute-done | bytes 262176 | tf_op jit(solution)/shard_map/ppermute | solution.py:116
  92.9 3.0 %collective-permute-start.16 = (bf16[256,512]{1,0:T(8,128)(2,1)S(1)}, bf16[256,512]{1,0:T(8,128)(2,1)S(1)}, u32[]{:S(2)}, u32[]{:S(2)}) collective-permute-start(bf16[256,512]{1,0:T(8,128)(2,1)S(1)} %collective-permute-done.15.refs_6_), channel_id=1, source_target_pairs={{0,4},{4,0},{8,12},{12,8},{1,5},{5,1},{9,13},{13,9},{2,6},{6,2},{1... | collective-permute-start | bytes 786440 | tf_op jit(solution)/shard_map/ppermute | solution.py:116
  95.9 1.5 %collective-permute-start.17 = (bf16[256,512]{1,0:T(8,128)(2,1)S(1)}, bf16[256,512]{1,0:T(8,128)(2,1)S(1)}, u32[]{:S(2)}, u32[]{:S(2)}) collective-permute-start(bf16[256,512]{1,0:T(8,128)(2,1)S(1)} %collective-permute-done.15.refs_6_), channel_id=1, source_target_pairs={{0,16},{16,0},{1,17},{17,1},{2,18},{18,2},{3,19},{19,3},{4,20},{20... | collective-permute-start | bytes 786440 | tf_op jit(solution)/shard_map/ppermute | solution.py:116
  97.4 3.9 %shard_map.89 = (f32[1280,256]{1,0:T(8,128)}, f32[1280,256]{1,0:T(8,128)S(1)}) custom-call(bf16[640,512]{1,0:T(8,128)(2,1)S(1)} %copy-done.7, bf16[640,512]{1,0:T(8,128)(2,1)S(1)} %collective-permute-done.2.refs_1_, bf16[640,512]{1,0:T(8,128)(2,1)S(1)} %collective-permute-done.refs_2_, bf16[640,512]{1,0:T(8,128)(2,1)S(1)} %collective-permute-done.6.refs_3_, ...), custom_call_target="tpu_custom_call" | custom-call | tf_op jit(solution)/shard_map/pallas_call | solution.py:130
  101.4 0.9 collective-permute-done.17.refs_7_
  102.3 0.7 copy-done.8
  103.1 0.1 fusion.1
  103.1 0.1 div.18
  103.2 0.1 fusion.2
  103.3 0.1 reshape.123
  103.4 1.5 %collective-permute-start.22 = (bf16[256,512]{1,0:T(8,128)(2,1)S(1)}, bf16[256,512]{1,0:T(8,128)(2,1)S(1)}, u32[]{:S(2)}, u32[]{:S(2)}) collective-permute-start(bf16[256,512]{1,0:T(8,128)(2,1)S(1)} %collective-permute-done.16.refs_8_), channel_id=1, source_target_pairs={{0,16},{16,0},{1,17},{17,1},{2,18},{18,2},{3,19},{19,3},{4,20},{20... | collective-permute-start | bytes 786440 | tf_op jit(solution)/shard_map/ppermute | solution.py:116
  104.9 0.2 copy.10.refs_1_
  105.2 1.2 collective-permute-done.18.refs_3_
  106.4 3.5 %shard_map.90 = (bf16[256,128]{1,0:T(8,128)(2,1)S(1)}, bf16[256,128]{1,0:T(8,128)(2,1)S(1)}, bf16[256,128]{1,0:T(8,128)(2,1)S(1)}, bf16[256,128]{1,0:T(8,128)(2,1)S(1)}) custom-call(f32[1,768]{1,0:T(1,128)S(1)} %fusion.3.refs_0_, f32[4,256,1]{2,1,0:T(8,128)S(1)} %copy.10.refs_1_, f32[1280,256]{1,0:T(8,128)S(1)} %get-tuple-element.52.refs_2_, ...), custom_call_target="tpu_custom_call" | custom-call | tf_op jit(solution)/shard_map/pallas_call | solution.py:130
  109.9 2.4 %collective-permute-start.20 = (bf16[256,128]{1,0:T(8,128)(2,1)S(1)}, bf16[256,128]{1,0:T(8,128)(2,1)S(1)}, u32[]{:S(2)}, u32[]{:S(2)}) collective-permute-start(bf16[256,128]{1,0:T(8,128)(2,1)S(1)} %get-tuple-element.58), channel_id=1, source_target_pairs={{0,8},{4,12},{8,0},{12,4},{1,9},{5,13},{9,1},{13,5},{2,10},{6,14},... | collective-permute-start | bytes 196616 | tf_op jit(solution)/shard_map/ppermute | solution.py:116
  112.3 1.9 %collective-permute-start.21 = (bf16[256,128]{1,0:T(8,128)(2,1)S(1)}, bf16[256,128]{1,0:T(8,128)(2,1)S(1)}, u32[]{:S(2)}, u32[]{:S(2)}) collective-permute-start(bf16[256,128]{1,0:T(8,128)(2,1)S(1)} %get-tuple-element.59), channel_id=1, source_target_pairs={{0,12},{4,8},{8,4},{12,0},{1,13},{5,9},{9,5},{13,1},{2,14},{6,10},... | collective-permute-start | bytes 196616 | tf_op jit(solution)/shard_map/ppermute | solution.py:116
  114.3 0.7 copy-done.10
  115.0 3.5 %collective-permute-done.20.refs_2_ = bf16[256,128]{1,0:T(8,128)(2,1)S(1)} collective-permute-done((bf16[256,128]{1,0:T(8,128)(2,1)S(1)}, bf16[256,128]{1,0:T(8,128)(2,1)S(1)}, u32[]{:S(2)}, u32[]{:S(2)}) %collective-permute-start.20) | collective-permute-done | bytes 65568 | tf_op jit(solution)/shard_map/ppermute | solution.py:116
  118.5 0.9 copy-done.11
  119.5 1.4 %shard_map.91 = (bf16[2,256,512]{2,1,0:T(8,128)(2,1)S(1)}, f32[2,256,512]{2,1,0:T(8,128)S(1)}) custom-call(bf16[256,128]{1,0:T(8,128)(2,1)S(1)} %get-tuple-element.56.refs_0_, bf16[256,128]{1,0:T(8,128)(2,1)S(1)} %collective-permute-done.19.refs_1_, bf16[256,128]{1,0:T(8,128)(2,1)S(1)} %collective-permute-done.20.refs_2_, ...), custom_call_target="tpu_custom_call" | custom-call | tf_op jit(solution)/shard_map/pallas_call | solution.py:130
  121.0 1.9 %collective-permute-done.23 = bf16[2,256,512]{2,1,0:T(8,128)(2,1)S(1)} collective-permute-done((bf16[2,256,512]{2,1,0:T(8,128)(2,1)S(1)}, bf16[2,256,512]{2,1,0:T(8,128)(2,1)S(1)}, u32[]{:S(2)}, u32[]{:S(2)}) %collective-permute-start.23) | collective-permute-done | bytes 524320 | tf_op jit(solution)/shard_map/ppermute | solution.py:116
  122.9 0.9 fusion
  123.8 1.5 %collective-permute-start.24 = (bf16[256,512]{1,0:T(8,128)(2,1)}, bf16[256,512]{1,0:T(8,128)(2,1)}, u32[]{:S(2)}, u32[]{:S(2)}) collective-permute-start(bf16[256,512]{1,0:T(8,128)(2,1)} %fusion), channel_id=1, source_target_pairs={{0,2},{2,0},{1,3},{3,1},{4,6},{6,4},{5,7},{7,5},{8,10},{10,8},{9,1... | collective-permute-start | bytes 786440 | tf_op jit(solution)/shard_map/ppermute | solution.py:116
  125.3 1.8 %shard_map.86 = bf16[192,2048]{1,0:T(8,128)(2,1)} custom-call(s32[8]{0:T(128)S(1)} %copy-done.12, bf16[3,192,2048]{2,1,0:T(8,128)(2,1)S(1)} %copy-done), custom_call_target="tpu_custom_call" | custom-call | tf_op jit(solution)/shard_map/pallas_call | solution.py:168
  127.1 1.1 bitcast_add_fusion
  128.2 4.2 %collective-permute-done.24 = bf16[256,512]{1,0:T(8,128)(2,1)} collective-permute-done((bf16[256,512]{1,0:T(8,128)(2,1)}, bf16[256,512]{1,0:T(8,128)(2,1)}, u32[]{:S(2)}, u32[]{:S(2)}) %collective-permute-start.24) | collective-permute-done | bytes 262176 | tf_op jit(solution)/shard_map/ppermute | solution.py:116
  132.4 1.7 %add_convert_fusion = bf16[256,512]{1,0:T(8,128)(2,1)} fusion(f32[256,512]{1,0:T(8,128)S(1)} %bitcast_add_fusion, bf16[256,512]{1,0:T(8,128)(2,1)} %collective-permute-done.24), kind=kLoop, calls=%fused_computation.1 | loop fusion | flops 393216 | bytes 1048576 | tf_op jit(solution)/shard_map/convert_element_type | solution.py:543
  (54 shorter events, 0.4 us)
Async XLA Ops:
  0.6 10.7 %copy-start.2 = (bf16[512,512]{1,0:T(8,128)(2,1)S(1)}, bf16[512,512]{1,0:T(8,128)(2,1)}, u32[]{:S(2)}) copy-start(bf16[512,512]{1,0:T(8,128)(2,1)} %refs_1_.3) | copy-start | bytes 1572868
  0.6 10.7 %copy-start.1 = (bf16[1024,1024]{1,0:T(8,128)(2,1)S(1)}, bf16[1024,1024]{1,0:T(8,128)(2,1)}, u32[]{:S(2)}) copy-start(bf16[1024,1024]{1,0:T(8,128)(2,1)} %refs_0_.3) | copy-start | bytes 6291460
  4.0 7.3 %collective-permute-start.3 = (bf16[640,1024]{1,0:T(8,128)(2,1)}, bf16[640,1024]{1,0:T(8,128)(2,1)S(1)}, u32[]{:S(2)}, u32[]{:S(2)}) collective-permute-start(bf16[640,1024]{1,0:T(8,128)(2,1)} %get-tuple-element.35), channel_id=1, source_target_pairs={{0,1},{1,0},{2,3},{3,2},{4,5},{5,4},{6,7},{7,6},{8,9},{9,8},{10,11... | collective-permute-start | bytes 3932168 | tf_op jit(solution)/shard_map/ppermute | solution.py:116
  4.5 7.6 %copy-start.14 = (s32[256]{0:T(256)S(1)}, s32[256]{0:T(256)}, u32[]{:S(2)}) copy-start(s32[256]{0:T(256)} %param.9) | copy-start | bytes 3076
  4.5 72.7 %copy-start.3 = (bf16[512,512]{1,0:T(8,128)(2,1)S(1)}, bf16[512,512]{1,0:T(8,128)(2,1)}, u32[]{:S(2)}) copy-start(bf16[512,512]{1,0:T(8,128)(2,1)} %refs_4_.3) | copy-start | bytes 1572868
  4.5 75.1 %copy-start.15 = (bf16[256,512]{1,0:T(8,128)(2,1)S(1)}, bf16[256,512]{1,0:T(8,128)(2,1)}, u32[]{:S(2)}) copy-start(bf16[256,512]{1,0:T(8,128)(2,1)} %get-tuple-element.54) | copy-start | bytes 786436
  4.5 92.9 %copy-start.7 = (bf16[640,512]{1,0:T(8,128)(2,1)S(1)}, bf16[640,512]{1,0:T(8,128)(2,1)}, u32[]{:S(2)}) copy-start(bf16[640,512]{1,0:T(8,128)(2,1)} %get-tuple-element.34.refs_0_) | copy-start | bytes 1966084
  4.5 42.2 %collective-permute-start = (bf16[640,512]{1,0:T(8,128)(2,1)}, bf16[640,512]{1,0:T(8,128)(2,1)S(1)}, u32[]{:S(2)}, u32[]{:S(2)}) collective-permute-start(bf16[640,512]{1,0:T(8,128)(2,1)} %get-tuple-element.34.refs_0_), channel_id=1, source_target_pairs={{0,4},{4,0},{8,12},{12,8},{1,5},{5,1},{9,13},{13,9},{2,6},{6,2},{1... | collective-permute-start | bytes 1966088 | tf_op jit(solution)/shard_map/ppermute | solution.py:116
  7.2 39.5 %collective-permute-start.1 = (bf16[640,512]{1,0:T(8,128)(2,1)}, bf16[640,512]{1,0:T(8,128)(2,1)S(1)}, u32[]{:S(2)}, u32[]{:S(2)}) collective-permute-start(bf16[640,512]{1,0:T(8,128)(2,1)} %get-tuple-element.34.refs_0_), channel_id=1, source_target_pairs={{0,8},{4,12},{8,0},{12,4},{1,9},{5,13},{9,1},{13,5},{2,10},{6,14},... | collective-permute-start | bytes 1966088 | tf_op jit(solution)/shard_map/ppermute | solution.py:116
  9.8 37.0 %collective-permute-start.2 = (bf16[640,512]{1,0:T(8,128)(2,1)}, bf16[640,512]{1,0:T(8,128)(2,1)S(1)}, u32[]{:S(2)}, u32[]{:S(2)}) collective-permute-start(bf16[640,512]{1,0:T(8,128)(2,1)} %get-tuple-element.34.refs_0_), channel_id=1, source_target_pairs={{0,2},{2,0},{1,3},{3,1},{4,6},{6,4},{5,7},{7,5},{8,10},{10,8},{9,1... | collective-permute-start | bytes 1966088 | tf_op jit(solution)/shard_map/ppermute | solution.py:116
  11.6 35.2 %collective-permute-start.4 = (bf16[320,512]{1,0:T(8,128)(2,1)S(1)}, bf16[320,512]{1,0:T(8,128)(2,1)S(1)}, u32[]{:S(2)}, u32[]{:S(2)}) collective-permute-start(bf16[320,512]{1,0:T(8,128)(2,1)S(1)} %get-tuple-element.36), channel_id=1, source_target_pairs={{0,4},{4,0},{8,12},{12,8},{1,5},{5,1},{9,13},{13,9},{2,6},{6,2},{1... | collective-permute-start | bytes 983048 | tf_op jit(solution)/shard_map/ppermute | solution.py:116
  46.1 17.1 %collective-permute-start.8 = (bf16[320,512]{1,0:T(8,128)(2,1)S(1)}, bf16[320,512]{1,0:T(8,128)(2,1)S(1)}, u32[]{:S(2)}, u32[]{:S(2)}) collective-permute-start(bf16[320,512]{1,0:T(8,128)(2,1)S(1)} %get-tuple-element.41), channel_id=1, source_target_pairs={{0,8},{4,12},{8,0},{12,4},{1,9},{5,13},{9,1},{13,5},{2,10},{6,14},... | collective-permute-start | bytes 983048 | tf_op jit(solution)/shard_map/ppermute | solution.py:116
  46.8 30.4 %collective-permute-start.5 = (bf16[640,512]{1,0:T(8,128)(2,1)S(1)}, bf16[640,512]{1,0:T(8,128)(2,1)S(1)}, u32[]{:S(2)}, u32[]{:S(2)}) collective-permute-start(bf16[640,512]{1,0:T(8,128)(2,1)S(1)} %collective-permute-done.1.refs_4_), channel_id=1, source_target_pairs={{0,4},{4,0},{8,12},{12,8},{1,5},{5,1},{9,13},{13,9},{2,6},{6,2},{1... | collective-permute-start | bytes 1966088 | tf_op jit(solution)/shard_map/ppermute | solution.py:116
  48.4 28.8 %collective-permute-start.7 = (bf16[640,512]{1,0:T(8,128)(2,1)S(1)}, bf16[640,512]{1,0:T(8,128)(2,1)S(1)}, u32[]{:S(2)}, u32[]{:S(2)}) collective-permute-start(bf16[640,512]{1,0:T(8,128)(2,1)S(1)} %collective-permute-done.1.refs_4_), channel_id=1, source_target_pairs={{0,2},{2,0},{1,3},{3,1},{4,6},{6,4},{5,7},{7,5},{8,10},{10,8},{9,1... | collective-permute-start | bytes 1966088 | tf_op jit(solution)/shard_map/ppermute | solution.py:116
  49.9 28.3 %collective-permute-start.6 = (bf16[640,512]{1,0:T(8,128)(2,1)S(1)}, bf16[640,512]{1,0:T(8,128)(2,1)S(1)}, u32[]{:S(2)}, u32[]{:S(2)}) collective-permute-start(bf16[640,512]{1,0:T(8,128)(2,1)S(1)} %collective-permute-done.refs_2_), channel_id=1, source_target_pairs={{0,2},{2,0},{1,3},{3,1},{4,6},{6,4},{5,7},{7,5},{8,10},{10,8},{9,1... | collective-permute-start | bytes 1966088 | tf_op jit(solution)/shard_map/ppermute | solution.py:116
  50.4 26.8 %collective-permute-start.9 = (bf16[320,512]{1,0:T(8,128)(2,1)S(1)}, bf16[320,512]{1,0:T(8,128)(2,1)S(1)}, u32[]{:S(2)}, u32[]{:S(2)}) collective-permute-start(bf16[320,512]{1,0:T(8,128)(2,1)S(1)} %get-tuple-element.42), channel_id=1, source_target_pairs={{0,12},{4,8},{8,4},{12,0},{1,13},{5,9},{9,5},{13,1},{2,14},{6,10},... | collective-permute-start | bytes 983048 | tf_op jit(solution)/shard_map/ppermute | solution.py:116
  63.2 14.0 %collective-permute-start.10 = (bf16[320,512]{1,0:T(8,128)(2,1)S(1)}, bf16[320,512]{1,0:T(8,128)(2,1)S(1)}, u32[]{:S(2)}, u32[]{:S(2)}) collective-permute-start(bf16[320,512]{1,0:T(8,128)(2,1)S(1)} %collective-permute-done.4.refs_9_), channel_id=1, source_target_pairs={{0,16},{16,0},{1,17},{17,1},{2,18},{18,2},{3,19},{19,3},{4,20},{20... | collective-permute-start | bytes 983048 | tf_op jit(solution)/shard_map/ppermute | solution.py:116
  77.2 18.7 %collective-permute-start.14 = (bf16[512,512]{1,0:T(8,128)(2,1)S(1)}, bf16[512,512]{1,0:T(8,128)(2,1)S(1)}, u32[]{:S(2)}, u32[]{:S(2)}) collective-permute-start(bf16[512,512]{1,0:T(8,128)(2,1)S(1)} %copy-done.3), channel_id=1, source_target_pairs={{0,4},{4,0},{8,12},{12,8},{1,5},{5,1},{9,13},{13,9},{2,6},{6,2},{1... | collective-permute-start | bytes 1572872 | tf_op jit(solution)/shard_map/ppermute | solution.py:116
  78.1 19.3 %collective-permute-start.11 = (bf16[640,512]{1,0:T(8,128)(2,1)S(1)}, bf16[640,512]{1,0:T(8,128)(2,1)S(1)}, u32[]{:S(2)}, u32[]{:S(2)}) collective-permute-start(bf16[640,512]{1,0:T(8,128)(2,1)S(1)} %collective-permute-done.5.refs_6_), channel_id=1, source_target_pairs={{0,2},{2,0},{1,3},{3,1},{4,6},{6,4},{5,7},{7,5},{8,10},{10,8},{9,1... | collective-permute-start | bytes 1966088 | tf_op jit(solution)/shard_map/ppermute | solution.py:116
  79.6 13.3 %collective-permute-start.15 = (bf16[256,512]{1,0:T(8,128)(2,1)S(1)}, bf16[256,512]{1,0:T(8,128)(2,1)S(1)}, u32[]{:S(2)}, u32[]{:S(2)}) collective-permute-start(bf16[256,512]{1,0:T(8,128)(2,1)S(1)} %copy-done.15), channel_id=1, source_target_pairs={{0,8},{4,12},{8,0},{12,4},{1,9},{5,13},{9,1},{13,5},{2,10},{6,14},... | collective-permute-start | bytes 786440 | tf_op jit(solution)/shard_map/ppermute | solution.py:116
  81.1 16.3 %collective-permute-start.12 = (bf16[320,512]{1,0:T(8,128)(2,1)S(1)}, bf16[320,512]{1,0:T(8,128)(2,1)S(1)}, u32[]{:S(2)}, u32[]{:S(2)}) collective-permute-start(bf16[320,512]{1,0:T(8,128)(2,1)S(1)} %collective-permute-done.8.refs_11_), channel_id=1, source_target_pairs={{0,16},{16,0},{1,17},{17,1},{2,18},{18,2},{3,19},{19,3},{4,20},{20... | collective-permute-start | bytes 983048 | tf_op jit(solution)/shard_map/ppermute | solution.py:116
  82.6 14.8 %collective-permute-start.13 = (bf16[320,512]{1,0:T(8,128)(2,1)S(1)}, bf16[320,512]{1,0:T(8,128)(2,1)S(1)}, u32[]{:S(2)}, u32[]{:S(2)}) collective-permute-start(bf16[320,512]{1,0:T(8,128)(2,1)S(1)} %collective-permute-done.9.refs_13_), channel_id=1, source_target_pairs={{0,16},{16,0},{1,17},{17,1},{2,18},{18,2},{3,19},{19,3},{4,20},{20... | collective-permute-start | bytes 983048 | tf_op jit(solution)/shard_map/ppermute | solution.py:116
  92.9 8.5 %collective-permute-start.16 = (bf16[256,512]{1,0:T(8,128)(2,1)S(1)}, bf16[256,512]{1,0:T(8,128)(2,1)S(1)}, u32[]{:S(2)}, u32[]{:S(2)}) collective-permute-start(bf16[256,512]{1,0:T(8,128)(2,1)S(1)} %collective-permute-done.15.refs_6_), channel_id=1, source_target_pairs={{0,4},{4,0},{8,12},{12,8},{1,5},{5,1},{9,13},{13,9},{2,6},{6,2},{1... | collective-permute-start | bytes 786440 | tf_op jit(solution)/shard_map/ppermute | solution.py:116
  95.9 6.4 %collective-permute-start.17 = (bf16[256,512]{1,0:T(8,128)(2,1)S(1)}, bf16[256,512]{1,0:T(8,128)(2,1)S(1)}, u32[]{:S(2)}, u32[]{:S(2)}) collective-permute-start(bf16[256,512]{1,0:T(8,128)(2,1)S(1)} %collective-permute-done.15.refs_6_), channel_id=1, source_target_pairs={{0,16},{16,0},{1,17},{17,1},{2,18},{18,2},{3,19},{19,3},{4,20},{20... | collective-permute-start | bytes 786440 | tf_op jit(solution)/shard_map/ppermute | solution.py:116
  102.3 0.7 copy-start.8
  103.0 3.4 %collective-permute-start.18 = (f32[1280,256]{1,0:T(8,128)}, f32[1280,256]{1,0:T(8,128)}, u32[]{:S(2)}, u32[]{:S(2)}) collective-permute-start(f32[1280,256]{1,0:T(8,128)} %get-tuple-element.55), channel_id=1, source_target_pairs={{0,1},{1,0},{2,3},{3,2},{4,5},{5,4},{6,7},{7,6},{8,9},{9,8},{10,11... | collective-permute-start | bytes 3932168 | tf_op jit(solution)/shard_map/ppermute | solution.py:116
  103.4 10.9 %collective-permute-start.22 = (bf16[256,512]{1,0:T(8,128)(2,1)S(1)}, bf16[256,512]{1,0:T(8,128)(2,1)S(1)}, u32[]{:S(2)}, u32[]{:S(2)}) collective-permute-start(bf16[256,512]{1,0:T(8,128)(2,1)S(1)} %collective-permute-done.16.refs_8_), channel_id=1, source_target_pairs={{0,16},{16,0},{1,17},{17,1},{2,18},{18,2},{3,19},{19,3},{4,20},{20... | collective-permute-start | bytes 786440 | tf_op jit(solution)/shard_map/ppermute | solution.py:116
  106.3 12.2 %copy-start.4 = (bf16[512,512]{1,0:T(8,128)(2,1)S(1)}, bf16[512,512]{1,0:T(8,128)(2,1)}, u32[]{:S(2)}) copy-start(bf16[512,512]{1,0:T(8,128)(2,1)} %refs_4_.3) | copy-start | bytes 1572868
  106.4 12.2 %copy-start.9 = (bf16[256,512]{1,0:T(8,128)(2,1)S(1)}, bf16[256,512]{1,0:T(8,128)(2,1)}, u32[]{:S(2)}) copy-start(bf16[256,512]{1,0:T(8,128)(2,1)} %copy-done.8) | copy-start | bytes 786436
  109.8 5.2 %collective-permute-start.19 = (bf16[256,128]{1,0:T(8,128)(2,1)S(1)}, bf16[256,128]{1,0:T(8,128)(2,1)S(1)}, u32[]{:S(2)}, u32[]{:S(2)}) collective-permute-start(bf16[256,128]{1,0:T(8,128)(2,1)S(1)} %get-tuple-element.57), channel_id=1, source_target_pairs={{0,4},{4,0},{8,12},{12,8},{1,5},{5,1},{9,13},{13,9},{2,6},{6,2},{1... | collective-permute-start | bytes 196616 | tf_op jit(solution)/shard_map/ppermute | solution.py:116
  109.9 8.6 %collective-permute-start.20 = (bf16[256,128]{1,0:T(8,128)(2,1)S(1)}, bf16[256,128]{1,0:T(8,128)(2,1)S(1)}, u32[]{:S(2)}, u32[]{:S(2)}) collective-permute-start(bf16[256,128]{1,0:T(8,128)(2,1)S(1)} %get-tuple-element.58), channel_id=1, source_target_pairs={{0,8},{4,12},{8,0},{12,4},{1,9},{5,13},{9,1},{13,5},{2,10},{6,14},... | collective-permute-start | bytes 196616 | tf_op jit(solution)/shard_map/ppermute | solution.py:116
  112.3 6.2 %collective-permute-start.21 = (bf16[256,128]{1,0:T(8,128)(2,1)S(1)}, bf16[256,128]{1,0:T(8,128)(2,1)S(1)}, u32[]{:S(2)}, u32[]{:S(2)}) collective-permute-start(bf16[256,128]{1,0:T(8,128)(2,1)S(1)} %get-tuple-element.59), channel_id=1, source_target_pairs={{0,12},{4,8},{8,4},{12,0},{1,13},{5,9},{9,5},{13,1},{2,14},{6,10},... | collective-permute-start | bytes 196616 | tf_op jit(solution)/shard_map/ppermute | solution.py:116
  114.3 0.7 copy-start.10
  118.5 1.0 copy-start.11
  119.5 5.8 %copy-start = (bf16[3,192,2048]{2,1,0:T(8,128)(2,1)S(1)}, bf16[3,192,2048]{2,1,0:T(8,128)(2,1)}, u32[]{:S(2)}) copy-start(bf16[3,192,2048]{2,1,0:T(8,128)(2,1)} %refs_1_.2) | copy-start | bytes 7077892
  119.5 5.8 %copy-start.12 = (s32[8]{0:T(128)S(1)}, s32[8]{0:T(128)}, u32[]{:S(2)}) copy-start(s32[8]{0:T(128)} %refs_0_.2) | copy-start | bytes 100
  120.9 2.0 %copy-start.5 = (f32[2,256,512]{2,1,0:T(8,128)}, f32[2,256,512]{2,1,0:T(8,128)S(1)}, u32[]{:S(2)}) copy-start(f32[2,256,512]{2,1,0:T(8,128)S(1)} %get-tuple-element.62) | copy-start | bytes 3145732
  120.9 2.0 %collective-permute-start.23 = (bf16[2,256,512]{2,1,0:T(8,128)(2,1)S(1)}, bf16[2,256,512]{2,1,0:T(8,128)(2,1)S(1)}, u32[]{:S(2)}, u32[]{:S(2)}) collective-permute-start(bf16[2,256,512]{2,1,0:T(8,128)(2,1)S(1)} %get-tuple-element.63), channel_id=1, source_target_pairs={{0,1},{1,0},{2,3},{3,2},{4,5},{5,4},{6,7},{7,6},{8,9},{9,8},{10,11... | collective-permute-start | bytes 1572872 | tf_op jit(solution)/shard_map/ppermute | solution.py:116
  122.9 2.4 %copy-start.13 = (bf16[2,256,512]{2,1,0:T(8,128)(2,1)}, bf16[2,256,512]{2,1,0:T(8,128)(2,1)S(1)}, u32[]{:S(2)}) copy-start(bf16[2,256,512]{2,1,0:T(8,128)(2,1)S(1)} %collective-permute-done.23) | copy-start | bytes 1572868
  123.8 8.7 %collective-permute-start.24 = (bf16[256,512]{1,0:T(8,128)(2,1)}, bf16[256,512]{1,0:T(8,128)(2,1)}, u32[]{:S(2)}, u32[]{:S(2)}) collective-permute-start(bf16[256,512]{1,0:T(8,128)(2,1)} %fusion), channel_id=1, source_target_pairs={{0,2},{2,0},{1,3},{3,1},{4,6},{6,4},{5,7},{7,5},{8,10},{10,8},{9,1... | collective-permute-start | bytes 786440 | tf_op jit(solution)/shard_map/ppermute | solution.py:116
  125.3 1.9 %copy-start.6 = (f32[2,256,512]{2,1,0:T(8,128)S(1)}, f32[2,256,512]{2,1,0:T(8,128)}, u32[]{:S(2)}) copy-start(f32[2,256,512]{2,1,0:T(8,128)} %copy-done.5) | copy-start | bytes 3145732

commit v8 on v7

--- a/solution.py
+++ b/solution.py
@@ -171,7 +171,7 @@
         grid=(columns // width,),
         in_specs=[SMEM, pl.BlockSpec((orders, rows, width), lambda i: (0, 0, i))],
         out_specs=pl.BlockSpec((rows, width), lambda i: (0, i)),
-        compiler_params=pltpu.CompilerParams(vmem_limit_bytes=8 * 2**20),
+        compiler_params=pltpu.CompilerParams(vmem_limit_bytes=6 * 2**20),
     )(plan, video_cache)
 
 
@@ -376,8 +376,7 @@
             slice(side * HEAD_DIM, (side + 1) * HEAD_DIM),
         )
     for bit, out_ref in enumerate(out_refs):
-        align = align_ref[lax.axis_index("seq") ^ bit]
-        out_ref[...] = attend(query_ref[bit], kv_ref, frames_ref, align)
+        out_ref[...] = attend(query_ref[bit], kv_ref, frames_ref, align_ref[bit])
 
 
 def out_body(*refs):
@@ -456,13 +455,12 @@
         weight_body,
         [bfloat(2 * rows, 2 * width)] + [bfloat(rows, 2 * width)] * 3,
         [kv_weight, query_weight, other],
+        limit=4,
     )
     pieces[0] = swap(pieces[0], "seq", 1)
-    align_all = lax.all_to_all(
-        jnp.broadcast_to(alignment[None], (seq_size, audio_rows)), "seq", 0, 0, tiled=True
-    ).astype(jnp.float32)
-    tokens[1], tokens[2], across[0], pieces[0], align_all = lax.optimization_barrier(
-        (tokens[1], tokens[2], across[0], pieces[0], align_all)
+    aligns = [alignment, *(swap(alignment, "seq", bit) for bit in (1, 2, 3))]
+    tokens[1], tokens[2], across[0], pieces[0], *aligns = lax.optimization_barrier(
+        (tokens[1], tokens[2], across[0], pieces[0], *aligns)
     )
 
     tokens.append(swap(tokens[2], "seq", 1))
@@ -494,12 +492,10 @@
             pltpu.VMEM((4 * half_depth, 2 * width), jnp.bfloat16),
             pltpu.VMEM((8 * query_quarter, width), jnp.bfloat16),
         ],
-        limit=26,
+        limit=15,
     )
     out_fourth, third_rest = swap(out_third, "seq", 1), swap(out_third, "grp", 1)
-    send, out_fourth, third_rest = lax.optimization_barrier((send, out_fourth, third_rest))
     came = swap(send, "rep", 1)
-    fourth_rest = swap(out_fourth, "grp", 1)
 
     span = video_rows * seq_size
     blocks = jnp.stack([seq_at, seq_at ^ 1, seq_at ^ 2, seq_at ^ 3])
@@ -508,12 +504,15 @@
     own_piece, near_piece, far_piece, farther_piece = kernel_call(
         attention_body,
         [bfloat(audio_rows, HEAD_DIM)] * 4,
-        [frames_video, align_all[:, :, None], keep, came],
+        [frames_video, jnp.stack(aligns).astype(jnp.float32)[:, :, None], keep, came],
         scratch=[
             pltpu.VMEM((span, width), jnp.bfloat16),
             pltpu.VMEM((seq_size, audio_rows, HEAD_DIM), jnp.bfloat16),
         ],
-    )
+        limit=9,
+    )
+    out_fourth, own_piece = lax.optimization_barrier((out_fourth, own_piece))
+    fourth_rest = swap(out_fourth, "grp", 1)
     far_piece = swap(far_piece, "seq", 2)
     farther_piece = swap(farther_piece, "seq", 3)
     near_piece = swap(near_piece, "seq", 1)
@@ -533,6 +532,7 @@
             pltpu.SemaphoreType.DMA,
         ],
         loose_in=(4,),
+        limit=7,
     )
     came = swap(send, "rep", 1)
     across = swap((keep[1] + came[1].astype(jnp.float32)).astype(jnp.bfloat16), "mem", 1)

time: 134 us -> 151 us (1.13)
  waiting for transfers between devices: 45.5 us -> 92 us
  blocking collectives: 34 us -> 0 us
  starting transfers between devices: 32.8 us -> 38.8 us
  local copies, waits for them, and re-layouts: 2.81 us -> 0.81 us
    ppermute x25 -> x28, waiting for transfers between devices: 45.5 us -> 92 us  [swap(): return lax.ppermute(value, axis, [(i, i ^ bit) for i in range(size)])]
    all_to_all x1 -> x0, blocking collectives: 34 us -> none  [by_head(): lax.all_to_all(jnp.broadcast_to(alignment[None], (seq_size, audio_rows)),...]
    ppermute x25 -> x28, starting transfers between devices: 32.8 us -> 38.8 us  [swap(): return lax.ppermute(value, axis, [(i, i ^ bit) for i in range(size)])]
    unnamed x33 -> x24, local copies, waits for them, and re-layouts: 2.4 us -> 0.08 us
  transfers between devices with their start and end apart: 25 -> 28, of which waited for: 10 -> 14; matrix products, arithmetic and copies ran while one was open for 1% -> 1% of each run, Pallas kernels for 7% -> 4%
where the time goes in v8:
time: 151 us
  waiting for transfers between devices  92 us (61%)
  starting transfers between devices  38.8 us (26%)
  Pallas kernels  14.3 us (9%)
  other arithmetic  4.01 us (3%)
    ppermute x28, waiting for transfers between devices, swap(): return lax.ppermute(value, axis, [(i, i ^ bit) for i in range(size)])  92 us
    ppermute x28, starting transfers between devices, swap(): return lax.ppermute(value, axis, [(i, i ^ bit) for i in range(size)])  38.8 us
    pallas_call x5, Pallas kernels, kernel_call(): pl.pallas_call(whole, out_shape=outs, in_specs=spots + [ANY] * len(after)...  12.5 us
  transfers between devices with their start and end apart: 28, of which 14 were waited for; matrix products, arithmetic and copies ran while one was open for 1% of the time, Pallas kernels for 4%

profile of v8, /device:TPU:0, one launch (start us, length us, event | category | flops | bytes accessed | tf_op | source)
XLA Modules:
  0.0 150.7 jit_solution(6110142331564010763)
XLA Ops:
  0.6 3.3 %shard_map.87 = (bf16[640,512]{1,0:T(8,128)(2,1)}, bf16[640,1024]{1,0:T(8,128)(2,1)}, bf16[256,512]{1,0:T(8,128)(2,1)}) custom-call(s32[8]{0:T(128)} %refs_0_.2, bf16[3,192,2048]{2,1,0:T(8,128)(2,1)} %refs_1_.2, bf16[256,2048]{1,0:T(8,128)(2,1)} %refs_2_.1, bf16[1024,1024]{1,0:T(8,128)(2,1)} %refs_0_.3, bf16[512,512]{1,0:T(8,128)(2,1)} %refs_1_.3, ...), custom_call_target="tpu_custom_call" | custom-call | tf_op jit(solution)/shard_map/pallas_call | solution.py:130
  4.0 0.5 collective-permute-start.3
  4.5 2.7 %collective-permute-start = (bf16[640,512]{1,0:T(8,128)(2,1)}, bf16[640,512]{1,0:T(8,128)(2,1)S(1)}, u32[]{:S(2)}, u32[]{:S(2)}) collective-permute-start(bf16[640,512]{1,0:T(8,128)(2,1)} %get-tuple-element.36.refs_0_), channel_id=1, source_target_pairs={{0,4},{4,0},{8,12},{12,8},{1,5},{5,1},{9,13},{13,9},{2,6},{6,2},{1... | collective-permute-start | bytes 1966088 | tf_op jit(solution)/shard_map/ppermute | solution.py:116
  7.2 2.6 %collective-permute-start.1 = (bf16[640,512]{1,0:T(8,128)(2,1)}, bf16[640,512]{1,0:T(8,128)(2,1)S(1)}, u32[]{:S(2)}, u32[]{:S(2)}) collective-permute-start(bf16[640,512]{1,0:T(8,128)(2,1)} %get-tuple-element.36.refs_0_), channel_id=1, source_target_pairs={{0,8},{4,12},{8,0},{12,4},{1,9},{5,13},{9,1},{13,5},{2,10},{6,14},... | collective-permute-start | bytes 1966088 | tf_op jit(solution)/shard_map/ppermute | solution.py:116
  9.8 1.5 collective-permute-start.2
  11.3 0.3 shard_map.88
  11.5 0.5 collective-permute-start.4
  12.1 1.6 %collective-permute-start.5 = (s32[256]{0:T(256)S(1)}, s32[256]{0:T(256)S(1)}, u32[]{:S(2)}, u32[]{:S(2)}) collective-permute-start(s32[256]{0:T(256)S(1)} %copy-done.10), channel_id=1, source_target_pairs={{0,4},{4,0},{8,12},{12,8},{1,5},{5,1},{9,13},{13,9},{2,6},{6,2},{1... | collective-permute-start | bytes 3080 | tf_op jit(solution)/shard_map/ppermute | solution.py:116
  13.6 30.2 %collective-permute-done.5 = s32[256]{0:T(256)S(1)} collective-permute-done((s32[256]{0:T(256)S(1)}, s32[256]{0:T(256)S(1)}, u32[]{:S(2)}, u32[]{:S(2)}) %collective-permute-start.5) | collective-permute-done | bytes 1056 | tf_op jit(solution)/shard_map/ppermute | solution.py:116
  43.9 2.8 %collective-permute-start.6 = (s32[256]{0:T(256)S(1)}, s32[256]{0:T(256)S(1)}, u32[]{:S(2)}, u32[]{:S(2)}) collective-permute-start(s32[256]{0:T(256)S(1)} %copy-done.10), channel_id=1, source_target_pairs={{0,8},{4,12},{8,0},{12,4},{1,9},{5,13},{9,1},{13,5},{2,10},{6,14},... | collective-permute-start | bytes 3080 | tf_op jit(solution)/shard_map/ppermute | solution.py:116
  46.7 1.7 %collective-permute-done.6 = s32[256]{0:T(256)S(1)} collective-permute-done((s32[256]{0:T(256)S(1)}, s32[256]{0:T(256)S(1)}, u32[]{:S(2)}, u32[]{:S(2)}) %collective-permute-start.6) | collective-permute-done | bytes 1056 | tf_op jit(solution)/shard_map/ppermute | solution.py:116
  48.3 3.8 %collective-permute-start.7 = (s32[256]{0:T(256)S(1)}, s32[256]{0:T(256)S(1)}, u32[]{:S(2)}, u32[]{:S(2)}) collective-permute-start(s32[256]{0:T(256)S(1)} %copy-done.10), channel_id=1, source_target_pairs={{0,12},{4,8},{8,4},{12,0},{1,13},{5,9},{9,5},{13,1},{2,14},{6,10},... | collective-permute-start | bytes 3080 | tf_op jit(solution)/shard_map/ppermute | solution.py:116
  52.1 1.6 %collective-permute-done.7 = s32[256]{0:T(256)S(1)} collective-permute-done((s32[256]{0:T(256)S(1)}, s32[256]{0:T(256)S(1)}, u32[]{:S(2)}, u32[]{:S(2)}) %collective-permute-start.7) | collective-permute-done | bytes 1056 | tf_op jit(solution)/shard_map/ppermute | solution.py:116
  53.7 1.0 collective-permute-start.11
  54.7 1.6 %collective-permute-start.10 = (bf16[640,512]{1,0:T(8,128)(2,1)S(1)}, bf16[640,512]{1,0:T(8,128)(2,1)S(1)}, u32[]{:S(2)}, u32[]{:S(2)}) collective-permute-start(bf16[640,512]{1,0:T(8,128)(2,1)S(1)} %collective-permute-done.1.refs_4_), channel_id=1, source_target_pairs={{0,2},{2,0},{1,3},{3,1},{4,6},{6,4},{5,7},{7,5},{8,10},{10,8},{9,1... | collective-permute-start | bytes 1966088 | tf_op jit(solution)/shard_map/ppermute | solution.py:116
  56.3 3.3 %collective-permute-start.8 = (bf16[640,512]{1,0:T(8,128)(2,1)S(1)}, bf16[640,512]{1,0:T(8,128)(2,1)S(1)}, u32[]{:S(2)}, u32[]{:S(2)}) collective-permute-start(bf16[640,512]{1,0:T(8,128)(2,1)S(1)} %collective-permute-done.1.refs_4_), channel_id=1, source_target_pairs={{0,4},{4,0},{8,12},{12,8},{1,5},{5,1},{9,13},{13,9},{2,6},{6,2},{1... | collective-permute-start | bytes 1966088 | tf_op jit(solution)/shard_map/ppermute | solution.py:116
  59.6 0.5 collective-permute-start.9
  60.2 9.7 %collective-permute-done.11.refs_11_ = bf16[320,512]{1,0:T(8,128)(2,1)S(1)} collective-permute-done((bf16[320,512]{1,0:T(8,128)(2,1)S(1)}, bf16[320,512]{1,0:T(8,128)(2,1)S(1)}, u32[]{:S(2)}, u32[]{:S(2)}) %collective-permute-start.11) | collective-permute-done | bytes 327712 | tf_op jit(solution)/shard_map/ppermute | solution.py:116
  69.9 1.5 %collective-permute-start.13 = (bf16[320,512]{1,0:T(8,128)(2,1)S(1)}, bf16[320,512]{1,0:T(8,128)(2,1)S(1)}, u32[]{:S(2)}, u32[]{:S(2)}) collective-permute-start(bf16[320,512]{1,0:T(8,128)(2,1)S(1)} %collective-permute-done.4.refs_9_), channel_id=1, source_target_pairs={{0,16},{16,0},{1,17},{17,1},{2,18},{18,2},{3,19},{19,3},{4,20},{20... | collective-permute-start | bytes 983048 | tf_op jit(solution)/shard_map/ppermute | solution.py:116
  71.4 12.5 %collective-permute-done.12.refs_13_ = bf16[320,512]{1,0:T(8,128)(2,1)S(1)} collective-permute-done((bf16[320,512]{1,0:T(8,128)(2,1)S(1)}, bf16[320,512]{1,0:T(8,128)(2,1)S(1)}, u32[]{:S(2)}, u32[]{:S(2)}) %collective-permute-start.12) | collective-permute-done | bytes 327712 | tf_op jit(solution)/shard_map/ppermute | solution.py:116
  83.9 0.4 collective-permute-done.8.refs_6_
  84.3 1.5 collective-permute-start.16
  85.8 2.8 %collective-permute-start.19 = (bf16[512,512]{1,0:T(8,128)(2,1)S(1)}, bf16[512,512]{1,0:T(8,128)(2,1)S(1)}, u32[]{:S(2)}, u32[]{:S(2)}) collective-permute-start(bf16[512,512]{1,0:T(8,128)(2,1)S(1)} %copy-done.3), channel_id=1, source_target_pairs={{0,4},{4,0},{8,12},{12,8},{1,5},{5,1},{9,13},{13,9},{2,6},{6,2},{1... | collective-permute-start | bytes 1572872 | tf_op jit(solution)/shard_map/ppermute | solution.py:116
  88.6 1.5 %collective-permute-start.17 = (bf16[320,512]{1,0:T(8,128)(2,1)S(1)}, bf16[320,512]{1,0:T(8,128)(2,1)S(1)}, u32[]{:S(2)}, u32[]{:S(2)}) collective-permute-start(bf16[320,512]{1,0:T(8,128)(2,1)S(1)} %collective-permute-done.11.refs_11_), channel_id=1, source_target_pairs={{0,16},{16,0},{1,17},{17,1},{2,18},{18,2},{3,19},{19,3},{4,20},{20... | collective-permute-start | bytes 983048 | tf_op jit(solution)/shard_map/ppermute | solution.py:116
  90.1 0.5 collective-permute-start.18
  90.6 5.1 %collective-permute-done.19.refs_15_.refs_5_ = bf16[512,512]{1,0:T(8,128)(2,1)S(1)} collective-permute-done((bf16[512,512]{1,0:T(8,128)(2,1)S(1)}, bf16[512,512]{1,0:T(8,128)(2,1)S(1)}, u32[]{:S(2)}, u32[]{:S(2)}) %collective-permute-start.19) | collective-permute-done | bytes 524320 | tf_op jit(solution)/shard_map/ppermute | solution.py:116
  95.7 0.2 collective-permute-done.17.refs_12_
  96.0 3.5 %collective-permute-done.18.refs_14_ = bf16[320,512]{1,0:T(8,128)(2,1)S(1)} collective-permute-done((bf16[320,512]{1,0:T(8,128)(2,1)S(1)}, bf16[320,512]{1,0:T(8,128)(2,1)S(1)}, u32[]{:S(2)}, u32[]{:S(2)}) %collective-permute-start.18) | collective-permute-done | bytes 327712 | tf_op jit(solution)/shard_map/ppermute | solution.py:116
  99.5 3.9 %shard_map.89 = (f32[1280,256]{1,0:T(8,128)}, f32[1280,256]{1,0:T(8,128)S(1)}) custom-call(bf16[640,512]{1,0:T(8,128)(2,1)S(1)} %copy-done.7, bf16[640,512]{1,0:T(8,128)(2,1)S(1)} %collective-permute-done.2.refs_1_, bf16[640,512]{1,0:T(8,128)(2,1)S(1)} %collective-permute-done.refs_2_, bf16[640,512]{1,0:T(8,128)(2,1)S(1)} %collective-permute-done.9.refs_3_, ...), custom_call_target="tpu_custom_call" | custom-call | tf_op jit(solution)/shard_map/pallas_call | solution.py:130
  103.5 0.6 collective-permute-start.14
  104.4 14.3 %collective-permute-done.14.refs_6_ = bf16[256,512]{1,0:T(8,128)(2,1)S(1)} collective-permute-done((bf16[256,512]{1,0:T(8,128)(2,1)S(1)}, bf16[256,512]{1,0:T(8,128)(2,1)S(1)}, u32[]{:S(2)}, u32[]{:S(2)}) %collective-permute-start.14) | collective-permute-done | bytes 262176 | tf_op jit(solution)/shard_map/ppermute | solution.py:116
  118.9 0.1 copy.19
  119.4 1.6 %collective-permute-start.24 = (bf16[256,512]{1,0:T(8,128)(2,1)S(1)}, bf16[256,512]{1,0:T(8,128)(2,1)S(1)}, u32[]{:S(2)}, u32[]{:S(2)}) collective-permute-start(bf16[256,512]{1,0:T(8,128)(2,1)S(1)} %collective-permute-done.14.refs_6_), channel_id=1, source_target_pairs={{0,16},{16,0},{1,17},{17,1},{2,18},{18,2},{3,19},{19,3},{4,20},{20... | collective-permute-start | bytes 786440 | tf_op jit(solution)/shard_map/ppermute | solution.py:116
  121.0 3.5 %shard_map.90 = (bf16[256,128]{1,0:T(8,128)(2,1)S(1)}, bf16[256,128]{1,0:T(8,128)(2,1)S(1)}, bf16[256,128]{1,0:T(8,128)(2,1)S(1)}, bf16[256,128]{1,0:T(8,128)(2,1)S(1)}) custom-call(f32[1,768]{1,0:T(1,128)S(1)} %fusion.3.refs_0_, f32[4,256,1]{2,1,0:T(8,128)S(1)} %add_convert_fusion.refs_1_, f32[1280,256]{1,0:T(8,128)S(1)} %get-tuple-element.58.refs_2_, ...), custom_call_target="tpu_custom_call" | custom-call | tf_op jit(solution)/shard_map/pallas_call | solution.py:130
  124.4 2.5 %collective-permute-done.15.refs_8_ = bf16[256,512]{1,0:T(8,128)(2,1)S(1)} collective-permute-done((bf16[256,512]{1,0:T(8,128)(2,1)S(1)}, bf16[256,512]{1,0:T(8,128)(2,1)S(1)}, u32[]{:S(2)}, u32[]{:S(2)}) %collective-permute-start.15) | collective-permute-done | bytes 262176 | tf_op jit(solution)/shard_map/ppermute | solution.py:116
  126.9 1.5 collective-permute-start.25
  128.4 0.3 collective-permute-start.21
  128.7 0.5 collective-permute-start.22
  129.1 3.6 %collective-permute-start.23 = (bf16[256,128]{1,0:T(8,128)(2,1)S(1)}, bf16[256,128]{1,0:T(8,128)(2,1)S(1)}, u32[]{:S(2)}, u32[]{:S(2)}) collective-permute-start(bf16[256,128]{1,0:T(8,128)(2,1)S(1)} %get-tuple-element.64), channel_id=1, source_target_pairs={{0,12},{4,8},{8,4},{12,0},{1,13},{5,9},{9,5},{13,1},{2,14},{6,10},... | collective-permute-start | bytes 196616 | tf_op jit(solution)/shard_map/ppermute | solution.py:116
  132.8 3.1 %collective-permute-done.22.refs_2_ = bf16[256,128]{1,0:T(8,128)(2,1)S(1)} collective-permute-done((bf16[256,128]{1,0:T(8,128)(2,1)S(1)}, bf16[256,128]{1,0:T(8,128)(2,1)S(1)}, u32[]{:S(2)}, u32[]{:S(2)}) %collective-permute-start.22) | collective-permute-done | bytes 65568 | tf_op jit(solution)/shard_map/ppermute | solution.py:116
  135.9 1.5 shard_map.91
  137.5 1.9 %collective-permute-done.26 = bf16[2,256,512]{2,1,0:T(8,128)(2,1)S(1)} collective-permute-done((bf16[2,256,512]{2,1,0:T(8,128)(2,1)S(1)}, bf16[2,256,512]{2,1,0:T(8,128)(2,1)S(1)}, u32[]{:S(2)}, u32[]{:S(2)}) %collective-permute-start.26) | collective-permute-done | bytes 524320 | tf_op jit(solution)/shard_map/ppermute | solution.py:116
  139.4 0.9 fusion
  140.3 0.5 collective-permute-start.27
  140.9 1.8 %shard_map.86 = bf16[192,2048]{1,0:T(8,128)(2,1)} custom-call(s32[8]{0:T(128)S(1)} %copy-done.8, bf16[3,192,2048]{2,1,0:T(8,128)(2,1)S(1)} %copy-done), custom_call_target="tpu_custom_call" | custom-call | tf_op jit(solution)/shard_map/pallas_call | solution.py:168
  142.7 1.1 bitcast_add_fusion
  143.8 5.2 %collective-permute-done.27 = bf16[256,512]{1,0:T(8,128)(2,1)} collective-permute-done((bf16[256,512]{1,0:T(8,128)(2,1)}, bf16[256,512]{1,0:T(8,128)(2,1)}, u32[]{:S(2)}, u32[]{:S(2)}) %collective-permute-start.27) | collective-permute-done | bytes 262176 | tf_op jit(solution)/shard_map/ppermute | solution.py:116
  149.0 1.7 %add_convert_fusion.1 = bf16[256,512]{1,0:T(8,128)(2,1)} fusion(f32[256,512]{1,0:T(8,128)S(1)} %bitcast_add_fusion, bf16[256,512]{1,0:T(8,128)(2,1)} %collective-permute-done.27), kind=kLoop, calls=%fused_computation.2 | loop fusion | flops 393216 | bytes 1048576 | tf_op jit(solution)/shard_map/convert_element_type | solution.py:543
  (52 shorter events, 1.1 us)
Async XLA Ops:
  0.6 10.7 %copy-start.2 = (bf16[512,512]{1,0:T(8,128)(2,1)S(1)}, bf16[512,512]{1,0:T(8,128)(2,1)}, u32[]{:S(2)}) copy-start(bf16[512,512]{1,0:T(8,128)(2,1)} %refs_1_.3) | copy-start | bytes 1572868
  0.6 10.7 %copy-start.1 = (bf16[1024,1024]{1,0:T(8,128)(2,1)S(1)}, bf16[1024,1024]{1,0:T(8,128)(2,1)}, u32[]{:S(2)}) copy-start(bf16[1024,1024]{1,0:T(8,128)(2,1)} %refs_0_.3) | copy-start | bytes 6291460
  4.0 7.3 %collective-permute-start.3 = (bf16[640,1024]{1,0:T(8,128)(2,1)}, bf16[640,1024]{1,0:T(8,128)(2,1)S(1)}, u32[]{:S(2)}, u32[]{:S(2)}) collective-permute-start(bf16[640,1024]{1,0:T(8,128)(2,1)} %get-tuple-element.37), channel_id=1, source_target_pairs={{0,1},{1,0},{2,3},{3,2},{4,5},{5,4},{6,7},{7,6},{8,9},{9,8},{10,11... | collective-permute-start | bytes 3932168 | tf_op jit(solution)/shard_map/ppermute | solution.py:116
  4.5 7.5 %copy-start.10 = (s32[256]{0:T(256)S(1)}, s32[256]{0:T(256)}, u32[]{:S(2)}) copy-start(s32[256]{0:T(256)} %param.9) | copy-start | bytes 3076
  4.5 81.3 %copy-start.3 = (bf16[512,512]{1,0:T(8,128)(2,1)S(1)}, bf16[512,512]{1,0:T(8,128)(2,1)}, u32[]{:S(2)}) copy-start(bf16[512,512]{1,0:T(8,128)(2,1)} %refs_4_.3) | copy-start | bytes 1572868
  4.5 95.0 %copy-start.7 = (bf16[640,512]{1,0:T(8,128)(2,1)S(1)}, bf16[640,512]{1,0:T(8,128)(2,1)}, u32[]{:S(2)}) copy-start(bf16[640,512]{1,0:T(8,128)(2,1)} %get-tuple-element.36.refs_0_) | copy-start | bytes 1966084
  4.5 50.2 %collective-permute-start = (bf16[640,512]{1,0:T(8,128)(2,1)}, bf16[640,512]{1,0:T(8,128)(2,1)S(1)}, u32[]{:S(2)}, u32[]{:S(2)}) collective-permute-start(bf16[640,512]{1,0:T(8,128)(2,1)} %get-tuple-element.36.refs_0_), channel_id=1, source_target_pairs={{0,4},{4,0},{8,12},{12,8},{1,5},{5,1},{9,13},{13,9},{2,6},{6,2},{1... | collective-permute-start | bytes 1966088 | tf_op jit(solution)/shard_map/ppermute | solution.py:116
  7.2 47.5 %collective-permute-start.1 = (bf16[640,512]{1,0:T(8,128)(2,1)}, bf16[640,512]{1,0:T(8,128)(2,1)S(1)}, u32[]{:S(2)}, u32[]{:S(2)}) collective-permute-start(bf16[640,512]{1,0:T(8,128)(2,1)} %get-tuple-element.36.refs_0_), channel_id=1, source_target_pairs={{0,8},{4,12},{8,0},{12,4},{1,9},{5,13},{9,1},{13,5},{2,10},{6,14},... | collective-permute-start | bytes 1966088 | tf_op jit(solution)/shard_map/ppermute | solution.py:116
  9.8 44.9 %collective-permute-start.2 = (bf16[640,512]{1,0:T(8,128)(2,1)}, bf16[640,512]{1,0:T(8,128)(2,1)S(1)}, u32[]{:S(2)}, u32[]{:S(2)}) collective-permute-start(bf16[640,512]{1,0:T(8,128)(2,1)} %get-tuple-element.36.refs_0_), channel_id=1, source_target_pairs={{0,2},{2,0},{1,3},{3,1},{4,6},{6,4},{5,7},{7,5},{8,10},{10,8},{9,1... | collective-permute-start | bytes 1966088 | tf_op jit(solution)/shard_map/ppermute | solution.py:116
  11.5 43.2 %collective-permute-start.4 = (bf16[320,512]{1,0:T(8,128)(2,1)S(1)}, bf16[320,512]{1,0:T(8,128)(2,1)S(1)}, u32[]{:S(2)}, u32[]{:S(2)}) collective-permute-start(bf16[320,512]{1,0:T(8,128)(2,1)S(1)} %get-tuple-element.38), channel_id=1, source_target_pairs={{0,4},{4,0},{8,12},{12,8},{1,5},{5,1},{9,13},{13,9},{2,6},{6,2},{1... | collective-permute-start | bytes 983048 | tf_op jit(solution)/shard_map/ppermute | solution.py:116
  12.1 31.8 %collective-permute-start.5 = (s32[256]{0:T(256)S(1)}, s32[256]{0:T(256)S(1)}, u32[]{:S(2)}, u32[]{:S(2)}) collective-permute-start(s32[256]{0:T(256)S(1)} %copy-done.10), channel_id=1, source_target_pairs={{0,4},{4,0},{8,12},{12,8},{1,5},{5,1},{9,13},{13,9},{2,6},{6,2},{1... | collective-permute-start | bytes 3080 | tf_op jit(solution)/shard_map/ppermute | solution.py:116
  43.9 4.5 %collective-permute-start.6 = (s32[256]{0:T(256)S(1)}, s32[256]{0:T(256)S(1)}, u32[]{:S(2)}, u32[]{:S(2)}) collective-permute-start(s32[256]{0:T(256)S(1)} %copy-done.10), channel_id=1, source_target_pairs={{0,8},{4,12},{8,0},{12,4},{1,9},{5,13},{9,1},{13,5},{2,10},{6,14},... | collective-permute-start | bytes 3080 | tf_op jit(solution)/shard_map/ppermute | solution.py:116
  48.3 5.4 %collective-permute-start.7 = (s32[256]{0:T(256)S(1)}, s32[256]{0:T(256)S(1)}, u32[]{:S(2)}, u32[]{:S(2)}) collective-permute-start(s32[256]{0:T(256)S(1)} %copy-done.10), channel_id=1, source_target_pairs={{0,12},{4,8},{8,4},{12,0},{1,13},{5,9},{9,5},{13,1},{2,14},{6,10},... | collective-permute-start | bytes 3080 | tf_op jit(solution)/shard_map/ppermute | solution.py:116
  53.7 16.2 %collective-permute-start.11 = (bf16[320,512]{1,0:T(8,128)(2,1)S(1)}, bf16[320,512]{1,0:T(8,128)(2,1)S(1)}, u32[]{:S(2)}, u32[]{:S(2)}) collective-permute-start(bf16[320,512]{1,0:T(8,128)(2,1)S(1)} %get-tuple-element.41), channel_id=1, source_target_pairs={{0,8},{4,12},{8,0},{12,4},{1,9},{5,13},{9,1},{13,5},{2,10},{6,14},... | collective-permute-start | bytes 983048 | tf_op jit(solution)/shard_map/ppermute | solution.py:116
  54.7 29.1 %collective-permute-start.10 = (bf16[640,512]{1,0:T(8,128)(2,1)S(1)}, bf16[640,512]{1,0:T(8,128)(2,1)S(1)}, u32[]{:S(2)}, u32[]{:S(2)}) collective-permute-start(bf16[640,512]{1,0:T(8,128)(2,1)S(1)} %collective-permute-done.1.refs_4_), channel_id=1, source_target_pairs={{0,2},{2,0},{1,3},{3,1},{4,6},{6,4},{5,7},{7,5},{8,10},{10,8},{9,1... | collective-permute-start | bytes 1966088 | tf_op jit(solution)/shard_map/ppermute | solution.py:116
  56.3 28.0 %collective-permute-start.8 = (bf16[640,512]{1,0:T(8,128)(2,1)S(1)}, bf16[640,512]{1,0:T(8,128)(2,1)S(1)}, u32[]{:S(2)}, u32[]{:S(2)}) collective-permute-start(bf16[640,512]{1,0:T(8,128)(2,1)S(1)} %collective-permute-done.1.refs_4_), channel_id=1, source_target_pairs={{0,4},{4,0},{8,12},{12,8},{1,5},{5,1},{9,13},{13,9},{2,6},{6,2},{1... | collective-permute-start | bytes 1966088 | tf_op jit(solution)/shard_map/ppermute | solution.py:116
  59.6 24.7 %collective-permute-start.9 = (bf16[640,512]{1,0:T(8,128)(2,1)S(1)}, bf16[640,512]{1,0:T(8,128)(2,1)S(1)}, u32[]{:S(2)}, u32[]{:S(2)}) collective-permute-start(bf16[640,512]{1,0:T(8,128)(2,1)S(1)} %collective-permute-done.refs_2_), channel_id=1, source_target_pairs={{0,2},{2,0},{1,3},{3,1},{4,6},{6,4},{5,7},{7,5},{8,10},{10,8},{9,1... | collective-permute-start | bytes 1966088 | tf_op jit(solution)/shard_map/ppermute | solution.py:116
  60.2 23.7 %collective-permute-start.12 = (bf16[320,512]{1,0:T(8,128)(2,1)S(1)}, bf16[320,512]{1,0:T(8,128)(2,1)S(1)}, u32[]{:S(2)}, u32[]{:S(2)}) collective-permute-start(bf16[320,512]{1,0:T(8,128)(2,1)S(1)} %get-tuple-element.42), channel_id=1, source_target_pairs={{0,12},{4,8},{8,4},{12,0},{1,13},{5,9},{9,5},{13,1},{2,14},{6,10},... | collective-permute-start | bytes 983048 | tf_op jit(solution)/shard_map/ppermute | solution.py:116
  69.9 14.0 %collective-permute-start.13 = (bf16[320,512]{1,0:T(8,128)(2,1)S(1)}, bf16[320,512]{1,0:T(8,128)(2,1)S(1)}, u32[]{:S(2)}, u32[]{:S(2)}) collective-permute-start(bf16[320,512]{1,0:T(8,128)(2,1)S(1)} %collective-permute-done.4.refs_9_), channel_id=1, source_target_pairs={{0,16},{16,0},{1,17},{17,1},{2,18},{18,2},{3,19},{19,3},{4,20},{20... | collective-permute-start | bytes 983048 | tf_op jit(solution)/shard_map/ppermute | solution.py:116
  84.3 15.2 %collective-permute-start.16 = (bf16[640,512]{1,0:T(8,128)(2,1)S(1)}, bf16[640,512]{1,0:T(8,128)(2,1)S(1)}, u32[]{:S(2)}, u32[]{:S(2)}) collective-permute-start(bf16[640,512]{1,0:T(8,128)(2,1)S(1)} %collective-permute-done.8.refs_6_), channel_id=1, source_target_pairs={{0,2},{2,0},{1,3},{3,1},{4,6},{6,4},{5,7},{7,5},{8,10},{10,8},{9,1... | collective-permute-start | bytes 1966088 | tf_op jit(solution)/shard_map/ppermute | solution.py:116
  85.8 10.0 %collective-permute-start.19 = (bf16[512,512]{1,0:T(8,128)(2,1)S(1)}, bf16[512,512]{1,0:T(8,128)(2,1)S(1)}, u32[]{:S(2)}, u32[]{:S(2)}) collective-permute-start(bf16[512,512]{1,0:T(8,128)(2,1)S(1)} %copy-done.3), channel_id=1, source_target_pairs={{0,4},{4,0},{8,12},{12,8},{1,5},{5,1},{9,13},{13,9},{2,6},{6,2},{1... | collective-permute-start | bytes 1572872 | tf_op jit(solution)/shard_map/ppermute | solution.py:116
  88.6 7.4 %collective-permute-start.17 = (bf16[320,512]{1,0:T(8,128)(2,1)S(1)}, bf16[320,512]{1,0:T(8,128)(2,1)S(1)}, u32[]{:S(2)}, u32[]{:S(2)}) collective-permute-start(bf16[320,512]{1,0:T(8,128)(2,1)S(1)} %collective-permute-done.11.refs_11_), channel_id=1, source_target_pairs={{0,16},{16,0},{1,17},{17,1},{2,18},{18,2},{3,19},{19,3},{4,20},{20... | collective-permute-start | bytes 983048 | tf_op jit(solution)/shard_map/ppermute | solution.py:116
  90.1 9.4 %collective-permute-start.18 = (bf16[320,512]{1,0:T(8,128)(2,1)S(1)}, bf16[320,512]{1,0:T(8,128)(2,1)S(1)}, u32[]{:S(2)}, u32[]{:S(2)}) collective-permute-start(bf16[320,512]{1,0:T(8,128)(2,1)S(1)} %collective-permute-done.12.refs_13_), channel_id=1, source_target_pairs={{0,16},{16,0},{1,17},{17,1},{2,18},{18,2},{3,19},{19,3},{4,20},{20... | collective-permute-start | bytes 983048 | tf_op jit(solution)/shard_map/ppermute | solution.py:116
  99.5 4.0 %copy-start.11 = (bf16[256,512]{1,0:T(8,128)(2,1)S(1)}, bf16[256,512]{1,0:T(8,128)(2,1)}, u32[]{:S(2)}) copy-start(bf16[256,512]{1,0:T(8,128)(2,1)} %get-tuple-element.45) | copy-start | bytes 786436
  103.4 17.5 %collective-permute-start.20 = (f32[1280,256]{1,0:T(8,128)}, f32[1280,256]{1,0:T(8,128)}, u32[]{:S(2)}, u32[]{:S(2)}) collective-permute-start(f32[1280,256]{1,0:T(8,128)} %get-tuple-element.59), channel_id=1, source_target_pairs={{0,1},{1,0},{2,3},{3,2},{4,5},{5,4},{6,7},{7,6},{8,9},{9,8},{10,11... | collective-permute-start | bytes 3932168 | tf_op jit(solution)/shard_map/ppermute | solution.py:116
  103.5 15.2 %collective-permute-start.14 = (bf16[256,512]{1,0:T(8,128)(2,1)S(1)}, bf16[256,512]{1,0:T(8,128)(2,1)S(1)}, u32[]{:S(2)}, u32[]{:S(2)}) collective-permute-start(bf16[256,512]{1,0:T(8,128)(2,1)S(1)} %copy-done.11), channel_id=1, source_target_pairs={{0,8},{4,12},{8,0},{12,4},{1,9},{5,13},{9,1},{13,5},{2,10},{6,14},... | collective-permute-start | bytes 786440 | tf_op jit(solution)/shard_map/ppermute | solution.py:116
  118.8 8.2 %collective-permute-start.15 = (bf16[256,512]{1,0:T(8,128)(2,1)S(1)}, bf16[256,512]{1,0:T(8,128)(2,1)S(1)}, u32[]{:S(2)}, u32[]{:S(2)}) collective-permute-start(bf16[256,512]{1,0:T(8,128)(2,1)S(1)} %collective-permute-done.14.refs_6_), channel_id=1, source_target_pairs={{0,4},{4,0},{8,12},{12,8},{1,5},{5,1},{9,13},{13,9},{2,6},{6,2},{1... | collective-permute-start | bytes 786440 | tf_op jit(solution)/shard_map/ppermute | solution.py:116
  119.4 13.4 %collective-permute-start.24 = (bf16[256,512]{1,0:T(8,128)(2,1)S(1)}, bf16[256,512]{1,0:T(8,128)(2,1)S(1)}, u32[]{:S(2)}, u32[]{:S(2)}) collective-permute-start(bf16[256,512]{1,0:T(8,128)(2,1)S(1)} %collective-permute-done.14.refs_6_), channel_id=1, source_target_pairs={{0,16},{16,0},{1,17},{17,1},{2,18},{18,2},{3,19},{19,3},{4,20},{20... | collective-permute-start | bytes 786440 | tf_op jit(solution)/shard_map/ppermute | solution.py:116
  121.0 15.0 %copy-start.4 = (bf16[512,512]{1,0:T(8,128)(2,1)S(1)}, bf16[512,512]{1,0:T(8,128)(2,1)}, u32[]{:S(2)}) copy-start(bf16[512,512]{1,0:T(8,128)(2,1)} %refs_4_.3) | copy-start | bytes 1572868
  126.9 9.0 %collective-permute-start.25 = (bf16[256,512]{1,0:T(8,128)(2,1)S(1)}, bf16[256,512]{1,0:T(8,128)(2,1)S(1)}, u32[]{:S(2)}, u32[]{:S(2)}) collective-permute-start(bf16[256,512]{1,0:T(8,128)(2,1)S(1)} %collective-permute-done.15.refs_8_), channel_id=1, source_target_pairs={{0,16},{16,0},{1,17},{17,1},{2,18},{18,2},{3,19},{19,3},{4,20},{20... | collective-permute-start | bytes 786440 | tf_op jit(solution)/shard_map/ppermute | solution.py:116
  128.4 4.4 %collective-permute-start.21 = (bf16[256,128]{1,0:T(8,128)(2,1)S(1)}, bf16[256,128]{1,0:T(8,128)(2,1)S(1)}, u32[]{:S(2)}, u32[]{:S(2)}) collective-permute-start(bf16[256,128]{1,0:T(8,128)(2,1)S(1)} %get-tuple-element.62), channel_id=1, source_target_pairs={{0,4},{4,0},{8,12},{12,8},{1,5},{5,1},{9,13},{13,9},{2,6},{6,2},{1... | collective-permute-start | bytes 196616 | tf_op jit(solution)/shard_map/ppermute | solution.py:116
  128.7 7.2 %collective-permute-start.22 = (bf16[256,128]{1,0:T(8,128)(2,1)S(1)}, bf16[256,128]{1,0:T(8,128)(2,1)S(1)}, u32[]{:S(2)}, u32[]{:S(2)}) collective-permute-start(bf16[256,128]{1,0:T(8,128)(2,1)S(1)} %get-tuple-element.63), channel_id=1, source_target_pairs={{0,8},{4,12},{8,0},{12,4},{1,9},{5,13},{9,1},{13,5},{2,10},{6,14},... | collective-permute-start | bytes 196616 | tf_op jit(solution)/shard_map/ppermute | solution.py:116
  129.1 11.7 %copy-start = (bf16[3,192,2048]{2,1,0:T(8,128)(2,1)S(1)}, bf16[3,192,2048]{2,1,0:T(8,128)(2,1)}, u32[]{:S(2)}) copy-start(bf16[3,192,2048]{2,1,0:T(8,128)(2,1)} %refs_1_.2) | copy-start | bytes 7077892
  129.1 11.7 %copy-start.8 = (s32[8]{0:T(128)S(1)}, s32[8]{0:T(128)}, u32[]{:S(2)}) copy-start(s32[8]{0:T(128)} %refs_0_.2) | copy-start | bytes 100
  129.1 6.8 %collective-permute-start.23 = (bf16[256,128]{1,0:T(8,128)(2,1)S(1)}, bf16[256,128]{1,0:T(8,128)(2,1)S(1)}, u32[]{:S(2)}, u32[]{:S(2)}) collective-permute-start(bf16[256,128]{1,0:T(8,128)(2,1)S(1)} %get-tuple-element.64), channel_id=1, source_target_pairs={{0,12},{4,8},{8,4},{12,0},{1,13},{5,9},{9,5},{13,1},{2,14},{6,10},... | collective-permute-start | bytes 196616 | tf_op jit(solution)/shard_map/ppermute | solution.py:116
  137.4 2.0 %copy-start.5 = (f32[2,256,512]{2,1,0:T(8,128)}, f32[2,256,512]{2,1,0:T(8,128)S(1)}, u32[]{:S(2)}) copy-start(f32[2,256,512]{2,1,0:T(8,128)S(1)} %get-tuple-element.66) | copy-start | bytes 3145732
  137.4 2.0 %collective-permute-start.26 = (bf16[2,256,512]{2,1,0:T(8,128)(2,1)S(1)}, bf16[2,256,512]{2,1,0:T(8,128)(2,1)S(1)}, u32[]{:S(2)}, u32[]{:S(2)}) collective-permute-start(bf16[2,256,512]{2,1,0:T(8,128)(2,1)S(1)} %get-tuple-element.67), channel_id=1, source_target_pairs={{0,1},{1,0},{2,3},{3,2},{4,5},{5,4},{6,7},{7,6},{8,9},{9,8},{10,11... | collective-permute-start | bytes 1572872 | tf_op jit(solution)/shard_map/ppermute | solution.py:116
  139.4 0.9 copy-start.9
  140.3 8.7 %collective-permute-start.27 = (bf16[256,512]{1,0:T(8,128)(2,1)}, bf16[256,512]{1,0:T(8,128)(2,1)}, u32[]{:S(2)}, u32[]{:S(2)}) collective-permute-start(bf16[256,512]{1,0:T(8,128)(2,1)} %fusion), channel_id=1, source_target_pairs={{0,2},{2,0},{1,3},{3,1},{4,6},{6,4},{5,7},{7,5},{8,10},{10,8},{9,1... | collective-permute-start | bytes 786440 | tf_op jit(solution)/shard_map/ppermute | solution.py:116
  140.9 1.8 %copy-start.6 = (f32[2,256,512]{2,1,0:T(8,128)S(1)}, f32[2,256,512]{2,1,0:T(8,128)}, u32[]{:S(2)}) copy-start(f32[2,256,512]{2,1,0:T(8,128)} %copy-done.5) | copy-start | bytes 3145732

commit v9 on v8

--- a/solution.py
+++ b/solution.py
@@ -263,7 +263,7 @@
         leaving.wait()
 
 
-def weight_body(kv_ref, query_ref, other_ref, own_ref, *piece_refs):
+def weight_body(align_ref, kv_ref, query_ref, other_ref, own_ref, *piece_refs):
     seq_at, rep_at, grp_at = (lax.axis_index(name) for name in ("seq", "rep", "grp"))
     kv_half, query_half = kv_ref.shape[0] // 2, query_ref.shape[0] // 2
     kv_rows, query_rows = kv_half // 2, query_half // 2
@@ -294,11 +294,17 @@
         fill(own_ref, 0, group, group * kv_rows, kv_half + group * fold)
     for bit, piece_ref in enumerate(piece_refs, 1):
         fill(piece_ref, bit, grp_at, 0, kv_rows)
+        spare = (piece_ref.shape[0] - kv_rows - fold, piece_ref.shape[1])
+        align = align_ref[...].astype(jnp.float32).astype(piece_ref.dtype)
+        row = jnp.concatenate(
+            [align, jnp.zeros((1, spare[1] - align.shape[1]), piece_ref.dtype)], axis=1
+        )
+        piece_ref[kv_rows + fold :, :] = jnp.broadcast_to(row, spare)
 
 
 def products_body(*refs):
     packed_refs, weight_refs = refs[:8], refs[8:15]
-    send_ref, keep_ref, rows_ref, audio_ref, kv_ref, query_ref = refs[15:]
+    own_align, align_ref, send_ref, keep_ref, rows_ref, audio_ref, kv_ref, query_ref = refs[15:]
     seq_at, mem_at, grp_at = (lax.axis_index(name) for name in ("seq", "mem", "grp"))
     rows, audio_rows = rows_ref.shape[0] // 4, audio_ref.shape[0] // 4
     depth, lane = rows_ref.shape[1] // 4, audio_ref.shape[1] // 4
@@ -331,6 +337,10 @@
     for bit in range(1, 4):
         place(weight_refs[2 * bit - 1], seq_at ^ bit, grp_at, 0, kv_half)
         place(weight_refs[2 * bit], seq_at ^ bit, 1 - grp_at, 0, kv_half)
+        align_ref[bit] = weight_refs[2 * bit - 1][kv_half + fold :, : align_ref.shape[2]]
+    align_ref[0] = jnp.broadcast_to(
+        own_align[...].astype(jnp.float32).astype(align_ref.dtype), align_ref.shape[1:]
+    )
 
     count = 4 * rows
     columns = keep_ref.shape[1]
@@ -376,14 +386,15 @@
             slice(side * HEAD_DIM, (side + 1) * HEAD_DIM),
         )
     for bit, out_ref in enumerate(out_refs):
-        out_ref[...] = attend(query_ref[bit], kv_ref, frames_ref, align_ref[bit])
+        align = align_ref[bit].astype(jnp.float32)[:8].T[:, :1]
+        out_ref[...] = attend(query_ref[bit], kv_ref, frames_ref, align)
 
 
 def out_body(*refs):
-    piece_refs, (own_w, partner_w, *part_refs), (send_ref, keep_ref, heads_ref, weight_ref, sem) = (
+    piece_refs, (own_w, *part_refs), (send_ref, keep_ref, heads_ref, weight_ref, sem) = (
         refs[:4],
-        refs[4:10],
-        refs[10:],
+        refs[4:11],
+        refs[11:],
     )
     seq_at, grp_at = lax.axis_index("seq"), lax.axis_index("grp")
     place = lax.axis_index("mem") * 2 + lax.axis_index("rep")
@@ -395,15 +406,14 @@
     depth = part_refs[0].shape[0]
     mine = pl.ds(pl.multiple_of(grp_at * depth, depth), depth)
     rest = pl.ds(pl.multiple_of((1 - grp_at) * depth, depth), depth)
-    for bit in range(2):
-        weight_ref[1 + bit, mine] = part_refs[2 * bit][...]
-        weight_ref[1 + bit, rest] = part_refs[2 * bit + 1][...]
+    for bit in range(1, 4):
+        weight_ref[bit, mine] = part_refs[2 * bit - 2][...]
+        weight_ref[bit, rest] = part_refs[2 * bit - 1][...]
     for bit in (1, 2, 3, 0):
         if bit == 0:
             copy.wait()
         slot = seq_at ^ bit ^ place
-        weight = partner_w[...] if bit == 1 else weight_ref[max(bit - 1, 0)]
-        value = jnp.dot(heads, weight, preferred_element_type=jnp.float32)
+        value = jnp.dot(heads, weight_ref[bit], preferred_element_type=jnp.float32)
 
         @pl.when(slot % 2 == 1)
         def _():
@@ -453,39 +463,36 @@
     rows = half_depth // 2 + query_quarter // 2
     weight_own, *pieces = kernel_call(
         weight_body,
-        [bfloat(2 * rows, 2 * width)] + [bfloat(rows, 2 * width)] * 3,
-        [kv_weight, query_weight, other],
+        [bfloat(2 * rows, 2 * width)] + [bfloat(rows + 16, 2 * width)] * 3,
+        [alignment[None], kv_weight, query_weight, other],
         limit=4,
     )
-    pieces[0] = swap(pieces[0], "seq", 1)
-    aligns = [alignment, *(swap(alignment, "seq", bit) for bit in (1, 2, 3))]
-    tokens[1], tokens[2], across[0], pieces[0], *aligns = lax.optimization_barrier(
-        (tokens[1], tokens[2], across[0], pieces[0], *aligns)
-    )
-
+    pieces = [swap(piece, "seq", bit) for bit, piece in enumerate(pieces, 1)]
+
+    across.append(swap(tokens[1], "mem", 1))
     tokens.append(swap(tokens[2], "seq", 1))
-    across += [swap(tokens[1], "mem", 1), swap(tokens[2], "mem", 1)]
-    pieces[1:] = [swap(piece, "seq", bit) for bit, piece in enumerate(pieces[1:], 2)]
+    across.append(swap(tokens[2], "mem", 1))
+    pieces[0], across[0], across[1] = lax.optimization_barrier(
+        (pieces[0], across[0], across[1])
+    )
     rest = [swap(pieces[0], "grp", 1)]
-    tokens[3], across[1], across[2], pieces[1], pieces[2], rest[0], out_half = (
-        lax.optimization_barrier(
-            (tokens[3], across[1], across[2], pieces[1], pieces[2], rest[0], out_half)
-        )
-    )
-
+    tokens[3], across[2], rest[0], pieces[1] = lax.optimization_barrier(
+        (tokens[3], across[2], rest[0], pieces[1])
+    )
     across.append(swap(tokens[3], "mem", 1))
     rest += [swap(piece, "grp", 1) for piece in pieces[1:]]
-    out_partner, out_third = swap(out_weight, "seq", 1), swap(out_half, "seq", 2)
+
+    out_half, tokens[3] = lax.optimization_barrier((out_half, tokens[3]))
+    out_third, out_partner = swap(out_half, "seq", 2), swap(out_half, "seq", 1)
     weights = [weight_own]
     for piece, other in zip(pieces, rest):
         weights += [piece, other]
     rows = seq_size * (video_rows + audio_rows // 2)
     sums = jax.ShapeDtypeStruct((rows, width), jnp.float32)
-    send, keep = kernel_call(
+    aligns, send, keep = kernel_call(
         products_body,
-        [sums, sums],
-        [value for pair in zip(tokens, across) for value in pair] + weights,
-        after=(out_partner,),
+        [bfloat(4, 16, audio_rows), sums, sums],
+        [value for pair in zip(tokens, across) for value in pair] + weights + [alignment[None]],
         scratch=[
             pltpu.VMEM((seq_size * video_rows, 4 * half_depth), jnp.bfloat16),
             pltpu.VMEM((seq_size * audio_rows, 8 * query_quarter), jnp.bfloat16),
@@ -494,8 +501,10 @@
         ],
         limit=15,
     )
+    send, out_third, out_partner = lax.optimization_barrier((send, out_third, out_partner))
+    came = swap(send, "rep", 1)
     out_fourth, third_rest = swap(out_third, "seq", 1), swap(out_third, "grp", 1)
-    came = swap(send, "rep", 1)
+    partner_rest = swap(out_partner, "grp", 1)
 
     span = video_rows * seq_size
     blocks = jnp.stack([seq_at, seq_at ^ 1, seq_at ^ 2, seq_at ^ 3])
@@ -504,7 +513,7 @@
     own_piece, near_piece, far_piece, farther_piece = kernel_call(
         attention_body,
         [bfloat(audio_rows, HEAD_DIM)] * 4,
-        [frames_video, jnp.stack(aligns).astype(jnp.float32)[:, :, None], keep, came],
+        [frames_video, aligns, keep, came],
         scratch=[
             pltpu.VMEM((span, width), jnp.bfloat16),
             pltpu.VMEM((seq_size, audio_rows, HEAD_DIM), jnp.bfloat16),
@@ -518,7 +527,8 @@
     near_piece = swap(near_piece, "seq", 1)
 
     columns = out_weight.shape[1]
-    weights = [out_weight, out_partner, out_third, third_rest, out_fourth, fourth_rest]
+    weights = [out_weight, out_partner, partner_rest]
+    weights += [out_third, third_rest, out_fourth, fourth_rest]
     send, keep = kernel_call(
         out_body,
         [
@@ -528,7 +538,7 @@
         [own_piece, near_piece, far_piece, farther_piece, *weights],
         scratch=[
             pltpu.VMEM((seq_size, audio_rows, HEAD_DIM), jnp.bfloat16),
-            pltpu.VMEM((3, *out_weight.shape), jnp.bfloat16),
+            pltpu.VMEM((seq_size, *out_weight.shape), jnp.bfloat16),
             pltpu.SemaphoreType.DMA,
         ],
         loose_in=(4,),

time: 151 us -> 136 us (0.901)
  waiting for transfers between devices: 92 us -> 82.9 us
  starting transfers between devices: 38.8 us -> 31.9 us
    ppermute x28 -> x26, waiting for transfers between devices: 92 us -> 82.9 us  [swap(): return lax.ppermute(value, axis, [(i, i ^ bit) for i in range(size)])]
    ppermute x28 -> x26, starting transfers between devices: 38.8 us -> 31.9 us  [swap(): return lax.ppermute(value, axis, [(i, i ^ bit) for i in range(size)])]
    unnamed x24 -> x22, local copies, waits for them, and re-layouts: 0.08 us -> 1.77 us
  transfers between devices with their start and end apart: 28 -> 26, of which waited for: 14 -> 17; matrix products, arithmetic and copies ran while one was open for 1% -> 1% of each run, Pallas kernels for 4% -> 6%
where the time goes in v9:
time: 136 us
  waiting for transfers between devices  82.9 us (61%)
  starting transfers between devices  31.9 us (23%)
  Pallas kernels  14.1 us (10%)
  other arithmetic  3.88 us (3%)
  local copies, waits for them, and re-layouts  1.94 us (1%)
    ppermute x26, waiting for transfers between devices, swap(): return lax.ppermute(value, axis, [(i, i ^ bit) for i in range(size)])  82.9 us
    ppermute x26, starting transfers between devices, swap(): return lax.ppermute(value, axis, [(i, i ^ bit) for i in range(size)])  31.9 us
    pallas_call x5, Pallas kernels, kernel_call(): pl.pallas_call(whole, out_shape=outs, in_specs=spots + [ANY] * len(after)...  12.3 us
  transfers between devices with their start and end apart: 26, of which 17 were waited for; matrix products, arithmetic and copies ran while one was open for 1% of the time, Pallas kernels for 6%

profile of v9, /device:TPU:0, one launch (start us, length us, event | category | flops | bytes accessed | tf_op | source)
XLA Modules:
  0.0 135.5 jit_solution(8843746981331677943)
XLA Ops:
  0.7 3.3 %shard_map.87 = (bf16[640,512]{1,0:T(8,128)(2,1)}, bf16[640,1024]{1,0:T(8,128)(2,1)}, bf16[256,512]{1,0:T(8,128)(2,1)}) custom-call(s32[8]{0:T(128)} %refs_0_.1, bf16[3,192,2048]{2,1,0:T(8,128)(2,1)} %refs_1_.2, bf16[256,2048]{1,0:T(8,128)(2,1)} %refs_2_.2, bf16[1024,1024]{1,0:T(8,128)(2,1)} %refs_1_.3, bf16[512,512]{1,0:T(8,128)(2,1)} %refs_2_.3, ...), custom_call_target="tpu_custom_call" | custom-call | tf_op jit(solution)/shard_map/pallas_call | solution.py:130
  4.0 0.5 collective-permute-start
  4.5 2.6 %collective-permute-start.3 = (bf16[640,512]{1,0:T(8,128)(2,1)}, bf16[640,512]{1,0:T(8,128)(2,1)S(1)}, u32[]{:S(2)}, u32[]{:S(2)}) collective-permute-start(bf16[640,512]{1,0:T(8,128)(2,1)} %get-tuple-element.34.refs_0_), channel_id=1, source_target_pairs={{0,4},{4,0},{8,12},{12,8},{1,5},{5,1},{9,13},{13,9},{2,6},{6,2},{1... | collective-permute-start | bytes 1966088 | tf_op jit(solution)/shard_map/ppermute | solution.py:116
  7.2 2.6 %collective-permute-start.5 = (bf16[640,512]{1,0:T(8,128)(2,1)}, bf16[640,512]{1,0:T(8,128)(2,1)S(1)}, u32[]{:S(2)}, u32[]{:S(2)}) collective-permute-start(bf16[640,512]{1,0:T(8,128)(2,1)} %get-tuple-element.34.refs_0_), channel_id=1, source_target_pairs={{0,8},{4,12},{8,0},{12,4},{1,9},{5,13},{9,1},{13,5},{2,10},{6,14},... | collective-permute-start | bytes 1966088 | tf_op jit(solution)/shard_map/ppermute | solution.py:116
  9.8 1.5 %collective-permute-start.2 = (bf16[640,512]{1,0:T(8,128)(2,1)}, bf16[640,512]{1,0:T(8,128)(2,1)S(1)}, u32[]{:S(2)}, u32[]{:S(2)}) collective-permute-start(bf16[640,512]{1,0:T(8,128)(2,1)} %get-tuple-element.34.refs_0_), channel_id=1, source_target_pairs={{0,2},{2,0},{1,3},{3,1},{4,6},{6,4},{5,7},{7,5},{8,10},{10,8},{9,1... | collective-permute-start | bytes 1966088 | tf_op jit(solution)/shard_map/ppermute | solution.py:116
  11.3 25.4 %collective-permute-done.3.refs_2_ = bf16[640,512]{1,0:T(8,128)(2,1)S(1)} collective-permute-done((bf16[640,512]{1,0:T(8,128)(2,1)}, bf16[640,512]{1,0:T(8,128)(2,1)S(1)}, u32[]{:S(2)}, u32[]{:S(2)}) %collective-permute-start.3) | collective-permute-done | bytes 655392 | tf_op jit(solution)/shard_map/ppermute | solution.py:116
  36.6 1.7 %collective-permute-start.4 = (bf16[640,512]{1,0:T(8,128)(2,1)S(1)}, bf16[640,512]{1,0:T(8,128)(2,1)S(1)}, u32[]{:S(2)}, u32[]{:S(2)}) collective-permute-start(bf16[640,512]{1,0:T(8,128)(2,1)S(1)} %collective-permute-done.3.refs_2_), channel_id=1, source_target_pairs={{0,2},{2,0},{1,3},{3,1},{4,6},{6,4},{5,7},{7,5},{8,10},{10,8},{9,1... | collective-permute-start | bytes 1966088 | tf_op jit(solution)/shard_map/ppermute | solution.py:116
  38.3 0.3 shard_map.88
  38.7 0.5 collective-permute-done.5.refs_4_
  39.2 1.5 %collective-permute-start.6 = (bf16[640,512]{1,0:T(8,128)(2,1)S(1)}, bf16[640,512]{1,0:T(8,128)(2,1)S(1)}, u32[]{:S(2)}, u32[]{:S(2)}) collective-permute-start(bf16[640,512]{1,0:T(8,128)(2,1)S(1)} %collective-permute-done.5.refs_4_), channel_id=1, source_target_pairs={{0,4},{4,0},{8,12},{12,8},{1,5},{5,1},{9,13},{13,9},{2,6},{6,2},{1... | collective-permute-start | bytes 1966088 | tf_op jit(solution)/shard_map/ppermute | solution.py:116
  40.7 0.4 collective-permute-start.7
  41.1 2.6 %collective-permute-start.9 = (bf16[336,512]{1,0:T(8,128)(2,1)S(1)}, bf16[336,512]{1,0:T(8,128)(2,1)S(1)}, u32[]{:S(2)}, u32[]{:S(2)}) collective-permute-start(bf16[336,512]{1,0:T(8,128)(2,1)S(1)} %get-tuple-element.40), channel_id=1, source_target_pairs={{0,8},{4,12},{8,0},{12,4},{1,9},{5,13},{9,1},{13,5},{2,10},{6,14},... | collective-permute-start | bytes 1032200 | tf_op jit(solution)/shard_map/ppermute | solution.py:116
  43.7 10.5 %collective-permute-done.4.refs_3_ = bf16[640,512]{1,0:T(8,128)(2,1)S(1)} collective-permute-done((bf16[640,512]{1,0:T(8,128)(2,1)S(1)}, bf16[640,512]{1,0:T(8,128)(2,1)S(1)}, u32[]{:S(2)}, u32[]{:S(2)}) %collective-permute-start.4) | collective-permute-done | bytes 655392 | tf_op jit(solution)/shard_map/ppermute | solution.py:116
  54.2 2.8 %collective-permute-done.1.refs_9_ = bf16[336,512]{1,0:T(8,128)(2,1)S(1)} collective-permute-done((bf16[336,512]{1,0:T(8,128)(2,1)S(1)}, bf16[336,512]{1,0:T(8,128)(2,1)S(1)}, u32[]{:S(2)}, u32[]{:S(2)}) %collective-permute-start.1) | collective-permute-done | bytes 344096 | tf_op jit(solution)/shard_map/ppermute | solution.py:116
  57.0 1.5 %collective-permute-start.8 = (bf16[336,512]{1,0:T(8,128)(2,1)S(1)}, bf16[336,512]{1,0:T(8,128)(2,1)S(1)}, u32[]{:S(2)}, u32[]{:S(2)}) collective-permute-start(bf16[336,512]{1,0:T(8,128)(2,1)S(1)} %collective-permute-done.1.refs_9_), channel_id=1, source_target_pairs={{0,16},{16,0},{1,17},{17,1},{2,18},{18,2},{3,19},{19,3},{4,20},{20... | collective-permute-start | bytes 1032200 | tf_op jit(solution)/shard_map/ppermute | solution.py:116
  58.6 2.5 %collective-permute-start.12 = (bf16[336,512]{1,0:T(8,128)(2,1)S(1)}, bf16[336,512]{1,0:T(8,128)(2,1)S(1)}, u32[]{:S(2)}, u32[]{:S(2)}) collective-permute-start(bf16[336,512]{1,0:T(8,128)(2,1)S(1)} %get-tuple-element.48), channel_id=1, source_target_pairs={{0,12},{4,8},{8,4},{12,0},{1,13},{5,9},{9,5},{13,1},{2,14},{6,10},... | collective-permute-start | bytes 1032200 | tf_op jit(solution)/shard_map/ppermute | solution.py:116
  61.0 8.9 %collective-permute-done.6.refs_6_ = bf16[640,512]{1,0:T(8,128)(2,1)S(1)} collective-permute-done((bf16[640,512]{1,0:T(8,128)(2,1)S(1)}, bf16[640,512]{1,0:T(8,128)(2,1)S(1)}, u32[]{:S(2)}, u32[]{:S(2)}) %collective-permute-start.6) | collective-permute-done | bytes 655392 | tf_op jit(solution)/shard_map/ppermute | solution.py:116
  69.9 0.6 collective-permute-start.10
  70.6 7.1 %collective-permute-done.12.refs_13_ = bf16[336,512]{1,0:T(8,128)(2,1)S(1)} collective-permute-done((bf16[336,512]{1,0:T(8,128)(2,1)S(1)}, bf16[336,512]{1,0:T(8,128)(2,1)S(1)}, u32[]{:S(2)}, u32[]{:S(2)}) %collective-permute-start.12) | collective-permute-done | bytes 344096 | tf_op jit(solution)/shard_map/ppermute | solution.py:116
  77.7 1.5 %collective-permute-start.13 = (bf16[336,512]{1,0:T(8,128)(2,1)S(1)}, bf16[336,512]{1,0:T(8,128)(2,1)S(1)}, u32[]{:S(2)}, u32[]{:S(2)}) collective-permute-start(bf16[336,512]{1,0:T(8,128)(2,1)S(1)} %collective-permute-done.12.refs_13_), channel_id=1, source_target_pairs={{0,16},{16,0},{1,17},{17,1},{2,18},{18,2},{3,19},{19,3},{4,20},{20... | collective-permute-start | bytes 1032200 | tf_op jit(solution)/shard_map/ppermute | solution.py:116
  79.2 0.5 collective-permute-start.11
  79.7 3.1 %collective-permute-start.14 = (bf16[256,512]{1,0:T(8,128)(2,1)S(1)}, bf16[256,512]{1,0:T(8,128)(2,1)}, u32[]{:S(2)}, u32[]{:S(2)}) collective-permute-start(bf16[256,512]{1,0:T(8,128)(2,1)S(1)} %copy-done.10), channel_id=1, source_target_pairs={{0,8},{4,12},{8,0},{12,4},{1,9},{5,13},{9,1},{13,5},{2,10},{6,14},... | collective-permute-start | bytes 786440 | tf_op jit(solution)/shard_map/ppermute | solution.py:116
  82.8 5.9 %collective-permute-done.13.refs_14_ = bf16[336,512]{1,0:T(8,128)(2,1)S(1)} collective-permute-done((bf16[336,512]{1,0:T(8,128)(2,1)S(1)}, bf16[336,512]{1,0:T(8,128)(2,1)S(1)}, u32[]{:S(2)}, u32[]{:S(2)}) %collective-permute-start.13) | collective-permute-done | bytes 344096 | tf_op jit(solution)/shard_map/ppermute | solution.py:116
  88.7 5.0 %collective-permute-done.11.refs_12_ = bf16[336,512]{1,0:T(8,128)(2,1)S(1)} collective-permute-done((bf16[336,512]{1,0:T(8,128)(2,1)S(1)}, bf16[336,512]{1,0:T(8,128)(2,1)S(1)}, u32[]{:S(2)}, u32[]{:S(2)}) %collective-permute-start.11) | collective-permute-done | bytes 344096 | tf_op jit(solution)/shard_map/ppermute | solution.py:116
  93.7 3.9 %shard_map.89 = (bf16[4,16,256]{2,1,0:T(8,128)(2,1)S(1)}, f32[1280,256]{1,0:T(8,128)}, f32[1280,256]{1,0:T(8,128)S(1)}) custom-call(bf16[640,512]{1,0:T(8,128)(2,1)S(1)} %copy-done.4, bf16[640,512]{1,0:T(8,128)(2,1)S(1)} %collective-permute-done.2.refs_1_, bf16[640,512]{1,0:T(8,128)(2,1)S(1)} %collective-permute-done.3.refs_2_, ...), custom_call_target="tpu_custom_call" | custom-call | tf_op jit(solution)/shard_map/pallas_call | solution.py:130
  98.1 0.1 reshape.116
  98.2 1.5 %collective-permute-start.21 = (bf16[256,512]{1,0:T(8,128)(2,1)S(1)}, bf16[256,512]{1,0:T(8,128)(2,1)S(1)}, u32[]{:S(2)}, u32[]{:S(2)}) collective-permute-start(bf16[256,512]{1,0:T(8,128)(2,1)S(1)} %collective-permute-done.15.refs_5_), channel_id=1, source_target_pairs={{0,16},{16,0},{1,17},{17,1},{2,18},{18,2},{3,19},{19,3},{4,20},{20... | collective-permute-start | bytes 786440 | tf_op jit(solution)/shard_map/ppermute | solution.py:116
  99.7 0.6 collective-permute-start.22
  100.3 0.7 collective-permute-done.17.refs_3_
  101.0 2.2 %shard_map.90 = (bf16[256,128]{1,0:T(8,128)(2,1)S(1)}, bf16[256,128]{1,0:T(8,128)(2,1)S(1)}, bf16[256,128]{1,0:T(8,128)(2,1)S(1)}, bf16[256,128]{1,0:T(8,128)(2,1)S(1)}) custom-call(f32[1,768]{1,0:T(1,128)S(1)} %fusion.3.refs_0_, bf16[4,16,256]{2,1,0:T(8,128)(2,1)S(1)} %get-tuple-element.52.refs_1_, f32[1280,256]{1,0:T(8,128)S(1)} %get-tuple-element.53.refs_2_, ...), custom_call_target="tpu_custom_call" | custom-call | tf_op jit(solution)/shard_map/pallas_call | solution.py:130
  103.2 3.7 %collective-permute-done.16.refs_9_ = bf16[256,512]{1,0:T(8,128)(2,1)} collective-permute-done((bf16[256,512]{1,0:T(8,128)(2,1)}, bf16[256,512]{1,0:T(8,128)(2,1)}, u32[]{:S(2)}, u32[]{:S(2)}) %collective-permute-start.16) | collective-permute-done | bytes 262176 | tf_op jit(solution)/shard_map/ppermute | solution.py:116
  106.9 1.5 %collective-permute-start.23 = (bf16[256,512]{1,0:T(8,128)(2,1)}, bf16[256,512]{1,0:T(8,128)(2,1)S(1)}, u32[]{:S(2)}, u32[]{:S(2)}) collective-permute-start(bf16[256,512]{1,0:T(8,128)(2,1)} %collective-permute-done.16.refs_9_), channel_id=1, source_target_pairs={{0,16},{16,0},{1,17},{17,1},{2,18},{18,2},{3,19},{19,3},{4,20},{20... | collective-permute-start | bytes 786440 | tf_op jit(solution)/shard_map/ppermute | solution.py:116
  108.4 0.3 collective-permute-start.18
  108.7 1.7 %collective-permute-start.19 = (bf16[256,128]{1,0:T(8,128)(2,1)S(1)}, bf16[256,128]{1,0:T(8,128)(2,1)S(1)}, u32[]{:S(2)}, u32[]{:S(2)}) collective-permute-start(bf16[256,128]{1,0:T(8,128)(2,1)S(1)} %get-tuple-element.58), channel_id=1, source_target_pairs={{0,8},{4,12},{8,0},{12,4},{1,9},{5,13},{9,1},{13,5},{2,10},{6,14},... | collective-permute-start | bytes 196616 | tf_op jit(solution)/shard_map/ppermute | solution.py:116
  110.4 2.4 %collective-permute-start.20 = (bf16[256,128]{1,0:T(8,128)(2,1)S(1)}, bf16[256,128]{1,0:T(8,128)(2,1)S(1)}, u32[]{:S(2)}, u32[]{:S(2)}) collective-permute-start(bf16[256,128]{1,0:T(8,128)(2,1)S(1)} %get-tuple-element.59), channel_id=1, source_target_pairs={{0,12},{4,8},{8,4},{12,0},{1,13},{5,9},{9,5},{13,1},{2,14},{6,10},... | collective-permute-start | bytes 196616 | tf_op jit(solution)/shard_map/ppermute | solution.py:116
  113.0 2.8 %collective-permute-done.19.refs_2_ = bf16[256,128]{1,0:T(8,128)(2,1)S(1)} collective-permute-done((bf16[256,128]{1,0:T(8,128)(2,1)S(1)}, bf16[256,128]{1,0:T(8,128)(2,1)S(1)}, u32[]{:S(2)}, u32[]{:S(2)}) %collective-permute-start.19) | collective-permute-done | bytes 65568 | tf_op jit(solution)/shard_map/ppermute | solution.py:116
  115.8 0.8 collective-permute-done.20.refs_3_
  116.5 1.5 %collective-permute-done.23.refs_10_ = bf16[256,512]{1,0:T(8,128)(2,1)S(1)} collective-permute-done((bf16[256,512]{1,0:T(8,128)(2,1)}, bf16[256,512]{1,0:T(8,128)(2,1)S(1)}, u32[]{:S(2)}, u32[]{:S(2)}) %collective-permute-start.23) | collective-permute-done | bytes 262176 | tf_op jit(solution)/shard_map/ppermute | solution.py:116
  118.1 0.9 copy-done.6
  119.0 2.5 %shard_map.91 = (bf16[2,256,512]{2,1,0:T(8,128)(2,1)S(1)}, f32[2,256,512]{2,1,0:T(8,128)S(1)}) custom-call(bf16[256,128]{1,0:T(8,128)(2,1)S(1)} %get-tuple-element.56.refs_0_, bf16[256,128]{1,0:T(8,128)(2,1)S(1)} %collective-permute-done.18.refs_1_, bf16[256,128]{1,0:T(8,128)(2,1)S(1)} %collective-permute-done.19.refs_2_, ...), custom_call_target="tpu_custom_call" | custom-call | tf_op jit(solution)/shard_map/pallas_call | solution.py:130
  121.7 1.9 %collective-permute-done.24 = bf16[2,256,512]{2,1,0:T(8,128)(2,1)S(1)} collective-permute-done((bf16[2,256,512]{2,1,0:T(8,128)(2,1)S(1)}, bf16[2,256,512]{2,1,0:T(8,128)(2,1)S(1)}, u32[]{:S(2)}, u32[]{:S(2)}) %collective-permute-start.24) | collective-permute-done | bytes 524320 | tf_op jit(solution)/shard_map/ppermute | solution.py:116
  123.6 0.8 copy-done.9
  124.3 0.8 fusion
  125.1 0.5 collective-permute-start.25
  125.7 1.8 %shard_map.86 = bf16[192,2048]{1,0:T(8,128)(2,1)} custom-call(s32[8]{0:T(128)S(1)} %copy-done.8, bf16[3,192,2048]{2,1,0:T(8,128)(2,1)S(1)} %copy-done), custom_call_target="tpu_custom_call" | custom-call | tf_op jit(solution)/shard_map/pallas_call | solution.py:168
  127.5 1.1 bitcast_add_fusion
  128.6 5.2 %collective-permute-done.25 = bf16[256,512]{1,0:T(8,128)(2,1)} collective-permute-done((bf16[256,512]{1,0:T(8,128)(2,1)}, bf16[256,512]{1,0:T(8,128)(2,1)}, u32[]{:S(2)}, u32[]{:S(2)}) %collective-permute-start.25) | collective-permute-done | bytes 262176 | tf_op jit(solution)/shard_map/ppermute | solution.py:116
  133.8 1.7 %add_convert_fusion = bf16[256,512]{1,0:T(8,128)(2,1)} fusion(f32[256,512]{1,0:T(8,128)S(1)} %bitcast_add_fusion, bf16[256,512]{1,0:T(8,128)(2,1)} %collective-permute-done.25), kind=kLoop, calls=%fused_computation.1 | loop fusion | flops 393216 | bytes 1048576 | tf_op jit(solution)/shard_map/convert_element_type | solution.py:553
  (41 shorter events, 0.8 us)
Async XLA Ops:
  0.6 37.7 %copy-start.2 = (bf16[512,512]{1,0:T(8,128)(2,1)S(1)}, bf16[512,512]{1,0:T(8,128)(2,1)}, u32[]{:S(2)}) copy-start(bf16[512,512]{1,0:T(8,128)(2,1)} %refs_2_.3) | copy-start | bytes 1572868
  0.6 37.7 %copy-start.1 = (bf16[1024,1024]{1,0:T(8,128)(2,1)S(1)}, bf16[1024,1024]{1,0:T(8,128)(2,1)}, u32[]{:S(2)}) copy-start(bf16[1024,1024]{1,0:T(8,128)(2,1)} %refs_1_.3) | copy-start | bytes 6291460
  0.7 37.7 %copy-start.7 = (s32[256]{0:T(256)S(1)}, s32[256]{0:T(256)}, u32[]{:S(2)}) copy-start(s32[256]{0:T(256)} %param.9) | copy-start | bytes 3076
  4.0 34.3 %collective-permute-start = (bf16[640,1024]{1,0:T(8,128)(2,1)}, bf16[640,1024]{1,0:T(8,128)(2,1)S(1)}, u32[]{:S(2)}, u32[]{:S(2)}) collective-permute-start(bf16[640,1024]{1,0:T(8,128)(2,1)} %get-tuple-element.35), channel_id=1, source_target_pairs={{0,1},{1,0},{2,3},{3,2},{4,5},{5,4},{6,7},{7,6},{8,9},{9,8},{10,11... | collective-permute-start | bytes 3932168 | tf_op jit(solution)/shard_map/ppermute | solution.py:116
  4.5 32.1 %collective-permute-start.3 = (bf16[640,512]{1,0:T(8,128)(2,1)}, bf16[640,512]{1,0:T(8,128)(2,1)S(1)}, u32[]{:S(2)}, u32[]{:S(2)}) collective-permute-start(bf16[640,512]{1,0:T(8,128)(2,1)} %get-tuple-element.34.refs_0_), channel_id=1, source_target_pairs={{0,4},{4,0},{8,12},{12,8},{1,5},{5,1},{9,13},{13,9},{2,6},{6,2},{1... | collective-permute-start | bytes 1966088 | tf_op jit(solution)/shard_map/ppermute | solution.py:116
  7.2 32.0 %collective-permute-start.5 = (bf16[640,512]{1,0:T(8,128)(2,1)}, bf16[640,512]{1,0:T(8,128)(2,1)S(1)}, u32[]{:S(2)}, u32[]{:S(2)}) collective-permute-start(bf16[640,512]{1,0:T(8,128)(2,1)} %get-tuple-element.34.refs_0_), channel_id=1, source_target_pairs={{0,8},{4,12},{8,0},{12,4},{1,9},{5,13},{9,1},{13,5},{2,10},{6,14},... | collective-permute-start | bytes 1966088 | tf_op jit(solution)/shard_map/ppermute | solution.py:116
  9.8 31.4 %collective-permute-start.2 = (bf16[640,512]{1,0:T(8,128)(2,1)}, bf16[640,512]{1,0:T(8,128)(2,1)S(1)}, u32[]{:S(2)}, u32[]{:S(2)}) collective-permute-start(bf16[640,512]{1,0:T(8,128)(2,1)} %get-tuple-element.34.refs_0_), channel_id=1, source_target_pairs={{0,2},{2,0},{1,3},{3,1},{4,6},{6,4},{5,7},{7,5},{8,10},{10,8},{9,1... | collective-permute-start | bytes 1966088 | tf_op jit(solution)/shard_map/ppermute | solution.py:116
  36.6 17.6 %collective-permute-start.4 = (bf16[640,512]{1,0:T(8,128)(2,1)S(1)}, bf16[640,512]{1,0:T(8,128)(2,1)S(1)}, u32[]{:S(2)}, u32[]{:S(2)}) collective-permute-start(bf16[640,512]{1,0:T(8,128)(2,1)S(1)} %collective-permute-done.3.refs_2_), channel_id=1, source_target_pairs={{0,2},{2,0},{1,3},{3,1},{4,6},{6,4},{5,7},{7,5},{8,10},{10,8},{9,1... | collective-permute-start | bytes 1966088 | tf_op jit(solution)/shard_map/ppermute | solution.py:116
  38.3 41.4 %copy-start.10 = (bf16[256,512]{1,0:T(8,128)(2,1)S(1)}, bf16[256,512]{1,0:T(8,128)(2,1)}, u32[]{:S(2)}) copy-start(bf16[256,512]{1,0:T(8,128)(2,1)} %get-tuple-element.50) | copy-start | bytes 786436
  38.3 55.4 %copy-start.4 = (bf16[640,512]{1,0:T(8,128)(2,1)S(1)}, bf16[640,512]{1,0:T(8,128)(2,1)}, u32[]{:S(2)}) copy-start(bf16[640,512]{1,0:T(8,128)(2,1)} %get-tuple-element.34.refs_0_) | copy-start | bytes 1966084
  38.6 18.4 %collective-permute-start.1 = (bf16[336,512]{1,0:T(8,128)(2,1)S(1)}, bf16[336,512]{1,0:T(8,128)(2,1)S(1)}, u32[]{:S(2)}, u32[]{:S(2)}) collective-permute-start(bf16[336,512]{1,0:T(8,128)(2,1)S(1)} %get-tuple-element.36), channel_id=1, source_target_pairs={{0,4},{4,0},{8,12},{12,8},{1,5},{5,1},{9,13},{13,9},{2,6},{6,2},{1... | collective-permute-start | bytes 1032200 | tf_op jit(solution)/shard_map/ppermute | solution.py:116
  39.2 30.7 %collective-permute-start.6 = (bf16[640,512]{1,0:T(8,128)(2,1)S(1)}, bf16[640,512]{1,0:T(8,128)(2,1)S(1)}, u32[]{:S(2)}, u32[]{:S(2)}) collective-permute-start(bf16[640,512]{1,0:T(8,128)(2,1)S(1)} %collective-permute-done.5.refs_4_), channel_id=1, source_target_pairs={{0,4},{4,0},{8,12},{12,8},{1,5},{5,1},{9,13},{13,9},{2,6},{6,2},{1... | collective-permute-start | bytes 1966088 | tf_op jit(solution)/shard_map/ppermute | solution.py:116
  40.7 29.2 %collective-permute-start.7 = (bf16[640,512]{1,0:T(8,128)(2,1)S(1)}, bf16[640,512]{1,0:T(8,128)(2,1)S(1)}, u32[]{:S(2)}, u32[]{:S(2)}) collective-permute-start(bf16[640,512]{1,0:T(8,128)(2,1)S(1)} %collective-permute-done.5.refs_4_), channel_id=1, source_target_pairs={{0,2},{2,0},{1,3},{3,1},{4,6},{6,4},{5,7},{7,5},{8,10},{10,8},{9,1... | collective-permute-start | bytes 1966088 | tf_op jit(solution)/shard_map/ppermute | solution.py:116
  41.1 28.8 %collective-permute-start.9 = (bf16[336,512]{1,0:T(8,128)(2,1)S(1)}, bf16[336,512]{1,0:T(8,128)(2,1)S(1)}, u32[]{:S(2)}, u32[]{:S(2)}) collective-permute-start(bf16[336,512]{1,0:T(8,128)(2,1)S(1)} %get-tuple-element.40), channel_id=1, source_target_pairs={{0,8},{4,12},{8,0},{12,4},{1,9},{5,13},{9,1},{13,5},{2,10},{6,14},... | collective-permute-start | bytes 1032200 | tf_op jit(solution)/shard_map/ppermute | solution.py:116
  57.0 12.9 %collective-permute-start.8 = (bf16[336,512]{1,0:T(8,128)(2,1)S(1)}, bf16[336,512]{1,0:T(8,128)(2,1)S(1)}, u32[]{:S(2)}, u32[]{:S(2)}) collective-permute-start(bf16[336,512]{1,0:T(8,128)(2,1)S(1)} %collective-permute-done.1.refs_9_), channel_id=1, source_target_pairs={{0,16},{16,0},{1,17},{17,1},{2,18},{18,2},{3,19},{19,3},{4,20},{20... | collective-permute-start | bytes 1032200 | tf_op jit(solution)/shard_map/ppermute | solution.py:116
  58.6 19.1 %collective-permute-start.12 = (bf16[336,512]{1,0:T(8,128)(2,1)S(1)}, bf16[336,512]{1,0:T(8,128)(2,1)S(1)}, u32[]{:S(2)}, u32[]{:S(2)}) collective-permute-start(bf16[336,512]{1,0:T(8,128)(2,1)S(1)} %get-tuple-element.48), channel_id=1, source_target_pairs={{0,12},{4,8},{8,4},{12,0},{1,13},{5,9},{9,5},{13,1},{2,14},{6,10},... | collective-permute-start | bytes 1032200 | tf_op jit(solution)/shard_map/ppermute | solution.py:116
  69.9 23.8 %collective-permute-start.10 = (bf16[640,512]{1,0:T(8,128)(2,1)S(1)}, bf16[640,512]{1,0:T(8,128)(2,1)S(1)}, u32[]{:S(2)}, u32[]{:S(2)}) collective-permute-start(bf16[640,512]{1,0:T(8,128)(2,1)S(1)} %collective-permute-done.6.refs_6_), channel_id=1, source_target_pairs={{0,2},{2,0},{1,3},{3,1},{4,6},{6,4},{5,7},{7,5},{8,10},{10,8},{9,1... | collective-permute-start | bytes 1966088 | tf_op jit(solution)/shard_map/ppermute | solution.py:116
  77.7 11.0 %collective-permute-start.13 = (bf16[336,512]{1,0:T(8,128)(2,1)S(1)}, bf16[336,512]{1,0:T(8,128)(2,1)S(1)}, u32[]{:S(2)}, u32[]{:S(2)}) collective-permute-start(bf16[336,512]{1,0:T(8,128)(2,1)S(1)} %collective-permute-done.12.refs_13_), channel_id=1, source_target_pairs={{0,16},{16,0},{1,17},{17,1},{2,18},{18,2},{3,19},{19,3},{4,20},{20... | collective-permute-start | bytes 1032200 | tf_op jit(solution)/shard_map/ppermute | solution.py:116
  79.2 14.5 %collective-permute-start.11 = (bf16[336,512]{1,0:T(8,128)(2,1)S(1)}, bf16[336,512]{1,0:T(8,128)(2,1)S(1)}, u32[]{:S(2)}, u32[]{:S(2)}) collective-permute-start(bf16[336,512]{1,0:T(8,128)(2,1)S(1)} %collective-permute-done.9.refs_11_), channel_id=1, source_target_pairs={{0,16},{16,0},{1,17},{17,1},{2,18},{18,2},{3,19},{19,3},{4,20},{20... | collective-permute-start | bytes 1032200 | tf_op jit(solution)/shard_map/ppermute | solution.py:116
  79.7 17.9 %collective-permute-start.14 = (bf16[256,512]{1,0:T(8,128)(2,1)S(1)}, bf16[256,512]{1,0:T(8,128)(2,1)}, u32[]{:S(2)}, u32[]{:S(2)}) collective-permute-start(bf16[256,512]{1,0:T(8,128)(2,1)S(1)} %copy-done.10), channel_id=1, source_target_pairs={{0,8},{4,12},{8,0},{12,4},{1,9},{5,13},{9,1},{13,5},{2,10},{6,14},... | collective-permute-start | bytes 786440 | tf_op jit(solution)/shard_map/ppermute | solution.py:116
  82.8 14.9 %collective-permute-start.15 = (bf16[256,512]{1,0:T(8,128)(2,1)S(1)}, bf16[256,512]{1,0:T(8,128)(2,1)S(1)}, u32[]{:S(2)}, u32[]{:S(2)}) collective-permute-start(bf16[256,512]{1,0:T(8,128)(2,1)S(1)} %copy-done.10), channel_id=1, source_target_pairs={{0,4},{4,0},{8,12},{12,8},{1,5},{5,1},{9,13},{13,9},{2,6},{6,2},{1... | collective-permute-start | bytes 786440 | tf_op jit(solution)/shard_map/ppermute | solution.py:116
  97.6 5.5 %copy-start.5 = (bf16[256,512]{1,0:T(8,128)(2,1)}, bf16[256,512]{1,0:T(8,128)(2,1)S(1)}, u32[]{:S(2)}) copy-start(bf16[256,512]{1,0:T(8,128)(2,1)S(1)} %collective-permute-done.15.refs_5_) | copy-start | bytes 786436
  97.6 3.3 %collective-permute-start.17 = (f32[1280,256]{1,0:T(8,128)}, f32[1280,256]{1,0:T(8,128)S(1)}, u32[]{:S(2)}, u32[]{:S(2)}) collective-permute-start(f32[1280,256]{1,0:T(8,128)} %get-tuple-element.54), channel_id=1, source_target_pairs={{0,1},{1,0},{2,3},{3,2},{4,5},{5,4},{6,7},{7,6},{8,9},{9,8},{10,11... | collective-permute-start | bytes 3932168 | tf_op jit(solution)/shard_map/ppermute | solution.py:116
  97.9 9.0 %collective-permute-start.16 = (bf16[256,512]{1,0:T(8,128)(2,1)}, bf16[256,512]{1,0:T(8,128)(2,1)}, u32[]{:S(2)}, u32[]{:S(2)}) collective-permute-start(bf16[256,512]{1,0:T(8,128)(2,1)} %collective-permute-done.14.refs_7_), channel_id=1, source_target_pairs={{0,4},{4,0},{8,12},{12,8},{1,5},{5,1},{9,13},{13,9},{2,6},{6,2},{1... | collective-permute-start | bytes 786440 | tf_op jit(solution)/shard_map/ppermute | solution.py:116
  98.2 12.2 %collective-permute-start.21 = (bf16[256,512]{1,0:T(8,128)(2,1)S(1)}, bf16[256,512]{1,0:T(8,128)(2,1)S(1)}, u32[]{:S(2)}, u32[]{:S(2)}) collective-permute-start(bf16[256,512]{1,0:T(8,128)(2,1)S(1)} %collective-permute-done.15.refs_5_), channel_id=1, source_target_pairs={{0,16},{16,0},{1,17},{17,1},{2,18},{18,2},{3,19},{19,3},{4,20},{20... | collective-permute-start | bytes 786440 | tf_op jit(solution)/shard_map/ppermute | solution.py:116
  99.7 13.2 %collective-permute-start.22 = (bf16[256,512]{1,0:T(8,128)(2,1)}, bf16[256,512]{1,0:T(8,128)(2,1)S(1)}, u32[]{:S(2)}, u32[]{:S(2)}) collective-permute-start(bf16[256,512]{1,0:T(8,128)(2,1)} %collective-permute-done.14.refs_7_), channel_id=1, source_target_pairs={{0,16},{16,0},{1,17},{17,1},{2,18},{18,2},{3,19},{19,3},{4,20},{20... | collective-permute-start | bytes 786440 | tf_op jit(solution)/shard_map/ppermute | solution.py:116
  101.0 17.1 %copy-start.3 = (bf16[512,512]{1,0:T(8,128)(2,1)S(1)}, bf16[512,512]{1,0:T(8,128)(2,1)}, u32[]{:S(2)}) copy-start(bf16[512,512]{1,0:T(8,128)(2,1)} %refs_4_.3) | copy-start | bytes 1572868
  106.9 11.2 %collective-permute-start.23 = (bf16[256,512]{1,0:T(8,128)(2,1)}, bf16[256,512]{1,0:T(8,128)(2,1)S(1)}, u32[]{:S(2)}, u32[]{:S(2)}) collective-permute-start(bf16[256,512]{1,0:T(8,128)(2,1)} %collective-permute-done.16.refs_9_), channel_id=1, source_target_pairs={{0,16},{16,0},{1,17},{17,1},{2,18},{18,2},{3,19},{19,3},{4,20},{20... | collective-permute-start | bytes 786440 | tf_op jit(solution)/shard_map/ppermute | solution.py:116
  108.4 4.5 %collective-permute-start.18 = (bf16[256,128]{1,0:T(8,128)(2,1)S(1)}, bf16[256,128]{1,0:T(8,128)(2,1)S(1)}, u32[]{:S(2)}, u32[]{:S(2)}) collective-permute-start(bf16[256,128]{1,0:T(8,128)(2,1)S(1)} %get-tuple-element.57), channel_id=1, source_target_pairs={{0,4},{4,0},{8,12},{12,8},{1,5},{5,1},{9,13},{13,9},{2,6},{6,2},{1... | collective-permute-start | bytes 196616 | tf_op jit(solution)/shard_map/ppermute | solution.py:116
  108.7 7.1 %collective-permute-start.19 = (bf16[256,128]{1,0:T(8,128)(2,1)S(1)}, bf16[256,128]{1,0:T(8,128)(2,1)S(1)}, u32[]{:S(2)}, u32[]{:S(2)}) collective-permute-start(bf16[256,128]{1,0:T(8,128)(2,1)S(1)} %get-tuple-element.58), channel_id=1, source_target_pairs={{0,8},{4,12},{8,0},{12,4},{1,9},{5,13},{9,1},{13,5},{2,10},{6,14},... | collective-permute-start | bytes 196616 | tf_op jit(solution)/shard_map/ppermute | solution.py:116
  110.4 15.3 %copy-start.8 = (s32[8]{0:T(128)S(1)}, s32[8]{0:T(128)}, u32[]{:S(2)}) copy-start(s32[8]{0:T(128)} %refs_0_.1) | copy-start | bytes 100
  110.4 15.3 %copy-start = (bf16[3,192,2048]{2,1,0:T(8,128)(2,1)S(1)}, bf16[3,192,2048]{2,1,0:T(8,128)(2,1)}, u32[]{:S(2)}) copy-start(bf16[3,192,2048]{2,1,0:T(8,128)(2,1)} %refs_1_.2) | copy-start | bytes 7077892
  110.4 6.2 %collective-permute-start.20 = (bf16[256,128]{1,0:T(8,128)(2,1)S(1)}, bf16[256,128]{1,0:T(8,128)(2,1)S(1)}, u32[]{:S(2)}, u32[]{:S(2)}) collective-permute-start(bf16[256,128]{1,0:T(8,128)(2,1)S(1)} %get-tuple-element.59), channel_id=1, source_target_pairs={{0,12},{4,8},{8,4},{12,0},{1,13},{5,9},{9,5},{13,1},{2,14},{6,10},... | collective-permute-start | bytes 196616 | tf_op jit(solution)/shard_map/ppermute | solution.py:116
  118.1 1.0 copy-start.6
  121.6 2.0 %collective-permute-start.24 = (bf16[2,256,512]{2,1,0:T(8,128)(2,1)S(1)}, bf16[2,256,512]{2,1,0:T(8,128)(2,1)S(1)}, u32[]{:S(2)}, u32[]{:S(2)}) collective-permute-start(bf16[2,256,512]{2,1,0:T(8,128)(2,1)S(1)} %get-tuple-element.63), channel_id=1, source_target_pairs={{0,1},{1,0},{2,3},{3,2},{4,5},{5,4},{6,7},{7,6},{8,9},{9,8},{10,11... | collective-permute-start | bytes 1572872 | tf_op jit(solution)/shard_map/ppermute | solution.py:116
  123.6 0.8 copy-start.9
  125.1 8.7 %collective-permute-start.25 = (bf16[256,512]{1,0:T(8,128)(2,1)}, bf16[256,512]{1,0:T(8,128)(2,1)}, u32[]{:S(2)}, u32[]{:S(2)}) collective-permute-start(bf16[256,512]{1,0:T(8,128)(2,1)} %fusion), channel_id=1, source_target_pairs={{0,2},{2,0},{1,3},{3,1},{4,6},{6,4},{5,7},{7,5},{8,10},{10,8},{9,1... | collective-permute-start | bytes 786440 | tf_op jit(solution)/shard_map/ppermute | solution.py:116

commit v10 on v9

--- a/solution.py
+++ b/solution.py
@@ -457,7 +457,7 @@
         limit=61,
     )
 
-    tokens = [packed, swap(packed, "seq", 1), swap(packed, "seq", 2)]
+    tokens = [packed, swap(packed, "seq", 1)]
     across = [swap(packed, "mem", 1)]
     other = swap(other, "rep", 1)
     rows = half_depth // 2 + query_quarter // 2
@@ -467,6 +467,8 @@
         [alignment[None], kv_weight, query_weight, other],
         limit=4,
     )
+    packed, weight_own = lax.optimization_barrier((packed, weight_own))
+    tokens.append(swap(packed, "seq", 2))
     pieces = [swap(piece, "seq", bit) for bit, piece in enumerate(pieces, 1)]
 
     across.append(swap(tokens[1], "mem", 1))
@@ -480,7 +482,9 @@
         (tokens[3], across[2], rest[0], pieces[1])
     )
     across.append(swap(tokens[3], "mem", 1))
-    rest += [swap(piece, "grp", 1) for piece in pieces[1:]]
+    rest.append(swap(pieces[1], "grp", 1))
+    pieces[2], rest[1] = lax.optimization_barrier((pieces[2], rest[1]))
+    rest.append(swap(pieces[2], "grp", 1))
 
     out_half, tokens[3] = lax.optimization_barrier((out_half, tokens[3]))
     out_third, out_partner = swap(out_half, "seq", 2), swap(out_half, "seq", 1)
@@ -493,6 +497,7 @@
         products_body,
         [bfloat(4, 16, audio_rows), sums, sums],
         [value for pair in zip(tokens, across) for value in pair] + weights + [alignment[None]],
+        after=(out_third, out_partner),
         scratch=[
             pltpu.VMEM((seq_size * video_rows, 4 * half_depth), jnp.bfloat16),
             pltpu.VMEM((seq_size * audio_rows, 8 * query_quarter), jnp.bfloat16),
@@ -501,7 +506,6 @@
         ],
         limit=15,
     )
-    send, out_third, out_partner = lax.optimization_barrier((send, out_third, out_partner))
     came = swap(send, "rep", 1)
     out_fourth, third_rest = swap(out_third, "seq", 1), swap(out_third, "grp", 1)
     partner_rest = swap(out_partner, "grp", 1)

time: 136 us -> 139 us (1.022)
  starting transfers between devices: 31.9 us -> 38.1 us
    ppermute x26, starting transfers between devices: 31.9 us -> 38.1 us  [swap(): return lax.ppermute(value, axis, [(i, i ^ bit) for i in range(size)])]
  transfers between devices with their start and end apart: 26 -> 26, of which waited for: 17 -> 17; matrix products, arithmetic and copies ran while one was open for 1% -> 1% of each run, Pallas kernels for 6% -> 3%
where the time goes in v10:
time: 139 us
  waiting for transfers between devices  81.8 us (59%)
  starting transfers between devices  38.1 us (27%)
  Pallas kernels  13.1 us (9%)
  other arithmetic  3.98 us (3%)
    ppermute x26, waiting for transfers between devices, swap(): return lax.ppermute(value, axis, [(i, i ^ bit) for i in range(size)])  81.8 us
    ppermute x26, starting transfers between devices, swap(): return lax.ppermute(value, axis, [(i, i ^ bit) for i in range(size)])  38.1 us
    pallas_call x5, Pallas kernels, kernel_call(): pl.pallas_call(whole, out_shape=outs, in_specs=spots + [ANY] * len(after)...  11.2 us
  transfers between devices with their start and end apart: 26, of which 17 were waited for; matrix products, arithmetic and copies ran while one was open for 1% of the time, Pallas kernels for 3%

profile of v10, /device:TPU:0, one launch (start us, length us, event | category | flops | bytes accessed | tf_op | source)
XLA Modules:
  0.0 138.8 jit_solution(10056569830283543197)
XLA Ops:
  0.7 3.3 %shard_map.87 = (bf16[640,512]{1,0:T(8,128)(2,1)}, bf16[640,1024]{1,0:T(8,128)(2,1)}, bf16[256,512]{1,0:T(8,128)(2,1)}) custom-call(s32[8]{0:T(128)} %refs_0_.1, bf16[3,192,2048]{2,1,0:T(8,128)(2,1)} %refs_1_.2, bf16[256,2048]{1,0:T(8,128)(2,1)} %refs_2_.2, bf16[1024,1024]{1,0:T(8,128)(2,1)} %refs_1_.3, bf16[512,512]{1,0:T(8,128)(2,1)} %refs_2_.3, ...), custom_call_target="tpu_custom_call" | custom-call | tf_op jit(solution)/shard_map/pallas_call | solution.py:130
  4.0 0.5 collective-permute-start
  4.5 2.6 %collective-permute-start.6 = (bf16[640,512]{1,0:T(8,128)(2,1)}, bf16[640,512]{1,0:T(8,128)(2,1)S(1)}, u32[]{:S(2)}, u32[]{:S(2)}) collective-permute-start(bf16[640,512]{1,0:T(8,128)(2,1)} %get-tuple-element.39.refs_0_), channel_id=1, source_target_pairs={{0,4},{4,0},{8,12},{12,8},{1,5},{5,1},{9,13},{13,9},{2,6},{6,2},{1... | collective-permute-start | bytes 1966088 | tf_op jit(solution)/shard_map/ppermute | solution.py:116
  7.2 0.2 collective-permute-done.refs_3_
  7.4 0.3 shard_map.88
  7.7 0.8 copy-done.6
  8.5 4.0 %collective-permute-start.1 = (bf16[640,512]{1,0:T(8,128)(2,1)S(1)}, bf16[640,512]{1,0:T(8,128)(2,1)S(1)}, u32[]{:S(2)}, u32[]{:S(2)}) collective-permute-start(bf16[640,512]{1,0:T(8,128)(2,1)S(1)} %copy-done.6), channel_id=1, source_target_pairs={{0,8},{4,12},{8,0},{12,4},{1,9},{5,13},{9,1},{13,5},{2,10},{6,14},... | collective-permute-start | bytes 1966088 | tf_op jit(solution)/shard_map/ppermute | solution.py:116
  12.5 1.5 %collective-permute-start.5 = (bf16[640,512]{1,0:T(8,128)(2,1)S(1)}, bf16[640,512]{1,0:T(8,128)(2,1)S(1)}, u32[]{:S(2)}, u32[]{:S(2)}) collective-permute-start(bf16[640,512]{1,0:T(8,128)(2,1)S(1)} %copy-done.6), channel_id=1, source_target_pairs={{0,2},{2,0},{1,3},{3,1},{4,6},{6,4},{5,7},{7,5},{8,10},{10,8},{9,1... | collective-permute-start | bytes 1966088 | tf_op jit(solution)/shard_map/ppermute | solution.py:116
  13.9 20.3 %collective-permute-done.6.refs_2_ = bf16[640,512]{1,0:T(8,128)(2,1)S(1)} collective-permute-done((bf16[640,512]{1,0:T(8,128)(2,1)}, bf16[640,512]{1,0:T(8,128)(2,1)S(1)}, u32[]{:S(2)}, u32[]{:S(2)}) %collective-permute-start.6) | collective-permute-done | bytes 655392 | tf_op jit(solution)/shard_map/ppermute | solution.py:116
  34.3 1.6 %collective-permute-start.7 = (bf16[640,512]{1,0:T(8,128)(2,1)S(1)}, bf16[640,512]{1,0:T(8,128)(2,1)S(1)}, u32[]{:S(2)}, u32[]{:S(2)}) collective-permute-start(bf16[640,512]{1,0:T(8,128)(2,1)S(1)} %collective-permute-done.6.refs_2_), channel_id=1, source_target_pairs={{0,2},{2,0},{1,3},{3,1},{4,6},{6,4},{5,7},{7,5},{8,10},{10,8},{9,1... | collective-permute-start | bytes 1966088 | tf_op jit(solution)/shard_map/ppermute | solution.py:116
  35.9 5.8 %collective-permute-done.1.refs_4_ = bf16[640,512]{1,0:T(8,128)(2,1)S(1)} collective-permute-done((bf16[640,512]{1,0:T(8,128)(2,1)S(1)}, bf16[640,512]{1,0:T(8,128)(2,1)S(1)}, u32[]{:S(2)}, u32[]{:S(2)}) %collective-permute-start.1) | collective-permute-done | bytes 655392 | tf_op jit(solution)/shard_map/ppermute | solution.py:116
  41.7 0.8 collective-permute-start.2
  42.5 1.5 %collective-permute-start.3 = (bf16[640,512]{1,0:T(8,128)(2,1)S(1)}, bf16[640,512]{1,0:T(8,128)(2,1)S(1)}, u32[]{:S(2)}, u32[]{:S(2)}) collective-permute-start(bf16[640,512]{1,0:T(8,128)(2,1)S(1)} %collective-permute-done.1.refs_4_), channel_id=1, source_target_pairs={{0,2},{2,0},{1,3},{3,1},{4,6},{6,4},{5,7},{7,5},{8,10},{10,8},{9,1... | collective-permute-start | bytes 1966088 | tf_op jit(solution)/shard_map/ppermute | solution.py:116
  44.0 3.4 %collective-permute-start.9 = (bf16[336,512]{1,0:T(8,128)(2,1)S(1)}, bf16[336,512]{1,0:T(8,128)(2,1)S(1)}, u32[]{:S(2)}, u32[]{:S(2)}) collective-permute-start(bf16[336,512]{1,0:T(8,128)(2,1)S(1)} %get-tuple-element.42), channel_id=1, source_target_pairs={{0,8},{4,12},{8,0},{12,4},{1,9},{5,13},{9,1},{13,5},{2,10},{6,14},... | collective-permute-start | bytes 1032200 | tf_op jit(solution)/shard_map/ppermute | solution.py:116
  47.4 4.5 %collective-permute-done.7.refs_3_ = bf16[640,512]{1,0:T(8,128)(2,1)S(1)} collective-permute-done((bf16[640,512]{1,0:T(8,128)(2,1)S(1)}, bf16[640,512]{1,0:T(8,128)(2,1)S(1)}, u32[]{:S(2)}, u32[]{:S(2)}) %collective-permute-start.7) | collective-permute-done | bytes 655392 | tf_op jit(solution)/shard_map/ppermute | solution.py:116
  51.9 4.5 %collective-permute-done.4.refs_9_ = bf16[336,512]{1,0:T(8,128)(2,1)S(1)} collective-permute-done((bf16[336,512]{1,0:T(8,128)(2,1)S(1)}, bf16[336,512]{1,0:T(8,128)(2,1)S(1)}, u32[]{:S(2)}, u32[]{:S(2)}) %collective-permute-start.4) | collective-permute-done | bytes 344096 | tf_op jit(solution)/shard_map/ppermute | solution.py:116
  56.4 1.6 %collective-permute-start.8 = (bf16[336,512]{1,0:T(8,128)(2,1)S(1)}, bf16[336,512]{1,0:T(8,128)(2,1)S(1)}, u32[]{:S(2)}, u32[]{:S(2)}) collective-permute-start(bf16[336,512]{1,0:T(8,128)(2,1)S(1)} %collective-permute-done.4.refs_9_), channel_id=1, source_target_pairs={{0,16},{16,0},{1,17},{17,1},{2,18},{18,2},{3,19},{19,3},{4,20},{20... | collective-permute-start | bytes 1032200 | tf_op jit(solution)/shard_map/ppermute | solution.py:116
  57.9 3.7 %collective-permute-start.13 = (bf16[336,512]{1,0:T(8,128)(2,1)S(1)}, bf16[336,512]{1,0:T(8,128)(2,1)S(1)}, u32[]{:S(2)}, u32[]{:S(2)}) collective-permute-start(bf16[336,512]{1,0:T(8,128)(2,1)S(1)} %get-tuple-element.52), channel_id=1, source_target_pairs={{0,12},{4,8},{8,4},{12,0},{1,13},{5,9},{9,5},{13,1},{2,14},{6,10},... | collective-permute-start | bytes 1032200 | tf_op jit(solution)/shard_map/ppermute | solution.py:116
  61.6 4.2 %collective-permute-done.9.refs_11_ = bf16[336,512]{1,0:T(8,128)(2,1)S(1)} collective-permute-done((bf16[336,512]{1,0:T(8,128)(2,1)S(1)}, bf16[336,512]{1,0:T(8,128)(2,1)S(1)}, u32[]{:S(2)}, u32[]{:S(2)}) %collective-permute-start.9) | collective-permute-done | bytes 344096 | tf_op jit(solution)/shard_map/ppermute | solution.py:116
  65.8 10.7 %collective-permute-done.2.refs_6_ = bf16[640,512]{1,0:T(8,128)(2,1)S(1)} collective-permute-done((bf16[640,512]{1,0:T(8,128)(2,1)S(1)}, bf16[640,512]{1,0:T(8,128)(2,1)S(1)}, u32[]{:S(2)}, u32[]{:S(2)}) %collective-permute-start.2) | collective-permute-done | bytes 655392 | tf_op jit(solution)/shard_map/ppermute | solution.py:116
  76.5 1.6 %collective-permute-start.14 = (bf16[336,512]{1,0:T(8,128)(2,1)S(1)}, bf16[336,512]{1,0:T(8,128)(2,1)S(1)}, u32[]{:S(2)}, u32[]{:S(2)}) collective-permute-start(bf16[336,512]{1,0:T(8,128)(2,1)S(1)} %collective-permute-done.9.refs_11_), channel_id=1, source_target_pairs={{0,16},{16,0},{1,17},{17,1},{2,18},{18,2},{3,19},{19,3},{4,20},{20... | collective-permute-start | bytes 1032200 | tf_op jit(solution)/shard_map/ppermute | solution.py:116
  78.1 0.5 collective-permute-start.12
  78.6 6.2 %collective-permute-done.14.refs_12_ = bf16[336,512]{1,0:T(8,128)(2,1)S(1)} collective-permute-done((bf16[336,512]{1,0:T(8,128)(2,1)S(1)}, bf16[336,512]{1,0:T(8,128)(2,1)S(1)}, u32[]{:S(2)}, u32[]{:S(2)}) %collective-permute-start.14) | collective-permute-done | bytes 344096 | tf_op jit(solution)/shard_map/ppermute | solution.py:116
  84.9 1.6 %collective-permute-start.15 = (bf16[336,512]{1,0:T(8,128)(2,1)S(1)}, bf16[336,512]{1,0:T(8,128)(2,1)S(1)}, u32[]{:S(2)}, u32[]{:S(2)}) collective-permute-start(bf16[336,512]{1,0:T(8,128)(2,1)S(1)} %collective-permute-done.13.refs_13_), channel_id=1, source_target_pairs={{0,16},{16,0},{1,17},{17,1},{2,18},{18,2},{3,19},{19,3},{4,20},{20... | collective-permute-start | bytes 1032200 | tf_op jit(solution)/shard_map/ppermute | solution.py:116
  86.5 2.0 %collective-permute-start.10 = (bf16[256,512]{1,0:T(8,128)(2,1)S(1)}, bf16[256,512]{1,0:T(8,128)(2,1)S(1)}, u32[]{:S(2)}, u32[]{:S(2)}) collective-permute-start(bf16[256,512]{1,0:T(8,128)(2,1)S(1)} %copy-done.10), channel_id=1, source_target_pairs={{0,8},{4,12},{8,0},{12,4},{1,9},{5,13},{9,1},{13,5},{2,10},{6,14},... | collective-permute-start | bytes 786440 | tf_op jit(solution)/shard_map/ppermute | solution.py:116
  88.5 2.5 %collective-permute-start.16 = (bf16[256,512]{1,0:T(8,128)(2,1)S(1)}, bf16[256,512]{1,0:T(8,128)(2,1)S(1)}, u32[]{:S(2)}, u32[]{:S(2)}) collective-permute-start(bf16[256,512]{1,0:T(8,128)(2,1)S(1)} %copy-done.10), channel_id=1, source_target_pairs={{0,4},{4,0},{8,12},{12,8},{1,5},{5,1},{9,13},{13,9},{2,6},{6,2},{1... | collective-permute-start | bytes 786440 | tf_op jit(solution)/shard_map/ppermute | solution.py:116
  91.0 7.2 %collective-permute-done.10.refs_16_.refs_7_ = bf16[256,512]{1,0:T(8,128)(2,1)S(1)} collective-permute-done((bf16[256,512]{1,0:T(8,128)(2,1)S(1)}, bf16[256,512]{1,0:T(8,128)(2,1)S(1)}, u32[]{:S(2)}, u32[]{:S(2)}) %collective-permute-start.10) | collective-permute-done | bytes 262176 | tf_op jit(solution)/shard_map/ppermute | solution.py:116
  98.4 3.9 %shard_map.89 = (bf16[4,16,256]{2,1,0:T(8,128)(2,1)S(1)}, f32[1280,256]{1,0:T(8,128)}, f32[1280,256]{1,0:T(8,128)S(1)}) custom-call(bf16[640,512]{1,0:T(8,128)(2,1)S(1)} %copy-done.6, bf16[640,512]{1,0:T(8,128)(2,1)S(1)} %collective-permute-done.5.refs_1_, bf16[640,512]{1,0:T(8,128)(2,1)S(1)} %collective-permute-done.6.refs_2_, ...), custom_call_target="tpu_custom_call" | custom-call | tf_op jit(solution)/shard_map/pallas_call | solution.py:130
  102.5 1.6 %collective-permute-start.11 = (bf16[256,512]{1,0:T(8,128)(2,1)S(1)}, bf16[256,512]{1,0:T(8,128)(2,1)S(1)}, u32[]{:S(2)}, u32[]{:S(2)}) collective-permute-start(bf16[256,512]{1,0:T(8,128)(2,1)S(1)} %collective-permute-done.10.refs_16_.refs_7_), channel_id=1, source_target_pairs={{0,4},{4,0},{8,12},{12,8},{1,5},{5,1},{9,13},{13,9},{2,6},{6,2},{1... | collective-permute-start | bytes 786440 | tf_op jit(solution)/shard_map/ppermute | solution.py:116
  104.3 0.5 collective-permute-start.22
  104.8 1.6 %collective-permute-start.21 = (bf16[256,512]{1,0:T(8,128)(2,1)S(1)}, bf16[256,512]{1,0:T(8,128)(2,1)S(1)}, u32[]{:S(2)}, u32[]{:S(2)}) collective-permute-start(bf16[256,512]{1,0:T(8,128)(2,1)S(1)} %collective-permute-done.16.refs_17_.refs_5_), channel_id=1, source_target_pairs={{0,16},{16,0},{1,17},{17,1},{2,18},{18,2},{3,19},{19,3},{4,20},{20... | collective-permute-start | bytes 786440 | tf_op jit(solution)/shard_map/ppermute | solution.py:116
  106.4 2.2 %shard_map.90 = (bf16[256,128]{1,0:T(8,128)(2,1)S(1)}, bf16[256,128]{1,0:T(8,128)(2,1)S(1)}, bf16[256,128]{1,0:T(8,128)(2,1)S(1)}, bf16[256,128]{1,0:T(8,128)(2,1)S(1)}) custom-call(f32[1,768]{1,0:T(1,128)S(1)} %fusion.3.refs_0_, bf16[4,16,256]{2,1,0:T(8,128)(2,1)S(1)} %get-tuple-element.55.refs_1_, f32[1280,256]{1,0:T(8,128)S(1)} %get-tuple-element.56.refs_2_, ...), custom_call_target="tpu_custom_call" | custom-call | tf_op jit(solution)/shard_map/pallas_call | solution.py:130
  108.6 2.6 %collective-permute-done.11.refs_9_ = bf16[256,512]{1,0:T(8,128)(2,1)S(1)} collective-permute-done((bf16[256,512]{1,0:T(8,128)(2,1)S(1)}, bf16[256,512]{1,0:T(8,128)(2,1)S(1)}, u32[]{:S(2)}, u32[]{:S(2)}) %collective-permute-start.11) | collective-permute-done | bytes 262176 | tf_op jit(solution)/shard_map/ppermute | solution.py:116
  111.2 0.5 collective-permute-start.23
  111.8 1.5 %collective-permute-start.18 = (bf16[256,128]{1,0:T(8,128)(2,1)S(1)}, bf16[256,128]{1,0:T(8,128)(2,1)S(1)}, u32[]{:S(2)}, u32[]{:S(2)}) collective-permute-start(bf16[256,128]{1,0:T(8,128)(2,1)S(1)} %get-tuple-element.60), channel_id=1, source_target_pairs={{0,4},{4,0},{8,12},{12,8},{1,5},{5,1},{9,13},{13,9},{2,6},{6,2},{1... | collective-permute-start | bytes 196616 | tf_op jit(solution)/shard_map/ppermute | solution.py:116
  113.3 2.5 %collective-permute-start.19 = (bf16[256,128]{1,0:T(8,128)(2,1)S(1)}, bf16[256,128]{1,0:T(8,128)(2,1)S(1)}, u32[]{:S(2)}, u32[]{:S(2)}) collective-permute-start(bf16[256,128]{1,0:T(8,128)(2,1)S(1)} %get-tuple-element.61), channel_id=1, source_target_pairs={{0,8},{4,12},{8,0},{12,4},{1,9},{5,13},{9,1},{13,5},{2,10},{6,14},... | collective-permute-start | bytes 196616 | tf_op jit(solution)/shard_map/ppermute | solution.py:116
  115.8 0.4 collective-permute-start.20
  116.2 2.9 %collective-permute-done.21.refs_6_ = bf16[256,512]{1,0:T(8,128)(2,1)S(1)} collective-permute-done((bf16[256,512]{1,0:T(8,128)(2,1)S(1)}, bf16[256,512]{1,0:T(8,128)(2,1)S(1)}, u32[]{:S(2)}, u32[]{:S(2)}) %collective-permute-start.21) | collective-permute-done | bytes 262176 | tf_op jit(solution)/shard_map/ppermute | solution.py:116
  119.1 1.1 collective-permute-done.19.refs_2_
  120.2 1.7 %collective-permute-done.20.refs_3_ = bf16[256,128]{1,0:T(8,128)(2,1)S(1)} collective-permute-done((bf16[256,128]{1,0:T(8,128)(2,1)S(1)}, bf16[256,128]{1,0:T(8,128)(2,1)S(1)}, u32[]{:S(2)}, u32[]{:S(2)}) %collective-permute-start.20) | collective-permute-done | bytes 65568 | tf_op jit(solution)/shard_map/ppermute | solution.py:116
  121.8 2.2 %collective-permute-done.23.refs_10_ = bf16[256,512]{1,0:T(8,128)(2,1)S(1)} collective-permute-done((bf16[256,512]{1,0:T(8,128)(2,1)S(1)}, bf16[256,512]{1,0:T(8,128)(2,1)S(1)}, u32[]{:S(2)}, u32[]{:S(2)}) %collective-permute-start.23) | collective-permute-done | bytes 262176 | tf_op jit(solution)/shard_map/ppermute | solution.py:116
  124.0 1.5 %shard_map.91 = (bf16[2,256,512]{2,1,0:T(8,128)(2,1)S(1)}, f32[2,256,512]{2,1,0:T(8,128)S(1)}) custom-call(bf16[256,128]{1,0:T(8,128)(2,1)S(1)} %get-tuple-element.59.refs_0_, bf16[256,128]{1,0:T(8,128)(2,1)S(1)} %collective-permute-done.18.refs_1_, bf16[256,128]{1,0:T(8,128)(2,1)S(1)} %collective-permute-done.19.refs_2_, ...), custom_call_target="tpu_custom_call" | custom-call | tf_op jit(solution)/shard_map/pallas_call | solution.py:130
  125.6 1.9 %collective-permute-done.24 = bf16[2,256,512]{2,1,0:T(8,128)(2,1)S(1)} collective-permute-done((bf16[2,256,512]{2,1,0:T(8,128)(2,1)S(1)}, bf16[2,256,512]{2,1,0:T(8,128)(2,1)S(1)}, u32[]{:S(2)}, u32[]{:S(2)}) %collective-permute-start.24) | collective-permute-done | bytes 524320 | tf_op jit(solution)/shard_map/ppermute | solution.py:116
  127.5 0.9 fusion
  128.4 1.8 %shard_map.86 = bf16[192,2048]{1,0:T(8,128)(2,1)} custom-call(s32[8]{0:T(128)S(1)} %copy-done.8, bf16[3,192,2048]{2,1,0:T(8,128)(2,1)S(1)} %copy-done), custom_call_target="tpu_custom_call" | custom-call | tf_op jit(solution)/shard_map/pallas_call | solution.py:168
  130.3 1.1 bitcast_add_fusion
  131.4 5.7 %collective-permute-done.25 = bf16[256,512]{1,0:T(8,128)(2,1)} collective-permute-done((bf16[256,512]{1,0:T(8,128)(2,1)}, bf16[256,512]{1,0:T(8,128)(2,1)}, u32[]{:S(2)}, u32[]{:S(2)}) %collective-permute-start.25) | collective-permute-done | bytes 262176 | tf_op jit(solution)/shard_map/ppermute | solution.py:116
  137.1 1.7 %add_convert_fusion = bf16[256,512]{1,0:T(8,128)(2,1)} fusion(f32[256,512]{1,0:T(8,128)S(1)} %bitcast_add_fusion, bf16[256,512]{1,0:T(8,128)(2,1)} %collective-permute-done.25), kind=kLoop, calls=%fused_computation.1 | loop fusion | flops 393216 | bytes 1048576 | tf_op jit(solution)/shard_map/convert_element_type | solution.py:557
  (41 shorter events, 0.7 us)
Async XLA Ops:
  0.6 6.8 %copy-start.2 = (bf16[512,512]{1,0:T(8,128)(2,1)S(1)}, bf16[512,512]{1,0:T(8,128)(2,1)}, u32[]{:S(2)}) copy-start(bf16[512,512]{1,0:T(8,128)(2,1)} %refs_2_.3) | copy-start | bytes 1572868
  0.6 6.8 %copy-start.1 = (bf16[1024,1024]{1,0:T(8,128)(2,1)S(1)}, bf16[1024,1024]{1,0:T(8,128)(2,1)}, u32[]{:S(2)}) copy-start(bf16[1024,1024]{1,0:T(8,128)(2,1)} %refs_1_.3) | copy-start | bytes 6291460
  0.7 6.8 %copy-start.7 = (s32[256]{0:T(256)S(1)}, s32[256]{0:T(256)}, u32[]{:S(2)}) copy-start(s32[256]{0:T(256)} %param.9) | copy-start | bytes 3076
  4.0 3.4 %collective-permute-start = (bf16[640,1024]{1,0:T(8,128)(2,1)}, bf16[640,1024]{1,0:T(8,128)(2,1)S(1)}, u32[]{:S(2)}, u32[]{:S(2)}) collective-permute-start(bf16[640,1024]{1,0:T(8,128)(2,1)} %get-tuple-element.37), channel_id=1, source_target_pairs={{0,1},{1,0},{2,3},{3,2},{4,5},{5,4},{6,7},{7,6},{8,9},{9,8},{10,11... | collective-permute-start | bytes 3932168 | tf_op jit(solution)/shard_map/ppermute | solution.py:116
  4.5 29.7 %collective-permute-start.6 = (bf16[640,512]{1,0:T(8,128)(2,1)}, bf16[640,512]{1,0:T(8,128)(2,1)S(1)}, u32[]{:S(2)}, u32[]{:S(2)}) collective-permute-start(bf16[640,512]{1,0:T(8,128)(2,1)} %get-tuple-element.39.refs_0_), channel_id=1, source_target_pairs={{0,4},{4,0},{8,12},{12,8},{1,5},{5,1},{9,13},{13,9},{2,6},{6,2},{1... | collective-permute-start | bytes 1966088 | tf_op jit(solution)/shard_map/ppermute | solution.py:116
  7.4 1.1 copy-start.6
  7.4 79.1 %copy-start.10 = (bf16[256,512]{1,0:T(8,128)(2,1)S(1)}, bf16[256,512]{1,0:T(8,128)(2,1)}, u32[]{:S(2)}) copy-start(bf16[256,512]{1,0:T(8,128)(2,1)} %get-tuple-element.44) | copy-start | bytes 786436
  8.5 33.2 %collective-permute-start.1 = (bf16[640,512]{1,0:T(8,128)(2,1)S(1)}, bf16[640,512]{1,0:T(8,128)(2,1)S(1)}, u32[]{:S(2)}, u32[]{:S(2)}) collective-permute-start(bf16[640,512]{1,0:T(8,128)(2,1)S(1)} %copy-done.6), channel_id=1, source_target_pairs={{0,8},{4,12},{8,0},{12,4},{1,9},{5,13},{9,1},{13,5},{2,10},{6,14},... | collective-permute-start | bytes 1966088 | tf_op jit(solution)/shard_map/ppermute | solution.py:116
  12.5 31.5 %collective-permute-start.5 = (bf16[640,512]{1,0:T(8,128)(2,1)S(1)}, bf16[640,512]{1,0:T(8,128)(2,1)S(1)}, u32[]{:S(2)}, u32[]{:S(2)}) collective-permute-start(bf16[640,512]{1,0:T(8,128)(2,1)S(1)} %copy-done.6), channel_id=1, source_target_pairs={{0,2},{2,0},{1,3},{3,1},{4,6},{6,4},{5,7},{7,5},{8,10},{10,8},{9,1... | collective-permute-start | bytes 1966088 | tf_op jit(solution)/shard_map/ppermute | solution.py:116
  34.3 17.6 %collective-permute-start.7 = (bf16[640,512]{1,0:T(8,128)(2,1)S(1)}, bf16[640,512]{1,0:T(8,128)(2,1)S(1)}, u32[]{:S(2)}, u32[]{:S(2)}) collective-permute-start(bf16[640,512]{1,0:T(8,128)(2,1)S(1)} %collective-permute-done.6.refs_2_), channel_id=1, source_target_pairs={{0,2},{2,0},{1,3},{3,1},{4,6},{6,4},{5,7},{7,5},{8,10},{10,8},{9,1... | collective-permute-start | bytes 1966088 | tf_op jit(solution)/shard_map/ppermute | solution.py:116
  35.9 20.5 %collective-permute-start.4 = (bf16[336,512]{1,0:T(8,128)(2,1)S(1)}, bf16[336,512]{1,0:T(8,128)(2,1)S(1)}, u32[]{:S(2)}, u32[]{:S(2)}) collective-permute-start(bf16[336,512]{1,0:T(8,128)(2,1)S(1)} %get-tuple-element.40), channel_id=1, source_target_pairs={{0,4},{4,0},{8,12},{12,8},{1,5},{5,1},{9,13},{13,9},{2,6},{6,2},{1... | collective-permute-start | bytes 1032200 | tf_op jit(solution)/shard_map/ppermute | solution.py:116
  41.7 34.8 %collective-permute-start.2 = (bf16[640,512]{1,0:T(8,128)(2,1)S(1)}, bf16[640,512]{1,0:T(8,128)(2,1)S(1)}, u32[]{:S(2)}, u32[]{:S(2)}) collective-permute-start(bf16[640,512]{1,0:T(8,128)(2,1)S(1)} %collective-permute-done.1.refs_4_), channel_id=1, source_target_pairs={{0,4},{4,0},{8,12},{12,8},{1,5},{5,1},{9,13},{13,9},{2,6},{6,2},{1... | collective-permute-start | bytes 1966088 | tf_op jit(solution)/shard_map/ppermute | solution.py:116
  42.5 34.1 %collective-permute-start.3 = (bf16[640,512]{1,0:T(8,128)(2,1)S(1)}, bf16[640,512]{1,0:T(8,128)(2,1)S(1)}, u32[]{:S(2)}, u32[]{:S(2)}) collective-permute-start(bf16[640,512]{1,0:T(8,128)(2,1)S(1)} %collective-permute-done.1.refs_4_), channel_id=1, source_target_pairs={{0,2},{2,0},{1,3},{3,1},{4,6},{6,4},{5,7},{7,5},{8,10},{10,8},{9,1... | collective-permute-start | bytes 1966088 | tf_op jit(solution)/shard_map/ppermute | solution.py:116
  44.0 21.9 %collective-permute-start.9 = (bf16[336,512]{1,0:T(8,128)(2,1)S(1)}, bf16[336,512]{1,0:T(8,128)(2,1)S(1)}, u32[]{:S(2)}, u32[]{:S(2)}) collective-permute-start(bf16[336,512]{1,0:T(8,128)(2,1)S(1)} %get-tuple-element.42), channel_id=1, source_target_pairs={{0,8},{4,12},{8,0},{12,4},{1,9},{5,13},{9,1},{13,5},{2,10},{6,14},... | collective-permute-start | bytes 1032200 | tf_op jit(solution)/shard_map/ppermute | solution.py:116
  56.4 9.5 %collective-permute-start.8 = (bf16[336,512]{1,0:T(8,128)(2,1)S(1)}, bf16[336,512]{1,0:T(8,128)(2,1)S(1)}, u32[]{:S(2)}, u32[]{:S(2)}) collective-permute-start(bf16[336,512]{1,0:T(8,128)(2,1)S(1)} %collective-permute-done.4.refs_9_), channel_id=1, source_target_pairs={{0,16},{16,0},{1,17},{17,1},{2,18},{18,2},{3,19},{19,3},{4,20},{20... | collective-permute-start | bytes 1032200 | tf_op jit(solution)/shard_map/ppermute | solution.py:116
  57.9 20.7 %collective-permute-start.13 = (bf16[336,512]{1,0:T(8,128)(2,1)S(1)}, bf16[336,512]{1,0:T(8,128)(2,1)S(1)}, u32[]{:S(2)}, u32[]{:S(2)}) collective-permute-start(bf16[336,512]{1,0:T(8,128)(2,1)S(1)} %get-tuple-element.52), channel_id=1, source_target_pairs={{0,12},{4,8},{8,4},{12,0},{1,13},{5,9},{9,5},{13,1},{2,14},{6,10},... | collective-permute-start | bytes 1032200 | tf_op jit(solution)/shard_map/ppermute | solution.py:116
  76.5 8.3 %collective-permute-start.14 = (bf16[336,512]{1,0:T(8,128)(2,1)S(1)}, bf16[336,512]{1,0:T(8,128)(2,1)S(1)}, u32[]{:S(2)}, u32[]{:S(2)}) collective-permute-start(bf16[336,512]{1,0:T(8,128)(2,1)S(1)} %collective-permute-done.9.refs_11_), channel_id=1, source_target_pairs={{0,16},{16,0},{1,17},{17,1},{2,18},{18,2},{3,19},{19,3},{4,20},{20... | collective-permute-start | bytes 1032200 | tf_op jit(solution)/shard_map/ppermute | solution.py:116
  78.1 20.3 %collective-permute-start.12 = (bf16[640,512]{1,0:T(8,128)(2,1)S(1)}, bf16[640,512]{1,0:T(8,128)(2,1)S(1)}, u32[]{:S(2)}, u32[]{:S(2)}) collective-permute-start(bf16[640,512]{1,0:T(8,128)(2,1)S(1)} %collective-permute-done.2.refs_6_), channel_id=1, source_target_pairs={{0,2},{2,0},{1,3},{3,1},{4,6},{6,4},{5,7},{7,5},{8,10},{10,8},{9,1... | collective-permute-start | bytes 1966088 | tf_op jit(solution)/shard_map/ppermute | solution.py:116
  84.9 13.6 %collective-permute-start.15 = (bf16[336,512]{1,0:T(8,128)(2,1)S(1)}, bf16[336,512]{1,0:T(8,128)(2,1)S(1)}, u32[]{:S(2)}, u32[]{:S(2)}) collective-permute-start(bf16[336,512]{1,0:T(8,128)(2,1)S(1)} %collective-permute-done.13.refs_13_), channel_id=1, source_target_pairs={{0,16},{16,0},{1,17},{17,1},{2,18},{18,2},{3,19},{19,3},{4,20},{20... | collective-permute-start | bytes 1032200 | tf_op jit(solution)/shard_map/ppermute | solution.py:116
  86.5 11.8 %collective-permute-start.10 = (bf16[256,512]{1,0:T(8,128)(2,1)S(1)}, bf16[256,512]{1,0:T(8,128)(2,1)S(1)}, u32[]{:S(2)}, u32[]{:S(2)}) collective-permute-start(bf16[256,512]{1,0:T(8,128)(2,1)S(1)} %copy-done.10), channel_id=1, source_target_pairs={{0,8},{4,12},{8,0},{12,4},{1,9},{5,13},{9,1},{13,5},{2,10},{6,14},... | collective-permute-start | bytes 786440 | tf_op jit(solution)/shard_map/ppermute | solution.py:116
  88.5 9.9 %collective-permute-start.16 = (bf16[256,512]{1,0:T(8,128)(2,1)S(1)}, bf16[256,512]{1,0:T(8,128)(2,1)S(1)}, u32[]{:S(2)}, u32[]{:S(2)}) collective-permute-start(bf16[256,512]{1,0:T(8,128)(2,1)S(1)} %copy-done.10), channel_id=1, source_target_pairs={{0,4},{4,0},{8,12},{12,8},{1,5},{5,1},{9,13},{13,9},{2,6},{6,2},{1... | collective-permute-start | bytes 786440 | tf_op jit(solution)/shard_map/ppermute | solution.py:116
  102.4 4.1 %collective-permute-start.17 = (f32[1280,256]{1,0:T(8,128)}, f32[1280,256]{1,0:T(8,128)S(1)}, u32[]{:S(2)}, u32[]{:S(2)}) collective-permute-start(f32[1280,256]{1,0:T(8,128)} %get-tuple-element.57), channel_id=1, source_target_pairs={{0,1},{1,0},{2,3},{3,2},{4,5},{5,4},{6,7},{7,6},{8,9},{9,8},{10,11... | collective-permute-start | bytes 3932168 | tf_op jit(solution)/shard_map/ppermute | solution.py:116
  102.5 8.7 %collective-permute-start.11 = (bf16[256,512]{1,0:T(8,128)(2,1)S(1)}, bf16[256,512]{1,0:T(8,128)(2,1)S(1)}, u32[]{:S(2)}, u32[]{:S(2)}) collective-permute-start(bf16[256,512]{1,0:T(8,128)(2,1)S(1)} %collective-permute-done.10.refs_16_.refs_7_), channel_id=1, source_target_pairs={{0,4},{4,0},{8,12},{12,8},{1,5},{5,1},{9,13},{13,9},{2,6},{6,2},{1... | collective-permute-start | bytes 786440 | tf_op jit(solution)/shard_map/ppermute | solution.py:116
  104.3 11.4 %collective-permute-start.22 = (bf16[256,512]{1,0:T(8,128)(2,1)S(1)}, bf16[256,512]{1,0:T(8,128)(2,1)S(1)}, u32[]{:S(2)}, u32[]{:S(2)}) collective-permute-start(bf16[256,512]{1,0:T(8,128)(2,1)S(1)} %collective-permute-done.10.refs_16_.refs_7_), channel_id=1, source_target_pairs={{0,16},{16,0},{1,17},{17,1},{2,18},{18,2},{3,19},{19,3},{4,20},{20... | collective-permute-start | bytes 786440 | tf_op jit(solution)/shard_map/ppermute | solution.py:116
  104.8 14.2 %collective-permute-start.21 = (bf16[256,512]{1,0:T(8,128)(2,1)S(1)}, bf16[256,512]{1,0:T(8,128)(2,1)S(1)}, u32[]{:S(2)}, u32[]{:S(2)}) collective-permute-start(bf16[256,512]{1,0:T(8,128)(2,1)S(1)} %collective-permute-done.16.refs_17_.refs_5_), channel_id=1, source_target_pairs={{0,16},{16,0},{1,17},{17,1},{2,18},{18,2},{3,19},{19,3},{4,20},{20... | collective-permute-start | bytes 786440 | tf_op jit(solution)/shard_map/ppermute | solution.py:116
  106.4 17.6 %copy-start.3 = (bf16[512,512]{1,0:T(8,128)(2,1)S(1)}, bf16[512,512]{1,0:T(8,128)(2,1)}, u32[]{:S(2)}) copy-start(bf16[512,512]{1,0:T(8,128)(2,1)} %refs_4_.3) | copy-start | bytes 1572868
  111.2 12.8 %collective-permute-start.23 = (bf16[256,512]{1,0:T(8,128)(2,1)S(1)}, bf16[256,512]{1,0:T(8,128)(2,1)S(1)}, u32[]{:S(2)}, u32[]{:S(2)}) collective-permute-start(bf16[256,512]{1,0:T(8,128)(2,1)S(1)} %collective-permute-done.11.refs_9_), channel_id=1, source_target_pairs={{0,16},{16,0},{1,17},{17,1},{2,18},{18,2},{3,19},{19,3},{4,20},{20... | collective-permute-start | bytes 786440 | tf_op jit(solution)/shard_map/ppermute | solution.py:116
  111.8 7.3 %collective-permute-start.18 = (bf16[256,128]{1,0:T(8,128)(2,1)S(1)}, bf16[256,128]{1,0:T(8,128)(2,1)S(1)}, u32[]{:S(2)}, u32[]{:S(2)}) collective-permute-start(bf16[256,128]{1,0:T(8,128)(2,1)S(1)} %get-tuple-element.60), channel_id=1, source_target_pairs={{0,4},{4,0},{8,12},{12,8},{1,5},{5,1},{9,13},{13,9},{2,6},{6,2},{1... | collective-permute-start | bytes 196616 | tf_op jit(solution)/shard_map/ppermute | solution.py:116
  113.3 6.9 %collective-permute-start.19 = (bf16[256,128]{1,0:T(8,128)(2,1)S(1)}, bf16[256,128]{1,0:T(8,128)(2,1)S(1)}, u32[]{:S(2)}, u32[]{:S(2)}) collective-permute-start(bf16[256,128]{1,0:T(8,128)(2,1)S(1)} %get-tuple-element.61), channel_id=1, source_target_pairs={{0,8},{4,12},{8,0},{12,4},{1,9},{5,13},{9,1},{13,5},{2,10},{6,14},... | collective-permute-start | bytes 196616 | tf_op jit(solution)/shard_map/ppermute | solution.py:116
  115.8 12.7 %copy-start = (bf16[3,192,2048]{2,1,0:T(8,128)(2,1)S(1)}, bf16[3,192,2048]{2,1,0:T(8,128)(2,1)}, u32[]{:S(2)}) copy-start(bf16[3,192,2048]{2,1,0:T(8,128)(2,1)} %refs_1_.2) | copy-start | bytes 7077892
  115.8 12.7 %copy-start.8 = (s32[8]{0:T(128)S(1)}, s32[8]{0:T(128)}, u32[]{:S(2)}) copy-start(s32[8]{0:T(128)} %refs_0_.1) | copy-start | bytes 100
  115.8 6.1 %collective-permute-start.20 = (bf16[256,128]{1,0:T(8,128)(2,1)S(1)}, bf16[256,128]{1,0:T(8,128)(2,1)S(1)}, u32[]{:S(2)}, u32[]{:S(2)}) collective-permute-start(bf16[256,128]{1,0:T(8,128)(2,1)S(1)} %get-tuple-element.62), channel_id=1, source_target_pairs={{0,12},{4,8},{8,4},{12,0},{1,13},{5,9},{9,5},{13,1},{2,14},{6,10},... | collective-permute-start | bytes 196616 | tf_op jit(solution)/shard_map/ppermute | solution.py:116
  125.5 2.0 %copy-start.4 = (f32[2,256,512]{2,1,0:T(8,128)}, f32[2,256,512]{2,1,0:T(8,128)S(1)}, u32[]{:S(2)}) copy-start(f32[2,256,512]{2,1,0:T(8,128)S(1)} %get-tuple-element.64) | copy-start | bytes 3145732
  125.5 2.0 %collective-permute-start.24 = (bf16[2,256,512]{2,1,0:T(8,128)(2,1)S(1)}, bf16[2,256,512]{2,1,0:T(8,128)(2,1)S(1)}, u32[]{:S(2)}, u32[]{:S(2)}) collective-permute-start(bf16[2,256,512]{2,1,0:T(8,128)(2,1)S(1)} %get-tuple-element.65), channel_id=1, source_target_pairs={{0,1},{1,0},{2,3},{3,2},{4,5},{5,4},{6,7},{7,6},{8,9},{9,8},{10,11... | collective-permute-start | bytes 1572872 | tf_op jit(solution)/shard_map/ppermute | solution.py:116
  127.5 0.9 copy-start.9
  128.4 8.7 %collective-permute-start.25 = (bf16[256,512]{1,0:T(8,128)(2,1)}, bf16[256,512]{1,0:T(8,128)(2,1)}, u32[]{:S(2)}, u32[]{:S(2)}) collective-permute-start(bf16[256,512]{1,0:T(8,128)(2,1)} %fusion), channel_id=1, source_target_pairs={{0,2},{2,0},{1,3},{3,1},{4,6},{6,4},{5,7},{7,5},{8,10},{10,8},{9,1... | collective-permute-start | bytes 786440 | tf_op jit(solution)/shard_map/ppermute | solution.py:116
  128.4 1.9 %copy-start.5 = (f32[2,256,512]{2,1,0:T(8,128)S(1)}, f32[2,256,512]{2,1,0:T(8,128)}, u32[]{:S(2)}) copy-start(f32[2,256,512]{2,1,0:T(8,128)} %copy-done.4) | copy-start | bytes 3145732

commit v11 on v8

--- a/solution.py
+++ b/solution.py
@@ -263,7 +263,7 @@
         leaving.wait()
 
 
-def weight_body(kv_ref, query_ref, other_ref, own_ref, *piece_refs):
+def weight_body(align_ref, kv_ref, query_ref, other_ref, own_ref, *piece_refs):
     seq_at, rep_at, grp_at = (lax.axis_index(name) for name in ("seq", "rep", "grp"))
     kv_half, query_half = kv_ref.shape[0] // 2, query_ref.shape[0] // 2
     kv_rows, query_rows = kv_half // 2, query_half // 2
@@ -294,11 +294,17 @@
         fill(own_ref, 0, group, group * kv_rows, kv_half + group * fold)
     for bit, piece_ref in enumerate(piece_refs, 1):
         fill(piece_ref, bit, grp_at, 0, kv_rows)
+        spare = (piece_ref.shape[0] - kv_rows - fold, piece_ref.shape[1])
+        align = align_ref[...].astype(jnp.float32).astype(piece_ref.dtype)
+        row = jnp.concatenate(
+            [align, jnp.zeros((1, spare[1] - align.shape[1]), piece_ref.dtype)], axis=1
+        )
+        piece_ref[kv_rows + fold :, :] = jnp.broadcast_to(row, spare)
 
 
 def products_body(*refs):
     packed_refs, weight_refs = refs[:8], refs[8:15]
-    send_ref, keep_ref, rows_ref, audio_ref, kv_ref, query_ref = refs[15:]
+    own_align, align_ref, send_ref, keep_ref, rows_ref, audio_ref, kv_ref, query_ref = refs[15:]
     seq_at, mem_at, grp_at = (lax.axis_index(name) for name in ("seq", "mem", "grp"))
     rows, audio_rows = rows_ref.shape[0] // 4, audio_ref.shape[0] // 4
     depth, lane = rows_ref.shape[1] // 4, audio_ref.shape[1] // 4
@@ -331,6 +337,10 @@
     for bit in range(1, 4):
         place(weight_refs[2 * bit - 1], seq_at ^ bit, grp_at, 0, kv_half)
         place(weight_refs[2 * bit], seq_at ^ bit, 1 - grp_at, 0, kv_half)
+        align_ref[bit] = weight_refs[2 * bit - 1][kv_half + fold :, : align_ref.shape[2]]
+    align_ref[0] = jnp.broadcast_to(
+        own_align[...].astype(jnp.float32).astype(align_ref.dtype), align_ref.shape[1:]
+    )
 
     count = 4 * rows
     columns = keep_ref.shape[1]
@@ -376,19 +386,21 @@
             slice(side * HEAD_DIM, (side + 1) * HEAD_DIM),
         )
     for bit, out_ref in enumerate(out_refs):
-        out_ref[...] = attend(query_ref[bit], kv_ref, frames_ref, align_ref[bit])
+        align = align_ref[bit].astype(jnp.float32)[:8].T[:, :1]
+        out_ref[...] = attend(query_ref[bit], kv_ref, frames_ref, align)
 
 
 def out_body(*refs):
-    piece_refs, (own_w, partner_w, *part_refs), (send_ref, keep_ref, heads_ref, weight_ref, sem) = (
-        refs[:4],
-        refs[4:10],
-        refs[10:],
-    )
+    piece_refs, (audio_ref, own_w, partner_w, *part_refs) = refs[:4], refs[4:11]
+    send_ref, keep_ref, heads_ref, weight_ref, residual_ref, sems = refs[11:]
     seq_at, grp_at = lax.axis_index("seq"), lax.axis_index("grp")
     place = lax.axis_index("mem") * 2 + lax.axis_index("rep")
-    copy = pltpu.make_async_copy(own_w, weight_ref.at[0], sem)
+    copy = pltpu.make_async_copy(own_w, weight_ref.at[0], sems.at[0])
     copy.start()
+    width = residual_ref.shape[1]
+    columns = pl.ds(pl.multiple_of(place * width, width), width)
+    residual_copy = pltpu.make_async_copy(audio_ref.at[:, columns], residual_ref, sems.at[1])
+    residual_copy.start()
     for bit, piece_ref in enumerate(piece_refs):
         heads_ref[seq_at ^ bit] = piece_ref[...]
     heads = jnp.concatenate([heads_ref[head] for head in range(heads_ref.shape[0])], axis=1)
@@ -413,11 +425,13 @@
         def _():
             keep_ref[slot // 2] = value
 
+    residual_copy.wait()
+    keep_ref[0] += residual_ref[...].astype(jnp.float32)
+
 
 def by_head(video_cache, plan, alignment, audio_tokens, kv_weight, query_weight, out_weight):
     seq_size = lax.axis_size("seq")
     seq_at = lax.axis_index("seq")
-    place = lax.axis_index("mem") * 2 + lax.axis_index("rep")
     video_rows = video_cache.shape[1]
     audio_rows = audio_tokens.shape[0]
     half_depth, width = kv_weight.shape[0] // 2, 2 * HEAD_DIM
@@ -453,14 +467,13 @@
     rows = half_depth // 2 + query_quarter // 2
     weight_own, *pieces = kernel_call(
         weight_body,
-        [bfloat(2 * rows, 2 * width)] + [bfloat(rows, 2 * width)] * 3,
-        [kv_weight, query_weight, other],
+        [bfloat(2 * rows, 2 * width)] + [bfloat(rows + 16, 2 * width)] * 3,
+        [alignment[None], kv_weight, query_weight, other],
         limit=4,
     )
     pieces[0] = swap(pieces[0], "seq", 1)
-    aligns = [alignment, *(swap(alignment, "seq", bit) for bit in (1, 2, 3))]
-    tokens[1], tokens[2], across[0], pieces[0], *aligns = lax.optimization_barrier(
-        (tokens[1], tokens[2], across[0], pieces[0], *aligns)
+    tokens[1], tokens[2], across[0], *pieces = lax.optimization_barrier(
+        (tokens[1], tokens[2], across[0], *pieces)
     )
 
     tokens.append(swap(tokens[2], "seq", 1))
@@ -481,11 +494,11 @@
         weights += [piece, other]
     rows = seq_size * (video_rows + audio_rows // 2)
     sums = jax.ShapeDtypeStruct((rows, width), jnp.float32)
-    send, keep = kernel_call(
+    aligns, send, keep = kernel_call(
         products_body,
-        [sums, sums],
-        [value for pair in zip(tokens, across) for value in pair] + weights,
-        after=(out_partner,),
+        [bfloat(4, 16, audio_rows), sums, sums],
+        [value for pair in zip(tokens, across) for value in pair] + weights + [alignment[None]],
+        after=(out_partner, out_third),
         scratch=[
             pltpu.VMEM((seq_size * video_rows, 4 * half_depth), jnp.bfloat16),
             pltpu.VMEM((seq_size * audio_rows, 8 * query_quarter), jnp.bfloat16),
@@ -504,7 +517,7 @@
     own_piece, near_piece, far_piece, farther_piece = kernel_call(
         attention_body,
         [bfloat(audio_rows, HEAD_DIM)] * 4,
-        [frames_video, jnp.stack(aligns).astype(jnp.float32)[:, :, None], keep, came],
+        [frames_video, aligns, keep, came],
         scratch=[
             pltpu.VMEM((span, width), jnp.bfloat16),
             pltpu.VMEM((seq_size, audio_rows, HEAD_DIM), jnp.bfloat16),
@@ -525,22 +538,22 @@
             jax.ShapeDtypeStruct((2, audio_rows, columns), jnp.bfloat16),
             jax.ShapeDtypeStruct((2, audio_rows, columns), jnp.float32),
         ],
-        [own_piece, near_piece, far_piece, farther_piece, *weights],
+        [own_piece, near_piece, far_piece, farther_piece, audio_tokens, *weights],
         scratch=[
             pltpu.VMEM((seq_size, audio_rows, HEAD_DIM), jnp.bfloat16),
             pltpu.VMEM((3, *out_weight.shape), jnp.bfloat16),
-            pltpu.SemaphoreType.DMA,
+            pltpu.VMEM((audio_rows, columns), jnp.bfloat16),
+            pltpu.SemaphoreType.DMA((2,)),
         ],
-        loose_in=(4,),
+        loose_in=(4, 5),
         limit=7,
     )
     came = swap(send, "rep", 1)
     across = swap((keep[1] + came[1].astype(jnp.float32)).astype(jnp.bfloat16), "mem", 1)
-    residual = lax.dynamic_slice_in_dim(audio_tokens, place * columns, columns, 1)
     own_part = taylor(video_cache, plan, 2 * half_depth)
-    base = residual.astype(jnp.float32) + (keep[0] + came[0].astype(jnp.float32))
-    base, across = lax.optimization_barrier((base, across))
-    audio_output = (base + across.astype(jnp.float32)).astype(jnp.bfloat16)
+    audio_output = (
+        keep[0] + came[0].astype(jnp.float32) + across.astype(jnp.float32)
+    ).astype(jnp.bfloat16)
     return (own_part, audio_output)
 
 

time: 151 us -> 137 us (0.907)
  waiting for transfers between devices: 92 us -> 82.7 us
  other arithmetic: 4.01 us -> 1.14 us
    ppermute x28 -> x25, waiting for transfers between devices: 92 us -> 82.7 us  [swap(): return lax.ppermute(value, axis, [(i, i ^ bit) for i in range(size)])]
    ppermute x28 -> x25, starting transfers between devices: 38.8 us -> 37.8 us  [swap(): return lax.ppermute(value, axis, [(i, i ^ bit) for i in range(size)])]
  transfers between devices with their start and end apart: 28 -> 25, of which waited for: 14 -> 11; matrix products, arithmetic and copies ran while one was open for 1% -> 0% of each run, Pallas kernels for 4% -> 3%
where the time goes in v11:
time: 137 us
  waiting for transfers between devices  82.7 us (60%)
  starting transfers between devices  37.8 us (28%)
  Pallas kernels  14.2 us (10%)
    ppermute x25, waiting for transfers between devices, swap(): return lax.ppermute(value, axis, [(i, i ^ bit) for i in range(size)])  82.7 us
    ppermute x25, starting transfers between devices, swap(): return lax.ppermute(value, axis, [(i, i ^ bit) for i in range(size)])  37.8 us
    pallas_call x5, Pallas kernels, kernel_call(): pl.pallas_call(whole, out_shape=outs, in_specs=spots + [ANY] * len(after)...  12.4 us
  transfers between devices with their start and end apart: 25, of which 11 were waited for; matrix products, arithmetic and copies ran while one was open for 0% of the time, Pallas kernels for 3%

profile of v11, /device:TPU:0, one launch (start us, length us, event | category | flops | bytes accessed | tf_op | source)
XLA Modules:
  0.0 136.9 jit_solution(15992842751973022392)
XLA Ops:
  0.7 3.3 %shard_map.87 = (bf16[640,512]{1,0:T(8,128)(2,1)}, bf16[640,1024]{1,0:T(8,128)(2,1)}, bf16[256,512]{1,0:T(8,128)(2,1)}) custom-call(s32[8]{0:T(128)} %refs_0_.1, bf16[3,192,2048]{2,1,0:T(8,128)(2,1)} %refs_1_.2, bf16[256,2048]{1,0:T(8,128)(2,1)} %refs_4_.3, bf16[1024,1024]{1,0:T(8,128)(2,1)} %refs_1_.3, bf16[512,512]{1,0:T(8,128)(2,1)} %refs_2_.3, ...), custom_call_target="tpu_custom_call" | custom-call | tf_op jit(solution)/shard_map/pallas_call | solution.py:130
  4.0 0.5 collective-permute-start.3
  4.5 2.6 %collective-permute-start = (bf16[640,512]{1,0:T(8,128)(2,1)}, bf16[640,512]{1,0:T(8,128)(2,1)S(1)}, u32[]{:S(2)}, u32[]{:S(2)}) collective-permute-start(bf16[640,512]{1,0:T(8,128)(2,1)} %get-tuple-element.33.refs_0_), channel_id=1, source_target_pairs={{0,4},{4,0},{8,12},{12,8},{1,5},{5,1},{9,13},{13,9},{2,6},{6,2},{1... | collective-permute-start | bytes 1966088 | tf_op jit(solution)/shard_map/ppermute | solution.py:116
  7.2 2.6 %collective-permute-start.1 = (bf16[640,512]{1,0:T(8,128)(2,1)}, bf16[640,512]{1,0:T(8,128)(2,1)S(1)}, u32[]{:S(2)}, u32[]{:S(2)}) collective-permute-start(bf16[640,512]{1,0:T(8,128)(2,1)} %get-tuple-element.33.refs_0_), channel_id=1, source_target_pairs={{0,8},{4,12},{8,0},{12,4},{1,9},{5,13},{9,1},{13,5},{2,10},{6,14},... | collective-permute-start | bytes 1966088 | tf_op jit(solution)/shard_map/ppermute | solution.py:116
  9.8 1.5 %collective-permute-start.2 = (bf16[640,512]{1,0:T(8,128)(2,1)}, bf16[640,512]{1,0:T(8,128)(2,1)S(1)}, u32[]{:S(2)}, u32[]{:S(2)}) collective-permute-start(bf16[640,512]{1,0:T(8,128)(2,1)} %get-tuple-element.33.refs_0_), channel_id=1, source_target_pairs={{0,2},{2,0},{1,3},{3,1},{4,6},{6,4},{5,7},{7,5},{8,10},{10,8},{9,1... | collective-permute-start | bytes 1966088 | tf_op jit(solution)/shard_map/ppermute | solution.py:116
  11.3 0.3 shard_map.88
  11.6 0.5 collective-permute-start.4
  12.1 24.8 %collective-permute-done.refs_2_ = bf16[640,512]{1,0:T(8,128)(2,1)S(1)} collective-permute-done((bf16[640,512]{1,0:T(8,128)(2,1)}, bf16[640,512]{1,0:T(8,128)(2,1)S(1)}, u32[]{:S(2)}, u32[]{:S(2)}) %collective-permute-start) | collective-permute-done | bytes 655392 | tf_op jit(solution)/shard_map/ppermute | solution.py:116
  36.9 2.0 %collective-permute-done.1.refs_4_ = bf16[640,512]{1,0:T(8,128)(2,1)S(1)} collective-permute-done((bf16[640,512]{1,0:T(8,128)(2,1)}, bf16[640,512]{1,0:T(8,128)(2,1)S(1)}, u32[]{:S(2)}, u32[]{:S(2)}) %collective-permute-start.1) | collective-permute-done | bytes 655392 | tf_op jit(solution)/shard_map/ppermute | solution.py:116
  38.9 5.2 %collective-permute-done.4.refs_9_ = bf16[336,512]{1,0:T(8,128)(2,1)S(1)} collective-permute-done((bf16[336,512]{1,0:T(8,128)(2,1)S(1)}, bf16[336,512]{1,0:T(8,128)(2,1)S(1)}, u32[]{:S(2)}, u32[]{:S(2)}) %collective-permute-start.4) | collective-permute-done | bytes 344096 | tf_op jit(solution)/shard_map/ppermute | solution.py:116
  44.1 1.7 %collective-permute-start.10 = (bf16[336,512]{1,0:T(8,128)(2,1)S(1)}, bf16[336,512]{1,0:T(8,128)(2,1)S(1)}, u32[]{:S(2)}, u32[]{:S(2)}) collective-permute-start(bf16[336,512]{1,0:T(8,128)(2,1)S(1)} %collective-permute-done.4.refs_9_), channel_id=1, source_target_pairs={{0,16},{16,0},{1,17},{17,1},{2,18},{18,2},{3,19},{19,3},{4,20},{20... | collective-permute-start | bytes 1032200 | tf_op jit(solution)/shard_map/ppermute | solution.py:116
  45.8 1.6 %collective-permute-start.5 = (bf16[640,512]{1,0:T(8,128)(2,1)S(1)}, bf16[640,512]{1,0:T(8,128)(2,1)S(1)}, u32[]{:S(2)}, u32[]{:S(2)}) collective-permute-start(bf16[640,512]{1,0:T(8,128)(2,1)S(1)} %collective-permute-done.1.refs_4_), channel_id=1, source_target_pairs={{0,4},{4,0},{8,12},{12,8},{1,5},{5,1},{9,13},{13,9},{2,6},{6,2},{1... | collective-permute-start | bytes 1966088 | tf_op jit(solution)/shard_map/ppermute | solution.py:116
  47.5 1.5 %collective-permute-start.7 = (bf16[640,512]{1,0:T(8,128)(2,1)S(1)}, bf16[640,512]{1,0:T(8,128)(2,1)S(1)}, u32[]{:S(2)}, u32[]{:S(2)}) collective-permute-start(bf16[640,512]{1,0:T(8,128)(2,1)S(1)} %collective-permute-done.1.refs_4_), channel_id=1, source_target_pairs={{0,2},{2,0},{1,3},{3,1},{4,6},{6,4},{5,7},{7,5},{8,10},{10,8},{9,1... | collective-permute-start | bytes 1966088 | tf_op jit(solution)/shard_map/ppermute | solution.py:116
  48.9 0.5 collective-permute-start.6
  49.5 2.5 %collective-permute-start.8 = (bf16[336,512]{1,0:T(8,128)(2,1)S(1)}, bf16[336,512]{1,0:T(8,128)(2,1)S(1)}, u32[]{:S(2)}, u32[]{:S(2)}) collective-permute-start(bf16[336,512]{1,0:T(8,128)(2,1)S(1)} %get-tuple-element.40), channel_id=1, source_target_pairs={{0,8},{4,12},{8,0},{12,4},{1,9},{5,13},{9,1},{13,5},{2,10},{6,14},... | collective-permute-start | bytes 1032200 | tf_op jit(solution)/shard_map/ppermute | solution.py:116
  52.0 1.9 %collective-permute-done.10.refs_10_ = bf16[336,512]{1,0:T(8,128)(2,1)S(1)} collective-permute-done((bf16[336,512]{1,0:T(8,128)(2,1)S(1)}, bf16[336,512]{1,0:T(8,128)(2,1)S(1)}, u32[]{:S(2)}, u32[]{:S(2)}) %collective-permute-start.10) | collective-permute-done | bytes 344096 | tf_op jit(solution)/shard_map/ppermute | solution.py:116
  54.0 3.6 %collective-permute-start.9 = (bf16[336,512]{1,0:T(8,128)(2,1)S(1)}, bf16[336,512]{1,0:T(8,128)(2,1)S(1)}, u32[]{:S(2)}, u32[]{:S(2)}) collective-permute-start(bf16[336,512]{1,0:T(8,128)(2,1)S(1)} %get-tuple-element.41), channel_id=1, source_target_pairs={{0,12},{4,8},{8,4},{12,0},{1,13},{5,9},{9,5},{13,1},{2,14},{6,10},... | collective-permute-start | bytes 1032200 | tf_op jit(solution)/shard_map/ppermute | solution.py:116
  57.5 12.5 %collective-permute-done.8.refs_11_ = bf16[336,512]{1,0:T(8,128)(2,1)S(1)} collective-permute-done((bf16[336,512]{1,0:T(8,128)(2,1)S(1)}, bf16[336,512]{1,0:T(8,128)(2,1)S(1)}, u32[]{:S(2)}, u32[]{:S(2)}) %collective-permute-start.8) | collective-permute-done | bytes 344096 | tf_op jit(solution)/shard_map/ppermute | solution.py:116
  70.1 8.7 %collective-permute-done.9.refs_13_ = bf16[336,512]{1,0:T(8,128)(2,1)S(1)} collective-permute-done((bf16[336,512]{1,0:T(8,128)(2,1)S(1)}, bf16[336,512]{1,0:T(8,128)(2,1)S(1)}, u32[]{:S(2)}, u32[]{:S(2)}) %collective-permute-start.9) | collective-permute-done | bytes 344096 | tf_op jit(solution)/shard_map/ppermute | solution.py:116
  78.8 1.6 %collective-permute-start.13 = (bf16[640,512]{1,0:T(8,128)(2,1)S(1)}, bf16[640,512]{1,0:T(8,128)(2,1)S(1)}, u32[]{:S(2)}, u32[]{:S(2)}) collective-permute-start(bf16[640,512]{1,0:T(8,128)(2,1)S(1)} %collective-permute-done.5.refs_6_), channel_id=1, source_target_pairs={{0,2},{2,0},{1,3},{3,1},{4,6},{6,4},{5,7},{7,5},{8,10},{10,8},{9,1... | collective-permute-start | bytes 1966088 | tf_op jit(solution)/shard_map/ppermute | solution.py:116
  80.3 2.8 %collective-permute-start.16 = (bf16[512,512]{1,0:T(8,128)(2,1)S(1)}, bf16[512,512]{1,0:T(8,128)(2,1)S(1)}, u32[]{:S(2)}, u32[]{:S(2)}) collective-permute-start(bf16[512,512]{1,0:T(8,128)(2,1)S(1)} %copy-done.4), channel_id=1, source_target_pairs={{0,4},{4,0},{8,12},{12,8},{1,5},{5,1},{9,13},{13,9},{2,6},{6,2},{1... | collective-permute-start | bytes 1572872 | tf_op jit(solution)/shard_map/ppermute | solution.py:116
  83.2 0.5 collective-permute-start.14
  83.7 1.5 %collective-permute-start.15 = (bf16[336,512]{1,0:T(8,128)(2,1)S(1)}, bf16[336,512]{1,0:T(8,128)(2,1)S(1)}, u32[]{:S(2)}, u32[]{:S(2)}) collective-permute-start(bf16[336,512]{1,0:T(8,128)(2,1)S(1)} %collective-permute-done.9.refs_13_), channel_id=1, source_target_pairs={{0,16},{16,0},{1,17},{17,1},{2,18},{18,2},{3,19},{19,3},{4,20},{20... | collective-permute-start | bytes 1032200 | tf_op jit(solution)/shard_map/ppermute | solution.py:116
  85.2 1.0 collective-permute-start.11
  86.2 11.7 %collective-permute-done.16.refs_16_.refs_6_ = bf16[512,512]{1,0:T(8,128)(2,1)S(1)} collective-permute-done((bf16[512,512]{1,0:T(8,128)(2,1)S(1)}, bf16[512,512]{1,0:T(8,128)(2,1)S(1)}, u32[]{:S(2)}, u32[]{:S(2)}) %collective-permute-start.16) | collective-permute-done | bytes 524320 | tf_op jit(solution)/shard_map/ppermute | solution.py:116
  97.9 3.9 %shard_map.89 = (bf16[4,16,256]{2,1,0:T(8,128)(2,1)S(1)}, f32[1280,256]{1,0:T(8,128)}, f32[1280,256]{1,0:T(8,128)S(1)}) custom-call(bf16[640,512]{1,0:T(8,128)(2,1)S(1)} %copy-done.6, bf16[640,512]{1,0:T(8,128)(2,1)S(1)} %collective-permute-done.2.refs_1_, bf16[640,512]{1,0:T(8,128)(2,1)S(1)} %collective-permute-done.refs_2_, ...), custom_call_target="tpu_custom_call" | custom-call | tf_op jit(solution)/shard_map/pallas_call | solution.py:130
  101.9 0.1 add_multiply_fusion.1
  101.9 0.1 fusion.2
  102.0 3.1 %collective-permute-start.12 = (bf16[256,512]{1,0:T(8,128)(2,1)S(1)}, bf16[256,512]{1,0:T(8,128)(2,1)}, u32[]{:S(2)}, u32[]{:S(2)}) collective-permute-start(bf16[256,512]{1,0:T(8,128)(2,1)S(1)} %collective-permute-done.11.refs_17_.refs_7_), channel_id=1, source_target_pairs={{0,4},{4,0},{8,12},{12,8},{1,5},{5,1},{9,13},{13,9},{2,6},{6,2},{1... | collective-permute-start | bytes 786440 | tf_op jit(solution)/shard_map/ppermute | solution.py:116
  105.1 0.1 fusion.3
  105.2 0.1 div.18
  105.3 0.1 reshape.116
  105.4 1.5 %collective-permute-start.21 = (bf16[256,512]{1,0:T(8,128)(2,1)S(1)}, bf16[256,512]{1,0:T(8,128)(2,1)S(1)}, u32[]{:S(2)}, u32[]{:S(2)}) collective-permute-start(bf16[256,512]{1,0:T(8,128)(2,1)S(1)} %collective-permute-done.11.refs_17_.refs_7_), channel_id=1, source_target_pairs={{0,16},{16,0},{1,17},{17,1},{2,18},{18,2},{3,19},{19,3},{4,20},{20... | collective-permute-start | bytes 786440 | tf_op jit(solution)/shard_map/ppermute | solution.py:116
  106.9 2.2 %shard_map.90 = (bf16[256,128]{1,0:T(8,128)(2,1)S(1)}, bf16[256,128]{1,0:T(8,128)(2,1)S(1)}, bf16[256,128]{1,0:T(8,128)(2,1)S(1)}, bf16[256,128]{1,0:T(8,128)(2,1)S(1)}) custom-call(f32[1,768]{1,0:T(1,128)S(1)} %fusion.4.refs_0_, bf16[4,16,256]{2,1,0:T(8,128)(2,1)S(1)} %get-tuple-element.53.refs_1_, f32[1280,256]{1,0:T(8,128)S(1)} %get-tuple-element.54.refs_2_, ...), custom_call_target="tpu_custom_call" | custom-call | tf_op jit(solution)/shard_map/pallas_call | solution.py:130
  109.2 3.1 %collective-permute-done.12.refs_9_ = bf16[256,512]{1,0:T(8,128)(2,1)} collective-permute-done((bf16[256,512]{1,0:T(8,128)(2,1)S(1)}, bf16[256,512]{1,0:T(8,128)(2,1)}, u32[]{:S(2)}, u32[]{:S(2)}) %collective-permute-start.12) | collective-permute-done | bytes 262176 | tf_op jit(solution)/shard_map/ppermute | solution.py:116
  112.2 1.5 %collective-permute-start.22 = (bf16[256,512]{1,0:T(8,128)(2,1)}, bf16[256,512]{1,0:T(8,128)(2,1)S(1)}, u32[]{:S(2)}, u32[]{:S(2)}) collective-permute-start(bf16[256,512]{1,0:T(8,128)(2,1)} %collective-permute-done.12.refs_9_), channel_id=1, source_target_pairs={{0,16},{16,0},{1,17},{17,1},{2,18},{18,2},{3,19},{19,3},{4,20},{20... | collective-permute-start | bytes 786440 | tf_op jit(solution)/shard_map/ppermute | solution.py:116
  113.7 1.7 %collective-permute-start.18 = (bf16[256,128]{1,0:T(8,128)(2,1)S(1)}, bf16[256,128]{1,0:T(8,128)(2,1)S(1)}, u32[]{:S(2)}, u32[]{:S(2)}) collective-permute-start(bf16[256,128]{1,0:T(8,128)(2,1)S(1)} %get-tuple-element.58), channel_id=1, source_target_pairs={{0,4},{4,0},{8,12},{12,8},{1,5},{5,1},{9,13},{13,9},{2,6},{6,2},{1... | collective-permute-start | bytes 196616 | tf_op jit(solution)/shard_map/ppermute | solution.py:116
  115.4 0.3 collective-permute-start.19
  115.7 2.3 %collective-permute-start.20 = (bf16[256,128]{1,0:T(8,128)(2,1)S(1)}, bf16[256,128]{1,0:T(8,128)(2,1)S(1)}, u32[]{:S(2)}, u32[]{:S(2)}) collective-permute-start(bf16[256,128]{1,0:T(8,128)(2,1)S(1)} %get-tuple-element.60), channel_id=1, source_target_pairs={{0,12},{4,8},{8,4},{12,0},{1,13},{5,9},{9,5},{13,1},{2,14},{6,10},... | collective-permute-start | bytes 196616 | tf_op jit(solution)/shard_map/ppermute | solution.py:116
  118.1 4.8 %collective-permute-done.19.refs_2_ = bf16[256,128]{1,0:T(8,128)(2,1)S(1)} collective-permute-done((bf16[256,128]{1,0:T(8,128)(2,1)S(1)}, bf16[256,128]{1,0:T(8,128)(2,1)S(1)}, u32[]{:S(2)}, u32[]{:S(2)}) %collective-permute-start.19) | collective-permute-done | bytes 65568 | tf_op jit(solution)/shard_map/ppermute | solution.py:116
  122.9 2.6 %shard_map.91 = (bf16[2,256,512]{2,1,0:T(8,128)(2,1)S(1)}, f32[2,256,512]{2,1,0:T(8,128)S(1)}) custom-call(bf16[256,128]{1,0:T(8,128)(2,1)S(1)} %get-tuple-element.57.refs_0_, bf16[256,128]{1,0:T(8,128)(2,1)S(1)} %collective-permute-done.18.refs_1_, bf16[256,128]{1,0:T(8,128)(2,1)S(1)} %collective-permute-done.19.refs_2_, ...), custom_call_target="tpu_custom_call" | custom-call | tf_op jit(solution)/shard_map/pallas_call | solution.py:130
  125.6 0.1 collective-permute-start.23
  125.7 1.9 %collective-permute-done.23 = bf16[2,256,512]{2,1,0:T(8,128)(2,1)S(1)} collective-permute-done((bf16[2,256,512]{2,1,0:T(8,128)(2,1)S(1)}, bf16[2,256,512]{2,1,0:T(8,128)(2,1)S(1)}, u32[]{:S(2)}, u32[]{:S(2)}) %collective-permute-start.23) | collective-permute-done | bytes 524320 | tf_op jit(solution)/shard_map/ppermute | solution.py:116
  127.6 0.1 fusion.1
  127.6 0.6 collective-permute-start.24
  128.3 1.8 %shard_map.86 = bf16[192,2048]{1,0:T(8,128)(2,1)} custom-call(s32[8]{0:T(128)S(1)} %copy-done.8, bf16[3,192,2048]{2,1,0:T(8,128)(2,1)S(1)} %copy-done), custom_call_target="tpu_custom_call" | custom-call | tf_op jit(solution)/shard_map/pallas_call | solution.py:168
  130.1 6.0 %collective-permute-done.24 = bf16[256,512]{1,0:T(8,128)(2,1)S(1)} collective-permute-done((bf16[256,512]{1,0:T(8,128)(2,1)S(1)}, bf16[256,512]{1,0:T(8,128)(2,1)S(1)}, u32[]{:S(2)}, u32[]{:S(2)}) %collective-permute-start.24) | collective-permute-done | bytes 262176 | tf_op jit(solution)/shard_map/ppermute | solution.py:116
  136.1 0.8 fusion
  (36 shorter events, 0.1 us)
Async XLA Ops:
  0.6 10.6 %copy-start.3 = (bf16[512,512]{1,0:T(8,128)(2,1)S(1)}, bf16[512,512]{1,0:T(8,128)(2,1)}, u32[]{:S(2)}) copy-start(bf16[512,512]{1,0:T(8,128)(2,1)} %refs_2_.3) | copy-start | bytes 1572868
  0.6 10.6 %copy-start.1 = (bf16[1024,1024]{1,0:T(8,128)(2,1)S(1)}, bf16[1024,1024]{1,0:T(8,128)(2,1)}, u32[]{:S(2)}) copy-start(bf16[1024,1024]{1,0:T(8,128)(2,1)} %refs_1_.3) | copy-start | bytes 6291460
  0.7 10.6 %copy-start.7 = (s32[256]{0:T(256)S(1)}, s32[256]{0:T(256)}, u32[]{:S(2)}) copy-start(s32[256]{0:T(256)} %param.9) | copy-start | bytes 3076
  4.0 7.3 %collective-permute-start.3 = (bf16[640,1024]{1,0:T(8,128)(2,1)}, bf16[640,1024]{1,0:T(8,128)(2,1)S(1)}, u32[]{:S(2)}, u32[]{:S(2)}) collective-permute-start(bf16[640,1024]{1,0:T(8,128)(2,1)} %get-tuple-element.34), channel_id=1, source_target_pairs={{0,1},{1,0},{2,3},{3,2},{4,5},{5,4},{6,7},{7,6},{8,9},{9,8},{10,11... | collective-permute-start | bytes 3932168 | tf_op jit(solution)/shard_map/ppermute | solution.py:116
  4.5 32.4 %collective-permute-start = (bf16[640,512]{1,0:T(8,128)(2,1)}, bf16[640,512]{1,0:T(8,128)(2,1)S(1)}, u32[]{:S(2)}, u32[]{:S(2)}) collective-permute-start(bf16[640,512]{1,0:T(8,128)(2,1)} %get-tuple-element.33.refs_0_), channel_id=1, source_target_pairs={{0,4},{4,0},{8,12},{12,8},{1,5},{5,1},{9,13},{13,9},{2,6},{6,2},{1... | collective-permute-start | bytes 1966088 | tf_op jit(solution)/shard_map/ppermute | solution.py:116
  7.2 31.8 %collective-permute-start.1 = (bf16[640,512]{1,0:T(8,128)(2,1)}, bf16[640,512]{1,0:T(8,128)(2,1)S(1)}, u32[]{:S(2)}, u32[]{:S(2)}) collective-permute-start(bf16[640,512]{1,0:T(8,128)(2,1)} %get-tuple-element.33.refs_0_), channel_id=1, source_target_pairs={{0,8},{4,12},{8,0},{12,4},{1,9},{5,13},{9,1},{13,5},{2,10},{6,14},... | collective-permute-start | bytes 1966088 | tf_op jit(solution)/shard_map/ppermute | solution.py:116
  9.8 29.2 %collective-permute-start.2 = (bf16[640,512]{1,0:T(8,128)(2,1)}, bf16[640,512]{1,0:T(8,128)(2,1)S(1)}, u32[]{:S(2)}, u32[]{:S(2)}) collective-permute-start(bf16[640,512]{1,0:T(8,128)(2,1)} %get-tuple-element.33.refs_0_), channel_id=1, source_target_pairs={{0,2},{2,0},{1,3},{3,1},{4,6},{6,4},{5,7},{7,5},{8,10},{10,8},{9,1... | collective-permute-start | bytes 1966088 | tf_op jit(solution)/shard_map/ppermute | solution.py:116
  11.3 69.1 %copy-start.4 = (bf16[512,512]{1,0:T(8,128)(2,1)S(1)}, bf16[512,512]{1,0:T(8,128)(2,1)}, u32[]{:S(2)}) copy-start(bf16[512,512]{1,0:T(8,128)(2,1)} %refs_5_.3) | copy-start | bytes 1572868
  11.3 73.9 %copy-start.9 = (bf16[256,512]{1,0:T(8,128)(2,1)S(1)}, bf16[256,512]{1,0:T(8,128)(2,1)}, u32[]{:S(2)}) copy-start(bf16[256,512]{1,0:T(8,128)(2,1)} %get-tuple-element.44) | copy-start | bytes 786436
  11.3 86.6 %copy-start.6 = (bf16[640,512]{1,0:T(8,128)(2,1)S(1)}, bf16[640,512]{1,0:T(8,128)(2,1)}, u32[]{:S(2)}) copy-start(bf16[640,512]{1,0:T(8,128)(2,1)} %get-tuple-element.33.refs_0_) | copy-start | bytes 1966084
  11.6 32.6 %collective-permute-start.4 = (bf16[336,512]{1,0:T(8,128)(2,1)S(1)}, bf16[336,512]{1,0:T(8,128)(2,1)S(1)}, u32[]{:S(2)}, u32[]{:S(2)}) collective-permute-start(bf16[336,512]{1,0:T(8,128)(2,1)S(1)} %get-tuple-element.35), channel_id=1, source_target_pairs={{0,4},{4,0},{8,12},{12,8},{1,5},{5,1},{9,13},{13,9},{2,6},{6,2},{1... | collective-permute-start | bytes 1032200 | tf_op jit(solution)/shard_map/ppermute | solution.py:116
  44.1 9.8 %collective-permute-start.10 = (bf16[336,512]{1,0:T(8,128)(2,1)S(1)}, bf16[336,512]{1,0:T(8,128)(2,1)S(1)}, u32[]{:S(2)}, u32[]{:S(2)}) collective-permute-start(bf16[336,512]{1,0:T(8,128)(2,1)S(1)} %collective-permute-done.4.refs_9_), channel_id=1, source_target_pairs={{0,16},{16,0},{1,17},{17,1},{2,18},{18,2},{3,19},{19,3},{4,20},{20... | collective-permute-start | bytes 1032200 | tf_op jit(solution)/shard_map/ppermute | solution.py:116
  45.8 32.9 %collective-permute-start.5 = (bf16[640,512]{1,0:T(8,128)(2,1)S(1)}, bf16[640,512]{1,0:T(8,128)(2,1)S(1)}, u32[]{:S(2)}, u32[]{:S(2)}) collective-permute-start(bf16[640,512]{1,0:T(8,128)(2,1)S(1)} %collective-permute-done.1.refs_4_), channel_id=1, source_target_pairs={{0,4},{4,0},{8,12},{12,8},{1,5},{5,1},{9,13},{13,9},{2,6},{6,2},{1... | collective-permute-start | bytes 1966088 | tf_op jit(solution)/shard_map/ppermute | solution.py:116
  47.5 31.3 %collective-permute-start.7 = (bf16[640,512]{1,0:T(8,128)(2,1)S(1)}, bf16[640,512]{1,0:T(8,128)(2,1)S(1)}, u32[]{:S(2)}, u32[]{:S(2)}) collective-permute-start(bf16[640,512]{1,0:T(8,128)(2,1)S(1)} %collective-permute-done.1.refs_4_), channel_id=1, source_target_pairs={{0,2},{2,0},{1,3},{3,1},{4,6},{6,4},{5,7},{7,5},{8,10},{10,8},{9,1... | collective-permute-start | bytes 1966088 | tf_op jit(solution)/shard_map/ppermute | solution.py:116
  48.9 29.8 %collective-permute-start.6 = (bf16[640,512]{1,0:T(8,128)(2,1)S(1)}, bf16[640,512]{1,0:T(8,128)(2,1)S(1)}, u32[]{:S(2)}, u32[]{:S(2)}) collective-permute-start(bf16[640,512]{1,0:T(8,128)(2,1)S(1)} %collective-permute-done.refs_2_), channel_id=1, source_target_pairs={{0,2},{2,0},{1,3},{3,1},{4,6},{6,4},{5,7},{7,5},{8,10},{10,8},{9,1... | collective-permute-start | bytes 1966088 | tf_op jit(solution)/shard_map/ppermute | solution.py:116
  49.5 20.6 %collective-permute-start.8 = (bf16[336,512]{1,0:T(8,128)(2,1)S(1)}, bf16[336,512]{1,0:T(8,128)(2,1)S(1)}, u32[]{:S(2)}, u32[]{:S(2)}) collective-permute-start(bf16[336,512]{1,0:T(8,128)(2,1)S(1)} %get-tuple-element.40), channel_id=1, source_target_pairs={{0,8},{4,12},{8,0},{12,4},{1,9},{5,13},{9,1},{13,5},{2,10},{6,14},... | collective-permute-start | bytes 1032200 | tf_op jit(solution)/shard_map/ppermute | solution.py:116
  54.0 24.8 %collective-permute-start.9 = (bf16[336,512]{1,0:T(8,128)(2,1)S(1)}, bf16[336,512]{1,0:T(8,128)(2,1)S(1)}, u32[]{:S(2)}, u32[]{:S(2)}) collective-permute-start(bf16[336,512]{1,0:T(8,128)(2,1)S(1)} %get-tuple-element.41), channel_id=1, source_target_pairs={{0,12},{4,8},{8,4},{12,0},{1,13},{5,9},{9,5},{13,1},{2,14},{6,10},... | collective-permute-start | bytes 1032200 | tf_op jit(solution)/shard_map/ppermute | solution.py:116
  78.8 19.1 %collective-permute-start.13 = (bf16[640,512]{1,0:T(8,128)(2,1)S(1)}, bf16[640,512]{1,0:T(8,128)(2,1)S(1)}, u32[]{:S(2)}, u32[]{:S(2)}) collective-permute-start(bf16[640,512]{1,0:T(8,128)(2,1)S(1)} %collective-permute-done.5.refs_6_), channel_id=1, source_target_pairs={{0,2},{2,0},{1,3},{3,1},{4,6},{6,4},{5,7},{7,5},{8,10},{10,8},{9,1... | collective-permute-start | bytes 1966088 | tf_op jit(solution)/shard_map/ppermute | solution.py:116
  80.3 17.6 %collective-permute-start.16 = (bf16[512,512]{1,0:T(8,128)(2,1)S(1)}, bf16[512,512]{1,0:T(8,128)(2,1)S(1)}, u32[]{:S(2)}, u32[]{:S(2)}) collective-permute-start(bf16[512,512]{1,0:T(8,128)(2,1)S(1)} %copy-done.4), channel_id=1, source_target_pairs={{0,4},{4,0},{8,12},{12,8},{1,5},{5,1},{9,13},{13,9},{2,6},{6,2},{1... | collective-permute-start | bytes 1572872 | tf_op jit(solution)/shard_map/ppermute | solution.py:116
  83.2 14.7 %collective-permute-start.14 = (bf16[336,512]{1,0:T(8,128)(2,1)S(1)}, bf16[336,512]{1,0:T(8,128)(2,1)S(1)}, u32[]{:S(2)}, u32[]{:S(2)}) collective-permute-start(bf16[336,512]{1,0:T(8,128)(2,1)S(1)} %collective-permute-done.8.refs_11_), channel_id=1, source_target_pairs={{0,16},{16,0},{1,17},{17,1},{2,18},{18,2},{3,19},{19,3},{4,20},{20... | collective-permute-start | bytes 1032200 | tf_op jit(solution)/shard_map/ppermute | solution.py:116
  83.7 14.2 %collective-permute-start.15 = (bf16[336,512]{1,0:T(8,128)(2,1)S(1)}, bf16[336,512]{1,0:T(8,128)(2,1)S(1)}, u32[]{:S(2)}, u32[]{:S(2)}) collective-permute-start(bf16[336,512]{1,0:T(8,128)(2,1)S(1)} %collective-permute-done.9.refs_13_), channel_id=1, source_target_pairs={{0,16},{16,0},{1,17},{17,1},{2,18},{18,2},{3,19},{19,3},{4,20},{20... | collective-permute-start | bytes 1032200 | tf_op jit(solution)/shard_map/ppermute | solution.py:116
  85.2 12.7 %collective-permute-start.11 = (bf16[256,512]{1,0:T(8,128)(2,1)S(1)}, bf16[256,512]{1,0:T(8,128)(2,1)S(1)}, u32[]{:S(2)}, u32[]{:S(2)}) collective-permute-start(bf16[256,512]{1,0:T(8,128)(2,1)S(1)} %copy-done.9), channel_id=1, source_target_pairs={{0,8},{4,12},{8,0},{12,4},{1,9},{5,13},{9,1},{13,5},{2,10},{6,14},... | collective-permute-start | bytes 786440 | tf_op jit(solution)/shard_map/ppermute | solution.py:116
  101.9 5.1 %collective-permute-start.17 = (f32[1280,256]{1,0:T(8,128)}, f32[1280,256]{1,0:T(8,128)S(1)}, u32[]{:S(2)}, u32[]{:S(2)}) collective-permute-start(f32[1280,256]{1,0:T(8,128)} %get-tuple-element.55), channel_id=1, source_target_pairs={{0,1},{1,0},{2,3},{3,2},{4,5},{5,4},{6,7},{7,6},{8,9},{9,8},{10,11... | collective-permute-start | bytes 3932168 | tf_op jit(solution)/shard_map/ppermute | solution.py:116
  102.0 10.2 %collective-permute-start.12 = (bf16[256,512]{1,0:T(8,128)(2,1)S(1)}, bf16[256,512]{1,0:T(8,128)(2,1)}, u32[]{:S(2)}, u32[]{:S(2)}) collective-permute-start(bf16[256,512]{1,0:T(8,128)(2,1)S(1)} %collective-permute-done.11.refs_17_.refs_7_), channel_id=1, source_target_pairs={{0,4},{4,0},{8,12},{12,8},{1,5},{5,1},{9,13},{13,9},{2,6},{6,2},{1... | collective-permute-start | bytes 786440 | tf_op jit(solution)/shard_map/ppermute | solution.py:116
  105.4 12.7 %collective-permute-start.21 = (bf16[256,512]{1,0:T(8,128)(2,1)S(1)}, bf16[256,512]{1,0:T(8,128)(2,1)S(1)}, u32[]{:S(2)}, u32[]{:S(2)}) collective-permute-start(bf16[256,512]{1,0:T(8,128)(2,1)S(1)} %collective-permute-done.11.refs_17_.refs_7_), channel_id=1, source_target_pairs={{0,16},{16,0},{1,17},{17,1},{2,18},{18,2},{3,19},{19,3},{4,20},{20... | collective-permute-start | bytes 786440 | tf_op jit(solution)/shard_map/ppermute | solution.py:116
  106.9 16.0 %copy-start.2 = (bf16[256,2048]{1,0:T(8,128)(2,1)S(1)}, bf16[256,2048]{1,0:T(8,128)(2,1)}, u32[]{:S(2)}) copy-start(bf16[256,2048]{1,0:T(8,128)(2,1)} %refs_4_.3) | copy-start | bytes 3145732
  106.9 16.0 %copy-start.5 = (bf16[512,512]{1,0:T(8,128)(2,1)S(1)}, bf16[512,512]{1,0:T(8,128)(2,1)}, u32[]{:S(2)}) copy-start(bf16[512,512]{1,0:T(8,128)(2,1)} %refs_5_.3) | copy-start | bytes 1572868
  112.2 10.7 %collective-permute-start.22 = (bf16[256,512]{1,0:T(8,128)(2,1)}, bf16[256,512]{1,0:T(8,128)(2,1)S(1)}, u32[]{:S(2)}, u32[]{:S(2)}) collective-permute-start(bf16[256,512]{1,0:T(8,128)(2,1)} %collective-permute-done.12.refs_9_), channel_id=1, source_target_pairs={{0,16},{16,0},{1,17},{17,1},{2,18},{18,2},{3,19},{19,3},{4,20},{20... | collective-permute-start | bytes 786440 | tf_op jit(solution)/shard_map/ppermute | solution.py:116
  113.7 4.4 %collective-permute-start.18 = (bf16[256,128]{1,0:T(8,128)(2,1)S(1)}, bf16[256,128]{1,0:T(8,128)(2,1)S(1)}, u32[]{:S(2)}, u32[]{:S(2)}) collective-permute-start(bf16[256,128]{1,0:T(8,128)(2,1)S(1)} %get-tuple-element.58), channel_id=1, source_target_pairs={{0,4},{4,0},{8,12},{12,8},{1,5},{5,1},{9,13},{13,9},{2,6},{6,2},{1... | collective-permute-start | bytes 196616 | tf_op jit(solution)/shard_map/ppermute | solution.py:116
  115.4 7.5 %collective-permute-start.19 = (bf16[256,128]{1,0:T(8,128)(2,1)S(1)}, bf16[256,128]{1,0:T(8,128)(2,1)S(1)}, u32[]{:S(2)}, u32[]{:S(2)}) collective-permute-start(bf16[256,128]{1,0:T(8,128)(2,1)S(1)} %get-tuple-element.59), channel_id=1, source_target_pairs={{0,8},{4,12},{8,0},{12,4},{1,9},{5,13},{9,1},{13,5},{2,10},{6,14},... | collective-permute-start | bytes 196616 | tf_op jit(solution)/shard_map/ppermute | solution.py:116
  115.7 12.5 %copy-start.8 = (s32[8]{0:T(128)S(1)}, s32[8]{0:T(128)}, u32[]{:S(2)}) copy-start(s32[8]{0:T(128)} %refs_0_.1) | copy-start | bytes 100
  115.7 7.2 %collective-permute-start.20 = (bf16[256,128]{1,0:T(8,128)(2,1)S(1)}, bf16[256,128]{1,0:T(8,128)(2,1)S(1)}, u32[]{:S(2)}, u32[]{:S(2)}) collective-permute-start(bf16[256,128]{1,0:T(8,128)(2,1)S(1)} %get-tuple-element.60), channel_id=1, source_target_pairs={{0,12},{4,8},{8,4},{12,0},{1,13},{5,9},{9,5},{13,1},{2,14},{6,10},... | collective-permute-start | bytes 196616 | tf_op jit(solution)/shard_map/ppermute | solution.py:116
  122.9 5.3 %copy-start = (bf16[3,192,2048]{2,1,0:T(8,128)(2,1)S(1)}, bf16[3,192,2048]{2,1,0:T(8,128)(2,1)}, u32[]{:S(2)}) copy-start(bf16[3,192,2048]{2,1,0:T(8,128)(2,1)} %refs_1_.2) | copy-start | bytes 7077892
  125.6 2.0 %collective-permute-start.23 = (bf16[2,256,512]{2,1,0:T(8,128)(2,1)S(1)}, bf16[2,256,512]{2,1,0:T(8,128)(2,1)S(1)}, u32[]{:S(2)}, u32[]{:S(2)}) collective-permute-start(bf16[2,256,512]{2,1,0:T(8,128)(2,1)S(1)} %get-tuple-element.63), channel_id=1, source_target_pairs={{0,1},{1,0},{2,3},{3,2},{4,5},{5,4},{6,7},{7,6},{8,9},{9,8},{10,11... | collective-permute-start | bytes 1572872 | tf_op jit(solution)/shard_map/ppermute | solution.py:116
  127.6 8.4 %collective-permute-start.24 = (bf16[256,512]{1,0:T(8,128)(2,1)S(1)}, bf16[256,512]{1,0:T(8,128)(2,1)S(1)}, u32[]{:S(2)}, u32[]{:S(2)}) collective-permute-start(bf16[256,512]{1,0:T(8,128)(2,1)S(1)} %fusion.1), channel_id=1, source_target_pairs={{0,2},{2,0},{1,3},{3,1},{4,6},{6,4},{5,7},{7,5},{8,10},{10,8},{9,1... | collective-permute-start | bytes 786440 | tf_op jit(solution)/shard_map/ppermute | solution.py:116

commit v12 on v9

--- a/solution.py
+++ b/solution.py
@@ -304,7 +304,7 @@
 
 def products_body(*refs):
     packed_refs, weight_refs = refs[:8], refs[8:15]
-    own_align, align_ref, send_ref, keep_ref, rows_ref, audio_ref, kv_ref, query_ref = refs[15:]
+    own_align, near_align, align_ref, send_ref, keep_ref, rows_ref, audio_ref, kv_ref, query_ref = refs[15:]
     seq_at, mem_at, grp_at = (lax.axis_index(name) for name in ("seq", "mem", "grp"))
     rows, audio_rows = rows_ref.shape[0] // 4, audio_ref.shape[0] // 4
     depth, lane = rows_ref.shape[1] // 4, audio_ref.shape[1] // 4
@@ -337,7 +337,9 @@
     for bit in range(1, 4):
         place(weight_refs[2 * bit - 1], seq_at ^ bit, grp_at, 0, kv_half)
         place(weight_refs[2 * bit], seq_at ^ bit, 1 - grp_at, 0, kv_half)
-        align_ref[bit] = weight_refs[2 * bit - 1][kv_half + fold :, : align_ref.shape[2]]
+        if bit > 1:
+            align_ref[bit] = weight_refs[2 * bit - 1][kv_half + fold :, : align_ref.shape[2]]
+    align_ref[1] = near_align[...].astype(align_ref.dtype)
     align_ref[0] = jnp.broadcast_to(
         own_align[...].astype(jnp.float32).astype(align_ref.dtype), align_ref.shape[1:]
     )
@@ -391,15 +393,16 @@
 
 
 def out_body(*refs):
-    piece_refs, (own_w, *part_refs), (send_ref, keep_ref, heads_ref, weight_ref, sem) = (
-        refs[:4],
-        refs[4:11],
-        refs[11:],
-    )
+    piece_refs, (audio_ref, own_w, *part_refs) = refs[:4], refs[4:12]
+    send_ref, keep_ref, heads_ref, weight_ref, residual_ref, sems = refs[12:]
     seq_at, grp_at = lax.axis_index("seq"), lax.axis_index("grp")
     place = lax.axis_index("mem") * 2 + lax.axis_index("rep")
-    copy = pltpu.make_async_copy(own_w, weight_ref.at[0], sem)
+    copy = pltpu.make_async_copy(own_w, weight_ref.at[0], sems.at[0])
     copy.start()
+    width = residual_ref.shape[1]
+    columns = pl.ds(pl.multiple_of(place * width, width), width)
+    residual_copy = pltpu.make_async_copy(audio_ref.at[:, columns], residual_ref, sems.at[1])
+    residual_copy.start()
     for bit, piece_ref in enumerate(piece_refs):
         heads_ref[seq_at ^ bit] = piece_ref[...]
     heads = jnp.concatenate([heads_ref[head] for head in range(heads_ref.shape[0])], axis=1)
@@ -423,11 +426,13 @@
         def _():
             keep_ref[slot // 2] = value
 
+    residual_copy.wait()
+    keep_ref[0] += residual_ref[...].astype(jnp.float32)
+
 
 def by_head(video_cache, plan, alignment, audio_tokens, kv_weight, query_weight, out_weight):
     seq_size = lax.axis_size("seq")
     seq_at = lax.axis_index("seq")
-    place = lax.axis_index("mem") * 2 + lax.axis_index("rep")
     video_rows = video_cache.shape[1]
     audio_rows = audio_tokens.shape[0]
     half_depth, width = kv_weight.shape[0] // 2, 2 * HEAD_DIM
@@ -469,9 +474,10 @@
     )
     pieces = [swap(piece, "seq", bit) for bit, piece in enumerate(pieces, 1)]
 
-    across.append(swap(tokens[1], "mem", 1))
+    across += [swap(tokens[1], "mem", 1), swap(tokens[2], "mem", 1)]
+    near_align = pieces[0][rows:, :audio_rows].astype(jnp.float32)
+    tokens[2], near_align = lax.optimization_barrier((tokens[2], near_align))
     tokens.append(swap(tokens[2], "seq", 1))
-    across.append(swap(tokens[2], "mem", 1))
     pieces[0], across[0], across[1] = lax.optimization_barrier(
         (pieces[0], across[0], across[1])
     )
@@ -480,7 +486,9 @@
         (tokens[3], across[2], rest[0], pieces[1])
     )
     across.append(swap(tokens[3], "mem", 1))
-    rest += [swap(piece, "grp", 1) for piece in pieces[1:]]
+    rest.append(swap(pieces[1], "grp", 1))
+    pieces[2], rest[1] = lax.optimization_barrier((pieces[2], rest[1]))
+    rest.append(swap(pieces[2], "grp", 1))
 
     out_half, tokens[3] = lax.optimization_barrier((out_half, tokens[3]))
     out_third, out_partner = swap(out_half, "seq", 2), swap(out_half, "seq", 1)
@@ -492,7 +500,8 @@
     aligns, send, keep = kernel_call(
         products_body,
         [bfloat(4, 16, audio_rows), sums, sums],
-        [value for pair in zip(tokens, across) for value in pair] + weights + [alignment[None]],
+        [value for pair in zip(tokens, across) for value in pair] + weights
+        + [alignment[None], near_align],
         scratch=[
             pltpu.VMEM((seq_size * video_rows, 4 * half_depth), jnp.bfloat16),
             pltpu.VMEM((seq_size * audio_rows, 8 * query_quarter), jnp.bfloat16),
@@ -535,22 +544,22 @@
             jax.ShapeDtypeStruct((2, audio_rows, columns), jnp.bfloat16),
             jax.ShapeDtypeStruct((2, audio_rows, columns), jnp.float32),
         ],
-        [own_piece, near_piece, far_piece, farther_piece, *weights],
+        [own_piece, near_piece, far_piece, farther_piece, audio_tokens, *weights],
         scratch=[
             pltpu.VMEM((seq_size, audio_rows, HEAD_DIM), jnp.bfloat16),
             pltpu.VMEM((seq_size, *out_weight.shape), jnp.bfloat16),
-            pltpu.SemaphoreType.DMA,
+            pltpu.VMEM((audio_rows, columns), jnp.bfloat16),
+            pltpu.SemaphoreType.DMA((2,)),
         ],
-        loose_in=(4,),
+        loose_in=(4, 5),
         limit=7,
     )
     came = swap(send, "rep", 1)
     across = swap((keep[1] + came[1].astype(jnp.float32)).astype(jnp.bfloat16), "mem", 1)
-    residual = lax.dynamic_slice_in_dim(audio_tokens, place * columns, columns, 1)
     own_part = taylor(video_cache, plan, 2 * half_depth)
-    base = residual.astype(jnp.float32) + (keep[0] + came[0].astype(jnp.float32))
-    base, across = lax.optimization_barrier((base, across))
-    audio_output = (base + across.astype(jnp.float32)).astype(jnp.bfloat16)
+    audio_output = (
+        keep[0] + came[0].astype(jnp.float32) + across.astype(jnp.float32)
+    ).astype(jnp.bfloat16)
     return (own_part, audio_output)
 
 

time: 136 us -> 125 us (0.919)
  waiting for transfers between devices: 82.9 us -> 71.8 us
  starting transfers between devices: 31.9 us -> 37.4 us
  other arithmetic: 3.88 us -> 1.14 us
  local copies, waits for them, and re-layouts: 1.94 us -> 0.4 us
    ppermute x26, waiting for transfers between devices: 82.9 us -> 71.8 us  [swap(): return lax.ppermute(value, axis, [(i, i ^ bit) for i in range(size)])]
    ppermute x26, starting transfers between devices: 31.9 us -> 37.4 us  [swap(): return lax.ppermute(value, axis, [(i, i ^ bit) for i in range(size)])]
    unnamed x22 -> x18, local copies, waits for them, and re-layouts: 1.77 us -> 0.23 us
  transfers between devices with their start and end apart: 26 -> 26, of which waited for: 17 -> 18; matrix products, arithmetic and copies ran while one was open for 1% -> 0% of each run, Pallas kernels for 6% -> 7%
where the time goes in v12:
time: 125 us
  waiting for transfers between devices  71.8 us (57%)
  starting transfers between devices  37.4 us (30%)
  Pallas kernels  13.1 us (10%)
    ppermute x26, waiting for transfers between devices, swap(): return lax.ppermute(value, axis, [(i, i ^ bit) for i in range(size)])  71.8 us
    ppermute x26, starting transfers between devices, swap(): return lax.ppermute(value, axis, [(i, i ^ bit) for i in range(size)])  37.4 us
    pallas_call x5, Pallas kernels, kernel_call(): pl.pallas_call(whole, out_shape=outs, in_specs=spots + [ANY] * len(after)...  11.3 us
  transfers between devices with their start and end apart: 26, of which 18 were waited for; matrix products, arithmetic and copies ran while one was open for 0% of the time, Pallas kernels for 7%

profile of v12, /device:TPU:0, one launch (start us, length us, event | category | flops | bytes accessed | tf_op | source)
XLA Modules:
  0.0 124.7 jit_solution(1852202113946514879)
XLA Ops:
  0.7 3.3 %shard_map.87 = (bf16[640,512]{1,0:T(8,128)(2,1)}, bf16[640,1024]{1,0:T(8,128)(2,1)}, bf16[256,512]{1,0:T(8,128)(2,1)}) custom-call(s32[8]{0:T(128)} %refs_0_.1, bf16[3,192,2048]{2,1,0:T(8,128)(2,1)} %refs_1_.2, bf16[256,2048]{1,0:T(8,128)(2,1)} %refs_4_.3, bf16[1024,1024]{1,0:T(8,128)(2,1)} %refs_1_.3, bf16[512,512]{1,0:T(8,128)(2,1)} %refs_2_.3, ...), custom_call_target="tpu_custom_call" | custom-call | tf_op jit(solution)/shard_map/pallas_call | solution.py:130
  4.0 0.5 collective-permute-start
  4.5 2.6 %collective-permute-start.3 = (bf16[640,512]{1,0:T(8,128)(2,1)}, bf16[640,512]{1,0:T(8,128)(2,1)S(1)}, u32[]{:S(2)}, u32[]{:S(2)}) collective-permute-start(bf16[640,512]{1,0:T(8,128)(2,1)} %get-tuple-element.36.refs_0_), channel_id=1, source_target_pairs={{0,4},{4,0},{8,12},{12,8},{1,5},{5,1},{9,13},{13,9},{2,6},{6,2},{1... | collective-permute-start | bytes 1966088 | tf_op jit(solution)/shard_map/ppermute | solution.py:116
  7.2 2.6 %collective-permute-start.5 = (bf16[640,512]{1,0:T(8,128)(2,1)}, bf16[640,512]{1,0:T(8,128)(2,1)S(1)}, u32[]{:S(2)}, u32[]{:S(2)}) collective-permute-start(bf16[640,512]{1,0:T(8,128)(2,1)} %get-tuple-element.36.refs_0_), channel_id=1, source_target_pairs={{0,8},{4,12},{8,0},{12,4},{1,9},{5,13},{9,1},{13,5},{2,10},{6,14},... | collective-permute-start | bytes 1966088 | tf_op jit(solution)/shard_map/ppermute | solution.py:116
  9.8 0.3 shard_map.88
  10.1 0.6 collective-permute-start.1
  10.9 1.5 %collective-permute-start.2 = (bf16[640,512]{1,0:T(8,128)(2,1)S(1)}, bf16[640,512]{1,0:T(8,128)(2,1)S(1)}, u32[]{:S(2)}, u32[]{:S(2)}) collective-permute-start(bf16[640,512]{1,0:T(8,128)(2,1)S(1)} %copy-done.5), channel_id=1, source_target_pairs={{0,2},{2,0},{1,3},{3,1},{4,6},{6,4},{5,7},{7,5},{8,10},{10,8},{9,1... | collective-permute-start | bytes 1966088 | tf_op jit(solution)/shard_map/ppermute | solution.py:116
  12.4 24.5 %collective-permute-done.3.refs_2_ = bf16[640,512]{1,0:T(8,128)(2,1)S(1)} collective-permute-done((bf16[640,512]{1,0:T(8,128)(2,1)}, bf16[640,512]{1,0:T(8,128)(2,1)S(1)}, u32[]{:S(2)}, u32[]{:S(2)}) %collective-permute-start.3) | collective-permute-done | bytes 655392 | tf_op jit(solution)/shard_map/ppermute | solution.py:116
  36.9 1.9 %collective-permute-start.4 = (bf16[640,512]{1,0:T(8,128)(2,1)S(1)}, bf16[640,512]{1,0:T(8,128)(2,1)S(1)}, u32[]{:S(2)}, u32[]{:S(2)}) collective-permute-start(bf16[640,512]{1,0:T(8,128)(2,1)S(1)} %collective-permute-done.3.refs_2_), channel_id=1, source_target_pairs={{0,2},{2,0},{1,3},{3,1},{4,6},{6,4},{5,7},{7,5},{8,10},{10,8},{9,1... | collective-permute-start | bytes 1966088 | tf_op jit(solution)/shard_map/ppermute | solution.py:116
  38.9 1.5 %collective-permute-start.7 = (bf16[640,512]{1,0:T(8,128)(2,1)S(1)}, bf16[640,512]{1,0:T(8,128)(2,1)S(1)}, u32[]{:S(2)}, u32[]{:S(2)}) collective-permute-start(bf16[640,512]{1,0:T(8,128)(2,1)S(1)} %collective-permute-done.5.refs_4_), channel_id=1, source_target_pairs={{0,2},{2,0},{1,3},{3,1},{4,6},{6,4},{5,7},{7,5},{8,10},{10,8},{9,1... | collective-permute-start | bytes 1966088 | tf_op jit(solution)/shard_map/ppermute | solution.py:116
  40.4 3.7 %collective-permute-done.1.refs_9_ = bf16[336,512]{1,0:T(8,128)(2,1)S(1)} collective-permute-done((bf16[336,512]{1,0:T(8,128)(2,1)S(1)}, bf16[336,512]{1,0:T(8,128)(2,1)S(1)}, u32[]{:S(2)}, u32[]{:S(2)}) %collective-permute-start.1) | collective-permute-done | bytes 344096 | tf_op jit(solution)/shard_map/ppermute | solution.py:116
  44.1 1.8 %collective-permute-start.6 = (bf16[640,512]{1,0:T(8,128)(2,1)S(1)}, bf16[640,512]{1,0:T(8,128)(2,1)S(1)}, u32[]{:S(2)}, u32[]{:S(2)}) collective-permute-start(bf16[640,512]{1,0:T(8,128)(2,1)S(1)} %collective-permute-done.5.refs_4_), channel_id=1, source_target_pairs={{0,4},{4,0},{8,12},{12,8},{1,5},{5,1},{9,13},{13,9},{2,6},{6,2},{1... | collective-permute-start | bytes 1966088 | tf_op jit(solution)/shard_map/ppermute | solution.py:116
  45.9 2.5 %collective-permute-start.9 = (bf16[336,512]{1,0:T(8,128)(2,1)S(1)}, bf16[336,512]{1,0:T(8,128)(2,1)S(1)}, u32[]{:S(2)}, u32[]{:S(2)}) collective-permute-start(bf16[336,512]{1,0:T(8,128)(2,1)S(1)} %get-tuple-element.43), channel_id=1, source_target_pairs={{0,8},{4,12},{8,0},{12,4},{1,9},{5,13},{9,1},{13,5},{2,10},{6,14},... | collective-permute-start | bytes 1032200 | tf_op jit(solution)/shard_map/ppermute | solution.py:116
  48.5 6.1 %collective-permute-done.4.refs_3_ = bf16[640,512]{1,0:T(8,128)(2,1)S(1)} collective-permute-done((bf16[640,512]{1,0:T(8,128)(2,1)S(1)}, bf16[640,512]{1,0:T(8,128)(2,1)S(1)}, u32[]{:S(2)}, u32[]{:S(2)}) %collective-permute-start.4) | collective-permute-done | bytes 655392 | tf_op jit(solution)/shard_map/ppermute | solution.py:116
  54.5 1.9 %collective-permute-start.8 = (bf16[336,512]{1,0:T(8,128)(2,1)S(1)}, bf16[336,512]{1,0:T(8,128)(2,1)S(1)}, u32[]{:S(2)}, u32[]{:S(2)}) collective-permute-start(bf16[336,512]{1,0:T(8,128)(2,1)S(1)} %collective-permute-done.1.refs_9_), channel_id=1, source_target_pairs={{0,16},{16,0},{1,17},{17,1},{2,18},{18,2},{3,19},{19,3},{4,20},{20... | collective-permute-start | bytes 1032200 | tf_op jit(solution)/shard_map/ppermute | solution.py:116
  56.4 2.5 %collective-permute-start.11 = (bf16[336,512]{1,0:T(8,128)(2,1)S(1)}, bf16[336,512]{1,0:T(8,128)(2,1)S(1)}, u32[]{:S(2)}, u32[]{:S(2)}) collective-permute-start(bf16[336,512]{1,0:T(8,128)(2,1)S(1)} %get-tuple-element.51), channel_id=1, source_target_pairs={{0,12},{4,8},{8,4},{12,0},{1,13},{5,9},{9,5},{13,1},{2,14},{6,10},... | collective-permute-start | bytes 1032200 | tf_op jit(solution)/shard_map/ppermute | solution.py:116
  58.9 8.2 %collective-permute-done.7.refs_5_ = bf16[640,512]{1,0:T(8,128)(2,1)S(1)} collective-permute-done((bf16[640,512]{1,0:T(8,128)(2,1)S(1)}, bf16[640,512]{1,0:T(8,128)(2,1)S(1)}, u32[]{:S(2)}, u32[]{:S(2)}) %collective-permute-start.7) | collective-permute-done | bytes 655392 | tf_op jit(solution)/shard_map/ppermute | solution.py:116
  67.2 1.4 %collective-permute-done.9.refs_11_ = bf16[336,512]{1,0:T(8,128)(2,1)S(1)} collective-permute-done((bf16[336,512]{1,0:T(8,128)(2,1)S(1)}, bf16[336,512]{1,0:T(8,128)(2,1)S(1)}, u32[]{:S(2)}, u32[]{:S(2)}) %collective-permute-start.9) | collective-permute-done | bytes 344096 | tf_op jit(solution)/shard_map/ppermute | solution.py:116
  68.5 1.5 %collective-permute-start.12 = (bf16[336,512]{1,0:T(8,128)(2,1)S(1)}, bf16[336,512]{1,0:T(8,128)(2,1)S(1)}, u32[]{:S(2)}, u32[]{:S(2)}) collective-permute-start(bf16[336,512]{1,0:T(8,128)(2,1)S(1)} %collective-permute-done.9.refs_11_), channel_id=1, source_target_pairs={{0,16},{16,0},{1,17},{17,1},{2,18},{18,2},{3,19},{19,3},{4,20},{20... | collective-permute-start | bytes 1032200 | tf_op jit(solution)/shard_map/ppermute | solution.py:116
  70.0 1.5 %collective-permute-start.10 = (bf16[640,512]{1,0:T(8,128)(2,1)S(1)}, bf16[640,512]{1,0:T(8,128)(2,1)S(1)}, u32[]{:S(2)}, u32[]{:S(2)}) collective-permute-start(bf16[640,512]{1,0:T(8,128)(2,1)S(1)} %collective-permute-done.6.refs_6_), channel_id=1, source_target_pairs={{0,2},{2,0},{1,3},{3,1},{4,6},{6,4},{5,7},{7,5},{8,10},{10,8},{9,1... | collective-permute-start | bytes 1966088 | tf_op jit(solution)/shard_map/ppermute | solution.py:116
  71.5 6.0 %collective-permute-done.11.refs_13_ = bf16[336,512]{1,0:T(8,128)(2,1)S(1)} collective-permute-done((bf16[336,512]{1,0:T(8,128)(2,1)S(1)}, bf16[336,512]{1,0:T(8,128)(2,1)S(1)}, u32[]{:S(2)}, u32[]{:S(2)}) %collective-permute-start.11) | collective-permute-done | bytes 344096 | tf_op jit(solution)/shard_map/ppermute | solution.py:116
  77.5 1.5 %collective-permute-start.13 = (bf16[336,512]{1,0:T(8,128)(2,1)S(1)}, bf16[336,512]{1,0:T(8,128)(2,1)S(1)}, u32[]{:S(2)}, u32[]{:S(2)}) collective-permute-start(bf16[336,512]{1,0:T(8,128)(2,1)S(1)} %collective-permute-done.11.refs_13_), channel_id=1, source_target_pairs={{0,16},{16,0},{1,17},{17,1},{2,18},{18,2},{3,19},{19,3},{4,20},{20... | collective-permute-start | bytes 1032200 | tf_op jit(solution)/shard_map/ppermute | solution.py:116
  79.1 2.6 %collective-permute-start.14 = (bf16[256,512]{1,0:T(8,128)(2,1)S(1)}, bf16[256,512]{1,0:T(8,128)(2,1)S(1)}, u32[]{:S(2)}, u32[]{:S(2)}) collective-permute-start(bf16[256,512]{1,0:T(8,128)(2,1)S(1)} %copy-done.8), channel_id=1, source_target_pairs={{0,8},{4,12},{8,0},{12,4},{1,9},{5,13},{9,1},{13,5},{2,10},{6,14},... | collective-permute-start | bytes 786440 | tf_op jit(solution)/shard_map/ppermute | solution.py:116
  81.7 1.3 %collective-permute-start.15 = (bf16[256,512]{1,0:T(8,128)(2,1)S(1)}, bf16[256,512]{1,0:T(8,128)(2,1)S(1)}, u32[]{:S(2)}, u32[]{:S(2)}) collective-permute-start(bf16[256,512]{1,0:T(8,128)(2,1)S(1)} %copy-done.8), channel_id=1, source_target_pairs={{0,4},{4,0},{8,12},{12,8},{1,5},{5,1},{9,13},{13,9},{2,6},{6,2},{1... | collective-permute-start | bytes 786440 | tf_op jit(solution)/shard_map/ppermute | solution.py:116
  83.0 1.7 %collective-permute-done.10.refs_7_ = bf16[640,512]{1,0:T(8,128)(2,1)S(1)} collective-permute-done((bf16[640,512]{1,0:T(8,128)(2,1)S(1)}, bf16[640,512]{1,0:T(8,128)(2,1)S(1)}, u32[]{:S(2)}, u32[]{:S(2)}) %collective-permute-start.10) | collective-permute-done | bytes 655392 | tf_op jit(solution)/shard_map/ppermute | solution.py:116
  84.6 1.6 %collective-permute-done.13.refs_14_ = bf16[336,512]{1,0:T(8,128)(2,1)S(1)} collective-permute-done((bf16[336,512]{1,0:T(8,128)(2,1)S(1)}, bf16[336,512]{1,0:T(8,128)(2,1)S(1)}, u32[]{:S(2)}, u32[]{:S(2)}) %collective-permute-start.13) | collective-permute-done | bytes 344096 | tf_op jit(solution)/shard_map/ppermute | solution.py:116
  86.2 3.9 %shard_map.89 = (bf16[4,16,256]{2,1,0:T(8,128)(2,1)S(1)}, f32[1280,256]{1,0:T(8,128)}, f32[1280,256]{1,0:T(8,128)S(1)}) custom-call(bf16[640,512]{1,0:T(8,128)(2,1)S(1)} %copy-done.5, bf16[640,512]{1,0:T(8,128)(2,1)S(1)} %collective-permute-done.2.refs_1_, bf16[640,512]{1,0:T(8,128)(2,1)S(1)} %collective-permute-done.3.refs_2_, ...), custom_call_target="tpu_custom_call" | custom-call | tf_op jit(solution)/shard_map/pallas_call | solution.py:130
  90.1 1.2 collective-permute-done.14.refs_8_
  91.5 0.4 collective-permute-start.16
  92.1 1.3 %collective-permute-start.21 = (bf16[256,512]{1,0:T(8,128)(2,1)S(1)}, bf16[256,512]{1,0:T(8,128)(2,1)S(1)}, u32[]{:S(2)}, u32[]{:S(2)}) collective-permute-start(bf16[256,512]{1,0:T(8,128)(2,1)S(1)} %collective-permute-done.15.refs_6_), channel_id=1, source_target_pairs={{0,16},{16,0},{1,17},{17,1},{2,18},{18,2},{3,19},{19,3},{4,20},{20... | collective-permute-start | bytes 786440 | tf_op jit(solution)/shard_map/ppermute | solution.py:116
  93.4 0.8 collective-permute-start.22
  94.2 0.4 collective-permute-done.17.refs_3_
  94.6 2.2 %shard_map.90 = (bf16[256,128]{1,0:T(8,128)(2,1)S(1)}, bf16[256,128]{1,0:T(8,128)(2,1)S(1)}, bf16[256,128]{1,0:T(8,128)(2,1)S(1)}, bf16[256,128]{1,0:T(8,128)(2,1)S(1)}) custom-call(f32[1,768]{1,0:T(1,128)S(1)} %fusion.4.refs_0_, bf16[4,16,256]{2,1,0:T(8,128)(2,1)S(1)} %get-tuple-element.58.refs_1_, f32[1280,256]{1,0:T(8,128)S(1)} %get-tuple-element.59.refs_2_, ...), custom_call_target="tpu_custom_call" | custom-call | tf_op jit(solution)/shard_map/pallas_call | solution.py:130
  96.8 3.4 %collective-permute-done.16.refs_10_ = bf16[256,512]{1,0:T(8,128)(2,1)S(1)} collective-permute-done((bf16[256,512]{1,0:T(8,128)(2,1)S(1)}, bf16[256,512]{1,0:T(8,128)(2,1)S(1)}, u32[]{:S(2)}, u32[]{:S(2)}) %collective-permute-start.16) | collective-permute-done | bytes 262176 | tf_op jit(solution)/shard_map/ppermute | solution.py:116
  100.2 0.5 collective-permute-start.23
  100.7 1.2 collective-permute-start.18
  101.9 1.8 %collective-permute-start.19 = (bf16[256,128]{1,0:T(8,128)(2,1)S(1)}, bf16[256,128]{1,0:T(8,128)(2,1)S(1)}, u32[]{:S(2)}, u32[]{:S(2)}) collective-permute-start(bf16[256,128]{1,0:T(8,128)(2,1)S(1)} %get-tuple-element.64), channel_id=1, source_target_pairs={{0,8},{4,12},{8,0},{12,4},{1,9},{5,13},{9,1},{13,5},{2,10},{6,14},... | collective-permute-start | bytes 196616 | tf_op jit(solution)/shard_map/ppermute | solution.py:116
  103.7 1.4 %collective-permute-start.20 = (bf16[256,128]{1,0:T(8,128)(2,1)S(1)}, bf16[256,128]{1,0:T(8,128)(2,1)S(1)}, u32[]{:S(2)}, u32[]{:S(2)}) collective-permute-start(bf16[256,128]{1,0:T(8,128)(2,1)S(1)} %get-tuple-element.65), channel_id=1, source_target_pairs={{0,12},{4,8},{8,4},{12,0},{1,13},{5,9},{9,5},{13,1},{2,14},{6,10},... | collective-permute-start | bytes 196616 | tf_op jit(solution)/shard_map/ppermute | solution.py:116
  105.1 1.8 %collective-permute-done.22.refs_9_ = bf16[256,512]{1,0:T(8,128)(2,1)S(1)} collective-permute-done((bf16[256,512]{1,0:T(8,128)(2,1)S(1)}, bf16[256,512]{1,0:T(8,128)(2,1)S(1)}, u32[]{:S(2)}, u32[]{:S(2)}) %collective-permute-start.22) | collective-permute-done | bytes 262176 | tf_op jit(solution)/shard_map/ppermute | solution.py:116
  106.9 1.9 %collective-permute-done.19.refs_2_ = bf16[256,128]{1,0:T(8,128)(2,1)S(1)} collective-permute-done((bf16[256,128]{1,0:T(8,128)(2,1)S(1)}, bf16[256,128]{1,0:T(8,128)(2,1)S(1)}, u32[]{:S(2)}, u32[]{:S(2)}) %collective-permute-start.19) | collective-permute-done | bytes 65568 | tf_op jit(solution)/shard_map/ppermute | solution.py:116
  108.7 1.2 collective-permute-done.20.refs_3_
  109.9 1.9 %collective-permute-done.23.refs_11_ = bf16[256,512]{1,0:T(8,128)(2,1)S(1)} collective-permute-done((bf16[256,512]{1,0:T(8,128)(2,1)S(1)}, bf16[256,512]{1,0:T(8,128)(2,1)S(1)}, u32[]{:S(2)}, u32[]{:S(2)}) %collective-permute-start.23) | collective-permute-done | bytes 262176 | tf_op jit(solution)/shard_map/ppermute | solution.py:116
  111.8 1.6 %shard_map.91 = (bf16[2,256,512]{2,1,0:T(8,128)(2,1)S(1)}, f32[2,256,512]{2,1,0:T(8,128)S(1)}) custom-call(bf16[256,128]{1,0:T(8,128)(2,1)S(1)} %get-tuple-element.62.refs_0_, bf16[256,128]{1,0:T(8,128)(2,1)S(1)} %collective-permute-done.18.refs_1_, bf16[256,128]{1,0:T(8,128)(2,1)S(1)} %collective-permute-done.19.refs_2_, ...), custom_call_target="tpu_custom_call" | custom-call | tf_op jit(solution)/shard_map/pallas_call | solution.py:130
  113.5 1.9 %collective-permute-done.24 = bf16[2,256,512]{2,1,0:T(8,128)(2,1)S(1)} collective-permute-done((bf16[2,256,512]{2,1,0:T(8,128)(2,1)S(1)}, bf16[2,256,512]{2,1,0:T(8,128)(2,1)S(1)}, u32[]{:S(2)}, u32[]{:S(2)}) %collective-permute-start.24) | collective-permute-done | bytes 524320 | tf_op jit(solution)/shard_map/ppermute | solution.py:116
  115.5 1.6 %collective-permute-start.25 = (bf16[256,512]{1,0:T(8,128)(2,1)S(1)}, bf16[256,512]{1,0:T(8,128)(2,1)S(1)}, u32[]{:S(2)}, u32[]{:S(2)}) collective-permute-start(bf16[256,512]{1,0:T(8,128)(2,1)S(1)} %fusion.1), channel_id=1, source_target_pairs={{0,2},{2,0},{1,3},{3,1},{4,6},{6,4},{5,7},{7,5},{8,10},{10,8},{9,1... | collective-permute-start | bytes 786440 | tf_op jit(solution)/shard_map/ppermute | solution.py:116
  117.0 1.8 %shard_map.86 = bf16[192,2048]{1,0:T(8,128)(2,1)} custom-call(s32[8]{0:T(128)S(1)} %copy-done.7, bf16[3,192,2048]{2,1,0:T(8,128)(2,1)S(1)} %copy-done), custom_call_target="tpu_custom_call" | custom-call | tf_op jit(solution)/shard_map/pallas_call | solution.py:168
  118.9 5.0 %collective-permute-done.25 = bf16[256,512]{1,0:T(8,128)(2,1)S(1)} collective-permute-done((bf16[256,512]{1,0:T(8,128)(2,1)S(1)}, bf16[256,512]{1,0:T(8,128)(2,1)S(1)}, u32[]{:S(2)}, u32[]{:S(2)}) %collective-permute-start.25) | collective-permute-done | bytes 262176 | tf_op jit(solution)/shard_map/ppermute | solution.py:116
  123.9 0.8 fusion
  (37 shorter events, 1.0 us)
Async XLA Ops:
  0.6 9.1 %copy-start.3 = (bf16[512,512]{1,0:T(8,128)(2,1)S(1)}, bf16[512,512]{1,0:T(8,128)(2,1)}, u32[]{:S(2)}) copy-start(bf16[512,512]{1,0:T(8,128)(2,1)} %refs_2_.3) | copy-start | bytes 1572868
  0.6 9.1 %copy-start.1 = (bf16[1024,1024]{1,0:T(8,128)(2,1)S(1)}, bf16[1024,1024]{1,0:T(8,128)(2,1)}, u32[]{:S(2)}) copy-start(bf16[1024,1024]{1,0:T(8,128)(2,1)} %refs_1_.3) | copy-start | bytes 6291460
  0.7 9.1 %copy-start.6 = (s32[256]{0:T(256)S(1)}, s32[256]{0:T(256)}, u32[]{:S(2)}) copy-start(s32[256]{0:T(256)} %param.9) | copy-start | bytes 3076
  4.0 5.8 %collective-permute-start = (bf16[640,1024]{1,0:T(8,128)(2,1)}, bf16[640,1024]{1,0:T(8,128)(2,1)S(1)}, u32[]{:S(2)}, u32[]{:S(2)}) collective-permute-start(bf16[640,1024]{1,0:T(8,128)(2,1)} %get-tuple-element.37), channel_id=1, source_target_pairs={{0,1},{1,0},{2,3},{3,2},{4,5},{5,4},{6,7},{7,6},{8,9},{9,8},{10,11... | collective-permute-start | bytes 3932168 | tf_op jit(solution)/shard_map/ppermute | solution.py:116
  4.5 32.4 %collective-permute-start.3 = (bf16[640,512]{1,0:T(8,128)(2,1)}, bf16[640,512]{1,0:T(8,128)(2,1)S(1)}, u32[]{:S(2)}, u32[]{:S(2)}) collective-permute-start(bf16[640,512]{1,0:T(8,128)(2,1)} %get-tuple-element.36.refs_0_), channel_id=1, source_target_pairs={{0,4},{4,0},{8,12},{12,8},{1,5},{5,1},{9,13},{13,9},{2,6},{6,2},{1... | collective-permute-start | bytes 1966088 | tf_op jit(solution)/shard_map/ppermute | solution.py:116
  7.2 31.8 %collective-permute-start.5 = (bf16[640,512]{1,0:T(8,128)(2,1)}, bf16[640,512]{1,0:T(8,128)(2,1)S(1)}, u32[]{:S(2)}, u32[]{:S(2)}) collective-permute-start(bf16[640,512]{1,0:T(8,128)(2,1)} %get-tuple-element.36.refs_0_), channel_id=1, source_target_pairs={{0,8},{4,12},{8,0},{12,4},{1,9},{5,13},{9,1},{13,5},{2,10},{6,14},... | collective-permute-start | bytes 1966088 | tf_op jit(solution)/shard_map/ppermute | solution.py:116
  9.8 1.1 copy-start.5
  9.8 69.3 %copy-start.8 = (bf16[256,512]{1,0:T(8,128)(2,1)S(1)}, bf16[256,512]{1,0:T(8,128)(2,1)}, u32[]{:S(2)}) copy-start(bf16[256,512]{1,0:T(8,128)(2,1)} %get-tuple-element.56) | copy-start | bytes 786436
  10.1 34.1 %collective-permute-start.1 = (bf16[336,512]{1,0:T(8,128)(2,1)S(1)}, bf16[336,512]{1,0:T(8,128)(2,1)S(1)}, u32[]{:S(2)}, u32[]{:S(2)}) collective-permute-start(bf16[336,512]{1,0:T(8,128)(2,1)S(1)} %get-tuple-element.38), channel_id=1, source_target_pairs={{0,4},{4,0},{8,12},{12,8},{1,5},{5,1},{9,13},{13,9},{2,6},{6,2},{1... | collective-permute-start | bytes 1032200 | tf_op jit(solution)/shard_map/ppermute | solution.py:116
  10.9 37.6 %collective-permute-start.2 = (bf16[640,512]{1,0:T(8,128)(2,1)S(1)}, bf16[640,512]{1,0:T(8,128)(2,1)S(1)}, u32[]{:S(2)}, u32[]{:S(2)}) collective-permute-start(bf16[640,512]{1,0:T(8,128)(2,1)S(1)} %copy-done.5), channel_id=1, source_target_pairs={{0,2},{2,0},{1,3},{3,1},{4,6},{6,4},{5,7},{7,5},{8,10},{10,8},{9,1... | collective-permute-start | bytes 1966088 | tf_op jit(solution)/shard_map/ppermute | solution.py:116
  36.9 17.7 %collective-permute-start.4 = (bf16[640,512]{1,0:T(8,128)(2,1)S(1)}, bf16[640,512]{1,0:T(8,128)(2,1)S(1)}, u32[]{:S(2)}, u32[]{:S(2)}) collective-permute-start(bf16[640,512]{1,0:T(8,128)(2,1)S(1)} %collective-permute-done.3.refs_2_), channel_id=1, source_target_pairs={{0,2},{2,0},{1,3},{3,1},{4,6},{6,4},{5,7},{7,5},{8,10},{10,8},{9,1... | collective-permute-start | bytes 1966088 | tf_op jit(solution)/shard_map/ppermute | solution.py:116
  38.9 28.2 %collective-permute-start.7 = (bf16[640,512]{1,0:T(8,128)(2,1)S(1)}, bf16[640,512]{1,0:T(8,128)(2,1)S(1)}, u32[]{:S(2)}, u32[]{:S(2)}) collective-permute-start(bf16[640,512]{1,0:T(8,128)(2,1)S(1)} %collective-permute-done.5.refs_4_), channel_id=1, source_target_pairs={{0,2},{2,0},{1,3},{3,1},{4,6},{6,4},{5,7},{7,5},{8,10},{10,8},{9,1... | collective-permute-start | bytes 1966088 | tf_op jit(solution)/shard_map/ppermute | solution.py:116
  44.1 24.4 %collective-permute-start.6 = (bf16[640,512]{1,0:T(8,128)(2,1)S(1)}, bf16[640,512]{1,0:T(8,128)(2,1)S(1)}, u32[]{:S(2)}, u32[]{:S(2)}) collective-permute-start(bf16[640,512]{1,0:T(8,128)(2,1)S(1)} %collective-permute-done.5.refs_4_), channel_id=1, source_target_pairs={{0,4},{4,0},{8,12},{12,8},{1,5},{5,1},{9,13},{13,9},{2,6},{6,2},{1... | collective-permute-start | bytes 1966088 | tf_op jit(solution)/shard_map/ppermute | solution.py:116
  45.9 22.6 %collective-permute-start.9 = (bf16[336,512]{1,0:T(8,128)(2,1)S(1)}, bf16[336,512]{1,0:T(8,128)(2,1)S(1)}, u32[]{:S(2)}, u32[]{:S(2)}) collective-permute-start(bf16[336,512]{1,0:T(8,128)(2,1)S(1)} %get-tuple-element.43), channel_id=1, source_target_pairs={{0,8},{4,12},{8,0},{12,4},{1,9},{5,13},{9,1},{13,5},{2,10},{6,14},... | collective-permute-start | bytes 1032200 | tf_op jit(solution)/shard_map/ppermute | solution.py:116
  54.5 14.0 %collective-permute-start.8 = (bf16[336,512]{1,0:T(8,128)(2,1)S(1)}, bf16[336,512]{1,0:T(8,128)(2,1)S(1)}, u32[]{:S(2)}, u32[]{:S(2)}) collective-permute-start(bf16[336,512]{1,0:T(8,128)(2,1)S(1)} %collective-permute-done.1.refs_9_), channel_id=1, source_target_pairs={{0,16},{16,0},{1,17},{17,1},{2,18},{18,2},{3,19},{19,3},{4,20},{20... | collective-permute-start | bytes 1032200 | tf_op jit(solution)/shard_map/ppermute | solution.py:116
  56.4 21.1 %collective-permute-start.11 = (bf16[336,512]{1,0:T(8,128)(2,1)S(1)}, bf16[336,512]{1,0:T(8,128)(2,1)S(1)}, u32[]{:S(2)}, u32[]{:S(2)}) collective-permute-start(bf16[336,512]{1,0:T(8,128)(2,1)S(1)} %get-tuple-element.51), channel_id=1, source_target_pairs={{0,12},{4,8},{8,4},{12,0},{1,13},{5,9},{9,5},{13,1},{2,14},{6,10},... | collective-permute-start | bytes 1032200 | tf_op jit(solution)/shard_map/ppermute | solution.py:116
  68.5 9.0 %collective-permute-start.12 = (bf16[336,512]{1,0:T(8,128)(2,1)S(1)}, bf16[336,512]{1,0:T(8,128)(2,1)S(1)}, u32[]{:S(2)}, u32[]{:S(2)}) collective-permute-start(bf16[336,512]{1,0:T(8,128)(2,1)S(1)} %collective-permute-done.9.refs_11_), channel_id=1, source_target_pairs={{0,16},{16,0},{1,17},{17,1},{2,18},{18,2},{3,19},{19,3},{4,20},{20... | collective-permute-start | bytes 1032200 | tf_op jit(solution)/shard_map/ppermute | solution.py:116
  70.0 14.6 %collective-permute-start.10 = (bf16[640,512]{1,0:T(8,128)(2,1)S(1)}, bf16[640,512]{1,0:T(8,128)(2,1)S(1)}, u32[]{:S(2)}, u32[]{:S(2)}) collective-permute-start(bf16[640,512]{1,0:T(8,128)(2,1)S(1)} %collective-permute-done.6.refs_6_), channel_id=1, source_target_pairs={{0,2},{2,0},{1,3},{3,1},{4,6},{6,4},{5,7},{7,5},{8,10},{10,8},{9,1... | collective-permute-start | bytes 1966088 | tf_op jit(solution)/shard_map/ppermute | solution.py:116
  77.5 8.7 %collective-permute-start.13 = (bf16[336,512]{1,0:T(8,128)(2,1)S(1)}, bf16[336,512]{1,0:T(8,128)(2,1)S(1)}, u32[]{:S(2)}, u32[]{:S(2)}) collective-permute-start(bf16[336,512]{1,0:T(8,128)(2,1)S(1)} %collective-permute-done.11.refs_13_), channel_id=1, source_target_pairs={{0,16},{16,0},{1,17},{17,1},{2,18},{18,2},{3,19},{19,3},{4,20},{20... | collective-permute-start | bytes 1032200 | tf_op jit(solution)/shard_map/ppermute | solution.py:116
  79.1 12.3 %collective-permute-start.14 = (bf16[256,512]{1,0:T(8,128)(2,1)S(1)}, bf16[256,512]{1,0:T(8,128)(2,1)S(1)}, u32[]{:S(2)}, u32[]{:S(2)}) collective-permute-start(bf16[256,512]{1,0:T(8,128)(2,1)S(1)} %copy-done.8), channel_id=1, source_target_pairs={{0,8},{4,12},{8,0},{12,4},{1,9},{5,13},{9,1},{13,5},{2,10},{6,14},... | collective-permute-start | bytes 786440 | tf_op jit(solution)/shard_map/ppermute | solution.py:116
  81.7 9.6 %collective-permute-start.15 = (bf16[256,512]{1,0:T(8,128)(2,1)S(1)}, bf16[256,512]{1,0:T(8,128)(2,1)S(1)}, u32[]{:S(2)}, u32[]{:S(2)}) collective-permute-start(bf16[256,512]{1,0:T(8,128)(2,1)S(1)} %copy-done.8), channel_id=1, source_target_pairs={{0,4},{4,0},{8,12},{12,8},{1,5},{5,1},{9,13},{13,9},{2,6},{6,2},{1... | collective-permute-start | bytes 786440 | tf_op jit(solution)/shard_map/ppermute | solution.py:116
  91.3 3.2 %collective-permute-start.17 = (f32[1280,256]{1,0:T(8,128)}, f32[1280,256]{1,0:T(8,128)S(1)}, u32[]{:S(2)}, u32[]{:S(2)}) collective-permute-start(f32[1280,256]{1,0:T(8,128)} %get-tuple-element.60), channel_id=1, source_target_pairs={{0,1},{1,0},{2,3},{3,2},{4,5},{5,4},{6,7},{7,6},{8,9},{9,8},{10,11... | collective-permute-start | bytes 3932168 | tf_op jit(solution)/shard_map/ppermute | solution.py:116
  91.5 8.7 %collective-permute-start.16 = (bf16[256,512]{1,0:T(8,128)(2,1)S(1)}, bf16[256,512]{1,0:T(8,128)(2,1)S(1)}, u32[]{:S(2)}, u32[]{:S(2)}) collective-permute-start(bf16[256,512]{1,0:T(8,128)(2,1)S(1)} %collective-permute-done.14.refs_8_), channel_id=1, source_target_pairs={{0,4},{4,0},{8,12},{12,8},{1,5},{5,1},{9,13},{13,9},{2,6},{6,2},{1... | collective-permute-start | bytes 786440 | tf_op jit(solution)/shard_map/ppermute | solution.py:116
  92.1 11.6 %collective-permute-start.21 = (bf16[256,512]{1,0:T(8,128)(2,1)S(1)}, bf16[256,512]{1,0:T(8,128)(2,1)S(1)}, u32[]{:S(2)}, u32[]{:S(2)}) collective-permute-start(bf16[256,512]{1,0:T(8,128)(2,1)S(1)} %collective-permute-done.15.refs_6_), channel_id=1, source_target_pairs={{0,16},{16,0},{1,17},{17,1},{2,18},{18,2},{3,19},{19,3},{4,20},{20... | collective-permute-start | bytes 786440 | tf_op jit(solution)/shard_map/ppermute | solution.py:116
  93.4 13.4 %collective-permute-start.22 = (bf16[256,512]{1,0:T(8,128)(2,1)S(1)}, bf16[256,512]{1,0:T(8,128)(2,1)S(1)}, u32[]{:S(2)}, u32[]{:S(2)}) collective-permute-start(bf16[256,512]{1,0:T(8,128)(2,1)S(1)} %collective-permute-done.14.refs_8_), channel_id=1, source_target_pairs={{0,16},{16,0},{1,17},{17,1},{2,18},{18,2},{3,19},{19,3},{4,20},{20... | collective-permute-start | bytes 786440 | tf_op jit(solution)/shard_map/ppermute | solution.py:116
  94.6 17.2 %copy-start.2 = (bf16[256,2048]{1,0:T(8,128)(2,1)S(1)}, bf16[256,2048]{1,0:T(8,128)(2,1)}, u32[]{:S(2)}) copy-start(bf16[256,2048]{1,0:T(8,128)(2,1)} %refs_4_.3) | copy-start | bytes 3145732
  94.6 17.2 %copy-start.4 = (bf16[512,512]{1,0:T(8,128)(2,1)S(1)}, bf16[512,512]{1,0:T(8,128)(2,1)}, u32[]{:S(2)}) copy-start(bf16[512,512]{1,0:T(8,128)(2,1)} %refs_5_.3) | copy-start | bytes 1572868
  100.2 11.6 %collective-permute-start.23 = (bf16[256,512]{1,0:T(8,128)(2,1)S(1)}, bf16[256,512]{1,0:T(8,128)(2,1)S(1)}, u32[]{:S(2)}, u32[]{:S(2)}) collective-permute-start(bf16[256,512]{1,0:T(8,128)(2,1)S(1)} %collective-permute-done.16.refs_10_), channel_id=1, source_target_pairs={{0,16},{16,0},{1,17},{17,1},{2,18},{18,2},{3,19},{19,3},{4,20},{20... | collective-permute-start | bytes 786440 | tf_op jit(solution)/shard_map/ppermute | solution.py:116
  100.7 6.2 %collective-permute-start.18 = (bf16[256,128]{1,0:T(8,128)(2,1)S(1)}, bf16[256,128]{1,0:T(8,128)(2,1)S(1)}, u32[]{:S(2)}, u32[]{:S(2)}) collective-permute-start(bf16[256,128]{1,0:T(8,128)(2,1)S(1)} %get-tuple-element.63), channel_id=1, source_target_pairs={{0,4},{4,0},{8,12},{12,8},{1,5},{5,1},{9,13},{13,9},{2,6},{6,2},{1... | collective-permute-start | bytes 196616 | tf_op jit(solution)/shard_map/ppermute | solution.py:116
  101.9 6.9 %collective-permute-start.19 = (bf16[256,128]{1,0:T(8,128)(2,1)S(1)}, bf16[256,128]{1,0:T(8,128)(2,1)S(1)}, u32[]{:S(2)}, u32[]{:S(2)}) collective-permute-start(bf16[256,128]{1,0:T(8,128)(2,1)S(1)} %get-tuple-element.64), channel_id=1, source_target_pairs={{0,8},{4,12},{8,0},{12,4},{1,9},{5,13},{9,1},{13,5},{2,10},{6,14},... | collective-permute-start | bytes 196616 | tf_op jit(solution)/shard_map/ppermute | solution.py:116
  103.7 13.3 %copy-start.7 = (s32[8]{0:T(128)S(1)}, s32[8]{0:T(128)}, u32[]{:S(2)}) copy-start(s32[8]{0:T(128)} %refs_0_.1) | copy-start | bytes 100
  103.7 6.2 %collective-permute-start.20 = (bf16[256,128]{1,0:T(8,128)(2,1)S(1)}, bf16[256,128]{1,0:T(8,128)(2,1)S(1)}, u32[]{:S(2)}, u32[]{:S(2)}) collective-permute-start(bf16[256,128]{1,0:T(8,128)(2,1)S(1)} %get-tuple-element.65), channel_id=1, source_target_pairs={{0,12},{4,8},{8,4},{12,0},{1,13},{5,9},{9,5},{13,1},{2,14},{6,10},... | collective-permute-start | bytes 196616 | tf_op jit(solution)/shard_map/ppermute | solution.py:116
  111.8 5.2 %copy-start = (bf16[3,192,2048]{2,1,0:T(8,128)(2,1)S(1)}, bf16[3,192,2048]{2,1,0:T(8,128)(2,1)}, u32[]{:S(2)}) copy-start(bf16[3,192,2048]{2,1,0:T(8,128)(2,1)} %refs_1_.2) | copy-start | bytes 7077892
  113.4 2.0 %collective-permute-start.24 = (bf16[2,256,512]{2,1,0:T(8,128)(2,1)S(1)}, bf16[2,256,512]{2,1,0:T(8,128)(2,1)S(1)}, u32[]{:S(2)}, u32[]{:S(2)}) collective-permute-start(bf16[2,256,512]{2,1,0:T(8,128)(2,1)S(1)} %get-tuple-element.69), channel_id=1, source_target_pairs={{0,1},{1,0},{2,3},{3,2},{4,5},{5,4},{6,7},{7,6},{8,9},{9,8},{10,11... | collective-permute-start | bytes 1572872 | tf_op jit(solution)/shard_map/ppermute | solution.py:116
  115.5 8.4 %collective-permute-start.25 = (bf16[256,512]{1,0:T(8,128)(2,1)S(1)}, bf16[256,512]{1,0:T(8,128)(2,1)S(1)}, u32[]{:S(2)}, u32[]{:S(2)}) collective-permute-start(bf16[256,512]{1,0:T(8,128)(2,1)S(1)} %fusion.1), channel_id=1, source_target_pairs={{0,2},{2,0},{1,3},{3,1},{4,6},{6,4},{5,7},{7,5},{8,10},{10,8},{9,1... | collective-permute-start | bytes 786440 | tf_op jit(solution)/shard_map/ppermute | solution.py:116

commit v13 on v12

--- a/solution.py
+++ b/solution.py
@@ -478,16 +478,13 @@
     near_align = pieces[0][rows:, :audio_rows].astype(jnp.float32)
     tokens[2], near_align = lax.optimization_barrier((tokens[2], near_align))
     tokens.append(swap(tokens[2], "seq", 1))
-    pieces[0], across[0], across[1] = lax.optimization_barrier(
-        (pieces[0], across[0], across[1])
-    )
     rest = [swap(pieces[0], "grp", 1)]
-    tokens[3], across[2], rest[0], pieces[1] = lax.optimization_barrier(
-        (tokens[3], across[2], rest[0], pieces[1])
-    )
+    pieces[1], across[0], across[1], rest[0] = lax.optimization_barrier(
+        (pieces[1], across[0], across[1], rest[0])
+    )
+    rest.append(swap(pieces[1], "grp", 1))
+    tokens[3], across[2], rest[1] = lax.optimization_barrier((tokens[3], across[2], rest[1]))
     across.append(swap(tokens[3], "mem", 1))
-    rest.append(swap(pieces[1], "grp", 1))
-    pieces[2], rest[1] = lax.optimization_barrier((pieces[2], rest[1]))
     rest.append(swap(pieces[2], "grp", 1))
 
     out_half, tokens[3] = lax.optimization_barrier((out_half, tokens[3]))

time: 125 us -> 130 us (1.040)
  waiting for transfers between devices: 71.8 us -> 82.9 us
  starting transfers between devices: 37.4 us -> 31.2 us
    ppermute x26, waiting for transfers between devices: 71.8 us -> 82.9 us  [swap(): return lax.ppermute(value, axis, [(i, i ^ bit) for i in range(size)])]
    ppermute x26, starting transfers between devices: 37.4 us -> 31.2 us  [swap(): return lax.ppermute(value, axis, [(i, i ^ bit) for i in range(size)])]
  transfers between devices with their start and end apart: 26 -> 26, of which waited for: 18 -> 18; matrix products, arithmetic and copies ran while one was open for 0% -> 0% of each run, Pallas kernels for 7% -> 6%
where the time goes in v13:
time: 130 us; the launch traced here: 129 us
  waiting for transfers between devices  82.9 us (64%)
  starting transfers between devices  31.2 us (24%)
  Pallas kernels  13.2 us (10%)
    ppermute x26, waiting for transfers between devices, swap(): return lax.ppermute(value, axis, [(i, i ^ bit) for i in range(size)])  82.9 us
    ppermute x26, starting transfers between devices, swap(): return lax.ppermute(value, axis, [(i, i ^ bit) for i in range(size)])  31.2 us
    pallas_call x5, Pallas kernels, kernel_call(): pl.pallas_call(whole, out_shape=outs, in_specs=spots + [ANY] * len(after)...  11.3 us
  transfers between devices with their start and end apart: 26, of which 18 were waited for; matrix products, arithmetic and copies ran while one was open for 0% of the time, Pallas kernels for 6%

profile of v13, /device:TPU:0, one launch (start us, length us, event | category | flops | bytes accessed | tf_op | source)
XLA Modules:
  0.0 129.4 jit_solution(7231673930084146348)
XLA Ops:
  0.7 3.3 %shard_map.87 = (bf16[640,512]{1,0:T(8,128)(2,1)}, bf16[640,1024]{1,0:T(8,128)(2,1)}, bf16[256,512]{1,0:T(8,128)(2,1)}) custom-call(s32[8]{0:T(128)} %refs_0_.1, bf16[3,192,2048]{2,1,0:T(8,128)(2,1)} %refs_1_.2, bf16[256,2048]{1,0:T(8,128)(2,1)} %refs_4_.3, bf16[1024,1024]{1,0:T(8,128)(2,1)} %refs_1_.3, bf16[512,512]{1,0:T(8,128)(2,1)} %refs_2_.3, ...), custom_call_target="tpu_custom_call" | custom-call | tf_op jit(solution)/shard_map/pallas_call | solution.py:130
  4.0 0.5 collective-permute-start
  4.5 2.6 %collective-permute-start.3 = (bf16[640,512]{1,0:T(8,128)(2,1)}, bf16[640,512]{1,0:T(8,128)(2,1)S(1)}, u32[]{:S(2)}, u32[]{:S(2)}) collective-permute-start(bf16[640,512]{1,0:T(8,128)(2,1)} %get-tuple-element.34.refs_0_), channel_id=1, source_target_pairs={{0,4},{4,0},{8,12},{12,8},{1,5},{5,1},{9,13},{13,9},{2,6},{6,2},{1... | collective-permute-start | bytes 1966088 | tf_op jit(solution)/shard_map/ppermute | solution.py:116
  7.2 2.6 %collective-permute-start.7 = (bf16[640,512]{1,0:T(8,128)(2,1)}, bf16[640,512]{1,0:T(8,128)(2,1)S(1)}, u32[]{:S(2)}, u32[]{:S(2)}) collective-permute-start(bf16[640,512]{1,0:T(8,128)(2,1)} %get-tuple-element.34.refs_0_), channel_id=1, source_target_pairs={{0,8},{4,12},{8,0},{12,4},{1,9},{5,13},{9,1},{13,5},{2,10},{6,14},... | collective-permute-start | bytes 1966088 | tf_op jit(solution)/shard_map/ppermute | solution.py:116
  9.8 1.5 %collective-permute-start.2 = (bf16[640,512]{1,0:T(8,128)(2,1)}, bf16[640,512]{1,0:T(8,128)(2,1)S(1)}, u32[]{:S(2)}, u32[]{:S(2)}) collective-permute-start(bf16[640,512]{1,0:T(8,128)(2,1)} %get-tuple-element.34.refs_0_), channel_id=1, source_target_pairs={{0,2},{2,0},{1,3},{3,1},{4,6},{6,4},{5,7},{7,5},{8,10},{10,8},{9,1... | collective-permute-start | bytes 1966088 | tf_op jit(solution)/shard_map/ppermute | solution.py:116
  11.3 0.3 shard_map.88
  11.6 0.5 collective-permute-start.5
  12.1 24.8 %collective-permute-done.3.refs_2_ = bf16[640,512]{1,0:T(8,128)(2,1)S(1)} collective-permute-done((bf16[640,512]{1,0:T(8,128)(2,1)}, bf16[640,512]{1,0:T(8,128)(2,1)S(1)}, u32[]{:S(2)}, u32[]{:S(2)}) %collective-permute-start.3) | collective-permute-done | bytes 655392 | tf_op jit(solution)/shard_map/ppermute | solution.py:116
  36.9 1.9 %collective-permute-start.4 = (bf16[640,512]{1,0:T(8,128)(2,1)S(1)}, bf16[640,512]{1,0:T(8,128)(2,1)S(1)}, u32[]{:S(2)}, u32[]{:S(2)}) collective-permute-start(bf16[640,512]{1,0:T(8,128)(2,1)S(1)} %collective-permute-done.3.refs_2_), channel_id=1, source_target_pairs={{0,2},{2,0},{1,3},{3,1},{4,6},{6,4},{5,7},{7,5},{8,10},{10,8},{9,1... | collective-permute-start | bytes 1966088 | tf_op jit(solution)/shard_map/ppermute | solution.py:116
  38.7 0.2 collective-permute-done.7.refs_4_
  38.9 1.5 %collective-permute-start.9 = (bf16[640,512]{1,0:T(8,128)(2,1)S(1)}, bf16[640,512]{1,0:T(8,128)(2,1)S(1)}, u32[]{:S(2)}, u32[]{:S(2)}) collective-permute-start(bf16[640,512]{1,0:T(8,128)(2,1)S(1)} %collective-permute-done.7.refs_4_), channel_id=1, source_target_pairs={{0,2},{2,0},{1,3},{3,1},{4,6},{6,4},{5,7},{7,5},{8,10},{10,8},{9,1... | collective-permute-start | bytes 1966088 | tf_op jit(solution)/shard_map/ppermute | solution.py:116
  40.4 1.0 collective-permute-start.1
  41.4 7.7 %collective-permute-done.5.refs_9_ = bf16[336,512]{1,0:T(8,128)(2,1)S(1)} collective-permute-done((bf16[336,512]{1,0:T(8,128)(2,1)S(1)}, bf16[336,512]{1,0:T(8,128)(2,1)S(1)}, u32[]{:S(2)}, u32[]{:S(2)}) %collective-permute-start.5) | collective-permute-done | bytes 344096 | tf_op jit(solution)/shard_map/ppermute | solution.py:116
  49.1 1.7 %collective-permute-start.6 = (bf16[336,512]{1,0:T(8,128)(2,1)S(1)}, bf16[336,512]{1,0:T(8,128)(2,1)S(1)}, u32[]{:S(2)}, u32[]{:S(2)}) collective-permute-start(bf16[336,512]{1,0:T(8,128)(2,1)S(1)} %collective-permute-done.5.refs_9_), channel_id=1, source_target_pairs={{0,16},{16,0},{1,17},{17,1},{2,18},{18,2},{3,19},{19,3},{4,20},{20... | collective-permute-start | bytes 1032200 | tf_op jit(solution)/shard_map/ppermute | solution.py:116
  50.9 3.7 %collective-permute-done.4.refs_3_ = bf16[640,512]{1,0:T(8,128)(2,1)S(1)} collective-permute-done((bf16[640,512]{1,0:T(8,128)(2,1)S(1)}, bf16[640,512]{1,0:T(8,128)(2,1)S(1)}, u32[]{:S(2)}, u32[]{:S(2)}) %collective-permute-start.4) | collective-permute-done | bytes 655392 | tf_op jit(solution)/shard_map/ppermute | solution.py:116
  54.5 1.8 %collective-permute-done.1.refs_11_ = bf16[336,512]{1,0:T(8,128)(2,1)S(1)} collective-permute-done((bf16[336,512]{1,0:T(8,128)(2,1)S(1)}, bf16[336,512]{1,0:T(8,128)(2,1)S(1)}, u32[]{:S(2)}, u32[]{:S(2)}) %collective-permute-start.1) | collective-permute-done | bytes 344096 | tf_op jit(solution)/shard_map/ppermute | solution.py:116
  56.3 2.6 %collective-permute-done.6.refs_10_ = bf16[336,512]{1,0:T(8,128)(2,1)S(1)} collective-permute-done((bf16[336,512]{1,0:T(8,128)(2,1)S(1)}, bf16[336,512]{1,0:T(8,128)(2,1)S(1)}, u32[]{:S(2)}, u32[]{:S(2)}) %collective-permute-start.6) | collective-permute-done | bytes 344096 | tf_op jit(solution)/shard_map/ppermute | solution.py:116
  58.9 1.5 %collective-permute-start.10 = (bf16[336,512]{1,0:T(8,128)(2,1)S(1)}, bf16[336,512]{1,0:T(8,128)(2,1)S(1)}, u32[]{:S(2)}, u32[]{:S(2)}) collective-permute-start(bf16[336,512]{1,0:T(8,128)(2,1)S(1)} %collective-permute-done.1.refs_11_), channel_id=1, source_target_pairs={{0,16},{16,0},{1,17},{17,1},{2,18},{18,2},{3,19},{19,3},{4,20},{20... | collective-permute-start | bytes 1032200 | tf_op jit(solution)/shard_map/ppermute | solution.py:116
  60.5 1.7 %collective-permute-start.12 = (bf16[336,512]{1,0:T(8,128)(2,1)S(1)}, bf16[336,512]{1,0:T(8,128)(2,1)S(1)}, u32[]{:S(2)}, u32[]{:S(2)}) collective-permute-start(bf16[336,512]{1,0:T(8,128)(2,1)S(1)} %get-tuple-element.49), channel_id=1, source_target_pairs={{0,12},{4,8},{8,4},{12,0},{1,13},{5,9},{9,5},{13,1},{2,14},{6,10},... | collective-permute-start | bytes 1032200 | tf_op jit(solution)/shard_map/ppermute | solution.py:116
  62.1 5.0 %collective-permute-done.9.refs_5_ = bf16[640,512]{1,0:T(8,128)(2,1)S(1)} collective-permute-done((bf16[640,512]{1,0:T(8,128)(2,1)S(1)}, bf16[640,512]{1,0:T(8,128)(2,1)S(1)}, u32[]{:S(2)}, u32[]{:S(2)}) %collective-permute-start.9) | collective-permute-done | bytes 655392 | tf_op jit(solution)/shard_map/ppermute | solution.py:116
  67.2 9.5 %collective-permute-done.8.refs_6_ = bf16[640,512]{1,0:T(8,128)(2,1)S(1)} collective-permute-done((bf16[640,512]{1,0:T(8,128)(2,1)S(1)}, bf16[640,512]{1,0:T(8,128)(2,1)S(1)}, u32[]{:S(2)}, u32[]{:S(2)}) %collective-permute-start.8) | collective-permute-done | bytes 655392 | tf_op jit(solution)/shard_map/ppermute | solution.py:116
  76.6 1.5 %collective-permute-start.11 = (bf16[640,512]{1,0:T(8,128)(2,1)S(1)}, bf16[640,512]{1,0:T(8,128)(2,1)S(1)}, u32[]{:S(2)}, u32[]{:S(2)}) collective-permute-start(bf16[640,512]{1,0:T(8,128)(2,1)S(1)} %collective-permute-done.8.refs_6_), channel_id=1, source_target_pairs={{0,2},{2,0},{1,3},{3,1},{4,6},{6,4},{5,7},{7,5},{8,10},{10,8},{9,1... | collective-permute-start | bytes 1966088 | tf_op jit(solution)/shard_map/ppermute | solution.py:116
  78.1 0.5 collective-permute-start.13
  78.6 1.7 %collective-permute-start.14 = (bf16[256,512]{1,0:T(8,128)(2,1)S(1)}, bf16[256,512]{1,0:T(8,128)(2,1)S(1)}, u32[]{:S(2)}, u32[]{:S(2)}) collective-permute-start(bf16[256,512]{1,0:T(8,128)(2,1)S(1)} %copy-done.8), channel_id=1, source_target_pairs={{0,8},{4,12},{8,0},{12,4},{1,9},{5,13},{9,1},{13,5},{2,10},{6,14},... | collective-permute-start | bytes 786440 | tf_op jit(solution)/shard_map/ppermute | solution.py:116
  80.3 2.5 %collective-permute-start.15 = (bf16[256,512]{1,0:T(8,128)(2,1)S(1)}, bf16[256,512]{1,0:T(8,128)(2,1)S(1)}, u32[]{:S(2)}, u32[]{:S(2)}) collective-permute-start(bf16[256,512]{1,0:T(8,128)(2,1)S(1)} %copy-done.8), channel_id=1, source_target_pairs={{0,4},{4,0},{8,12},{12,8},{1,5},{5,1},{9,13},{13,9},{2,6},{6,2},{1... | collective-permute-start | bytes 786440 | tf_op jit(solution)/shard_map/ppermute | solution.py:116
  82.8 3.9 %collective-permute-done.13.refs_14_ = bf16[336,512]{1,0:T(8,128)(2,1)S(1)} collective-permute-done((bf16[336,512]{1,0:T(8,128)(2,1)S(1)}, bf16[336,512]{1,0:T(8,128)(2,1)S(1)}, u32[]{:S(2)}, u32[]{:S(2)}) %collective-permute-start.13) | collective-permute-done | bytes 344096 | tf_op jit(solution)/shard_map/ppermute | solution.py:116
  86.7 5.5 %collective-permute-done.11.refs_7_ = bf16[640,512]{1,0:T(8,128)(2,1)S(1)} collective-permute-done((bf16[640,512]{1,0:T(8,128)(2,1)S(1)}, bf16[640,512]{1,0:T(8,128)(2,1)S(1)}, u32[]{:S(2)}, u32[]{:S(2)}) %collective-permute-start.11) | collective-permute-done | bytes 655392 | tf_op jit(solution)/shard_map/ppermute | solution.py:116
  92.2 3.9 %shard_map.89 = (bf16[4,16,256]{2,1,0:T(8,128)(2,1)S(1)}, f32[1280,256]{1,0:T(8,128)}, f32[1280,256]{1,0:T(8,128)S(1)}) custom-call(bf16[640,512]{1,0:T(8,128)(2,1)S(1)} %copy-done.5, bf16[640,512]{1,0:T(8,128)(2,1)S(1)} %collective-permute-done.2.refs_1_, bf16[640,512]{1,0:T(8,128)(2,1)S(1)} %collective-permute-done.3.refs_2_, ...), custom_call_target="tpu_custom_call" | custom-call | tf_op jit(solution)/shard_map/pallas_call | solution.py:130
  96.3 0.1 fusion.3
  96.4 0.1 div.18
  96.4 0.1 reshape.116
  96.5 2.1 %collective-permute-start.22 = (bf16[256,512]{1,0:T(8,128)(2,1)S(1)}, bf16[256,512]{1,0:T(8,128)(2,1)S(1)}, u32[]{:S(2)}, u32[]{:S(2)}) collective-permute-start(bf16[256,512]{1,0:T(8,128)(2,1)S(1)} %collective-permute-done.14.refs_8_), channel_id=1, source_target_pairs={{0,16},{16,0},{1,17},{17,1},{2,18},{18,2},{3,19},{19,3},{4,20},{20... | collective-permute-start | bytes 786440 | tf_op jit(solution)/shard_map/ppermute | solution.py:116
  98.6 0.7 collective-permute-done.17.refs_3_
  99.3 2.2 %shard_map.90 = (bf16[256,128]{1,0:T(8,128)(2,1)S(1)}, bf16[256,128]{1,0:T(8,128)(2,1)S(1)}, bf16[256,128]{1,0:T(8,128)(2,1)S(1)}, bf16[256,128]{1,0:T(8,128)(2,1)S(1)}) custom-call(f32[1,768]{1,0:T(1,128)S(1)} %fusion.4.refs_0_, bf16[4,16,256]{2,1,0:T(8,128)(2,1)S(1)} %get-tuple-element.54.refs_1_, f32[1280,256]{1,0:T(8,128)S(1)} %get-tuple-element.55.refs_2_, ...), custom_call_target="tpu_custom_call" | custom-call | tf_op jit(solution)/shard_map/pallas_call | solution.py:130
  101.6 3.4 %collective-permute-done.16.refs_10_ = bf16[256,512]{1,0:T(8,128)(2,1)S(1)} collective-permute-done((bf16[256,512]{1,0:T(8,128)(2,1)S(1)}, bf16[256,512]{1,0:T(8,128)(2,1)S(1)}, u32[]{:S(2)}, u32[]{:S(2)}) %collective-permute-start.16) | collective-permute-done | bytes 262176 | tf_op jit(solution)/shard_map/ppermute | solution.py:116
  105.0 0.3 collective-permute-start.18
  105.3 3.9 %collective-permute-start.19 = (bf16[256,128]{1,0:T(8,128)(2,1)S(1)}, bf16[256,128]{1,0:T(8,128)(2,1)S(1)}, u32[]{:S(2)}, u32[]{:S(2)}) collective-permute-start(bf16[256,128]{1,0:T(8,128)(2,1)S(1)} %get-tuple-element.60), channel_id=1, source_target_pairs={{0,8},{4,12},{8,0},{12,4},{1,9},{5,13},{9,1},{13,5},{2,10},{6,14},... | collective-permute-start | bytes 196616 | tf_op jit(solution)/shard_map/ppermute | solution.py:116
  109.2 0.2 collective-permute-start.20
  109.4 1.9 %collective-permute-done.22.refs_9_ = bf16[256,512]{1,0:T(8,128)(2,1)S(1)} collective-permute-done((bf16[256,512]{1,0:T(8,128)(2,1)S(1)}, bf16[256,512]{1,0:T(8,128)(2,1)S(1)}, u32[]{:S(2)}, u32[]{:S(2)}) %collective-permute-start.22) | collective-permute-done | bytes 262176 | tf_op jit(solution)/shard_map/ppermute | solution.py:116
  111.2 2.4 %collective-permute-done.19.refs_2_ = bf16[256,128]{1,0:T(8,128)(2,1)S(1)} collective-permute-done((bf16[256,128]{1,0:T(8,128)(2,1)S(1)}, bf16[256,128]{1,0:T(8,128)(2,1)S(1)}, u32[]{:S(2)}, u32[]{:S(2)}) %collective-permute-start.19) | collective-permute-done | bytes 65568 | tf_op jit(solution)/shard_map/ppermute | solution.py:116
  113.7 1.6 %collective-permute-done.20.refs_3_ = bf16[256,128]{1,0:T(8,128)(2,1)S(1)} collective-permute-done((bf16[256,128]{1,0:T(8,128)(2,1)S(1)}, bf16[256,128]{1,0:T(8,128)(2,1)S(1)}, u32[]{:S(2)}, u32[]{:S(2)}) %collective-permute-start.20) | collective-permute-done | bytes 65568 | tf_op jit(solution)/shard_map/ppermute | solution.py:116
  115.2 1.2 collective-permute-done.23.refs_11_
  116.5 1.6 %shard_map.91 = (bf16[2,256,512]{2,1,0:T(8,128)(2,1)S(1)}, f32[2,256,512]{2,1,0:T(8,128)S(1)}) custom-call(bf16[256,128]{1,0:T(8,128)(2,1)S(1)} %get-tuple-element.58.refs_0_, bf16[256,128]{1,0:T(8,128)(2,1)S(1)} %collective-permute-done.18.refs_1_, bf16[256,128]{1,0:T(8,128)(2,1)S(1)} %collective-permute-done.19.refs_2_, ...), custom_call_target="tpu_custom_call" | custom-call | tf_op jit(solution)/shard_map/pallas_call | solution.py:130
  118.2 1.9 %collective-permute-done.24 = bf16[2,256,512]{2,1,0:T(8,128)(2,1)S(1)} collective-permute-done((bf16[2,256,512]{2,1,0:T(8,128)(2,1)S(1)}, bf16[2,256,512]{2,1,0:T(8,128)(2,1)S(1)}, u32[]{:S(2)}, u32[]{:S(2)}) %collective-permute-start.24) | collective-permute-done | bytes 524320 | tf_op jit(solution)/shard_map/ppermute | solution.py:116
  120.2 1.5 %collective-permute-start.25 = (bf16[256,512]{1,0:T(8,128)(2,1)S(1)}, bf16[256,512]{1,0:T(8,128)(2,1)S(1)}, u32[]{:S(2)}, u32[]{:S(2)}) collective-permute-start(bf16[256,512]{1,0:T(8,128)(2,1)S(1)} %fusion.1), channel_id=1, source_target_pairs={{0,2},{2,0},{1,3},{3,1},{4,6},{6,4},{5,7},{7,5},{8,10},{10,8},{9,1... | collective-permute-start | bytes 786440 | tf_op jit(solution)/shard_map/ppermute | solution.py:116
  121.7 1.8 %shard_map.86 = bf16[192,2048]{1,0:T(8,128)(2,1)} custom-call(s32[8]{0:T(128)S(1)} %copy-done.7, bf16[3,192,2048]{2,1,0:T(8,128)(2,1)S(1)} %copy-done), custom_call_target="tpu_custom_call" | custom-call | tf_op jit(solution)/shard_map/pallas_call | solution.py:168
  123.5 5.1 %collective-permute-done.25 = bf16[256,512]{1,0:T(8,128)(2,1)S(1)} collective-permute-done((bf16[256,512]{1,0:T(8,128)(2,1)S(1)}, bf16[256,512]{1,0:T(8,128)(2,1)S(1)}, u32[]{:S(2)}, u32[]{:S(2)}) %collective-permute-start.25) | collective-permute-done | bytes 262176 | tf_op jit(solution)/shard_map/ppermute | solution.py:116
  128.6 0.8 fusion
  (37 shorter events, 0.4 us)
Async XLA Ops:
  0.6 10.6 %copy-start.3 = (bf16[512,512]{1,0:T(8,128)(2,1)S(1)}, bf16[512,512]{1,0:T(8,128)(2,1)}, u32[]{:S(2)}) copy-start(bf16[512,512]{1,0:T(8,128)(2,1)} %refs_2_.3) | copy-start | bytes 1572868
  0.6 10.6 %copy-start.1 = (bf16[1024,1024]{1,0:T(8,128)(2,1)S(1)}, bf16[1024,1024]{1,0:T(8,128)(2,1)}, u32[]{:S(2)}) copy-start(bf16[1024,1024]{1,0:T(8,128)(2,1)} %refs_1_.3) | copy-start | bytes 6291460
  0.7 10.6 %copy-start.6 = (s32[256]{0:T(256)S(1)}, s32[256]{0:T(256)}, u32[]{:S(2)}) copy-start(s32[256]{0:T(256)} %param.9) | copy-start | bytes 3076
  4.0 7.3 %collective-permute-start = (bf16[640,1024]{1,0:T(8,128)(2,1)}, bf16[640,1024]{1,0:T(8,128)(2,1)S(1)}, u32[]{:S(2)}, u32[]{:S(2)}) collective-permute-start(bf16[640,1024]{1,0:T(8,128)(2,1)} %get-tuple-element.35), channel_id=1, source_target_pairs={{0,1},{1,0},{2,3},{3,2},{4,5},{5,4},{6,7},{7,6},{8,9},{9,8},{10,11... | collective-permute-start | bytes 3932168 | tf_op jit(solution)/shard_map/ppermute | solution.py:116
  4.5 32.4 %collective-permute-start.3 = (bf16[640,512]{1,0:T(8,128)(2,1)}, bf16[640,512]{1,0:T(8,128)(2,1)S(1)}, u32[]{:S(2)}, u32[]{:S(2)}) collective-permute-start(bf16[640,512]{1,0:T(8,128)(2,1)} %get-tuple-element.34.refs_0_), channel_id=1, source_target_pairs={{0,4},{4,0},{8,12},{12,8},{1,5},{5,1},{9,13},{13,9},{2,6},{6,2},{1... | collective-permute-start | bytes 1966088 | tf_op jit(solution)/shard_map/ppermute | solution.py:116
  7.2 31.8 %collective-permute-start.7 = (bf16[640,512]{1,0:T(8,128)(2,1)}, bf16[640,512]{1,0:T(8,128)(2,1)S(1)}, u32[]{:S(2)}, u32[]{:S(2)}) collective-permute-start(bf16[640,512]{1,0:T(8,128)(2,1)} %get-tuple-element.34.refs_0_), channel_id=1, source_target_pairs={{0,8},{4,12},{8,0},{12,4},{1,9},{5,13},{9,1},{13,5},{2,10},{6,14},... | collective-permute-start | bytes 1966088 | tf_op jit(solution)/shard_map/ppermute | solution.py:116
  9.8 41.1 %collective-permute-start.2 = (bf16[640,512]{1,0:T(8,128)(2,1)}, bf16[640,512]{1,0:T(8,128)(2,1)S(1)}, u32[]{:S(2)}, u32[]{:S(2)}) collective-permute-start(bf16[640,512]{1,0:T(8,128)(2,1)} %get-tuple-element.34.refs_0_), channel_id=1, source_target_pairs={{0,2},{2,0},{1,3},{3,1},{4,6},{6,4},{5,7},{7,5},{8,10},{10,8},{9,1... | collective-permute-start | bytes 1966088 | tf_op jit(solution)/shard_map/ppermute | solution.py:116
  11.3 67.3 %copy-start.8 = (bf16[256,512]{1,0:T(8,128)(2,1)S(1)}, bf16[256,512]{1,0:T(8,128)(2,1)}, u32[]{:S(2)}) copy-start(bf16[256,512]{1,0:T(8,128)(2,1)} %get-tuple-element.52) | copy-start | bytes 786436
  11.3 80.9 %copy-start.5 = (bf16[640,512]{1,0:T(8,128)(2,1)S(1)}, bf16[640,512]{1,0:T(8,128)(2,1)}, u32[]{:S(2)}) copy-start(bf16[640,512]{1,0:T(8,128)(2,1)} %get-tuple-element.34.refs_0_) | copy-start | bytes 1966084
  11.6 37.6 %collective-permute-start.5 = (bf16[336,512]{1,0:T(8,128)(2,1)S(1)}, bf16[336,512]{1,0:T(8,128)(2,1)S(1)}, u32[]{:S(2)}, u32[]{:S(2)}) collective-permute-start(bf16[336,512]{1,0:T(8,128)(2,1)S(1)} %get-tuple-element.37), channel_id=1, source_target_pairs={{0,4},{4,0},{8,12},{12,8},{1,5},{5,1},{9,13},{13,9},{2,6},{6,2},{1... | collective-permute-start | bytes 1032200 | tf_op jit(solution)/shard_map/ppermute | solution.py:116
  36.9 17.7 %collective-permute-start.4 = (bf16[640,512]{1,0:T(8,128)(2,1)S(1)}, bf16[640,512]{1,0:T(8,128)(2,1)S(1)}, u32[]{:S(2)}, u32[]{:S(2)}) collective-permute-start(bf16[640,512]{1,0:T(8,128)(2,1)S(1)} %collective-permute-done.3.refs_2_), channel_id=1, source_target_pairs={{0,2},{2,0},{1,3},{3,1},{4,6},{6,4},{5,7},{7,5},{8,10},{10,8},{9,1... | collective-permute-start | bytes 1966088 | tf_op jit(solution)/shard_map/ppermute | solution.py:116
  38.9 28.2 %collective-permute-start.9 = (bf16[640,512]{1,0:T(8,128)(2,1)S(1)}, bf16[640,512]{1,0:T(8,128)(2,1)S(1)}, u32[]{:S(2)}, u32[]{:S(2)}) collective-permute-start(bf16[640,512]{1,0:T(8,128)(2,1)S(1)} %collective-permute-done.7.refs_4_), channel_id=1, source_target_pairs={{0,2},{2,0},{1,3},{3,1},{4,6},{6,4},{5,7},{7,5},{8,10},{10,8},{9,1... | collective-permute-start | bytes 1966088 | tf_op jit(solution)/shard_map/ppermute | solution.py:116
  40.4 15.9 %collective-permute-start.1 = (bf16[336,512]{1,0:T(8,128)(2,1)S(1)}, bf16[336,512]{1,0:T(8,128)(2,1)S(1)}, u32[]{:S(2)}, u32[]{:S(2)}) collective-permute-start(bf16[336,512]{1,0:T(8,128)(2,1)S(1)} %get-tuple-element.36), channel_id=1, source_target_pairs={{0,8},{4,12},{8,0},{12,4},{1,9},{5,13},{9,1},{13,5},{2,10},{6,14},... | collective-permute-start | bytes 1032200 | tf_op jit(solution)/shard_map/ppermute | solution.py:116
  49.1 9.8 %collective-permute-start.6 = (bf16[336,512]{1,0:T(8,128)(2,1)S(1)}, bf16[336,512]{1,0:T(8,128)(2,1)S(1)}, u32[]{:S(2)}, u32[]{:S(2)}) collective-permute-start(bf16[336,512]{1,0:T(8,128)(2,1)S(1)} %collective-permute-done.5.refs_9_), channel_id=1, source_target_pairs={{0,16},{16,0},{1,17},{17,1},{2,18},{18,2},{3,19},{19,3},{4,20},{20... | collective-permute-start | bytes 1032200 | tf_op jit(solution)/shard_map/ppermute | solution.py:116
  50.8 25.8 %collective-permute-start.8 = (bf16[640,512]{1,0:T(8,128)(2,1)S(1)}, bf16[640,512]{1,0:T(8,128)(2,1)S(1)}, u32[]{:S(2)}, u32[]{:S(2)}) collective-permute-start(bf16[640,512]{1,0:T(8,128)(2,1)S(1)} %collective-permute-done.7.refs_4_), channel_id=1, source_target_pairs={{0,4},{4,0},{8,12},{12,8},{1,5},{5,1},{9,13},{13,9},{2,6},{6,2},{1... | collective-permute-start | bytes 1966088 | tf_op jit(solution)/shard_map/ppermute | solution.py:116
  58.9 17.7 %collective-permute-start.10 = (bf16[336,512]{1,0:T(8,128)(2,1)S(1)}, bf16[336,512]{1,0:T(8,128)(2,1)S(1)}, u32[]{:S(2)}, u32[]{:S(2)}) collective-permute-start(bf16[336,512]{1,0:T(8,128)(2,1)S(1)} %collective-permute-done.1.refs_11_), channel_id=1, source_target_pairs={{0,16},{16,0},{1,17},{17,1},{2,18},{18,2},{3,19},{19,3},{4,20},{20... | collective-permute-start | bytes 1032200 | tf_op jit(solution)/shard_map/ppermute | solution.py:116
  60.5 17.6 %collective-permute-start.12 = (bf16[336,512]{1,0:T(8,128)(2,1)S(1)}, bf16[336,512]{1,0:T(8,128)(2,1)S(1)}, u32[]{:S(2)}, u32[]{:S(2)}) collective-permute-start(bf16[336,512]{1,0:T(8,128)(2,1)S(1)} %get-tuple-element.49), channel_id=1, source_target_pairs={{0,12},{4,8},{8,4},{12,0},{1,13},{5,9},{9,5},{13,1},{2,14},{6,10},... | collective-permute-start | bytes 1032200 | tf_op jit(solution)/shard_map/ppermute | solution.py:116
  76.6 15.6 %collective-permute-start.11 = (bf16[640,512]{1,0:T(8,128)(2,1)S(1)}, bf16[640,512]{1,0:T(8,128)(2,1)S(1)}, u32[]{:S(2)}, u32[]{:S(2)}) collective-permute-start(bf16[640,512]{1,0:T(8,128)(2,1)S(1)} %collective-permute-done.8.refs_6_), channel_id=1, source_target_pairs={{0,2},{2,0},{1,3},{3,1},{4,6},{6,4},{5,7},{7,5},{8,10},{10,8},{9,1... | collective-permute-start | bytes 1966088 | tf_op jit(solution)/shard_map/ppermute | solution.py:116
  78.1 8.6 %collective-permute-start.13 = (bf16[336,512]{1,0:T(8,128)(2,1)S(1)}, bf16[336,512]{1,0:T(8,128)(2,1)S(1)}, u32[]{:S(2)}, u32[]{:S(2)}) collective-permute-start(bf16[336,512]{1,0:T(8,128)(2,1)S(1)} %collective-permute-done.12.refs_13_), channel_id=1, source_target_pairs={{0,16},{16,0},{1,17},{17,1},{2,18},{18,2},{3,19},{19,3},{4,20},{20... | collective-permute-start | bytes 1032200 | tf_op jit(solution)/shard_map/ppermute | solution.py:116
  78.6 17.5 %collective-permute-start.14 = (bf16[256,512]{1,0:T(8,128)(2,1)S(1)}, bf16[256,512]{1,0:T(8,128)(2,1)S(1)}, u32[]{:S(2)}, u32[]{:S(2)}) collective-permute-start(bf16[256,512]{1,0:T(8,128)(2,1)S(1)} %copy-done.8), channel_id=1, source_target_pairs={{0,8},{4,12},{8,0},{12,4},{1,9},{5,13},{9,1},{13,5},{2,10},{6,14},... | collective-permute-start | bytes 786440 | tf_op jit(solution)/shard_map/ppermute | solution.py:116
  80.3 15.8 %collective-permute-start.15 = (bf16[256,512]{1,0:T(8,128)(2,1)S(1)}, bf16[256,512]{1,0:T(8,128)(2,1)S(1)}, u32[]{:S(2)}, u32[]{:S(2)}) collective-permute-start(bf16[256,512]{1,0:T(8,128)(2,1)S(1)} %copy-done.8), channel_id=1, source_target_pairs={{0,4},{4,0},{8,12},{12,8},{1,5},{5,1},{9,13},{13,9},{2,6},{6,2},{1... | collective-permute-start | bytes 786440 | tf_op jit(solution)/shard_map/ppermute | solution.py:116
  96.1 3.2 %collective-permute-start.17 = (f32[1280,256]{1,0:T(8,128)}, f32[1280,256]{1,0:T(8,128)S(1)}, u32[]{:S(2)}, u32[]{:S(2)}) collective-permute-start(f32[1280,256]{1,0:T(8,128)} %get-tuple-element.56), channel_id=1, source_target_pairs={{0,1},{1,0},{2,3},{3,2},{4,5},{5,4},{6,7},{7,6},{8,9},{9,8},{10,11... | collective-permute-start | bytes 3932168 | tf_op jit(solution)/shard_map/ppermute | solution.py:116
  96.3 8.7 %collective-permute-start.16 = (bf16[256,512]{1,0:T(8,128)(2,1)S(1)}, bf16[256,512]{1,0:T(8,128)(2,1)S(1)}, u32[]{:S(2)}, u32[]{:S(2)}) collective-permute-start(bf16[256,512]{1,0:T(8,128)(2,1)S(1)} %collective-permute-done.14.refs_8_), channel_id=1, source_target_pairs={{0,4},{4,0},{8,12},{12,8},{1,5},{5,1},{9,13},{13,9},{2,6},{6,2},{1... | collective-permute-start | bytes 786440 | tf_op jit(solution)/shard_map/ppermute | solution.py:116
  96.5 12.7 %collective-permute-start.21 = (bf16[256,512]{1,0:T(8,128)(2,1)S(1)}, bf16[256,512]{1,0:T(8,128)(2,1)S(1)}, u32[]{:S(2)}, u32[]{:S(2)}) collective-permute-start(bf16[256,512]{1,0:T(8,128)(2,1)S(1)} %collective-permute-done.15.refs_6_), channel_id=1, source_target_pairs={{0,16},{16,0},{1,17},{17,1},{2,18},{18,2},{3,19},{19,3},{4,20},{20... | collective-permute-start | bytes 786440 | tf_op jit(solution)/shard_map/ppermute | solution.py:116
  96.5 14.7 %collective-permute-start.22 = (bf16[256,512]{1,0:T(8,128)(2,1)S(1)}, bf16[256,512]{1,0:T(8,128)(2,1)S(1)}, u32[]{:S(2)}, u32[]{:S(2)}) collective-permute-start(bf16[256,512]{1,0:T(8,128)(2,1)S(1)} %collective-permute-done.14.refs_8_), channel_id=1, source_target_pairs={{0,16},{16,0},{1,17},{17,1},{2,18},{18,2},{3,19},{19,3},{4,20},{20... | collective-permute-start | bytes 786440 | tf_op jit(solution)/shard_map/ppermute | solution.py:116
  99.3 17.2 %copy-start.2 = (bf16[256,2048]{1,0:T(8,128)(2,1)S(1)}, bf16[256,2048]{1,0:T(8,128)(2,1)}, u32[]{:S(2)}) copy-start(bf16[256,2048]{1,0:T(8,128)(2,1)} %refs_4_.3) | copy-start | bytes 3145732
  99.3 17.2 %copy-start.4 = (bf16[512,512]{1,0:T(8,128)(2,1)S(1)}, bf16[512,512]{1,0:T(8,128)(2,1)}, u32[]{:S(2)}) copy-start(bf16[512,512]{1,0:T(8,128)(2,1)} %refs_5_.3) | copy-start | bytes 1572868
  105.0 11.5 %collective-permute-start.23 = (bf16[256,512]{1,0:T(8,128)(2,1)S(1)}, bf16[256,512]{1,0:T(8,128)(2,1)S(1)}, u32[]{:S(2)}, u32[]{:S(2)}) collective-permute-start(bf16[256,512]{1,0:T(8,128)(2,1)S(1)} %collective-permute-done.16.refs_10_), channel_id=1, source_target_pairs={{0,16},{16,0},{1,17},{17,1},{2,18},{18,2},{3,19},{19,3},{4,20},{20... | collective-permute-start | bytes 786440 | tf_op jit(solution)/shard_map/ppermute | solution.py:116
  105.0 6.3 %collective-permute-start.18 = (bf16[256,128]{1,0:T(8,128)(2,1)S(1)}, bf16[256,128]{1,0:T(8,128)(2,1)S(1)}, u32[]{:S(2)}, u32[]{:S(2)}) collective-permute-start(bf16[256,128]{1,0:T(8,128)(2,1)S(1)} %get-tuple-element.59), channel_id=1, source_target_pairs={{0,4},{4,0},{8,12},{12,8},{1,5},{5,1},{9,13},{13,9},{2,6},{6,2},{1... | collective-permute-start | bytes 196616 | tf_op jit(solution)/shard_map/ppermute | solution.py:116
  105.3 8.4 %collective-permute-start.19 = (bf16[256,128]{1,0:T(8,128)(2,1)S(1)}, bf16[256,128]{1,0:T(8,128)(2,1)S(1)}, u32[]{:S(2)}, u32[]{:S(2)}) collective-permute-start(bf16[256,128]{1,0:T(8,128)(2,1)S(1)} %get-tuple-element.60), channel_id=1, source_target_pairs={{0,8},{4,12},{8,0},{12,4},{1,9},{5,13},{9,1},{13,5},{2,10},{6,14},... | collective-permute-start | bytes 196616 | tf_op jit(solution)/shard_map/ppermute | solution.py:116
  109.2 12.5 %copy-start.7 = (s32[8]{0:T(128)S(1)}, s32[8]{0:T(128)}, u32[]{:S(2)}) copy-start(s32[8]{0:T(128)} %refs_0_.1) | copy-start | bytes 100
  109.2 6.1 %collective-permute-start.20 = (bf16[256,128]{1,0:T(8,128)(2,1)S(1)}, bf16[256,128]{1,0:T(8,128)(2,1)S(1)}, u32[]{:S(2)}, u32[]{:S(2)}) collective-permute-start(bf16[256,128]{1,0:T(8,128)(2,1)S(1)} %get-tuple-element.61), channel_id=1, source_target_pairs={{0,12},{4,8},{8,4},{12,0},{1,13},{5,9},{9,5},{13,1},{2,14},{6,10},... | collective-permute-start | bytes 196616 | tf_op jit(solution)/shard_map/ppermute | solution.py:116
  116.5 5.2 %copy-start = (bf16[3,192,2048]{2,1,0:T(8,128)(2,1)S(1)}, bf16[3,192,2048]{2,1,0:T(8,128)(2,1)}, u32[]{:S(2)}) copy-start(bf16[3,192,2048]{2,1,0:T(8,128)(2,1)} %refs_1_.2) | copy-start | bytes 7077892
  118.1 2.0 %collective-permute-start.24 = (bf16[2,256,512]{2,1,0:T(8,128)(2,1)S(1)}, bf16[2,256,512]{2,1,0:T(8,128)(2,1)S(1)}, u32[]{:S(2)}, u32[]{:S(2)}) collective-permute-start(bf16[2,256,512]{2,1,0:T(8,128)(2,1)S(1)} %get-tuple-element.65), channel_id=1, source_target_pairs={{0,1},{1,0},{2,3},{3,2},{4,5},{5,4},{6,7},{7,6},{8,9},{9,8},{10,11... | collective-permute-start | bytes 1572872 | tf_op jit(solution)/shard_map/ppermute | solution.py:116
  120.2 8.4 %collective-permute-start.25 = (bf16[256,512]{1,0:T(8,128)(2,1)S(1)}, bf16[256,512]{1,0:T(8,128)(2,1)S(1)}, u32[]{:S(2)}, u32[]{:S(2)}) collective-permute-start(bf16[256,512]{1,0:T(8,128)(2,1)S(1)} %fusion.1), channel_id=1, source_target_pairs={{0,2},{2,0},{1,3},{3,1},{4,6},{6,4},{5,7},{7,5},{8,10},{10,8},{9,1... | collective-permute-start | bytes 786440 | tf_op jit(solution)/shard_map/ppermute | solution.py:116

commit v14 on v12

--- a/solution.py
+++ b/solution.py
@@ -512,8 +512,7 @@
     )
     send, out_third, out_partner = lax.optimization_barrier((send, out_third, out_partner))
     came = swap(send, "rep", 1)
-    out_fourth, third_rest = swap(out_third, "seq", 1), swap(out_third, "grp", 1)
-    partner_rest = swap(out_partner, "grp", 1)
+    third_rest, out_fourth = swap(out_third, "grp", 1), swap(out_third, "seq", 1)
 
     span = video_rows * seq_size
     blocks = jnp.stack([seq_at, seq_at ^ 1, seq_at ^ 2, seq_at ^ 3])
@@ -529,8 +528,10 @@
         ],
         limit=9,
     )
-    out_fourth, own_piece = lax.optimization_barrier((out_fourth, own_piece))
-    fourth_rest = swap(out_fourth, "grp", 1)
+    third_rest, out_partner, own_piece = lax.optimization_barrier(
+        (third_rest, out_partner, own_piece)
+    )
+    fourth_rest, partner_rest = swap(third_rest, "seq", 1), swap(out_partner, "grp", 1)
     far_piece = swap(far_piece, "seq", 2)
     farther_piece = swap(farther_piece, "seq", 3)
     near_piece = swap(near_piece, "seq", 1)

time: 125 us -> 126 us (level)
  transfers between devices with their start and end apart: 26 -> 26, of which waited for: 18 -> 16; matrix products, arithmetic and copies ran while one was open for 0% -> 0% of each run, Pallas kernels for 7% -> 6%
where the time goes in v14:
time: 126 us
  waiting for transfers between devices  73 us (58%)
  starting transfers between devices  37.8 us (30%)
  Pallas kernels  13.1 us (10%)
    ppermute x26, waiting for transfers between devices, swap(): return lax.ppermute(value, axis, [(i, i ^ bit) for i in range(size)])  73 us
    ppermute x26, starting transfers between devices, swap(): return lax.ppermute(value, axis, [(i, i ^ bit) for i in range(size)])  37.8 us
    pallas_call x5, Pallas kernels, kernel_call(): pl.pallas_call(whole, out_shape=outs, in_specs=spots + [ANY] * len(after)...  11.3 us
  transfers between devices with their start and end apart: 26, of which 16 were waited for; matrix products, arithmetic and copies ran while one was open for 0% of the time, Pallas kernels for 6%

profile of v14, /device:TPU:0, one launch (start us, length us, event | category | flops | bytes accessed | tf_op | source)
XLA Modules:
  0.0 126.2 jit_solution(1429768632540293451)
XLA Ops:
  0.7 3.3 %shard_map.87 = (bf16[640,512]{1,0:T(8,128)(2,1)}, bf16[640,1024]{1,0:T(8,128)(2,1)}, bf16[256,512]{1,0:T(8,128)(2,1)}) custom-call(s32[8]{0:T(128)} %refs_0_.1, bf16[3,192,2048]{2,1,0:T(8,128)(2,1)} %refs_1_.2, bf16[256,2048]{1,0:T(8,128)(2,1)} %refs_4_.3, bf16[1024,1024]{1,0:T(8,128)(2,1)} %refs_1_.3, bf16[512,512]{1,0:T(8,128)(2,1)} %refs_2_.3, ...), custom_call_target="tpu_custom_call" | custom-call | tf_op jit(solution)/shard_map/pallas_call | solution.py:130
  4.0 0.5 collective-permute-start
  4.5 2.6 %collective-permute-start.3 = (bf16[640,512]{1,0:T(8,128)(2,1)}, bf16[640,512]{1,0:T(8,128)(2,1)S(1)}, u32[]{:S(2)}, u32[]{:S(2)}) collective-permute-start(bf16[640,512]{1,0:T(8,128)(2,1)} %get-tuple-element.37.refs_0_), channel_id=1, source_target_pairs={{0,4},{4,0},{8,12},{12,8},{1,5},{5,1},{9,13},{13,9},{2,6},{6,2},{1... | collective-permute-start | bytes 1966088 | tf_op jit(solution)/shard_map/ppermute | solution.py:116
  7.2 2.6 %collective-permute-start.5 = (bf16[640,512]{1,0:T(8,128)(2,1)}, bf16[640,512]{1,0:T(8,128)(2,1)S(1)}, u32[]{:S(2)}, u32[]{:S(2)}) collective-permute-start(bf16[640,512]{1,0:T(8,128)(2,1)} %get-tuple-element.37.refs_0_), channel_id=1, source_target_pairs={{0,8},{4,12},{8,0},{12,4},{1,9},{5,13},{9,1},{13,5},{2,10},{6,14},... | collective-permute-start | bytes 1966088 | tf_op jit(solution)/shard_map/ppermute | solution.py:116
  9.8 0.3 shard_map.88
  10.1 0.6 collective-permute-start.1
  10.7 0.2 copy-done.5
  10.9 1.5 %collective-permute-start.2 = (bf16[640,512]{1,0:T(8,128)(2,1)S(1)}, bf16[640,512]{1,0:T(8,128)(2,1)S(1)}, u32[]{:S(2)}, u32[]{:S(2)}) collective-permute-start(bf16[640,512]{1,0:T(8,128)(2,1)S(1)} %copy-done.5), channel_id=1, source_target_pairs={{0,2},{2,0},{1,3},{3,1},{4,6},{6,4},{5,7},{7,5},{8,10},{10,8},{9,1... | collective-permute-start | bytes 1966088 | tf_op jit(solution)/shard_map/ppermute | solution.py:116
  12.4 24.5 %collective-permute-done.3.refs_2_ = bf16[640,512]{1,0:T(8,128)(2,1)S(1)} collective-permute-done((bf16[640,512]{1,0:T(8,128)(2,1)}, bf16[640,512]{1,0:T(8,128)(2,1)S(1)}, u32[]{:S(2)}, u32[]{:S(2)}) %collective-permute-start.3) | collective-permute-done | bytes 655392 | tf_op jit(solution)/shard_map/ppermute | solution.py:116
  36.9 1.9 %collective-permute-start.4 = (bf16[640,512]{1,0:T(8,128)(2,1)S(1)}, bf16[640,512]{1,0:T(8,128)(2,1)S(1)}, u32[]{:S(2)}, u32[]{:S(2)}) collective-permute-start(bf16[640,512]{1,0:T(8,128)(2,1)S(1)} %collective-permute-done.3.refs_2_), channel_id=1, source_target_pairs={{0,2},{2,0},{1,3},{3,1},{4,6},{6,4},{5,7},{7,5},{8,10},{10,8},{9,1... | collective-permute-start | bytes 1966088 | tf_op jit(solution)/shard_map/ppermute | solution.py:116
  38.7 0.2 collective-permute-done.5.refs_4_
  38.9 1.5 %collective-permute-start.7 = (bf16[640,512]{1,0:T(8,128)(2,1)S(1)}, bf16[640,512]{1,0:T(8,128)(2,1)S(1)}, u32[]{:S(2)}, u32[]{:S(2)}) collective-permute-start(bf16[640,512]{1,0:T(8,128)(2,1)S(1)} %collective-permute-done.5.refs_4_), channel_id=1, source_target_pairs={{0,2},{2,0},{1,3},{3,1},{4,6},{6,4},{5,7},{7,5},{8,10},{10,8},{9,1... | collective-permute-start | bytes 1966088 | tf_op jit(solution)/shard_map/ppermute | solution.py:116
  40.4 3.7 %collective-permute-done.1.refs_9_ = bf16[336,512]{1,0:T(8,128)(2,1)S(1)} collective-permute-done((bf16[336,512]{1,0:T(8,128)(2,1)S(1)}, bf16[336,512]{1,0:T(8,128)(2,1)S(1)}, u32[]{:S(2)}, u32[]{:S(2)}) %collective-permute-start.1) | collective-permute-done | bytes 344096 | tf_op jit(solution)/shard_map/ppermute | solution.py:116
  44.1 1.8 %collective-permute-start.6 = (bf16[640,512]{1,0:T(8,128)(2,1)S(1)}, bf16[640,512]{1,0:T(8,128)(2,1)S(1)}, u32[]{:S(2)}, u32[]{:S(2)}) collective-permute-start(bf16[640,512]{1,0:T(8,128)(2,1)S(1)} %collective-permute-done.5.refs_4_), channel_id=1, source_target_pairs={{0,4},{4,0},{8,12},{12,8},{1,5},{5,1},{9,13},{13,9},{2,6},{6,2},{1... | collective-permute-start | bytes 1966088 | tf_op jit(solution)/shard_map/ppermute | solution.py:116
  45.9 2.5 %collective-permute-start.9 = (bf16[336,512]{1,0:T(8,128)(2,1)S(1)}, bf16[336,512]{1,0:T(8,128)(2,1)S(1)}, u32[]{:S(2)}, u32[]{:S(2)}) collective-permute-start(bf16[336,512]{1,0:T(8,128)(2,1)S(1)} %get-tuple-element.44), channel_id=1, source_target_pairs={{0,8},{4,12},{8,0},{12,4},{1,9},{5,13},{9,1},{13,5},{2,10},{6,14},... | collective-permute-start | bytes 1032200 | tf_op jit(solution)/shard_map/ppermute | solution.py:116
  48.5 6.1 %collective-permute-done.4.refs_3_ = bf16[640,512]{1,0:T(8,128)(2,1)S(1)} collective-permute-done((bf16[640,512]{1,0:T(8,128)(2,1)S(1)}, bf16[640,512]{1,0:T(8,128)(2,1)S(1)}, u32[]{:S(2)}, u32[]{:S(2)}) %collective-permute-start.4) | collective-permute-done | bytes 655392 | tf_op jit(solution)/shard_map/ppermute | solution.py:116
  54.5 1.9 %collective-permute-start.8 = (bf16[336,512]{1,0:T(8,128)(2,1)S(1)}, bf16[336,512]{1,0:T(8,128)(2,1)S(1)}, u32[]{:S(2)}, u32[]{:S(2)}) collective-permute-start(bf16[336,512]{1,0:T(8,128)(2,1)S(1)} %collective-permute-done.1.refs_9_), channel_id=1, source_target_pairs={{0,16},{16,0},{1,17},{17,1},{2,18},{18,2},{3,19},{19,3},{4,20},{20... | collective-permute-start | bytes 1032200 | tf_op jit(solution)/shard_map/ppermute | solution.py:116
  56.4 2.5 %collective-permute-start.11 = (bf16[336,512]{1,0:T(8,128)(2,1)S(1)}, bf16[336,512]{1,0:T(8,128)(2,1)S(1)}, u32[]{:S(2)}, u32[]{:S(2)}) collective-permute-start(bf16[336,512]{1,0:T(8,128)(2,1)S(1)} %get-tuple-element.52), channel_id=1, source_target_pairs={{0,12},{4,8},{8,4},{12,0},{1,13},{5,9},{9,5},{13,1},{2,14},{6,10},... | collective-permute-start | bytes 1032200 | tf_op jit(solution)/shard_map/ppermute | solution.py:116
  58.9 8.2 %collective-permute-done.7.refs_5_ = bf16[640,512]{1,0:T(8,128)(2,1)S(1)} collective-permute-done((bf16[640,512]{1,0:T(8,128)(2,1)S(1)}, bf16[640,512]{1,0:T(8,128)(2,1)S(1)}, u32[]{:S(2)}, u32[]{:S(2)}) %collective-permute-start.7) | collective-permute-done | bytes 655392 | tf_op jit(solution)/shard_map/ppermute | solution.py:116
  67.2 1.4 %collective-permute-done.9.refs_11_ = bf16[336,512]{1,0:T(8,128)(2,1)S(1)} collective-permute-done((bf16[336,512]{1,0:T(8,128)(2,1)S(1)}, bf16[336,512]{1,0:T(8,128)(2,1)S(1)}, u32[]{:S(2)}, u32[]{:S(2)}) %collective-permute-start.9) | collective-permute-done | bytes 344096 | tf_op jit(solution)/shard_map/ppermute | solution.py:116
  68.5 1.5 %collective-permute-start.12 = (bf16[336,512]{1,0:T(8,128)(2,1)S(1)}, bf16[336,512]{1,0:T(8,128)(2,1)S(1)}, u32[]{:S(2)}, u32[]{:S(2)}) collective-permute-start(bf16[336,512]{1,0:T(8,128)(2,1)S(1)} %collective-permute-done.9.refs_11_), channel_id=1, source_target_pairs={{0,16},{16,0},{1,17},{17,1},{2,18},{18,2},{3,19},{19,3},{4,20},{20... | collective-permute-start | bytes 1032200 | tf_op jit(solution)/shard_map/ppermute | solution.py:116
  70.0 1.5 %collective-permute-start.10 = (bf16[640,512]{1,0:T(8,128)(2,1)S(1)}, bf16[640,512]{1,0:T(8,128)(2,1)S(1)}, u32[]{:S(2)}, u32[]{:S(2)}) collective-permute-start(bf16[640,512]{1,0:T(8,128)(2,1)S(1)} %collective-permute-done.6.refs_6_), channel_id=1, source_target_pairs={{0,2},{2,0},{1,3},{3,1},{4,6},{6,4},{5,7},{7,5},{8,10},{10,8},{9,1... | collective-permute-start | bytes 1966088 | tf_op jit(solution)/shard_map/ppermute | solution.py:116
  71.5 6.0 %collective-permute-done.11.refs_13_ = bf16[336,512]{1,0:T(8,128)(2,1)S(1)} collective-permute-done((bf16[336,512]{1,0:T(8,128)(2,1)S(1)}, bf16[336,512]{1,0:T(8,128)(2,1)S(1)}, u32[]{:S(2)}, u32[]{:S(2)}) %collective-permute-start.11) | collective-permute-done | bytes 344096 | tf_op jit(solution)/shard_map/ppermute | solution.py:116
  77.5 1.5 %collective-permute-start.13 = (bf16[336,512]{1,0:T(8,128)(2,1)S(1)}, bf16[336,512]{1,0:T(8,128)(2,1)S(1)}, u32[]{:S(2)}, u32[]{:S(2)}) collective-permute-start(bf16[336,512]{1,0:T(8,128)(2,1)S(1)} %collective-permute-done.11.refs_13_), channel_id=1, source_target_pairs={{0,16},{16,0},{1,17},{17,1},{2,18},{18,2},{3,19},{19,3},{4,20},{20... | collective-permute-start | bytes 1032200 | tf_op jit(solution)/shard_map/ppermute | solution.py:116
  79.1 2.6 %collective-permute-start.14 = (bf16[256,512]{1,0:T(8,128)(2,1)S(1)}, bf16[256,512]{1,0:T(8,128)(2,1)S(1)}, u32[]{:S(2)}, u32[]{:S(2)}) collective-permute-start(bf16[256,512]{1,0:T(8,128)(2,1)S(1)} %copy-done.8), channel_id=1, source_target_pairs={{0,8},{4,12},{8,0},{12,4},{1,9},{5,13},{9,1},{13,5},{2,10},{6,14},... | collective-permute-start | bytes 786440 | tf_op jit(solution)/shard_map/ppermute | solution.py:116
  81.7 1.3 %collective-permute-start.15 = (bf16[256,512]{1,0:T(8,128)(2,1)S(1)}, bf16[256,512]{1,0:T(8,128)(2,1)S(1)}, u32[]{:S(2)}, u32[]{:S(2)}) collective-permute-start(bf16[256,512]{1,0:T(8,128)(2,1)S(1)} %copy-done.8), channel_id=1, source_target_pairs={{0,4},{4,0},{8,12},{12,8},{1,5},{5,1},{9,13},{13,9},{2,6},{6,2},{1... | collective-permute-start | bytes 786440 | tf_op jit(solution)/shard_map/ppermute | solution.py:116
  83.0 1.7 %collective-permute-done.10.refs_7_ = bf16[640,512]{1,0:T(8,128)(2,1)S(1)} collective-permute-done((bf16[640,512]{1,0:T(8,128)(2,1)S(1)}, bf16[640,512]{1,0:T(8,128)(2,1)S(1)}, u32[]{:S(2)}, u32[]{:S(2)}) %collective-permute-start.10) | collective-permute-done | bytes 655392 | tf_op jit(solution)/shard_map/ppermute | solution.py:116
  84.6 1.6 %collective-permute-done.13.refs_14_ = bf16[336,512]{1,0:T(8,128)(2,1)S(1)} collective-permute-done((bf16[336,512]{1,0:T(8,128)(2,1)S(1)}, bf16[336,512]{1,0:T(8,128)(2,1)S(1)}, u32[]{:S(2)}, u32[]{:S(2)}) %collective-permute-start.13) | collective-permute-done | bytes 344096 | tf_op jit(solution)/shard_map/ppermute | solution.py:116
  86.2 3.9 %shard_map.89 = (bf16[4,16,256]{2,1,0:T(8,128)(2,1)S(1)}, f32[1280,256]{1,0:T(8,128)}, f32[1280,256]{1,0:T(8,128)S(1)}) custom-call(bf16[640,512]{1,0:T(8,128)(2,1)S(1)} %copy-done.5, bf16[640,512]{1,0:T(8,128)(2,1)S(1)} %collective-permute-done.2.refs_1_, bf16[640,512]{1,0:T(8,128)(2,1)S(1)} %collective-permute-done.3.refs_2_, ...), custom_call_target="tpu_custom_call" | custom-call | tf_op jit(solution)/shard_map/pallas_call | solution.py:130
  90.1 1.2 collective-permute-done.14.refs_8_
  91.5 0.5 collective-permute-start.16
  92.3 1.2 collective-permute-start.22
  93.4 1.1 collective-permute-done.17.refs_3_
  94.6 2.2 %shard_map.90 = (bf16[256,128]{1,0:T(8,128)(2,1)S(1)}, bf16[256,128]{1,0:T(8,128)(2,1)S(1)}, bf16[256,128]{1,0:T(8,128)(2,1)S(1)}, bf16[256,128]{1,0:T(8,128)(2,1)S(1)}) custom-call(f32[1,768]{1,0:T(1,128)S(1)} %fusion.4.refs_0_, bf16[4,16,256]{2,1,0:T(8,128)(2,1)S(1)} %get-tuple-element.60.refs_1_, f32[1280,256]{1,0:T(8,128)S(1)} %get-tuple-element.61.refs_2_, ...), custom_call_target="tpu_custom_call" | custom-call | tf_op jit(solution)/shard_map/pallas_call | solution.py:130
  96.8 3.4 %collective-permute-done.16.refs_9_ = bf16[256,512]{1,0:T(8,128)(2,1)S(1)} collective-permute-done((bf16[256,512]{1,0:T(8,128)(2,1)S(1)}, bf16[256,512]{1,0:T(8,128)(2,1)S(1)}, u32[]{:S(2)}, u32[]{:S(2)}) %collective-permute-start.16) | collective-permute-done | bytes 262176 | tf_op jit(solution)/shard_map/ppermute | solution.py:116
  100.2 0.5 collective-permute-start.21
  100.7 1.2 collective-permute-start.23
  101.9 0.9 collective-permute-start.18
  102.7 1.0 collective-permute-start.19
  103.8 2.5 %collective-permute-start.20 = (bf16[256,128]{1,0:T(8,128)(2,1)S(1)}, bf16[256,128]{1,0:T(8,128)(2,1)S(1)}, u32[]{:S(2)}, u32[]{:S(2)}) collective-permute-start(bf16[256,128]{1,0:T(8,128)(2,1)S(1)} %get-tuple-element.67), channel_id=1, source_target_pairs={{0,12},{4,8},{8,4},{12,0},{1,13},{5,9},{9,5},{13,1},{2,14},{6,10},... | collective-permute-start | bytes 196616 | tf_op jit(solution)/shard_map/ppermute | solution.py:116
  106.3 5.6 %collective-permute-done.18.refs_1_ = bf16[256,128]{1,0:T(8,128)(2,1)S(1)} collective-permute-done((bf16[256,128]{1,0:T(8,128)(2,1)S(1)}, bf16[256,128]{1,0:T(8,128)(2,1)S(1)}, u32[]{:S(2)}, u32[]{:S(2)}) %collective-permute-start.18) | collective-permute-done | bytes 65568 | tf_op jit(solution)/shard_map/ppermute | solution.py:116
  111.9 1.4 %collective-permute-done.20.refs_3_ = bf16[256,128]{1,0:T(8,128)(2,1)S(1)} collective-permute-done((bf16[256,128]{1,0:T(8,128)(2,1)S(1)}, bf16[256,128]{1,0:T(8,128)(2,1)S(1)}, u32[]{:S(2)}, u32[]{:S(2)}) %collective-permute-start.20) | collective-permute-done | bytes 65568 | tf_op jit(solution)/shard_map/ppermute | solution.py:116
  113.3 1.6 %shard_map.91 = (bf16[2,256,512]{2,1,0:T(8,128)(2,1)S(1)}, f32[2,256,512]{2,1,0:T(8,128)S(1)}) custom-call(bf16[256,128]{1,0:T(8,128)(2,1)S(1)} %get-tuple-element.64.refs_0_, bf16[256,128]{1,0:T(8,128)(2,1)S(1)} %collective-permute-done.18.refs_1_, bf16[256,128]{1,0:T(8,128)(2,1)S(1)} %collective-permute-done.19.refs_2_, ...), custom_call_target="tpu_custom_call" | custom-call | tf_op jit(solution)/shard_map/pallas_call | solution.py:130
  115.0 1.9 %collective-permute-done.24 = bf16[2,256,512]{2,1,0:T(8,128)(2,1)S(1)} collective-permute-done((bf16[2,256,512]{2,1,0:T(8,128)(2,1)S(1)}, bf16[2,256,512]{2,1,0:T(8,128)(2,1)S(1)}, u32[]{:S(2)}, u32[]{:S(2)}) %collective-permute-start.24) | collective-permute-done | bytes 524320 | tf_op jit(solution)/shard_map/ppermute | solution.py:116
  117.0 1.6 %collective-permute-start.25 = (bf16[256,512]{1,0:T(8,128)(2,1)S(1)}, bf16[256,512]{1,0:T(8,128)(2,1)S(1)}, u32[]{:S(2)}, u32[]{:S(2)}) collective-permute-start(bf16[256,512]{1,0:T(8,128)(2,1)S(1)} %fusion.1), channel_id=1, source_target_pairs={{0,2},{2,0},{1,3},{3,1},{4,6},{6,4},{5,7},{7,5},{8,10},{10,8},{9,1... | collective-permute-start | bytes 786440 | tf_op jit(solution)/shard_map/ppermute | solution.py:116
  118.5 1.8 %shard_map.86 = bf16[192,2048]{1,0:T(8,128)(2,1)} custom-call(s32[8]{0:T(128)S(1)} %copy-done.7, bf16[3,192,2048]{2,1,0:T(8,128)(2,1)S(1)} %copy-done), custom_call_target="tpu_custom_call" | custom-call | tf_op jit(solution)/shard_map/pallas_call | solution.py:168
  120.4 5.0 %collective-permute-done.25 = bf16[256,512]{1,0:T(8,128)(2,1)S(1)} collective-permute-done((bf16[256,512]{1,0:T(8,128)(2,1)S(1)}, bf16[256,512]{1,0:T(8,128)(2,1)S(1)}, u32[]{:S(2)}, u32[]{:S(2)}) %collective-permute-start.25) | collective-permute-done | bytes 262176 | tf_op jit(solution)/shard_map/ppermute | solution.py:116
  125.4 0.8 fusion
  (37 shorter events, 0.6 us)
Async XLA Ops:
  0.6 9.1 %copy-start.3 = (bf16[512,512]{1,0:T(8,128)(2,1)S(1)}, bf16[512,512]{1,0:T(8,128)(2,1)}, u32[]{:S(2)}) copy-start(bf16[512,512]{1,0:T(8,128)(2,1)} %refs_2_.3) | copy-start | bytes 1572868
  0.6 9.1 %copy-start.1 = (bf16[1024,1024]{1,0:T(8,128)(2,1)S(1)}, bf16[1024,1024]{1,0:T(8,128)(2,1)}, u32[]{:S(2)}) copy-start(bf16[1024,1024]{1,0:T(8,128)(2,1)} %refs_1_.3) | copy-start | bytes 6291460
  0.7 9.1 %copy-start.6 = (s32[256]{0:T(256)S(1)}, s32[256]{0:T(256)}, u32[]{:S(2)}) copy-start(s32[256]{0:T(256)} %param.9) | copy-start | bytes 3076
  4.0 5.8 %collective-permute-start = (bf16[640,1024]{1,0:T(8,128)(2,1)}, bf16[640,1024]{1,0:T(8,128)(2,1)S(1)}, u32[]{:S(2)}, u32[]{:S(2)}) collective-permute-start(bf16[640,1024]{1,0:T(8,128)(2,1)} %get-tuple-element.38), channel_id=1, source_target_pairs={{0,1},{1,0},{2,3},{3,2},{4,5},{5,4},{6,7},{7,6},{8,9},{9,8},{10,11... | collective-permute-start | bytes 3932168 | tf_op jit(solution)/shard_map/ppermute | solution.py:116
  4.5 32.4 %collective-permute-start.3 = (bf16[640,512]{1,0:T(8,128)(2,1)}, bf16[640,512]{1,0:T(8,128)(2,1)S(1)}, u32[]{:S(2)}, u32[]{:S(2)}) collective-permute-start(bf16[640,512]{1,0:T(8,128)(2,1)} %get-tuple-element.37.refs_0_), channel_id=1, source_target_pairs={{0,4},{4,0},{8,12},{12,8},{1,5},{5,1},{9,13},{13,9},{2,6},{6,2},{1... | collective-permute-start | bytes 1966088 | tf_op jit(solution)/shard_map/ppermute | solution.py:116
  7.2 31.8 %collective-permute-start.5 = (bf16[640,512]{1,0:T(8,128)(2,1)}, bf16[640,512]{1,0:T(8,128)(2,1)S(1)}, u32[]{:S(2)}, u32[]{:S(2)}) collective-permute-start(bf16[640,512]{1,0:T(8,128)(2,1)} %get-tuple-element.37.refs_0_), channel_id=1, source_target_pairs={{0,8},{4,12},{8,0},{12,4},{1,9},{5,13},{9,1},{13,5},{2,10},{6,14},... | collective-permute-start | bytes 1966088 | tf_op jit(solution)/shard_map/ppermute | solution.py:116
  9.8 1.1 copy-start.5
  9.8 69.3 %copy-start.8 = (bf16[256,512]{1,0:T(8,128)(2,1)S(1)}, bf16[256,512]{1,0:T(8,128)(2,1)}, u32[]{:S(2)}) copy-start(bf16[256,512]{1,0:T(8,128)(2,1)} %get-tuple-element.57) | copy-start | bytes 786436
  10.1 34.1 %collective-permute-start.1 = (bf16[336,512]{1,0:T(8,128)(2,1)S(1)}, bf16[336,512]{1,0:T(8,128)(2,1)S(1)}, u32[]{:S(2)}, u32[]{:S(2)}) collective-permute-start(bf16[336,512]{1,0:T(8,128)(2,1)S(1)} %get-tuple-element.39), channel_id=1, source_target_pairs={{0,4},{4,0},{8,12},{12,8},{1,5},{5,1},{9,13},{13,9},{2,6},{6,2},{1... | collective-permute-start | bytes 1032200 | tf_op jit(solution)/shard_map/ppermute | solution.py:116
  10.9 37.6 %collective-permute-start.2 = (bf16[640,512]{1,0:T(8,128)(2,1)S(1)}, bf16[640,512]{1,0:T(8,128)(2,1)S(1)}, u32[]{:S(2)}, u32[]{:S(2)}) collective-permute-start(bf16[640,512]{1,0:T(8,128)(2,1)S(1)} %copy-done.5), channel_id=1, source_target_pairs={{0,2},{2,0},{1,3},{3,1},{4,6},{6,4},{5,7},{7,5},{8,10},{10,8},{9,1... | collective-permute-start | bytes 1966088 | tf_op jit(solution)/shard_map/ppermute | solution.py:116
  36.9 17.7 %collective-permute-start.4 = (bf16[640,512]{1,0:T(8,128)(2,1)S(1)}, bf16[640,512]{1,0:T(8,128)(2,1)S(1)}, u32[]{:S(2)}, u32[]{:S(2)}) collective-permute-start(bf16[640,512]{1,0:T(8,128)(2,1)S(1)} %collective-permute-done.3.refs_2_), channel_id=1, source_target_pairs={{0,2},{2,0},{1,3},{3,1},{4,6},{6,4},{5,7},{7,5},{8,10},{10,8},{9,1... | collective-permute-start | bytes 1966088 | tf_op jit(solution)/shard_map/ppermute | solution.py:116
  38.9 28.2 %collective-permute-start.7 = (bf16[640,512]{1,0:T(8,128)(2,1)S(1)}, bf16[640,512]{1,0:T(8,128)(2,1)S(1)}, u32[]{:S(2)}, u32[]{:S(2)}) collective-permute-start(bf16[640,512]{1,0:T(8,128)(2,1)S(1)} %collective-permute-done.5.refs_4_), channel_id=1, source_target_pairs={{0,2},{2,0},{1,3},{3,1},{4,6},{6,4},{5,7},{7,5},{8,10},{10,8},{9,1... | collective-permute-start | bytes 1966088 | tf_op jit(solution)/shard_map/ppermute | solution.py:116
  44.1 24.4 %collective-permute-start.6 = (bf16[640,512]{1,0:T(8,128)(2,1)S(1)}, bf16[640,512]{1,0:T(8,128)(2,1)S(1)}, u32[]{:S(2)}, u32[]{:S(2)}) collective-permute-start(bf16[640,512]{1,0:T(8,128)(2,1)S(1)} %collective-permute-done.5.refs_4_), channel_id=1, source_target_pairs={{0,4},{4,0},{8,12},{12,8},{1,5},{5,1},{9,13},{13,9},{2,6},{6,2},{1... | collective-permute-start | bytes 1966088 | tf_op jit(solution)/shard_map/ppermute | solution.py:116
  45.9 22.6 %collective-permute-start.9 = (bf16[336,512]{1,0:T(8,128)(2,1)S(1)}, bf16[336,512]{1,0:T(8,128)(2,1)S(1)}, u32[]{:S(2)}, u32[]{:S(2)}) collective-permute-start(bf16[336,512]{1,0:T(8,128)(2,1)S(1)} %get-tuple-element.44), channel_id=1, source_target_pairs={{0,8},{4,12},{8,0},{12,4},{1,9},{5,13},{9,1},{13,5},{2,10},{6,14},... | collective-permute-start | bytes 1032200 | tf_op jit(solution)/shard_map/ppermute | solution.py:116
  54.5 14.0 %collective-permute-start.8 = (bf16[336,512]{1,0:T(8,128)(2,1)S(1)}, bf16[336,512]{1,0:T(8,128)(2,1)S(1)}, u32[]{:S(2)}, u32[]{:S(2)}) collective-permute-start(bf16[336,512]{1,0:T(8,128)(2,1)S(1)} %collective-permute-done.1.refs_9_), channel_id=1, source_target_pairs={{0,16},{16,0},{1,17},{17,1},{2,18},{18,2},{3,19},{19,3},{4,20},{20... | collective-permute-start | bytes 1032200 | tf_op jit(solution)/shard_map/ppermute | solution.py:116
  56.4 21.1 %collective-permute-start.11 = (bf16[336,512]{1,0:T(8,128)(2,1)S(1)}, bf16[336,512]{1,0:T(8,128)(2,1)S(1)}, u32[]{:S(2)}, u32[]{:S(2)}) collective-permute-start(bf16[336,512]{1,0:T(8,128)(2,1)S(1)} %get-tuple-element.52), channel_id=1, source_target_pairs={{0,12},{4,8},{8,4},{12,0},{1,13},{5,9},{9,5},{13,1},{2,14},{6,10},... | collective-permute-start | bytes 1032200 | tf_op jit(solution)/shard_map/ppermute | solution.py:116
  68.5 9.0 %collective-permute-start.12 = (bf16[336,512]{1,0:T(8,128)(2,1)S(1)}, bf16[336,512]{1,0:T(8,128)(2,1)S(1)}, u32[]{:S(2)}, u32[]{:S(2)}) collective-permute-start(bf16[336,512]{1,0:T(8,128)(2,1)S(1)} %collective-permute-done.9.refs_11_), channel_id=1, source_target_pairs={{0,16},{16,0},{1,17},{17,1},{2,18},{18,2},{3,19},{19,3},{4,20},{20... | collective-permute-start | bytes 1032200 | tf_op jit(solution)/shard_map/ppermute | solution.py:116
  70.0 14.6 %collective-permute-start.10 = (bf16[640,512]{1,0:T(8,128)(2,1)S(1)}, bf16[640,512]{1,0:T(8,128)(2,1)S(1)}, u32[]{:S(2)}, u32[]{:S(2)}) collective-permute-start(bf16[640,512]{1,0:T(8,128)(2,1)S(1)} %collective-permute-done.6.refs_6_), channel_id=1, source_target_pairs={{0,2},{2,0},{1,3},{3,1},{4,6},{6,4},{5,7},{7,5},{8,10},{10,8},{9,1... | collective-permute-start | bytes 1966088 | tf_op jit(solution)/shard_map/ppermute | solution.py:116
  77.5 8.7 %collective-permute-start.13 = (bf16[336,512]{1,0:T(8,128)(2,1)S(1)}, bf16[336,512]{1,0:T(8,128)(2,1)S(1)}, u32[]{:S(2)}, u32[]{:S(2)}) collective-permute-start(bf16[336,512]{1,0:T(8,128)(2,1)S(1)} %collective-permute-done.11.refs_13_), channel_id=1, source_target_pairs={{0,16},{16,0},{1,17},{17,1},{2,18},{18,2},{3,19},{19,3},{4,20},{20... | collective-permute-start | bytes 1032200 | tf_op jit(solution)/shard_map/ppermute | solution.py:116
  79.1 12.3 %collective-permute-start.14 = (bf16[256,512]{1,0:T(8,128)(2,1)S(1)}, bf16[256,512]{1,0:T(8,128)(2,1)S(1)}, u32[]{:S(2)}, u32[]{:S(2)}) collective-permute-start(bf16[256,512]{1,0:T(8,128)(2,1)S(1)} %copy-done.8), channel_id=1, source_target_pairs={{0,8},{4,12},{8,0},{12,4},{1,9},{5,13},{9,1},{13,5},{2,10},{6,14},... | collective-permute-start | bytes 786440 | tf_op jit(solution)/shard_map/ppermute | solution.py:116
  81.7 9.6 %collective-permute-start.15 = (bf16[256,512]{1,0:T(8,128)(2,1)S(1)}, bf16[256,512]{1,0:T(8,128)(2,1)S(1)}, u32[]{:S(2)}, u32[]{:S(2)}) collective-permute-start(bf16[256,512]{1,0:T(8,128)(2,1)S(1)} %copy-done.8), channel_id=1, source_target_pairs={{0,4},{4,0},{8,12},{12,8},{1,5},{5,1},{9,13},{13,9},{2,6},{6,2},{1... | collective-permute-start | bytes 786440 | tf_op jit(solution)/shard_map/ppermute | solution.py:116
  91.3 3.2 %collective-permute-start.17 = (f32[1280,256]{1,0:T(8,128)}, f32[1280,256]{1,0:T(8,128)S(1)}, u32[]{:S(2)}, u32[]{:S(2)}) collective-permute-start(f32[1280,256]{1,0:T(8,128)} %get-tuple-element.62), channel_id=1, source_target_pairs={{0,1},{1,0},{2,3},{3,2},{4,5},{5,4},{6,7},{7,6},{8,9},{9,8},{10,11... | collective-permute-start | bytes 3932168 | tf_op jit(solution)/shard_map/ppermute | solution.py:116
  91.5 8.7 %collective-permute-start.16 = (bf16[256,512]{1,0:T(8,128)(2,1)S(1)}, bf16[256,512]{1,0:T(8,128)(2,1)S(1)}, u32[]{:S(2)}, u32[]{:S(2)}) collective-permute-start(bf16[256,512]{1,0:T(8,128)(2,1)S(1)} %collective-permute-done.14.refs_8_), channel_id=1, source_target_pairs={{0,16},{16,0},{1,17},{17,1},{2,18},{18,2},{3,19},{19,3},{4,20},{20... | collective-permute-start | bytes 786440 | tf_op jit(solution)/shard_map/ppermute | solution.py:116
  92.3 11.5 %collective-permute-start.22 = (bf16[256,512]{1,0:T(8,128)(2,1)S(1)}, bf16[256,512]{1,0:T(8,128)(2,1)S(1)}, u32[]{:S(2)}, u32[]{:S(2)}) collective-permute-start(bf16[256,512]{1,0:T(8,128)(2,1)S(1)} %collective-permute-done.14.refs_8_), channel_id=1, source_target_pairs={{0,4},{4,0},{8,12},{12,8},{1,5},{5,1},{9,13},{13,9},{2,6},{6,2},{1... | collective-permute-start | bytes 786440 | tf_op jit(solution)/shard_map/ppermute | solution.py:116
  94.6 18.7 %copy-start.2 = (bf16[256,2048]{1,0:T(8,128)(2,1)S(1)}, bf16[256,2048]{1,0:T(8,128)(2,1)}, u32[]{:S(2)}) copy-start(bf16[256,2048]{1,0:T(8,128)(2,1)} %refs_4_.3) | copy-start | bytes 3145732
  94.6 18.7 %copy-start.4 = (bf16[512,512]{1,0:T(8,128)(2,1)S(1)}, bf16[512,512]{1,0:T(8,128)(2,1)}, u32[]{:S(2)}) copy-start(bf16[512,512]{1,0:T(8,128)(2,1)} %refs_5_.3) | copy-start | bytes 1572868
  100.2 13.1 %collective-permute-start.21 = (bf16[256,512]{1,0:T(8,128)(2,1)S(1)}, bf16[256,512]{1,0:T(8,128)(2,1)S(1)}, u32[]{:S(2)}, u32[]{:S(2)}) collective-permute-start(bf16[256,512]{1,0:T(8,128)(2,1)S(1)} %collective-permute-done.15.refs_6_), channel_id=1, source_target_pairs={{0,16},{16,0},{1,17},{17,1},{2,18},{18,2},{3,19},{19,3},{4,20},{20... | collective-permute-start | bytes 786440 | tf_op jit(solution)/shard_map/ppermute | solution.py:116
  100.7 12.6 %collective-permute-start.23 = (bf16[256,512]{1,0:T(8,128)(2,1)S(1)}, bf16[256,512]{1,0:T(8,128)(2,1)S(1)}, u32[]{:S(2)}, u32[]{:S(2)}) collective-permute-start(bf16[256,512]{1,0:T(8,128)(2,1)S(1)} %collective-permute-done.16.refs_9_), channel_id=1, source_target_pairs={{0,4},{4,0},{8,12},{12,8},{1,5},{5,1},{9,13},{13,9},{2,6},{6,2},{1... | collective-permute-start | bytes 786440 | tf_op jit(solution)/shard_map/ppermute | solution.py:116
  101.9 10.0 %collective-permute-start.18 = (bf16[256,128]{1,0:T(8,128)(2,1)S(1)}, bf16[256,128]{1,0:T(8,128)(2,1)S(1)}, u32[]{:S(2)}, u32[]{:S(2)}) collective-permute-start(bf16[256,128]{1,0:T(8,128)(2,1)S(1)} %get-tuple-element.65), channel_id=1, source_target_pairs={{0,4},{4,0},{8,12},{12,8},{1,5},{5,1},{9,13},{13,9},{2,6},{6,2},{1... | collective-permute-start | bytes 196616 | tf_op jit(solution)/shard_map/ppermute | solution.py:116
  102.7 9.1 %collective-permute-start.19 = (bf16[256,128]{1,0:T(8,128)(2,1)S(1)}, bf16[256,128]{1,0:T(8,128)(2,1)S(1)}, u32[]{:S(2)}, u32[]{:S(2)}) collective-permute-start(bf16[256,128]{1,0:T(8,128)(2,1)S(1)} %get-tuple-element.66), channel_id=1, source_target_pairs={{0,8},{4,12},{8,0},{12,4},{1,9},{5,13},{9,1},{13,5},{2,10},{6,14},... | collective-permute-start | bytes 196616 | tf_op jit(solution)/shard_map/ppermute | solution.py:116
  103.8 14.8 %copy-start.7 = (s32[8]{0:T(128)S(1)}, s32[8]{0:T(128)}, u32[]{:S(2)}) copy-start(s32[8]{0:T(128)} %refs_0_.1) | copy-start | bytes 100
  103.8 9.5 %collective-permute-start.20 = (bf16[256,128]{1,0:T(8,128)(2,1)S(1)}, bf16[256,128]{1,0:T(8,128)(2,1)S(1)}, u32[]{:S(2)}, u32[]{:S(2)}) collective-permute-start(bf16[256,128]{1,0:T(8,128)(2,1)S(1)} %get-tuple-element.67), channel_id=1, source_target_pairs={{0,12},{4,8},{8,4},{12,0},{1,13},{5,9},{9,5},{13,1},{2,14},{6,10},... | collective-permute-start | bytes 196616 | tf_op jit(solution)/shard_map/ppermute | solution.py:116
  113.3 5.3 %copy-start = (bf16[3,192,2048]{2,1,0:T(8,128)(2,1)S(1)}, bf16[3,192,2048]{2,1,0:T(8,128)(2,1)}, u32[]{:S(2)}) copy-start(bf16[3,192,2048]{2,1,0:T(8,128)(2,1)} %refs_1_.2) | copy-start | bytes 7077892
  114.9 2.0 %collective-permute-start.24 = (bf16[2,256,512]{2,1,0:T(8,128)(2,1)S(1)}, bf16[2,256,512]{2,1,0:T(8,128)(2,1)S(1)}, u32[]{:S(2)}, u32[]{:S(2)}) collective-permute-start(bf16[2,256,512]{2,1,0:T(8,128)(2,1)S(1)} %get-tuple-element.71), channel_id=1, source_target_pairs={{0,1},{1,0},{2,3},{3,2},{4,5},{5,4},{6,7},{7,6},{8,9},{9,8},{10,11... | collective-permute-start | bytes 1572872 | tf_op jit(solution)/shard_map/ppermute | solution.py:116
  117.0 8.4 %collective-permute-start.25 = (bf16[256,512]{1,0:T(8,128)(2,1)S(1)}, bf16[256,512]{1,0:T(8,128)(2,1)S(1)}, u32[]{:S(2)}, u32[]{:S(2)}) collective-permute-start(bf16[256,512]{1,0:T(8,128)(2,1)S(1)} %fusion.1), channel_id=1, source_target_pairs={{0,2},{2,0},{1,3},{3,1},{4,6},{6,4},{5,7},{7,5},{8,10},{10,8},{9,1... | collective-permute-start | bytes 786440 | tf_op jit(solution)/shard_map/ppermute | solution.py:116

commit v15 on v14

--- a/solution.py
+++ b/solution.py
@@ -122,7 +122,7 @@
 HBM = pl.BlockSpec(memory_space=pltpu.HBM)
 
 
-def kernel_call(body, outs, ins, after=(), scratch=(), smem=(), loose_in=(), loose_out=(), limit=14):
+def kernel_call(body, outs, ins, after=(), scratch=(), smem=(), loose_in=(), loose_out=(), limit=14, cost=None):
     def whole(*refs):
         body(*refs[: len(ins)], *refs[len(ins) + len(after) :])
 
@@ -133,6 +133,7 @@
         in_specs=spots + [ANY] * len(after),
         out_specs=[HBM if i in loose_out else VMEM for i in range(len(outs))],
         scratch_shapes=scratch,
+        cost_estimate=cost,
         compiler_params=pltpu.CompilerParams(vmem_limit_bytes=limit * 2**20),
     )(*ins, *after)
 
@@ -393,8 +394,8 @@
 
 
 def out_body(*refs):
-    piece_refs, (audio_ref, own_w, *part_refs) = refs[:4], refs[4:12]
-    send_ref, keep_ref, heads_ref, weight_ref, residual_ref, sems = refs[12:]
+    piece_refs, (audio_ref, own_w, *part_refs) = refs[:4], refs[4:10]
+    total_ref, late_ref, heads_ref, weight_ref, residual_ref, sems = refs[10:]
     seq_at, grp_at = lax.axis_index("seq"), lax.axis_index("grp")
     place = lax.axis_index("mem") * 2 + lax.axis_index("rep")
     copy = pltpu.make_async_copy(own_w, weight_ref.at[0], sems.at[0])
@@ -406,17 +407,37 @@
     for bit, piece_ref in enumerate(piece_refs):
         heads_ref[seq_at ^ bit] = piece_ref[...]
     heads = jnp.concatenate([heads_ref[head] for head in range(heads_ref.shape[0])], axis=1)
-    depth = part_refs[0].shape[0]
-    mine = pl.ds(pl.multiple_of(grp_at * depth, depth), depth)
-    rest = pl.ds(pl.multiple_of((1 - grp_at) * depth, depth), depth)
-    for bit in range(1, 4):
-        weight_ref[bit, mine] = part_refs[2 * bit - 2][...]
-        weight_ref[bit, rest] = part_refs[2 * bit - 1][...]
-    for bit in (1, 2, 3, 0):
-        if bit == 0:
-            copy.wait()
-        slot = seq_at ^ bit ^ place
-        value = jnp.dot(heads, weight_ref[bit], preferred_element_type=jnp.float32)
+
+    def half(group):
+        return jnp.concatenate([heads_ref[2 * group], heads_ref[2 * group + 1]], axis=1)
+
+    mine = half(grp_at)
+    late_ref[...] = half(1 - grp_at)
+    partner_w, third_w, third_rest_w, fourth_w = part_refs
+    depth = partner_w.shape[0]
+    weight_ref[1, pl.ds(pl.multiple_of(grp_at * depth, depth), depth)] = third_w[...]
+    weight_ref[1, pl.ds(pl.multiple_of((1 - grp_at) * depth, depth), depth)] = third_rest_w[...]
+
+    def product(rows, weight):
+        return jnp.dot(rows, weight, preferred_element_type=jnp.float32)
+
+    total_ref[1] = product(mine, partner_w[...])
+    total_ref[3] = product(mine, fourth_w[...])
+    total_ref[2] = product(heads, weight_ref[1])
+    copy.wait()
+    total_ref[0] = product(heads, weight_ref[0])
+    residual_copy.wait()
+    total_ref[seq_at ^ place] += residual_ref[...].astype(jnp.float32)
+
+
+def late_out_body(total_ref, late_ref, partner_w, fourth_w, send_ref, keep_ref):
+    place = lax.axis_index("mem") * 2 + lax.axis_index("rep")
+    for bit in range(4):
+        slot = lax.axis_index("seq") ^ bit ^ place
+        value = total_ref[bit]
+        if bit % 2:
+            weight = (partner_w if bit == 1 else fourth_w)[...]
+            value += jnp.dot(late_ref[...], weight, preferred_element_type=jnp.float32)
 
         @pl.when(slot % 2 == 1)
         def _():
@@ -425,9 +446,6 @@
         @pl.when(slot % 2 == 0)
         def _():
             keep_ref[slot // 2] = value
-
-    residual_copy.wait()
-    keep_ref[0] += residual_ref[...].astype(jnp.float32)
 
 
 def by_head(video_cache, plan, alignment, audio_tokens, kv_weight, query_weight, out_weight):
@@ -537,23 +555,42 @@
     near_piece = swap(near_piece, "seq", 1)
 
     columns = out_weight.shape[1]
-    weights = [out_weight, out_partner, partner_rest]
-    weights += [out_third, third_rest, out_fourth, fourth_rest]
-    send, keep = kernel_call(
+    total, late_heads = kernel_call(
         out_body,
         [
-            jax.ShapeDtypeStruct((2, audio_rows, columns), jnp.bfloat16),
-            jax.ShapeDtypeStruct((2, audio_rows, columns), jnp.float32),
-        ],
-        [own_piece, near_piece, far_piece, farther_piece, audio_tokens, *weights],
+            jax.ShapeDtypeStruct((seq_size, audio_rows, columns), jnp.float32),
+            bfloat(audio_rows, 2 * HEAD_DIM),
+        ],
+        [
+            own_piece,
+            near_piece,
+            far_piece,
+            farther_piece,
+            audio_tokens,
+            out_weight,
+            out_partner,
+            out_third,
+            third_rest,
+            out_fourth,
+        ],
         scratch=[
             pltpu.VMEM((seq_size, audio_rows, HEAD_DIM), jnp.bfloat16),
-            pltpu.VMEM((seq_size, *out_weight.shape), jnp.bfloat16),
+            pltpu.VMEM((2, *out_weight.shape), jnp.bfloat16),
             pltpu.VMEM((audio_rows, columns), jnp.bfloat16),
             pltpu.SemaphoreType.DMA((2,)),
         ],
         loose_in=(4, 5),
         limit=7,
+        cost=pl.CostEstimate(flops=10000000000, bytes_accessed=10000000, transcendentals=0),
+    )
+    send, keep = kernel_call(
+        late_out_body,
+        [
+            bfloat(2, audio_rows, columns),
+            jax.ShapeDtypeStruct((2, audio_rows, columns), jnp.float32),
+        ],
+        [total, late_heads, partner_rest, fourth_rest],
+        limit=5,
     )
     came = swap(send, "rep", 1)
     across = swap((keep[1] + came[1].astype(jnp.float32)).astype(jnp.bfloat16), "mem", 1)

time: 126 us -> 123 us (0.976)
  waiting for transfers between devices: 73 us -> 70.4 us
    ppermute x26, waiting for transfers between devices: 73 us -> 70.4 us  [swap(): return lax.ppermute(value, axis, [(i, i ^ bit) for i in range(size)])]
    pallas_call x5 -> x6, Pallas kernels: 11.3 us -> 11.3 us  [kernel_call(): pl.pallas_call(whole, out_shape=outs, in_specs=spots + [ANY] * len(after)...]
  transfers between devices with their start and end apart: 26 -> 26, of which waited for: 16 -> 19; matrix products, arithmetic and copies ran while one was open for 0% -> 0% of each run, Pallas kernels for 6% -> 7%
where the time goes in v15:
time: 123 us; the launch traced here: 122 us
  waiting for transfers between devices  70.4 us (57%)
  starting transfers between devices  36.7 us (30%)
  Pallas kernels  13.1 us (11%)
    ppermute x26, waiting for transfers between devices, swap(): return lax.ppermute(value, axis, [(i, i ^ bit) for i in range(size)])  70.4 us
    ppermute x26, starting transfers between devices, swap(): return lax.ppermute(value, axis, [(i, i ^ bit) for i in range(size)])  36.7 us
    pallas_call x6, Pallas kernels, kernel_call(): pl.pallas_call(whole, out_shape=outs, in_specs=spots + [ANY] * len(after)...  11.3 us
  transfers between devices with their start and end apart: 26, of which 19 were waited for; matrix products, arithmetic and copies ran while one was open for 0% of the time, Pallas kernels for 7%

profile of v15, /device:TPU:0, one launch (start us, length us, event | category | flops | bytes accessed | tf_op | source)
XLA Modules:
  0.0 122.5 jit_solution(7726968929566288218)
XLA Ops:
  0.7 3.3 %shard_map.87 = (bf16[640,512]{1,0:T(8,128)(2,1)}, bf16[640,1024]{1,0:T(8,128)(2,1)}, bf16[256,512]{1,0:T(8,128)(2,1)}) custom-call(s32[8]{0:T(128)} %refs_0_.1, bf16[3,192,2048]{2,1,0:T(8,128)(2,1)} %refs_1_.2, bf16[256,2048]{1,0:T(8,128)(2,1)} %refs_4_.3, bf16[1024,1024]{1,0:T(8,128)(2,1)} %refs_1_.3, bf16[512,512]{1,0:T(8,128)(2,1)} %refs_2_.3, ...), custom_call_target="tpu_custom_call" | custom-call | tf_op jit(solution)/shard_map/pallas_call | solution.py:130
  4.0 0.5 collective-permute-start
  4.5 2.6 %collective-permute-start.3 = (bf16[640,512]{1,0:T(8,128)(2,1)}, bf16[640,512]{1,0:T(8,128)(2,1)S(1)}, u32[]{:S(2)}, u32[]{:S(2)}) collective-permute-start(bf16[640,512]{1,0:T(8,128)(2,1)} %get-tuple-element.39.refs_0_), channel_id=1, source_target_pairs={{0,4},{4,0},{8,12},{12,8},{1,5},{5,1},{9,13},{13,9},{2,6},{6,2},{1... | collective-permute-start | bytes 1966088 | tf_op jit(solution)/shard_map/ppermute | solution.py:116
  7.2 2.6 %collective-permute-start.5 = (bf16[640,512]{1,0:T(8,128)(2,1)}, bf16[640,512]{1,0:T(8,128)(2,1)S(1)}, u32[]{:S(2)}, u32[]{:S(2)}) collective-permute-start(bf16[640,512]{1,0:T(8,128)(2,1)} %get-tuple-element.39.refs_0_), channel_id=1, source_target_pairs={{0,8},{4,12},{8,0},{12,4},{1,9},{5,13},{9,1},{13,5},{2,10},{6,14},... | collective-permute-start | bytes 1966088 | tf_op jit(solution)/shard_map/ppermute | solution.py:116
  10.1 0.6 collective-permute-start.1
  10.9 1.5 %collective-permute-start.2 = (bf16[640,512]{1,0:T(8,128)(2,1)S(1)}, bf16[640,512]{1,0:T(8,128)(2,1)S(1)}, u32[]{:S(2)}, u32[]{:S(2)}) collective-permute-start(bf16[640,512]{1,0:T(8,128)(2,1)S(1)} %copy-done.4), channel_id=1, source_target_pairs={{0,2},{2,0},{1,3},{3,1},{4,6},{6,4},{5,7},{7,5},{8,10},{10,8},{9,1... | collective-permute-start | bytes 1966088 | tf_op jit(solution)/shard_map/ppermute | solution.py:116
  12.4 24.5 %collective-permute-done.3.refs_2_ = bf16[640,512]{1,0:T(8,128)(2,1)S(1)} collective-permute-done((bf16[640,512]{1,0:T(8,128)(2,1)}, bf16[640,512]{1,0:T(8,128)(2,1)S(1)}, u32[]{:S(2)}, u32[]{:S(2)}) %collective-permute-start.3) | collective-permute-done | bytes 655392 | tf_op jit(solution)/shard_map/ppermute | solution.py:116
  36.9 1.9 %collective-permute-start.4 = (bf16[640,512]{1,0:T(8,128)(2,1)S(1)}, bf16[640,512]{1,0:T(8,128)(2,1)S(1)}, u32[]{:S(2)}, u32[]{:S(2)}) collective-permute-start(bf16[640,512]{1,0:T(8,128)(2,1)S(1)} %collective-permute-done.3.refs_2_), channel_id=1, source_target_pairs={{0,2},{2,0},{1,3},{3,1},{4,6},{6,4},{5,7},{7,5},{8,10},{10,8},{9,1... | collective-permute-start | bytes 1966088 | tf_op jit(solution)/shard_map/ppermute | solution.py:116
  38.9 1.5 %collective-permute-start.7 = (bf16[640,512]{1,0:T(8,128)(2,1)S(1)}, bf16[640,512]{1,0:T(8,128)(2,1)S(1)}, u32[]{:S(2)}, u32[]{:S(2)}) collective-permute-start(bf16[640,512]{1,0:T(8,128)(2,1)S(1)} %collective-permute-done.5.refs_4_), channel_id=1, source_target_pairs={{0,2},{2,0},{1,3},{3,1},{4,6},{6,4},{5,7},{7,5},{8,10},{10,8},{9,1... | collective-permute-start | bytes 1966088 | tf_op jit(solution)/shard_map/ppermute | solution.py:116
  40.4 3.7 %collective-permute-done.1.refs_9_ = bf16[336,512]{1,0:T(8,128)(2,1)S(1)} collective-permute-done((bf16[336,512]{1,0:T(8,128)(2,1)S(1)}, bf16[336,512]{1,0:T(8,128)(2,1)S(1)}, u32[]{:S(2)}, u32[]{:S(2)}) %collective-permute-start.1) | collective-permute-done | bytes 344096 | tf_op jit(solution)/shard_map/ppermute | solution.py:116
  44.1 1.8 %collective-permute-start.6 = (bf16[640,512]{1,0:T(8,128)(2,1)S(1)}, bf16[640,512]{1,0:T(8,128)(2,1)S(1)}, u32[]{:S(2)}, u32[]{:S(2)}) collective-permute-start(bf16[640,512]{1,0:T(8,128)(2,1)S(1)} %collective-permute-done.5.refs_4_), channel_id=1, source_target_pairs={{0,4},{4,0},{8,12},{12,8},{1,5},{5,1},{9,13},{13,9},{2,6},{6,2},{1... | collective-permute-start | bytes 1966088 | tf_op jit(solution)/shard_map/ppermute | solution.py:116
  45.9 2.5 %collective-permute-start.9 = (bf16[336,512]{1,0:T(8,128)(2,1)S(1)}, bf16[336,512]{1,0:T(8,128)(2,1)S(1)}, u32[]{:S(2)}, u32[]{:S(2)}) collective-permute-start(bf16[336,512]{1,0:T(8,128)(2,1)S(1)} %get-tuple-element.46), channel_id=1, source_target_pairs={{0,8},{4,12},{8,0},{12,4},{1,9},{5,13},{9,1},{13,5},{2,10},{6,14},... | collective-permute-start | bytes 1032200 | tf_op jit(solution)/shard_map/ppermute | solution.py:116
  48.5 6.1 %collective-permute-done.4.refs_3_ = bf16[640,512]{1,0:T(8,128)(2,1)S(1)} collective-permute-done((bf16[640,512]{1,0:T(8,128)(2,1)S(1)}, bf16[640,512]{1,0:T(8,128)(2,1)S(1)}, u32[]{:S(2)}, u32[]{:S(2)}) %collective-permute-start.4) | collective-permute-done | bytes 655392 | tf_op jit(solution)/shard_map/ppermute | solution.py:116
  54.5 1.9 %collective-permute-start.8 = (bf16[336,512]{1,0:T(8,128)(2,1)S(1)}, bf16[336,512]{1,0:T(8,128)(2,1)S(1)}, u32[]{:S(2)}, u32[]{:S(2)}) collective-permute-start(bf16[336,512]{1,0:T(8,128)(2,1)S(1)} %collective-permute-done.1.refs_9_), channel_id=1, source_target_pairs={{0,16},{16,0},{1,17},{17,1},{2,18},{18,2},{3,19},{19,3},{4,20},{20... | collective-permute-start | bytes 1032200 | tf_op jit(solution)/shard_map/ppermute | solution.py:116
  56.4 2.5 %collective-permute-start.11 = (bf16[336,512]{1,0:T(8,128)(2,1)S(1)}, bf16[336,512]{1,0:T(8,128)(2,1)S(1)}, u32[]{:S(2)}, u32[]{:S(2)}) collective-permute-start(bf16[336,512]{1,0:T(8,128)(2,1)S(1)} %get-tuple-element.54), channel_id=1, source_target_pairs={{0,12},{4,8},{8,4},{12,0},{1,13},{5,9},{9,5},{13,1},{2,14},{6,10},... | collective-permute-start | bytes 1032200 | tf_op jit(solution)/shard_map/ppermute | solution.py:116
  58.9 8.2 %collective-permute-done.7.refs_5_ = bf16[640,512]{1,0:T(8,128)(2,1)S(1)} collective-permute-done((bf16[640,512]{1,0:T(8,128)(2,1)S(1)}, bf16[640,512]{1,0:T(8,128)(2,1)S(1)}, u32[]{:S(2)}, u32[]{:S(2)}) %collective-permute-start.7) | collective-permute-done | bytes 655392 | tf_op jit(solution)/shard_map/ppermute | solution.py:116
  67.2 1.4 %collective-permute-done.9.refs_11_ = bf16[336,512]{1,0:T(8,128)(2,1)S(1)} collective-permute-done((bf16[336,512]{1,0:T(8,128)(2,1)S(1)}, bf16[336,512]{1,0:T(8,128)(2,1)S(1)}, u32[]{:S(2)}, u32[]{:S(2)}) %collective-permute-start.9) | collective-permute-done | bytes 344096 | tf_op jit(solution)/shard_map/ppermute | solution.py:116
  68.5 1.5 %collective-permute-start.12 = (bf16[336,512]{1,0:T(8,128)(2,1)S(1)}, bf16[336,512]{1,0:T(8,128)(2,1)S(1)}, u32[]{:S(2)}, u32[]{:S(2)}) collective-permute-start(bf16[336,512]{1,0:T(8,128)(2,1)S(1)} %collective-permute-done.9.refs_11_), channel_id=1, source_target_pairs={{0,16},{16,0},{1,17},{17,1},{2,18},{18,2},{3,19},{19,3},{4,20},{20... | collective-permute-start | bytes 1032200 | tf_op jit(solution)/shard_map/ppermute | solution.py:116
  70.0 1.5 %collective-permute-start.10 = (bf16[640,512]{1,0:T(8,128)(2,1)S(1)}, bf16[640,512]{1,0:T(8,128)(2,1)S(1)}, u32[]{:S(2)}, u32[]{:S(2)}) collective-permute-start(bf16[640,512]{1,0:T(8,128)(2,1)S(1)} %collective-permute-done.6.refs_6_), channel_id=1, source_target_pairs={{0,2},{2,0},{1,3},{3,1},{4,6},{6,4},{5,7},{7,5},{8,10},{10,8},{9,1... | collective-permute-start | bytes 1966088 | tf_op jit(solution)/shard_map/ppermute | solution.py:116
  71.5 6.0 %collective-permute-done.11.refs_13_ = bf16[336,512]{1,0:T(8,128)(2,1)S(1)} collective-permute-done((bf16[336,512]{1,0:T(8,128)(2,1)S(1)}, bf16[336,512]{1,0:T(8,128)(2,1)S(1)}, u32[]{:S(2)}, u32[]{:S(2)}) %collective-permute-start.11) | collective-permute-done | bytes 344096 | tf_op jit(solution)/shard_map/ppermute | solution.py:116
  77.5 1.5 %collective-permute-start.13 = (bf16[336,512]{1,0:T(8,128)(2,1)S(1)}, bf16[336,512]{1,0:T(8,128)(2,1)S(1)}, u32[]{:S(2)}, u32[]{:S(2)}) collective-permute-start(bf16[336,512]{1,0:T(8,128)(2,1)S(1)} %collective-permute-done.11.refs_13_), channel_id=1, source_target_pairs={{0,16},{16,0},{1,17},{17,1},{2,18},{18,2},{3,19},{19,3},{4,20},{20... | collective-permute-start | bytes 1032200 | tf_op jit(solution)/shard_map/ppermute | solution.py:116
  79.1 2.6 %collective-permute-start.14 = (bf16[256,512]{1,0:T(8,128)(2,1)S(1)}, bf16[256,512]{1,0:T(8,128)(2,1)S(1)}, u32[]{:S(2)}, u32[]{:S(2)}) collective-permute-start(bf16[256,512]{1,0:T(8,128)(2,1)S(1)} %copy-done.8), channel_id=1, source_target_pairs={{0,8},{4,12},{8,0},{12,4},{1,9},{5,13},{9,1},{13,5},{2,10},{6,14},... | collective-permute-start | bytes 786440 | tf_op jit(solution)/shard_map/ppermute | solution.py:116
  81.7 1.3 %collective-permute-start.15 = (bf16[256,512]{1,0:T(8,128)(2,1)S(1)}, bf16[256,512]{1,0:T(8,128)(2,1)S(1)}, u32[]{:S(2)}, u32[]{:S(2)}) collective-permute-start(bf16[256,512]{1,0:T(8,128)(2,1)S(1)} %copy-done.8), channel_id=1, source_target_pairs={{0,4},{4,0},{8,12},{12,8},{1,5},{5,1},{9,13},{13,9},{2,6},{6,2},{1... | collective-permute-start | bytes 786440 | tf_op jit(solution)/shard_map/ppermute | solution.py:116
  83.0 1.7 %collective-permute-done.10.refs_7_ = bf16[640,512]{1,0:T(8,128)(2,1)S(1)} collective-permute-done((bf16[640,512]{1,0:T(8,128)(2,1)S(1)}, bf16[640,512]{1,0:T(8,128)(2,1)S(1)}, u32[]{:S(2)}, u32[]{:S(2)}) %collective-permute-start.10) | collective-permute-done | bytes 655392 | tf_op jit(solution)/shard_map/ppermute | solution.py:116
  84.6 1.6 %collective-permute-done.13.refs_14_ = bf16[336,512]{1,0:T(8,128)(2,1)S(1)} collective-permute-done((bf16[336,512]{1,0:T(8,128)(2,1)S(1)}, bf16[336,512]{1,0:T(8,128)(2,1)S(1)}, u32[]{:S(2)}, u32[]{:S(2)}) %collective-permute-start.13) | collective-permute-done | bytes 344096 | tf_op jit(solution)/shard_map/ppermute | solution.py:116
  86.2 3.9 %shard_map.89 = (bf16[4,16,256]{2,1,0:T(8,128)(2,1)S(1)}, f32[1280,256]{1,0:T(8,128)}, f32[1280,256]{1,0:T(8,128)S(1)}) custom-call(bf16[640,512]{1,0:T(8,128)(2,1)S(1)} %copy-done.4, bf16[640,512]{1,0:T(8,128)(2,1)S(1)} %collective-permute-done.2.refs_1_, bf16[640,512]{1,0:T(8,128)(2,1)S(1)} %collective-permute-done.3.refs_2_, ...), custom_call_target="tpu_custom_call" | custom-call | tf_op jit(solution)/shard_map/pallas_call | solution.py:130
  90.1 1.2 collective-permute-done.14.refs_7_
  91.7 0.5 collective-permute-start.16
  92.3 1.2 collective-permute-start.21
  93.4 1.1 collective-permute-done.17.refs_3_
  94.6 2.2 %shard_map.90 = (bf16[256,128]{1,0:T(8,128)(2,1)S(1)}, bf16[256,128]{1,0:T(8,128)(2,1)S(1)}, bf16[256,128]{1,0:T(8,128)(2,1)S(1)}, bf16[256,128]{1,0:T(8,128)(2,1)S(1)}) custom-call(f32[1,768]{1,0:T(1,128)S(1)} %fusion.4.refs_0_, bf16[4,16,256]{2,1,0:T(8,128)(2,1)S(1)} %get-tuple-element.62.refs_1_, f32[1280,256]{1,0:T(8,128)S(1)} %get-tuple-element.63.refs_2_, ...), custom_call_target="tpu_custom_call" | custom-call | tf_op jit(solution)/shard_map/pallas_call | solution.py:130
  96.8 0.4 collective-permute-start.18
  97.2 2.6 %collective-permute-start.19 = (bf16[256,128]{1,0:T(8,128)(2,1)S(1)}, bf16[256,128]{1,0:T(8,128)(2,1)S(1)}, u32[]{:S(2)}, u32[]{:S(2)}) collective-permute-start(bf16[256,128]{1,0:T(8,128)(2,1)S(1)} %get-tuple-element.68), channel_id=1, source_target_pairs={{0,8},{4,12},{8,0},{12,4},{1,9},{5,13},{9,1},{13,5},{2,10},{6,14},... | collective-permute-start | bytes 196616 | tf_op jit(solution)/shard_map/ppermute | solution.py:116
  99.8 1.4 %collective-permute-start.20 = (bf16[256,128]{1,0:T(8,128)(2,1)S(1)}, bf16[256,128]{1,0:T(8,128)(2,1)S(1)}, u32[]{:S(2)}, u32[]{:S(2)}) collective-permute-start(bf16[256,128]{1,0:T(8,128)(2,1)S(1)} %get-tuple-element.69), channel_id=1, source_target_pairs={{0,12},{4,8},{8,4},{12,0},{1,13},{5,9},{9,5},{13,1},{2,14},{6,10},... | collective-permute-start | bytes 196616 | tf_op jit(solution)/shard_map/ppermute | solution.py:116
  101.2 0.5 collective-permute-start.22
  101.8 0.8 collective-permute-done.21.refs_9_
  102.6 0.9 collective-permute-done.18.refs_1_
  103.5 1.7 %collective-permute-done.19.refs_2_ = bf16[256,128]{1,0:T(8,128)(2,1)S(1)} collective-permute-done((bf16[256,128]{1,0:T(8,128)(2,1)S(1)}, bf16[256,128]{1,0:T(8,128)(2,1)S(1)}, u32[]{:S(2)}, u32[]{:S(2)}) %collective-permute-start.19) | collective-permute-done | bytes 65568 | tf_op jit(solution)/shard_map/ppermute | solution.py:116
  105.1 1.5 %collective-permute-done.20.refs_3_ = bf16[256,128]{1,0:T(8,128)(2,1)S(1)} collective-permute-done((bf16[256,128]{1,0:T(8,128)(2,1)S(1)}, bf16[256,128]{1,0:T(8,128)(2,1)S(1)}, u32[]{:S(2)}, u32[]{:S(2)}) %collective-permute-start.20) | collective-permute-done | bytes 65568 | tf_op jit(solution)/shard_map/ppermute | solution.py:116
  106.7 0.9 shard_map.91
  107.6 1.2 collective-permute-done.22.refs_2_
  108.8 1.8 %collective-permute-done.23.refs_3_ = bf16[256,512]{1,0:T(8,128)(2,1)S(1)} collective-permute-done((bf16[256,512]{1,0:T(8,128)(2,1)S(1)}, bf16[256,512]{1,0:T(8,128)(2,1)S(1)}, u32[]{:S(2)}, u32[]{:S(2)}) %collective-permute-start.23) | collective-permute-done | bytes 262176 | tf_op jit(solution)/shard_map/ppermute | solution.py:116
  110.5 0.7 shard_map.92
  111.3 1.9 %collective-permute-done.24 = bf16[2,256,512]{2,1,0:T(8,128)(2,1)S(1)} collective-permute-done((bf16[2,256,512]{2,1,0:T(8,128)(2,1)S(1)}, bf16[2,256,512]{2,1,0:T(8,128)(2,1)S(1)}, u32[]{:S(2)}, u32[]{:S(2)}) %collective-permute-start.24) | collective-permute-done | bytes 524320 | tf_op jit(solution)/shard_map/ppermute | solution.py:116
  113.2 1.5 %collective-permute-start.25 = (bf16[256,512]{1,0:T(8,128)(2,1)S(1)}, bf16[256,512]{1,0:T(8,128)(2,1)S(1)}, u32[]{:S(2)}, u32[]{:S(2)}) collective-permute-start(bf16[256,512]{1,0:T(8,128)(2,1)S(1)} %fusion.1), channel_id=1, source_target_pairs={{0,2},{2,0},{1,3},{3,1},{4,6},{6,4},{5,7},{7,5},{8,10},{10,8},{9,1... | collective-permute-start | bytes 786440 | tf_op jit(solution)/shard_map/ppermute | solution.py:116
  114.8 1.8 %shard_map.86 = bf16[192,2048]{1,0:T(8,128)(2,1)} custom-call(s32[8]{0:T(128)S(1)} %copy-done.7, bf16[3,192,2048]{2,1,0:T(8,128)(2,1)S(1)} %copy-done), custom_call_target="tpu_custom_call" | custom-call | tf_op jit(solution)/shard_map/pallas_call | solution.py:169
  116.6 5.0 %collective-permute-done.25 = bf16[256,512]{1,0:T(8,128)(2,1)S(1)} collective-permute-done((bf16[256,512]{1,0:T(8,128)(2,1)S(1)}, bf16[256,512]{1,0:T(8,128)(2,1)S(1)}, u32[]{:S(2)}, u32[]{:S(2)}) %collective-permute-start.25) | collective-permute-done | bytes 262176 | tf_op jit(solution)/shard_map/ppermute | solution.py:116
  121.7 0.8 fusion
  (38 shorter events, 1.3 us)
Async XLA Ops:
  0.6 9.1 %copy-start.2 = (bf16[512,512]{1,0:T(8,128)(2,1)S(1)}, bf16[512,512]{1,0:T(8,128)(2,1)}, u32[]{:S(2)}) copy-start(bf16[512,512]{1,0:T(8,128)(2,1)} %refs_2_.3) | copy-start | bytes 1572868
  0.6 9.1 %copy-start.1 = (bf16[1024,1024]{1,0:T(8,128)(2,1)S(1)}, bf16[1024,1024]{1,0:T(8,128)(2,1)}, u32[]{:S(2)}) copy-start(bf16[1024,1024]{1,0:T(8,128)(2,1)} %refs_1_.3) | copy-start | bytes 6291460
  0.7 9.1 %copy-start.6 = (s32[256]{0:T(256)S(1)}, s32[256]{0:T(256)}, u32[]{:S(2)}) copy-start(s32[256]{0:T(256)} %param.9) | copy-start | bytes 3076
  4.0 5.8 %collective-permute-start = (bf16[640,1024]{1,0:T(8,128)(2,1)}, bf16[640,1024]{1,0:T(8,128)(2,1)S(1)}, u32[]{:S(2)}, u32[]{:S(2)}) collective-permute-start(bf16[640,1024]{1,0:T(8,128)(2,1)} %get-tuple-element.40), channel_id=1, source_target_pairs={{0,1},{1,0},{2,3},{3,2},{4,5},{5,4},{6,7},{7,6},{8,9},{9,8},{10,11... | collective-permute-start | bytes 3932168 | tf_op jit(solution)/shard_map/ppermute | solution.py:116
  4.5 32.4 %collective-permute-start.3 = (bf16[640,512]{1,0:T(8,128)(2,1)}, bf16[640,512]{1,0:T(8,128)(2,1)S(1)}, u32[]{:S(2)}, u32[]{:S(2)}) collective-permute-start(bf16[640,512]{1,0:T(8,128)(2,1)} %get-tuple-element.39.refs_0_), channel_id=1, source_target_pairs={{0,4},{4,0},{8,12},{12,8},{1,5},{5,1},{9,13},{13,9},{2,6},{6,2},{1... | collective-permute-start | bytes 1966088 | tf_op jit(solution)/shard_map/ppermute | solution.py:116
  7.2 31.8 %collective-permute-start.5 = (bf16[640,512]{1,0:T(8,128)(2,1)}, bf16[640,512]{1,0:T(8,128)(2,1)S(1)}, u32[]{:S(2)}, u32[]{:S(2)}) collective-permute-start(bf16[640,512]{1,0:T(8,128)(2,1)} %get-tuple-element.39.refs_0_), channel_id=1, source_target_pairs={{0,8},{4,12},{8,0},{12,4},{1,9},{5,13},{9,1},{13,5},{2,10},{6,14},... | collective-permute-start | bytes 1966088 | tf_op jit(solution)/shard_map/ppermute | solution.py:116
  9.8 1.1 copy-start.4
  9.8 69.3 %copy-start.8 = (bf16[256,512]{1,0:T(8,128)(2,1)S(1)}, bf16[256,512]{1,0:T(8,128)(2,1)}, u32[]{:S(2)}) copy-start(bf16[256,512]{1,0:T(8,128)(2,1)} %get-tuple-element.59) | copy-start | bytes 786436
  10.1 34.1 %collective-permute-start.1 = (bf16[336,512]{1,0:T(8,128)(2,1)S(1)}, bf16[336,512]{1,0:T(8,128)(2,1)S(1)}, u32[]{:S(2)}, u32[]{:S(2)}) collective-permute-start(bf16[336,512]{1,0:T(8,128)(2,1)S(1)} %get-tuple-element.41), channel_id=1, source_target_pairs={{0,4},{4,0},{8,12},{12,8},{1,5},{5,1},{9,13},{13,9},{2,6},{6,2},{1... | collective-permute-start | bytes 1032200 | tf_op jit(solution)/shard_map/ppermute | solution.py:116
  10.9 37.6 %collective-permute-start.2 = (bf16[640,512]{1,0:T(8,128)(2,1)S(1)}, bf16[640,512]{1,0:T(8,128)(2,1)S(1)}, u32[]{:S(2)}, u32[]{:S(2)}) collective-permute-start(bf16[640,512]{1,0:T(8,128)(2,1)S(1)} %copy-done.4), channel_id=1, source_target_pairs={{0,2},{2,0},{1,3},{3,1},{4,6},{6,4},{5,7},{7,5},{8,10},{10,8},{9,1... | collective-permute-start | bytes 1966088 | tf_op jit(solution)/shard_map/ppermute | solution.py:116
  36.9 17.7 %collective-permute-start.4 = (bf16[640,512]{1,0:T(8,128)(2,1)S(1)}, bf16[640,512]{1,0:T(8,128)(2,1)S(1)}, u32[]{:S(2)}, u32[]{:S(2)}) collective-permute-start(bf16[640,512]{1,0:T(8,128)(2,1)S(1)} %collective-permute-done.3.refs_2_), channel_id=1, source_target_pairs={{0,2},{2,0},{1,3},{3,1},{4,6},{6,4},{5,7},{7,5},{8,10},{10,8},{9,1... | collective-permute-start | bytes 1966088 | tf_op jit(solution)/shard_map/ppermute | solution.py:116
  38.9 28.2 %collective-permute-start.7 = (bf16[640,512]{1,0:T(8,128)(2,1)S(1)}, bf16[640,512]{1,0:T(8,128)(2,1)S(1)}, u32[]{:S(2)}, u32[]{:S(2)}) collective-permute-start(bf16[640,512]{1,0:T(8,128)(2,1)S(1)} %collective-permute-done.5.refs_4_), channel_id=1, source_target_pairs={{0,2},{2,0},{1,3},{3,1},{4,6},{6,4},{5,7},{7,5},{8,10},{10,8},{9,1... | collective-permute-start | bytes 1966088 | tf_op jit(solution)/shard_map/ppermute | solution.py:116
  44.1 24.4 %collective-permute-start.6 = (bf16[640,512]{1,0:T(8,128)(2,1)S(1)}, bf16[640,512]{1,0:T(8,128)(2,1)S(1)}, u32[]{:S(2)}, u32[]{:S(2)}) collective-permute-start(bf16[640,512]{1,0:T(8,128)(2,1)S(1)} %collective-permute-done.5.refs_4_), channel_id=1, source_target_pairs={{0,4},{4,0},{8,12},{12,8},{1,5},{5,1},{9,13},{13,9},{2,6},{6,2},{1... | collective-permute-start | bytes 1966088 | tf_op jit(solution)/shard_map/ppermute | solution.py:116
  45.9 22.6 %collective-permute-start.9 = (bf16[336,512]{1,0:T(8,128)(2,1)S(1)}, bf16[336,512]{1,0:T(8,128)(2,1)S(1)}, u32[]{:S(2)}, u32[]{:S(2)}) collective-permute-start(bf16[336,512]{1,0:T(8,128)(2,1)S(1)} %get-tuple-element.46), channel_id=1, source_target_pairs={{0,8},{4,12},{8,0},{12,4},{1,9},{5,13},{9,1},{13,5},{2,10},{6,14},... | collective-permute-start | bytes 1032200 | tf_op jit(solution)/shard_map/ppermute | solution.py:116
  54.5 14.0 %collective-permute-start.8 = (bf16[336,512]{1,0:T(8,128)(2,1)S(1)}, bf16[336,512]{1,0:T(8,128)(2,1)S(1)}, u32[]{:S(2)}, u32[]{:S(2)}) collective-permute-start(bf16[336,512]{1,0:T(8,128)(2,1)S(1)} %collective-permute-done.1.refs_9_), channel_id=1, source_target_pairs={{0,16},{16,0},{1,17},{17,1},{2,18},{18,2},{3,19},{19,3},{4,20},{20... | collective-permute-start | bytes 1032200 | tf_op jit(solution)/shard_map/ppermute | solution.py:116
  56.4 21.1 %collective-permute-start.11 = (bf16[336,512]{1,0:T(8,128)(2,1)S(1)}, bf16[336,512]{1,0:T(8,128)(2,1)S(1)}, u32[]{:S(2)}, u32[]{:S(2)}) collective-permute-start(bf16[336,512]{1,0:T(8,128)(2,1)S(1)} %get-tuple-element.54), channel_id=1, source_target_pairs={{0,12},{4,8},{8,4},{12,0},{1,13},{5,9},{9,5},{13,1},{2,14},{6,10},... | collective-permute-start | bytes 1032200 | tf_op jit(solution)/shard_map/ppermute | solution.py:116
  68.5 9.0 %collective-permute-start.12 = (bf16[336,512]{1,0:T(8,128)(2,1)S(1)}, bf16[336,512]{1,0:T(8,128)(2,1)S(1)}, u32[]{:S(2)}, u32[]{:S(2)}) collective-permute-start(bf16[336,512]{1,0:T(8,128)(2,1)S(1)} %collective-permute-done.9.refs_11_), channel_id=1, source_target_pairs={{0,16},{16,0},{1,17},{17,1},{2,18},{18,2},{3,19},{19,3},{4,20},{20... | collective-permute-start | bytes 1032200 | tf_op jit(solution)/shard_map/ppermute | solution.py:116
  70.0 14.6 %collective-permute-start.10 = (bf16[640,512]{1,0:T(8,128)(2,1)S(1)}, bf16[640,512]{1,0:T(8,128)(2,1)S(1)}, u32[]{:S(2)}, u32[]{:S(2)}) collective-permute-start(bf16[640,512]{1,0:T(8,128)(2,1)S(1)} %collective-permute-done.6.refs_6_), channel_id=1, source_target_pairs={{0,2},{2,0},{1,3},{3,1},{4,6},{6,4},{5,7},{7,5},{8,10},{10,8},{9,1... | collective-permute-start | bytes 1966088 | tf_op jit(solution)/shard_map/ppermute | solution.py:116
  77.5 8.7 %collective-permute-start.13 = (bf16[336,512]{1,0:T(8,128)(2,1)S(1)}, bf16[336,512]{1,0:T(8,128)(2,1)S(1)}, u32[]{:S(2)}, u32[]{:S(2)}) collective-permute-start(bf16[336,512]{1,0:T(8,128)(2,1)S(1)} %collective-permute-done.11.refs_13_), channel_id=1, source_target_pairs={{0,16},{16,0},{1,17},{17,1},{2,18},{18,2},{3,19},{19,3},{4,20},{20... | collective-permute-start | bytes 1032200 | tf_op jit(solution)/shard_map/ppermute | solution.py:116
  79.1 12.3 %collective-permute-start.14 = (bf16[256,512]{1,0:T(8,128)(2,1)S(1)}, bf16[256,512]{1,0:T(8,128)(2,1)S(1)}, u32[]{:S(2)}, u32[]{:S(2)}) collective-permute-start(bf16[256,512]{1,0:T(8,128)(2,1)S(1)} %copy-done.8), channel_id=1, source_target_pairs={{0,8},{4,12},{8,0},{12,4},{1,9},{5,13},{9,1},{13,5},{2,10},{6,14},... | collective-permute-start | bytes 786440 | tf_op jit(solution)/shard_map/ppermute | solution.py:116
  81.7 9.6 %collective-permute-start.15 = (bf16[256,512]{1,0:T(8,128)(2,1)S(1)}, bf16[256,512]{1,0:T(8,128)(2,1)S(1)}, u32[]{:S(2)}, u32[]{:S(2)}) collective-permute-start(bf16[256,512]{1,0:T(8,128)(2,1)S(1)} %copy-done.8), channel_id=1, source_target_pairs={{0,4},{4,0},{8,12},{12,8},{1,5},{5,1},{9,13},{13,9},{2,6},{6,2},{1... | collective-permute-start | bytes 786440 | tf_op jit(solution)/shard_map/ppermute | solution.py:116
  91.3 3.2 %collective-permute-start.17 = (f32[1280,256]{1,0:T(8,128)}, f32[1280,256]{1,0:T(8,128)S(1)}, u32[]{:S(2)}, u32[]{:S(2)}) collective-permute-start(f32[1280,256]{1,0:T(8,128)} %get-tuple-element.64), channel_id=1, source_target_pairs={{0,1},{1,0},{2,3},{3,2},{4,5},{5,4},{6,7},{7,6},{8,9},{9,8},{10,11... | collective-permute-start | bytes 3932168 | tf_op jit(solution)/shard_map/ppermute | solution.py:116
  91.7 9.5 %collective-permute-start.16 = (bf16[256,512]{1,0:T(8,128)(2,1)S(1)}, bf16[256,512]{1,0:T(8,128)(2,1)S(1)}, u32[]{:S(2)}, u32[]{:S(2)}) collective-permute-start(bf16[256,512]{1,0:T(8,128)(2,1)S(1)} %collective-permute-done.14.refs_7_), channel_id=1, source_target_pairs={{0,16},{16,0},{1,17},{17,1},{2,18},{18,2},{3,19},{19,3},{4,20},{20... | collective-permute-start | bytes 786440 | tf_op jit(solution)/shard_map/ppermute | solution.py:116
  92.3 10.3 %collective-permute-start.21 = (bf16[256,512]{1,0:T(8,128)(2,1)S(1)}, bf16[256,512]{1,0:T(8,128)(2,1)S(1)}, u32[]{:S(2)}, u32[]{:S(2)}) collective-permute-start(bf16[256,512]{1,0:T(8,128)(2,1)S(1)} %collective-permute-done.14.refs_7_), channel_id=1, source_target_pairs={{0,4},{4,0},{8,12},{12,8},{1,5},{5,1},{9,13},{13,9},{2,6},{6,2},{1... | collective-permute-start | bytes 786440 | tf_op jit(solution)/shard_map/ppermute | solution.py:116
  94.6 12.1 %copy-start.3 = (bf16[256,2048]{1,0:T(8,128)(2,1)S(1)}, bf16[256,2048]{1,0:T(8,128)(2,1)}, u32[]{:S(2)}) copy-start(bf16[256,2048]{1,0:T(8,128)(2,1)} %refs_4_.3) | copy-start | bytes 3145732
  94.6 12.1 %copy-start.5 = (bf16[512,512]{1,0:T(8,128)(2,1)S(1)}, bf16[512,512]{1,0:T(8,128)(2,1)}, u32[]{:S(2)}) copy-start(bf16[512,512]{1,0:T(8,128)(2,1)} %refs_5_.3) | copy-start | bytes 1572868
  96.8 6.7 %collective-permute-start.18 = (bf16[256,128]{1,0:T(8,128)(2,1)S(1)}, bf16[256,128]{1,0:T(8,128)(2,1)S(1)}, u32[]{:S(2)}, u32[]{:S(2)}) collective-permute-start(bf16[256,128]{1,0:T(8,128)(2,1)S(1)} %get-tuple-element.67), channel_id=1, source_target_pairs={{0,4},{4,0},{8,12},{12,8},{1,5},{5,1},{9,13},{13,9},{2,6},{6,2},{1... | collective-permute-start | bytes 196616 | tf_op jit(solution)/shard_map/ppermute | solution.py:116
  97.2 7.9 %collective-permute-start.19 = (bf16[256,128]{1,0:T(8,128)(2,1)S(1)}, bf16[256,128]{1,0:T(8,128)(2,1)S(1)}, u32[]{:S(2)}, u32[]{:S(2)}) collective-permute-start(bf16[256,128]{1,0:T(8,128)(2,1)S(1)} %get-tuple-element.68), channel_id=1, source_target_pairs={{0,8},{4,12},{8,0},{12,4},{1,9},{5,13},{9,1},{13,5},{2,10},{6,14},... | collective-permute-start | bytes 196616 | tf_op jit(solution)/shard_map/ppermute | solution.py:116
  99.8 6.8 %collective-permute-start.20 = (bf16[256,128]{1,0:T(8,128)(2,1)S(1)}, bf16[256,128]{1,0:T(8,128)(2,1)S(1)}, u32[]{:S(2)}, u32[]{:S(2)}) collective-permute-start(bf16[256,128]{1,0:T(8,128)(2,1)S(1)} %get-tuple-element.69), channel_id=1, source_target_pairs={{0,12},{4,8},{8,4},{12,0},{1,13},{5,9},{9,5},{13,1},{2,14},{6,10},... | collective-permute-start | bytes 196616 | tf_op jit(solution)/shard_map/ppermute | solution.py:116
  101.2 7.5 %collective-permute-start.22 = (bf16[256,512]{1,0:T(8,128)(2,1)S(1)}, bf16[256,512]{1,0:T(8,128)(2,1)S(1)}, u32[]{:S(2)}, u32[]{:S(2)}) collective-permute-start(bf16[256,512]{1,0:T(8,128)(2,1)S(1)} %collective-permute-done.15.refs_6_), channel_id=1, source_target_pairs={{0,16},{16,0},{1,17},{17,1},{2,18},{18,2},{3,19},{19,3},{4,20},{20... | collective-permute-start | bytes 786440 | tf_op jit(solution)/shard_map/ppermute | solution.py:116
  102.5 8.0 %collective-permute-start.23 = (bf16[256,512]{1,0:T(8,128)(2,1)S(1)}, bf16[256,512]{1,0:T(8,128)(2,1)S(1)}, u32[]{:S(2)}, u32[]{:S(2)}) collective-permute-start(bf16[256,512]{1,0:T(8,128)(2,1)S(1)} %collective-permute-done.16.refs_8_), channel_id=1, source_target_pairs={{0,4},{4,0},{8,12},{12,8},{1,5},{5,1},{9,13},{13,9},{2,6},{6,2},{1... | collective-permute-start | bytes 786440 | tf_op jit(solution)/shard_map/ppermute | solution.py:116
  110.5 4.3 %copy-start = (bf16[3,192,2048]{2,1,0:T(8,128)(2,1)S(1)}, bf16[3,192,2048]{2,1,0:T(8,128)(2,1)}, u32[]{:S(2)}) copy-start(bf16[3,192,2048]{2,1,0:T(8,128)(2,1)} %refs_1_.2) | copy-start | bytes 7077892
  110.5 4.3 %copy-start.7 = (s32[8]{0:T(128)S(1)}, s32[8]{0:T(128)}, u32[]{:S(2)}) copy-start(s32[8]{0:T(128)} %refs_0_.1) | copy-start | bytes 100
  111.2 2.0 %collective-permute-start.24 = (bf16[2,256,512]{2,1,0:T(8,128)(2,1)S(1)}, bf16[2,256,512]{2,1,0:T(8,128)(2,1)S(1)}, u32[]{:S(2)}, u32[]{:S(2)}) collective-permute-start(bf16[2,256,512]{2,1,0:T(8,128)(2,1)S(1)} %get-tuple-element.75), channel_id=1, source_target_pairs={{0,1},{1,0},{2,3},{3,2},{4,5},{5,4},{6,7},{7,6},{8,9},{9,8},{10,11... | collective-permute-start | bytes 1572872 | tf_op jit(solution)/shard_map/ppermute | solution.py:116
  113.2 8.4 %collective-permute-start.25 = (bf16[256,512]{1,0:T(8,128)(2,1)S(1)}, bf16[256,512]{1,0:T(8,128)(2,1)S(1)}, u32[]{:S(2)}, u32[]{:S(2)}) collective-permute-start(bf16[256,512]{1,0:T(8,128)(2,1)S(1)} %fusion.1), channel_id=1, source_target_pairs={{0,2},{2,0},{1,3},{3,1},{4,6},{6,4},{5,7},{7,5},{8,10},{10,8},{9,1... | collective-permute-start | bytes 786440 | tf_op jit(solution)/shard_map/ppermute | solution.py:116

commit v16 on v15

--- a/solution.py
+++ b/solution.py
@@ -303,60 +303,97 @@
         piece_ref[kv_rows + fold :, :] = jnp.broadcast_to(row, spare)
 
 
+def lay_tokens(slot, rows, use_own, own_ref, across_ref, rows_ref, audio_ref):
+    depth, lane = rows_ref.shape[1] // 2, audio_ref.shape[1] // 2
+    audio_rows = own_ref.shape[0] - 2 * rows
+    for used, packed_ref in ((use_own, own_ref), (jnp.logical_not(use_own), across_ref)):
+
+        @pl.when(used)
+        def _():
+            for part in range(2):
+                rows_ref[
+                    slot * rows : (slot + 1) * rows, part * depth : (part + 1) * depth
+                ] = packed_ref[part * rows : (part + 1) * rows, :]
+                audio_ref[
+                    slot * audio_rows : (slot + 1) * audio_rows, part * lane : (part + 1) * lane
+                ] = packed_ref[2 * rows :, part * lane : (part + 1) * lane]
+
+
+def lay_weights(piece_ref, part, group, at, kv_ref, query_ref):
+    kv_half, fold, width = kv_ref.shape[0] // 4, query_ref.shape[0] // 8, query_ref.shape[1]
+    to = pl.ds(pl.multiple_of((2 * part + group) * kv_half, kv_half), kv_half)
+    kv_ref[to, :] = piece_ref[at[0] : at[0] + kv_half, :]
+    for side in range(2):
+        to = pl.ds(pl.multiple_of((4 * part + 2 * group + side) * fold, fold), fold)
+        query_ref[to, :] = piece_ref[at[1] : at[1] + fold, side * width : (side + 1) * width]
+
+
+def half_places():
+    seq_at = lax.axis_index("seq")
+    return seq_at % 2, lax.axis_index("mem") == seq_at // 2, lax.axis_index("grp")
+
+
+def near_body(*refs):
+    packed_refs, (own_w, near_w, near_rest) = refs[:6], refs[6:9]
+    kv_sum, query_sum, kv_ref, query_ref, rows_ref, audio_ref = refs[9:]
+    part, use_own, grp_at = half_places()
+    rows = rows_ref.shape[0] // 3
+    for slot in range(3):
+        lay_tokens(slot, rows, use_own, *packed_refs[2 * slot : 2 * slot + 2], rows_ref, audio_ref)
+    kv_half, fold = kv_ref.shape[0] // 4, query_ref.shape[0] // 8
+    for group in range(2):
+        at = (group * kv_half, 2 * kv_half + group * fold)
+        lay_weights(own_w, part, group, at, kv_ref, query_ref)
+    for group, piece_ref in ((grp_at, near_w), (1 - grp_at, near_rest)):
+        lay_weights(piece_ref, 1 - part, group, (0, kv_half), kv_ref, query_ref)
+    kv_sum[...] = jnp.dot(rows_ref[...], kv_ref[...], preferred_element_type=jnp.float32)
+    query_sum[...] = jnp.dot(audio_ref[...], query_ref[...], preferred_element_type=jnp.float32)
+
+
 def products_body(*refs):
-    packed_refs, weight_refs = refs[:8], refs[8:15]
-    own_align, near_align, align_ref, send_ref, keep_ref, rows_ref, audio_ref, kv_ref, query_ref = refs[15:]
-    seq_at, mem_at, grp_at = (lax.axis_index(name) for name in ("seq", "mem", "grp"))
-    rows, audio_rows = rows_ref.shape[0] // 4, audio_ref.shape[0] // 4
-    depth, lane = rows_ref.shape[1] // 4, audio_ref.shape[1] // 4
-    for at, packed_ref in enumerate(packed_refs):
-        slot, mem = divmod(at, 2)
-        for part in range(2):
-            shard = 2 * (mem_at ^ mem) + part
-            lanes = pl.ds(pl.multiple_of(shard * depth, depth), depth)
-            rows_ref[slot * rows : (slot + 1) * rows, lanes] = packed_ref[
-                part * rows : (part + 1) * rows, :
-            ]
-            lanes = pl.ds(pl.multiple_of(shard * lane, lane), lane)
-            audio_ref[slot * audio_rows : (slot + 1) * audio_rows, lanes] = packed_ref[
-                2 * rows :, part * lane : (part + 1) * lane
-            ]
-    kv_half, fold = depth // 2, lane // 4
-    width = query_ref.shape[1]
-
-    def place(piece_ref, shard, group, kv_at, query_at):
-        to = pl.ds(pl.multiple_of((2 * shard + group) * kv_half, kv_half), kv_half)
-        kv_ref[to, :] = piece_ref[kv_at : kv_at + kv_half, :]
-        for side in range(2):
-            to = pl.ds(pl.multiple_of((4 * shard + 2 * group + side) * fold, fold), fold)
-            query_ref[to, :] = piece_ref[
-                query_at : query_at + fold, side * width : (side + 1) * width
-            ]
-
-    for group in range(2):
-        place(weight_refs[0], seq_at, group, group * kv_half, 2 * kv_half + group * fold)
-    for bit in range(1, 4):
-        place(weight_refs[2 * bit - 1], seq_at ^ bit, grp_at, 0, kv_half)
-        place(weight_refs[2 * bit], seq_at ^ bit, 1 - grp_at, 0, kv_half)
-        if bit > 1:
-            align_ref[bit] = weight_refs[2 * bit - 1][kv_half + fold :, : align_ref.shape[2]]
-    align_ref[1] = near_align[...].astype(align_ref.dtype)
+    packed_refs, piece_refs = refs[:8], refs[8:12]
+    kv_sum, query_sum, near_kv, near_query, own_align, near_align = refs[12:18]
+    align_ref, send_ref, keep_ref = refs[18:21]
+    rows_ref, audio_ref, last_rows, last_audio, kv_ref, query_ref = refs[21:]
+    part, use_own, grp_at = half_places()
+    rows, audio_rows = last_rows.shape[0], last_audio.shape[0]
+    kv_half, fold = kv_ref.shape[0] // 4, query_ref.shape[0] // 8
+    lay_tokens(0, rows, use_own, *packed_refs[6:], last_rows, last_audio)
+    for slot in range(4):
+        across = jnp.logical_not(use_own)
+        lay_tokens(slot, rows, across, *packed_refs[2 * slot : 2 * slot + 2], rows_ref, audio_ref)
+    for at, shard in enumerate((part, 1 - part)):
+        for group, piece_ref in ((grp_at, piece_refs[2 * at]), (1 - grp_at, piece_refs[2 * at + 1])):
+            lay_weights(piece_ref, shard, group, (0, kv_half), kv_ref, query_ref)
     align_ref[0] = jnp.broadcast_to(
         own_align[...].astype(jnp.float32).astype(align_ref.dtype), align_ref.shape[1:]
     )
-
-    count = 4 * rows
+    align_ref[1] = near_align[...].astype(align_ref.dtype)
+    for bit, piece_ref in ((2, piece_refs[0]), (3, piece_refs[2])):
+        align_ref[bit] = piece_ref[kv_half + fold :, : align_ref.shape[2]]
+
+    def product(left, right):
+        return jnp.dot(left[...], right[...], preferred_element_type=jnp.float32)
+
     columns = keep_ref.shape[1]
-    total = jnp.dot(rows_ref[...], kv_ref[...], preferred_element_type=jnp.float32)
-    keep_ref[:count, :] = total[:, :columns]
-    send_ref[:count, :] = total[:, columns:]
-    total = jnp.dot(audio_ref[...], query_ref[...], preferred_element_type=jnp.float32)
-    folded = 2 * audio_rows
-    for side in range(2):
-        at = slice(side * folded, (side + 1) * folded)
+    first, count = 3 * rows, 4 * rows
+    total = product(rows_ref, kv_ref)
+    for at, more in (
+        (slice(0, first), kv_sum[...]),
+        (slice(first, count), product(last_rows, near_kv)),
+    ):
+        keep_ref[at, :] = total[at, :columns] + more[:, :columns]
+        send_ref[at, :] = total[at, columns:] + more[:, columns:]
+    total = product(audio_ref, query_ref)
+    last = product(last_audio, near_query)
+    for slot in range(4):
+        side, half = divmod(slot, 2)
+        more = last if slot == 3 else query_sum[slot * audio_rows : (slot + 1) * audio_rows, :]
+        part_sum = total[slot * audio_rows : (slot + 1) * audio_rows] + more
+        at = slice(count + half * audio_rows, count + (half + 1) * audio_rows)
         to = slice(side * HEAD_DIM, (side + 1) * HEAD_DIM)
-        keep_ref[count:, to] = total[at, :HEAD_DIM]
-        send_ref[count:, to] = total[at, HEAD_DIM:]
+        keep_ref[at, to] = part_sum[:, :HEAD_DIM]
+        send_ref[at, to] = part_sum[:, HEAD_DIM:]
 
 
 def attend(queries, kv_ref, frames_ref, align):
@@ -483,7 +520,7 @@
     tokens = [packed, swap(packed, "seq", 1), swap(packed, "seq", 2)]
     across = [swap(packed, "mem", 1)]
     other = swap(other, "rep", 1)
-    rows = half_depth // 2 + query_quarter // 2
+    rows = (half_depth + query_quarter) // 2
     weight_own, *pieces = kernel_call(
         weight_body,
         [bfloat(2 * rows, 2 * width)] + [bfloat(rows + 16, 2 * width)] * 3,
@@ -503,30 +540,45 @@
     tokens[3], across[2], rest[0], pieces[1] = lax.optimization_barrier(
         (tokens[3], across[2], rest[0], pieces[1])
     )
+    packed_shape = (seq_size * video_rows, 2 * half_depth), (seq_size * audio_rows, half_depth)
+    weight_shape = (2 * half_depth, 2 * width), (half_depth, width)
+    near_sums = kernel_call(
+        near_body,
+        [
+            jax.ShapeDtypeStruct((3 * video_rows, 2 * width), jnp.float32),
+            jax.ShapeDtypeStruct((3 * audio_rows, width), jnp.float32),
+            *(bfloat(*shape) for shape in weight_shape),
+        ],
+        [value for pair in zip(tokens[:3], across) for value in pair]
+        + [weight_own, pieces[0], rest[0]],
+        scratch=[
+            pltpu.VMEM((3 * video_rows, 2 * half_depth), jnp.bfloat16),
+            pltpu.VMEM((3 * audio_rows, half_depth), jnp.bfloat16),
+        ],
+        limit=12,
+        cost=pl.CostEstimate(flops=1000000000, bytes_accessed=1000000, transcendentals=0),
+    )
     across.append(swap(tokens[3], "mem", 1))
     rest.append(swap(pieces[1], "grp", 1))
-    pieces[2], rest[1] = lax.optimization_barrier((pieces[2], rest[1]))
+    pieces[2], rest[1], *near_sums = lax.optimization_barrier((pieces[2], rest[1], *near_sums))
     rest.append(swap(pieces[2], "grp", 1))
 
     out_half, tokens[3] = lax.optimization_barrier((out_half, tokens[3]))
     out_third, out_partner = swap(out_half, "seq", 2), swap(out_half, "seq", 1)
-    weights = [weight_own]
-    for piece, other in zip(pieces, rest):
-        weights += [piece, other]
     rows = seq_size * (video_rows + audio_rows // 2)
     sums = jax.ShapeDtypeStruct((rows, width), jnp.float32)
     aligns, send, keep = kernel_call(
         products_body,
-        [bfloat(4, 16, audio_rows), sums, sums],
-        [value for pair in zip(tokens, across) for value in pair] + weights
-        + [alignment[None], near_align],
+        [bfloat(seq_size, 16, audio_rows), sums, sums],
+        [value for pair in zip(tokens, across) for value in pair]
+        + [pieces[1], rest[1], pieces[2], rest[2], *near_sums, alignment[None], near_align],
         scratch=[
-            pltpu.VMEM((seq_size * video_rows, 4 * half_depth), jnp.bfloat16),
-            pltpu.VMEM((seq_size * audio_rows, 8 * query_quarter), jnp.bfloat16),
-            pltpu.VMEM((4 * half_depth, 2 * width), jnp.bfloat16),
-            pltpu.VMEM((8 * query_quarter, width), jnp.bfloat16),
-        ],
-        limit=15,
+            *(pltpu.VMEM(shape, jnp.bfloat16) for shape in packed_shape),
+            pltpu.VMEM((video_rows, 2 * half_depth), jnp.bfloat16),
+            pltpu.VMEM((audio_rows, half_depth), jnp.bfloat16),
+            *(pltpu.VMEM(shape, jnp.bfloat16) for shape in weight_shape),
+        ],
+        limit=14,
     )
     send, out_third, out_partner = lax.optimization_barrier((send, out_third, out_partner))
     came = swap(send, "rep", 1)

time: 123 us -> 123 us (level)
    pallas_call x6 -> x7, Pallas kernels: 11.3 us -> 11.5 us  [kernel_call(): pl.pallas_call(whole, out_shape=outs, in_specs=spots + [ANY] * len(after)...]
  transfers between devices with their start and end apart: 26 -> 26, of which waited for: 19 -> 19; matrix products, arithmetic and copies ran while one was open for 0% -> 0% of each run, Pallas kernels for 7% -> 8%
where the time goes in v16:
time: 123 us; the launch traced here: 122 us
  waiting for transfers between devices  71 us (58%)
  starting transfers between devices  35.9 us (29%)
  Pallas kernels  13.3 us (11%)
    ppermute x26, waiting for transfers between devices, swap(): return lax.ppermute(value, axis, [(i, i ^ bit) for i in range(size)])  71 us
    ppermute x26, starting transfers between devices, swap(): return lax.ppermute(value, axis, [(i, i ^ bit) for i in range(size)])  35.9 us
    pallas_call x7, Pallas kernels, kernel_call(): pl.pallas_call(whole, out_shape=outs, in_specs=spots + [ANY] * len(after)...  11.5 us
  transfers between devices with their start and end apart: 26, of which 19 were waited for; matrix products, arithmetic and copies ran while one was open for 0% of the time, Pallas kernels for 8%

profile of v16, /device:TPU:0, one launch (start us, length us, event | category | flops | bytes accessed | tf_op | source)
XLA Modules:
  0.0 122.5 jit_solution(10496688093321338113)
XLA Ops:
  0.7 3.3 %shard_map.87 = (bf16[640,512]{1,0:T(8,128)(2,1)}, bf16[640,1024]{1,0:T(8,128)(2,1)}, bf16[256,512]{1,0:T(8,128)(2,1)}) custom-call(s32[8]{0:T(128)} %refs_0_.1, bf16[3,192,2048]{2,1,0:T(8,128)(2,1)} %refs_1_.2, bf16[256,2048]{1,0:T(8,128)(2,1)} %refs_4_.3, bf16[1024,1024]{1,0:T(8,128)(2,1)} %refs_1_.3, bf16[512,512]{1,0:T(8,128)(2,1)} %refs_2_.3, ...), custom_call_target="tpu_custom_call" | custom-call | tf_op jit(solution)/shard_map/pallas_call | solution.py:130
  4.0 0.5 collective-permute-start
  4.5 2.6 %collective-permute-start.3 = (bf16[640,512]{1,0:T(8,128)(2,1)}, bf16[640,512]{1,0:T(8,128)(2,1)S(1)}, u32[]{:S(2)}, u32[]{:S(2)}) collective-permute-start(bf16[640,512]{1,0:T(8,128)(2,1)} %get-tuple-element.47.refs_0_), channel_id=1, source_target_pairs={{0,4},{4,0},{8,12},{12,8},{1,5},{5,1},{9,13},{13,9},{2,6},{6,2},{1... | collective-permute-start | bytes 1966088 | tf_op jit(solution)/shard_map/ppermute | solution.py:116
  7.2 2.6 %collective-permute-start.5 = (bf16[640,512]{1,0:T(8,128)(2,1)}, bf16[640,512]{1,0:T(8,128)(2,1)S(1)}, u32[]{:S(2)}, u32[]{:S(2)}) collective-permute-start(bf16[640,512]{1,0:T(8,128)(2,1)} %get-tuple-element.47.refs_0_), channel_id=1, source_target_pairs={{0,8},{4,12},{8,0},{12,4},{1,9},{5,13},{9,1},{13,5},{2,10},{6,14},... | collective-permute-start | bytes 1966088 | tf_op jit(solution)/shard_map/ppermute | solution.py:116
  10.1 0.6 collective-permute-start.1
  10.9 1.5 %collective-permute-start.2 = (bf16[640,512]{1,0:T(8,128)(2,1)S(1)}, bf16[640,512]{1,0:T(8,128)(2,1)S(1)}, u32[]{:S(2)}, u32[]{:S(2)}) collective-permute-start(bf16[640,512]{1,0:T(8,128)(2,1)S(1)} %copy-done.2), channel_id=1, source_target_pairs={{0,2},{2,0},{1,3},{3,1},{4,6},{6,4},{5,7},{7,5},{8,10},{10,8},{9,1... | collective-permute-start | bytes 1966088 | tf_op jit(solution)/shard_map/ppermute | solution.py:116
  12.4 24.5 %collective-permute-done.3.refs_2_ = bf16[640,512]{1,0:T(8,128)(2,1)S(1)} collective-permute-done((bf16[640,512]{1,0:T(8,128)(2,1)}, bf16[640,512]{1,0:T(8,128)(2,1)S(1)}, u32[]{:S(2)}, u32[]{:S(2)}) %collective-permute-start.3) | collective-permute-done | bytes 655392 | tf_op jit(solution)/shard_map/ppermute | solution.py:116
  36.9 1.9 %collective-permute-start.4 = (bf16[640,512]{1,0:T(8,128)(2,1)S(1)}, bf16[640,512]{1,0:T(8,128)(2,1)S(1)}, u32[]{:S(2)}, u32[]{:S(2)}) collective-permute-start(bf16[640,512]{1,0:T(8,128)(2,1)S(1)} %collective-permute-done.3.refs_2_), channel_id=1, source_target_pairs={{0,2},{2,0},{1,3},{3,1},{4,6},{6,4},{5,7},{7,5},{8,10},{10,8},{9,1... | collective-permute-start | bytes 1966088 | tf_op jit(solution)/shard_map/ppermute | solution.py:116
  38.9 1.5 %collective-permute-start.7 = (bf16[640,512]{1,0:T(8,128)(2,1)S(1)}, bf16[640,512]{1,0:T(8,128)(2,1)S(1)}, u32[]{:S(2)}, u32[]{:S(2)}) collective-permute-start(bf16[640,512]{1,0:T(8,128)(2,1)S(1)} %collective-permute-done.5.refs_4_), channel_id=1, source_target_pairs={{0,2},{2,0},{1,3},{3,1},{4,6},{6,4},{5,7},{7,5},{8,10},{10,8},{9,1... | collective-permute-start | bytes 1966088 | tf_op jit(solution)/shard_map/ppermute | solution.py:116
  40.4 3.7 %collective-permute-done.1.refs_7_ = bf16[336,512]{1,0:T(8,128)(2,1)S(1)} collective-permute-done((bf16[336,512]{1,0:T(8,128)(2,1)S(1)}, bf16[336,512]{1,0:T(8,128)(2,1)S(1)}, u32[]{:S(2)}, u32[]{:S(2)}) %collective-permute-start.1) | collective-permute-done | bytes 344096 | tf_op jit(solution)/shard_map/ppermute | solution.py:116
  44.1 1.8 %collective-permute-start.6 = (bf16[640,512]{1,0:T(8,128)(2,1)S(1)}, bf16[640,512]{1,0:T(8,128)(2,1)S(1)}, u32[]{:S(2)}, u32[]{:S(2)}) collective-permute-start(bf16[640,512]{1,0:T(8,128)(2,1)S(1)} %collective-permute-done.5.refs_4_), channel_id=1, source_target_pairs={{0,4},{4,0},{8,12},{12,8},{1,5},{5,1},{9,13},{13,9},{2,6},{6,2},{1... | collective-permute-start | bytes 1966088 | tf_op jit(solution)/shard_map/ppermute | solution.py:116
  45.9 2.5 %collective-permute-start.9 = (bf16[336,512]{1,0:T(8,128)(2,1)S(1)}, bf16[336,512]{1,0:T(8,128)(2,1)S(1)}, u32[]{:S(2)}, u32[]{:S(2)}) collective-permute-start(bf16[336,512]{1,0:T(8,128)(2,1)S(1)} %get-tuple-element.54), channel_id=1, source_target_pairs={{0,8},{4,12},{8,0},{12,4},{1,9},{5,13},{9,1},{13,5},{2,10},{6,14},... | collective-permute-start | bytes 1032200 | tf_op jit(solution)/shard_map/ppermute | solution.py:116
  48.5 6.1 %collective-permute-done.4.refs_3_ = bf16[640,512]{1,0:T(8,128)(2,1)S(1)} collective-permute-done((bf16[640,512]{1,0:T(8,128)(2,1)S(1)}, bf16[640,512]{1,0:T(8,128)(2,1)S(1)}, u32[]{:S(2)}, u32[]{:S(2)}) %collective-permute-start.4) | collective-permute-done | bytes 655392 | tf_op jit(solution)/shard_map/ppermute | solution.py:116
  54.5 1.9 %collective-permute-start.8 = (bf16[336,512]{1,0:T(8,128)(2,1)S(1)}, bf16[336,512]{1,0:T(8,128)(2,1)S(1)}, u32[]{:S(2)}, u32[]{:S(2)}) collective-permute-start(bf16[336,512]{1,0:T(8,128)(2,1)S(1)} %collective-permute-done.1.refs_7_), channel_id=1, source_target_pairs={{0,16},{16,0},{1,17},{17,1},{2,18},{18,2},{3,19},{19,3},{4,20},{20... | collective-permute-start | bytes 1032200 | tf_op jit(solution)/shard_map/ppermute | solution.py:116
  56.4 2.5 %collective-permute-start.11 = (bf16[336,512]{1,0:T(8,128)(2,1)S(1)}, bf16[336,512]{1,0:T(8,128)(2,1)S(1)}, u32[]{:S(2)}, u32[]{:S(2)}) collective-permute-start(bf16[336,512]{1,0:T(8,128)(2,1)S(1)} %get-tuple-element.60), channel_id=1, source_target_pairs={{0,12},{4,8},{8,4},{12,0},{1,13},{5,9},{9,5},{13,1},{2,14},{6,10},... | collective-permute-start | bytes 1032200 | tf_op jit(solution)/shard_map/ppermute | solution.py:116
  58.9 8.2 %collective-permute-done.7.refs_5_ = bf16[640,512]{1,0:T(8,128)(2,1)S(1)} collective-permute-done((bf16[640,512]{1,0:T(8,128)(2,1)S(1)}, bf16[640,512]{1,0:T(8,128)(2,1)S(1)}, u32[]{:S(2)}, u32[]{:S(2)}) %collective-permute-start.7) | collective-permute-done | bytes 655392 | tf_op jit(solution)/shard_map/ppermute | solution.py:116
  67.2 1.4 %collective-permute-done.9.refs_8_ = bf16[336,512]{1,0:T(8,128)(2,1)S(1)} collective-permute-done((bf16[336,512]{1,0:T(8,128)(2,1)S(1)}, bf16[336,512]{1,0:T(8,128)(2,1)S(1)}, u32[]{:S(2)}, u32[]{:S(2)}) %collective-permute-start.9) | collective-permute-done | bytes 344096 | tf_op jit(solution)/shard_map/ppermute | solution.py:116
  68.5 1.5 %collective-permute-start.12 = (bf16[336,512]{1,0:T(8,128)(2,1)S(1)}, bf16[336,512]{1,0:T(8,128)(2,1)S(1)}, u32[]{:S(2)}, u32[]{:S(2)}) collective-permute-start(bf16[336,512]{1,0:T(8,128)(2,1)S(1)} %collective-permute-done.9.refs_8_), channel_id=1, source_target_pairs={{0,16},{16,0},{1,17},{17,1},{2,18},{18,2},{3,19},{19,3},{4,20},{20... | collective-permute-start | bytes 1032200 | tf_op jit(solution)/shard_map/ppermute | solution.py:116
  70.0 1.5 %collective-permute-start.10 = (bf16[640,512]{1,0:T(8,128)(2,1)S(1)}, bf16[640,512]{1,0:T(8,128)(2,1)S(1)}, u32[]{:S(2)}, u32[]{:S(2)}) collective-permute-start(bf16[640,512]{1,0:T(8,128)(2,1)S(1)} %collective-permute-done.6.refs_6_), channel_id=1, source_target_pairs={{0,2},{2,0},{1,3},{3,1},{4,6},{6,4},{5,7},{7,5},{8,10},{10,8},{9,1... | collective-permute-start | bytes 1966088 | tf_op jit(solution)/shard_map/ppermute | solution.py:116
  71.5 1.2 shard_map.89
  72.7 4.8 %collective-permute-done.11.refs_10_ = bf16[336,512]{1,0:T(8,128)(2,1)S(1)} collective-permute-done((bf16[336,512]{1,0:T(8,128)(2,1)S(1)}, bf16[336,512]{1,0:T(8,128)(2,1)S(1)}, u32[]{:S(2)}, u32[]{:S(2)}) %collective-permute-start.11) | collective-permute-done | bytes 344096 | tf_op jit(solution)/shard_map/ppermute | solution.py:116
  77.5 1.5 %collective-permute-start.13 = (bf16[336,512]{1,0:T(8,128)(2,1)S(1)}, bf16[336,512]{1,0:T(8,128)(2,1)S(1)}, u32[]{:S(2)}, u32[]{:S(2)}) collective-permute-start(bf16[336,512]{1,0:T(8,128)(2,1)S(1)} %collective-permute-done.11.refs_10_), channel_id=1, source_target_pairs={{0,16},{16,0},{1,17},{17,1},{2,18},{18,2},{3,19},{19,3},{4,20},{20... | collective-permute-start | bytes 1032200 | tf_op jit(solution)/shard_map/ppermute | solution.py:116
  79.1 2.6 %collective-permute-start.14 = (bf16[256,512]{1,0:T(8,128)(2,1)S(1)}, bf16[256,512]{1,0:T(8,128)(2,1)S(1)}, u32[]{:S(2)}, u32[]{:S(2)}) collective-permute-start(bf16[256,512]{1,0:T(8,128)(2,1)S(1)} %copy-done.8), channel_id=1, source_target_pairs={{0,8},{4,12},{8,0},{12,4},{1,9},{5,13},{9,1},{13,5},{2,10},{6,14},... | collective-permute-start | bytes 786440 | tf_op jit(solution)/shard_map/ppermute | solution.py:116
  81.7 1.3 %collective-permute-start.15 = (bf16[256,512]{1,0:T(8,128)(2,1)S(1)}, bf16[256,512]{1,0:T(8,128)(2,1)S(1)}, u32[]{:S(2)}, u32[]{:S(2)}) collective-permute-start(bf16[256,512]{1,0:T(8,128)(2,1)S(1)} %copy-done.8), channel_id=1, source_target_pairs={{0,4},{4,0},{8,12},{12,8},{1,5},{5,1},{9,13},{13,9},{2,6},{6,2},{1... | collective-permute-start | bytes 786440 | tf_op jit(solution)/shard_map/ppermute | solution.py:116
  83.0 1.7 %collective-permute-done.10.refs_7_ = bf16[640,512]{1,0:T(8,128)(2,1)S(1)} collective-permute-done((bf16[640,512]{1,0:T(8,128)(2,1)S(1)}, bf16[640,512]{1,0:T(8,128)(2,1)S(1)}, u32[]{:S(2)}, u32[]{:S(2)}) %collective-permute-start.10) | collective-permute-done | bytes 655392 | tf_op jit(solution)/shard_map/ppermute | solution.py:116
  84.6 1.6 %collective-permute-done.13.refs_11_ = bf16[336,512]{1,0:T(8,128)(2,1)S(1)} collective-permute-done((bf16[336,512]{1,0:T(8,128)(2,1)S(1)}, bf16[336,512]{1,0:T(8,128)(2,1)S(1)}, u32[]{:S(2)}, u32[]{:S(2)}) %collective-permute-start.13) | collective-permute-done | bytes 344096 | tf_op jit(solution)/shard_map/ppermute | solution.py:116
  86.2 2.9 %shard_map.90 = (bf16[4,16,256]{2,1,0:T(8,128)(2,1)S(1)}, f32[1280,256]{1,0:T(8,128)}, f32[1280,256]{1,0:T(8,128)S(1)}) custom-call(bf16[640,512]{1,0:T(8,128)(2,1)S(1)} %copy-done.2, bf16[640,512]{1,0:T(8,128)(2,1)S(1)} %collective-permute-done.2.refs_1_, bf16[640,512]{1,0:T(8,128)(2,1)S(1)} %collective-permute-done.3.refs_2_, ...), custom_call_target="tpu_custom_call" | custom-call | tf_op jit(solution)/shard_map/pallas_call | solution.py:130
  89.1 2.2 %collective-permute-done.14.refs_7_ = bf16[256,512]{1,0:T(8,128)(2,1)S(1)} collective-permute-done((bf16[256,512]{1,0:T(8,128)(2,1)S(1)}, bf16[256,512]{1,0:T(8,128)(2,1)S(1)}, u32[]{:S(2)}, u32[]{:S(2)}) %collective-permute-start.14) | collective-permute-done | bytes 262176 | tf_op jit(solution)/shard_map/ppermute | solution.py:116
  91.7 0.5 collective-permute-start.16
  92.6 1.9 %collective-permute-done.17.refs_3_ = f32[1280,256]{1,0:T(8,128)S(1)} collective-permute-done((f32[1280,256]{1,0:T(8,128)}, f32[1280,256]{1,0:T(8,128)S(1)}, u32[]{:S(2)}, u32[]{:S(2)}) %collective-permute-start.17) | collective-permute-done | bytes 1310752 | tf_op jit(solution)/shard_map/ppermute | solution.py:116
  94.6 2.2 %shard_map.91 = (bf16[256,128]{1,0:T(8,128)(2,1)S(1)}, bf16[256,128]{1,0:T(8,128)(2,1)S(1)}, bf16[256,128]{1,0:T(8,128)(2,1)S(1)}, bf16[256,128]{1,0:T(8,128)(2,1)S(1)}) custom-call(f32[1,768]{1,0:T(1,128)S(1)} %fusion.4.refs_0_, bf16[4,16,256]{2,1,0:T(8,128)(2,1)S(1)} %get-tuple-element.78.refs_1_, f32[1280,256]{1,0:T(8,128)S(1)} %get-tuple-element.79.refs_2_, ...), custom_call_target="tpu_custom_call" | custom-call | tf_op jit(solution)/shard_map/pallas_call | solution.py:130
  96.8 0.4 collective-permute-start.18
  97.2 2.6 %collective-permute-start.19 = (bf16[256,128]{1,0:T(8,128)(2,1)S(1)}, bf16[256,128]{1,0:T(8,128)(2,1)S(1)}, u32[]{:S(2)}, u32[]{:S(2)}) collective-permute-start(bf16[256,128]{1,0:T(8,128)(2,1)S(1)} %get-tuple-element.84), channel_id=1, source_target_pairs={{0,8},{4,12},{8,0},{12,4},{1,9},{5,13},{9,1},{13,5},{2,10},{6,14},... | collective-permute-start | bytes 196616 | tf_op jit(solution)/shard_map/ppermute | solution.py:116
  99.8 1.4 %collective-permute-start.20 = (bf16[256,128]{1,0:T(8,128)(2,1)S(1)}, bf16[256,128]{1,0:T(8,128)(2,1)S(1)}, u32[]{:S(2)}, u32[]{:S(2)}) collective-permute-start(bf16[256,128]{1,0:T(8,128)(2,1)S(1)} %get-tuple-element.85), channel_id=1, source_target_pairs={{0,12},{4,8},{8,4},{12,0},{1,13},{5,9},{9,5},{13,1},{2,14},{6,10},... | collective-permute-start | bytes 196616 | tf_op jit(solution)/shard_map/ppermute | solution.py:116
  101.2 0.5 collective-permute-start.22
  101.8 0.8 collective-permute-done.21.refs_9_
  102.6 0.9 collective-permute-done.18.refs_1_
  103.5 1.7 %collective-permute-done.19.refs_2_ = bf16[256,128]{1,0:T(8,128)(2,1)S(1)} collective-permute-done((bf16[256,128]{1,0:T(8,128)(2,1)S(1)}, bf16[256,128]{1,0:T(8,128)(2,1)S(1)}, u32[]{:S(2)}, u32[]{:S(2)}) %collective-permute-start.19) | collective-permute-done | bytes 65568 | tf_op jit(solution)/shard_map/ppermute | solution.py:116
  105.1 1.5 %collective-permute-done.20.refs_3_ = bf16[256,128]{1,0:T(8,128)(2,1)S(1)} collective-permute-done((bf16[256,128]{1,0:T(8,128)(2,1)S(1)}, bf16[256,128]{1,0:T(8,128)(2,1)S(1)}, u32[]{:S(2)}, u32[]{:S(2)}) %collective-permute-start.20) | collective-permute-done | bytes 65568 | tf_op jit(solution)/shard_map/ppermute | solution.py:116
  106.7 0.9 shard_map.92
  107.6 1.2 collective-permute-done.22.refs_2_
  108.8 1.8 %collective-permute-done.23.refs_3_ = bf16[256,512]{1,0:T(8,128)(2,1)S(1)} collective-permute-done((bf16[256,512]{1,0:T(8,128)(2,1)S(1)}, bf16[256,512]{1,0:T(8,128)(2,1)S(1)}, u32[]{:S(2)}, u32[]{:S(2)}) %collective-permute-start.23) | collective-permute-done | bytes 262176 | tf_op jit(solution)/shard_map/ppermute | solution.py:116
  110.5 0.7 shard_map.93
  111.3 1.9 %collective-permute-done.24 = bf16[2,256,512]{2,1,0:T(8,128)(2,1)S(1)} collective-permute-done((bf16[2,256,512]{2,1,0:T(8,128)(2,1)S(1)}, bf16[2,256,512]{2,1,0:T(8,128)(2,1)S(1)}, u32[]{:S(2)}, u32[]{:S(2)}) %collective-permute-start.24) | collective-permute-done | bytes 524320 | tf_op jit(solution)/shard_map/ppermute | solution.py:116
  113.2 1.5 %collective-permute-start.25 = (bf16[256,512]{1,0:T(8,128)(2,1)S(1)}, bf16[256,512]{1,0:T(8,128)(2,1)S(1)}, u32[]{:S(2)}, u32[]{:S(2)}) collective-permute-start(bf16[256,512]{1,0:T(8,128)(2,1)S(1)} %fusion.1), channel_id=1, source_target_pairs={{0,2},{2,0},{1,3},{3,1},{4,6},{6,4},{5,7},{7,5},{8,10},{10,8},{9,1... | collective-permute-start | bytes 786440 | tf_op jit(solution)/shard_map/ppermute | solution.py:116
  114.8 1.8 %shard_map.86 = bf16[192,2048]{1,0:T(8,128)(2,1)} custom-call(s32[8]{0:T(128)S(1)} %copy-done.7, bf16[3,192,2048]{2,1,0:T(8,128)(2,1)S(1)} %copy-done), custom_call_target="tpu_custom_call" | custom-call | tf_op jit(solution)/shard_map/pallas_call | solution.py:169
  116.6 5.0 %collective-permute-done.25 = bf16[256,512]{1,0:T(8,128)(2,1)S(1)} collective-permute-done((bf16[256,512]{1,0:T(8,128)(2,1)S(1)}, bf16[256,512]{1,0:T(8,128)(2,1)S(1)}, u32[]{:S(2)}, u32[]{:S(2)}) %collective-permute-start.25) | collective-permute-done | bytes 262176 | tf_op jit(solution)/shard_map/ppermute | solution.py:116
  121.7 0.8 fusion
  (39 shorter events, 1.6 us)
Async XLA Ops:
  0.6 9.1 %copy-start.3 = (bf16[512,512]{1,0:T(8,128)(2,1)S(1)}, bf16[512,512]{1,0:T(8,128)(2,1)}, u32[]{:S(2)}) copy-start(bf16[512,512]{1,0:T(8,128)(2,1)} %refs_2_.3) | copy-start | bytes 1572868
  0.6 9.1 %copy-start.1 = (bf16[1024,1024]{1,0:T(8,128)(2,1)S(1)}, bf16[1024,1024]{1,0:T(8,128)(2,1)}, u32[]{:S(2)}) copy-start(bf16[1024,1024]{1,0:T(8,128)(2,1)} %refs_1_.3) | copy-start | bytes 6291460
  0.7 9.1 %copy-start.6 = (s32[256]{0:T(256)S(1)}, s32[256]{0:T(256)}, u32[]{:S(2)}) copy-start(s32[256]{0:T(256)} %param.9) | copy-start | bytes 3076
  4.0 5.8 %collective-permute-start = (bf16[640,1024]{1,0:T(8,128)(2,1)}, bf16[640,1024]{1,0:T(8,128)(2,1)S(1)}, u32[]{:S(2)}, u32[]{:S(2)}) collective-permute-start(bf16[640,1024]{1,0:T(8,128)(2,1)} %get-tuple-element.48), channel_id=1, source_target_pairs={{0,1},{1,0},{2,3},{3,2},{4,5},{5,4},{6,7},{7,6},{8,9},{9,8},{10,11... | collective-permute-start | bytes 3932168 | tf_op jit(solution)/shard_map/ppermute | solution.py:116
  4.5 32.4 %collective-permute-start.3 = (bf16[640,512]{1,0:T(8,128)(2,1)}, bf16[640,512]{1,0:T(8,128)(2,1)S(1)}, u32[]{:S(2)}, u32[]{:S(2)}) collective-permute-start(bf16[640,512]{1,0:T(8,128)(2,1)} %get-tuple-element.47.refs_0_), channel_id=1, source_target_pairs={{0,4},{4,0},{8,12},{12,8},{1,5},{5,1},{9,13},{13,9},{2,6},{6,2},{1... | collective-permute-start | bytes 1966088 | tf_op jit(solution)/shard_map/ppermute | solution.py:116
  7.2 31.8 %collective-permute-start.5 = (bf16[640,512]{1,0:T(8,128)(2,1)}, bf16[640,512]{1,0:T(8,128)(2,1)S(1)}, u32[]{:S(2)}, u32[]{:S(2)}) collective-permute-start(bf16[640,512]{1,0:T(8,128)(2,1)} %get-tuple-element.47.refs_0_), channel_id=1, source_target_pairs={{0,8},{4,12},{8,0},{12,4},{1,9},{5,13},{9,1},{13,5},{2,10},{6,14},... | collective-permute-start | bytes 1966088 | tf_op jit(solution)/shard_map/ppermute | solution.py:116
  9.8 1.1 copy-start.2
  10.1 34.1 %collective-permute-start.1 = (bf16[336,512]{1,0:T(8,128)(2,1)S(1)}, bf16[336,512]{1,0:T(8,128)(2,1)S(1)}, u32[]{:S(2)}, u32[]{:S(2)}) collective-permute-start(bf16[336,512]{1,0:T(8,128)(2,1)S(1)} %get-tuple-element.49), channel_id=1, source_target_pairs={{0,4},{4,0},{8,12},{12,8},{1,5},{5,1},{9,13},{13,9},{2,6},{6,2},{1... | collective-permute-start | bytes 1032200 | tf_op jit(solution)/shard_map/ppermute | solution.py:116
  10.9 37.6 %collective-permute-start.2 = (bf16[640,512]{1,0:T(8,128)(2,1)S(1)}, bf16[640,512]{1,0:T(8,128)(2,1)S(1)}, u32[]{:S(2)}, u32[]{:S(2)}) collective-permute-start(bf16[640,512]{1,0:T(8,128)(2,1)S(1)} %copy-done.2), channel_id=1, source_target_pairs={{0,2},{2,0},{1,3},{3,1},{4,6},{6,4},{5,7},{7,5},{8,10},{10,8},{9,1... | collective-permute-start | bytes 1966088 | tf_op jit(solution)/shard_map/ppermute | solution.py:116
  36.9 17.7 %collective-permute-start.4 = (bf16[640,512]{1,0:T(8,128)(2,1)S(1)}, bf16[640,512]{1,0:T(8,128)(2,1)S(1)}, u32[]{:S(2)}, u32[]{:S(2)}) collective-permute-start(bf16[640,512]{1,0:T(8,128)(2,1)S(1)} %collective-permute-done.3.refs_2_), channel_id=1, source_target_pairs={{0,2},{2,0},{1,3},{3,1},{4,6},{6,4},{5,7},{7,5},{8,10},{10,8},{9,1... | collective-permute-start | bytes 1966088 | tf_op jit(solution)/shard_map/ppermute | solution.py:116
  38.9 28.2 %collective-permute-start.7 = (bf16[640,512]{1,0:T(8,128)(2,1)S(1)}, bf16[640,512]{1,0:T(8,128)(2,1)S(1)}, u32[]{:S(2)}, u32[]{:S(2)}) collective-permute-start(bf16[640,512]{1,0:T(8,128)(2,1)S(1)} %collective-permute-done.5.refs_4_), channel_id=1, source_target_pairs={{0,2},{2,0},{1,3},{3,1},{4,6},{6,4},{5,7},{7,5},{8,10},{10,8},{9,1... | collective-permute-start | bytes 1966088 | tf_op jit(solution)/shard_map/ppermute | solution.py:116
  44.1 24.4 %collective-permute-start.6 = (bf16[640,512]{1,0:T(8,128)(2,1)S(1)}, bf16[640,512]{1,0:T(8,128)(2,1)S(1)}, u32[]{:S(2)}, u32[]{:S(2)}) collective-permute-start(bf16[640,512]{1,0:T(8,128)(2,1)S(1)} %collective-permute-done.5.refs_4_), channel_id=1, source_target_pairs={{0,4},{4,0},{8,12},{12,8},{1,5},{5,1},{9,13},{13,9},{2,6},{6,2},{1... | collective-permute-start | bytes 1966088 | tf_op jit(solution)/shard_map/ppermute | solution.py:116
  45.9 22.6 %collective-permute-start.9 = (bf16[336,512]{1,0:T(8,128)(2,1)S(1)}, bf16[336,512]{1,0:T(8,128)(2,1)S(1)}, u32[]{:S(2)}, u32[]{:S(2)}) collective-permute-start(bf16[336,512]{1,0:T(8,128)(2,1)S(1)} %get-tuple-element.54), channel_id=1, source_target_pairs={{0,8},{4,12},{8,0},{12,4},{1,9},{5,13},{9,1},{13,5},{2,10},{6,14},... | collective-permute-start | bytes 1032200 | tf_op jit(solution)/shard_map/ppermute | solution.py:116
  54.5 14.0 %collective-permute-start.8 = (bf16[336,512]{1,0:T(8,128)(2,1)S(1)}, bf16[336,512]{1,0:T(8,128)(2,1)S(1)}, u32[]{:S(2)}, u32[]{:S(2)}) collective-permute-start(bf16[336,512]{1,0:T(8,128)(2,1)S(1)} %collective-permute-done.1.refs_7_), channel_id=1, source_target_pairs={{0,16},{16,0},{1,17},{17,1},{2,18},{18,2},{3,19},{19,3},{4,20},{20... | collective-permute-start | bytes 1032200 | tf_op jit(solution)/shard_map/ppermute | solution.py:116
  56.4 21.1 %collective-permute-start.11 = (bf16[336,512]{1,0:T(8,128)(2,1)S(1)}, bf16[336,512]{1,0:T(8,128)(2,1)S(1)}, u32[]{:S(2)}, u32[]{:S(2)}) collective-permute-start(bf16[336,512]{1,0:T(8,128)(2,1)S(1)} %get-tuple-element.60), channel_id=1, source_target_pairs={{0,12},{4,8},{8,4},{12,0},{1,13},{5,9},{9,5},{13,1},{2,14},{6,10},... | collective-permute-start | bytes 1032200 | tf_op jit(solution)/shard_map/ppermute | solution.py:116
  68.5 9.0 %collective-permute-start.12 = (bf16[336,512]{1,0:T(8,128)(2,1)S(1)}, bf16[336,512]{1,0:T(8,128)(2,1)S(1)}, u32[]{:S(2)}, u32[]{:S(2)}) collective-permute-start(bf16[336,512]{1,0:T(8,128)(2,1)S(1)} %collective-permute-done.9.refs_8_), channel_id=1, source_target_pairs={{0,16},{16,0},{1,17},{17,1},{2,18},{18,2},{3,19},{19,3},{4,20},{20... | collective-permute-start | bytes 1032200 | tf_op jit(solution)/shard_map/ppermute | solution.py:116
  70.0 14.6 %collective-permute-start.10 = (bf16[640,512]{1,0:T(8,128)(2,1)S(1)}, bf16[640,512]{1,0:T(8,128)(2,1)S(1)}, u32[]{:S(2)}, u32[]{:S(2)}) collective-permute-start(bf16[640,512]{1,0:T(8,128)(2,1)S(1)} %collective-permute-done.6.refs_6_), channel_id=1, source_target_pairs={{0,2},{2,0},{1,3},{3,1},{4,6},{6,4},{5,7},{7,5},{8,10},{10,8},{9,1... | collective-permute-start | bytes 1966088 | tf_op jit(solution)/shard_map/ppermute | solution.py:116
  71.5 7.5 %copy-start.8 = (bf16[256,512]{1,0:T(8,128)(2,1)S(1)}, bf16[256,512]{1,0:T(8,128)(2,1)}, u32[]{:S(2)}) copy-start(bf16[256,512]{1,0:T(8,128)(2,1)} %get-tuple-element.75) | copy-start | bytes 786436
  77.5 8.7 %collective-permute-start.13 = (bf16[336,512]{1,0:T(8,128)(2,1)S(1)}, bf16[336,512]{1,0:T(8,128)(2,1)S(1)}, u32[]{:S(2)}, u32[]{:S(2)}) collective-permute-start(bf16[336,512]{1,0:T(8,128)(2,1)S(1)} %collective-permute-done.11.refs_10_), channel_id=1, source_target_pairs={{0,16},{16,0},{1,17},{17,1},{2,18},{18,2},{3,19},{19,3},{4,20},{20... | collective-permute-start | bytes 1032200 | tf_op jit(solution)/shard_map/ppermute | solution.py:116
  79.1 12.3 %collective-permute-start.14 = (bf16[256,512]{1,0:T(8,128)(2,1)S(1)}, bf16[256,512]{1,0:T(8,128)(2,1)S(1)}, u32[]{:S(2)}, u32[]{:S(2)}) collective-permute-start(bf16[256,512]{1,0:T(8,128)(2,1)S(1)} %copy-done.8), channel_id=1, source_target_pairs={{0,8},{4,12},{8,0},{12,4},{1,9},{5,13},{9,1},{13,5},{2,10},{6,14},... | collective-permute-start | bytes 786440 | tf_op jit(solution)/shard_map/ppermute | solution.py:116
  81.7 9.6 %collective-permute-start.15 = (bf16[256,512]{1,0:T(8,128)(2,1)S(1)}, bf16[256,512]{1,0:T(8,128)(2,1)S(1)}, u32[]{:S(2)}, u32[]{:S(2)}) collective-permute-start(bf16[256,512]{1,0:T(8,128)(2,1)S(1)} %copy-done.8), channel_id=1, source_target_pairs={{0,4},{4,0},{8,12},{12,8},{1,5},{5,1},{9,13},{13,9},{2,6},{6,2},{1... | collective-permute-start | bytes 786440 | tf_op jit(solution)/shard_map/ppermute | solution.py:116
  91.3 3.2 %collective-permute-start.17 = (f32[1280,256]{1,0:T(8,128)}, f32[1280,256]{1,0:T(8,128)S(1)}, u32[]{:S(2)}, u32[]{:S(2)}) collective-permute-start(f32[1280,256]{1,0:T(8,128)} %get-tuple-element.80), channel_id=1, source_target_pairs={{0,1},{1,0},{2,3},{3,2},{4,5},{5,4},{6,7},{7,6},{8,9},{9,8},{10,11... | collective-permute-start | bytes 3932168 | tf_op jit(solution)/shard_map/ppermute | solution.py:116
  91.7 9.5 %collective-permute-start.16 = (bf16[256,512]{1,0:T(8,128)(2,1)S(1)}, bf16[256,512]{1,0:T(8,128)(2,1)S(1)}, u32[]{:S(2)}, u32[]{:S(2)}) collective-permute-start(bf16[256,512]{1,0:T(8,128)(2,1)S(1)} %collective-permute-done.14.refs_7_), channel_id=1, source_target_pairs={{0,16},{16,0},{1,17},{17,1},{2,18},{18,2},{3,19},{19,3},{4,20},{20... | collective-permute-start | bytes 786440 | tf_op jit(solution)/shard_map/ppermute | solution.py:116
  92.3 10.3 %collective-permute-start.21 = (bf16[256,512]{1,0:T(8,128)(2,1)S(1)}, bf16[256,512]{1,0:T(8,128)(2,1)S(1)}, u32[]{:S(2)}, u32[]{:S(2)}) collective-permute-start(bf16[256,512]{1,0:T(8,128)(2,1)S(1)} %collective-permute-done.14.refs_7_), channel_id=1, source_target_pairs={{0,4},{4,0},{8,12},{12,8},{1,5},{5,1},{9,13},{13,9},{2,6},{6,2},{1... | collective-permute-start | bytes 786440 | tf_op jit(solution)/shard_map/ppermute | solution.py:116
  94.6 12.1 %copy-start.4 = (bf16[256,2048]{1,0:T(8,128)(2,1)S(1)}, bf16[256,2048]{1,0:T(8,128)(2,1)}, u32[]{:S(2)}) copy-start(bf16[256,2048]{1,0:T(8,128)(2,1)} %refs_4_.3) | copy-start | bytes 3145732
  94.6 12.1 %copy-start.5 = (bf16[512,512]{1,0:T(8,128)(2,1)S(1)}, bf16[512,512]{1,0:T(8,128)(2,1)}, u32[]{:S(2)}) copy-start(bf16[512,512]{1,0:T(8,128)(2,1)} %refs_5_.3) | copy-start | bytes 1572868
  96.8 6.7 %collective-permute-start.18 = (bf16[256,128]{1,0:T(8,128)(2,1)S(1)}, bf16[256,128]{1,0:T(8,128)(2,1)S(1)}, u32[]{:S(2)}, u32[]{:S(2)}) collective-permute-start(bf16[256,128]{1,0:T(8,128)(2,1)S(1)} %get-tuple-element.83), channel_id=1, source_target_pairs={{0,4},{4,0},{8,12},{12,8},{1,5},{5,1},{9,13},{13,9},{2,6},{6,2},{1... | collective-permute-start | bytes 196616 | tf_op jit(solution)/shard_map/ppermute | solution.py:116
  97.2 7.9 %collective-permute-start.19 = (bf16[256,128]{1,0:T(8,128)(2,1)S(1)}, bf16[256,128]{1,0:T(8,128)(2,1)S(1)}, u32[]{:S(2)}, u32[]{:S(2)}) collective-permute-start(bf16[256,128]{1,0:T(8,128)(2,1)S(1)} %get-tuple-element.84), channel_id=1, source_target_pairs={{0,8},{4,12},{8,0},{12,4},{1,9},{5,13},{9,1},{13,5},{2,10},{6,14},... | collective-permute-start | bytes 196616 | tf_op jit(solution)/shard_map/ppermute | solution.py:116
  99.8 6.8 %collective-permute-start.20 = (bf16[256,128]{1,0:T(8,128)(2,1)S(1)}, bf16[256,128]{1,0:T(8,128)(2,1)S(1)}, u32[]{:S(2)}, u32[]{:S(2)}) collective-permute-start(bf16[256,128]{1,0:T(8,128)(2,1)S(1)} %get-tuple-element.85), channel_id=1, source_target_pairs={{0,12},{4,8},{8,4},{12,0},{1,13},{5,9},{9,5},{13,1},{2,14},{6,10},... | collective-permute-start | bytes 196616 | tf_op jit(solution)/shard_map/ppermute | solution.py:116
  101.2 7.5 %collective-permute-start.22 = (bf16[256,512]{1,0:T(8,128)(2,1)S(1)}, bf16[256,512]{1,0:T(8,128)(2,1)S(1)}, u32[]{:S(2)}, u32[]{:S(2)}) collective-permute-start(bf16[256,512]{1,0:T(8,128)(2,1)S(1)} %collective-permute-done.15.refs_6_), channel_id=1, source_target_pairs={{0,16},{16,0},{1,17},{17,1},{2,18},{18,2},{3,19},{19,3},{4,20},{20... | collective-permute-start | bytes 786440 | tf_op jit(solution)/shard_map/ppermute | solution.py:116
  102.6 8.0 %collective-permute-start.23 = (bf16[256,512]{1,0:T(8,128)(2,1)S(1)}, bf16[256,512]{1,0:T(8,128)(2,1)S(1)}, u32[]{:S(2)}, u32[]{:S(2)}) collective-permute-start(bf16[256,512]{1,0:T(8,128)(2,1)S(1)} %collective-permute-done.16.refs_8_), channel_id=1, source_target_pairs={{0,4},{4,0},{8,12},{12,8},{1,5},{5,1},{9,13},{13,9},{2,6},{6,2},{1... | collective-permute-start | bytes 786440 | tf_op jit(solution)/shard_map/ppermute | solution.py:116
  110.5 4.3 %copy-start = (bf16[3,192,2048]{2,1,0:T(8,128)(2,1)S(1)}, bf16[3,192,2048]{2,1,0:T(8,128)(2,1)}, u32[]{:S(2)}) copy-start(bf16[3,192,2048]{2,1,0:T(8,128)(2,1)} %refs_1_.2) | copy-start | bytes 7077892
  110.5 4.3 %copy-start.7 = (s32[8]{0:T(128)S(1)}, s32[8]{0:T(128)}, u32[]{:S(2)}) copy-start(s32[8]{0:T(128)} %refs_0_.1) | copy-start | bytes 100
  111.2 2.0 %collective-permute-start.24 = (bf16[2,256,512]{2,1,0:T(8,128)(2,1)S(1)}, bf16[2,256,512]{2,1,0:T(8,128)(2,1)S(1)}, u32[]{:S(2)}, u32[]{:S(2)}) collective-permute-start(bf16[2,256,512]{2,1,0:T(8,128)(2,1)S(1)} %get-tuple-element.91), channel_id=1, source_target_pairs={{0,1},{1,0},{2,3},{3,2},{4,5},{5,4},{6,7},{7,6},{8,9},{9,8},{10,11... | collective-permute-start | bytes 1572872 | tf_op jit(solution)/shard_map/ppermute | solution.py:116
  113.2 8.4 %collective-permute-start.25 = (bf16[256,512]{1,0:T(8,128)(2,1)S(1)}, bf16[256,512]{1,0:T(8,128)(2,1)S(1)}, u32[]{:S(2)}, u32[]{:S(2)}) collective-permute-start(bf16[256,512]{1,0:T(8,128)(2,1)S(1)} %fusion.1), channel_id=1, source_target_pairs={{0,2},{2,0},{1,3},{3,1},{4,6},{6,4},{5,7},{7,5},{8,10},{10,8},{9,1... | collective-permute-start | bytes 786440 | tf_op jit(solution)/shard_map/ppermute | solution.py:116

commit v17 on v16

--- a/solution.py
+++ b/solution.py
@@ -467,7 +467,7 @@
     total_ref[seq_at ^ place] += residual_ref[...].astype(jnp.float32)
 
 
-def late_out_body(total_ref, late_ref, partner_w, fourth_w, send_ref, keep_ref):
+def late_out_body(total_ref, late_ref, fourth_w, partner_w, send_ref, keep_ref):
     place = lax.axis_index("mem") * 2 + lax.axis_index("rep")
     for bit in range(4):
         slot = lax.axis_index("seq") ^ bit ^ place
@@ -533,12 +533,9 @@
     near_align = pieces[0][rows:, :audio_rows].astype(jnp.float32)
     tokens[2], near_align = lax.optimization_barrier((tokens[2], near_align))
     tokens.append(swap(tokens[2], "seq", 1))
-    pieces[0], across[0], across[1] = lax.optimization_barrier(
-        (pieces[0], across[0], across[1])
-    )
     rest = [swap(pieces[0], "grp", 1)]
-    tokens[3], across[2], rest[0], pieces[1] = lax.optimization_barrier(
-        (tokens[3], across[2], rest[0], pieces[1])
+    tokens[3], rest[0], pieces[1], across[0], across[1], across[2] = lax.optimization_barrier(
+        (tokens[3], rest[0], pieces[1], across[0], across[1], across[2])
     )
     packed_shape = (seq_size * video_rows, 2 * half_depth), (seq_size * audio_rows, half_depth)
     weight_shape = (2 * half_depth, 2 * width), (half_depth, width)
@@ -641,7 +638,7 @@
             bfloat(2, audio_rows, columns),
             jax.ShapeDtypeStruct((2, audio_rows, columns), jnp.float32),
         ],
-        [total, late_heads, partner_rest, fourth_rest],
+        [total, late_heads, fourth_rest, partner_rest],
         limit=5,
     )
     came = swap(send, "rep", 1)

time: 123 us -> 124 us (level)
  starting transfers between devices: 35.9 us -> 37.2 us
    ppermute x26, starting transfers between devices: 35.9 us -> 37.2 us  [swap(): return lax.ppermute(value, axis, [(i, i ^ bit) for i in range(size)])]
  transfers between devices with their start and end apart: 26 -> 26, of which waited for: 19 -> 18; matrix products, arithmetic and copies ran while one was open for 0% -> 0% of each run, Pallas kernels for 8% -> 8%
where the time goes in v17:
time: 124 us
  waiting for transfers between devices  71.4 us (58%)
  starting transfers between devices  37.2 us (30%)
  Pallas kernels  13.3 us (11%)
    ppermute x26, waiting for transfers between devices, swap(): return lax.ppermute(value, axis, [(i, i ^ bit) for i in range(size)])  71.4 us
    ppermute x26, starting transfers between devices, swap(): return lax.ppermute(value, axis, [(i, i ^ bit) for i in range(size)])  37.2 us
    pallas_call x7, Pallas kernels, kernel_call(): pl.pallas_call(whole, out_shape=outs, in_specs=spots + [ANY] * len(after)...  11.5 us
  transfers between devices with their start and end apart: 26, of which 18 were waited for; matrix products, arithmetic and copies ran while one was open for 0% of the time, Pallas kernels for 8%

profile of v17, /device:TPU:0, one launch (start us, length us, event | category | flops | bytes accessed | tf_op | source)
XLA Modules:
  0.0 124.3 jit_solution(14238784002049374914)
XLA Ops:
  0.7 3.3 %shard_map.87 = (bf16[640,512]{1,0:T(8,128)(2,1)}, bf16[640,1024]{1,0:T(8,128)(2,1)}, bf16[256,512]{1,0:T(8,128)(2,1)}) custom-call(s32[8]{0:T(128)} %refs_0_.1, bf16[3,192,2048]{2,1,0:T(8,128)(2,1)} %refs_1_.2, bf16[256,2048]{1,0:T(8,128)(2,1)} %refs_4_.3, bf16[1024,1024]{1,0:T(8,128)(2,1)} %refs_1_.3, bf16[512,512]{1,0:T(8,128)(2,1)} %refs_2_.3, ...), custom_call_target="tpu_custom_call" | custom-call | tf_op jit(solution)/shard_map/pallas_call | solution.py:130
  4.0 0.5 collective-permute-start.1
  4.5 2.6 %collective-permute-start.7 = (bf16[640,512]{1,0:T(8,128)(2,1)}, bf16[640,512]{1,0:T(8,128)(2,1)S(1)}, u32[]{:S(2)}, u32[]{:S(2)}) collective-permute-start(bf16[640,512]{1,0:T(8,128)(2,1)} %get-tuple-element.46.refs_0_), channel_id=1, source_target_pairs={{0,4},{4,0},{8,12},{12,8},{1,5},{5,1},{9,13},{13,9},{2,6},{6,2},{1... | collective-permute-start | bytes 1966088 | tf_op jit(solution)/shard_map/ppermute | solution.py:116
  7.2 2.6 %collective-permute-start = (bf16[640,512]{1,0:T(8,128)(2,1)}, bf16[640,512]{1,0:T(8,128)(2,1)S(1)}, u32[]{:S(2)}, u32[]{:S(2)}) collective-permute-start(bf16[640,512]{1,0:T(8,128)(2,1)} %get-tuple-element.46.refs_0_), channel_id=1, source_target_pairs={{0,8},{4,12},{8,0},{12,4},{1,9},{5,13},{9,1},{13,5},{2,10},{6,14},... | collective-permute-start | bytes 1966088 | tf_op jit(solution)/shard_map/ppermute | solution.py:116
  9.8 0.3 shard_map.88
  10.1 0.6 collective-permute-start.2
  10.9 1.5 %collective-permute-start.6 = (bf16[640,512]{1,0:T(8,128)(2,1)S(1)}, bf16[640,512]{1,0:T(8,128)(2,1)S(1)}, u32[]{:S(2)}, u32[]{:S(2)}) collective-permute-start(bf16[640,512]{1,0:T(8,128)(2,1)S(1)} %copy-done.2), channel_id=1, source_target_pairs={{0,2},{2,0},{1,3},{3,1},{4,6},{6,4},{5,7},{7,5},{8,10},{10,8},{9,1... | collective-permute-start | bytes 1966088 | tf_op jit(solution)/shard_map/ppermute | solution.py:116
  12.4 24.5 %collective-permute-done.7.refs_2_ = bf16[640,512]{1,0:T(8,128)(2,1)S(1)} collective-permute-done((bf16[640,512]{1,0:T(8,128)(2,1)}, bf16[640,512]{1,0:T(8,128)(2,1)S(1)}, u32[]{:S(2)}, u32[]{:S(2)}) %collective-permute-start.7) | collective-permute-done | bytes 655392 | tf_op jit(solution)/shard_map/ppermute | solution.py:116
  36.9 1.9 %collective-permute-start.8 = (bf16[640,512]{1,0:T(8,128)(2,1)S(1)}, bf16[640,512]{1,0:T(8,128)(2,1)S(1)}, u32[]{:S(2)}, u32[]{:S(2)}) collective-permute-start(bf16[640,512]{1,0:T(8,128)(2,1)S(1)} %collective-permute-done.7.refs_2_), channel_id=1, source_target_pairs={{0,2},{2,0},{1,3},{3,1},{4,6},{6,4},{5,7},{7,5},{8,10},{10,8},{9,1... | collective-permute-start | bytes 1966088 | tf_op jit(solution)/shard_map/ppermute | solution.py:116
  38.9 1.5 %collective-permute-start.9 = (bf16[640,512]{1,0:T(8,128)(2,1)S(1)}, bf16[640,512]{1,0:T(8,128)(2,1)S(1)}, u32[]{:S(2)}, u32[]{:S(2)}) collective-permute-start(bf16[640,512]{1,0:T(8,128)(2,1)S(1)} %collective-permute-done.refs_4_), channel_id=1, source_target_pairs={{0,2},{2,0},{1,3},{3,1},{4,6},{6,4},{5,7},{7,5},{8,10},{10,8},{9,1... | collective-permute-start | bytes 1966088 | tf_op jit(solution)/shard_map/ppermute | solution.py:116
  40.4 3.7 %collective-permute-done.2.refs_7_ = bf16[336,512]{1,0:T(8,128)(2,1)S(1)} collective-permute-done((bf16[336,512]{1,0:T(8,128)(2,1)S(1)}, bf16[336,512]{1,0:T(8,128)(2,1)S(1)}, u32[]{:S(2)}, u32[]{:S(2)}) %collective-permute-start.2) | collective-permute-done | bytes 344096 | tf_op jit(solution)/shard_map/ppermute | solution.py:116
  44.1 1.8 %collective-permute-start.3 = (bf16[640,512]{1,0:T(8,128)(2,1)S(1)}, bf16[640,512]{1,0:T(8,128)(2,1)S(1)}, u32[]{:S(2)}, u32[]{:S(2)}) collective-permute-start(bf16[640,512]{1,0:T(8,128)(2,1)S(1)} %collective-permute-done.refs_4_), channel_id=1, source_target_pairs={{0,4},{4,0},{8,12},{12,8},{1,5},{5,1},{9,13},{13,9},{2,6},{6,2},{1... | collective-permute-start | bytes 1966088 | tf_op jit(solution)/shard_map/ppermute | solution.py:116
  45.9 2.5 %collective-permute-start.5 = (bf16[336,512]{1,0:T(8,128)(2,1)S(1)}, bf16[336,512]{1,0:T(8,128)(2,1)S(1)}, u32[]{:S(2)}, u32[]{:S(2)}) collective-permute-start(bf16[336,512]{1,0:T(8,128)(2,1)S(1)} %get-tuple-element.50), channel_id=1, source_target_pairs={{0,8},{4,12},{8,0},{12,4},{1,9},{5,13},{9,1},{13,5},{2,10},{6,14},... | collective-permute-start | bytes 1032200 | tf_op jit(solution)/shard_map/ppermute | solution.py:116
  48.5 1.5 %collective-permute-start.4 = (bf16[336,512]{1,0:T(8,128)(2,1)S(1)}, bf16[336,512]{1,0:T(8,128)(2,1)S(1)}, u32[]{:S(2)}, u32[]{:S(2)}) collective-permute-start(bf16[336,512]{1,0:T(8,128)(2,1)S(1)} %collective-permute-done.2.refs_7_), channel_id=1, source_target_pairs={{0,16},{16,0},{1,17},{17,1},{2,18},{18,2},{3,19},{19,3},{4,20},{20... | collective-permute-start | bytes 1032200 | tf_op jit(solution)/shard_map/ppermute | solution.py:116
  50.0 4.5 %collective-permute-done.8.refs_3_ = bf16[640,512]{1,0:T(8,128)(2,1)S(1)} collective-permute-done((bf16[640,512]{1,0:T(8,128)(2,1)S(1)}, bf16[640,512]{1,0:T(8,128)(2,1)S(1)}, u32[]{:S(2)}, u32[]{:S(2)}) %collective-permute-start.8) | collective-permute-done | bytes 655392 | tf_op jit(solution)/shard_map/ppermute | solution.py:116
  54.5 2.9 %collective-permute-start.11 = (bf16[336,512]{1,0:T(8,128)(2,1)S(1)}, bf16[336,512]{1,0:T(8,128)(2,1)S(1)}, u32[]{:S(2)}, u32[]{:S(2)}) collective-permute-start(bf16[336,512]{1,0:T(8,128)(2,1)S(1)} %get-tuple-element.58), channel_id=1, source_target_pairs={{0,12},{4,8},{8,4},{12,0},{1,13},{5,9},{9,5},{13,1},{2,14},{6,10},... | collective-permute-start | bytes 1032200 | tf_op jit(solution)/shard_map/ppermute | solution.py:116
  57.4 9.7 %collective-permute-done.9.refs_5_ = bf16[640,512]{1,0:T(8,128)(2,1)S(1)} collective-permute-done((bf16[640,512]{1,0:T(8,128)(2,1)S(1)}, bf16[640,512]{1,0:T(8,128)(2,1)S(1)}, u32[]{:S(2)}, u32[]{:S(2)}) %collective-permute-start.9) | collective-permute-done | bytes 655392 | tf_op jit(solution)/shard_map/ppermute | solution.py:116
  67.2 1.4 %collective-permute-done.5.refs_8_ = bf16[336,512]{1,0:T(8,128)(2,1)S(1)} collective-permute-done((bf16[336,512]{1,0:T(8,128)(2,1)S(1)}, bf16[336,512]{1,0:T(8,128)(2,1)S(1)}, u32[]{:S(2)}, u32[]{:S(2)}) %collective-permute-start.5) | collective-permute-done | bytes 344096 | tf_op jit(solution)/shard_map/ppermute | solution.py:116
  68.5 1.5 %collective-permute-start.12 = (bf16[336,512]{1,0:T(8,128)(2,1)S(1)}, bf16[336,512]{1,0:T(8,128)(2,1)S(1)}, u32[]{:S(2)}, u32[]{:S(2)}) collective-permute-start(bf16[336,512]{1,0:T(8,128)(2,1)S(1)} %collective-permute-done.5.refs_8_), channel_id=1, source_target_pairs={{0,16},{16,0},{1,17},{17,1},{2,18},{18,2},{3,19},{19,3},{4,20},{20... | collective-permute-start | bytes 1032200 | tf_op jit(solution)/shard_map/ppermute | solution.py:116
  70.0 1.5 %collective-permute-start.10 = (bf16[640,512]{1,0:T(8,128)(2,1)S(1)}, bf16[640,512]{1,0:T(8,128)(2,1)S(1)}, u32[]{:S(2)}, u32[]{:S(2)}) collective-permute-start(bf16[640,512]{1,0:T(8,128)(2,1)S(1)} %collective-permute-done.3.refs_6_), channel_id=1, source_target_pairs={{0,2},{2,0},{1,3},{3,1},{4,6},{6,4},{5,7},{7,5},{8,10},{10,8},{9,1... | collective-permute-start | bytes 1966088 | tf_op jit(solution)/shard_map/ppermute | solution.py:116
  71.5 1.2 shard_map.89
  72.7 4.8 %collective-permute-done.11.refs_10_ = bf16[336,512]{1,0:T(8,128)(2,1)S(1)} collective-permute-done((bf16[336,512]{1,0:T(8,128)(2,1)S(1)}, bf16[336,512]{1,0:T(8,128)(2,1)S(1)}, u32[]{:S(2)}, u32[]{:S(2)}) %collective-permute-start.11) | collective-permute-done | bytes 344096 | tf_op jit(solution)/shard_map/ppermute | solution.py:116
  77.5 1.5 %collective-permute-start.13 = (bf16[336,512]{1,0:T(8,128)(2,1)S(1)}, bf16[336,512]{1,0:T(8,128)(2,1)S(1)}, u32[]{:S(2)}, u32[]{:S(2)}) collective-permute-start(bf16[336,512]{1,0:T(8,128)(2,1)S(1)} %collective-permute-done.11.refs_10_), channel_id=1, source_target_pairs={{0,16},{16,0},{1,17},{17,1},{2,18},{18,2},{3,19},{19,3},{4,20},{20... | collective-permute-start | bytes 1032200 | tf_op jit(solution)/shard_map/ppermute | solution.py:116
  79.1 2.4 %collective-permute-start.14 = (bf16[256,512]{1,0:T(8,128)(2,1)S(1)}, bf16[256,512]{1,0:T(8,128)(2,1)S(1)}, u32[]{:S(2)}, u32[]{:S(2)}) collective-permute-start(bf16[256,512]{1,0:T(8,128)(2,1)S(1)} %copy-done.8), channel_id=1, source_target_pairs={{0,8},{4,12},{8,0},{12,4},{1,9},{5,13},{9,1},{13,5},{2,10},{6,14},... | collective-permute-start | bytes 786440 | tf_op jit(solution)/shard_map/ppermute | solution.py:116
  81.5 1.5 %collective-permute-start.15 = (bf16[256,512]{1,0:T(8,128)(2,1)S(1)}, bf16[256,512]{1,0:T(8,128)(2,1)S(1)}, u32[]{:S(2)}, u32[]{:S(2)}) collective-permute-start(bf16[256,512]{1,0:T(8,128)(2,1)S(1)} %copy-done.8), channel_id=1, source_target_pairs={{0,4},{4,0},{8,12},{12,8},{1,5},{5,1},{9,13},{13,9},{2,6},{6,2},{1... | collective-permute-start | bytes 786440 | tf_op jit(solution)/shard_map/ppermute | solution.py:116
  83.0 1.7 %collective-permute-done.10.refs_7_ = bf16[640,512]{1,0:T(8,128)(2,1)S(1)} collective-permute-done((bf16[640,512]{1,0:T(8,128)(2,1)S(1)}, bf16[640,512]{1,0:T(8,128)(2,1)S(1)}, u32[]{:S(2)}, u32[]{:S(2)}) %collective-permute-start.10) | collective-permute-done | bytes 655392 | tf_op jit(solution)/shard_map/ppermute | solution.py:116
  84.6 1.6 %collective-permute-done.13.refs_11_ = bf16[336,512]{1,0:T(8,128)(2,1)S(1)} collective-permute-done((bf16[336,512]{1,0:T(8,128)(2,1)S(1)}, bf16[336,512]{1,0:T(8,128)(2,1)S(1)}, u32[]{:S(2)}, u32[]{:S(2)}) %collective-permute-start.13) | collective-permute-done | bytes 344096 | tf_op jit(solution)/shard_map/ppermute | solution.py:116
  86.2 2.9 %shard_map.90 = (bf16[4,16,256]{2,1,0:T(8,128)(2,1)S(1)}, f32[1280,256]{1,0:T(8,128)}, f32[1280,256]{1,0:T(8,128)S(1)}) custom-call(bf16[640,512]{1,0:T(8,128)(2,1)S(1)} %copy-done.2, bf16[640,512]{1,0:T(8,128)(2,1)S(1)} %collective-permute-done.6.refs_1_, bf16[640,512]{1,0:T(8,128)(2,1)S(1)} %collective-permute-done.7.refs_2_, ...), custom_call_target="tpu_custom_call" | custom-call | tf_op jit(solution)/shard_map/pallas_call | solution.py:130
  89.1 2.3 %collective-permute-done.14.refs_7_ = bf16[256,512]{1,0:T(8,128)(2,1)S(1)} collective-permute-done((bf16[256,512]{1,0:T(8,128)(2,1)S(1)}, bf16[256,512]{1,0:T(8,128)(2,1)S(1)}, u32[]{:S(2)}, u32[]{:S(2)}) %collective-permute-start.14) | collective-permute-done | bytes 262176 | tf_op jit(solution)/shard_map/ppermute | solution.py:116
  91.4 1.7 %collective-permute-done.15.refs_6_ = bf16[256,512]{1,0:T(8,128)(2,1)S(1)} collective-permute-done((bf16[256,512]{1,0:T(8,128)(2,1)S(1)}, bf16[256,512]{1,0:T(8,128)(2,1)S(1)}, u32[]{:S(2)}, u32[]{:S(2)}) %collective-permute-start.15) | collective-permute-done | bytes 262176 | tf_op jit(solution)/shard_map/ppermute | solution.py:116
  93.6 0.5 collective-permute-start.16
  94.1 0.4 collective-permute-start.21
  94.5 1.9 %collective-permute-done.17.refs_3_ = f32[1280,256]{1,0:T(8,128)S(1)} collective-permute-done((f32[1280,256]{1,0:T(8,128)}, f32[1280,256]{1,0:T(8,128)S(1)}, u32[]{:S(2)}, u32[]{:S(2)}) %collective-permute-start.17) | collective-permute-done | bytes 1310752 | tf_op jit(solution)/shard_map/ppermute | solution.py:116
  96.4 2.2 %shard_map.91 = (bf16[256,128]{1,0:T(8,128)(2,1)S(1)}, bf16[256,128]{1,0:T(8,128)(2,1)S(1)}, bf16[256,128]{1,0:T(8,128)(2,1)S(1)}, bf16[256,128]{1,0:T(8,128)(2,1)S(1)}) custom-call(f32[1,768]{1,0:T(1,128)S(1)} %fusion.4.refs_0_, bf16[4,16,256]{2,1,0:T(8,128)(2,1)S(1)} %get-tuple-element.76.refs_1_, f32[1280,256]{1,0:T(8,128)S(1)} %get-tuple-element.77.refs_2_, ...), custom_call_target="tpu_custom_call" | custom-call | tf_op jit(solution)/shard_map/pallas_call | solution.py:130
  98.6 0.5 collective-permute-start.18
  99.1 1.1 collective-permute-start.19
  100.1 2.9 %collective-permute-start.20 = (bf16[256,128]{1,0:T(8,128)(2,1)S(1)}, bf16[256,128]{1,0:T(8,128)(2,1)S(1)}, u32[]{:S(2)}, u32[]{:S(2)}) collective-permute-start(bf16[256,128]{1,0:T(8,128)(2,1)S(1)} %get-tuple-element.83), channel_id=1, source_target_pairs={{0,12},{4,8},{8,4},{12,0},{1,13},{5,9},{9,5},{13,1},{2,14},{6,10},... | collective-permute-start | bytes 196616 | tf_op jit(solution)/shard_map/ppermute | solution.py:116
  103.1 0.9 collective-permute-done.21.refs_9_
  103.9 1.8 %collective-permute-start.23 = (bf16[256,512]{1,0:T(8,128)(2,1)S(1)}, bf16[256,512]{1,0:T(8,128)(2,1)S(1)}, u32[]{:S(2)}, u32[]{:S(2)}) collective-permute-start(bf16[256,512]{1,0:T(8,128)(2,1)S(1)} %collective-permute-done.15.refs_6_), channel_id=1, source_target_pairs={{0,16},{16,0},{1,17},{17,1},{2,18},{18,2},{3,19},{19,3},{4,20},{20... | collective-permute-start | bytes 786440 | tf_op jit(solution)/shard_map/ppermute | solution.py:116
  105.7 1.7 %collective-permute-done.19.refs_2_ = bf16[256,128]{1,0:T(8,128)(2,1)S(1)} collective-permute-done((bf16[256,128]{1,0:T(8,128)(2,1)S(1)}, bf16[256,128]{1,0:T(8,128)(2,1)S(1)}, u32[]{:S(2)}, u32[]{:S(2)}) %collective-permute-start.19) | collective-permute-done | bytes 65568 | tf_op jit(solution)/shard_map/ppermute | solution.py:116
  107.4 0.9 shard_map.92
  108.4 4.0 %collective-permute-done.22.refs_2_ = bf16[256,512]{1,0:T(8,128)(2,1)S(1)} collective-permute-done((bf16[256,512]{1,0:T(8,128)(2,1)S(1)}, bf16[256,512]{1,0:T(8,128)(2,1)S(1)}, u32[]{:S(2)}, u32[]{:S(2)}) %collective-permute-start.22) | collective-permute-done | bytes 262176 | tf_op jit(solution)/shard_map/ppermute | solution.py:116
  112.3 0.6 shard_map.93
  113.1 1.9 %collective-permute-done.24 = bf16[2,256,512]{2,1,0:T(8,128)(2,1)S(1)} collective-permute-done((bf16[2,256,512]{2,1,0:T(8,128)(2,1)S(1)}, bf16[2,256,512]{2,1,0:T(8,128)(2,1)S(1)}, u32[]{:S(2)}, u32[]{:S(2)}) %collective-permute-start.24) | collective-permute-done | bytes 524320 | tf_op jit(solution)/shard_map/ppermute | solution.py:116
  115.0 1.6 %collective-permute-start.25 = (bf16[256,512]{1,0:T(8,128)(2,1)S(1)}, bf16[256,512]{1,0:T(8,128)(2,1)S(1)}, u32[]{:S(2)}, u32[]{:S(2)}) collective-permute-start(bf16[256,512]{1,0:T(8,128)(2,1)S(1)} %fusion.1), channel_id=1, source_target_pairs={{0,2},{2,0},{1,3},{3,1},{4,6},{6,4},{5,7},{7,5},{8,10},{10,8},{9,1... | collective-permute-start | bytes 786440 | tf_op jit(solution)/shard_map/ppermute | solution.py:116
  116.6 1.8 %shard_map.86 = bf16[192,2048]{1,0:T(8,128)(2,1)} custom-call(s32[8]{0:T(128)S(1)} %copy-done.7, bf16[3,192,2048]{2,1,0:T(8,128)(2,1)S(1)} %copy-done), custom_call_target="tpu_custom_call" | custom-call | tf_op jit(solution)/shard_map/pallas_call | solution.py:169
  118.4 5.0 %collective-permute-done.25 = bf16[256,512]{1,0:T(8,128)(2,1)S(1)} collective-permute-done((bf16[256,512]{1,0:T(8,128)(2,1)S(1)}, bf16[256,512]{1,0:T(8,128)(2,1)S(1)}, u32[]{:S(2)}, u32[]{:S(2)}) %collective-permute-start.25) | collective-permute-done | bytes 262176 | tf_op jit(solution)/shard_map/ppermute | solution.py:116
  123.5 0.8 fusion
  (39 shorter events, 1.1 us)
Async XLA Ops:
  0.6 9.1 %copy-start.3 = (bf16[512,512]{1,0:T(8,128)(2,1)S(1)}, bf16[512,512]{1,0:T(8,128)(2,1)}, u32[]{:S(2)}) copy-start(bf16[512,512]{1,0:T(8,128)(2,1)} %refs_2_.3) | copy-start | bytes 1572868
  0.6 9.1 %copy-start.1 = (bf16[1024,1024]{1,0:T(8,128)(2,1)S(1)}, bf16[1024,1024]{1,0:T(8,128)(2,1)}, u32[]{:S(2)}) copy-start(bf16[1024,1024]{1,0:T(8,128)(2,1)} %refs_1_.3) | copy-start | bytes 6291460
  0.7 9.1 %copy-start.6 = (s32[256]{0:T(256)S(1)}, s32[256]{0:T(256)}, u32[]{:S(2)}) copy-start(s32[256]{0:T(256)} %param.9) | copy-start | bytes 3076
  4.0 5.8 %collective-permute-start.1 = (bf16[640,1024]{1,0:T(8,128)(2,1)}, bf16[640,1024]{1,0:T(8,128)(2,1)S(1)}, u32[]{:S(2)}, u32[]{:S(2)}) collective-permute-start(bf16[640,1024]{1,0:T(8,128)(2,1)} %get-tuple-element.47), channel_id=1, source_target_pairs={{0,1},{1,0},{2,3},{3,2},{4,5},{5,4},{6,7},{7,6},{8,9},{9,8},{10,11... | collective-permute-start | bytes 3932168 | tf_op jit(solution)/shard_map/ppermute | solution.py:116
  4.5 32.4 %collective-permute-start.7 = (bf16[640,512]{1,0:T(8,128)(2,1)}, bf16[640,512]{1,0:T(8,128)(2,1)S(1)}, u32[]{:S(2)}, u32[]{:S(2)}) collective-permute-start(bf16[640,512]{1,0:T(8,128)(2,1)} %get-tuple-element.46.refs_0_), channel_id=1, source_target_pairs={{0,4},{4,0},{8,12},{12,8},{1,5},{5,1},{9,13},{13,9},{2,6},{6,2},{1... | collective-permute-start | bytes 1966088 | tf_op jit(solution)/shard_map/ppermute | solution.py:116
  7.2 31.8 %collective-permute-start = (bf16[640,512]{1,0:T(8,128)(2,1)}, bf16[640,512]{1,0:T(8,128)(2,1)S(1)}, u32[]{:S(2)}, u32[]{:S(2)}) collective-permute-start(bf16[640,512]{1,0:T(8,128)(2,1)} %get-tuple-element.46.refs_0_), channel_id=1, source_target_pairs={{0,8},{4,12},{8,0},{12,4},{1,9},{5,13},{9,1},{13,5},{2,10},{6,14},... | collective-permute-start | bytes 1966088 | tf_op jit(solution)/shard_map/ppermute | solution.py:116
  9.8 1.1 copy-start.2
  10.1 34.1 %collective-permute-start.2 = (bf16[336,512]{1,0:T(8,128)(2,1)S(1)}, bf16[336,512]{1,0:T(8,128)(2,1)S(1)}, u32[]{:S(2)}, u32[]{:S(2)}) collective-permute-start(bf16[336,512]{1,0:T(8,128)(2,1)S(1)} %get-tuple-element.48), channel_id=1, source_target_pairs={{0,4},{4,0},{8,12},{12,8},{1,5},{5,1},{9,13},{13,9},{2,6},{6,2},{1... | collective-permute-start | bytes 1032200 | tf_op jit(solution)/shard_map/ppermute | solution.py:116
  10.9 37.6 %collective-permute-start.6 = (bf16[640,512]{1,0:T(8,128)(2,1)S(1)}, bf16[640,512]{1,0:T(8,128)(2,1)S(1)}, u32[]{:S(2)}, u32[]{:S(2)}) collective-permute-start(bf16[640,512]{1,0:T(8,128)(2,1)S(1)} %copy-done.2), channel_id=1, source_target_pairs={{0,2},{2,0},{1,3},{3,1},{4,6},{6,4},{5,7},{7,5},{8,10},{10,8},{9,1... | collective-permute-start | bytes 1966088 | tf_op jit(solution)/shard_map/ppermute | solution.py:116
  36.9 17.7 %collective-permute-start.8 = (bf16[640,512]{1,0:T(8,128)(2,1)S(1)}, bf16[640,512]{1,0:T(8,128)(2,1)S(1)}, u32[]{:S(2)}, u32[]{:S(2)}) collective-permute-start(bf16[640,512]{1,0:T(8,128)(2,1)S(1)} %collective-permute-done.7.refs_2_), channel_id=1, source_target_pairs={{0,2},{2,0},{1,3},{3,1},{4,6},{6,4},{5,7},{7,5},{8,10},{10,8},{9,1... | collective-permute-start | bytes 1966088 | tf_op jit(solution)/shard_map/ppermute | solution.py:116
  38.9 28.2 %collective-permute-start.9 = (bf16[640,512]{1,0:T(8,128)(2,1)S(1)}, bf16[640,512]{1,0:T(8,128)(2,1)S(1)}, u32[]{:S(2)}, u32[]{:S(2)}) collective-permute-start(bf16[640,512]{1,0:T(8,128)(2,1)S(1)} %collective-permute-done.refs_4_), channel_id=1, source_target_pairs={{0,2},{2,0},{1,3},{3,1},{4,6},{6,4},{5,7},{7,5},{8,10},{10,8},{9,1... | collective-permute-start | bytes 1966088 | tf_op jit(solution)/shard_map/ppermute | solution.py:116
  44.1 24.4 %collective-permute-start.3 = (bf16[640,512]{1,0:T(8,128)(2,1)S(1)}, bf16[640,512]{1,0:T(8,128)(2,1)S(1)}, u32[]{:S(2)}, u32[]{:S(2)}) collective-permute-start(bf16[640,512]{1,0:T(8,128)(2,1)S(1)} %collective-permute-done.refs_4_), channel_id=1, source_target_pairs={{0,4},{4,0},{8,12},{12,8},{1,5},{5,1},{9,13},{13,9},{2,6},{6,2},{1... | collective-permute-start | bytes 1966088 | tf_op jit(solution)/shard_map/ppermute | solution.py:116
  45.9 22.6 %collective-permute-start.5 = (bf16[336,512]{1,0:T(8,128)(2,1)S(1)}, bf16[336,512]{1,0:T(8,128)(2,1)S(1)}, u32[]{:S(2)}, u32[]{:S(2)}) collective-permute-start(bf16[336,512]{1,0:T(8,128)(2,1)S(1)} %get-tuple-element.50), channel_id=1, source_target_pairs={{0,8},{4,12},{8,0},{12,4},{1,9},{5,13},{9,1},{13,5},{2,10},{6,14},... | collective-permute-start | bytes 1032200 | tf_op jit(solution)/shard_map/ppermute | solution.py:116
  48.5 20.0 %collective-permute-start.4 = (bf16[336,512]{1,0:T(8,128)(2,1)S(1)}, bf16[336,512]{1,0:T(8,128)(2,1)S(1)}, u32[]{:S(2)}, u32[]{:S(2)}) collective-permute-start(bf16[336,512]{1,0:T(8,128)(2,1)S(1)} %collective-permute-done.2.refs_7_), channel_id=1, source_target_pairs={{0,16},{16,0},{1,17},{17,1},{2,18},{18,2},{3,19},{19,3},{4,20},{20... | collective-permute-start | bytes 1032200 | tf_op jit(solution)/shard_map/ppermute | solution.py:116
  54.5 23.0 %collective-permute-start.11 = (bf16[336,512]{1,0:T(8,128)(2,1)S(1)}, bf16[336,512]{1,0:T(8,128)(2,1)S(1)}, u32[]{:S(2)}, u32[]{:S(2)}) collective-permute-start(bf16[336,512]{1,0:T(8,128)(2,1)S(1)} %get-tuple-element.58), channel_id=1, source_target_pairs={{0,12},{4,8},{8,4},{12,0},{1,13},{5,9},{9,5},{13,1},{2,14},{6,10},... | collective-permute-start | bytes 1032200 | tf_op jit(solution)/shard_map/ppermute | solution.py:116
  68.5 9.0 %collective-permute-start.12 = (bf16[336,512]{1,0:T(8,128)(2,1)S(1)}, bf16[336,512]{1,0:T(8,128)(2,1)S(1)}, u32[]{:S(2)}, u32[]{:S(2)}) collective-permute-start(bf16[336,512]{1,0:T(8,128)(2,1)S(1)} %collective-permute-done.5.refs_8_), channel_id=1, source_target_pairs={{0,16},{16,0},{1,17},{17,1},{2,18},{18,2},{3,19},{19,3},{4,20},{20... | collective-permute-start | bytes 1032200 | tf_op jit(solution)/shard_map/ppermute | solution.py:116
  70.0 14.6 %collective-permute-start.10 = (bf16[640,512]{1,0:T(8,128)(2,1)S(1)}, bf16[640,512]{1,0:T(8,128)(2,1)S(1)}, u32[]{:S(2)}, u32[]{:S(2)}) collective-permute-start(bf16[640,512]{1,0:T(8,128)(2,1)S(1)} %collective-permute-done.3.refs_6_), channel_id=1, source_target_pairs={{0,2},{2,0},{1,3},{3,1},{4,6},{6,4},{5,7},{7,5},{8,10},{10,8},{9,1... | collective-permute-start | bytes 1966088 | tf_op jit(solution)/shard_map/ppermute | solution.py:116
  71.5 7.5 %copy-start.8 = (bf16[256,512]{1,0:T(8,128)(2,1)S(1)}, bf16[256,512]{1,0:T(8,128)(2,1)}, u32[]{:S(2)}) copy-start(bf16[256,512]{1,0:T(8,128)(2,1)} %get-tuple-element.73) | copy-start | bytes 786436
  77.5 8.7 %collective-permute-start.13 = (bf16[336,512]{1,0:T(8,128)(2,1)S(1)}, bf16[336,512]{1,0:T(8,128)(2,1)S(1)}, u32[]{:S(2)}, u32[]{:S(2)}) collective-permute-start(bf16[336,512]{1,0:T(8,128)(2,1)S(1)} %collective-permute-done.11.refs_10_), channel_id=1, source_target_pairs={{0,16},{16,0},{1,17},{17,1},{2,18},{18,2},{3,19},{19,3},{4,20},{20... | collective-permute-start | bytes 1032200 | tf_op jit(solution)/shard_map/ppermute | solution.py:116
  79.1 12.3 %collective-permute-start.14 = (bf16[256,512]{1,0:T(8,128)(2,1)S(1)}, bf16[256,512]{1,0:T(8,128)(2,1)S(1)}, u32[]{:S(2)}, u32[]{:S(2)}) collective-permute-start(bf16[256,512]{1,0:T(8,128)(2,1)S(1)} %copy-done.8), channel_id=1, source_target_pairs={{0,8},{4,12},{8,0},{12,4},{1,9},{5,13},{9,1},{13,5},{2,10},{6,14},... | collective-permute-start | bytes 786440 | tf_op jit(solution)/shard_map/ppermute | solution.py:116
  81.5 11.7 %collective-permute-start.15 = (bf16[256,512]{1,0:T(8,128)(2,1)S(1)}, bf16[256,512]{1,0:T(8,128)(2,1)S(1)}, u32[]{:S(2)}, u32[]{:S(2)}) collective-permute-start(bf16[256,512]{1,0:T(8,128)(2,1)S(1)} %copy-done.8), channel_id=1, source_target_pairs={{0,4},{4,0},{8,12},{12,8},{1,5},{5,1},{9,13},{13,9},{2,6},{6,2},{1... | collective-permute-start | bytes 786440 | tf_op jit(solution)/shard_map/ppermute | solution.py:116
  93.1 3.2 %collective-permute-start.17 = (f32[1280,256]{1,0:T(8,128)}, f32[1280,256]{1,0:T(8,128)S(1)}, u32[]{:S(2)}, u32[]{:S(2)}) collective-permute-start(f32[1280,256]{1,0:T(8,128)} %get-tuple-element.78), channel_id=1, source_target_pairs={{0,1},{1,0},{2,3},{3,2},{4,5},{5,4},{6,7},{7,6},{8,9},{9,8},{10,11... | collective-permute-start | bytes 3932168 | tf_op jit(solution)/shard_map/ppermute | solution.py:116
  93.6 9.5 %collective-permute-start.16 = (bf16[256,512]{1,0:T(8,128)(2,1)S(1)}, bf16[256,512]{1,0:T(8,128)(2,1)S(1)}, u32[]{:S(2)}, u32[]{:S(2)}) collective-permute-start(bf16[256,512]{1,0:T(8,128)(2,1)S(1)} %collective-permute-done.14.refs_7_), channel_id=1, source_target_pairs={{0,16},{16,0},{1,17},{17,1},{2,18},{18,2},{3,19},{19,3},{4,20},{20... | collective-permute-start | bytes 786440 | tf_op jit(solution)/shard_map/ppermute | solution.py:116
  94.1 9.9 %collective-permute-start.21 = (bf16[256,512]{1,0:T(8,128)(2,1)S(1)}, bf16[256,512]{1,0:T(8,128)(2,1)S(1)}, u32[]{:S(2)}, u32[]{:S(2)}) collective-permute-start(bf16[256,512]{1,0:T(8,128)(2,1)S(1)} %collective-permute-done.14.refs_7_), channel_id=1, source_target_pairs={{0,4},{4,0},{8,12},{12,8},{1,5},{5,1},{9,13},{13,9},{2,6},{6,2},{1... | collective-permute-start | bytes 786440 | tf_op jit(solution)/shard_map/ppermute | solution.py:116
  96.4 11.0 %copy-start.4 = (bf16[256,2048]{1,0:T(8,128)(2,1)S(1)}, bf16[256,2048]{1,0:T(8,128)(2,1)}, u32[]{:S(2)}) copy-start(bf16[256,2048]{1,0:T(8,128)(2,1)} %refs_4_.3) | copy-start | bytes 3145732
  96.4 11.0 %copy-start.5 = (bf16[512,512]{1,0:T(8,128)(2,1)S(1)}, bf16[512,512]{1,0:T(8,128)(2,1)}, u32[]{:S(2)}) copy-start(bf16[512,512]{1,0:T(8,128)(2,1)} %refs_5_.3) | copy-start | bytes 1572868
  98.6 7.1 %collective-permute-start.18 = (bf16[256,128]{1,0:T(8,128)(2,1)S(1)}, bf16[256,128]{1,0:T(8,128)(2,1)S(1)}, u32[]{:S(2)}, u32[]{:S(2)}) collective-permute-start(bf16[256,128]{1,0:T(8,128)(2,1)S(1)} %get-tuple-element.81), channel_id=1, source_target_pairs={{0,4},{4,0},{8,12},{12,8},{1,5},{5,1},{9,13},{13,9},{2,6},{6,2},{1... | collective-permute-start | bytes 196616 | tf_op jit(solution)/shard_map/ppermute | solution.py:116
  99.1 8.3 %collective-permute-start.19 = (bf16[256,128]{1,0:T(8,128)(2,1)S(1)}, bf16[256,128]{1,0:T(8,128)(2,1)S(1)}, u32[]{:S(2)}, u32[]{:S(2)}) collective-permute-start(bf16[256,128]{1,0:T(8,128)(2,1)S(1)} %get-tuple-element.82), channel_id=1, source_target_pairs={{0,8},{4,12},{8,0},{12,4},{1,9},{5,13},{9,1},{13,5},{2,10},{6,14},... | collective-permute-start | bytes 196616 | tf_op jit(solution)/shard_map/ppermute | solution.py:116
  100.1 7.3 %collective-permute-start.20 = (bf16[256,128]{1,0:T(8,128)(2,1)S(1)}, bf16[256,128]{1,0:T(8,128)(2,1)S(1)}, u32[]{:S(2)}, u32[]{:S(2)}) collective-permute-start(bf16[256,128]{1,0:T(8,128)(2,1)S(1)} %get-tuple-element.83), channel_id=1, source_target_pairs={{0,12},{4,8},{8,4},{12,0},{1,13},{5,9},{9,5},{13,1},{2,14},{6,10},... | collective-permute-start | bytes 196616 | tf_op jit(solution)/shard_map/ppermute | solution.py:116
  103.1 9.3 %collective-permute-start.22 = (bf16[256,512]{1,0:T(8,128)(2,1)S(1)}, bf16[256,512]{1,0:T(8,128)(2,1)S(1)}, u32[]{:S(2)}, u32[]{:S(2)}) collective-permute-start(bf16[256,512]{1,0:T(8,128)(2,1)S(1)} %collective-permute-done.16.refs_8_), channel_id=1, source_target_pairs={{0,4},{4,0},{8,12},{12,8},{1,5},{5,1},{9,13},{13,9},{2,6},{6,2},{1... | collective-permute-start | bytes 786440 | tf_op jit(solution)/shard_map/ppermute | solution.py:116
  103.9 8.4 %collective-permute-start.23 = (bf16[256,512]{1,0:T(8,128)(2,1)S(1)}, bf16[256,512]{1,0:T(8,128)(2,1)S(1)}, u32[]{:S(2)}, u32[]{:S(2)}) collective-permute-start(bf16[256,512]{1,0:T(8,128)(2,1)S(1)} %collective-permute-done.15.refs_6_), channel_id=1, source_target_pairs={{0,16},{16,0},{1,17},{17,1},{2,18},{18,2},{3,19},{19,3},{4,20},{20... | collective-permute-start | bytes 786440 | tf_op jit(solution)/shard_map/ppermute | solution.py:116
  112.3 4.3 %copy-start = (bf16[3,192,2048]{2,1,0:T(8,128)(2,1)S(1)}, bf16[3,192,2048]{2,1,0:T(8,128)(2,1)}, u32[]{:S(2)}) copy-start(bf16[3,192,2048]{2,1,0:T(8,128)(2,1)} %refs_1_.2) | copy-start | bytes 7077892
  112.3 4.3 %copy-start.7 = (s32[8]{0:T(128)S(1)}, s32[8]{0:T(128)}, u32[]{:S(2)}) copy-start(s32[8]{0:T(128)} %refs_0_.1) | copy-start | bytes 100
  113.0 2.0 %collective-permute-start.24 = (bf16[2,256,512]{2,1,0:T(8,128)(2,1)S(1)}, bf16[2,256,512]{2,1,0:T(8,128)(2,1)S(1)}, u32[]{:S(2)}, u32[]{:S(2)}) collective-permute-start(bf16[2,256,512]{2,1,0:T(8,128)(2,1)S(1)} %get-tuple-element.89), channel_id=1, source_target_pairs={{0,1},{1,0},{2,3},{3,2},{4,5},{5,4},{6,7},{7,6},{8,9},{9,8},{10,11... | collective-permute-start | bytes 1572872 | tf_op jit(solution)/shard_map/ppermute | solution.py:116
  115.0 8.4 %collective-permute-start.25 = (bf16[256,512]{1,0:T(8,128)(2,1)S(1)}, bf16[256,512]{1,0:T(8,128)(2,1)S(1)}, u32[]{:S(2)}, u32[]{:S(2)}) collective-permute-start(bf16[256,512]{1,0:T(8,128)(2,1)S(1)} %fusion.1), channel_id=1, source_target_pairs={{0,2},{2,0},{1,3},{3,1},{4,6},{6,4},{5,7},{7,5},{8,10},{10,8},{9,1... | collective-permute-start | bytes 786440 | tf_op jit(solution)/shard_map/ppermute | solution.py:116

commit v18 on v16

--- a/solution.py
+++ b/solution.py
@@ -467,7 +467,7 @@
     total_ref[seq_at ^ place] += residual_ref[...].astype(jnp.float32)
 
 
-def late_out_body(total_ref, late_ref, partner_w, fourth_w, send_ref, keep_ref):
+def late_out_body(total_ref, late_ref, fourth_w, partner_w, send_ref, keep_ref):
     place = lax.axis_index("mem") * 2 + lax.axis_index("rep")
     for bit in range(4):
         slot = lax.axis_index("seq") ^ bit ^ place
@@ -641,7 +641,7 @@
             bfloat(2, audio_rows, columns),
             jax.ShapeDtypeStruct((2, audio_rows, columns), jnp.float32),
         ],
-        [total, late_heads, partner_rest, fourth_rest],
+        [total, late_heads, fourth_rest, partner_rest],
         limit=5,
     )
     came = swap(send, "rep", 1)

time: 123 us -> 123 us (level)
  waiting for transfers between devices: 71 us -> 69.7 us
    ppermute x26, starting transfers between devices: 35.9 us -> 37.1 us  [swap(): return lax.ppermute(value, axis, [(i, i ^ bit) for i in range(size)])]
    ppermute x26, waiting for transfers between devices: 71 us -> 69.7 us  [swap(): return lax.ppermute(value, axis, [(i, i ^ bit) for i in range(size)])]
  transfers between devices with their start and end apart: 26 -> 26, of which waited for: 19 -> 17; matrix products, arithmetic and copies ran while one was open for 0% -> 0% of each run, Pallas kernels for 8% -> 8%
where the time goes in v18:
time: 123 us; the launch traced here: 122 us
  waiting for transfers between devices  69.7 us (57%)
  starting transfers between devices  37.1 us (30%)
  Pallas kernels  13.3 us (11%)
    ppermute x26, waiting for transfers between devices, swap(): return lax.ppermute(value, axis, [(i, i ^ bit) for i in range(size)])  69.7 us
    ppermute x26, starting transfers between devices, swap(): return lax.ppermute(value, axis, [(i, i ^ bit) for i in range(size)])  37.1 us
    pallas_call x7, Pallas kernels, kernel_call(): pl.pallas_call(whole, out_shape=outs, in_specs=spots + [ANY] * len(after)...  11.5 us
  transfers between devices with their start and end apart: 26, of which 17 were waited for; matrix products, arithmetic and copies ran while one was open for 0% of the time, Pallas kernels for 8%

profile of v18, /device:TPU:0, one launch (start us, length us, event | category | flops | bytes accessed | tf_op | source)
XLA Modules:
  0.0 122.5 jit_solution(17148592655018799824)
XLA Ops:
  0.7 3.3 %shard_map.87 = (bf16[640,512]{1,0:T(8,128)(2,1)}, bf16[640,1024]{1,0:T(8,128)(2,1)}, bf16[256,512]{1,0:T(8,128)(2,1)}) custom-call(s32[8]{0:T(128)} %refs_0_.1, bf16[3,192,2048]{2,1,0:T(8,128)(2,1)} %refs_1_.2, bf16[256,2048]{1,0:T(8,128)(2,1)} %refs_4_.3, bf16[1024,1024]{1,0:T(8,128)(2,1)} %refs_1_.3, bf16[512,512]{1,0:T(8,128)(2,1)} %refs_2_.3, ...), custom_call_target="tpu_custom_call" | custom-call | tf_op jit(solution)/shard_map/pallas_call | solution.py:130
  4.0 0.5 collective-permute-start
  4.5 2.6 %collective-permute-start.3 = (bf16[640,512]{1,0:T(8,128)(2,1)}, bf16[640,512]{1,0:T(8,128)(2,1)S(1)}, u32[]{:S(2)}, u32[]{:S(2)}) collective-permute-start(bf16[640,512]{1,0:T(8,128)(2,1)} %get-tuple-element.47.refs_0_), channel_id=1, source_target_pairs={{0,4},{4,0},{8,12},{12,8},{1,5},{5,1},{9,13},{13,9},{2,6},{6,2},{1... | collective-permute-start | bytes 1966088 | tf_op jit(solution)/shard_map/ppermute | solution.py:116
  7.2 2.6 %collective-permute-start.5 = (bf16[640,512]{1,0:T(8,128)(2,1)}, bf16[640,512]{1,0:T(8,128)(2,1)S(1)}, u32[]{:S(2)}, u32[]{:S(2)}) collective-permute-start(bf16[640,512]{1,0:T(8,128)(2,1)} %get-tuple-element.47.refs_0_), channel_id=1, source_target_pairs={{0,8},{4,12},{8,0},{12,4},{1,9},{5,13},{9,1},{13,5},{2,10},{6,14},... | collective-permute-start | bytes 1966088 | tf_op jit(solution)/shard_map/ppermute | solution.py:116
  9.8 0.3 shard_map.88
  10.1 0.6 collective-permute-start.1
  10.9 1.5 %collective-permute-start.2 = (bf16[640,512]{1,0:T(8,128)(2,1)S(1)}, bf16[640,512]{1,0:T(8,128)(2,1)S(1)}, u32[]{:S(2)}, u32[]{:S(2)}) collective-permute-start(bf16[640,512]{1,0:T(8,128)(2,1)S(1)} %copy-done.2), channel_id=1, source_target_pairs={{0,2},{2,0},{1,3},{3,1},{4,6},{6,4},{5,7},{7,5},{8,10},{10,8},{9,1... | collective-permute-start | bytes 1966088 | tf_op jit(solution)/shard_map/ppermute | solution.py:116
  12.4 24.5 %collective-permute-done.3.refs_2_ = bf16[640,512]{1,0:T(8,128)(2,1)S(1)} collective-permute-done((bf16[640,512]{1,0:T(8,128)(2,1)}, bf16[640,512]{1,0:T(8,128)(2,1)S(1)}, u32[]{:S(2)}, u32[]{:S(2)}) %collective-permute-start.3) | collective-permute-done | bytes 655392 | tf_op jit(solution)/shard_map/ppermute | solution.py:116
  36.9 1.9 %collective-permute-start.4 = (bf16[640,512]{1,0:T(8,128)(2,1)S(1)}, bf16[640,512]{1,0:T(8,128)(2,1)S(1)}, u32[]{:S(2)}, u32[]{:S(2)}) collective-permute-start(bf16[640,512]{1,0:T(8,128)(2,1)S(1)} %collective-permute-done.3.refs_2_), channel_id=1, source_target_pairs={{0,2},{2,0},{1,3},{3,1},{4,6},{6,4},{5,7},{7,5},{8,10},{10,8},{9,1... | collective-permute-start | bytes 1966088 | tf_op jit(solution)/shard_map/ppermute | solution.py:116
  38.9 1.5 %collective-permute-start.7 = (bf16[640,512]{1,0:T(8,128)(2,1)S(1)}, bf16[640,512]{1,0:T(8,128)(2,1)S(1)}, u32[]{:S(2)}, u32[]{:S(2)}) collective-permute-start(bf16[640,512]{1,0:T(8,128)(2,1)S(1)} %collective-permute-done.5.refs_4_), channel_id=1, source_target_pairs={{0,2},{2,0},{1,3},{3,1},{4,6},{6,4},{5,7},{7,5},{8,10},{10,8},{9,1... | collective-permute-start | bytes 1966088 | tf_op jit(solution)/shard_map/ppermute | solution.py:116
  40.4 3.7 %collective-permute-done.1.refs_7_ = bf16[336,512]{1,0:T(8,128)(2,1)S(1)} collective-permute-done((bf16[336,512]{1,0:T(8,128)(2,1)S(1)}, bf16[336,512]{1,0:T(8,128)(2,1)S(1)}, u32[]{:S(2)}, u32[]{:S(2)}) %collective-permute-start.1) | collective-permute-done | bytes 344096 | tf_op jit(solution)/shard_map/ppermute | solution.py:116
  44.1 1.8 %collective-permute-start.6 = (bf16[640,512]{1,0:T(8,128)(2,1)S(1)}, bf16[640,512]{1,0:T(8,128)(2,1)S(1)}, u32[]{:S(2)}, u32[]{:S(2)}) collective-permute-start(bf16[640,512]{1,0:T(8,128)(2,1)S(1)} %collective-permute-done.5.refs_4_), channel_id=1, source_target_pairs={{0,4},{4,0},{8,12},{12,8},{1,5},{5,1},{9,13},{13,9},{2,6},{6,2},{1... | collective-permute-start | bytes 1966088 | tf_op jit(solution)/shard_map/ppermute | solution.py:116
  45.9 2.5 %collective-permute-start.9 = (bf16[336,512]{1,0:T(8,128)(2,1)S(1)}, bf16[336,512]{1,0:T(8,128)(2,1)S(1)}, u32[]{:S(2)}, u32[]{:S(2)}) collective-permute-start(bf16[336,512]{1,0:T(8,128)(2,1)S(1)} %get-tuple-element.54), channel_id=1, source_target_pairs={{0,8},{4,12},{8,0},{12,4},{1,9},{5,13},{9,1},{13,5},{2,10},{6,14},... | collective-permute-start | bytes 1032200 | tf_op jit(solution)/shard_map/ppermute | solution.py:116
  48.5 6.1 %collective-permute-done.4.refs_3_ = bf16[640,512]{1,0:T(8,128)(2,1)S(1)} collective-permute-done((bf16[640,512]{1,0:T(8,128)(2,1)S(1)}, bf16[640,512]{1,0:T(8,128)(2,1)S(1)}, u32[]{:S(2)}, u32[]{:S(2)}) %collective-permute-start.4) | collective-permute-done | bytes 655392 | tf_op jit(solution)/shard_map/ppermute | solution.py:116
  54.5 1.9 %collective-permute-start.8 = (bf16[336,512]{1,0:T(8,128)(2,1)S(1)}, bf16[336,512]{1,0:T(8,128)(2,1)S(1)}, u32[]{:S(2)}, u32[]{:S(2)}) collective-permute-start(bf16[336,512]{1,0:T(8,128)(2,1)S(1)} %collective-permute-done.1.refs_7_), channel_id=1, source_target_pairs={{0,16},{16,0},{1,17},{17,1},{2,18},{18,2},{3,19},{19,3},{4,20},{20... | collective-permute-start | bytes 1032200 | tf_op jit(solution)/shard_map/ppermute | solution.py:116
  56.4 2.5 %collective-permute-start.11 = (bf16[336,512]{1,0:T(8,128)(2,1)S(1)}, bf16[336,512]{1,0:T(8,128)(2,1)S(1)}, u32[]{:S(2)}, u32[]{:S(2)}) collective-permute-start(bf16[336,512]{1,0:T(8,128)(2,1)S(1)} %get-tuple-element.60), channel_id=1, source_target_pairs={{0,12},{4,8},{8,4},{12,0},{1,13},{5,9},{9,5},{13,1},{2,14},{6,10},... | collective-permute-start | bytes 1032200 | tf_op jit(solution)/shard_map/ppermute | solution.py:116
  58.9 8.2 %collective-permute-done.7.refs_5_ = bf16[640,512]{1,0:T(8,128)(2,1)S(1)} collective-permute-done((bf16[640,512]{1,0:T(8,128)(2,1)S(1)}, bf16[640,512]{1,0:T(8,128)(2,1)S(1)}, u32[]{:S(2)}, u32[]{:S(2)}) %collective-permute-start.7) | collective-permute-done | bytes 655392 | tf_op jit(solution)/shard_map/ppermute | solution.py:116
  67.2 1.4 %collective-permute-done.9.refs_8_ = bf16[336,512]{1,0:T(8,128)(2,1)S(1)} collective-permute-done((bf16[336,512]{1,0:T(8,128)(2,1)S(1)}, bf16[336,512]{1,0:T(8,128)(2,1)S(1)}, u32[]{:S(2)}, u32[]{:S(2)}) %collective-permute-start.9) | collective-permute-done | bytes 344096 | tf_op jit(solution)/shard_map/ppermute | solution.py:116
  68.5 1.5 %collective-permute-start.12 = (bf16[336,512]{1,0:T(8,128)(2,1)S(1)}, bf16[336,512]{1,0:T(8,128)(2,1)S(1)}, u32[]{:S(2)}, u32[]{:S(2)}) collective-permute-start(bf16[336,512]{1,0:T(8,128)(2,1)S(1)} %collective-permute-done.9.refs_8_), channel_id=1, source_target_pairs={{0,16},{16,0},{1,17},{17,1},{2,18},{18,2},{3,19},{19,3},{4,20},{20... | collective-permute-start | bytes 1032200 | tf_op jit(solution)/shard_map/ppermute | solution.py:116
  70.0 1.5 %collective-permute-start.10 = (bf16[640,512]{1,0:T(8,128)(2,1)S(1)}, bf16[640,512]{1,0:T(8,128)(2,1)S(1)}, u32[]{:S(2)}, u32[]{:S(2)}) collective-permute-start(bf16[640,512]{1,0:T(8,128)(2,1)S(1)} %collective-permute-done.6.refs_6_), channel_id=1, source_target_pairs={{0,2},{2,0},{1,3},{3,1},{4,6},{6,4},{5,7},{7,5},{8,10},{10,8},{9,1... | collective-permute-start | bytes 1966088 | tf_op jit(solution)/shard_map/ppermute | solution.py:116
  71.5 1.2 shard_map.89
  72.7 4.8 %collective-permute-done.11.refs_10_ = bf16[336,512]{1,0:T(8,128)(2,1)S(1)} collective-permute-done((bf16[336,512]{1,0:T(8,128)(2,1)S(1)}, bf16[336,512]{1,0:T(8,128)(2,1)S(1)}, u32[]{:S(2)}, u32[]{:S(2)}) %collective-permute-start.11) | collective-permute-done | bytes 344096 | tf_op jit(solution)/shard_map/ppermute | solution.py:116
  77.5 1.5 %collective-permute-start.13 = (bf16[336,512]{1,0:T(8,128)(2,1)S(1)}, bf16[336,512]{1,0:T(8,128)(2,1)S(1)}, u32[]{:S(2)}, u32[]{:S(2)}) collective-permute-start(bf16[336,512]{1,0:T(8,128)(2,1)S(1)} %collective-permute-done.11.refs_10_), channel_id=1, source_target_pairs={{0,16},{16,0},{1,17},{17,1},{2,18},{18,2},{3,19},{19,3},{4,20},{20... | collective-permute-start | bytes 1032200 | tf_op jit(solution)/shard_map/ppermute | solution.py:116
  79.1 2.6 %collective-permute-start.14 = (bf16[256,512]{1,0:T(8,128)(2,1)S(1)}, bf16[256,512]{1,0:T(8,128)(2,1)S(1)}, u32[]{:S(2)}, u32[]{:S(2)}) collective-permute-start(bf16[256,512]{1,0:T(8,128)(2,1)S(1)} %copy-done.8), channel_id=1, source_target_pairs={{0,8},{4,12},{8,0},{12,4},{1,9},{5,13},{9,1},{13,5},{2,10},{6,14},... | collective-permute-start | bytes 786440 | tf_op jit(solution)/shard_map/ppermute | solution.py:116
  81.7 1.3 %collective-permute-start.15 = (bf16[256,512]{1,0:T(8,128)(2,1)S(1)}, bf16[256,512]{1,0:T(8,128)(2,1)S(1)}, u32[]{:S(2)}, u32[]{:S(2)}) collective-permute-start(bf16[256,512]{1,0:T(8,128)(2,1)S(1)} %copy-done.8), channel_id=1, source_target_pairs={{0,4},{4,0},{8,12},{12,8},{1,5},{5,1},{9,13},{13,9},{2,6},{6,2},{1... | collective-permute-start | bytes 786440 | tf_op jit(solution)/shard_map/ppermute | solution.py:116
  83.0 1.7 %collective-permute-done.10.refs_7_ = bf16[640,512]{1,0:T(8,128)(2,1)S(1)} collective-permute-done((bf16[640,512]{1,0:T(8,128)(2,1)S(1)}, bf16[640,512]{1,0:T(8,128)(2,1)S(1)}, u32[]{:S(2)}, u32[]{:S(2)}) %collective-permute-start.10) | collective-permute-done | bytes 655392 | tf_op jit(solution)/shard_map/ppermute | solution.py:116
  84.6 1.6 %collective-permute-done.13.refs_11_ = bf16[336,512]{1,0:T(8,128)(2,1)S(1)} collective-permute-done((bf16[336,512]{1,0:T(8,128)(2,1)S(1)}, bf16[336,512]{1,0:T(8,128)(2,1)S(1)}, u32[]{:S(2)}, u32[]{:S(2)}) %collective-permute-start.13) | collective-permute-done | bytes 344096 | tf_op jit(solution)/shard_map/ppermute | solution.py:116
  86.2 2.9 %shard_map.90 = (bf16[4,16,256]{2,1,0:T(8,128)(2,1)S(1)}, f32[1280,256]{1,0:T(8,128)}, f32[1280,256]{1,0:T(8,128)S(1)}) custom-call(bf16[640,512]{1,0:T(8,128)(2,1)S(1)} %copy-done.2, bf16[640,512]{1,0:T(8,128)(2,1)S(1)} %collective-permute-done.2.refs_1_, bf16[640,512]{1,0:T(8,128)(2,1)S(1)} %collective-permute-done.3.refs_2_, ...), custom_call_target="tpu_custom_call" | custom-call | tf_op jit(solution)/shard_map/pallas_call | solution.py:130
  89.1 2.2 %collective-permute-done.14.refs_7_ = bf16[256,512]{1,0:T(8,128)(2,1)S(1)} collective-permute-done((bf16[256,512]{1,0:T(8,128)(2,1)S(1)}, bf16[256,512]{1,0:T(8,128)(2,1)S(1)}, u32[]{:S(2)}, u32[]{:S(2)}) %collective-permute-start.14) | collective-permute-done | bytes 262176 | tf_op jit(solution)/shard_map/ppermute | solution.py:116
  91.7 0.5 collective-permute-start.16
  92.3 0.4 collective-permute-start.21
  92.6 1.9 %collective-permute-done.17.refs_3_ = f32[1280,256]{1,0:T(8,128)S(1)} collective-permute-done((f32[1280,256]{1,0:T(8,128)}, f32[1280,256]{1,0:T(8,128)S(1)}, u32[]{:S(2)}, u32[]{:S(2)}) %collective-permute-start.17) | collective-permute-done | bytes 1310752 | tf_op jit(solution)/shard_map/ppermute | solution.py:116
  94.6 2.2 %shard_map.91 = (bf16[256,128]{1,0:T(8,128)(2,1)S(1)}, bf16[256,128]{1,0:T(8,128)(2,1)S(1)}, bf16[256,128]{1,0:T(8,128)(2,1)S(1)}, bf16[256,128]{1,0:T(8,128)(2,1)S(1)}) custom-call(f32[1,768]{1,0:T(1,128)S(1)} %fusion.4.refs_0_, bf16[4,16,256]{2,1,0:T(8,128)(2,1)S(1)} %get-tuple-element.78.refs_1_, f32[1280,256]{1,0:T(8,128)S(1)} %get-tuple-element.79.refs_2_, ...), custom_call_target="tpu_custom_call" | custom-call | tf_op jit(solution)/shard_map/pallas_call | solution.py:130
  96.8 0.4 collective-permute-start.18
  97.2 2.6 %collective-permute-start.19 = (bf16[256,128]{1,0:T(8,128)(2,1)S(1)}, bf16[256,128]{1,0:T(8,128)(2,1)S(1)}, u32[]{:S(2)}, u32[]{:S(2)}) collective-permute-start(bf16[256,128]{1,0:T(8,128)(2,1)S(1)} %get-tuple-element.84), channel_id=1, source_target_pairs={{0,8},{4,12},{8,0},{12,4},{1,9},{5,13},{9,1},{13,5},{2,10},{6,14},... | collective-permute-start | bytes 196616 | tf_op jit(solution)/shard_map/ppermute | solution.py:116
  99.8 1.4 %collective-permute-start.20 = (bf16[256,128]{1,0:T(8,128)(2,1)S(1)}, bf16[256,128]{1,0:T(8,128)(2,1)S(1)}, u32[]{:S(2)}, u32[]{:S(2)}) collective-permute-start(bf16[256,128]{1,0:T(8,128)(2,1)S(1)} %get-tuple-element.85), channel_id=1, source_target_pairs={{0,12},{4,8},{8,4},{12,0},{1,13},{5,9},{9,5},{13,1},{2,14},{6,10},... | collective-permute-start | bytes 196616 | tf_op jit(solution)/shard_map/ppermute | solution.py:116
  101.3 1.3 %collective-permute-done.21.refs_9_ = bf16[256,512]{1,0:T(8,128)(2,1)S(1)} collective-permute-done((bf16[256,512]{1,0:T(8,128)(2,1)S(1)}, bf16[256,512]{1,0:T(8,128)(2,1)S(1)}, u32[]{:S(2)}, u32[]{:S(2)}) %collective-permute-start.21) | collective-permute-done | bytes 262176 | tf_op jit(solution)/shard_map/ppermute | solution.py:116
  102.6 1.8 %collective-permute-start.23 = (bf16[256,512]{1,0:T(8,128)(2,1)S(1)}, bf16[256,512]{1,0:T(8,128)(2,1)S(1)}, u32[]{:S(2)}, u32[]{:S(2)}) collective-permute-start(bf16[256,512]{1,0:T(8,128)(2,1)S(1)} %collective-permute-done.15.refs_6_), channel_id=1, source_target_pairs={{0,16},{16,0},{1,17},{17,1},{2,18},{18,2},{3,19},{19,3},{4,20},{20... | collective-permute-start | bytes 786440 | tf_op jit(solution)/shard_map/ppermute | solution.py:116
  104.3 0.8 collective-permute-done.19.refs_2_
  105.1 1.5 %collective-permute-done.20.refs_3_ = bf16[256,128]{1,0:T(8,128)(2,1)S(1)} collective-permute-done((bf16[256,128]{1,0:T(8,128)(2,1)S(1)}, bf16[256,128]{1,0:T(8,128)(2,1)S(1)}, u32[]{:S(2)}, u32[]{:S(2)}) %collective-permute-start.20) | collective-permute-done | bytes 65568 | tf_op jit(solution)/shard_map/ppermute | solution.py:116
  106.7 0.9 shard_map.92
  107.6 2.9 %collective-permute-done.22.refs_2_ = bf16[256,512]{1,0:T(8,128)(2,1)S(1)} collective-permute-done((bf16[256,512]{1,0:T(8,128)(2,1)S(1)}, bf16[256,512]{1,0:T(8,128)(2,1)S(1)}, u32[]{:S(2)}, u32[]{:S(2)}) %collective-permute-start.22) | collective-permute-done | bytes 262176 | tf_op jit(solution)/shard_map/ppermute | solution.py:116
  110.5 0.6 shard_map.93
  111.3 1.9 %collective-permute-done.24 = bf16[2,256,512]{2,1,0:T(8,128)(2,1)S(1)} collective-permute-done((bf16[2,256,512]{2,1,0:T(8,128)(2,1)S(1)}, bf16[2,256,512]{2,1,0:T(8,128)(2,1)S(1)}, u32[]{:S(2)}, u32[]{:S(2)}) %collective-permute-start.24) | collective-permute-done | bytes 524320 | tf_op jit(solution)/shard_map/ppermute | solution.py:116
  113.2 1.6 %collective-permute-start.25 = (bf16[256,512]{1,0:T(8,128)(2,1)S(1)}, bf16[256,512]{1,0:T(8,128)(2,1)S(1)}, u32[]{:S(2)}, u32[]{:S(2)}) collective-permute-start(bf16[256,512]{1,0:T(8,128)(2,1)S(1)} %fusion.1), channel_id=1, source_target_pairs={{0,2},{2,0},{1,3},{3,1},{4,6},{6,4},{5,7},{7,5},{8,10},{10,8},{9,1... | collective-permute-start | bytes 786440 | tf_op jit(solution)/shard_map/ppermute | solution.py:116
  114.8 1.8 %shard_map.86 = bf16[192,2048]{1,0:T(8,128)(2,1)} custom-call(s32[8]{0:T(128)S(1)} %copy-done.7, bf16[3,192,2048]{2,1,0:T(8,128)(2,1)S(1)} %copy-done), custom_call_target="tpu_custom_call" | custom-call | tf_op jit(solution)/shard_map/pallas_call | solution.py:169
  116.6 5.0 %collective-permute-done.25 = bf16[256,512]{1,0:T(8,128)(2,1)S(1)} collective-permute-done((bf16[256,512]{1,0:T(8,128)(2,1)S(1)}, bf16[256,512]{1,0:T(8,128)(2,1)S(1)}, u32[]{:S(2)}, u32[]{:S(2)}) %collective-permute-start.25) | collective-permute-done | bytes 262176 | tf_op jit(solution)/shard_map/ppermute | solution.py:116
  121.6 0.8 fusion
  (39 shorter events, 1.0 us)
Async XLA Ops:
  0.6 9.1 %copy-start.3 = (bf16[512,512]{1,0:T(8,128)(2,1)S(1)}, bf16[512,512]{1,0:T(8,128)(2,1)}, u32[]{:S(2)}) copy-start(bf16[512,512]{1,0:T(8,128)(2,1)} %refs_2_.3) | copy-start | bytes 1572868
  0.6 9.1 %copy-start.1 = (bf16[1024,1024]{1,0:T(8,128)(2,1)S(1)}, bf16[1024,1024]{1,0:T(8,128)(2,1)}, u32[]{:S(2)}) copy-start(bf16[1024,1024]{1,0:T(8,128)(2,1)} %refs_1_.3) | copy-start | bytes 6291460
  0.7 9.1 %copy-start.6 = (s32[256]{0:T(256)S(1)}, s32[256]{0:T(256)}, u32[]{:S(2)}) copy-start(s32[256]{0:T(256)} %param.9) | copy-start | bytes 3076
  4.0 5.8 %collective-permute-start = (bf16[640,1024]{1,0:T(8,128)(2,1)}, bf16[640,1024]{1,0:T(8,128)(2,1)S(1)}, u32[]{:S(2)}, u32[]{:S(2)}) collective-permute-start(bf16[640,1024]{1,0:T(8,128)(2,1)} %get-tuple-element.48), channel_id=1, source_target_pairs={{0,1},{1,0},{2,3},{3,2},{4,5},{5,4},{6,7},{7,6},{8,9},{9,8},{10,11... | collective-permute-start | bytes 3932168 | tf_op jit(solution)/shard_map/ppermute | solution.py:116
  4.5 32.4 %collective-permute-start.3 = (bf16[640,512]{1,0:T(8,128)(2,1)}, bf16[640,512]{1,0:T(8,128)(2,1)S(1)}, u32[]{:S(2)}, u32[]{:S(2)}) collective-permute-start(bf16[640,512]{1,0:T(8,128)(2,1)} %get-tuple-element.47.refs_0_), channel_id=1, source_target_pairs={{0,4},{4,0},{8,12},{12,8},{1,5},{5,1},{9,13},{13,9},{2,6},{6,2},{1... | collective-permute-start | bytes 1966088 | tf_op jit(solution)/shard_map/ppermute | solution.py:116
  7.2 31.8 %collective-permute-start.5 = (bf16[640,512]{1,0:T(8,128)(2,1)}, bf16[640,512]{1,0:T(8,128)(2,1)S(1)}, u32[]{:S(2)}, u32[]{:S(2)}) collective-permute-start(bf16[640,512]{1,0:T(8,128)(2,1)} %get-tuple-element.47.refs_0_), channel_id=1, source_target_pairs={{0,8},{4,12},{8,0},{12,4},{1,9},{5,13},{9,1},{13,5},{2,10},{6,14},... | collective-permute-start | bytes 1966088 | tf_op jit(solution)/shard_map/ppermute | solution.py:116
  9.8 1.1 copy-start.2
  10.1 34.1 %collective-permute-start.1 = (bf16[336,512]{1,0:T(8,128)(2,1)S(1)}, bf16[336,512]{1,0:T(8,128)(2,1)S(1)}, u32[]{:S(2)}, u32[]{:S(2)}) collective-permute-start(bf16[336,512]{1,0:T(8,128)(2,1)S(1)} %get-tuple-element.49), channel_id=1, source_target_pairs={{0,4},{4,0},{8,12},{12,8},{1,5},{5,1},{9,13},{13,9},{2,6},{6,2},{1... | collective-permute-start | bytes 1032200 | tf_op jit(solution)/shard_map/ppermute | solution.py:116
  10.9 37.6 %collective-permute-start.2 = (bf16[640,512]{1,0:T(8,128)(2,1)S(1)}, bf16[640,512]{1,0:T(8,128)(2,1)S(1)}, u32[]{:S(2)}, u32[]{:S(2)}) collective-permute-start(bf16[640,512]{1,0:T(8,128)(2,1)S(1)} %copy-done.2), channel_id=1, source_target_pairs={{0,2},{2,0},{1,3},{3,1},{4,6},{6,4},{5,7},{7,5},{8,10},{10,8},{9,1... | collective-permute-start | bytes 1966088 | tf_op jit(solution)/shard_map/ppermute | solution.py:116
  36.9 17.7 %collective-permute-start.4 = (bf16[640,512]{1,0:T(8,128)(2,1)S(1)}, bf16[640,512]{1,0:T(8,128)(2,1)S(1)}, u32[]{:S(2)}, u32[]{:S(2)}) collective-permute-start(bf16[640,512]{1,0:T(8,128)(2,1)S(1)} %collective-permute-done.3.refs_2_), channel_id=1, source_target_pairs={{0,2},{2,0},{1,3},{3,1},{4,6},{6,4},{5,7},{7,5},{8,10},{10,8},{9,1... | collective-permute-start | bytes 1966088 | tf_op jit(solution)/shard_map/ppermute | solution.py:116
  38.9 28.2 %collective-permute-start.7 = (bf16[640,512]{1,0:T(8,128)(2,1)S(1)}, bf16[640,512]{1,0:T(8,128)(2,1)S(1)}, u32[]{:S(2)}, u32[]{:S(2)}) collective-permute-start(bf16[640,512]{1,0:T(8,128)(2,1)S(1)} %collective-permute-done.5.refs_4_), channel_id=1, source_target_pairs={{0,2},{2,0},{1,3},{3,1},{4,6},{6,4},{5,7},{7,5},{8,10},{10,8},{9,1... | collective-permute-start | bytes 1966088 | tf_op jit(solution)/shard_map/ppermute | solution.py:116
  44.1 24.4 %collective-permute-start.6 = (bf16[640,512]{1,0:T(8,128)(2,1)S(1)}, bf16[640,512]{1,0:T(8,128)(2,1)S(1)}, u32[]{:S(2)}, u32[]{:S(2)}) collective-permute-start(bf16[640,512]{1,0:T(8,128)(2,1)S(1)} %collective-permute-done.5.refs_4_), channel_id=1, source_target_pairs={{0,4},{4,0},{8,12},{12,8},{1,5},{5,1},{9,13},{13,9},{2,6},{6,2},{1... | collective-permute-start | bytes 1966088 | tf_op jit(solution)/shard_map/ppermute | solution.py:116
  45.9 22.6 %collective-permute-start.9 = (bf16[336,512]{1,0:T(8,128)(2,1)S(1)}, bf16[336,512]{1,0:T(8,128)(2,1)S(1)}, u32[]{:S(2)}, u32[]{:S(2)}) collective-permute-start(bf16[336,512]{1,0:T(8,128)(2,1)S(1)} %get-tuple-element.54), channel_id=1, source_target_pairs={{0,8},{4,12},{8,0},{12,4},{1,9},{5,13},{9,1},{13,5},{2,10},{6,14},... | collective-permute-start | bytes 1032200 | tf_op jit(solution)/shard_map/ppermute | solution.py:116
  54.5 14.0 %collective-permute-start.8 = (bf16[336,512]{1,0:T(8,128)(2,1)S(1)}, bf16[336,512]{1,0:T(8,128)(2,1)S(1)}, u32[]{:S(2)}, u32[]{:S(2)}) collective-permute-start(bf16[336,512]{1,0:T(8,128)(2,1)S(1)} %collective-permute-done.1.refs_7_), channel_id=1, source_target_pairs={{0,16},{16,0},{1,17},{17,1},{2,18},{18,2},{3,19},{19,3},{4,20},{20... | collective-permute-start | bytes 1032200 | tf_op jit(solution)/shard_map/ppermute | solution.py:116
  56.4 21.1 %collective-permute-start.11 = (bf16[336,512]{1,0:T(8,128)(2,1)S(1)}, bf16[336,512]{1,0:T(8,128)(2,1)S(1)}, u32[]{:S(2)}, u32[]{:S(2)}) collective-permute-start(bf16[336,512]{1,0:T(8,128)(2,1)S(1)} %get-tuple-element.60), channel_id=1, source_target_pairs={{0,12},{4,8},{8,4},{12,0},{1,13},{5,9},{9,5},{13,1},{2,14},{6,10},... | collective-permute-start | bytes 1032200 | tf_op jit(solution)/shard_map/ppermute | solution.py:116
  68.5 9.0 %collective-permute-start.12 = (bf16[336,512]{1,0:T(8,128)(2,1)S(1)}, bf16[336,512]{1,0:T(8,128)(2,1)S(1)}, u32[]{:S(2)}, u32[]{:S(2)}) collective-permute-start(bf16[336,512]{1,0:T(8,128)(2,1)S(1)} %collective-permute-done.9.refs_8_), channel_id=1, source_target_pairs={{0,16},{16,0},{1,17},{17,1},{2,18},{18,2},{3,19},{19,3},{4,20},{20... | collective-permute-start | bytes 1032200 | tf_op jit(solution)/shard_map/ppermute | solution.py:116
  70.0 14.6 %collective-permute-start.10 = (bf16[640,512]{1,0:T(8,128)(2,1)S(1)}, bf16[640,512]{1,0:T(8,128)(2,1)S(1)}, u32[]{:S(2)}, u32[]{:S(2)}) collective-permute-start(bf16[640,512]{1,0:T(8,128)(2,1)S(1)} %collective-permute-done.6.refs_6_), channel_id=1, source_target_pairs={{0,2},{2,0},{1,3},{3,1},{4,6},{6,4},{5,7},{7,5},{8,10},{10,8},{9,1... | collective-permute-start | bytes 1966088 | tf_op jit(solution)/shard_map/ppermute | solution.py:116
  71.5 7.5 %copy-start.8 = (bf16[256,512]{1,0:T(8,128)(2,1)S(1)}, bf16[256,512]{1,0:T(8,128)(2,1)}, u32[]{:S(2)}) copy-start(bf16[256,512]{1,0:T(8,128)(2,1)} %get-tuple-element.75) | copy-start | bytes 786436
  77.5 8.7 %collective-permute-start.13 = (bf16[336,512]{1,0:T(8,128)(2,1)S(1)}, bf16[336,512]{1,0:T(8,128)(2,1)S(1)}, u32[]{:S(2)}, u32[]{:S(2)}) collective-permute-start(bf16[336,512]{1,0:T(8,128)(2,1)S(1)} %collective-permute-done.11.refs_10_), channel_id=1, source_target_pairs={{0,16},{16,0},{1,17},{17,1},{2,18},{18,2},{3,19},{19,3},{4,20},{20... | collective-permute-start | bytes 1032200 | tf_op jit(solution)/shard_map/ppermute | solution.py:116
  79.1 12.3 %collective-permute-start.14 = (bf16[256,512]{1,0:T(8,128)(2,1)S(1)}, bf16[256,512]{1,0:T(8,128)(2,1)S(1)}, u32[]{:S(2)}, u32[]{:S(2)}) collective-permute-start(bf16[256,512]{1,0:T(8,128)(2,1)S(1)} %copy-done.8), channel_id=1, source_target_pairs={{0,8},{4,12},{8,0},{12,4},{1,9},{5,13},{9,1},{13,5},{2,10},{6,14},... | collective-permute-start | bytes 786440 | tf_op jit(solution)/shard_map/ppermute | solution.py:116
  81.7 9.6 %collective-permute-start.15 = (bf16[256,512]{1,0:T(8,128)(2,1)S(1)}, bf16[256,512]{1,0:T(8,128)(2,1)S(1)}, u32[]{:S(2)}, u32[]{:S(2)}) collective-permute-start(bf16[256,512]{1,0:T(8,128)(2,1)S(1)} %copy-done.8), channel_id=1, source_target_pairs={{0,4},{4,0},{8,12},{12,8},{1,5},{5,1},{9,13},{13,9},{2,6},{6,2},{1... | collective-permute-start | bytes 786440 | tf_op jit(solution)/shard_map/ppermute | solution.py:116
  91.3 3.2 %collective-permute-start.17 = (f32[1280,256]{1,0:T(8,128)}, f32[1280,256]{1,0:T(8,128)S(1)}, u32[]{:S(2)}, u32[]{:S(2)}) collective-permute-start(f32[1280,256]{1,0:T(8,128)} %get-tuple-element.80), channel_id=1, source_target_pairs={{0,1},{1,0},{2,3},{3,2},{4,5},{5,4},{6,7},{7,6},{8,9},{9,8},{10,11... | collective-permute-start | bytes 3932168 | tf_op jit(solution)/shard_map/ppermute | solution.py:116
  91.7 9.5 %collective-permute-start.16 = (bf16[256,512]{1,0:T(8,128)(2,1)S(1)}, bf16[256,512]{1,0:T(8,128)(2,1)S(1)}, u32[]{:S(2)}, u32[]{:S(2)}) collective-permute-start(bf16[256,512]{1,0:T(8,128)(2,1)S(1)} %collective-permute-done.14.refs_7_), channel_id=1, source_target_pairs={{0,16},{16,0},{1,17},{17,1},{2,18},{18,2},{3,19},{19,3},{4,20},{20... | collective-permute-start | bytes 786440 | tf_op jit(solution)/shard_map/ppermute | solution.py:116
  92.3 10.3 %collective-permute-start.21 = (bf16[256,512]{1,0:T(8,128)(2,1)S(1)}, bf16[256,512]{1,0:T(8,128)(2,1)S(1)}, u32[]{:S(2)}, u32[]{:S(2)}) collective-permute-start(bf16[256,512]{1,0:T(8,128)(2,1)S(1)} %collective-permute-done.14.refs_7_), channel_id=1, source_target_pairs={{0,4},{4,0},{8,12},{12,8},{1,5},{5,1},{9,13},{13,9},{2,6},{6,2},{1... | collective-permute-start | bytes 786440 | tf_op jit(solution)/shard_map/ppermute | solution.py:116
  94.6 12.1 %copy-start.4 = (bf16[256,2048]{1,0:T(8,128)(2,1)S(1)}, bf16[256,2048]{1,0:T(8,128)(2,1)}, u32[]{:S(2)}) copy-start(bf16[256,2048]{1,0:T(8,128)(2,1)} %refs_4_.3) | copy-start | bytes 3145732
  94.6 12.1 %copy-start.5 = (bf16[512,512]{1,0:T(8,128)(2,1)S(1)}, bf16[512,512]{1,0:T(8,128)(2,1)}, u32[]{:S(2)}) copy-start(bf16[512,512]{1,0:T(8,128)(2,1)} %refs_5_.3) | copy-start | bytes 1572868
  96.8 7.5 %collective-permute-start.18 = (bf16[256,128]{1,0:T(8,128)(2,1)S(1)}, bf16[256,128]{1,0:T(8,128)(2,1)S(1)}, u32[]{:S(2)}, u32[]{:S(2)}) collective-permute-start(bf16[256,128]{1,0:T(8,128)(2,1)S(1)} %get-tuple-element.83), channel_id=1, source_target_pairs={{0,4},{4,0},{8,12},{12,8},{1,5},{5,1},{9,13},{13,9},{2,6},{6,2},{1... | collective-permute-start | bytes 196616 | tf_op jit(solution)/shard_map/ppermute | solution.py:116
  97.2 7.9 %collective-permute-start.19 = (bf16[256,128]{1,0:T(8,128)(2,1)S(1)}, bf16[256,128]{1,0:T(8,128)(2,1)S(1)}, u32[]{:S(2)}, u32[]{:S(2)}) collective-permute-start(bf16[256,128]{1,0:T(8,128)(2,1)S(1)} %get-tuple-element.84), channel_id=1, source_target_pairs={{0,8},{4,12},{8,0},{12,4},{1,9},{5,13},{9,1},{13,5},{2,10},{6,14},... | collective-permute-start | bytes 196616 | tf_op jit(solution)/shard_map/ppermute | solution.py:116
  99.8 6.8 %collective-permute-start.20 = (bf16[256,128]{1,0:T(8,128)(2,1)S(1)}, bf16[256,128]{1,0:T(8,128)(2,1)S(1)}, u32[]{:S(2)}, u32[]{:S(2)}) collective-permute-start(bf16[256,128]{1,0:T(8,128)(2,1)S(1)} %get-tuple-element.85), channel_id=1, source_target_pairs={{0,12},{4,8},{8,4},{12,0},{1,13},{5,9},{9,5},{13,1},{2,14},{6,10},... | collective-permute-start | bytes 196616 | tf_op jit(solution)/shard_map/ppermute | solution.py:116
  101.2 9.3 %collective-permute-start.22 = (bf16[256,512]{1,0:T(8,128)(2,1)S(1)}, bf16[256,512]{1,0:T(8,128)(2,1)S(1)}, u32[]{:S(2)}, u32[]{:S(2)}) collective-permute-start(bf16[256,512]{1,0:T(8,128)(2,1)S(1)} %collective-permute-done.16.refs_8_), channel_id=1, source_target_pairs={{0,4},{4,0},{8,12},{12,8},{1,5},{5,1},{9,13},{13,9},{2,6},{6,2},{1... | collective-permute-start | bytes 786440 | tf_op jit(solution)/shard_map/ppermute | solution.py:116
  102.6 8.0 %collective-permute-start.23 = (bf16[256,512]{1,0:T(8,128)(2,1)S(1)}, bf16[256,512]{1,0:T(8,128)(2,1)S(1)}, u32[]{:S(2)}, u32[]{:S(2)}) collective-permute-start(bf16[256,512]{1,0:T(8,128)(2,1)S(1)} %collective-permute-done.15.refs_6_), channel_id=1, source_target_pairs={{0,16},{16,0},{1,17},{17,1},{2,18},{18,2},{3,19},{19,3},{4,20},{20... | collective-permute-start | bytes 786440 | tf_op jit(solution)/shard_map/ppermute | solution.py:116
  110.5 4.3 %copy-start = (bf16[3,192,2048]{2,1,0:T(8,128)(2,1)S(1)}, bf16[3,192,2048]{2,1,0:T(8,128)(2,1)}, u32[]{:S(2)}) copy-start(bf16[3,192,2048]{2,1,0:T(8,128)(2,1)} %refs_1_.2) | copy-start | bytes 7077892
  110.5 4.3 %copy-start.7 = (s32[8]{0:T(128)S(1)}, s32[8]{0:T(128)}, u32[]{:S(2)}) copy-start(s32[8]{0:T(128)} %refs_0_.1) | copy-start | bytes 100
  111.2 2.0 %collective-permute-start.24 = (bf16[2,256,512]{2,1,0:T(8,128)(2,1)S(1)}, bf16[2,256,512]{2,1,0:T(8,128)(2,1)S(1)}, u32[]{:S(2)}, u32[]{:S(2)}) collective-permute-start(bf16[2,256,512]{2,1,0:T(8,128)(2,1)S(1)} %get-tuple-element.91), channel_id=1, source_target_pairs={{0,1},{1,0},{2,3},{3,2},{4,5},{5,4},{6,7},{7,6},{8,9},{9,8},{10,11... | collective-permute-start | bytes 1572872 | tf_op jit(solution)/shard_map/ppermute | solution.py:116
  113.2 8.4 %collective-permute-start.25 = (bf16[256,512]{1,0:T(8,128)(2,1)S(1)}, bf16[256,512]{1,0:T(8,128)(2,1)S(1)}, u32[]{:S(2)}, u32[]{:S(2)}) collective-permute-start(bf16[256,512]{1,0:T(8,128)(2,1)S(1)} %fusion.1), channel_id=1, source_target_pairs={{0,2},{2,0},{1,3},{3,1},{4,6},{6,4},{5,7},{7,5},{8,10},{10,8},{9,1... | collective-permute-start | bytes 786440 | tf_op jit(solution)/shard_map/ppermute | solution.py:116

commit v19 on v15

--- a/solution.py
+++ b/solution.py
@@ -430,7 +430,7 @@
     total_ref[seq_at ^ place] += residual_ref[...].astype(jnp.float32)
 
 
-def late_out_body(total_ref, late_ref, partner_w, fourth_w, send_ref, keep_ref):
+def late_out_body(total_ref, late_ref, fourth_w, partner_w, send_ref, keep_ref):
     place = lax.axis_index("mem") * 2 + lax.axis_index("rep")
     for bit in range(4):
         slot = lax.axis_index("seq") ^ bit ^ place
@@ -528,7 +528,7 @@
         ],
         limit=15,
     )
-    send, out_third, out_partner = lax.optimization_barrier((send, out_third, out_partner))
+    send, out_third = lax.optimization_barrier((send, out_third))
     came = swap(send, "rep", 1)
     third_rest, out_fourth = swap(out_third, "grp", 1), swap(out_third, "seq", 1)
 
@@ -589,7 +589,7 @@
             bfloat(2, audio_rows, columns),
             jax.ShapeDtypeStruct((2, audio_rows, columns), jnp.float32),
         ],
-        [total, late_heads, partner_rest, fourth_rest],
+        [total, late_heads, fourth_rest, partner_rest],
         limit=5,
     )
     came = swap(send, "rep", 1)

time: 123 us -> 128 us (1.041)
  waiting for transfers between devices: 70.4 us -> 75.4 us
    ppermute x26, waiting for transfers between devices: 70.4 us -> 75.4 us  [swap(): return lax.ppermute(value, axis, [(i, i ^ bit) for i in range(size)])]
  transfers between devices with their start and end apart: 26 -> 26, of which waited for: 19 -> 18; matrix products, arithmetic and copies ran while one was open for 0% -> 0% of each run, Pallas kernels for 7% -> 7%
where the time goes in v19:
time: 128 us
  waiting for transfers between devices  75.4 us (59%)
  starting transfers between devices  36.8 us (29%)
  Pallas kernels  13.1 us (10%)
    ppermute x26, waiting for transfers between devices, swap(): return lax.ppermute(value, axis, [(i, i ^ bit) for i in range(size)])  75.4 us
    ppermute x26, starting transfers between devices, swap(): return lax.ppermute(value, axis, [(i, i ^ bit) for i in range(size)])  36.8 us
    pallas_call x6, Pallas kernels, kernel_call(): pl.pallas_call(whole, out_shape=outs, in_specs=spots + [ANY] * len(after)...  11.3 us
  transfers between devices with their start and end apart: 26, of which 18 were waited for; matrix products, arithmetic and copies ran while one was open for 0% of the time, Pallas kernels for 7%

profile of v19, /device:TPU:0, one launch (start us, length us, event | category | flops | bytes accessed | tf_op | source)
XLA Modules:
  0.0 127.5 jit_solution(2549394773114309305)
XLA Ops:
  0.7 3.3 %shard_map.87 = (bf16[640,512]{1,0:T(8,128)(2,1)}, bf16[640,1024]{1,0:T(8,128)(2,1)}, bf16[256,512]{1,0:T(8,128)(2,1)}) custom-call(s32[8]{0:T(128)} %refs_0_.1, bf16[3,192,2048]{2,1,0:T(8,128)(2,1)} %refs_1_.2, bf16[256,2048]{1,0:T(8,128)(2,1)} %refs_4_.3, bf16[1024,1024]{1,0:T(8,128)(2,1)} %refs_1_.3, bf16[512,512]{1,0:T(8,128)(2,1)} %refs_2_.3, ...), custom_call_target="tpu_custom_call" | custom-call | tf_op jit(solution)/shard_map/pallas_call | solution.py:130
  4.0 0.5 collective-permute-start
  4.5 2.6 %collective-permute-start.3 = (bf16[640,512]{1,0:T(8,128)(2,1)}, bf16[640,512]{1,0:T(8,128)(2,1)S(1)}, u32[]{:S(2)}, u32[]{:S(2)}) collective-permute-start(bf16[640,512]{1,0:T(8,128)(2,1)} %get-tuple-element.38.refs_0_), channel_id=1, source_target_pairs={{0,4},{4,0},{8,12},{12,8},{1,5},{5,1},{9,13},{13,9},{2,6},{6,2},{1... | collective-permute-start | bytes 1966088 | tf_op jit(solution)/shard_map/ppermute | solution.py:116
  7.2 2.6 %collective-permute-start.5 = (bf16[640,512]{1,0:T(8,128)(2,1)}, bf16[640,512]{1,0:T(8,128)(2,1)S(1)}, u32[]{:S(2)}, u32[]{:S(2)}) collective-permute-start(bf16[640,512]{1,0:T(8,128)(2,1)} %get-tuple-element.38.refs_0_), channel_id=1, source_target_pairs={{0,8},{4,12},{8,0},{12,4},{1,9},{5,13},{9,1},{13,5},{2,10},{6,14},... | collective-permute-start | bytes 1966088 | tf_op jit(solution)/shard_map/ppermute | solution.py:116
  9.8 0.3 shard_map.88
  10.1 0.6 collective-permute-start.1
  10.9 1.5 %collective-permute-start.2 = (bf16[640,512]{1,0:T(8,128)(2,1)S(1)}, bf16[640,512]{1,0:T(8,128)(2,1)S(1)}, u32[]{:S(2)}, u32[]{:S(2)}) collective-permute-start(bf16[640,512]{1,0:T(8,128)(2,1)S(1)} %copy-done.4), channel_id=1, source_target_pairs={{0,2},{2,0},{1,3},{3,1},{4,6},{6,4},{5,7},{7,5},{8,10},{10,8},{9,1... | collective-permute-start | bytes 1966088 | tf_op jit(solution)/shard_map/ppermute | solution.py:116
  12.4 24.5 %collective-permute-done.3.refs_2_ = bf16[640,512]{1,0:T(8,128)(2,1)S(1)} collective-permute-done((bf16[640,512]{1,0:T(8,128)(2,1)}, bf16[640,512]{1,0:T(8,128)(2,1)S(1)}, u32[]{:S(2)}, u32[]{:S(2)}) %collective-permute-start.3) | collective-permute-done | bytes 655392 | tf_op jit(solution)/shard_map/ppermute | solution.py:116
  36.9 1.9 %collective-permute-start.4 = (bf16[640,512]{1,0:T(8,128)(2,1)S(1)}, bf16[640,512]{1,0:T(8,128)(2,1)S(1)}, u32[]{:S(2)}, u32[]{:S(2)}) collective-permute-start(bf16[640,512]{1,0:T(8,128)(2,1)S(1)} %collective-permute-done.3.refs_2_), channel_id=1, source_target_pairs={{0,2},{2,0},{1,3},{3,1},{4,6},{6,4},{5,7},{7,5},{8,10},{10,8},{9,1... | collective-permute-start | bytes 1966088 | tf_op jit(solution)/shard_map/ppermute | solution.py:116
  38.9 1.5 %collective-permute-start.7 = (bf16[640,512]{1,0:T(8,128)(2,1)S(1)}, bf16[640,512]{1,0:T(8,128)(2,1)S(1)}, u32[]{:S(2)}, u32[]{:S(2)}) collective-permute-start(bf16[640,512]{1,0:T(8,128)(2,1)S(1)} %collective-permute-done.5.refs_4_), channel_id=1, source_target_pairs={{0,2},{2,0},{1,3},{3,1},{4,6},{6,4},{5,7},{7,5},{8,10},{10,8},{9,1... | collective-permute-start | bytes 1966088 | tf_op jit(solution)/shard_map/ppermute | solution.py:116
  40.4 3.7 %collective-permute-done.1.refs_9_ = bf16[336,512]{1,0:T(8,128)(2,1)S(1)} collective-permute-done((bf16[336,512]{1,0:T(8,128)(2,1)S(1)}, bf16[336,512]{1,0:T(8,128)(2,1)S(1)}, u32[]{:S(2)}, u32[]{:S(2)}) %collective-permute-start.1) | collective-permute-done | bytes 344096 | tf_op jit(solution)/shard_map/ppermute | solution.py:116
  44.1 1.8 %collective-permute-start.6 = (bf16[640,512]{1,0:T(8,128)(2,1)S(1)}, bf16[640,512]{1,0:T(8,128)(2,1)S(1)}, u32[]{:S(2)}, u32[]{:S(2)}) collective-permute-start(bf16[640,512]{1,0:T(8,128)(2,1)S(1)} %collective-permute-done.5.refs_4_), channel_id=1, source_target_pairs={{0,4},{4,0},{8,12},{12,8},{1,5},{5,1},{9,13},{13,9},{2,6},{6,2},{1... | collective-permute-start | bytes 1966088 | tf_op jit(solution)/shard_map/ppermute | solution.py:116
  45.9 2.5 %collective-permute-start.9 = (bf16[336,512]{1,0:T(8,128)(2,1)S(1)}, bf16[336,512]{1,0:T(8,128)(2,1)S(1)}, u32[]{:S(2)}, u32[]{:S(2)}) collective-permute-start(bf16[336,512]{1,0:T(8,128)(2,1)S(1)} %get-tuple-element.45), channel_id=1, source_target_pairs={{0,8},{4,12},{8,0},{12,4},{1,9},{5,13},{9,1},{13,5},{2,10},{6,14},... | collective-permute-start | bytes 1032200 | tf_op jit(solution)/shard_map/ppermute | solution.py:116
  48.5 6.1 %collective-permute-done.4.refs_3_ = bf16[640,512]{1,0:T(8,128)(2,1)S(1)} collective-permute-done((bf16[640,512]{1,0:T(8,128)(2,1)S(1)}, bf16[640,512]{1,0:T(8,128)(2,1)S(1)}, u32[]{:S(2)}, u32[]{:S(2)}) %collective-permute-start.4) | collective-permute-done | bytes 655392 | tf_op jit(solution)/shard_map/ppermute | solution.py:116
  54.5 1.9 %collective-permute-start.8 = (bf16[336,512]{1,0:T(8,128)(2,1)S(1)}, bf16[336,512]{1,0:T(8,128)(2,1)S(1)}, u32[]{:S(2)}, u32[]{:S(2)}) collective-permute-start(bf16[336,512]{1,0:T(8,128)(2,1)S(1)} %collective-permute-done.1.refs_9_), channel_id=1, source_target_pairs={{0,16},{16,0},{1,17},{17,1},{2,18},{18,2},{3,19},{19,3},{4,20},{20... | collective-permute-start | bytes 1032200 | tf_op jit(solution)/shard_map/ppermute | solution.py:116
  56.4 2.5 %collective-permute-start.11 = (bf16[336,512]{1,0:T(8,128)(2,1)S(1)}, bf16[336,512]{1,0:T(8,128)(2,1)S(1)}, u32[]{:S(2)}, u32[]{:S(2)}) collective-permute-start(bf16[336,512]{1,0:T(8,128)(2,1)S(1)} %get-tuple-element.53), channel_id=1, source_target_pairs={{0,12},{4,8},{8,4},{12,0},{1,13},{5,9},{9,5},{13,1},{2,14},{6,10},... | collective-permute-start | bytes 1032200 | tf_op jit(solution)/shard_map/ppermute | solution.py:116
  58.9 8.2 %collective-permute-done.7.refs_5_ = bf16[640,512]{1,0:T(8,128)(2,1)S(1)} collective-permute-done((bf16[640,512]{1,0:T(8,128)(2,1)S(1)}, bf16[640,512]{1,0:T(8,128)(2,1)S(1)}, u32[]{:S(2)}, u32[]{:S(2)}) %collective-permute-start.7) | collective-permute-done | bytes 655392 | tf_op jit(solution)/shard_map/ppermute | solution.py:116
  67.2 1.4 %collective-permute-done.9.refs_11_ = bf16[336,512]{1,0:T(8,128)(2,1)S(1)} collective-permute-done((bf16[336,512]{1,0:T(8,128)(2,1)S(1)}, bf16[336,512]{1,0:T(8,128)(2,1)S(1)}, u32[]{:S(2)}, u32[]{:S(2)}) %collective-permute-start.9) | collective-permute-done | bytes 344096 | tf_op jit(solution)/shard_map/ppermute | solution.py:116
  68.5 1.5 %collective-permute-start.12 = (bf16[336,512]{1,0:T(8,128)(2,1)S(1)}, bf16[336,512]{1,0:T(8,128)(2,1)S(1)}, u32[]{:S(2)}, u32[]{:S(2)}) collective-permute-start(bf16[336,512]{1,0:T(8,128)(2,1)S(1)} %collective-permute-done.9.refs_11_), channel_id=1, source_target_pairs={{0,16},{16,0},{1,17},{17,1},{2,18},{18,2},{3,19},{19,3},{4,20},{20... | collective-permute-start | bytes 1032200 | tf_op jit(solution)/shard_map/ppermute | solution.py:116
  70.0 1.5 %collective-permute-start.10 = (bf16[640,512]{1,0:T(8,128)(2,1)S(1)}, bf16[640,512]{1,0:T(8,128)(2,1)S(1)}, u32[]{:S(2)}, u32[]{:S(2)}) collective-permute-start(bf16[640,512]{1,0:T(8,128)(2,1)S(1)} %collective-permute-done.6.refs_6_), channel_id=1, source_target_pairs={{0,2},{2,0},{1,3},{3,1},{4,6},{6,4},{5,7},{7,5},{8,10},{10,8},{9,1... | collective-permute-start | bytes 1966088 | tf_op jit(solution)/shard_map/ppermute | solution.py:116
  71.5 6.0 %collective-permute-done.11.refs_13_ = bf16[336,512]{1,0:T(8,128)(2,1)S(1)} collective-permute-done((bf16[336,512]{1,0:T(8,128)(2,1)S(1)}, bf16[336,512]{1,0:T(8,128)(2,1)S(1)}, u32[]{:S(2)}, u32[]{:S(2)}) %collective-permute-start.11) | collective-permute-done | bytes 344096 | tf_op jit(solution)/shard_map/ppermute | solution.py:116
  77.5 1.5 %collective-permute-start.13 = (bf16[336,512]{1,0:T(8,128)(2,1)S(1)}, bf16[336,512]{1,0:T(8,128)(2,1)S(1)}, u32[]{:S(2)}, u32[]{:S(2)}) collective-permute-start(bf16[336,512]{1,0:T(8,128)(2,1)S(1)} %collective-permute-done.11.refs_13_), channel_id=1, source_target_pairs={{0,16},{16,0},{1,17},{17,1},{2,18},{18,2},{3,19},{19,3},{4,20},{20... | collective-permute-start | bytes 1032200 | tf_op jit(solution)/shard_map/ppermute | solution.py:116
  79.1 2.6 %collective-permute-start.14 = (bf16[256,512]{1,0:T(8,128)(2,1)S(1)}, bf16[256,512]{1,0:T(8,128)(2,1)S(1)}, u32[]{:S(2)}, u32[]{:S(2)}) collective-permute-start(bf16[256,512]{1,0:T(8,128)(2,1)S(1)} %copy-done.8), channel_id=1, source_target_pairs={{0,8},{4,12},{8,0},{12,4},{1,9},{5,13},{9,1},{13,5},{2,10},{6,14},... | collective-permute-start | bytes 786440 | tf_op jit(solution)/shard_map/ppermute | solution.py:116
  81.7 2.9 %collective-permute-done.10.refs_7_ = bf16[640,512]{1,0:T(8,128)(2,1)S(1)} collective-permute-done((bf16[640,512]{1,0:T(8,128)(2,1)S(1)}, bf16[640,512]{1,0:T(8,128)(2,1)S(1)}, u32[]{:S(2)}, u32[]{:S(2)}) %collective-permute-start.10) | collective-permute-done | bytes 655392 | tf_op jit(solution)/shard_map/ppermute | solution.py:116
  84.6 1.6 %collective-permute-done.13.refs_14_ = bf16[336,512]{1,0:T(8,128)(2,1)S(1)} collective-permute-done((bf16[336,512]{1,0:T(8,128)(2,1)S(1)}, bf16[336,512]{1,0:T(8,128)(2,1)S(1)}, u32[]{:S(2)}, u32[]{:S(2)}) %collective-permute-start.13) | collective-permute-done | bytes 344096 | tf_op jit(solution)/shard_map/ppermute | solution.py:116
  86.2 3.9 %shard_map.89 = (bf16[4,16,256]{2,1,0:T(8,128)(2,1)S(1)}, f32[1280,256]{1,0:T(8,128)}, f32[1280,256]{1,0:T(8,128)S(1)}) custom-call(bf16[640,512]{1,0:T(8,128)(2,1)S(1)} %copy-done.4, bf16[640,512]{1,0:T(8,128)(2,1)S(1)} %collective-permute-done.2.refs_1_, bf16[640,512]{1,0:T(8,128)(2,1)S(1)} %collective-permute-done.3.refs_2_, ...), custom_call_target="tpu_custom_call" | custom-call | tf_op jit(solution)/shard_map/pallas_call | solution.py:130
  90.1 1.1 collective-permute-done.14.refs_7_
  91.4 0.2 collective-permute-start.16
  91.9 1.5 %collective-permute-start.15 = (bf16[256,512]{1,0:T(8,128)(2,1)S(1)}, bf16[256,512]{1,0:T(8,128)(2,1)S(1)}, u32[]{:S(2)}, u32[]{:S(2)}) collective-permute-start(bf16[256,512]{1,0:T(8,128)(2,1)S(1)} %collective-permute-done.14.refs_7_), channel_id=1, source_target_pairs={{0,16},{16,0},{1,17},{17,1},{2,18},{18,2},{3,19},{19,3},{4,20},{20... | collective-permute-start | bytes 786440 | tf_op jit(solution)/shard_map/ppermute | solution.py:116
  93.4 0.8 collective-permute-start.21
  94.2 0.3 collective-permute-done.17.refs_3_
  94.5 2.2 %shard_map.90 = (bf16[256,128]{1,0:T(8,128)(2,1)S(1)}, bf16[256,128]{1,0:T(8,128)(2,1)S(1)}, bf16[256,128]{1,0:T(8,128)(2,1)S(1)}, bf16[256,128]{1,0:T(8,128)(2,1)S(1)}) custom-call(f32[1,768]{1,0:T(1,128)S(1)} %fusion.4.refs_0_, bf16[4,16,256]{2,1,0:T(8,128)(2,1)S(1)} %get-tuple-element.60.refs_1_, f32[1280,256]{1,0:T(8,128)S(1)} %get-tuple-element.61.refs_2_, ...), custom_call_target="tpu_custom_call" | custom-call | tf_op jit(solution)/shard_map/pallas_call | solution.py:130
  96.7 1.0 collective-permute-start.18
  97.8 1.7 %collective-permute-start.19 = (bf16[256,128]{1,0:T(8,128)(2,1)S(1)}, bf16[256,128]{1,0:T(8,128)(2,1)S(1)}, u32[]{:S(2)}, u32[]{:S(2)}) collective-permute-start(bf16[256,128]{1,0:T(8,128)(2,1)S(1)} %get-tuple-element.66), channel_id=1, source_target_pairs={{0,8},{4,12},{8,0},{12,4},{1,9},{5,13},{9,1},{13,5},{2,10},{6,14},... | collective-permute-start | bytes 196616 | tf_op jit(solution)/shard_map/ppermute | solution.py:116
  99.5 1.0 collective-permute-done.16.refs_6_
  100.5 2.1 %collective-permute-start.20 = (bf16[256,128]{1,0:T(8,128)(2,1)S(1)}, bf16[256,128]{1,0:T(8,128)(2,1)S(1)}, u32[]{:S(2)}, u32[]{:S(2)}) collective-permute-start(bf16[256,128]{1,0:T(8,128)(2,1)S(1)} %get-tuple-element.67), channel_id=1, source_target_pairs={{0,12},{4,8},{8,4},{12,0},{1,13},{5,9},{9,5},{13,1},{2,14},{6,10},... | collective-permute-start | bytes 196616 | tf_op jit(solution)/shard_map/ppermute | solution.py:116
  102.7 4.9 %collective-permute-done.21.refs_9_ = bf16[256,512]{1,0:T(8,128)(2,1)S(1)} collective-permute-done((bf16[256,512]{1,0:T(8,128)(2,1)S(1)}, bf16[256,512]{1,0:T(8,128)(2,1)S(1)}, u32[]{:S(2)}, u32[]{:S(2)}) %collective-permute-start.21) | collective-permute-done | bytes 262176 | tf_op jit(solution)/shard_map/ppermute | solution.py:116
  107.5 0.5 collective-permute-start.23
  108.1 1.1 collective-permute-done.18.refs_1_
  109.1 1.4 %collective-permute-done.20.refs_3_ = bf16[256,128]{1,0:T(8,128)(2,1)S(1)} collective-permute-done((bf16[256,128]{1,0:T(8,128)(2,1)S(1)}, bf16[256,128]{1,0:T(8,128)(2,1)S(1)}, u32[]{:S(2)}, u32[]{:S(2)}) %collective-permute-start.20) | collective-permute-done | bytes 65568 | tf_op jit(solution)/shard_map/ppermute | solution.py:116
  110.6 0.9 shard_map.91
  111.5 4.1 %collective-permute-done.22.refs_2_ = bf16[256,512]{1,0:T(8,128)(2,1)S(1)} collective-permute-done((bf16[256,512]{1,0:T(8,128)(2,1)S(1)}, bf16[256,512]{1,0:T(8,128)(2,1)S(1)}, u32[]{:S(2)}, u32[]{:S(2)}) %collective-permute-start.22) | collective-permute-done | bytes 262176 | tf_op jit(solution)/shard_map/ppermute | solution.py:116
  115.6 0.7 shard_map.92
  116.3 1.9 %collective-permute-done.24 = bf16[2,256,512]{2,1,0:T(8,128)(2,1)S(1)} collective-permute-done((bf16[2,256,512]{2,1,0:T(8,128)(2,1)S(1)}, bf16[2,256,512]{2,1,0:T(8,128)(2,1)S(1)}, u32[]{:S(2)}, u32[]{:S(2)}) %collective-permute-start.24) | collective-permute-done | bytes 524320 | tf_op jit(solution)/shard_map/ppermute | solution.py:116
  118.3 1.6 %collective-permute-start.25 = (bf16[256,512]{1,0:T(8,128)(2,1)S(1)}, bf16[256,512]{1,0:T(8,128)(2,1)S(1)}, u32[]{:S(2)}, u32[]{:S(2)}) collective-permute-start(bf16[256,512]{1,0:T(8,128)(2,1)S(1)} %fusion.1), channel_id=1, source_target_pairs={{0,2},{2,0},{1,3},{3,1},{4,6},{6,4},{5,7},{7,5},{8,10},{10,8},{9,1... | collective-permute-start | bytes 786440 | tf_op jit(solution)/shard_map/ppermute | solution.py:116
  119.9 1.8 %shard_map.86 = bf16[192,2048]{1,0:T(8,128)(2,1)} custom-call(s32[8]{0:T(128)S(1)} %copy-done.7, bf16[3,192,2048]{2,1,0:T(8,128)(2,1)S(1)} %copy-done), custom_call_target="tpu_custom_call" | custom-call | tf_op jit(solution)/shard_map/pallas_call | solution.py:169
  121.7 5.0 %collective-permute-done.25 = bf16[256,512]{1,0:T(8,128)(2,1)S(1)} collective-permute-done((bf16[256,512]{1,0:T(8,128)(2,1)S(1)}, bf16[256,512]{1,0:T(8,128)(2,1)S(1)}, u32[]{:S(2)}, u32[]{:S(2)}) %collective-permute-start.25) | collective-permute-done | bytes 262176 | tf_op jit(solution)/shard_map/ppermute | solution.py:116
  126.7 0.8 fusion
  (38 shorter events, 1.0 us)
Async XLA Ops:
  0.6 9.1 %copy-start.2 = (bf16[512,512]{1,0:T(8,128)(2,1)S(1)}, bf16[512,512]{1,0:T(8,128)(2,1)}, u32[]{:S(2)}) copy-start(bf16[512,512]{1,0:T(8,128)(2,1)} %refs_2_.3) | copy-start | bytes 1572868
  0.6 9.1 %copy-start.1 = (bf16[1024,1024]{1,0:T(8,128)(2,1)S(1)}, bf16[1024,1024]{1,0:T(8,128)(2,1)}, u32[]{:S(2)}) copy-start(bf16[1024,1024]{1,0:T(8,128)(2,1)} %refs_1_.3) | copy-start | bytes 6291460
  0.7 9.1 %copy-start.6 = (s32[256]{0:T(256)S(1)}, s32[256]{0:T(256)}, u32[]{:S(2)}) copy-start(s32[256]{0:T(256)} %param.9) | copy-start | bytes 3076
  4.0 5.8 %collective-permute-start = (bf16[640,1024]{1,0:T(8,128)(2,1)}, bf16[640,1024]{1,0:T(8,128)(2,1)S(1)}, u32[]{:S(2)}, u32[]{:S(2)}) collective-permute-start(bf16[640,1024]{1,0:T(8,128)(2,1)} %get-tuple-element.39), channel_id=1, source_target_pairs={{0,1},{1,0},{2,3},{3,2},{4,5},{5,4},{6,7},{7,6},{8,9},{9,8},{10,11... | collective-permute-start | bytes 3932168 | tf_op jit(solution)/shard_map/ppermute | solution.py:116
  4.5 32.4 %collective-permute-start.3 = (bf16[640,512]{1,0:T(8,128)(2,1)}, bf16[640,512]{1,0:T(8,128)(2,1)S(1)}, u32[]{:S(2)}, u32[]{:S(2)}) collective-permute-start(bf16[640,512]{1,0:T(8,128)(2,1)} %get-tuple-element.38.refs_0_), channel_id=1, source_target_pairs={{0,4},{4,0},{8,12},{12,8},{1,5},{5,1},{9,13},{13,9},{2,6},{6,2},{1... | collective-permute-start | bytes 1966088 | tf_op jit(solution)/shard_map/ppermute | solution.py:116
  7.2 31.8 %collective-permute-start.5 = (bf16[640,512]{1,0:T(8,128)(2,1)}, bf16[640,512]{1,0:T(8,128)(2,1)S(1)}, u32[]{:S(2)}, u32[]{:S(2)}) collective-permute-start(bf16[640,512]{1,0:T(8,128)(2,1)} %get-tuple-element.38.refs_0_), channel_id=1, source_target_pairs={{0,8},{4,12},{8,0},{12,4},{1,9},{5,13},{9,1},{13,5},{2,10},{6,14},... | collective-permute-start | bytes 1966088 | tf_op jit(solution)/shard_map/ppermute | solution.py:116
  9.8 1.1 copy-start.4
  9.8 69.3 %copy-start.8 = (bf16[256,512]{1,0:T(8,128)(2,1)S(1)}, bf16[256,512]{1,0:T(8,128)(2,1)}, u32[]{:S(2)}) copy-start(bf16[256,512]{1,0:T(8,128)(2,1)} %get-tuple-element.58) | copy-start | bytes 786436
  10.1 34.1 %collective-permute-start.1 = (bf16[336,512]{1,0:T(8,128)(2,1)S(1)}, bf16[336,512]{1,0:T(8,128)(2,1)S(1)}, u32[]{:S(2)}, u32[]{:S(2)}) collective-permute-start(bf16[336,512]{1,0:T(8,128)(2,1)S(1)} %get-tuple-element.40), channel_id=1, source_target_pairs={{0,4},{4,0},{8,12},{12,8},{1,5},{5,1},{9,13},{13,9},{2,6},{6,2},{1... | collective-permute-start | bytes 1032200 | tf_op jit(solution)/shard_map/ppermute | solution.py:116
  10.9 37.6 %collective-permute-start.2 = (bf16[640,512]{1,0:T(8,128)(2,1)S(1)}, bf16[640,512]{1,0:T(8,128)(2,1)S(1)}, u32[]{:S(2)}, u32[]{:S(2)}) collective-permute-start(bf16[640,512]{1,0:T(8,128)(2,1)S(1)} %copy-done.4), channel_id=1, source_target_pairs={{0,2},{2,0},{1,3},{3,1},{4,6},{6,4},{5,7},{7,5},{8,10},{10,8},{9,1... | collective-permute-start | bytes 1966088 | tf_op jit(solution)/shard_map/ppermute | solution.py:116
  36.9 17.7 %collective-permute-start.4 = (bf16[640,512]{1,0:T(8,128)(2,1)S(1)}, bf16[640,512]{1,0:T(8,128)(2,1)S(1)}, u32[]{:S(2)}, u32[]{:S(2)}) collective-permute-start(bf16[640,512]{1,0:T(8,128)(2,1)S(1)} %collective-permute-done.3.refs_2_), channel_id=1, source_target_pairs={{0,2},{2,0},{1,3},{3,1},{4,6},{6,4},{5,7},{7,5},{8,10},{10,8},{9,1... | collective-permute-start | bytes 1966088 | tf_op jit(solution)/shard_map/ppermute | solution.py:116
  38.9 28.2 %collective-permute-start.7 = (bf16[640,512]{1,0:T(8,128)(2,1)S(1)}, bf16[640,512]{1,0:T(8,128)(2,1)S(1)}, u32[]{:S(2)}, u32[]{:S(2)}) collective-permute-start(bf16[640,512]{1,0:T(8,128)(2,1)S(1)} %collective-permute-done.5.refs_4_), channel_id=1, source_target_pairs={{0,2},{2,0},{1,3},{3,1},{4,6},{6,4},{5,7},{7,5},{8,10},{10,8},{9,1... | collective-permute-start | bytes 1966088 | tf_op jit(solution)/shard_map/ppermute | solution.py:116
  44.1 24.4 %collective-permute-start.6 = (bf16[640,512]{1,0:T(8,128)(2,1)S(1)}, bf16[640,512]{1,0:T(8,128)(2,1)S(1)}, u32[]{:S(2)}, u32[]{:S(2)}) collective-permute-start(bf16[640,512]{1,0:T(8,128)(2,1)S(1)} %collective-permute-done.5.refs_4_), channel_id=1, source_target_pairs={{0,4},{4,0},{8,12},{12,8},{1,5},{5,1},{9,13},{13,9},{2,6},{6,2},{1... | collective-permute-start | bytes 1966088 | tf_op jit(solution)/shard_map/ppermute | solution.py:116
  45.9 22.6 %collective-permute-start.9 = (bf16[336,512]{1,0:T(8,128)(2,1)S(1)}, bf16[336,512]{1,0:T(8,128)(2,1)S(1)}, u32[]{:S(2)}, u32[]{:S(2)}) collective-permute-start(bf16[336,512]{1,0:T(8,128)(2,1)S(1)} %get-tuple-element.45), channel_id=1, source_target_pairs={{0,8},{4,12},{8,0},{12,4},{1,9},{5,13},{9,1},{13,5},{2,10},{6,14},... | collective-permute-start | bytes 1032200 | tf_op jit(solution)/shard_map/ppermute | solution.py:116
  54.5 14.0 %collective-permute-start.8 = (bf16[336,512]{1,0:T(8,128)(2,1)S(1)}, bf16[336,512]{1,0:T(8,128)(2,1)S(1)}, u32[]{:S(2)}, u32[]{:S(2)}) collective-permute-start(bf16[336,512]{1,0:T(8,128)(2,1)S(1)} %collective-permute-done.1.refs_9_), channel_id=1, source_target_pairs={{0,16},{16,0},{1,17},{17,1},{2,18},{18,2},{3,19},{19,3},{4,20},{20... | collective-permute-start | bytes 1032200 | tf_op jit(solution)/shard_map/ppermute | solution.py:116
  56.4 21.1 %collective-permute-start.11 = (bf16[336,512]{1,0:T(8,128)(2,1)S(1)}, bf16[336,512]{1,0:T(8,128)(2,1)S(1)}, u32[]{:S(2)}, u32[]{:S(2)}) collective-permute-start(bf16[336,512]{1,0:T(8,128)(2,1)S(1)} %get-tuple-element.53), channel_id=1, source_target_pairs={{0,12},{4,8},{8,4},{12,0},{1,13},{5,9},{9,5},{13,1},{2,14},{6,10},... | collective-permute-start | bytes 1032200 | tf_op jit(solution)/shard_map/ppermute | solution.py:116
  68.5 9.0 %collective-permute-start.12 = (bf16[336,512]{1,0:T(8,128)(2,1)S(1)}, bf16[336,512]{1,0:T(8,128)(2,1)S(1)}, u32[]{:S(2)}, u32[]{:S(2)}) collective-permute-start(bf16[336,512]{1,0:T(8,128)(2,1)S(1)} %collective-permute-done.9.refs_11_), channel_id=1, source_target_pairs={{0,16},{16,0},{1,17},{17,1},{2,18},{18,2},{3,19},{19,3},{4,20},{20... | collective-permute-start | bytes 1032200 | tf_op jit(solution)/shard_map/ppermute | solution.py:116
  70.0 14.6 %collective-permute-start.10 = (bf16[640,512]{1,0:T(8,128)(2,1)S(1)}, bf16[640,512]{1,0:T(8,128)(2,1)S(1)}, u32[]{:S(2)}, u32[]{:S(2)}) collective-permute-start(bf16[640,512]{1,0:T(8,128)(2,1)S(1)} %collective-permute-done.6.refs_6_), channel_id=1, source_target_pairs={{0,2},{2,0},{1,3},{3,1},{4,6},{6,4},{5,7},{7,5},{8,10},{10,8},{9,1... | collective-permute-start | bytes 1966088 | tf_op jit(solution)/shard_map/ppermute | solution.py:116
  77.5 8.7 %collective-permute-start.13 = (bf16[336,512]{1,0:T(8,128)(2,1)S(1)}, bf16[336,512]{1,0:T(8,128)(2,1)S(1)}, u32[]{:S(2)}, u32[]{:S(2)}) collective-permute-start(bf16[336,512]{1,0:T(8,128)(2,1)S(1)} %collective-permute-done.11.refs_13_), channel_id=1, source_target_pairs={{0,16},{16,0},{1,17},{17,1},{2,18},{18,2},{3,19},{19,3},{4,20},{20... | collective-permute-start | bytes 1032200 | tf_op jit(solution)/shard_map/ppermute | solution.py:116
  79.1 12.2 %collective-permute-start.14 = (bf16[256,512]{1,0:T(8,128)(2,1)S(1)}, bf16[256,512]{1,0:T(8,128)(2,1)S(1)}, u32[]{:S(2)}, u32[]{:S(2)}) collective-permute-start(bf16[256,512]{1,0:T(8,128)(2,1)S(1)} %copy-done.8), channel_id=1, source_target_pairs={{0,8},{4,12},{8,0},{12,4},{1,9},{5,13},{9,1},{13,5},{2,10},{6,14},... | collective-permute-start | bytes 786440 | tf_op jit(solution)/shard_map/ppermute | solution.py:116
  91.3 3.2 %collective-permute-start.17 = (f32[1280,256]{1,0:T(8,128)}, f32[1280,256]{1,0:T(8,128)S(1)}, u32[]{:S(2)}, u32[]{:S(2)}) collective-permute-start(f32[1280,256]{1,0:T(8,128)} %get-tuple-element.62), channel_id=1, source_target_pairs={{0,1},{1,0},{2,3},{3,2},{4,5},{5,4},{6,7},{7,6},{8,9},{9,8},{10,11... | collective-permute-start | bytes 3932168 | tf_op jit(solution)/shard_map/ppermute | solution.py:116
  91.4 9.1 %collective-permute-start.16 = (bf16[256,512]{1,0:T(8,128)(2,1)S(1)}, bf16[256,512]{1,0:T(8,128)(2,1)S(1)}, u32[]{:S(2)}, u32[]{:S(2)}) collective-permute-start(bf16[256,512]{1,0:T(8,128)(2,1)S(1)} %copy-done.8), channel_id=1, source_target_pairs={{0,4},{4,0},{8,12},{12,8},{1,5},{5,1},{9,13},{13,9},{2,6},{6,2},{1... | collective-permute-start | bytes 786440 | tf_op jit(solution)/shard_map/ppermute | solution.py:116
  91.9 10.8 %collective-permute-start.15 = (bf16[256,512]{1,0:T(8,128)(2,1)S(1)}, bf16[256,512]{1,0:T(8,128)(2,1)S(1)}, u32[]{:S(2)}, u32[]{:S(2)}) collective-permute-start(bf16[256,512]{1,0:T(8,128)(2,1)S(1)} %collective-permute-done.14.refs_7_), channel_id=1, source_target_pairs={{0,16},{16,0},{1,17},{17,1},{2,18},{18,2},{3,19},{19,3},{4,20},{20... | collective-permute-start | bytes 786440 | tf_op jit(solution)/shard_map/ppermute | solution.py:116
  93.4 14.1 %collective-permute-start.21 = (bf16[256,512]{1,0:T(8,128)(2,1)S(1)}, bf16[256,512]{1,0:T(8,128)(2,1)S(1)}, u32[]{:S(2)}, u32[]{:S(2)}) collective-permute-start(bf16[256,512]{1,0:T(8,128)(2,1)S(1)} %collective-permute-done.14.refs_7_), channel_id=1, source_target_pairs={{0,4},{4,0},{8,12},{12,8},{1,5},{5,1},{9,13},{13,9},{2,6},{6,2},{1... | collective-permute-start | bytes 786440 | tf_op jit(solution)/shard_map/ppermute | solution.py:116
  94.5 16.1 %copy-start.3 = (bf16[256,2048]{1,0:T(8,128)(2,1)S(1)}, bf16[256,2048]{1,0:T(8,128)(2,1)}, u32[]{:S(2)}) copy-start(bf16[256,2048]{1,0:T(8,128)(2,1)} %refs_4_.3) | copy-start | bytes 3145732
  94.5 16.1 %copy-start.5 = (bf16[512,512]{1,0:T(8,128)(2,1)S(1)}, bf16[512,512]{1,0:T(8,128)(2,1)}, u32[]{:S(2)}) copy-start(bf16[512,512]{1,0:T(8,128)(2,1)} %refs_5_.3) | copy-start | bytes 1572868
  96.7 12.4 %collective-permute-start.18 = (bf16[256,128]{1,0:T(8,128)(2,1)S(1)}, bf16[256,128]{1,0:T(8,128)(2,1)S(1)}, u32[]{:S(2)}, u32[]{:S(2)}) collective-permute-start(bf16[256,128]{1,0:T(8,128)(2,1)S(1)} %get-tuple-element.65), channel_id=1, source_target_pairs={{0,4},{4,0},{8,12},{12,8},{1,5},{5,1},{9,13},{13,9},{2,6},{6,2},{1... | collective-permute-start | bytes 196616 | tf_op jit(solution)/shard_map/ppermute | solution.py:116
  97.8 11.4 %collective-permute-start.19 = (bf16[256,128]{1,0:T(8,128)(2,1)S(1)}, bf16[256,128]{1,0:T(8,128)(2,1)S(1)}, u32[]{:S(2)}, u32[]{:S(2)}) collective-permute-start(bf16[256,128]{1,0:T(8,128)(2,1)S(1)} %get-tuple-element.66), channel_id=1, source_target_pairs={{0,8},{4,12},{8,0},{12,4},{1,9},{5,13},{9,1},{13,5},{2,10},{6,14},... | collective-permute-start | bytes 196616 | tf_op jit(solution)/shard_map/ppermute | solution.py:116
  100.5 10.0 %collective-permute-start.20 = (bf16[256,128]{1,0:T(8,128)(2,1)S(1)}, bf16[256,128]{1,0:T(8,128)(2,1)S(1)}, u32[]{:S(2)}, u32[]{:S(2)}) collective-permute-start(bf16[256,128]{1,0:T(8,128)(2,1)S(1)} %get-tuple-element.67), channel_id=1, source_target_pairs={{0,12},{4,8},{8,4},{12,0},{1,13},{5,9},{9,5},{13,1},{2,14},{6,10},... | collective-permute-start | bytes 196616 | tf_op jit(solution)/shard_map/ppermute | solution.py:116
  102.7 12.9 %collective-permute-start.22 = (bf16[256,512]{1,0:T(8,128)(2,1)S(1)}, bf16[256,512]{1,0:T(8,128)(2,1)S(1)}, u32[]{:S(2)}, u32[]{:S(2)}) collective-permute-start(bf16[256,512]{1,0:T(8,128)(2,1)S(1)} %collective-permute-done.15.refs_8_), channel_id=1, source_target_pairs={{0,4},{4,0},{8,12},{12,8},{1,5},{5,1},{9,13},{13,9},{2,6},{6,2},{1... | collective-permute-start | bytes 786440 | tf_op jit(solution)/shard_map/ppermute | solution.py:116
  107.5 8.0 %collective-permute-start.23 = (bf16[256,512]{1,0:T(8,128)(2,1)S(1)}, bf16[256,512]{1,0:T(8,128)(2,1)S(1)}, u32[]{:S(2)}, u32[]{:S(2)}) collective-permute-start(bf16[256,512]{1,0:T(8,128)(2,1)S(1)} %collective-permute-done.16.refs_6_), channel_id=1, source_target_pairs={{0,16},{16,0},{1,17},{17,1},{2,18},{18,2},{3,19},{19,3},{4,20},{20... | collective-permute-start | bytes 786440 | tf_op jit(solution)/shard_map/ppermute | solution.py:116
  115.6 4.3 %copy-start = (bf16[3,192,2048]{2,1,0:T(8,128)(2,1)S(1)}, bf16[3,192,2048]{2,1,0:T(8,128)(2,1)}, u32[]{:S(2)}) copy-start(bf16[3,192,2048]{2,1,0:T(8,128)(2,1)} %refs_1_.2) | copy-start | bytes 7077892
  115.6 4.3 %copy-start.7 = (s32[8]{0:T(128)S(1)}, s32[8]{0:T(128)}, u32[]{:S(2)}) copy-start(s32[8]{0:T(128)} %refs_0_.1) | copy-start | bytes 100
  116.3 2.0 %collective-permute-start.24 = (bf16[2,256,512]{2,1,0:T(8,128)(2,1)S(1)}, bf16[2,256,512]{2,1,0:T(8,128)(2,1)S(1)}, u32[]{:S(2)}, u32[]{:S(2)}) collective-permute-start(bf16[2,256,512]{2,1,0:T(8,128)(2,1)S(1)} %get-tuple-element.73), channel_id=1, source_target_pairs={{0,1},{1,0},{2,3},{3,2},{4,5},{5,4},{6,7},{7,6},{8,9},{9,8},{10,11... | collective-permute-start | bytes 1572872 | tf_op jit(solution)/shard_map/ppermute | solution.py:116
  118.3 8.4 %collective-permute-start.25 = (bf16[256,512]{1,0:T(8,128)(2,1)S(1)}, bf16[256,512]{1,0:T(8,128)(2,1)S(1)}, u32[]{:S(2)}, u32[]{:S(2)}) collective-permute-start(bf16[256,512]{1,0:T(8,128)(2,1)S(1)} %fusion.1), channel_id=1, source_target_pairs={{0,2},{2,0},{1,3},{3,1},{4,6},{6,4},{5,7},{7,5},{8,10},{10,8},{9,1... | collective-permute-start | bytes 786440 | tf_op jit(solution)/shard_map/ppermute | solution.py:116

commit v20 on v15

--- a/solution.py
+++ b/solution.py
@@ -182,18 +182,15 @@
     audio_ref,
     kv_ref,
     query_ref,
-    out_w,
     packed_ref,
     other_ref,
-    half_ref,
     held_ref,
     made_ref,
     other_vmem,
-    half_vmem,
     plan_smem,
     sems,
 ):
-    rep_at, mem_at, grp_at = (lax.axis_index(name) for name in ("rep", "mem", "grp"))
+    rep_at, mem_at = lax.axis_index("rep"), lax.axis_index("mem")
     rows, width = held_ref.shape[1:]
     width = width // 2
     copies = []
@@ -206,7 +203,7 @@
 
     plan_copy = pltpu.make_async_copy(plan_ref, plan_smem, sems.at[25])
     plan_copy.start()
-    blocks = 4
+    blocks = 2
     step = rows // blocks
     for block in range(blocks):
         at = pl.ds(block * step, step)
@@ -229,7 +226,6 @@
             query_ref.at[part(2 * (1 - rep_at) + side, quarter)],
             other_vmem.at[pl.ds(depth, quarter), pl.ds(side * columns, columns)],
         )
-    copy(out_w.at[part(grp_at, half_ref.shape[0])], half_vmem)
     for started in copies:
         started.start()
     plan_copy.wait()
@@ -251,7 +247,6 @@
     stages = (
         (2, made_ref.at[audio_at], packed_ref.at[audio_at]),
         (3, other_vmem, other_ref),
-        (1, half_vmem, half_ref),
     )
     at = 2 * blocks
     for count, source, target in stages:
@@ -264,7 +259,7 @@
         leaving.wait()
 
 
-def weight_body(align_ref, kv_ref, query_ref, other_ref, own_ref, *piece_refs):
+def weight_body(align_ref, kv_ref, query_ref, other_ref, out_w, half_ref, own_ref, *piece_refs):
     seq_at, rep_at, grp_at = (lax.axis_index(name) for name in ("seq", "rep", "grp"))
     kv_half, query_half = kv_ref.shape[0] // 2, query_ref.shape[0] // 2
     kv_rows, query_rows = kv_half // 2, query_half // 2
@@ -291,6 +286,8 @@
                 kv_half + side * fold : kv_half + (side + 1) * fold, other_lanes
             ]
 
+    depth = half_ref.shape[0]
+    half_ref[...] = out_w[pl.ds(pl.multiple_of(grp_at * depth, depth), depth), :]
     for group in range(2):
         fill(own_ref, 0, group, group * kv_rows, kv_half + group * fold)
     for bit, piece_ref in enumerate(piece_refs, 1):
@@ -459,24 +456,22 @@
     def bfloat(*shape):
         return jax.ShapeDtypeStruct(shape, jnp.bfloat16)
 
-    packed, other, out_half = kernel_call(
+    packed, other = kernel_call(
         first_body,
         [
             bfloat(2 * video_rows + audio_rows, half_depth),
             bfloat(half_depth + query_quarter, kv_weight.shape[1]),
-            bfloat(out_weight.shape[0] // 2, out_weight.shape[1]),
-        ],
-        [plan, video_cache, audio_tokens, kv_weight, query_weight, out_weight],
+        ],
+        [plan, video_cache, audio_tokens, kv_weight, query_weight],
         scratch=[
             pltpu.VMEM((3, video_rows, 2 * half_depth), jnp.bfloat16),
             pltpu.VMEM((2 * video_rows + audio_rows, half_depth), jnp.bfloat16),
             pltpu.VMEM((half_depth + query_quarter, kv_weight.shape[1]), jnp.bfloat16),
-            pltpu.VMEM((out_weight.shape[0] // 2, out_weight.shape[1]), jnp.bfloat16),
             pltpu.SMEM(plan.shape, jnp.int32),
             pltpu.SemaphoreType.DMA((26,)),
         ],
-        loose_in=(0, 1, 2, 3, 4, 5),
-        loose_out=(0, 1, 2),
+        loose_in=(0, 1, 2, 3, 4),
+        loose_out=(0, 1),
         limit=61,
     )
 
@@ -484,10 +479,10 @@
     across = [swap(packed, "mem", 1)]
     other = swap(other, "rep", 1)
     rows = half_depth // 2 + query_quarter // 2
-    weight_own, *pieces = kernel_call(
+    out_half, weight_own, *pieces = kernel_call(
         weight_body,
-        [bfloat(2 * rows, 2 * width)] + [bfloat(rows + 16, 2 * width)] * 3,
-        [alignment[None], kv_weight, query_weight, other],
+        [bfloat(out_weight.shape[0] // 2, out_weight.shape[1]), bfloat(2 * rows, 2 * width)] + [bfloat(rows + 16, 2 * width)] * 3,
+        [alignment[None], kv_weight, query_weight, other, out_weight],
         limit=4,
     )
     pieces = [swap(piece, "seq", bit) for bit, piece in enumerate(pieces, 1)]

time: 123 us -> 123 us (level)
  no operation moved by 1% of the time
where the time goes in v20:
time: 123 us; the launch traced here: 122 us
  waiting for transfers between devices  69.3 us (56%)
  starting transfers between devices  36.7 us (30%)
  Pallas kernels  13 us (11%)
  local copies, waits for them, and re-layouts  1.43 us (1%)
    ppermute x26, waiting for transfers between devices, swap(): return lax.ppermute(value, axis, [(i, i ^ bit) for i in range(size)])  69.3 us
    ppermute x26, starting transfers between devices, swap(): return lax.ppermute(value, axis, [(i, i ^ bit) for i in range(size)])  36.7 us
    pallas_call x6, Pallas kernels, kernel_call(): pl.pallas_call(whole, out_shape=outs, in_specs=spots + [ANY] * len(after)...  11.1 us
  transfers between devices with their start and end apart: 26, of which 19 were waited for; matrix products, arithmetic and copies ran while one was open for 0% of the time, Pallas kernels for 7%

profile of v20, /device:TPU:0, one launch (start us, length us, event | category | flops | bytes accessed | tf_op | source)
XLA Modules:
  0.0 122.3 jit_solution(12511331886980242233)
XLA Ops:
  0.7 3.2 %shard_map.87 = (bf16[640,512]{1,0:T(8,128)(2,1)}, bf16[640,1024]{1,0:T(8,128)(2,1)}) custom-call(s32[8]{0:T(128)} %refs_0_.1, bf16[3,192,2048]{2,1,0:T(8,128)(2,1)} %refs_1_.2, bf16[256,2048]{1,0:T(8,128)(2,1)} %refs_4_.5, bf16[1024,1024]{1,0:T(8,128)(2,1)} %refs_1_.3, bf16[512,512]{1,0:T(8,128)(2,1)} %refs_2_.3), custom_call_target="tpu_custom_call" | custom-call | tf_op jit(solution)/shard_map/pallas_call | solution.py:130
  3.8 0.5 collective-permute-start
  4.4 2.6 %collective-permute-start.3 = (bf16[640,512]{1,0:T(8,128)(2,1)}, bf16[640,512]{1,0:T(8,128)(2,1)S(1)}, u32[]{:S(2)}, u32[]{:S(2)}) collective-permute-start(bf16[640,512]{1,0:T(8,128)(2,1)} %get-tuple-element.39.refs_0_), channel_id=1, source_target_pairs={{0,4},{4,0},{8,12},{12,8},{1,5},{5,1},{9,13},{13,9},{2,6},{6,2},{1... | collective-permute-start | bytes 1966088 | tf_op jit(solution)/shard_map/ppermute | solution.py:116
  7.0 2.6 %collective-permute-start.5 = (bf16[640,512]{1,0:T(8,128)(2,1)}, bf16[640,512]{1,0:T(8,128)(2,1)S(1)}, u32[]{:S(2)}, u32[]{:S(2)}) collective-permute-start(bf16[640,512]{1,0:T(8,128)(2,1)} %get-tuple-element.39.refs_0_), channel_id=1, source_target_pairs={{0,8},{4,12},{8,0},{12,4},{1,9},{5,13},{9,1},{13,5},{2,10},{6,14},... | collective-permute-start | bytes 1966088 | tf_op jit(solution)/shard_map/ppermute | solution.py:116
  9.6 1.0 copy-done.5
  10.9 0.6 collective-permute-start.1
  11.8 1.5 %collective-permute-start.2 = (bf16[640,512]{1,0:T(8,128)(2,1)S(1)}, bf16[640,512]{1,0:T(8,128)(2,1)S(1)}, u32[]{:S(2)}, u32[]{:S(2)}) collective-permute-start(bf16[640,512]{1,0:T(8,128)(2,1)S(1)} %copy-done.4), channel_id=1, source_target_pairs={{0,2},{2,0},{1,3},{3,1},{4,6},{6,4},{5,7},{7,5},{8,10},{10,8},{9,1... | collective-permute-start | bytes 1966088 | tf_op jit(solution)/shard_map/ppermute | solution.py:116
  13.2 23.5 %collective-permute-done.3.refs_2_ = bf16[640,512]{1,0:T(8,128)(2,1)S(1)} collective-permute-done((bf16[640,512]{1,0:T(8,128)(2,1)}, bf16[640,512]{1,0:T(8,128)(2,1)S(1)}, u32[]{:S(2)}, u32[]{:S(2)}) %collective-permute-start.3) | collective-permute-done | bytes 655392 | tf_op jit(solution)/shard_map/ppermute | solution.py:116
  36.7 1.9 %collective-permute-start.4 = (bf16[640,512]{1,0:T(8,128)(2,1)S(1)}, bf16[640,512]{1,0:T(8,128)(2,1)S(1)}, u32[]{:S(2)}, u32[]{:S(2)}) collective-permute-start(bf16[640,512]{1,0:T(8,128)(2,1)S(1)} %collective-permute-done.3.refs_2_), channel_id=1, source_target_pairs={{0,2},{2,0},{1,3},{3,1},{4,6},{6,4},{5,7},{7,5},{8,10},{10,8},{9,1... | collective-permute-start | bytes 1966088 | tf_op jit(solution)/shard_map/ppermute | solution.py:116
  38.8 1.5 %collective-permute-start.7 = (bf16[640,512]{1,0:T(8,128)(2,1)S(1)}, bf16[640,512]{1,0:T(8,128)(2,1)S(1)}, u32[]{:S(2)}, u32[]{:S(2)}) collective-permute-start(bf16[640,512]{1,0:T(8,128)(2,1)S(1)} %collective-permute-done.5.refs_4_), channel_id=1, source_target_pairs={{0,2},{2,0},{1,3},{3,1},{4,6},{6,4},{5,7},{7,5},{8,10},{10,8},{9,1... | collective-permute-start | bytes 1966088 | tf_op jit(solution)/shard_map/ppermute | solution.py:116
  40.3 3.7 %collective-permute-done.1.refs_9_ = bf16[336,512]{1,0:T(8,128)(2,1)S(1)} collective-permute-done((bf16[336,512]{1,0:T(8,128)(2,1)S(1)}, bf16[336,512]{1,0:T(8,128)(2,1)S(1)}, u32[]{:S(2)}, u32[]{:S(2)}) %collective-permute-start.1) | collective-permute-done | bytes 344096 | tf_op jit(solution)/shard_map/ppermute | solution.py:116
  44.0 1.8 %collective-permute-start.6 = (bf16[640,512]{1,0:T(8,128)(2,1)S(1)}, bf16[640,512]{1,0:T(8,128)(2,1)S(1)}, u32[]{:S(2)}, u32[]{:S(2)}) collective-permute-start(bf16[640,512]{1,0:T(8,128)(2,1)S(1)} %collective-permute-done.5.refs_4_), channel_id=1, source_target_pairs={{0,4},{4,0},{8,12},{12,8},{1,5},{5,1},{9,13},{13,9},{2,6},{6,2},{1... | collective-permute-start | bytes 1966088 | tf_op jit(solution)/shard_map/ppermute | solution.py:116
  45.8 2.5 %collective-permute-start.9 = (bf16[336,512]{1,0:T(8,128)(2,1)S(1)}, bf16[336,512]{1,0:T(8,128)(2,1)S(1)}, u32[]{:S(2)}, u32[]{:S(2)}) collective-permute-start(bf16[336,512]{1,0:T(8,128)(2,1)S(1)} %get-tuple-element.46), channel_id=1, source_target_pairs={{0,8},{4,12},{8,0},{12,4},{1,9},{5,13},{9,1},{13,5},{2,10},{6,14},... | collective-permute-start | bytes 1032200 | tf_op jit(solution)/shard_map/ppermute | solution.py:116
  48.3 6.1 %collective-permute-done.4.refs_3_ = bf16[640,512]{1,0:T(8,128)(2,1)S(1)} collective-permute-done((bf16[640,512]{1,0:T(8,128)(2,1)S(1)}, bf16[640,512]{1,0:T(8,128)(2,1)S(1)}, u32[]{:S(2)}, u32[]{:S(2)}) %collective-permute-start.4) | collective-permute-done | bytes 655392 | tf_op jit(solution)/shard_map/ppermute | solution.py:116
  54.4 1.9 %collective-permute-start.8 = (bf16[336,512]{1,0:T(8,128)(2,1)S(1)}, bf16[336,512]{1,0:T(8,128)(2,1)S(1)}, u32[]{:S(2)}, u32[]{:S(2)}) collective-permute-start(bf16[336,512]{1,0:T(8,128)(2,1)S(1)} %collective-permute-done.1.refs_9_), channel_id=1, source_target_pairs={{0,16},{16,0},{1,17},{17,1},{2,18},{18,2},{3,19},{19,3},{4,20},{20... | collective-permute-start | bytes 1032200 | tf_op jit(solution)/shard_map/ppermute | solution.py:116
  56.3 2.5 %collective-permute-start.11 = (bf16[336,512]{1,0:T(8,128)(2,1)S(1)}, bf16[336,512]{1,0:T(8,128)(2,1)S(1)}, u32[]{:S(2)}, u32[]{:S(2)}) collective-permute-start(bf16[336,512]{1,0:T(8,128)(2,1)S(1)} %get-tuple-element.54), channel_id=1, source_target_pairs={{0,12},{4,8},{8,4},{12,0},{1,13},{5,9},{9,5},{13,1},{2,14},{6,10},... | collective-permute-start | bytes 1032200 | tf_op jit(solution)/shard_map/ppermute | solution.py:116
  58.8 8.2 %collective-permute-done.7.refs_5_ = bf16[640,512]{1,0:T(8,128)(2,1)S(1)} collective-permute-done((bf16[640,512]{1,0:T(8,128)(2,1)S(1)}, bf16[640,512]{1,0:T(8,128)(2,1)S(1)}, u32[]{:S(2)}, u32[]{:S(2)}) %collective-permute-start.7) | collective-permute-done | bytes 655392 | tf_op jit(solution)/shard_map/ppermute | solution.py:116
  67.0 1.4 %collective-permute-done.9.refs_11_ = bf16[336,512]{1,0:T(8,128)(2,1)S(1)} collective-permute-done((bf16[336,512]{1,0:T(8,128)(2,1)S(1)}, bf16[336,512]{1,0:T(8,128)(2,1)S(1)}, u32[]{:S(2)}, u32[]{:S(2)}) %collective-permute-start.9) | collective-permute-done | bytes 344096 | tf_op jit(solution)/shard_map/ppermute | solution.py:116
  68.4 1.5 %collective-permute-start.12 = (bf16[336,512]{1,0:T(8,128)(2,1)S(1)}, bf16[336,512]{1,0:T(8,128)(2,1)S(1)}, u32[]{:S(2)}, u32[]{:S(2)}) collective-permute-start(bf16[336,512]{1,0:T(8,128)(2,1)S(1)} %collective-permute-done.9.refs_11_), channel_id=1, source_target_pairs={{0,16},{16,0},{1,17},{17,1},{2,18},{18,2},{3,19},{19,3},{4,20},{20... | collective-permute-start | bytes 1032200 | tf_op jit(solution)/shard_map/ppermute | solution.py:116
  69.9 1.5 %collective-permute-start.10 = (bf16[640,512]{1,0:T(8,128)(2,1)S(1)}, bf16[640,512]{1,0:T(8,128)(2,1)S(1)}, u32[]{:S(2)}, u32[]{:S(2)}) collective-permute-start(bf16[640,512]{1,0:T(8,128)(2,1)S(1)} %collective-permute-done.6.refs_6_), channel_id=1, source_target_pairs={{0,2},{2,0},{1,3},{3,1},{4,6},{6,4},{5,7},{7,5},{8,10},{10,8},{9,1... | collective-permute-start | bytes 1966088 | tf_op jit(solution)/shard_map/ppermute | solution.py:116
  71.4 6.0 %collective-permute-done.11.refs_13_ = bf16[336,512]{1,0:T(8,128)(2,1)S(1)} collective-permute-done((bf16[336,512]{1,0:T(8,128)(2,1)S(1)}, bf16[336,512]{1,0:T(8,128)(2,1)S(1)}, u32[]{:S(2)}, u32[]{:S(2)}) %collective-permute-start.11) | collective-permute-done | bytes 344096 | tf_op jit(solution)/shard_map/ppermute | solution.py:116
  77.4 1.5 %collective-permute-start.13 = (bf16[336,512]{1,0:T(8,128)(2,1)S(1)}, bf16[336,512]{1,0:T(8,128)(2,1)S(1)}, u32[]{:S(2)}, u32[]{:S(2)}) collective-permute-start(bf16[336,512]{1,0:T(8,128)(2,1)S(1)} %collective-permute-done.11.refs_13_), channel_id=1, source_target_pairs={{0,16},{16,0},{1,17},{17,1},{2,18},{18,2},{3,19},{19,3},{4,20},{20... | collective-permute-start | bytes 1032200 | tf_op jit(solution)/shard_map/ppermute | solution.py:116
  78.9 2.6 %collective-permute-start.14 = (bf16[256,512]{1,0:T(8,128)(2,1)S(1)}, bf16[256,512]{1,0:T(8,128)(2,1)S(1)}, u32[]{:S(2)}, u32[]{:S(2)}) collective-permute-start(bf16[256,512]{1,0:T(8,128)(2,1)S(1)} %get-tuple-element.59), channel_id=1, source_target_pairs={{0,8},{4,12},{8,0},{12,4},{1,9},{5,13},{9,1},{13,5},{2,10},{6,14},... | collective-permute-start | bytes 786440 | tf_op jit(solution)/shard_map/ppermute | solution.py:116
  81.5 1.3 %collective-permute-start.15 = (bf16[256,512]{1,0:T(8,128)(2,1)S(1)}, bf16[256,512]{1,0:T(8,128)(2,1)S(1)}, u32[]{:S(2)}, u32[]{:S(2)}) collective-permute-start(bf16[256,512]{1,0:T(8,128)(2,1)S(1)} %get-tuple-element.59), channel_id=1, source_target_pairs={{0,4},{4,0},{8,12},{12,8},{1,5},{5,1},{9,13},{13,9},{2,6},{6,2},{1... | collective-permute-start | bytes 786440 | tf_op jit(solution)/shard_map/ppermute | solution.py:116
  82.8 1.7 %collective-permute-done.10.refs_7_ = bf16[640,512]{1,0:T(8,128)(2,1)S(1)} collective-permute-done((bf16[640,512]{1,0:T(8,128)(2,1)S(1)}, bf16[640,512]{1,0:T(8,128)(2,1)S(1)}, u32[]{:S(2)}, u32[]{:S(2)}) %collective-permute-start.10) | collective-permute-done | bytes 655392 | tf_op jit(solution)/shard_map/ppermute | solution.py:116
  84.5 1.6 %collective-permute-done.13.refs_14_ = bf16[336,512]{1,0:T(8,128)(2,1)S(1)} collective-permute-done((bf16[336,512]{1,0:T(8,128)(2,1)S(1)}, bf16[336,512]{1,0:T(8,128)(2,1)S(1)}, u32[]{:S(2)}, u32[]{:S(2)}) %collective-permute-start.13) | collective-permute-done | bytes 344096 | tf_op jit(solution)/shard_map/ppermute | solution.py:116
  86.0 3.9 %shard_map.89 = (bf16[4,16,256]{2,1,0:T(8,128)(2,1)S(1)}, f32[1280,256]{1,0:T(8,128)}, f32[1280,256]{1,0:T(8,128)S(1)}) custom-call(bf16[640,512]{1,0:T(8,128)(2,1)S(1)} %copy-done.4, bf16[640,512]{1,0:T(8,128)(2,1)S(1)} %collective-permute-done.2.refs_1_, bf16[640,512]{1,0:T(8,128)(2,1)S(1)} %collective-permute-done.3.refs_2_, ...), custom_call_target="tpu_custom_call" | custom-call | tf_op jit(solution)/shard_map/pallas_call | solution.py:130
  90.0 1.2 collective-permute-done.14.refs_7_
  91.6 0.5 collective-permute-start.16
  92.1 1.2 collective-permute-start.21
  93.3 1.1 collective-permute-done.17.refs_3_
  94.4 2.2 %shard_map.90 = (bf16[256,128]{1,0:T(8,128)(2,1)S(1)}, bf16[256,128]{1,0:T(8,128)(2,1)S(1)}, bf16[256,128]{1,0:T(8,128)(2,1)S(1)}, bf16[256,128]{1,0:T(8,128)(2,1)S(1)}) custom-call(f32[1,768]{1,0:T(1,128)S(1)} %fusion.4.refs_0_, bf16[4,16,256]{2,1,0:T(8,128)(2,1)S(1)} %get-tuple-element.62.refs_1_, f32[1280,256]{1,0:T(8,128)S(1)} %get-tuple-element.63.refs_2_, ...), custom_call_target="tpu_custom_call" | custom-call | tf_op jit(solution)/shard_map/pallas_call | solution.py:130
  97.1 2.6 %collective-permute-start.19 = (bf16[256,128]{1,0:T(8,128)(2,1)S(1)}, bf16[256,128]{1,0:T(8,128)(2,1)S(1)}, u32[]{:S(2)}, u32[]{:S(2)}) collective-permute-start(bf16[256,128]{1,0:T(8,128)(2,1)S(1)} %get-tuple-element.68), channel_id=1, source_target_pairs={{0,8},{4,12},{8,0},{12,4},{1,9},{5,13},{9,1},{13,5},{2,10},{6,14},... | collective-permute-start | bytes 196616 | tf_op jit(solution)/shard_map/ppermute | solution.py:116
  99.7 1.4 %collective-permute-start.20 = (bf16[256,128]{1,0:T(8,128)(2,1)S(1)}, bf16[256,128]{1,0:T(8,128)(2,1)S(1)}, u32[]{:S(2)}, u32[]{:S(2)}) collective-permute-start(bf16[256,128]{1,0:T(8,128)(2,1)S(1)} %get-tuple-element.69), channel_id=1, source_target_pairs={{0,12},{4,8},{8,4},{12,0},{1,13},{5,9},{9,5},{13,1},{2,14},{6,10},... | collective-permute-start | bytes 196616 | tf_op jit(solution)/shard_map/ppermute | solution.py:116
  101.1 0.5 collective-permute-start.22
  101.6 0.8 collective-permute-done.21.refs_9_
  102.4 0.9 collective-permute-done.18.refs_1_
  103.3 1.7 %collective-permute-done.19.refs_2_ = bf16[256,128]{1,0:T(8,128)(2,1)S(1)} collective-permute-done((bf16[256,128]{1,0:T(8,128)(2,1)S(1)}, bf16[256,128]{1,0:T(8,128)(2,1)S(1)}, u32[]{:S(2)}, u32[]{:S(2)}) %collective-permute-start.19) | collective-permute-done | bytes 65568 | tf_op jit(solution)/shard_map/ppermute | solution.py:116
  105.0 1.5 %collective-permute-done.20.refs_3_ = bf16[256,128]{1,0:T(8,128)(2,1)S(1)} collective-permute-done((bf16[256,128]{1,0:T(8,128)(2,1)S(1)}, bf16[256,128]{1,0:T(8,128)(2,1)S(1)}, u32[]{:S(2)}, u32[]{:S(2)}) %collective-permute-start.20) | collective-permute-done | bytes 65568 | tf_op jit(solution)/shard_map/ppermute | solution.py:116
  106.5 0.9 shard_map.91
  107.4 1.2 collective-permute-done.22.refs_2_
  108.6 1.8 %collective-permute-done.23.refs_3_ = bf16[256,512]{1,0:T(8,128)(2,1)S(1)} collective-permute-done((bf16[256,512]{1,0:T(8,128)(2,1)S(1)}, bf16[256,512]{1,0:T(8,128)(2,1)S(1)}, u32[]{:S(2)}, u32[]{:S(2)}) %collective-permute-start.23) | collective-permute-done | bytes 262176 | tf_op jit(solution)/shard_map/ppermute | solution.py:116
  110.4 0.7 shard_map.92
  111.1 1.9 %collective-permute-done.24 = bf16[2,256,512]{2,1,0:T(8,128)(2,1)S(1)} collective-permute-done((bf16[2,256,512]{2,1,0:T(8,128)(2,1)S(1)}, bf16[2,256,512]{2,1,0:T(8,128)(2,1)S(1)}, u32[]{:S(2)}, u32[]{:S(2)}) %collective-permute-start.24) | collective-permute-done | bytes 524320 | tf_op jit(solution)/shard_map/ppermute | solution.py:116
  113.1 1.5 %collective-permute-start.25 = (bf16[256,512]{1,0:T(8,128)(2,1)S(1)}, bf16[256,512]{1,0:T(8,128)(2,1)S(1)}, u32[]{:S(2)}, u32[]{:S(2)}) collective-permute-start(bf16[256,512]{1,0:T(8,128)(2,1)S(1)} %fusion.1), channel_id=1, source_target_pairs={{0,2},{2,0},{1,3},{3,1},{4,6},{6,4},{5,7},{7,5},{8,10},{10,8},{9,1... | collective-permute-start | bytes 786440 | tf_op jit(solution)/shard_map/ppermute | solution.py:116
  114.6 1.8 %shard_map.86 = bf16[192,2048]{1,0:T(8,128)(2,1)} custom-call(s32[8]{0:T(128)S(1)} %copy-done.8, bf16[3,192,2048]{2,1,0:T(8,128)(2,1)S(1)} %copy-done), custom_call_target="tpu_custom_call" | custom-call | tf_op jit(solution)/shard_map/pallas_call | solution.py:169
  116.5 5.0 %collective-permute-done.25 = bf16[256,512]{1,0:T(8,128)(2,1)S(1)} collective-permute-done((bf16[256,512]{1,0:T(8,128)(2,1)S(1)}, bf16[256,512]{1,0:T(8,128)(2,1)S(1)}, u32[]{:S(2)}, u32[]{:S(2)}) %collective-permute-start.25) | collective-permute-done | bytes 262176 | tf_op jit(solution)/shard_map/ppermute | solution.py:116
  121.5 0.8 fusion
  (38 shorter events, 1.7 us)
Async XLA Ops:
  0.6 9.0 %copy-start.2 = (bf16[512,512]{1,0:T(8,128)(2,1)S(1)}, bf16[512,512]{1,0:T(8,128)(2,1)}, u32[]{:S(2)}) copy-start(bf16[512,512]{1,0:T(8,128)(2,1)} %refs_2_.3) | copy-start | bytes 1572868
  0.6 9.0 %copy-start.7 = (s32[256]{0:T(256)S(1)}, s32[256]{0:T(256)}, u32[]{:S(2)}) copy-start(s32[256]{0:T(256)} %param.9) | copy-start | bytes 3076
  0.7 9.0 %copy-start.1 = (bf16[1024,1024]{1,0:T(8,128)(2,1)S(1)}, bf16[1024,1024]{1,0:T(8,128)(2,1)}, u32[]{:S(2)}) copy-start(bf16[1024,1024]{1,0:T(8,128)(2,1)} %refs_1_.3) | copy-start | bytes 6291460
  3.8 5.8 %collective-permute-start = (bf16[640,1024]{1,0:T(8,128)(2,1)}, bf16[640,1024]{1,0:T(8,128)(2,1)S(1)}, u32[]{:S(2)}, u32[]{:S(2)}) collective-permute-start(bf16[640,1024]{1,0:T(8,128)(2,1)} %get-tuple-element.40), channel_id=1, source_target_pairs={{0,1},{1,0},{2,3},{3,2},{4,5},{5,4},{6,7},{7,6},{8,9},{9,8},{10,11... | collective-permute-start | bytes 3932168 | tf_op jit(solution)/shard_map/ppermute | solution.py:116
  4.4 32.4 %collective-permute-start.3 = (bf16[640,512]{1,0:T(8,128)(2,1)}, bf16[640,512]{1,0:T(8,128)(2,1)S(1)}, u32[]{:S(2)}, u32[]{:S(2)}) collective-permute-start(bf16[640,512]{1,0:T(8,128)(2,1)} %get-tuple-element.39.refs_0_), channel_id=1, source_target_pairs={{0,4},{4,0},{8,12},{12,8},{1,5},{5,1},{9,13},{13,9},{2,6},{6,2},{1... | collective-permute-start | bytes 1966088 | tf_op jit(solution)/shard_map/ppermute | solution.py:116
  7.0 31.8 %collective-permute-start.5 = (bf16[640,512]{1,0:T(8,128)(2,1)}, bf16[640,512]{1,0:T(8,128)(2,1)S(1)}, u32[]{:S(2)}, u32[]{:S(2)}) collective-permute-start(bf16[640,512]{1,0:T(8,128)(2,1)} %get-tuple-element.39.refs_0_), channel_id=1, source_target_pairs={{0,8},{4,12},{8,0},{12,4},{1,9},{5,13},{9,1},{13,5},{2,10},{6,14},... | collective-permute-start | bytes 1966088 | tf_op jit(solution)/shard_map/ppermute | solution.py:116
  9.6 1.0 copy-start.5
  10.7 1.1 copy-start.4
  10.9 33.0 %collective-permute-start.1 = (bf16[336,512]{1,0:T(8,128)(2,1)S(1)}, bf16[336,512]{1,0:T(8,128)(2,1)S(1)}, u32[]{:S(2)}, u32[]{:S(2)}) collective-permute-start(bf16[336,512]{1,0:T(8,128)(2,1)S(1)} %get-tuple-element.41), channel_id=1, source_target_pairs={{0,4},{4,0},{8,12},{12,8},{1,5},{5,1},{9,13},{13,9},{2,6},{6,2},{1... | collective-permute-start | bytes 1032200 | tf_op jit(solution)/shard_map/ppermute | solution.py:116
  11.8 36.6 %collective-permute-start.2 = (bf16[640,512]{1,0:T(8,128)(2,1)S(1)}, bf16[640,512]{1,0:T(8,128)(2,1)S(1)}, u32[]{:S(2)}, u32[]{:S(2)}) collective-permute-start(bf16[640,512]{1,0:T(8,128)(2,1)S(1)} %copy-done.4), channel_id=1, source_target_pairs={{0,2},{2,0},{1,3},{3,1},{4,6},{6,4},{5,7},{7,5},{8,10},{10,8},{9,1... | collective-permute-start | bytes 1966088 | tf_op jit(solution)/shard_map/ppermute | solution.py:116
  36.7 17.7 %collective-permute-start.4 = (bf16[640,512]{1,0:T(8,128)(2,1)S(1)}, bf16[640,512]{1,0:T(8,128)(2,1)S(1)}, u32[]{:S(2)}, u32[]{:S(2)}) collective-permute-start(bf16[640,512]{1,0:T(8,128)(2,1)S(1)} %collective-permute-done.3.refs_2_), channel_id=1, source_target_pairs={{0,2},{2,0},{1,3},{3,1},{4,6},{6,4},{5,7},{7,5},{8,10},{10,8},{9,1... | collective-permute-start | bytes 1966088 | tf_op jit(solution)/shard_map/ppermute | solution.py:116
  38.8 28.2 %collective-permute-start.7 = (bf16[640,512]{1,0:T(8,128)(2,1)S(1)}, bf16[640,512]{1,0:T(8,128)(2,1)S(1)}, u32[]{:S(2)}, u32[]{:S(2)}) collective-permute-start(bf16[640,512]{1,0:T(8,128)(2,1)S(1)} %collective-permute-done.5.refs_4_), channel_id=1, source_target_pairs={{0,2},{2,0},{1,3},{3,1},{4,6},{6,4},{5,7},{7,5},{8,10},{10,8},{9,1... | collective-permute-start | bytes 1966088 | tf_op jit(solution)/shard_map/ppermute | solution.py:116
  44.0 24.4 %collective-permute-start.6 = (bf16[640,512]{1,0:T(8,128)(2,1)S(1)}, bf16[640,512]{1,0:T(8,128)(2,1)S(1)}, u32[]{:S(2)}, u32[]{:S(2)}) collective-permute-start(bf16[640,512]{1,0:T(8,128)(2,1)S(1)} %collective-permute-done.5.refs_4_), channel_id=1, source_target_pairs={{0,4},{4,0},{8,12},{12,8},{1,5},{5,1},{9,13},{13,9},{2,6},{6,2},{1... | collective-permute-start | bytes 1966088 | tf_op jit(solution)/shard_map/ppermute | solution.py:116
  45.8 22.6 %collective-permute-start.9 = (bf16[336,512]{1,0:T(8,128)(2,1)S(1)}, bf16[336,512]{1,0:T(8,128)(2,1)S(1)}, u32[]{:S(2)}, u32[]{:S(2)}) collective-permute-start(bf16[336,512]{1,0:T(8,128)(2,1)S(1)} %get-tuple-element.46), channel_id=1, source_target_pairs={{0,8},{4,12},{8,0},{12,4},{1,9},{5,13},{9,1},{13,5},{2,10},{6,14},... | collective-permute-start | bytes 1032200 | tf_op jit(solution)/shard_map/ppermute | solution.py:116
  54.4 14.0 %collective-permute-start.8 = (bf16[336,512]{1,0:T(8,128)(2,1)S(1)}, bf16[336,512]{1,0:T(8,128)(2,1)S(1)}, u32[]{:S(2)}, u32[]{:S(2)}) collective-permute-start(bf16[336,512]{1,0:T(8,128)(2,1)S(1)} %collective-permute-done.1.refs_9_), channel_id=1, source_target_pairs={{0,16},{16,0},{1,17},{17,1},{2,18},{18,2},{3,19},{19,3},{4,20},{20... | collective-permute-start | bytes 1032200 | tf_op jit(solution)/shard_map/ppermute | solution.py:116
  56.3 21.1 %collective-permute-start.11 = (bf16[336,512]{1,0:T(8,128)(2,1)S(1)}, bf16[336,512]{1,0:T(8,128)(2,1)S(1)}, u32[]{:S(2)}, u32[]{:S(2)}) collective-permute-start(bf16[336,512]{1,0:T(8,128)(2,1)S(1)} %get-tuple-element.54), channel_id=1, source_target_pairs={{0,12},{4,8},{8,4},{12,0},{1,13},{5,9},{9,5},{13,1},{2,14},{6,10},... | collective-permute-start | bytes 1032200 | tf_op jit(solution)/shard_map/ppermute | solution.py:116
  68.4 9.0 %collective-permute-start.12 = (bf16[336,512]{1,0:T(8,128)(2,1)S(1)}, bf16[336,512]{1,0:T(8,128)(2,1)S(1)}, u32[]{:S(2)}, u32[]{:S(2)}) collective-permute-start(bf16[336,512]{1,0:T(8,128)(2,1)S(1)} %collective-permute-done.9.refs_11_), channel_id=1, source_target_pairs={{0,16},{16,0},{1,17},{17,1},{2,18},{18,2},{3,19},{19,3},{4,20},{20... | collective-permute-start | bytes 1032200 | tf_op jit(solution)/shard_map/ppermute | solution.py:116
  69.9 14.6 %collective-permute-start.10 = (bf16[640,512]{1,0:T(8,128)(2,1)S(1)}, bf16[640,512]{1,0:T(8,128)(2,1)S(1)}, u32[]{:S(2)}, u32[]{:S(2)}) collective-permute-start(bf16[640,512]{1,0:T(8,128)(2,1)S(1)} %collective-permute-done.6.refs_6_), channel_id=1, source_target_pairs={{0,2},{2,0},{1,3},{3,1},{4,6},{6,4},{5,7},{7,5},{8,10},{10,8},{9,1... | collective-permute-start | bytes 1966088 | tf_op jit(solution)/shard_map/ppermute | solution.py:116
  77.4 8.7 %collective-permute-start.13 = (bf16[336,512]{1,0:T(8,128)(2,1)S(1)}, bf16[336,512]{1,0:T(8,128)(2,1)S(1)}, u32[]{:S(2)}, u32[]{:S(2)}) collective-permute-start(bf16[336,512]{1,0:T(8,128)(2,1)S(1)} %collective-permute-done.11.refs_13_), channel_id=1, source_target_pairs={{0,16},{16,0},{1,17},{17,1},{2,18},{18,2},{3,19},{19,3},{4,20},{20... | collective-permute-start | bytes 1032200 | tf_op jit(solution)/shard_map/ppermute | solution.py:116
  78.9 12.3 %collective-permute-start.14 = (bf16[256,512]{1,0:T(8,128)(2,1)S(1)}, bf16[256,512]{1,0:T(8,128)(2,1)S(1)}, u32[]{:S(2)}, u32[]{:S(2)}) collective-permute-start(bf16[256,512]{1,0:T(8,128)(2,1)S(1)} %get-tuple-element.59), channel_id=1, source_target_pairs={{0,8},{4,12},{8,0},{12,4},{1,9},{5,13},{9,1},{13,5},{2,10},{6,14},... | collective-permute-start | bytes 786440 | tf_op jit(solution)/shard_map/ppermute | solution.py:116
  81.5 9.6 %collective-permute-start.15 = (bf16[256,512]{1,0:T(8,128)(2,1)S(1)}, bf16[256,512]{1,0:T(8,128)(2,1)S(1)}, u32[]{:S(2)}, u32[]{:S(2)}) collective-permute-start(bf16[256,512]{1,0:T(8,128)(2,1)S(1)} %get-tuple-element.59), channel_id=1, source_target_pairs={{0,4},{4,0},{8,12},{12,8},{1,5},{5,1},{9,13},{13,9},{2,6},{6,2},{1... | collective-permute-start | bytes 786440 | tf_op jit(solution)/shard_map/ppermute | solution.py:116
  91.2 3.2 %collective-permute-start.17 = (f32[1280,256]{1,0:T(8,128)}, f32[1280,256]{1,0:T(8,128)S(1)}, u32[]{:S(2)}, u32[]{:S(2)}) collective-permute-start(f32[1280,256]{1,0:T(8,128)} %get-tuple-element.64), channel_id=1, source_target_pairs={{0,1},{1,0},{2,3},{3,2},{4,5},{5,4},{6,7},{7,6},{8,9},{9,8},{10,11... | collective-permute-start | bytes 3932168 | tf_op jit(solution)/shard_map/ppermute | solution.py:116
  91.6 9.5 %collective-permute-start.16 = (bf16[256,512]{1,0:T(8,128)(2,1)S(1)}, bf16[256,512]{1,0:T(8,128)(2,1)S(1)}, u32[]{:S(2)}, u32[]{:S(2)}) collective-permute-start(bf16[256,512]{1,0:T(8,128)(2,1)S(1)} %collective-permute-done.14.refs_7_), channel_id=1, source_target_pairs={{0,16},{16,0},{1,17},{17,1},{2,18},{18,2},{3,19},{19,3},{4,20},{20... | collective-permute-start | bytes 786440 | tf_op jit(solution)/shard_map/ppermute | solution.py:116
  92.1 10.3 %collective-permute-start.21 = (bf16[256,512]{1,0:T(8,128)(2,1)S(1)}, bf16[256,512]{1,0:T(8,128)(2,1)S(1)}, u32[]{:S(2)}, u32[]{:S(2)}) collective-permute-start(bf16[256,512]{1,0:T(8,128)(2,1)S(1)} %collective-permute-done.14.refs_7_), channel_id=1, source_target_pairs={{0,4},{4,0},{8,12},{12,8},{1,5},{5,1},{9,13},{13,9},{2,6},{6,2},{1... | collective-permute-start | bytes 786440 | tf_op jit(solution)/shard_map/ppermute | solution.py:116
  94.4 12.1 %copy-start.3 = (bf16[256,2048]{1,0:T(8,128)(2,1)S(1)}, bf16[256,2048]{1,0:T(8,128)(2,1)}, u32[]{:S(2)}) copy-start(bf16[256,2048]{1,0:T(8,128)(2,1)} %refs_4_.5) | copy-start | bytes 3145732
  94.4 12.1 %copy-start.6 = (bf16[512,512]{1,0:T(8,128)(2,1)S(1)}, bf16[512,512]{1,0:T(8,128)(2,1)}, u32[]{:S(2)}) copy-start(bf16[512,512]{1,0:T(8,128)(2,1)} %refs_5_.1) | copy-start | bytes 1572868
  96.6 6.7 %collective-permute-start.18 = (bf16[256,128]{1,0:T(8,128)(2,1)S(1)}, bf16[256,128]{1,0:T(8,128)(2,1)S(1)}, u32[]{:S(2)}, u32[]{:S(2)}) collective-permute-start(bf16[256,128]{1,0:T(8,128)(2,1)S(1)} %get-tuple-element.67), channel_id=1, source_target_pairs={{0,4},{4,0},{8,12},{12,8},{1,5},{5,1},{9,13},{13,9},{2,6},{6,2},{1... | collective-permute-start | bytes 196616 | tf_op jit(solution)/shard_map/ppermute | solution.py:116
  97.1 7.9 %collective-permute-start.19 = (bf16[256,128]{1,0:T(8,128)(2,1)S(1)}, bf16[256,128]{1,0:T(8,128)(2,1)S(1)}, u32[]{:S(2)}, u32[]{:S(2)}) collective-permute-start(bf16[256,128]{1,0:T(8,128)(2,1)S(1)} %get-tuple-element.68), channel_id=1, source_target_pairs={{0,8},{4,12},{8,0},{12,4},{1,9},{5,13},{9,1},{13,5},{2,10},{6,14},... | collective-permute-start | bytes 196616 | tf_op jit(solution)/shard_map/ppermute | solution.py:116
  99.7 6.8 %collective-permute-start.20 = (bf16[256,128]{1,0:T(8,128)(2,1)S(1)}, bf16[256,128]{1,0:T(8,128)(2,1)S(1)}, u32[]{:S(2)}, u32[]{:S(2)}) collective-permute-start(bf16[256,128]{1,0:T(8,128)(2,1)S(1)} %get-tuple-element.69), channel_id=1, source_target_pairs={{0,12},{4,8},{8,4},{12,0},{1,13},{5,9},{9,5},{13,1},{2,14},{6,10},... | collective-permute-start | bytes 196616 | tf_op jit(solution)/shard_map/ppermute | solution.py:116
  101.1 7.5 %collective-permute-start.22 = (bf16[256,512]{1,0:T(8,128)(2,1)S(1)}, bf16[256,512]{1,0:T(8,128)(2,1)S(1)}, u32[]{:S(2)}, u32[]{:S(2)}) collective-permute-start(bf16[256,512]{1,0:T(8,128)(2,1)S(1)} %collective-permute-done.15.refs_6_), channel_id=1, source_target_pairs={{0,16},{16,0},{1,17},{17,1},{2,18},{18,2},{3,19},{19,3},{4,20},{20... | collective-permute-start | bytes 786440 | tf_op jit(solution)/shard_map/ppermute | solution.py:116
  102.4 8.0 %collective-permute-start.23 = (bf16[256,512]{1,0:T(8,128)(2,1)S(1)}, bf16[256,512]{1,0:T(8,128)(2,1)S(1)}, u32[]{:S(2)}, u32[]{:S(2)}) collective-permute-start(bf16[256,512]{1,0:T(8,128)(2,1)S(1)} %collective-permute-done.16.refs_8_), channel_id=1, source_target_pairs={{0,4},{4,0},{8,12},{12,8},{1,5},{5,1},{9,13},{13,9},{2,6},{6,2},{1... | collective-permute-start | bytes 786440 | tf_op jit(solution)/shard_map/ppermute | solution.py:116
  110.4 4.3 %copy-start = (bf16[3,192,2048]{2,1,0:T(8,128)(2,1)S(1)}, bf16[3,192,2048]{2,1,0:T(8,128)(2,1)}, u32[]{:S(2)}) copy-start(bf16[3,192,2048]{2,1,0:T(8,128)(2,1)} %refs_1_.2) | copy-start | bytes 7077892
  110.4 4.3 %copy-start.8 = (s32[8]{0:T(128)S(1)}, s32[8]{0:T(128)}, u32[]{:S(2)}) copy-start(s32[8]{0:T(128)} %refs_0_.1) | copy-start | bytes 100
  111.0 2.0 %collective-permute-start.24 = (bf16[2,256,512]{2,1,0:T(8,128)(2,1)S(1)}, bf16[2,256,512]{2,1,0:T(8,128)(2,1)S(1)}, u32[]{:S(2)}, u32[]{:S(2)}) collective-permute-start(bf16[2,256,512]{2,1,0:T(8,128)(2,1)S(1)} %get-tuple-element.75), channel_id=1, source_target_pairs={{0,1},{1,0},{2,3},{3,2},{4,5},{5,4},{6,7},{7,6},{8,9},{9,8},{10,11... | collective-permute-start | bytes 1572872 | tf_op jit(solution)/shard_map/ppermute | solution.py:116
  113.1 8.4 %collective-permute-start.25 = (bf16[256,512]{1,0:T(8,128)(2,1)S(1)}, bf16[256,512]{1,0:T(8,128)(2,1)S(1)}, u32[]{:S(2)}, u32[]{:S(2)}) collective-permute-start(bf16[256,512]{1,0:T(8,128)(2,1)S(1)} %fusion.1), channel_id=1, source_target_pairs={{0,2},{2,0},{1,3},{3,1},{4,6},{6,4},{5,7},{7,5},{8,10},{10,8},{9,1... | collective-permute-start | bytes 786440 | tf_op jit(solution)/shard_map/ppermute | solution.py:116

commit v21 on v20

--- a/solution.py
+++ b/solution.py
@@ -363,7 +363,7 @@
         (((1,), (1,)), ((), ())),
         preferred_element_type=jnp.float32,
     ) * (1.0 / HEAD_DIM**0.5)
-    scores = scores - SLOPE * jnp.abs(frames_ref[...] - align) / FRAMES
+    scores = scores - jnp.abs(frames_ref[...] - align)
     exp_terms = jnp.exp(scores - jnp.max(scores, axis=1, keepdims=True))
     weighted = jnp.dot(
         exp_terms.astype(jnp.bfloat16), kv_ref[:, HEAD_DIM:], preferred_element_type=jnp.float32
@@ -386,7 +386,7 @@
             slice(side * HEAD_DIM, (side + 1) * HEAD_DIM),
         )
     for bit, out_ref in enumerate(out_refs):
-        align = align_ref[bit].astype(jnp.float32)[:8].T[:, :1]
+        align = (align_ref[bit].astype(jnp.float32)[:8] * (SLOPE / FRAMES)).T[:, :1]
         out_ref[...] = attend(query_ref[bit], kv_ref, frames_ref, align)
 
 
@@ -531,6 +531,7 @@
     blocks = jnp.stack([seq_at, seq_at ^ 1, seq_at ^ 2, seq_at ^ 3])
     positions = blocks[:, None] * video_rows + jnp.arange(video_rows, dtype=jnp.int32)[None, :]
     frames_video = (positions.reshape(1, span) * FRAMES // span).astype(jnp.float32)
+    frames_video = frames_video * (SLOPE / FRAMES)
     own_piece, near_piece, far_piece, farther_piece = kernel_call(
         attention_body,
         [bfloat(audio_rows, HEAD_DIM)] * 4,

time: 123 us -> 123 us (level)
  no operation moved by 1% of the time
where the time goes in v21:
time: 123 us; the launch traced here: 122 us
  waiting for transfers between devices  69.4 us (56%)
  starting transfers between devices  36.7 us (30%)
  Pallas kernels  12.9 us (10%)
  local copies, waits for them, and re-layouts  1.43 us (1%)
    ppermute x26, waiting for transfers between devices, swap(): return lax.ppermute(value, axis, [(i, i ^ bit) for i in range(size)])  69.4 us
    ppermute x26, starting transfers between devices, swap(): return lax.ppermute(value, axis, [(i, i ^ bit) for i in range(size)])  36.7 us
    pallas_call x6, Pallas kernels, kernel_call(): pl.pallas_call(whole, out_shape=outs, in_specs=spots + [ANY] * len(after)...  11.1 us
  transfers between devices with their start and end apart: 26, of which 19 were waited for; matrix products, arithmetic and copies ran while one was open for 0% of the time, Pallas kernels for 7%

profile of v21, /device:TPU:0, one launch (start us, length us, event | category | flops | bytes accessed | tf_op | source)
XLA Modules:
  0.0 122.3 jit_solution(13950103699223559898)
XLA Ops:
  0.7 3.2 %shard_map.87 = (bf16[640,512]{1,0:T(8,128)(2,1)}, bf16[640,1024]{1,0:T(8,128)(2,1)}) custom-call(s32[8]{0:T(128)} %refs_0_.1, bf16[3,192,2048]{2,1,0:T(8,128)(2,1)} %refs_1_.2, bf16[256,2048]{1,0:T(8,128)(2,1)} %refs_4_.5, bf16[1024,1024]{1,0:T(8,128)(2,1)} %refs_1_.3, bf16[512,512]{1,0:T(8,128)(2,1)} %refs_2_.3), custom_call_target="tpu_custom_call" | custom-call | tf_op jit(solution)/shard_map/pallas_call | solution.py:130
  3.8 0.5 collective-permute-start
  4.4 2.6 %collective-permute-start.3 = (bf16[640,512]{1,0:T(8,128)(2,1)}, bf16[640,512]{1,0:T(8,128)(2,1)S(1)}, u32[]{:S(2)}, u32[]{:S(2)}) collective-permute-start(bf16[640,512]{1,0:T(8,128)(2,1)} %get-tuple-element.39.refs_0_), channel_id=1, source_target_pairs={{0,4},{4,0},{8,12},{12,8},{1,5},{5,1},{9,13},{13,9},{2,6},{6,2},{1... | collective-permute-start | bytes 1966088 | tf_op jit(solution)/shard_map/ppermute | solution.py:116
  7.0 2.6 %collective-permute-start.5 = (bf16[640,512]{1,0:T(8,128)(2,1)}, bf16[640,512]{1,0:T(8,128)(2,1)S(1)}, u32[]{:S(2)}, u32[]{:S(2)}) collective-permute-start(bf16[640,512]{1,0:T(8,128)(2,1)} %get-tuple-element.39.refs_0_), channel_id=1, source_target_pairs={{0,8},{4,12},{8,0},{12,4},{1,9},{5,13},{9,1},{13,5},{2,10},{6,14},... | collective-permute-start | bytes 1966088 | tf_op jit(solution)/shard_map/ppermute | solution.py:116
  9.6 1.0 copy-done.5
  10.9 0.6 collective-permute-start.1
  11.8 1.5 %collective-permute-start.2 = (bf16[640,512]{1,0:T(8,128)(2,1)S(1)}, bf16[640,512]{1,0:T(8,128)(2,1)S(1)}, u32[]{:S(2)}, u32[]{:S(2)}) collective-permute-start(bf16[640,512]{1,0:T(8,128)(2,1)S(1)} %copy-done.4), channel_id=1, source_target_pairs={{0,2},{2,0},{1,3},{3,1},{4,6},{6,4},{5,7},{7,5},{8,10},{10,8},{9,1... | collective-permute-start | bytes 1966088 | tf_op jit(solution)/shard_map/ppermute | solution.py:116
  13.2 23.5 %collective-permute-done.3.refs_2_ = bf16[640,512]{1,0:T(8,128)(2,1)S(1)} collective-permute-done((bf16[640,512]{1,0:T(8,128)(2,1)}, bf16[640,512]{1,0:T(8,128)(2,1)S(1)}, u32[]{:S(2)}, u32[]{:S(2)}) %collective-permute-start.3) | collective-permute-done | bytes 655392 | tf_op jit(solution)/shard_map/ppermute | solution.py:116
  36.7 1.9 %collective-permute-start.4 = (bf16[640,512]{1,0:T(8,128)(2,1)S(1)}, bf16[640,512]{1,0:T(8,128)(2,1)S(1)}, u32[]{:S(2)}, u32[]{:S(2)}) collective-permute-start(bf16[640,512]{1,0:T(8,128)(2,1)S(1)} %collective-permute-done.3.refs_2_), channel_id=1, source_target_pairs={{0,2},{2,0},{1,3},{3,1},{4,6},{6,4},{5,7},{7,5},{8,10},{10,8},{9,1... | collective-permute-start | bytes 1966088 | tf_op jit(solution)/shard_map/ppermute | solution.py:116
  38.8 1.5 %collective-permute-start.7 = (bf16[640,512]{1,0:T(8,128)(2,1)S(1)}, bf16[640,512]{1,0:T(8,128)(2,1)S(1)}, u32[]{:S(2)}, u32[]{:S(2)}) collective-permute-start(bf16[640,512]{1,0:T(8,128)(2,1)S(1)} %collective-permute-done.5.refs_4_), channel_id=1, source_target_pairs={{0,2},{2,0},{1,3},{3,1},{4,6},{6,4},{5,7},{7,5},{8,10},{10,8},{9,1... | collective-permute-start | bytes 1966088 | tf_op jit(solution)/shard_map/ppermute | solution.py:116
  40.3 3.7 %collective-permute-done.1.refs_9_ = bf16[336,512]{1,0:T(8,128)(2,1)S(1)} collective-permute-done((bf16[336,512]{1,0:T(8,128)(2,1)S(1)}, bf16[336,512]{1,0:T(8,128)(2,1)S(1)}, u32[]{:S(2)}, u32[]{:S(2)}) %collective-permute-start.1) | collective-permute-done | bytes 344096 | tf_op jit(solution)/shard_map/ppermute | solution.py:116
  44.0 1.8 %collective-permute-start.6 = (bf16[640,512]{1,0:T(8,128)(2,1)S(1)}, bf16[640,512]{1,0:T(8,128)(2,1)S(1)}, u32[]{:S(2)}, u32[]{:S(2)}) collective-permute-start(bf16[640,512]{1,0:T(8,128)(2,1)S(1)} %collective-permute-done.5.refs_4_), channel_id=1, source_target_pairs={{0,4},{4,0},{8,12},{12,8},{1,5},{5,1},{9,13},{13,9},{2,6},{6,2},{1... | collective-permute-start | bytes 1966088 | tf_op jit(solution)/shard_map/ppermute | solution.py:116
  45.8 2.5 %collective-permute-start.9 = (bf16[336,512]{1,0:T(8,128)(2,1)S(1)}, bf16[336,512]{1,0:T(8,128)(2,1)S(1)}, u32[]{:S(2)}, u32[]{:S(2)}) collective-permute-start(bf16[336,512]{1,0:T(8,128)(2,1)S(1)} %get-tuple-element.46), channel_id=1, source_target_pairs={{0,8},{4,12},{8,0},{12,4},{1,9},{5,13},{9,1},{13,5},{2,10},{6,14},... | collective-permute-start | bytes 1032200 | tf_op jit(solution)/shard_map/ppermute | solution.py:116
  48.3 6.1 %collective-permute-done.4.refs_3_ = bf16[640,512]{1,0:T(8,128)(2,1)S(1)} collective-permute-done((bf16[640,512]{1,0:T(8,128)(2,1)S(1)}, bf16[640,512]{1,0:T(8,128)(2,1)S(1)}, u32[]{:S(2)}, u32[]{:S(2)}) %collective-permute-start.4) | collective-permute-done | bytes 655392 | tf_op jit(solution)/shard_map/ppermute | solution.py:116
  54.4 1.9 %collective-permute-start.8 = (bf16[336,512]{1,0:T(8,128)(2,1)S(1)}, bf16[336,512]{1,0:T(8,128)(2,1)S(1)}, u32[]{:S(2)}, u32[]{:S(2)}) collective-permute-start(bf16[336,512]{1,0:T(8,128)(2,1)S(1)} %collective-permute-done.1.refs_9_), channel_id=1, source_target_pairs={{0,16},{16,0},{1,17},{17,1},{2,18},{18,2},{3,19},{19,3},{4,20},{20... | collective-permute-start | bytes 1032200 | tf_op jit(solution)/shard_map/ppermute | solution.py:116
  56.3 2.5 %collective-permute-start.11 = (bf16[336,512]{1,0:T(8,128)(2,1)S(1)}, bf16[336,512]{1,0:T(8,128)(2,1)S(1)}, u32[]{:S(2)}, u32[]{:S(2)}) collective-permute-start(bf16[336,512]{1,0:T(8,128)(2,1)S(1)} %get-tuple-element.54), channel_id=1, source_target_pairs={{0,12},{4,8},{8,4},{12,0},{1,13},{5,9},{9,5},{13,1},{2,14},{6,10},... | collective-permute-start | bytes 1032200 | tf_op jit(solution)/shard_map/ppermute | solution.py:116
  58.8 8.2 %collective-permute-done.7.refs_5_ = bf16[640,512]{1,0:T(8,128)(2,1)S(1)} collective-permute-done((bf16[640,512]{1,0:T(8,128)(2,1)S(1)}, bf16[640,512]{1,0:T(8,128)(2,1)S(1)}, u32[]{:S(2)}, u32[]{:S(2)}) %collective-permute-start.7) | collective-permute-done | bytes 655392 | tf_op jit(solution)/shard_map/ppermute | solution.py:116
  67.0 1.4 %collective-permute-done.9.refs_11_ = bf16[336,512]{1,0:T(8,128)(2,1)S(1)} collective-permute-done((bf16[336,512]{1,0:T(8,128)(2,1)S(1)}, bf16[336,512]{1,0:T(8,128)(2,1)S(1)}, u32[]{:S(2)}, u32[]{:S(2)}) %collective-permute-start.9) | collective-permute-done | bytes 344096 | tf_op jit(solution)/shard_map/ppermute | solution.py:116
  68.4 1.5 %collective-permute-start.12 = (bf16[336,512]{1,0:T(8,128)(2,1)S(1)}, bf16[336,512]{1,0:T(8,128)(2,1)S(1)}, u32[]{:S(2)}, u32[]{:S(2)}) collective-permute-start(bf16[336,512]{1,0:T(8,128)(2,1)S(1)} %collective-permute-done.9.refs_11_), channel_id=1, source_target_pairs={{0,16},{16,0},{1,17},{17,1},{2,18},{18,2},{3,19},{19,3},{4,20},{20... | collective-permute-start | bytes 1032200 | tf_op jit(solution)/shard_map/ppermute | solution.py:116
  69.9 1.5 %collective-permute-start.10 = (bf16[640,512]{1,0:T(8,128)(2,1)S(1)}, bf16[640,512]{1,0:T(8,128)(2,1)S(1)}, u32[]{:S(2)}, u32[]{:S(2)}) collective-permute-start(bf16[640,512]{1,0:T(8,128)(2,1)S(1)} %collective-permute-done.6.refs_6_), channel_id=1, source_target_pairs={{0,2},{2,0},{1,3},{3,1},{4,6},{6,4},{5,7},{7,5},{8,10},{10,8},{9,1... | collective-permute-start | bytes 1966088 | tf_op jit(solution)/shard_map/ppermute | solution.py:116
  71.4 6.0 %collective-permute-done.11.refs_13_ = bf16[336,512]{1,0:T(8,128)(2,1)S(1)} collective-permute-done((bf16[336,512]{1,0:T(8,128)(2,1)S(1)}, bf16[336,512]{1,0:T(8,128)(2,1)S(1)}, u32[]{:S(2)}, u32[]{:S(2)}) %collective-permute-start.11) | collective-permute-done | bytes 344096 | tf_op jit(solution)/shard_map/ppermute | solution.py:116
  77.4 1.5 %collective-permute-start.13 = (bf16[336,512]{1,0:T(8,128)(2,1)S(1)}, bf16[336,512]{1,0:T(8,128)(2,1)S(1)}, u32[]{:S(2)}, u32[]{:S(2)}) collective-permute-start(bf16[336,512]{1,0:T(8,128)(2,1)S(1)} %collective-permute-done.11.refs_13_), channel_id=1, source_target_pairs={{0,16},{16,0},{1,17},{17,1},{2,18},{18,2},{3,19},{19,3},{4,20},{20... | collective-permute-start | bytes 1032200 | tf_op jit(solution)/shard_map/ppermute | solution.py:116
  78.9 2.6 %collective-permute-start.14 = (bf16[256,512]{1,0:T(8,128)(2,1)S(1)}, bf16[256,512]{1,0:T(8,128)(2,1)S(1)}, u32[]{:S(2)}, u32[]{:S(2)}) collective-permute-start(bf16[256,512]{1,0:T(8,128)(2,1)S(1)} %get-tuple-element.59), channel_id=1, source_target_pairs={{0,8},{4,12},{8,0},{12,4},{1,9},{5,13},{9,1},{13,5},{2,10},{6,14},... | collective-permute-start | bytes 786440 | tf_op jit(solution)/shard_map/ppermute | solution.py:116
  81.5 1.3 %collective-permute-start.15 = (bf16[256,512]{1,0:T(8,128)(2,1)S(1)}, bf16[256,512]{1,0:T(8,128)(2,1)S(1)}, u32[]{:S(2)}, u32[]{:S(2)}) collective-permute-start(bf16[256,512]{1,0:T(8,128)(2,1)S(1)} %get-tuple-element.59), channel_id=1, source_target_pairs={{0,4},{4,0},{8,12},{12,8},{1,5},{5,1},{9,13},{13,9},{2,6},{6,2},{1... | collective-permute-start | bytes 786440 | tf_op jit(solution)/shard_map/ppermute | solution.py:116
  82.8 1.7 %collective-permute-done.10.refs_7_ = bf16[640,512]{1,0:T(8,128)(2,1)S(1)} collective-permute-done((bf16[640,512]{1,0:T(8,128)(2,1)S(1)}, bf16[640,512]{1,0:T(8,128)(2,1)S(1)}, u32[]{:S(2)}, u32[]{:S(2)}) %collective-permute-start.10) | collective-permute-done | bytes 655392 | tf_op jit(solution)/shard_map/ppermute | solution.py:116
  84.5 1.6 %collective-permute-done.13.refs_14_ = bf16[336,512]{1,0:T(8,128)(2,1)S(1)} collective-permute-done((bf16[336,512]{1,0:T(8,128)(2,1)S(1)}, bf16[336,512]{1,0:T(8,128)(2,1)S(1)}, u32[]{:S(2)}, u32[]{:S(2)}) %collective-permute-start.13) | collective-permute-done | bytes 344096 | tf_op jit(solution)/shard_map/ppermute | solution.py:116
  86.0 3.9 %shard_map.89 = (bf16[4,16,256]{2,1,0:T(8,128)(2,1)S(1)}, f32[1280,256]{1,0:T(8,128)}, f32[1280,256]{1,0:T(8,128)S(1)}) custom-call(bf16[640,512]{1,0:T(8,128)(2,1)S(1)} %copy-done.4, bf16[640,512]{1,0:T(8,128)(2,1)S(1)} %collective-permute-done.2.refs_1_, bf16[640,512]{1,0:T(8,128)(2,1)S(1)} %collective-permute-done.3.refs_2_, ...), custom_call_target="tpu_custom_call" | custom-call | tf_op jit(solution)/shard_map/pallas_call | solution.py:130
  90.0 1.2 collective-permute-done.14.refs_7_
  91.6 0.5 collective-permute-start.16
  92.1 1.2 collective-permute-start.21
  93.3 1.1 collective-permute-done.17.refs_3_
  94.4 2.2 %shard_map.90 = (bf16[256,128]{1,0:T(8,128)(2,1)S(1)}, bf16[256,128]{1,0:T(8,128)(2,1)S(1)}, bf16[256,128]{1,0:T(8,128)(2,1)S(1)}, bf16[256,128]{1,0:T(8,128)(2,1)S(1)}) custom-call(f32[1,768]{1,0:T(1,128)S(1)} %fusion.5.refs_0_, bf16[4,16,256]{2,1,0:T(8,128)(2,1)S(1)} %get-tuple-element.62.refs_1_, f32[1280,256]{1,0:T(8,128)S(1)} %get-tuple-element.63.refs_2_, ...), custom_call_target="tpu_custom_call" | custom-call | tf_op jit(solution)/shard_map/pallas_call | solution.py:130
  97.0 2.6 %collective-permute-start.19 = (bf16[256,128]{1,0:T(8,128)(2,1)S(1)}, bf16[256,128]{1,0:T(8,128)(2,1)S(1)}, u32[]{:S(2)}, u32[]{:S(2)}) collective-permute-start(bf16[256,128]{1,0:T(8,128)(2,1)S(1)} %get-tuple-element.68), channel_id=1, source_target_pairs={{0,8},{4,12},{8,0},{12,4},{1,9},{5,13},{9,1},{13,5},{2,10},{6,14},... | collective-permute-start | bytes 196616 | tf_op jit(solution)/shard_map/ppermute | solution.py:116
  99.6 1.4 %collective-permute-start.20 = (bf16[256,128]{1,0:T(8,128)(2,1)S(1)}, bf16[256,128]{1,0:T(8,128)(2,1)S(1)}, u32[]{:S(2)}, u32[]{:S(2)}) collective-permute-start(bf16[256,128]{1,0:T(8,128)(2,1)S(1)} %get-tuple-element.69), channel_id=1, source_target_pairs={{0,12},{4,8},{8,4},{12,0},{1,13},{5,9},{9,5},{13,1},{2,14},{6,10},... | collective-permute-start | bytes 196616 | tf_op jit(solution)/shard_map/ppermute | solution.py:116
  101.0 0.5 collective-permute-start.22
  101.5 0.9 collective-permute-done.21.refs_9_
  102.4 1.0 collective-permute-done.18.refs_1_
  103.4 1.5 %collective-permute-done.19.refs_2_ = bf16[256,128]{1,0:T(8,128)(2,1)S(1)} collective-permute-done((bf16[256,128]{1,0:T(8,128)(2,1)S(1)}, bf16[256,128]{1,0:T(8,128)(2,1)S(1)}, u32[]{:S(2)}, u32[]{:S(2)}) %collective-permute-start.19) | collective-permute-done | bytes 65568 | tf_op jit(solution)/shard_map/ppermute | solution.py:116
  104.9 1.5 %collective-permute-done.20.refs_3_ = bf16[256,128]{1,0:T(8,128)(2,1)S(1)} collective-permute-done((bf16[256,128]{1,0:T(8,128)(2,1)S(1)}, bf16[256,128]{1,0:T(8,128)(2,1)S(1)}, u32[]{:S(2)}, u32[]{:S(2)}) %collective-permute-start.20) | collective-permute-done | bytes 65568 | tf_op jit(solution)/shard_map/ppermute | solution.py:116
  106.5 0.9 shard_map.91
  107.4 1.2 collective-permute-done.22.refs_2_
  108.5 1.8 %collective-permute-done.23.refs_3_ = bf16[256,512]{1,0:T(8,128)(2,1)S(1)} collective-permute-done((bf16[256,512]{1,0:T(8,128)(2,1)S(1)}, bf16[256,512]{1,0:T(8,128)(2,1)S(1)}, u32[]{:S(2)}, u32[]{:S(2)}) %collective-permute-start.23) | collective-permute-done | bytes 262176 | tf_op jit(solution)/shard_map/ppermute | solution.py:116
  110.4 0.7 shard_map.92
  111.1 1.9 %collective-permute-done.24 = bf16[2,256,512]{2,1,0:T(8,128)(2,1)S(1)} collective-permute-done((bf16[2,256,512]{2,1,0:T(8,128)(2,1)S(1)}, bf16[2,256,512]{2,1,0:T(8,128)(2,1)S(1)}, u32[]{:S(2)}, u32[]{:S(2)}) %collective-permute-start.24) | collective-permute-done | bytes 524320 | tf_op jit(solution)/shard_map/ppermute | solution.py:116
  113.1 1.5 %collective-permute-start.25 = (bf16[256,512]{1,0:T(8,128)(2,1)S(1)}, bf16[256,512]{1,0:T(8,128)(2,1)S(1)}, u32[]{:S(2)}, u32[]{:S(2)}) collective-permute-start(bf16[256,512]{1,0:T(8,128)(2,1)S(1)} %fusion.1), channel_id=1, source_target_pairs={{0,2},{2,0},{1,3},{3,1},{4,6},{6,4},{5,7},{7,5},{8,10},{10,8},{9,1... | collective-permute-start | bytes 786440 | tf_op jit(solution)/shard_map/ppermute | solution.py:116
  114.6 1.8 %shard_map.86 = bf16[192,2048]{1,0:T(8,128)(2,1)} custom-call(s32[8]{0:T(128)S(1)} %copy-done.8, bf16[3,192,2048]{2,1,0:T(8,128)(2,1)S(1)} %copy-done), custom_call_target="tpu_custom_call" | custom-call | tf_op jit(solution)/shard_map/pallas_call | solution.py:169
  116.5 5.0 %collective-permute-done.25 = bf16[256,512]{1,0:T(8,128)(2,1)S(1)} collective-permute-done((bf16[256,512]{1,0:T(8,128)(2,1)S(1)}, bf16[256,512]{1,0:T(8,128)(2,1)S(1)}, u32[]{:S(2)}, u32[]{:S(2)}) %collective-permute-start.25) | collective-permute-done | bytes 262176 | tf_op jit(solution)/shard_map/ppermute | solution.py:116
  121.5 0.8 fusion
  (38 shorter events, 1.7 us)
Async XLA Ops:
  0.6 9.0 %copy-start.2 = (bf16[512,512]{1,0:T(8,128)(2,1)S(1)}, bf16[512,512]{1,0:T(8,128)(2,1)}, u32[]{:S(2)}) copy-start(bf16[512,512]{1,0:T(8,128)(2,1)} %refs_2_.3) | copy-start | bytes 1572868
  0.6 9.0 %copy-start.7 = (s32[256]{0:T(256)S(1)}, s32[256]{0:T(256)}, u32[]{:S(2)}) copy-start(s32[256]{0:T(256)} %param.9) | copy-start | bytes 3076
  0.7 9.0 %copy-start.1 = (bf16[1024,1024]{1,0:T(8,128)(2,1)S(1)}, bf16[1024,1024]{1,0:T(8,128)(2,1)}, u32[]{:S(2)}) copy-start(bf16[1024,1024]{1,0:T(8,128)(2,1)} %refs_1_.3) | copy-start | bytes 6291460
  3.8 5.8 %collective-permute-start = (bf16[640,1024]{1,0:T(8,128)(2,1)}, bf16[640,1024]{1,0:T(8,128)(2,1)S(1)}, u32[]{:S(2)}, u32[]{:S(2)}) collective-permute-start(bf16[640,1024]{1,0:T(8,128)(2,1)} %get-tuple-element.40), channel_id=1, source_target_pairs={{0,1},{1,0},{2,3},{3,2},{4,5},{5,4},{6,7},{7,6},{8,9},{9,8},{10,11... | collective-permute-start | bytes 3932168 | tf_op jit(solution)/shard_map/ppermute | solution.py:116
  4.4 32.4 %collective-permute-start.3 = (bf16[640,512]{1,0:T(8,128)(2,1)}, bf16[640,512]{1,0:T(8,128)(2,1)S(1)}, u32[]{:S(2)}, u32[]{:S(2)}) collective-permute-start(bf16[640,512]{1,0:T(8,128)(2,1)} %get-tuple-element.39.refs_0_), channel_id=1, source_target_pairs={{0,4},{4,0},{8,12},{12,8},{1,5},{5,1},{9,13},{13,9},{2,6},{6,2},{1... | collective-permute-start | bytes 1966088 | tf_op jit(solution)/shard_map/ppermute | solution.py:116
  7.0 31.8 %collective-permute-start.5 = (bf16[640,512]{1,0:T(8,128)(2,1)}, bf16[640,512]{1,0:T(8,128)(2,1)S(1)}, u32[]{:S(2)}, u32[]{:S(2)}) collective-permute-start(bf16[640,512]{1,0:T(8,128)(2,1)} %get-tuple-element.39.refs_0_), channel_id=1, source_target_pairs={{0,8},{4,12},{8,0},{12,4},{1,9},{5,13},{9,1},{13,5},{2,10},{6,14},... | collective-permute-start | bytes 1966088 | tf_op jit(solution)/shard_map/ppermute | solution.py:116
  9.6 1.0 copy-start.5
  10.7 1.1 copy-start.4
  10.9 33.0 %collective-permute-start.1 = (bf16[336,512]{1,0:T(8,128)(2,1)S(1)}, bf16[336,512]{1,0:T(8,128)(2,1)S(1)}, u32[]{:S(2)}, u32[]{:S(2)}) collective-permute-start(bf16[336,512]{1,0:T(8,128)(2,1)S(1)} %get-tuple-element.41), channel_id=1, source_target_pairs={{0,4},{4,0},{8,12},{12,8},{1,5},{5,1},{9,13},{13,9},{2,6},{6,2},{1... | collective-permute-start | bytes 1032200 | tf_op jit(solution)/shard_map/ppermute | solution.py:116
  11.8 36.6 %collective-permute-start.2 = (bf16[640,512]{1,0:T(8,128)(2,1)S(1)}, bf16[640,512]{1,0:T(8,128)(2,1)S(1)}, u32[]{:S(2)}, u32[]{:S(2)}) collective-permute-start(bf16[640,512]{1,0:T(8,128)(2,1)S(1)} %copy-done.4), channel_id=1, source_target_pairs={{0,2},{2,0},{1,3},{3,1},{4,6},{6,4},{5,7},{7,5},{8,10},{10,8},{9,1... | collective-permute-start | bytes 1966088 | tf_op jit(solution)/shard_map/ppermute | solution.py:116
  36.7 17.7 %collective-permute-start.4 = (bf16[640,512]{1,0:T(8,128)(2,1)S(1)}, bf16[640,512]{1,0:T(8,128)(2,1)S(1)}, u32[]{:S(2)}, u32[]{:S(2)}) collective-permute-start(bf16[640,512]{1,0:T(8,128)(2,1)S(1)} %collective-permute-done.3.refs_2_), channel_id=1, source_target_pairs={{0,2},{2,0},{1,3},{3,1},{4,6},{6,4},{5,7},{7,5},{8,10},{10,8},{9,1... | collective-permute-start | bytes 1966088 | tf_op jit(solution)/shard_map/ppermute | solution.py:116
  38.8 28.2 %collective-permute-start.7 = (bf16[640,512]{1,0:T(8,128)(2,1)S(1)}, bf16[640,512]{1,0:T(8,128)(2,1)S(1)}, u32[]{:S(2)}, u32[]{:S(2)}) collective-permute-start(bf16[640,512]{1,0:T(8,128)(2,1)S(1)} %collective-permute-done.5.refs_4_), channel_id=1, source_target_pairs={{0,2},{2,0},{1,3},{3,1},{4,6},{6,4},{5,7},{7,5},{8,10},{10,8},{9,1... | collective-permute-start | bytes 1966088 | tf_op jit(solution)/shard_map/ppermute | solution.py:116
  44.0 24.4 %collective-permute-start.6 = (bf16[640,512]{1,0:T(8,128)(2,1)S(1)}, bf16[640,512]{1,0:T(8,128)(2,1)S(1)}, u32[]{:S(2)}, u32[]{:S(2)}) collective-permute-start(bf16[640,512]{1,0:T(8,128)(2,1)S(1)} %collective-permute-done.5.refs_4_), channel_id=1, source_target_pairs={{0,4},{4,0},{8,12},{12,8},{1,5},{5,1},{9,13},{13,9},{2,6},{6,2},{1... | collective-permute-start | bytes 1966088 | tf_op jit(solution)/shard_map/ppermute | solution.py:116
  45.8 22.6 %collective-permute-start.9 = (bf16[336,512]{1,0:T(8,128)(2,1)S(1)}, bf16[336,512]{1,0:T(8,128)(2,1)S(1)}, u32[]{:S(2)}, u32[]{:S(2)}) collective-permute-start(bf16[336,512]{1,0:T(8,128)(2,1)S(1)} %get-tuple-element.46), channel_id=1, source_target_pairs={{0,8},{4,12},{8,0},{12,4},{1,9},{5,13},{9,1},{13,5},{2,10},{6,14},... | collective-permute-start | bytes 1032200 | tf_op jit(solution)/shard_map/ppermute | solution.py:116
  54.4 14.0 %collective-permute-start.8 = (bf16[336,512]{1,0:T(8,128)(2,1)S(1)}, bf16[336,512]{1,0:T(8,128)(2,1)S(1)}, u32[]{:S(2)}, u32[]{:S(2)}) collective-permute-start(bf16[336,512]{1,0:T(8,128)(2,1)S(1)} %collective-permute-done.1.refs_9_), channel_id=1, source_target_pairs={{0,16},{16,0},{1,17},{17,1},{2,18},{18,2},{3,19},{19,3},{4,20},{20... | collective-permute-start | bytes 1032200 | tf_op jit(solution)/shard_map/ppermute | solution.py:116
  56.3 21.1 %collective-permute-start.11 = (bf16[336,512]{1,0:T(8,128)(2,1)S(1)}, bf16[336,512]{1,0:T(8,128)(2,1)S(1)}, u32[]{:S(2)}, u32[]{:S(2)}) collective-permute-start(bf16[336,512]{1,0:T(8,128)(2,1)S(1)} %get-tuple-element.54), channel_id=1, source_target_pairs={{0,12},{4,8},{8,4},{12,0},{1,13},{5,9},{9,5},{13,1},{2,14},{6,10},... | collective-permute-start | bytes 1032200 | tf_op jit(solution)/shard_map/ppermute | solution.py:116
  68.4 9.0 %collective-permute-start.12 = (bf16[336,512]{1,0:T(8,128)(2,1)S(1)}, bf16[336,512]{1,0:T(8,128)(2,1)S(1)}, u32[]{:S(2)}, u32[]{:S(2)}) collective-permute-start(bf16[336,512]{1,0:T(8,128)(2,1)S(1)} %collective-permute-done.9.refs_11_), channel_id=1, source_target_pairs={{0,16},{16,0},{1,17},{17,1},{2,18},{18,2},{3,19},{19,3},{4,20},{20... | collective-permute-start | bytes 1032200 | tf_op jit(solution)/shard_map/ppermute | solution.py:116
  69.9 14.6 %collective-permute-start.10 = (bf16[640,512]{1,0:T(8,128)(2,1)S(1)}, bf16[640,512]{1,0:T(8,128)(2,1)S(1)}, u32[]{:S(2)}, u32[]{:S(2)}) collective-permute-start(bf16[640,512]{1,0:T(8,128)(2,1)S(1)} %collective-permute-done.6.refs_6_), channel_id=1, source_target_pairs={{0,2},{2,0},{1,3},{3,1},{4,6},{6,4},{5,7},{7,5},{8,10},{10,8},{9,1... | collective-permute-start | bytes 1966088 | tf_op jit(solution)/shard_map/ppermute | solution.py:116
  77.4 8.7 %collective-permute-start.13 = (bf16[336,512]{1,0:T(8,128)(2,1)S(1)}, bf16[336,512]{1,0:T(8,128)(2,1)S(1)}, u32[]{:S(2)}, u32[]{:S(2)}) collective-permute-start(bf16[336,512]{1,0:T(8,128)(2,1)S(1)} %collective-permute-done.11.refs_13_), channel_id=1, source_target_pairs={{0,16},{16,0},{1,17},{17,1},{2,18},{18,2},{3,19},{19,3},{4,20},{20... | collective-permute-start | bytes 1032200 | tf_op jit(solution)/shard_map/ppermute | solution.py:116
  78.9 12.3 %collective-permute-start.14 = (bf16[256,512]{1,0:T(8,128)(2,1)S(1)}, bf16[256,512]{1,0:T(8,128)(2,1)S(1)}, u32[]{:S(2)}, u32[]{:S(2)}) collective-permute-start(bf16[256,512]{1,0:T(8,128)(2,1)S(1)} %get-tuple-element.59), channel_id=1, source_target_pairs={{0,8},{4,12},{8,0},{12,4},{1,9},{5,13},{9,1},{13,5},{2,10},{6,14},... | collective-permute-start | bytes 786440 | tf_op jit(solution)/shard_map/ppermute | solution.py:116
  81.5 9.6 %collective-permute-start.15 = (bf16[256,512]{1,0:T(8,128)(2,1)S(1)}, bf16[256,512]{1,0:T(8,128)(2,1)S(1)}, u32[]{:S(2)}, u32[]{:S(2)}) collective-permute-start(bf16[256,512]{1,0:T(8,128)(2,1)S(1)} %get-tuple-element.59), channel_id=1, source_target_pairs={{0,4},{4,0},{8,12},{12,8},{1,5},{5,1},{9,13},{13,9},{2,6},{6,2},{1... | collective-permute-start | bytes 786440 | tf_op jit(solution)/shard_map/ppermute | solution.py:116
  91.2 3.2 %collective-permute-start.17 = (f32[1280,256]{1,0:T(8,128)}, f32[1280,256]{1,0:T(8,128)S(1)}, u32[]{:S(2)}, u32[]{:S(2)}) collective-permute-start(f32[1280,256]{1,0:T(8,128)} %get-tuple-element.64), channel_id=1, source_target_pairs={{0,1},{1,0},{2,3},{3,2},{4,5},{5,4},{6,7},{7,6},{8,9},{9,8},{10,11... | collective-permute-start | bytes 3932168 | tf_op jit(solution)/shard_map/ppermute | solution.py:116
  91.6 9.4 %collective-permute-start.16 = (bf16[256,512]{1,0:T(8,128)(2,1)S(1)}, bf16[256,512]{1,0:T(8,128)(2,1)S(1)}, u32[]{:S(2)}, u32[]{:S(2)}) collective-permute-start(bf16[256,512]{1,0:T(8,128)(2,1)S(1)} %collective-permute-done.14.refs_7_), channel_id=1, source_target_pairs={{0,16},{16,0},{1,17},{17,1},{2,18},{18,2},{3,19},{19,3},{4,20},{20... | collective-permute-start | bytes 786440 | tf_op jit(solution)/shard_map/ppermute | solution.py:116
  92.1 10.3 %collective-permute-start.21 = (bf16[256,512]{1,0:T(8,128)(2,1)S(1)}, bf16[256,512]{1,0:T(8,128)(2,1)S(1)}, u32[]{:S(2)}, u32[]{:S(2)}) collective-permute-start(bf16[256,512]{1,0:T(8,128)(2,1)S(1)} %collective-permute-done.14.refs_7_), channel_id=1, source_target_pairs={{0,4},{4,0},{8,12},{12,8},{1,5},{5,1},{9,13},{13,9},{2,6},{6,2},{1... | collective-permute-start | bytes 786440 | tf_op jit(solution)/shard_map/ppermute | solution.py:116
  94.4 12.0 %copy-start.3 = (bf16[256,2048]{1,0:T(8,128)(2,1)S(1)}, bf16[256,2048]{1,0:T(8,128)(2,1)}, u32[]{:S(2)}) copy-start(bf16[256,2048]{1,0:T(8,128)(2,1)} %refs_4_.5) | copy-start | bytes 3145732
  94.4 12.0 %copy-start.6 = (bf16[512,512]{1,0:T(8,128)(2,1)S(1)}, bf16[512,512]{1,0:T(8,128)(2,1)}, u32[]{:S(2)}) copy-start(bf16[512,512]{1,0:T(8,128)(2,1)} %refs_5_.1) | copy-start | bytes 1572868
  96.6 6.8 %collective-permute-start.18 = (bf16[256,128]{1,0:T(8,128)(2,1)S(1)}, bf16[256,128]{1,0:T(8,128)(2,1)S(1)}, u32[]{:S(2)}, u32[]{:S(2)}) collective-permute-start(bf16[256,128]{1,0:T(8,128)(2,1)S(1)} %get-tuple-element.67), channel_id=1, source_target_pairs={{0,4},{4,0},{8,12},{12,8},{1,5},{5,1},{9,13},{13,9},{2,6},{6,2},{1... | collective-permute-start | bytes 196616 | tf_op jit(solution)/shard_map/ppermute | solution.py:116
  97.0 7.9 %collective-permute-start.19 = (bf16[256,128]{1,0:T(8,128)(2,1)S(1)}, bf16[256,128]{1,0:T(8,128)(2,1)S(1)}, u32[]{:S(2)}, u32[]{:S(2)}) collective-permute-start(bf16[256,128]{1,0:T(8,128)(2,1)S(1)} %get-tuple-element.68), channel_id=1, source_target_pairs={{0,8},{4,12},{8,0},{12,4},{1,9},{5,13},{9,1},{13,5},{2,10},{6,14},... | collective-permute-start | bytes 196616 | tf_op jit(solution)/shard_map/ppermute | solution.py:116
  99.6 6.8 %collective-permute-start.20 = (bf16[256,128]{1,0:T(8,128)(2,1)S(1)}, bf16[256,128]{1,0:T(8,128)(2,1)S(1)}, u32[]{:S(2)}, u32[]{:S(2)}) collective-permute-start(bf16[256,128]{1,0:T(8,128)(2,1)S(1)} %get-tuple-element.69), channel_id=1, source_target_pairs={{0,12},{4,8},{8,4},{12,0},{1,13},{5,9},{9,5},{13,1},{2,14},{6,10},... | collective-permute-start | bytes 196616 | tf_op jit(solution)/shard_map/ppermute | solution.py:116
  101.0 7.5 %collective-permute-start.22 = (bf16[256,512]{1,0:T(8,128)(2,1)S(1)}, bf16[256,512]{1,0:T(8,128)(2,1)S(1)}, u32[]{:S(2)}, u32[]{:S(2)}) collective-permute-start(bf16[256,512]{1,0:T(8,128)(2,1)S(1)} %collective-permute-done.15.refs_6_), channel_id=1, source_target_pairs={{0,16},{16,0},{1,17},{17,1},{2,18},{18,2},{3,19},{19,3},{4,20},{20... | collective-permute-start | bytes 786440 | tf_op jit(solution)/shard_map/ppermute | solution.py:116
  102.4 8.0 %collective-permute-start.23 = (bf16[256,512]{1,0:T(8,128)(2,1)S(1)}, bf16[256,512]{1,0:T(8,128)(2,1)S(1)}, u32[]{:S(2)}, u32[]{:S(2)}) collective-permute-start(bf16[256,512]{1,0:T(8,128)(2,1)S(1)} %collective-permute-done.16.refs_8_), channel_id=1, source_target_pairs={{0,4},{4,0},{8,12},{12,8},{1,5},{5,1},{9,13},{13,9},{2,6},{6,2},{1... | collective-permute-start | bytes 786440 | tf_op jit(solution)/shard_map/ppermute | solution.py:116
  110.4 4.3 %copy-start = (bf16[3,192,2048]{2,1,0:T(8,128)(2,1)S(1)}, bf16[3,192,2048]{2,1,0:T(8,128)(2,1)}, u32[]{:S(2)}) copy-start(bf16[3,192,2048]{2,1,0:T(8,128)(2,1)} %refs_1_.2) | copy-start | bytes 7077892
  110.4 4.3 %copy-start.8 = (s32[8]{0:T(128)S(1)}, s32[8]{0:T(128)}, u32[]{:S(2)}) copy-start(s32[8]{0:T(128)} %refs_0_.1) | copy-start | bytes 100
  111.0 2.0 %collective-permute-start.24 = (bf16[2,256,512]{2,1,0:T(8,128)(2,1)S(1)}, bf16[2,256,512]{2,1,0:T(8,128)(2,1)S(1)}, u32[]{:S(2)}, u32[]{:S(2)}) collective-permute-start(bf16[2,256,512]{2,1,0:T(8,128)(2,1)S(1)} %get-tuple-element.75), channel_id=1, source_target_pairs={{0,1},{1,0},{2,3},{3,2},{4,5},{5,4},{6,7},{7,6},{8,9},{9,8},{10,11... | collective-permute-start | bytes 1572872 | tf_op jit(solution)/shard_map/ppermute | solution.py:116
  113.1 8.4 %collective-permute-start.25 = (bf16[256,512]{1,0:T(8,128)(2,1)S(1)}, bf16[256,512]{1,0:T(8,128)(2,1)S(1)}, u32[]{:S(2)}, u32[]{:S(2)}) collective-permute-start(bf16[256,512]{1,0:T(8,128)(2,1)S(1)} %fusion.1), channel_id=1, source_target_pairs={{0,2},{2,0},{1,3},{3,1},{4,6},{6,4},{5,7},{7,5},{8,10},{10,8},{9,1... | collective-permute-start | bytes 786440 | tf_op jit(solution)/shard_map/ppermute | solution.py:116

commit v22 on v20

--- a/solution.py
+++ b/solution.py
@@ -541,10 +541,11 @@
         ],
         limit=9,
     )
-    third_rest, out_partner, own_piece = lax.optimization_barrier(
-        (third_rest, out_partner, own_piece)
-    )
-    fourth_rest, partner_rest = swap(third_rest, "seq", 1), swap(out_partner, "grp", 1)
+    partner_rest = swap(out_partner, "grp", 1)
+    third_rest, partner_rest, own_piece = lax.optimization_barrier(
+        (third_rest, partner_rest, own_piece)
+    )
+    fourth_rest = swap(third_rest, "seq", 1)
     far_piece = swap(far_piece, "seq", 2)
     farther_piece = swap(farther_piece, "seq", 3)
     near_piece = swap(near_piece, "seq", 1)

time: 123 us -> 126 us (1.024)
  starting transfers between devices: 36.7 us -> 38.3 us
    ppermute x26, starting transfers between devices: 36.7 us -> 38.3 us  [swap(): return lax.ppermute(value, axis, [(i, i ^ bit) for i in range(size)])]
  transfers between devices with their start and end apart: 26 -> 26, of which waited for: 19 -> 17; matrix products, arithmetic and copies ran while one was open for 0% -> 0% of each run, Pallas kernels for 7% -> 8%
where the time goes in v22:
time: 126 us
  waiting for transfers between devices  70.2 us (56%)
  starting transfers between devices  38.3 us (30%)
  Pallas kernels  13.9 us (11%)
  local copies, waits for them, and re-layouts  1.42 us (1%)
    ppermute x26, waiting for transfers between devices, swap(): return lax.ppermute(value, axis, [(i, i ^ bit) for i in range(size)])  70.2 us
    ppermute x26, starting transfers between devices, swap(): return lax.ppermute(value, axis, [(i, i ^ bit) for i in range(size)])  38.3 us
    pallas_call x6, Pallas kernels, kernel_call(): pl.pallas_call(whole, out_shape=outs, in_specs=spots + [ANY] * len(after)...  12.1 us
  transfers between devices with their start and end apart: 26, of which 17 were waited for; matrix products, arithmetic and copies ran while one was open for 0% of the time, Pallas kernels for 8%

profile of v22, /device:TPU:0, one launch (start us, length us, event | category | flops | bytes accessed | tf_op | source)
XLA Modules:
  0.0 125.7 jit_solution(5839554262861000720)
XLA Ops:
  0.7 3.2 %shard_map.87 = (bf16[640,512]{1,0:T(8,128)(2,1)}, bf16[640,1024]{1,0:T(8,128)(2,1)}) custom-call(s32[8]{0:T(128)} %refs_0_.1, bf16[3,192,2048]{2,1,0:T(8,128)(2,1)} %refs_1_.2, bf16[256,2048]{1,0:T(8,128)(2,1)} %refs_4_.5, bf16[1024,1024]{1,0:T(8,128)(2,1)} %refs_1_.3, bf16[512,512]{1,0:T(8,128)(2,1)} %refs_2_.3), custom_call_target="tpu_custom_call" | custom-call | tf_op jit(solution)/shard_map/pallas_call | solution.py:130
  3.8 0.5 collective-permute-start
  4.4 2.6 %collective-permute-start.3 = (bf16[640,512]{1,0:T(8,128)(2,1)}, bf16[640,512]{1,0:T(8,128)(2,1)S(1)}, u32[]{:S(2)}, u32[]{:S(2)}) collective-permute-start(bf16[640,512]{1,0:T(8,128)(2,1)} %get-tuple-element.39.refs_0_), channel_id=1, source_target_pairs={{0,4},{4,0},{8,12},{12,8},{1,5},{5,1},{9,13},{13,9},{2,6},{6,2},{1... | collective-permute-start | bytes 1966088 | tf_op jit(solution)/shard_map/ppermute | solution.py:116
  7.0 2.6 %collective-permute-start.5 = (bf16[640,512]{1,0:T(8,128)(2,1)}, bf16[640,512]{1,0:T(8,128)(2,1)S(1)}, u32[]{:S(2)}, u32[]{:S(2)}) collective-permute-start(bf16[640,512]{1,0:T(8,128)(2,1)} %get-tuple-element.39.refs_0_), channel_id=1, source_target_pairs={{0,8},{4,12},{8,0},{12,4},{1,9},{5,13},{9,1},{13,5},{2,10},{6,14},... | collective-permute-start | bytes 1966088 | tf_op jit(solution)/shard_map/ppermute | solution.py:116
  9.6 1.0 copy-done.5
  10.9 0.6 collective-permute-start.1
  11.8 1.5 %collective-permute-start.2 = (bf16[640,512]{1,0:T(8,128)(2,1)S(1)}, bf16[640,512]{1,0:T(8,128)(2,1)S(1)}, u32[]{:S(2)}, u32[]{:S(2)}) collective-permute-start(bf16[640,512]{1,0:T(8,128)(2,1)S(1)} %copy-done.4), channel_id=1, source_target_pairs={{0,2},{2,0},{1,3},{3,1},{4,6},{6,4},{5,7},{7,5},{8,10},{10,8},{9,1... | collective-permute-start | bytes 1966088 | tf_op jit(solution)/shard_map/ppermute | solution.py:116
  13.2 23.5 %collective-permute-done.3.refs_2_ = bf16[640,512]{1,0:T(8,128)(2,1)S(1)} collective-permute-done((bf16[640,512]{1,0:T(8,128)(2,1)}, bf16[640,512]{1,0:T(8,128)(2,1)S(1)}, u32[]{:S(2)}, u32[]{:S(2)}) %collective-permute-start.3) | collective-permute-done | bytes 655392 | tf_op jit(solution)/shard_map/ppermute | solution.py:116
  36.7 1.9 %collective-permute-start.4 = (bf16[640,512]{1,0:T(8,128)(2,1)S(1)}, bf16[640,512]{1,0:T(8,128)(2,1)S(1)}, u32[]{:S(2)}, u32[]{:S(2)}) collective-permute-start(bf16[640,512]{1,0:T(8,128)(2,1)S(1)} %collective-permute-done.3.refs_2_), channel_id=1, source_target_pairs={{0,2},{2,0},{1,3},{3,1},{4,6},{6,4},{5,7},{7,5},{8,10},{10,8},{9,1... | collective-permute-start | bytes 1966088 | tf_op jit(solution)/shard_map/ppermute | solution.py:116
  38.8 1.5 %collective-permute-start.7 = (bf16[640,512]{1,0:T(8,128)(2,1)S(1)}, bf16[640,512]{1,0:T(8,128)(2,1)S(1)}, u32[]{:S(2)}, u32[]{:S(2)}) collective-permute-start(bf16[640,512]{1,0:T(8,128)(2,1)S(1)} %collective-permute-done.5.refs_4_), channel_id=1, source_target_pairs={{0,2},{2,0},{1,3},{3,1},{4,6},{6,4},{5,7},{7,5},{8,10},{10,8},{9,1... | collective-permute-start | bytes 1966088 | tf_op jit(solution)/shard_map/ppermute | solution.py:116
  40.3 3.7 %collective-permute-done.1.refs_9_ = bf16[336,512]{1,0:T(8,128)(2,1)S(1)} collective-permute-done((bf16[336,512]{1,0:T(8,128)(2,1)S(1)}, bf16[336,512]{1,0:T(8,128)(2,1)S(1)}, u32[]{:S(2)}, u32[]{:S(2)}) %collective-permute-start.1) | collective-permute-done | bytes 344096 | tf_op jit(solution)/shard_map/ppermute | solution.py:116
  44.0 1.8 %collective-permute-start.6 = (bf16[640,512]{1,0:T(8,128)(2,1)S(1)}, bf16[640,512]{1,0:T(8,128)(2,1)S(1)}, u32[]{:S(2)}, u32[]{:S(2)}) collective-permute-start(bf16[640,512]{1,0:T(8,128)(2,1)S(1)} %collective-permute-done.5.refs_4_), channel_id=1, source_target_pairs={{0,4},{4,0},{8,12},{12,8},{1,5},{5,1},{9,13},{13,9},{2,6},{6,2},{1... | collective-permute-start | bytes 1966088 | tf_op jit(solution)/shard_map/ppermute | solution.py:116
  45.8 2.5 %collective-permute-start.9 = (bf16[336,512]{1,0:T(8,128)(2,1)S(1)}, bf16[336,512]{1,0:T(8,128)(2,1)S(1)}, u32[]{:S(2)}, u32[]{:S(2)}) collective-permute-start(bf16[336,512]{1,0:T(8,128)(2,1)S(1)} %get-tuple-element.46), channel_id=1, source_target_pairs={{0,8},{4,12},{8,0},{12,4},{1,9},{5,13},{9,1},{13,5},{2,10},{6,14},... | collective-permute-start | bytes 1032200 | tf_op jit(solution)/shard_map/ppermute | solution.py:116
  48.3 6.1 %collective-permute-done.4.refs_3_ = bf16[640,512]{1,0:T(8,128)(2,1)S(1)} collective-permute-done((bf16[640,512]{1,0:T(8,128)(2,1)S(1)}, bf16[640,512]{1,0:T(8,128)(2,1)S(1)}, u32[]{:S(2)}, u32[]{:S(2)}) %collective-permute-start.4) | collective-permute-done | bytes 655392 | tf_op jit(solution)/shard_map/ppermute | solution.py:116
  54.4 1.9 %collective-permute-start.8 = (bf16[336,512]{1,0:T(8,128)(2,1)S(1)}, bf16[336,512]{1,0:T(8,128)(2,1)S(1)}, u32[]{:S(2)}, u32[]{:S(2)}) collective-permute-start(bf16[336,512]{1,0:T(8,128)(2,1)S(1)} %collective-permute-done.1.refs_9_), channel_id=1, source_target_pairs={{0,16},{16,0},{1,17},{17,1},{2,18},{18,2},{3,19},{19,3},{4,20},{20... | collective-permute-start | bytes 1032200 | tf_op jit(solution)/shard_map/ppermute | solution.py:116
  56.3 2.5 %collective-permute-start.11 = (bf16[336,512]{1,0:T(8,128)(2,1)S(1)}, bf16[336,512]{1,0:T(8,128)(2,1)S(1)}, u32[]{:S(2)}, u32[]{:S(2)}) collective-permute-start(bf16[336,512]{1,0:T(8,128)(2,1)S(1)} %get-tuple-element.54), channel_id=1, source_target_pairs={{0,12},{4,8},{8,4},{12,0},{1,13},{5,9},{9,5},{13,1},{2,14},{6,10},... | collective-permute-start | bytes 1032200 | tf_op jit(solution)/shard_map/ppermute | solution.py:116
  58.8 8.2 %collective-permute-done.7.refs_5_ = bf16[640,512]{1,0:T(8,128)(2,1)S(1)} collective-permute-done((bf16[640,512]{1,0:T(8,128)(2,1)S(1)}, bf16[640,512]{1,0:T(8,128)(2,1)S(1)}, u32[]{:S(2)}, u32[]{:S(2)}) %collective-permute-start.7) | collective-permute-done | bytes 655392 | tf_op jit(solution)/shard_map/ppermute | solution.py:116
  67.0 1.4 %collective-permute-done.9.refs_11_ = bf16[336,512]{1,0:T(8,128)(2,1)S(1)} collective-permute-done((bf16[336,512]{1,0:T(8,128)(2,1)S(1)}, bf16[336,512]{1,0:T(8,128)(2,1)S(1)}, u32[]{:S(2)}, u32[]{:S(2)}) %collective-permute-start.9) | collective-permute-done | bytes 344096 | tf_op jit(solution)/shard_map/ppermute | solution.py:116
  68.4 1.5 %collective-permute-start.12 = (bf16[336,512]{1,0:T(8,128)(2,1)S(1)}, bf16[336,512]{1,0:T(8,128)(2,1)S(1)}, u32[]{:S(2)}, u32[]{:S(2)}) collective-permute-start(bf16[336,512]{1,0:T(8,128)(2,1)S(1)} %collective-permute-done.9.refs_11_), channel_id=1, source_target_pairs={{0,16},{16,0},{1,17},{17,1},{2,18},{18,2},{3,19},{19,3},{4,20},{20... | collective-permute-start | bytes 1032200 | tf_op jit(solution)/shard_map/ppermute | solution.py:116
  69.9 1.5 %collective-permute-start.10 = (bf16[640,512]{1,0:T(8,128)(2,1)S(1)}, bf16[640,512]{1,0:T(8,128)(2,1)S(1)}, u32[]{:S(2)}, u32[]{:S(2)}) collective-permute-start(bf16[640,512]{1,0:T(8,128)(2,1)S(1)} %collective-permute-done.6.refs_6_), channel_id=1, source_target_pairs={{0,2},{2,0},{1,3},{3,1},{4,6},{6,4},{5,7},{7,5},{8,10},{10,8},{9,1... | collective-permute-start | bytes 1966088 | tf_op jit(solution)/shard_map/ppermute | solution.py:116
  71.4 6.0 %collective-permute-done.11.refs_13_ = bf16[336,512]{1,0:T(8,128)(2,1)S(1)} collective-permute-done((bf16[336,512]{1,0:T(8,128)(2,1)S(1)}, bf16[336,512]{1,0:T(8,128)(2,1)S(1)}, u32[]{:S(2)}, u32[]{:S(2)}) %collective-permute-start.11) | collective-permute-done | bytes 344096 | tf_op jit(solution)/shard_map/ppermute | solution.py:116
  77.4 1.5 %collective-permute-start.13 = (bf16[336,512]{1,0:T(8,128)(2,1)S(1)}, bf16[336,512]{1,0:T(8,128)(2,1)S(1)}, u32[]{:S(2)}, u32[]{:S(2)}) collective-permute-start(bf16[336,512]{1,0:T(8,128)(2,1)S(1)} %collective-permute-done.11.refs_13_), channel_id=1, source_target_pairs={{0,16},{16,0},{1,17},{17,1},{2,18},{18,2},{3,19},{19,3},{4,20},{20... | collective-permute-start | bytes 1032200 | tf_op jit(solution)/shard_map/ppermute | solution.py:116
  78.9 2.6 %collective-permute-start.14 = (bf16[256,512]{1,0:T(8,128)(2,1)S(1)}, bf16[256,512]{1,0:T(8,128)(2,1)S(1)}, u32[]{:S(2)}, u32[]{:S(2)}) collective-permute-start(bf16[256,512]{1,0:T(8,128)(2,1)S(1)} %get-tuple-element.59), channel_id=1, source_target_pairs={{0,8},{4,12},{8,0},{12,4},{1,9},{5,13},{9,1},{13,5},{2,10},{6,14},... | collective-permute-start | bytes 786440 | tf_op jit(solution)/shard_map/ppermute | solution.py:116
  81.5 1.3 %collective-permute-start.15 = (bf16[256,512]{1,0:T(8,128)(2,1)S(1)}, bf16[256,512]{1,0:T(8,128)(2,1)S(1)}, u32[]{:S(2)}, u32[]{:S(2)}) collective-permute-start(bf16[256,512]{1,0:T(8,128)(2,1)S(1)} %get-tuple-element.59), channel_id=1, source_target_pairs={{0,4},{4,0},{8,12},{12,8},{1,5},{5,1},{9,13},{13,9},{2,6},{6,2},{1... | collective-permute-start | bytes 786440 | tf_op jit(solution)/shard_map/ppermute | solution.py:116
  82.8 1.7 %collective-permute-done.10.refs_7_ = bf16[640,512]{1,0:T(8,128)(2,1)S(1)} collective-permute-done((bf16[640,512]{1,0:T(8,128)(2,1)S(1)}, bf16[640,512]{1,0:T(8,128)(2,1)S(1)}, u32[]{:S(2)}, u32[]{:S(2)}) %collective-permute-start.10) | collective-permute-done | bytes 655392 | tf_op jit(solution)/shard_map/ppermute | solution.py:116
  84.5 1.6 %collective-permute-done.13.refs_14_ = bf16[336,512]{1,0:T(8,128)(2,1)S(1)} collective-permute-done((bf16[336,512]{1,0:T(8,128)(2,1)S(1)}, bf16[336,512]{1,0:T(8,128)(2,1)S(1)}, u32[]{:S(2)}, u32[]{:S(2)}) %collective-permute-start.13) | collective-permute-done | bytes 344096 | tf_op jit(solution)/shard_map/ppermute | solution.py:116
  86.0 3.9 %shard_map.89 = (bf16[4,16,256]{2,1,0:T(8,128)(2,1)S(1)}, f32[1280,256]{1,0:T(8,128)}, f32[1280,256]{1,0:T(8,128)S(1)}) custom-call(bf16[640,512]{1,0:T(8,128)(2,1)S(1)} %copy-done.4, bf16[640,512]{1,0:T(8,128)(2,1)S(1)} %collective-permute-done.2.refs_1_, bf16[640,512]{1,0:T(8,128)(2,1)S(1)} %collective-permute-done.3.refs_2_, ...), custom_call_target="tpu_custom_call" | custom-call | tf_op jit(solution)/shard_map/pallas_call | solution.py:130
  90.0 1.2 collective-permute-done.14.refs_7_
  91.3 0.5 collective-permute-start.16
  92.1 1.2 collective-permute-start.22
  93.2 0.7 collective-permute-start.17
  94.0 0.4 collective-permute-done.18.refs_3_
  94.4 2.2 %shard_map.90 = (bf16[256,128]{1,0:T(8,128)(2,1)S(1)}, bf16[256,128]{1,0:T(8,128)(2,1)S(1)}, bf16[256,128]{1,0:T(8,128)(2,1)S(1)}, bf16[256,128]{1,0:T(8,128)(2,1)S(1)}) custom-call(f32[1,768]{1,0:T(1,128)S(1)} %fusion.4.refs_0_, bf16[4,16,256]{2,1,0:T(8,128)(2,1)S(1)} %get-tuple-element.62.refs_1_, f32[1280,256]{1,0:T(8,128)S(1)} %get-tuple-element.63.refs_2_, ...), custom_call_target="tpu_custom_call" | custom-call | tf_op jit(solution)/shard_map/pallas_call | solution.py:130
  96.6 1.3 %collective-permute-start.19 = (bf16[256,128]{1,0:T(8,128)(2,1)S(1)}, bf16[256,128]{1,0:T(8,128)(2,1)S(1)}, u32[]{:S(2)}, u32[]{:S(2)}) collective-permute-start(bf16[256,128]{1,0:T(8,128)(2,1)S(1)} %get-tuple-element.67), channel_id=1, source_target_pairs={{0,4},{4,0},{8,12},{12,8},{1,5},{5,1},{9,13},{13,9},{2,6},{6,2},{1... | collective-permute-start | bytes 196616 | tf_op jit(solution)/shard_map/ppermute | solution.py:116
  98.0 1.7 %collective-permute-start.20 = (bf16[256,128]{1,0:T(8,128)(2,1)S(1)}, bf16[256,128]{1,0:T(8,128)(2,1)S(1)}, u32[]{:S(2)}, u32[]{:S(2)}) collective-permute-start(bf16[256,128]{1,0:T(8,128)(2,1)S(1)} %get-tuple-element.68), channel_id=1, source_target_pairs={{0,8},{4,12},{8,0},{12,4},{1,9},{5,13},{9,1},{13,5},{2,10},{6,14},... | collective-permute-start | bytes 196616 | tf_op jit(solution)/shard_map/ppermute | solution.py:116
  99.7 0.8 collective-permute-done.16.refs_8_
  100.5 2.4 %collective-permute-start.21 = (bf16[256,128]{1,0:T(8,128)(2,1)S(1)}, bf16[256,128]{1,0:T(8,128)(2,1)S(1)}, u32[]{:S(2)}, u32[]{:S(2)}) collective-permute-start(bf16[256,128]{1,0:T(8,128)(2,1)S(1)} %get-tuple-element.69), channel_id=1, source_target_pairs={{0,12},{4,8},{8,4},{12,0},{1,13},{5,9},{9,5},{13,1},{2,14},{6,10},... | collective-permute-start | bytes 196616 | tf_op jit(solution)/shard_map/ppermute | solution.py:116
  103.0 2.7 %collective-permute-done.17.refs_2_ = bf16[256,512]{1,0:T(8,128)(2,1)S(1)} collective-permute-done((bf16[256,512]{1,0:T(8,128)(2,1)S(1)}, bf16[256,512]{1,0:T(8,128)(2,1)S(1)}, u32[]{:S(2)}, u32[]{:S(2)}) %collective-permute-start.17) | collective-permute-done | bytes 262176 | tf_op jit(solution)/shard_map/ppermute | solution.py:116
  105.7 0.4 collective-permute-start.23
  106.0 0.7 collective-permute-done.21.refs_3_
  106.7 1.9 %shard_map.91 = (f32[4,256,512]{2,1,0:T(8,128)S(1)}, bf16[256,256]{1,0:T(8,128)(2,1)S(1)}) custom-call(bf16[256,128]{1,0:T(8,128)(2,1)S(1)} %get-tuple-element.66.refs_0_, bf16[256,128]{1,0:T(8,128)(2,1)S(1)} %collective-permute-done.19.refs_1_, bf16[256,128]{1,0:T(8,128)(2,1)S(1)} %collective-permute-done.20.refs_2_, ...), custom_call_target="tpu_custom_call" | custom-call | flops 10000000000 | bytes 10000000 | tf_op jit(solution)/shard_map/pallas_call | solution.py:130
  108.6 5.2 %collective-permute-done.23.refs_3_ = bf16[256,512]{1,0:T(8,128)(2,1)S(1)} collective-permute-done((bf16[256,512]{1,0:T(8,128)(2,1)}, bf16[256,512]{1,0:T(8,128)(2,1)S(1)}, u32[]{:S(2)}, u32[]{:S(2)}) %collective-permute-start.23) | collective-permute-done | bytes 262176 | tf_op jit(solution)/shard_map/ppermute | solution.py:116
  113.8 0.6 shard_map.92
  114.5 1.9 %collective-permute-done.24 = bf16[2,256,512]{2,1,0:T(8,128)(2,1)S(1)} collective-permute-done((bf16[2,256,512]{2,1,0:T(8,128)(2,1)S(1)}, bf16[2,256,512]{2,1,0:T(8,128)(2,1)S(1)}, u32[]{:S(2)}, u32[]{:S(2)}) %collective-permute-start.24) | collective-permute-done | bytes 524320 | tf_op jit(solution)/shard_map/ppermute | solution.py:116
  116.5 1.6 %collective-permute-start.25 = (bf16[256,512]{1,0:T(8,128)(2,1)S(1)}, bf16[256,512]{1,0:T(8,128)(2,1)S(1)}, u32[]{:S(2)}, u32[]{:S(2)}) collective-permute-start(bf16[256,512]{1,0:T(8,128)(2,1)S(1)} %fusion.1), channel_id=1, source_target_pairs={{0,2},{2,0},{1,3},{3,1},{4,6},{6,4},{5,7},{7,5},{8,10},{10,8},{9,1... | collective-permute-start | bytes 786440 | tf_op jit(solution)/shard_map/ppermute | solution.py:116
  118.1 1.8 %shard_map.86 = bf16[192,2048]{1,0:T(8,128)(2,1)} custom-call(s32[8]{0:T(128)S(1)} %copy-done.8, bf16[3,192,2048]{2,1,0:T(8,128)(2,1)S(1)} %copy-done), custom_call_target="tpu_custom_call" | custom-call | tf_op jit(solution)/shard_map/pallas_call | solution.py:169
  119.9 5.0 %collective-permute-done.25 = bf16[256,512]{1,0:T(8,128)(2,1)S(1)} collective-permute-done((bf16[256,512]{1,0:T(8,128)(2,1)S(1)}, bf16[256,512]{1,0:T(8,128)(2,1)S(1)}, u32[]{:S(2)}, u32[]{:S(2)}) %collective-permute-start.25) | collective-permute-done | bytes 262176 | tf_op jit(solution)/shard_map/ppermute | solution.py:116
  124.9 0.8 fusion
  (38 shorter events, 1.3 us)
Async XLA Ops:
  0.6 9.0 %copy-start.2 = (bf16[512,512]{1,0:T(8,128)(2,1)S(1)}, bf16[512,512]{1,0:T(8,128)(2,1)}, u32[]{:S(2)}) copy-start(bf16[512,512]{1,0:T(8,128)(2,1)} %refs_2_.3) | copy-start | bytes 1572868
  0.6 9.0 %copy-start.7 = (s32[256]{0:T(256)S(1)}, s32[256]{0:T(256)}, u32[]{:S(2)}) copy-start(s32[256]{0:T(256)} %param.9) | copy-start | bytes 3076
  0.7 9.0 %copy-start.1 = (bf16[1024,1024]{1,0:T(8,128)(2,1)S(1)}, bf16[1024,1024]{1,0:T(8,128)(2,1)}, u32[]{:S(2)}) copy-start(bf16[1024,1024]{1,0:T(8,128)(2,1)} %refs_1_.3) | copy-start | bytes 6291460
  3.8 5.8 %collective-permute-start = (bf16[640,1024]{1,0:T(8,128)(2,1)}, bf16[640,1024]{1,0:T(8,128)(2,1)S(1)}, u32[]{:S(2)}, u32[]{:S(2)}) collective-permute-start(bf16[640,1024]{1,0:T(8,128)(2,1)} %get-tuple-element.40), channel_id=1, source_target_pairs={{0,1},{1,0},{2,3},{3,2},{4,5},{5,4},{6,7},{7,6},{8,9},{9,8},{10,11... | collective-permute-start | bytes 3932168 | tf_op jit(solution)/shard_map/ppermute | solution.py:116
  4.4 32.4 %collective-permute-start.3 = (bf16[640,512]{1,0:T(8,128)(2,1)}, bf16[640,512]{1,0:T(8,128)(2,1)S(1)}, u32[]{:S(2)}, u32[]{:S(2)}) collective-permute-start(bf16[640,512]{1,0:T(8,128)(2,1)} %get-tuple-element.39.refs_0_), channel_id=1, source_target_pairs={{0,4},{4,0},{8,12},{12,8},{1,5},{5,1},{9,13},{13,9},{2,6},{6,2},{1... | collective-permute-start | bytes 1966088 | tf_op jit(solution)/shard_map/ppermute | solution.py:116
  7.0 31.8 %collective-permute-start.5 = (bf16[640,512]{1,0:T(8,128)(2,1)}, bf16[640,512]{1,0:T(8,128)(2,1)S(1)}, u32[]{:S(2)}, u32[]{:S(2)}) collective-permute-start(bf16[640,512]{1,0:T(8,128)(2,1)} %get-tuple-element.39.refs_0_), channel_id=1, source_target_pairs={{0,8},{4,12},{8,0},{12,4},{1,9},{5,13},{9,1},{13,5},{2,10},{6,14},... | collective-permute-start | bytes 1966088 | tf_op jit(solution)/shard_map/ppermute | solution.py:116
  9.6 1.0 copy-start.5
  10.7 1.1 copy-start.4
  10.9 33.0 %collective-permute-start.1 = (bf16[336,512]{1,0:T(8,128)(2,1)S(1)}, bf16[336,512]{1,0:T(8,128)(2,1)S(1)}, u32[]{:S(2)}, u32[]{:S(2)}) collective-permute-start(bf16[336,512]{1,0:T(8,128)(2,1)S(1)} %get-tuple-element.41), channel_id=1, source_target_pairs={{0,4},{4,0},{8,12},{12,8},{1,5},{5,1},{9,13},{13,9},{2,6},{6,2},{1... | collective-permute-start | bytes 1032200 | tf_op jit(solution)/shard_map/ppermute | solution.py:116
  11.8 36.6 %collective-permute-start.2 = (bf16[640,512]{1,0:T(8,128)(2,1)S(1)}, bf16[640,512]{1,0:T(8,128)(2,1)S(1)}, u32[]{:S(2)}, u32[]{:S(2)}) collective-permute-start(bf16[640,512]{1,0:T(8,128)(2,1)S(1)} %copy-done.4), channel_id=1, source_target_pairs={{0,2},{2,0},{1,3},{3,1},{4,6},{6,4},{5,7},{7,5},{8,10},{10,8},{9,1... | collective-permute-start | bytes 1966088 | tf_op jit(solution)/shard_map/ppermute | solution.py:116
  36.7 17.7 %collective-permute-start.4 = (bf16[640,512]{1,0:T(8,128)(2,1)S(1)}, bf16[640,512]{1,0:T(8,128)(2,1)S(1)}, u32[]{:S(2)}, u32[]{:S(2)}) collective-permute-start(bf16[640,512]{1,0:T(8,128)(2,1)S(1)} %collective-permute-done.3.refs_2_), channel_id=1, source_target_pairs={{0,2},{2,0},{1,3},{3,1},{4,6},{6,4},{5,7},{7,5},{8,10},{10,8},{9,1... | collective-permute-start | bytes 1966088 | tf_op jit(solution)/shard_map/ppermute | solution.py:116
  38.8 28.2 %collective-permute-start.7 = (bf16[640,512]{1,0:T(8,128)(2,1)S(1)}, bf16[640,512]{1,0:T(8,128)(2,1)S(1)}, u32[]{:S(2)}, u32[]{:S(2)}) collective-permute-start(bf16[640,512]{1,0:T(8,128)(2,1)S(1)} %collective-permute-done.5.refs_4_), channel_id=1, source_target_pairs={{0,2},{2,0},{1,3},{3,1},{4,6},{6,4},{5,7},{7,5},{8,10},{10,8},{9,1... | collective-permute-start | bytes 1966088 | tf_op jit(solution)/shard_map/ppermute | solution.py:116
  44.0 24.4 %collective-permute-start.6 = (bf16[640,512]{1,0:T(8,128)(2,1)S(1)}, bf16[640,512]{1,0:T(8,128)(2,1)S(1)}, u32[]{:S(2)}, u32[]{:S(2)}) collective-permute-start(bf16[640,512]{1,0:T(8,128)(2,1)S(1)} %collective-permute-done.5.refs_4_), channel_id=1, source_target_pairs={{0,4},{4,0},{8,12},{12,8},{1,5},{5,1},{9,13},{13,9},{2,6},{6,2},{1... | collective-permute-start | bytes 1966088 | tf_op jit(solution)/shard_map/ppermute | solution.py:116
  45.8 22.6 %collective-permute-start.9 = (bf16[336,512]{1,0:T(8,128)(2,1)S(1)}, bf16[336,512]{1,0:T(8,128)(2,1)S(1)}, u32[]{:S(2)}, u32[]{:S(2)}) collective-permute-start(bf16[336,512]{1,0:T(8,128)(2,1)S(1)} %get-tuple-element.46), channel_id=1, source_target_pairs={{0,8},{4,12},{8,0},{12,4},{1,9},{5,13},{9,1},{13,5},{2,10},{6,14},... | collective-permute-start | bytes 1032200 | tf_op jit(solution)/shard_map/ppermute | solution.py:116
  54.4 14.0 %collective-permute-start.8 = (bf16[336,512]{1,0:T(8,128)(2,1)S(1)}, bf16[336,512]{1,0:T(8,128)(2,1)S(1)}, u32[]{:S(2)}, u32[]{:S(2)}) collective-permute-start(bf16[336,512]{1,0:T(8,128)(2,1)S(1)} %collective-permute-done.1.refs_9_), channel_id=1, source_target_pairs={{0,16},{16,0},{1,17},{17,1},{2,18},{18,2},{3,19},{19,3},{4,20},{20... | collective-permute-start | bytes 1032200 | tf_op jit(solution)/shard_map/ppermute | solution.py:116
  56.3 21.1 %collective-permute-start.11 = (bf16[336,512]{1,0:T(8,128)(2,1)S(1)}, bf16[336,512]{1,0:T(8,128)(2,1)S(1)}, u32[]{:S(2)}, u32[]{:S(2)}) collective-permute-start(bf16[336,512]{1,0:T(8,128)(2,1)S(1)} %get-tuple-element.54), channel_id=1, source_target_pairs={{0,12},{4,8},{8,4},{12,0},{1,13},{5,9},{9,5},{13,1},{2,14},{6,10},... | collective-permute-start | bytes 1032200 | tf_op jit(solution)/shard_map/ppermute | solution.py:116
  68.4 9.0 %collective-permute-start.12 = (bf16[336,512]{1,0:T(8,128)(2,1)S(1)}, bf16[336,512]{1,0:T(8,128)(2,1)S(1)}, u32[]{:S(2)}, u32[]{:S(2)}) collective-permute-start(bf16[336,512]{1,0:T(8,128)(2,1)S(1)} %collective-permute-done.9.refs_11_), channel_id=1, source_target_pairs={{0,16},{16,0},{1,17},{17,1},{2,18},{18,2},{3,19},{19,3},{4,20},{20... | collective-permute-start | bytes 1032200 | tf_op jit(solution)/shard_map/ppermute | solution.py:116
  69.9 14.6 %collective-permute-start.10 = (bf16[640,512]{1,0:T(8,128)(2,1)S(1)}, bf16[640,512]{1,0:T(8,128)(2,1)S(1)}, u32[]{:S(2)}, u32[]{:S(2)}) collective-permute-start(bf16[640,512]{1,0:T(8,128)(2,1)S(1)} %collective-permute-done.6.refs_6_), channel_id=1, source_target_pairs={{0,2},{2,0},{1,3},{3,1},{4,6},{6,4},{5,7},{7,5},{8,10},{10,8},{9,1... | collective-permute-start | bytes 1966088 | tf_op jit(solution)/shard_map/ppermute | solution.py:116
  77.4 8.7 %collective-permute-start.13 = (bf16[336,512]{1,0:T(8,128)(2,1)S(1)}, bf16[336,512]{1,0:T(8,128)(2,1)S(1)}, u32[]{:S(2)}, u32[]{:S(2)}) collective-permute-start(bf16[336,512]{1,0:T(8,128)(2,1)S(1)} %collective-permute-done.11.refs_13_), channel_id=1, source_target_pairs={{0,16},{16,0},{1,17},{17,1},{2,18},{18,2},{3,19},{19,3},{4,20},{20... | collective-permute-start | bytes 1032200 | tf_op jit(solution)/shard_map/ppermute | solution.py:116
  78.9 12.3 %collective-permute-start.14 = (bf16[256,512]{1,0:T(8,128)(2,1)S(1)}, bf16[256,512]{1,0:T(8,128)(2,1)S(1)}, u32[]{:S(2)}, u32[]{:S(2)}) collective-permute-start(bf16[256,512]{1,0:T(8,128)(2,1)S(1)} %get-tuple-element.59), channel_id=1, source_target_pairs={{0,8},{4,12},{8,0},{12,4},{1,9},{5,13},{9,1},{13,5},{2,10},{6,14},... | collective-permute-start | bytes 786440 | tf_op jit(solution)/shard_map/ppermute | solution.py:116
  81.5 9.6 %collective-permute-start.15 = (bf16[256,512]{1,0:T(8,128)(2,1)S(1)}, bf16[256,512]{1,0:T(8,128)(2,1)S(1)}, u32[]{:S(2)}, u32[]{:S(2)}) collective-permute-start(bf16[256,512]{1,0:T(8,128)(2,1)S(1)} %get-tuple-element.59), channel_id=1, source_target_pairs={{0,4},{4,0},{8,12},{12,8},{1,5},{5,1},{9,13},{13,9},{2,6},{6,2},{1... | collective-permute-start | bytes 786440 | tf_op jit(solution)/shard_map/ppermute | solution.py:116
  91.2 3.2 %collective-permute-start.18 = (f32[1280,256]{1,0:T(8,128)}, f32[1280,256]{1,0:T(8,128)S(1)}, u32[]{:S(2)}, u32[]{:S(2)}) collective-permute-start(f32[1280,256]{1,0:T(8,128)} %get-tuple-element.64), channel_id=1, source_target_pairs={{0,1},{1,0},{2,3},{3,2},{4,5},{5,4},{6,7},{7,6},{8,9},{9,8},{10,11... | collective-permute-start | bytes 3932168 | tf_op jit(solution)/shard_map/ppermute | solution.py:116
  91.3 9.2 %collective-permute-start.16 = (bf16[256,512]{1,0:T(8,128)(2,1)S(1)}, bf16[256,512]{1,0:T(8,128)(2,1)}, u32[]{:S(2)}, u32[]{:S(2)}) collective-permute-start(bf16[256,512]{1,0:T(8,128)(2,1)S(1)} %collective-permute-done.14.refs_7_), channel_id=1, source_target_pairs={{0,16},{16,0},{1,17},{17,1},{2,18},{18,2},{3,19},{19,3},{4,20},{20... | collective-permute-start | bytes 786440 | tf_op jit(solution)/shard_map/ppermute | solution.py:116
  92.1 13.9 %collective-permute-start.22 = (bf16[256,512]{1,0:T(8,128)(2,1)S(1)}, bf16[256,512]{1,0:T(8,128)(2,1)S(1)}, u32[]{:S(2)}, u32[]{:S(2)}) collective-permute-start(bf16[256,512]{1,0:T(8,128)(2,1)S(1)} %collective-permute-done.14.refs_7_), channel_id=1, source_target_pairs={{0,4},{4,0},{8,12},{12,8},{1,5},{5,1},{9,13},{13,9},{2,6},{6,2},{1... | collective-permute-start | bytes 786440 | tf_op jit(solution)/shard_map/ppermute | solution.py:116
  93.2 12.4 %collective-permute-start.17 = (bf16[256,512]{1,0:T(8,128)(2,1)S(1)}, bf16[256,512]{1,0:T(8,128)(2,1)S(1)}, u32[]{:S(2)}, u32[]{:S(2)}) collective-permute-start(bf16[256,512]{1,0:T(8,128)(2,1)S(1)} %collective-permute-done.15.refs_6_), channel_id=1, source_target_pairs={{0,16},{16,0},{1,17},{17,1},{2,18},{18,2},{3,19},{19,3},{4,20},{20... | collective-permute-start | bytes 786440 | tf_op jit(solution)/shard_map/ppermute | solution.py:116
  94.4 12.3 %copy-start.3 = (bf16[256,2048]{1,0:T(8,128)(2,1)S(1)}, bf16[256,2048]{1,0:T(8,128)(2,1)}, u32[]{:S(2)}) copy-start(bf16[256,2048]{1,0:T(8,128)(2,1)} %refs_4_.5) | copy-start | bytes 3145732
  94.4 12.3 %copy-start.6 = (bf16[512,512]{1,0:T(8,128)(2,1)S(1)}, bf16[512,512]{1,0:T(8,128)(2,1)}, u32[]{:S(2)}) copy-start(bf16[512,512]{1,0:T(8,128)(2,1)} %refs_5_.1) | copy-start | bytes 1572868
  96.6 9.4 %collective-permute-start.19 = (bf16[256,128]{1,0:T(8,128)(2,1)S(1)}, bf16[256,128]{1,0:T(8,128)(2,1)S(1)}, u32[]{:S(2)}, u32[]{:S(2)}) collective-permute-start(bf16[256,128]{1,0:T(8,128)(2,1)S(1)} %get-tuple-element.67), channel_id=1, source_target_pairs={{0,4},{4,0},{8,12},{12,8},{1,5},{5,1},{9,13},{13,9},{2,6},{6,2},{1... | collective-permute-start | bytes 196616 | tf_op jit(solution)/shard_map/ppermute | solution.py:116
  98.0 8.1 %collective-permute-start.20 = (bf16[256,128]{1,0:T(8,128)(2,1)S(1)}, bf16[256,128]{1,0:T(8,128)(2,1)S(1)}, u32[]{:S(2)}, u32[]{:S(2)}) collective-permute-start(bf16[256,128]{1,0:T(8,128)(2,1)S(1)} %get-tuple-element.68), channel_id=1, source_target_pairs={{0,8},{4,12},{8,0},{12,4},{1,9},{5,13},{9,1},{13,5},{2,10},{6,14},... | collective-permute-start | bytes 196616 | tf_op jit(solution)/shard_map/ppermute | solution.py:116
  100.5 6.2 %collective-permute-start.21 = (bf16[256,128]{1,0:T(8,128)(2,1)S(1)}, bf16[256,128]{1,0:T(8,128)(2,1)S(1)}, u32[]{:S(2)}, u32[]{:S(2)}) collective-permute-start(bf16[256,128]{1,0:T(8,128)(2,1)S(1)} %get-tuple-element.69), channel_id=1, source_target_pairs={{0,12},{4,8},{8,4},{12,0},{1,13},{5,9},{9,5},{13,1},{2,14},{6,10},... | collective-permute-start | bytes 196616 | tf_op jit(solution)/shard_map/ppermute | solution.py:116
  105.7 8.1 %collective-permute-start.23 = (bf16[256,512]{1,0:T(8,128)(2,1)}, bf16[256,512]{1,0:T(8,128)(2,1)S(1)}, u32[]{:S(2)}, u32[]{:S(2)}) collective-permute-start(bf16[256,512]{1,0:T(8,128)(2,1)} %collective-permute-done.16.refs_8_), channel_id=1, source_target_pairs={{0,4},{4,0},{8,12},{12,8},{1,5},{5,1},{9,13},{13,9},{2,6},{6,2},{1... | collective-permute-start | bytes 786440 | tf_op jit(solution)/shard_map/ppermute | solution.py:116
  113.8 4.3 %copy-start = (bf16[3,192,2048]{2,1,0:T(8,128)(2,1)S(1)}, bf16[3,192,2048]{2,1,0:T(8,128)(2,1)}, u32[]{:S(2)}) copy-start(bf16[3,192,2048]{2,1,0:T(8,128)(2,1)} %refs_1_.2) | copy-start | bytes 7077892
  113.8 4.3 %copy-start.8 = (s32[8]{0:T(128)S(1)}, s32[8]{0:T(128)}, u32[]{:S(2)}) copy-start(s32[8]{0:T(128)} %refs_0_.1) | copy-start | bytes 100
  114.5 2.0 %collective-permute-start.24 = (bf16[2,256,512]{2,1,0:T(8,128)(2,1)S(1)}, bf16[2,256,512]{2,1,0:T(8,128)(2,1)S(1)}, u32[]{:S(2)}, u32[]{:S(2)}) collective-permute-start(bf16[2,256,512]{2,1,0:T(8,128)(2,1)S(1)} %get-tuple-element.75), channel_id=1, source_target_pairs={{0,1},{1,0},{2,3},{3,2},{4,5},{5,4},{6,7},{7,6},{8,9},{9,8},{10,11... | collective-permute-start | bytes 1572872 | tf_op jit(solution)/shard_map/ppermute | solution.py:116
  116.5 8.4 %collective-permute-start.25 = (bf16[256,512]{1,0:T(8,128)(2,1)S(1)}, bf16[256,512]{1,0:T(8,128)(2,1)S(1)}, u32[]{:S(2)}, u32[]{:S(2)}) collective-permute-start(bf16[256,512]{1,0:T(8,128)(2,1)S(1)} %fusion.1), channel_id=1, source_target_pairs={{0,2},{2,0},{1,3},{3,1},{4,6},{6,4},{5,7},{7,5},{8,10},{10,8},{9,1... | collective-permute-start | bytes 786440 | tf_op jit(solution)/shard_map/ppermute | solution.py:116

commit v23 on v18

--- a/solution.py
+++ b/solution.py
@@ -182,18 +182,15 @@
     audio_ref,
     kv_ref,
     query_ref,
-    out_w,
     packed_ref,
     other_ref,
-    half_ref,
     held_ref,
     made_ref,
     other_vmem,
-    half_vmem,
     plan_smem,
     sems,
 ):
-    rep_at, mem_at, grp_at = (lax.axis_index(name) for name in ("rep", "mem", "grp"))
+    rep_at, mem_at = lax.axis_index("rep"), lax.axis_index("mem")
     rows, width = held_ref.shape[1:]
     width = width // 2
     copies = []
@@ -206,7 +203,7 @@
 
     plan_copy = pltpu.make_async_copy(plan_ref, plan_smem, sems.at[25])
     plan_copy.start()
-    blocks = 4
+    blocks = 2
     step = rows // blocks
     for block in range(blocks):
         at = pl.ds(block * step, step)
@@ -229,7 +226,6 @@
             query_ref.at[part(2 * (1 - rep_at) + side, quarter)],
             other_vmem.at[pl.ds(depth, quarter), pl.ds(side * columns, columns)],
         )
-    copy(out_w.at[part(grp_at, half_ref.shape[0])], half_vmem)
     for started in copies:
         started.start()
     plan_copy.wait()
@@ -251,7 +247,6 @@
     stages = (
         (2, made_ref.at[audio_at], packed_ref.at[audio_at]),
         (3, other_vmem, other_ref),
-        (1, half_vmem, half_ref),
     )
     at = 2 * blocks
     for count, source, target in stages:
@@ -264,7 +259,7 @@
         leaving.wait()
 
 
-def weight_body(align_ref, kv_ref, query_ref, other_ref, own_ref, *piece_refs):
+def weight_body(align_ref, kv_ref, query_ref, other_ref, out_w, half_ref, own_ref, *piece_refs):
     seq_at, rep_at, grp_at = (lax.axis_index(name) for name in ("seq", "rep", "grp"))
     kv_half, query_half = kv_ref.shape[0] // 2, query_ref.shape[0] // 2
     kv_rows, query_rows = kv_half // 2, query_half // 2
@@ -291,6 +286,8 @@
                 kv_half + side * fold : kv_half + (side + 1) * fold, other_lanes
             ]
 
+    depth = half_ref.shape[0]
+    half_ref[...] = out_w[pl.ds(pl.multiple_of(grp_at * depth, depth), depth), :]
     for group in range(2):
         fill(own_ref, 0, group, group * kv_rows, kv_half + group * fold)
     for bit, piece_ref in enumerate(piece_refs, 1):
@@ -496,24 +493,22 @@
     def bfloat(*shape):
         return jax.ShapeDtypeStruct(shape, jnp.bfloat16)
 
-    packed, other, out_half = kernel_call(
+    packed, other = kernel_call(
         first_body,
         [
             bfloat(2 * video_rows + audio_rows, half_depth),
             bfloat(half_depth + query_quarter, kv_weight.shape[1]),
-            bfloat(out_weight.shape[0] // 2, out_weight.shape[1]),
-        ],
-        [plan, video_cache, audio_tokens, kv_weight, query_weight, out_weight],
+        ],
+        [plan, video_cache, audio_tokens, kv_weight, query_weight],
         scratch=[
             pltpu.VMEM((3, video_rows, 2 * half_depth), jnp.bfloat16),
             pltpu.VMEM((2 * video_rows + audio_rows, half_depth), jnp.bfloat16),
             pltpu.VMEM((half_depth + query_quarter, kv_weight.shape[1]), jnp.bfloat16),
-            pltpu.VMEM((out_weight.shape[0] // 2, out_weight.shape[1]), jnp.bfloat16),
             pltpu.SMEM(plan.shape, jnp.int32),
             pltpu.SemaphoreType.DMA((26,)),
         ],
-        loose_in=(0, 1, 2, 3, 4, 5),
-        loose_out=(0, 1, 2),
+        loose_in=(0, 1, 2, 3, 4),
+        loose_out=(0, 1),
         limit=61,
     )
 
@@ -521,10 +516,10 @@
     across = [swap(packed, "mem", 1)]
     other = swap(other, "rep", 1)
     rows = (half_depth + query_quarter) // 2
-    weight_own, *pieces = kernel_call(
+    out_half, weight_own, *pieces = kernel_call(
         weight_body,
-        [bfloat(2 * rows, 2 * width)] + [bfloat(rows + 16, 2 * width)] * 3,
-        [alignment[None], kv_weight, query_weight, other],
+        [bfloat(out_weight.shape[0] // 2, out_weight.shape[1]), bfloat(2 * rows, 2 * width)] + [bfloat(rows + 16, 2 * width)] * 3,
+        [alignment[None], kv_weight, query_weight, other, out_weight],
         limit=4,
     )
     pieces = [swap(piece, "seq", bit) for bit, piece in enumerate(pieces, 1)]

time: 123 us -> 123 us (level)
  no operation moved by 1% of the time
where the time goes in v23:
time: 123 us; the launch traced here: 122 us
  waiting for transfers between devices  68.7 us (56%)
  starting transfers between devices  37.1 us (30%)
  Pallas kernels  13.2 us (11%)
  local copies, waits for them, and re-layouts  1.43 us (1%)
    ppermute x26, waiting for transfers between devices, swap(): return lax.ppermute(value, axis, [(i, i ^ bit) for i in range(size)])  68.7 us
    ppermute x26, starting transfers between devices, swap(): return lax.ppermute(value, axis, [(i, i ^ bit) for i in range(size)])  37.1 us
    pallas_call x7, Pallas kernels, kernel_call(): pl.pallas_call(whole, out_shape=outs, in_specs=spots + [ANY] * len(after)...  11.4 us
  transfers between devices with their start and end apart: 26, of which 17 were waited for; matrix products, arithmetic and copies ran while one was open for 0% of the time, Pallas kernels for 8%

profile of v23, /device:TPU:0, one launch (start us, length us, event | category | flops | bytes accessed | tf_op | source)
XLA Modules:
  0.0 122.3 jit_solution(11564851351654737970)
XLA Ops:
  0.7 3.2 %shard_map.87 = (bf16[640,512]{1,0:T(8,128)(2,1)}, bf16[640,1024]{1,0:T(8,128)(2,1)}) custom-call(s32[8]{0:T(128)} %refs_0_.1, bf16[3,192,2048]{2,1,0:T(8,128)(2,1)} %refs_1_.2, bf16[256,2048]{1,0:T(8,128)(2,1)} %refs_4_.5, bf16[1024,1024]{1,0:T(8,128)(2,1)} %refs_1_.3, bf16[512,512]{1,0:T(8,128)(2,1)} %refs_2_.3), custom_call_target="tpu_custom_call" | custom-call | tf_op jit(solution)/shard_map/pallas_call | solution.py:130
  3.9 0.5 collective-permute-start
  4.4 2.6 %collective-permute-start.3 = (bf16[640,512]{1,0:T(8,128)(2,1)}, bf16[640,512]{1,0:T(8,128)(2,1)S(1)}, u32[]{:S(2)}, u32[]{:S(2)}) collective-permute-start(bf16[640,512]{1,0:T(8,128)(2,1)} %get-tuple-element.47.refs_0_), channel_id=1, source_target_pairs={{0,4},{4,0},{8,12},{12,8},{1,5},{5,1},{9,13},{13,9},{2,6},{6,2},{1... | collective-permute-start | bytes 1966088 | tf_op jit(solution)/shard_map/ppermute | solution.py:116
  7.0 2.6 %collective-permute-start.5 = (bf16[640,512]{1,0:T(8,128)(2,1)}, bf16[640,512]{1,0:T(8,128)(2,1)S(1)}, u32[]{:S(2)}, u32[]{:S(2)}) collective-permute-start(bf16[640,512]{1,0:T(8,128)(2,1)} %get-tuple-element.47.refs_0_), channel_id=1, source_target_pairs={{0,8},{4,12},{8,0},{12,4},{1,9},{5,13},{9,1},{13,5},{2,10},{6,14},... | collective-permute-start | bytes 1966088 | tf_op jit(solution)/shard_map/ppermute | solution.py:116
  9.6 1.0 copy-done.5
  10.9 0.6 collective-permute-start.1
  11.8 1.5 %collective-permute-start.2 = (bf16[640,512]{1,0:T(8,128)(2,1)S(1)}, bf16[640,512]{1,0:T(8,128)(2,1)S(1)}, u32[]{:S(2)}, u32[]{:S(2)}) collective-permute-start(bf16[640,512]{1,0:T(8,128)(2,1)S(1)} %copy-done.2), channel_id=1, source_target_pairs={{0,2},{2,0},{1,3},{3,1},{4,6},{6,4},{5,7},{7,5},{8,10},{10,8},{9,1... | collective-permute-start | bytes 1966088 | tf_op jit(solution)/shard_map/ppermute | solution.py:116
  13.3 23.5 %collective-permute-done.3.refs_2_ = bf16[640,512]{1,0:T(8,128)(2,1)S(1)} collective-permute-done((bf16[640,512]{1,0:T(8,128)(2,1)}, bf16[640,512]{1,0:T(8,128)(2,1)S(1)}, u32[]{:S(2)}, u32[]{:S(2)}) %collective-permute-start.3) | collective-permute-done | bytes 655392 | tf_op jit(solution)/shard_map/ppermute | solution.py:116
  36.7 1.9 %collective-permute-start.4 = (bf16[640,512]{1,0:T(8,128)(2,1)S(1)}, bf16[640,512]{1,0:T(8,128)(2,1)S(1)}, u32[]{:S(2)}, u32[]{:S(2)}) collective-permute-start(bf16[640,512]{1,0:T(8,128)(2,1)S(1)} %collective-permute-done.3.refs_2_), channel_id=1, source_target_pairs={{0,2},{2,0},{1,3},{3,1},{4,6},{6,4},{5,7},{7,5},{8,10},{10,8},{9,1... | collective-permute-start | bytes 1966088 | tf_op jit(solution)/shard_map/ppermute | solution.py:116
  38.8 1.5 %collective-permute-start.7 = (bf16[640,512]{1,0:T(8,128)(2,1)S(1)}, bf16[640,512]{1,0:T(8,128)(2,1)S(1)}, u32[]{:S(2)}, u32[]{:S(2)}) collective-permute-start(bf16[640,512]{1,0:T(8,128)(2,1)S(1)} %collective-permute-done.5.refs_4_), channel_id=1, source_target_pairs={{0,2},{2,0},{1,3},{3,1},{4,6},{6,4},{5,7},{7,5},{8,10},{10,8},{9,1... | collective-permute-start | bytes 1966088 | tf_op jit(solution)/shard_map/ppermute | solution.py:116
  40.3 3.7 %collective-permute-done.1.refs_7_ = bf16[336,512]{1,0:T(8,128)(2,1)S(1)} collective-permute-done((bf16[336,512]{1,0:T(8,128)(2,1)S(1)}, bf16[336,512]{1,0:T(8,128)(2,1)S(1)}, u32[]{:S(2)}, u32[]{:S(2)}) %collective-permute-start.1) | collective-permute-done | bytes 344096 | tf_op jit(solution)/shard_map/ppermute | solution.py:116
  44.0 1.8 %collective-permute-start.6 = (bf16[640,512]{1,0:T(8,128)(2,1)S(1)}, bf16[640,512]{1,0:T(8,128)(2,1)S(1)}, u32[]{:S(2)}, u32[]{:S(2)}) collective-permute-start(bf16[640,512]{1,0:T(8,128)(2,1)S(1)} %collective-permute-done.5.refs_4_), channel_id=1, source_target_pairs={{0,4},{4,0},{8,12},{12,8},{1,5},{5,1},{9,13},{13,9},{2,6},{6,2},{1... | collective-permute-start | bytes 1966088 | tf_op jit(solution)/shard_map/ppermute | solution.py:116
  45.8 2.5 %collective-permute-start.9 = (bf16[336,512]{1,0:T(8,128)(2,1)S(1)}, bf16[336,512]{1,0:T(8,128)(2,1)S(1)}, u32[]{:S(2)}, u32[]{:S(2)}) collective-permute-start(bf16[336,512]{1,0:T(8,128)(2,1)S(1)} %get-tuple-element.54), channel_id=1, source_target_pairs={{0,8},{4,12},{8,0},{12,4},{1,9},{5,13},{9,1},{13,5},{2,10},{6,14},... | collective-permute-start | bytes 1032200 | tf_op jit(solution)/shard_map/ppermute | solution.py:116
  48.3 6.1 %collective-permute-done.4.refs_3_ = bf16[640,512]{1,0:T(8,128)(2,1)S(1)} collective-permute-done((bf16[640,512]{1,0:T(8,128)(2,1)S(1)}, bf16[640,512]{1,0:T(8,128)(2,1)S(1)}, u32[]{:S(2)}, u32[]{:S(2)}) %collective-permute-start.4) | collective-permute-done | bytes 655392 | tf_op jit(solution)/shard_map/ppermute | solution.py:116
  54.4 1.9 %collective-permute-start.8 = (bf16[336,512]{1,0:T(8,128)(2,1)S(1)}, bf16[336,512]{1,0:T(8,128)(2,1)S(1)}, u32[]{:S(2)}, u32[]{:S(2)}) collective-permute-start(bf16[336,512]{1,0:T(8,128)(2,1)S(1)} %collective-permute-done.1.refs_7_), channel_id=1, source_target_pairs={{0,16},{16,0},{1,17},{17,1},{2,18},{18,2},{3,19},{19,3},{4,20},{20... | collective-permute-start | bytes 1032200 | tf_op jit(solution)/shard_map/ppermute | solution.py:116
  56.3 2.5 %collective-permute-start.11 = (bf16[336,512]{1,0:T(8,128)(2,1)S(1)}, bf16[336,512]{1,0:T(8,128)(2,1)S(1)}, u32[]{:S(2)}, u32[]{:S(2)}) collective-permute-start(bf16[336,512]{1,0:T(8,128)(2,1)S(1)} %get-tuple-element.60), channel_id=1, source_target_pairs={{0,12},{4,8},{8,4},{12,0},{1,13},{5,9},{9,5},{13,1},{2,14},{6,10},... | collective-permute-start | bytes 1032200 | tf_op jit(solution)/shard_map/ppermute | solution.py:116
  58.8 8.2 %collective-permute-done.7.refs_5_ = bf16[640,512]{1,0:T(8,128)(2,1)S(1)} collective-permute-done((bf16[640,512]{1,0:T(8,128)(2,1)S(1)}, bf16[640,512]{1,0:T(8,128)(2,1)S(1)}, u32[]{:S(2)}, u32[]{:S(2)}) %collective-permute-start.7) | collective-permute-done | bytes 655392 | tf_op jit(solution)/shard_map/ppermute | solution.py:116
  67.0 1.4 %collective-permute-done.9.refs_8_ = bf16[336,512]{1,0:T(8,128)(2,1)S(1)} collective-permute-done((bf16[336,512]{1,0:T(8,128)(2,1)S(1)}, bf16[336,512]{1,0:T(8,128)(2,1)S(1)}, u32[]{:S(2)}, u32[]{:S(2)}) %collective-permute-start.9) | collective-permute-done | bytes 344096 | tf_op jit(solution)/shard_map/ppermute | solution.py:116
  68.4 1.5 %collective-permute-start.12 = (bf16[336,512]{1,0:T(8,128)(2,1)S(1)}, bf16[336,512]{1,0:T(8,128)(2,1)S(1)}, u32[]{:S(2)}, u32[]{:S(2)}) collective-permute-start(bf16[336,512]{1,0:T(8,128)(2,1)S(1)} %collective-permute-done.9.refs_8_), channel_id=1, source_target_pairs={{0,16},{16,0},{1,17},{17,1},{2,18},{18,2},{3,19},{19,3},{4,20},{20... | collective-permute-start | bytes 1032200 | tf_op jit(solution)/shard_map/ppermute | solution.py:116
  69.9 1.5 %collective-permute-start.10 = (bf16[640,512]{1,0:T(8,128)(2,1)S(1)}, bf16[640,512]{1,0:T(8,128)(2,1)S(1)}, u32[]{:S(2)}, u32[]{:S(2)}) collective-permute-start(bf16[640,512]{1,0:T(8,128)(2,1)S(1)} %collective-permute-done.6.refs_6_), channel_id=1, source_target_pairs={{0,2},{2,0},{1,3},{3,1},{4,6},{6,4},{5,7},{7,5},{8,10},{10,8},{9,1... | collective-permute-start | bytes 1966088 | tf_op jit(solution)/shard_map/ppermute | solution.py:116
  71.4 1.2 shard_map.89
  72.6 4.8 %collective-permute-done.11.refs_10_ = bf16[336,512]{1,0:T(8,128)(2,1)S(1)} collective-permute-done((bf16[336,512]{1,0:T(8,128)(2,1)S(1)}, bf16[336,512]{1,0:T(8,128)(2,1)S(1)}, u32[]{:S(2)}, u32[]{:S(2)}) %collective-permute-start.11) | collective-permute-done | bytes 344096 | tf_op jit(solution)/shard_map/ppermute | solution.py:116
  77.4 1.5 %collective-permute-start.13 = (bf16[336,512]{1,0:T(8,128)(2,1)S(1)}, bf16[336,512]{1,0:T(8,128)(2,1)S(1)}, u32[]{:S(2)}, u32[]{:S(2)}) collective-permute-start(bf16[336,512]{1,0:T(8,128)(2,1)S(1)} %collective-permute-done.11.refs_10_), channel_id=1, source_target_pairs={{0,16},{16,0},{1,17},{17,1},{2,18},{18,2},{3,19},{19,3},{4,20},{20... | collective-permute-start | bytes 1032200 | tf_op jit(solution)/shard_map/ppermute | solution.py:116
  78.9 2.6 %collective-permute-start.14 = (bf16[256,512]{1,0:T(8,128)(2,1)S(1)}, bf16[256,512]{1,0:T(8,128)(2,1)S(1)}, u32[]{:S(2)}, u32[]{:S(2)}) collective-permute-start(bf16[256,512]{1,0:T(8,128)(2,1)S(1)} %get-tuple-element.75), channel_id=1, source_target_pairs={{0,8},{4,12},{8,0},{12,4},{1,9},{5,13},{9,1},{13,5},{2,10},{6,14},... | collective-permute-start | bytes 786440 | tf_op jit(solution)/shard_map/ppermute | solution.py:116
  81.6 1.3 %collective-permute-start.15 = (bf16[256,512]{1,0:T(8,128)(2,1)S(1)}, bf16[256,512]{1,0:T(8,128)(2,1)S(1)}, u32[]{:S(2)}, u32[]{:S(2)}) collective-permute-start(bf16[256,512]{1,0:T(8,128)(2,1)S(1)} %get-tuple-element.75), channel_id=1, source_target_pairs={{0,4},{4,0},{8,12},{12,8},{1,5},{5,1},{9,13},{13,9},{2,6},{6,2},{1... | collective-permute-start | bytes 786440 | tf_op jit(solution)/shard_map/ppermute | solution.py:116
  82.8 1.7 %collective-permute-done.10.refs_7_ = bf16[640,512]{1,0:T(8,128)(2,1)S(1)} collective-permute-done((bf16[640,512]{1,0:T(8,128)(2,1)S(1)}, bf16[640,512]{1,0:T(8,128)(2,1)S(1)}, u32[]{:S(2)}, u32[]{:S(2)}) %collective-permute-start.10) | collective-permute-done | bytes 655392 | tf_op jit(solution)/shard_map/ppermute | solution.py:116
  84.5 1.6 %collective-permute-done.13.refs_11_ = bf16[336,512]{1,0:T(8,128)(2,1)S(1)} collective-permute-done((bf16[336,512]{1,0:T(8,128)(2,1)S(1)}, bf16[336,512]{1,0:T(8,128)(2,1)S(1)}, u32[]{:S(2)}, u32[]{:S(2)}) %collective-permute-start.13) | collective-permute-done | bytes 344096 | tf_op jit(solution)/shard_map/ppermute | solution.py:116
  86.1 2.9 %shard_map.90 = (bf16[4,16,256]{2,1,0:T(8,128)(2,1)S(1)}, f32[1280,256]{1,0:T(8,128)}, f32[1280,256]{1,0:T(8,128)S(1)}) custom-call(bf16[640,512]{1,0:T(8,128)(2,1)S(1)} %copy-done.2, bf16[640,512]{1,0:T(8,128)(2,1)S(1)} %collective-permute-done.2.refs_1_, bf16[640,512]{1,0:T(8,128)(2,1)S(1)} %collective-permute-done.3.refs_2_, ...), custom_call_target="tpu_custom_call" | custom-call | tf_op jit(solution)/shard_map/pallas_call | solution.py:130
  89.0 2.2 %collective-permute-done.14.refs_7_ = bf16[256,512]{1,0:T(8,128)(2,1)S(1)} collective-permute-done((bf16[256,512]{1,0:T(8,128)(2,1)S(1)}, bf16[256,512]{1,0:T(8,128)(2,1)S(1)}, u32[]{:S(2)}, u32[]{:S(2)}) %collective-permute-start.14) | collective-permute-done | bytes 262176 | tf_op jit(solution)/shard_map/ppermute | solution.py:116
  91.6 0.5 collective-permute-start.16
  92.1 0.4 collective-permute-start.21
  92.5 1.9 %collective-permute-done.17.refs_3_ = f32[1280,256]{1,0:T(8,128)S(1)} collective-permute-done((f32[1280,256]{1,0:T(8,128)}, f32[1280,256]{1,0:T(8,128)S(1)}, u32[]{:S(2)}, u32[]{:S(2)}) %collective-permute-start.17) | collective-permute-done | bytes 1310752 | tf_op jit(solution)/shard_map/ppermute | solution.py:116
  94.4 2.2 %shard_map.91 = (bf16[256,128]{1,0:T(8,128)(2,1)S(1)}, bf16[256,128]{1,0:T(8,128)(2,1)S(1)}, bf16[256,128]{1,0:T(8,128)(2,1)S(1)}, bf16[256,128]{1,0:T(8,128)(2,1)S(1)}) custom-call(f32[1,768]{1,0:T(1,128)S(1)} %fusion.4.refs_0_, bf16[4,16,256]{2,1,0:T(8,128)(2,1)S(1)} %get-tuple-element.78.refs_1_, f32[1280,256]{1,0:T(8,128)S(1)} %get-tuple-element.79.refs_2_, ...), custom_call_target="tpu_custom_call" | custom-call | tf_op jit(solution)/shard_map/pallas_call | solution.py:130
  96.6 0.4 collective-permute-start.18
  97.1 2.6 %collective-permute-start.19 = (bf16[256,128]{1,0:T(8,128)(2,1)S(1)}, bf16[256,128]{1,0:T(8,128)(2,1)S(1)}, u32[]{:S(2)}, u32[]{:S(2)}) collective-permute-start(bf16[256,128]{1,0:T(8,128)(2,1)S(1)} %get-tuple-element.84), channel_id=1, source_target_pairs={{0,8},{4,12},{8,0},{12,4},{1,9},{5,13},{9,1},{13,5},{2,10},{6,14},... | collective-permute-start | bytes 196616 | tf_op jit(solution)/shard_map/ppermute | solution.py:116
  99.7 1.4 %collective-permute-start.20 = (bf16[256,128]{1,0:T(8,128)(2,1)S(1)}, bf16[256,128]{1,0:T(8,128)(2,1)S(1)}, u32[]{:S(2)}, u32[]{:S(2)}) collective-permute-start(bf16[256,128]{1,0:T(8,128)(2,1)S(1)} %get-tuple-element.85), channel_id=1, source_target_pairs={{0,12},{4,8},{8,4},{12,0},{1,13},{5,9},{9,5},{13,1},{2,14},{6,10},... | collective-permute-start | bytes 196616 | tf_op jit(solution)/shard_map/ppermute | solution.py:116
  101.1 1.3 %collective-permute-done.21.refs_9_ = bf16[256,512]{1,0:T(8,128)(2,1)S(1)} collective-permute-done((bf16[256,512]{1,0:T(8,128)(2,1)S(1)}, bf16[256,512]{1,0:T(8,128)(2,1)S(1)}, u32[]{:S(2)}, u32[]{:S(2)}) %collective-permute-start.21) | collective-permute-done | bytes 262176 | tf_op jit(solution)/shard_map/ppermute | solution.py:116
  102.4 1.8 %collective-permute-start.23 = (bf16[256,512]{1,0:T(8,128)(2,1)S(1)}, bf16[256,512]{1,0:T(8,128)(2,1)S(1)}, u32[]{:S(2)}, u32[]{:S(2)}) collective-permute-start(bf16[256,512]{1,0:T(8,128)(2,1)S(1)} %collective-permute-done.15.refs_6_), channel_id=1, source_target_pairs={{0,16},{16,0},{1,17},{17,1},{2,18},{18,2},{3,19},{19,3},{4,20},{20... | collective-permute-start | bytes 786440 | tf_op jit(solution)/shard_map/ppermute | solution.py:116
  104.2 0.8 collective-permute-done.19.refs_2_
  105.0 1.5 %collective-permute-done.20.refs_3_ = bf16[256,128]{1,0:T(8,128)(2,1)S(1)} collective-permute-done((bf16[256,128]{1,0:T(8,128)(2,1)S(1)}, bf16[256,128]{1,0:T(8,128)(2,1)S(1)}, u32[]{:S(2)}, u32[]{:S(2)}) %collective-permute-start.20) | collective-permute-done | bytes 65568 | tf_op jit(solution)/shard_map/ppermute | solution.py:116
  106.5 0.9 shard_map.92
  107.5 2.9 %collective-permute-done.22.refs_2_ = bf16[256,512]{1,0:T(8,128)(2,1)S(1)} collective-permute-done((bf16[256,512]{1,0:T(8,128)(2,1)S(1)}, bf16[256,512]{1,0:T(8,128)(2,1)S(1)}, u32[]{:S(2)}, u32[]{:S(2)}) %collective-permute-start.22) | collective-permute-done | bytes 262176 | tf_op jit(solution)/shard_map/ppermute | solution.py:116
  110.4 0.7 shard_map.93
  111.1 1.9 %collective-permute-done.24 = bf16[2,256,512]{2,1,0:T(8,128)(2,1)S(1)} collective-permute-done((bf16[2,256,512]{2,1,0:T(8,128)(2,1)S(1)}, bf16[2,256,512]{2,1,0:T(8,128)(2,1)S(1)}, u32[]{:S(2)}, u32[]{:S(2)}) %collective-permute-start.24) | collective-permute-done | bytes 524320 | tf_op jit(solution)/shard_map/ppermute | solution.py:116
  113.1 1.5 %collective-permute-start.25 = (bf16[256,512]{1,0:T(8,128)(2,1)S(1)}, bf16[256,512]{1,0:T(8,128)(2,1)S(1)}, u32[]{:S(2)}, u32[]{:S(2)}) collective-permute-start(bf16[256,512]{1,0:T(8,128)(2,1)S(1)} %fusion.1), channel_id=1, source_target_pairs={{0,2},{2,0},{1,3},{3,1},{4,6},{6,4},{5,7},{7,5},{8,10},{10,8},{9,1... | collective-permute-start | bytes 786440 | tf_op jit(solution)/shard_map/ppermute | solution.py:116
  114.6 1.8 %shard_map.86 = bf16[192,2048]{1,0:T(8,128)(2,1)} custom-call(s32[8]{0:T(128)S(1)} %copy-done.8, bf16[3,192,2048]{2,1,0:T(8,128)(2,1)S(1)} %copy-done), custom_call_target="tpu_custom_call" | custom-call | tf_op jit(solution)/shard_map/pallas_call | solution.py:169
  116.5 5.0 %collective-permute-done.25 = bf16[256,512]{1,0:T(8,128)(2,1)S(1)} collective-permute-done((bf16[256,512]{1,0:T(8,128)(2,1)S(1)}, bf16[256,512]{1,0:T(8,128)(2,1)S(1)}, u32[]{:S(2)}, u32[]{:S(2)}) %collective-permute-start.25) | collective-permute-done | bytes 262176 | tf_op jit(solution)/shard_map/ppermute | solution.py:116
  121.5 0.8 fusion
  (39 shorter events, 1.3 us)
Async XLA Ops:
  0.6 9.0 %copy-start.3 = (bf16[512,512]{1,0:T(8,128)(2,1)S(1)}, bf16[512,512]{1,0:T(8,128)(2,1)}, u32[]{:S(2)}) copy-start(bf16[512,512]{1,0:T(8,128)(2,1)} %refs_2_.3) | copy-start | bytes 1572868
  0.6 9.0 %copy-start.7 = (s32[256]{0:T(256)S(1)}, s32[256]{0:T(256)}, u32[]{:S(2)}) copy-start(s32[256]{0:T(256)} %param.9) | copy-start | bytes 3076
  0.7 9.0 %copy-start.1 = (bf16[1024,1024]{1,0:T(8,128)(2,1)S(1)}, bf16[1024,1024]{1,0:T(8,128)(2,1)}, u32[]{:S(2)}) copy-start(bf16[1024,1024]{1,0:T(8,128)(2,1)} %refs_1_.3) | copy-start | bytes 6291460
  3.9 5.8 %collective-permute-start = (bf16[640,1024]{1,0:T(8,128)(2,1)}, bf16[640,1024]{1,0:T(8,128)(2,1)S(1)}, u32[]{:S(2)}, u32[]{:S(2)}) collective-permute-start(bf16[640,1024]{1,0:T(8,128)(2,1)} %get-tuple-element.48), channel_id=1, source_target_pairs={{0,1},{1,0},{2,3},{3,2},{4,5},{5,4},{6,7},{7,6},{8,9},{9,8},{10,11... | collective-permute-start | bytes 3932168 | tf_op jit(solution)/shard_map/ppermute | solution.py:116
  4.4 32.4 %collective-permute-start.3 = (bf16[640,512]{1,0:T(8,128)(2,1)}, bf16[640,512]{1,0:T(8,128)(2,1)S(1)}, u32[]{:S(2)}, u32[]{:S(2)}) collective-permute-start(bf16[640,512]{1,0:T(8,128)(2,1)} %get-tuple-element.47.refs_0_), channel_id=1, source_target_pairs={{0,4},{4,0},{8,12},{12,8},{1,5},{5,1},{9,13},{13,9},{2,6},{6,2},{1... | collective-permute-start | bytes 1966088 | tf_op jit(solution)/shard_map/ppermute | solution.py:116
  7.0 31.8 %collective-permute-start.5 = (bf16[640,512]{1,0:T(8,128)(2,1)}, bf16[640,512]{1,0:T(8,128)(2,1)S(1)}, u32[]{:S(2)}, u32[]{:S(2)}) collective-permute-start(bf16[640,512]{1,0:T(8,128)(2,1)} %get-tuple-element.47.refs_0_), channel_id=1, source_target_pairs={{0,8},{4,12},{8,0},{12,4},{1,9},{5,13},{9,1},{13,5},{2,10},{6,14},... | collective-permute-start | bytes 1966088 | tf_op jit(solution)/shard_map/ppermute | solution.py:116
  9.6 1.0 copy-start.5
  10.7 1.1 copy-start.2
  10.9 33.0 %collective-permute-start.1 = (bf16[336,512]{1,0:T(8,128)(2,1)S(1)}, bf16[336,512]{1,0:T(8,128)(2,1)S(1)}, u32[]{:S(2)}, u32[]{:S(2)}) collective-permute-start(bf16[336,512]{1,0:T(8,128)(2,1)S(1)} %get-tuple-element.49), channel_id=1, source_target_pairs={{0,4},{4,0},{8,12},{12,8},{1,5},{5,1},{9,13},{13,9},{2,6},{6,2},{1... | collective-permute-start | bytes 1032200 | tf_op jit(solution)/shard_map/ppermute | solution.py:116
  11.8 36.6 %collective-permute-start.2 = (bf16[640,512]{1,0:T(8,128)(2,1)S(1)}, bf16[640,512]{1,0:T(8,128)(2,1)S(1)}, u32[]{:S(2)}, u32[]{:S(2)}) collective-permute-start(bf16[640,512]{1,0:T(8,128)(2,1)S(1)} %copy-done.2), channel_id=1, source_target_pairs={{0,2},{2,0},{1,3},{3,1},{4,6},{6,4},{5,7},{7,5},{8,10},{10,8},{9,1... | collective-permute-start | bytes 1966088 | tf_op jit(solution)/shard_map/ppermute | solution.py:116
  36.7 17.7 %collective-permute-start.4 = (bf16[640,512]{1,0:T(8,128)(2,1)S(1)}, bf16[640,512]{1,0:T(8,128)(2,1)S(1)}, u32[]{:S(2)}, u32[]{:S(2)}) collective-permute-start(bf16[640,512]{1,0:T(8,128)(2,1)S(1)} %collective-permute-done.3.refs_2_), channel_id=1, source_target_pairs={{0,2},{2,0},{1,3},{3,1},{4,6},{6,4},{5,7},{7,5},{8,10},{10,8},{9,1... | collective-permute-start | bytes 1966088 | tf_op jit(solution)/shard_map/ppermute | solution.py:116
  38.8 28.2 %collective-permute-start.7 = (bf16[640,512]{1,0:T(8,128)(2,1)S(1)}, bf16[640,512]{1,0:T(8,128)(2,1)S(1)}, u32[]{:S(2)}, u32[]{:S(2)}) collective-permute-start(bf16[640,512]{1,0:T(8,128)(2,1)S(1)} %collective-permute-done.5.refs_4_), channel_id=1, source_target_pairs={{0,2},{2,0},{1,3},{3,1},{4,6},{6,4},{5,7},{7,5},{8,10},{10,8},{9,1... | collective-permute-start | bytes 1966088 | tf_op jit(solution)/shard_map/ppermute | solution.py:116
  44.0 24.4 %collective-permute-start.6 = (bf16[640,512]{1,0:T(8,128)(2,1)S(1)}, bf16[640,512]{1,0:T(8,128)(2,1)S(1)}, u32[]{:S(2)}, u32[]{:S(2)}) collective-permute-start(bf16[640,512]{1,0:T(8,128)(2,1)S(1)} %collective-permute-done.5.refs_4_), channel_id=1, source_target_pairs={{0,4},{4,0},{8,12},{12,8},{1,5},{5,1},{9,13},{13,9},{2,6},{6,2},{1... | collective-permute-start | bytes 1966088 | tf_op jit(solution)/shard_map/ppermute | solution.py:116
  45.8 22.6 %collective-permute-start.9 = (bf16[336,512]{1,0:T(8,128)(2,1)S(1)}, bf16[336,512]{1,0:T(8,128)(2,1)S(1)}, u32[]{:S(2)}, u32[]{:S(2)}) collective-permute-start(bf16[336,512]{1,0:T(8,128)(2,1)S(1)} %get-tuple-element.54), channel_id=1, source_target_pairs={{0,8},{4,12},{8,0},{12,4},{1,9},{5,13},{9,1},{13,5},{2,10},{6,14},... | collective-permute-start | bytes 1032200 | tf_op jit(solution)/shard_map/ppermute | solution.py:116
  54.4 14.0 %collective-permute-start.8 = (bf16[336,512]{1,0:T(8,128)(2,1)S(1)}, bf16[336,512]{1,0:T(8,128)(2,1)S(1)}, u32[]{:S(2)}, u32[]{:S(2)}) collective-permute-start(bf16[336,512]{1,0:T(8,128)(2,1)S(1)} %collective-permute-done.1.refs_7_), channel_id=1, source_target_pairs={{0,16},{16,0},{1,17},{17,1},{2,18},{18,2},{3,19},{19,3},{4,20},{20... | collective-permute-start | bytes 1032200 | tf_op jit(solution)/shard_map/ppermute | solution.py:116
  56.3 21.1 %collective-permute-start.11 = (bf16[336,512]{1,0:T(8,128)(2,1)S(1)}, bf16[336,512]{1,0:T(8,128)(2,1)S(1)}, u32[]{:S(2)}, u32[]{:S(2)}) collective-permute-start(bf16[336,512]{1,0:T(8,128)(2,1)S(1)} %get-tuple-element.60), channel_id=1, source_target_pairs={{0,12},{4,8},{8,4},{12,0},{1,13},{5,9},{9,5},{13,1},{2,14},{6,10},... | collective-permute-start | bytes 1032200 | tf_op jit(solution)/shard_map/ppermute | solution.py:116
  68.4 9.0 %collective-permute-start.12 = (bf16[336,512]{1,0:T(8,128)(2,1)S(1)}, bf16[336,512]{1,0:T(8,128)(2,1)S(1)}, u32[]{:S(2)}, u32[]{:S(2)}) collective-permute-start(bf16[336,512]{1,0:T(8,128)(2,1)S(1)} %collective-permute-done.9.refs_8_), channel_id=1, source_target_pairs={{0,16},{16,0},{1,17},{17,1},{2,18},{18,2},{3,19},{19,3},{4,20},{20... | collective-permute-start | bytes 1032200 | tf_op jit(solution)/shard_map/ppermute | solution.py:116
  69.9 14.6 %collective-permute-start.10 = (bf16[640,512]{1,0:T(8,128)(2,1)S(1)}, bf16[640,512]{1,0:T(8,128)(2,1)S(1)}, u32[]{:S(2)}, u32[]{:S(2)}) collective-permute-start(bf16[640,512]{1,0:T(8,128)(2,1)S(1)} %collective-permute-done.6.refs_6_), channel_id=1, source_target_pairs={{0,2},{2,0},{1,3},{3,1},{4,6},{6,4},{5,7},{7,5},{8,10},{10,8},{9,1... | collective-permute-start | bytes 1966088 | tf_op jit(solution)/shard_map/ppermute | solution.py:116
  77.4 8.7 %collective-permute-start.13 = (bf16[336,512]{1,0:T(8,128)(2,1)S(1)}, bf16[336,512]{1,0:T(8,128)(2,1)S(1)}, u32[]{:S(2)}, u32[]{:S(2)}) collective-permute-start(bf16[336,512]{1,0:T(8,128)(2,1)S(1)} %collective-permute-done.11.refs_10_), channel_id=1, source_target_pairs={{0,16},{16,0},{1,17},{17,1},{2,18},{18,2},{3,19},{19,3},{4,20},{20... | collective-permute-start | bytes 1032200 | tf_op jit(solution)/shard_map/ppermute | solution.py:116
  78.9 12.3 %collective-permute-start.14 = (bf16[256,512]{1,0:T(8,128)(2,1)S(1)}, bf16[256,512]{1,0:T(8,128)(2,1)S(1)}, u32[]{:S(2)}, u32[]{:S(2)}) collective-permute-start(bf16[256,512]{1,0:T(8,128)(2,1)S(1)} %get-tuple-element.75), channel_id=1, source_target_pairs={{0,8},{4,12},{8,0},{12,4},{1,9},{5,13},{9,1},{13,5},{2,10},{6,14},... | collective-permute-start | bytes 786440 | tf_op jit(solution)/shard_map/ppermute | solution.py:116
  81.6 9.6 %collective-permute-start.15 = (bf16[256,512]{1,0:T(8,128)(2,1)S(1)}, bf16[256,512]{1,0:T(8,128)(2,1)S(1)}, u32[]{:S(2)}, u32[]{:S(2)}) collective-permute-start(bf16[256,512]{1,0:T(8,128)(2,1)S(1)} %get-tuple-element.75), channel_id=1, source_target_pairs={{0,4},{4,0},{8,12},{12,8},{1,5},{5,1},{9,13},{13,9},{2,6},{6,2},{1... | collective-permute-start | bytes 786440 | tf_op jit(solution)/shard_map/ppermute | solution.py:116
  91.2 3.2 %collective-permute-start.17 = (f32[1280,256]{1,0:T(8,128)}, f32[1280,256]{1,0:T(8,128)S(1)}, u32[]{:S(2)}, u32[]{:S(2)}) collective-permute-start(f32[1280,256]{1,0:T(8,128)} %get-tuple-element.80), channel_id=1, source_target_pairs={{0,1},{1,0},{2,3},{3,2},{4,5},{5,4},{6,7},{7,6},{8,9},{9,8},{10,11... | collective-permute-start | bytes 3932168 | tf_op jit(solution)/shard_map/ppermute | solution.py:116
  91.6 9.5 %collective-permute-start.16 = (bf16[256,512]{1,0:T(8,128)(2,1)S(1)}, bf16[256,512]{1,0:T(8,128)(2,1)S(1)}, u32[]{:S(2)}, u32[]{:S(2)}) collective-permute-start(bf16[256,512]{1,0:T(8,128)(2,1)S(1)} %collective-permute-done.14.refs_7_), channel_id=1, source_target_pairs={{0,16},{16,0},{1,17},{17,1},{2,18},{18,2},{3,19},{19,3},{4,20},{20... | collective-permute-start | bytes 786440 | tf_op jit(solution)/shard_map/ppermute | solution.py:116
  92.1 10.3 %collective-permute-start.21 = (bf16[256,512]{1,0:T(8,128)(2,1)S(1)}, bf16[256,512]{1,0:T(8,128)(2,1)S(1)}, u32[]{:S(2)}, u32[]{:S(2)}) collective-permute-start(bf16[256,512]{1,0:T(8,128)(2,1)S(1)} %collective-permute-done.14.refs_7_), channel_id=1, source_target_pairs={{0,4},{4,0},{8,12},{12,8},{1,5},{5,1},{9,13},{13,9},{2,6},{6,2},{1... | collective-permute-start | bytes 786440 | tf_op jit(solution)/shard_map/ppermute | solution.py:116
  94.4 12.1 %copy-start.4 = (bf16[256,2048]{1,0:T(8,128)(2,1)S(1)}, bf16[256,2048]{1,0:T(8,128)(2,1)}, u32[]{:S(2)}) copy-start(bf16[256,2048]{1,0:T(8,128)(2,1)} %refs_4_.5) | copy-start | bytes 3145732
  94.4 12.1 %copy-start.6 = (bf16[512,512]{1,0:T(8,128)(2,1)S(1)}, bf16[512,512]{1,0:T(8,128)(2,1)}, u32[]{:S(2)}) copy-start(bf16[512,512]{1,0:T(8,128)(2,1)} %refs_5_.1) | copy-start | bytes 1572868
  96.6 7.5 %collective-permute-start.18 = (bf16[256,128]{1,0:T(8,128)(2,1)S(1)}, bf16[256,128]{1,0:T(8,128)(2,1)S(1)}, u32[]{:S(2)}, u32[]{:S(2)}) collective-permute-start(bf16[256,128]{1,0:T(8,128)(2,1)S(1)} %get-tuple-element.83), channel_id=1, source_target_pairs={{0,4},{4,0},{8,12},{12,8},{1,5},{5,1},{9,13},{13,9},{2,6},{6,2},{1... | collective-permute-start | bytes 196616 | tf_op jit(solution)/shard_map/ppermute | solution.py:116
  97.1 7.9 %collective-permute-start.19 = (bf16[256,128]{1,0:T(8,128)(2,1)S(1)}, bf16[256,128]{1,0:T(8,128)(2,1)S(1)}, u32[]{:S(2)}, u32[]{:S(2)}) collective-permute-start(bf16[256,128]{1,0:T(8,128)(2,1)S(1)} %get-tuple-element.84), channel_id=1, source_target_pairs={{0,8},{4,12},{8,0},{12,4},{1,9},{5,13},{9,1},{13,5},{2,10},{6,14},... | collective-permute-start | bytes 196616 | tf_op jit(solution)/shard_map/ppermute | solution.py:116
  99.7 6.8 %collective-permute-start.20 = (bf16[256,128]{1,0:T(8,128)(2,1)S(1)}, bf16[256,128]{1,0:T(8,128)(2,1)S(1)}, u32[]{:S(2)}, u32[]{:S(2)}) collective-permute-start(bf16[256,128]{1,0:T(8,128)(2,1)S(1)} %get-tuple-element.85), channel_id=1, source_target_pairs={{0,12},{4,8},{8,4},{12,0},{1,13},{5,9},{9,5},{13,1},{2,14},{6,10},... | collective-permute-start | bytes 196616 | tf_op jit(solution)/shard_map/ppermute | solution.py:116
  101.1 9.3 %collective-permute-start.22 = (bf16[256,512]{1,0:T(8,128)(2,1)S(1)}, bf16[256,512]{1,0:T(8,128)(2,1)S(1)}, u32[]{:S(2)}, u32[]{:S(2)}) collective-permute-start(bf16[256,512]{1,0:T(8,128)(2,1)S(1)} %collective-permute-done.16.refs_8_), channel_id=1, source_target_pairs={{0,4},{4,0},{8,12},{12,8},{1,5},{5,1},{9,13},{13,9},{2,6},{6,2},{1... | collective-permute-start | bytes 786440 | tf_op jit(solution)/shard_map/ppermute | solution.py:116
  102.4 8.0 %collective-permute-start.23 = (bf16[256,512]{1,0:T(8,128)(2,1)S(1)}, bf16[256,512]{1,0:T(8,128)(2,1)S(1)}, u32[]{:S(2)}, u32[]{:S(2)}) collective-permute-start(bf16[256,512]{1,0:T(8,128)(2,1)S(1)} %collective-permute-done.15.refs_6_), channel_id=1, source_target_pairs={{0,16},{16,0},{1,17},{17,1},{2,18},{18,2},{3,19},{19,3},{4,20},{20... | collective-permute-start | bytes 786440 | tf_op jit(solution)/shard_map/ppermute | solution.py:116
  110.4 4.3 %copy-start = (bf16[3,192,2048]{2,1,0:T(8,128)(2,1)S(1)}, bf16[3,192,2048]{2,1,0:T(8,128)(2,1)}, u32[]{:S(2)}) copy-start(bf16[3,192,2048]{2,1,0:T(8,128)(2,1)} %refs_1_.2) | copy-start | bytes 7077892
  110.4 4.3 %copy-start.8 = (s32[8]{0:T(128)S(1)}, s32[8]{0:T(128)}, u32[]{:S(2)}) copy-start(s32[8]{0:T(128)} %refs_0_.1) | copy-start | bytes 100
  111.0 2.0 %collective-permute-start.24 = (bf16[2,256,512]{2,1,0:T(8,128)(2,1)S(1)}, bf16[2,256,512]{2,1,0:T(8,128)(2,1)S(1)}, u32[]{:S(2)}, u32[]{:S(2)}) collective-permute-start(bf16[2,256,512]{2,1,0:T(8,128)(2,1)S(1)} %get-tuple-element.91), channel_id=1, source_target_pairs={{0,1},{1,0},{2,3},{3,2},{4,5},{5,4},{6,7},{7,6},{8,9},{9,8},{10,11... | collective-permute-start | bytes 1572872 | tf_op jit(solution)/shard_map/ppermute | solution.py:116
  113.1 8.4 %collective-permute-start.25 = (bf16[256,512]{1,0:T(8,128)(2,1)S(1)}, bf16[256,512]{1,0:T(8,128)(2,1)S(1)}, u32[]{:S(2)}, u32[]{:S(2)}) collective-permute-start(bf16[256,512]{1,0:T(8,128)(2,1)S(1)} %fusion.1), channel_id=1, source_target_pairs={{0,2},{2,0},{1,3},{3,1},{4,6},{6,4},{5,7},{7,5},{8,10},{10,8},{9,1... | collective-permute-start | bytes 786440 | tf_op jit(solution)/shard_map/ppermute | solution.py:116
